TPU v7x, 32 devices: a whole 2x2x4 slice. The times are simulated.
32 devices in a mesh: groups: 2 (over y), seq: 4 (over z), tp: 2 (over x), section: 2 (over core).
Axes of the slice: x: 2, y: 2, z: 4, core: 2. Of those that a mesh axis runs over, the one named last changes fastest.
Arguments:
- tokens: bfloat16 [2048, 16384], P(('groups', 'tp', 'section'), 'seq'), parts along dimension 0, may hold values from -6 to 6
- kv_weight: bfloat16 [16384, 1024], P('seq'), may hold values from -0.046875 to 0.046875
- owners: int32 [8, 256, 1], P(('groups', 'tp', 'section'), 'seq'), parts along dimension 0, may hold values from 0 to 3; in each aligned block of 64 rows (0 to 63, 64 to 127, ..., all dimensions but the last counted through in order) at most 32 rows name the same one
- requests: int32 [8, 256], P(('groups', 'tp', 'section'), 'seq'), parts along dimension 0, may hold values from 0 to 7
- signs: int32 [8, 128], replicated, may hold values from 0 to 1
- queries: bfloat16 [8, 2, 8, 4096], P(('groups', 'seq'), 'section'), parts along dimension 0, may hold values from -96 to 96
- kv_cache: bfloat16 [8, 2, 8, 256, 1024], P(('groups', 'seq'), 'section', None, 'tp'), parts along dimension 0, may hold values from -96 to 96
- lengths: int32 [8, 2, 8], P(('groups', 'seq'), 'section'), parts along dimension 0, may hold values from 1 to 256, 1280 in all within a row
Outputs:
- attended: bfloat16 [8, 2, 8, 4096], P(('groups', 'seq'), 'section'), parts along dimension 0
There are 2 independent parts, one for each index of `groups`. A program takes and returns all parts, laid end to end along the dimension named above; an argument that names none is the same for every part. Nothing has to cross between parts.
Inputs may be any that keep to these rules, and one draw needn't show every extreme that they name: `owners`: in the rows of one device (64 aligned rows) no owner is named more than 32 times. The lengths of one owner's requests sum to 1280.
All inputs are finite; a program needn't handle non-finite values.
Results may differ from a plain program's by a relative error of at most 0.025.
Values may be sent and summed in bfloat16 or wider, within the bound.
No kernel may reach another device: no remote copies, remote signals or barrier semaphores. Data moves between devices by JAX's collectives and lax.ppermute only.
A program may use at most 64 MiB of HBM per device.

v0:
```python
import math

import jax
import jax.numpy as jnp
from jax import lax
from jax.sharding import PartitionSpec as P


def hadamard(order):
    rows = lax.broadcasted_iota(jnp.int32, (order, order), 0)
    cols = lax.broadcasted_iota(jnp.int32, (order, order), 1)
    parity = jnp.zeros((order, order), jnp.int32)
    for bit_number in range(order.bit_length() - 1):
        parity = parity + rows // 2**bit_number % 2 * (cols // 2**bit_number % 2)
    return (1 - 2 * (parity % 2)).astype(jnp.float32)


def rotate(blocks, sign_rows, matrix):
    product = jnp.einsum(
        "...h,hk->...k", blocks * sign_rows, matrix, precision=lax.Precision.HIGHEST
    )
    return product / math.sqrt(matrix.shape[0])


def encode(rotated):
    largest = jnp.max(jnp.abs(rotated), axis=-1) + 1e-06
    scales = largest.astype(jnp.bfloat16)
    encoded = (rotated / scales.astype(jnp.float32)[..., None]).astype(jnp.bfloat16)
    return (encoded, scales)


def decode(encoded, scales):
    return (encoded.astype(jnp.float32) * scales.astype(jnp.float32)[..., None]).astype(
        jnp.bfloat16
    )


def slot_numbers(targets, count, room):
    onehot = (targets[:, None] == lax.iota(jnp.int32, count)[None, :]).astype(jnp.int32)
    within = jnp.sum((jnp.cumsum(onehot, axis=0) - 1) * onehot, axis=1)
    return targets * room + within


def on_device(tokens, kv_weight, owners, requests, signs, queries, kv_cache, lengths):
    seq_count = lax.axis_size("seq")
    per_device = owners.shape[1]
    slots = max(2, (2 * per_device + seq_count - 1) // seq_count)
    head_blocks = signs.shape[0]
    kv_heads = head_blocks // 2
    head_size = signs.shape[1]
    matrix = hadamard(head_size)
    sign_rows = (2 * signs - 1).astype(jnp.float32)
    summed = lax.psum_scatter(
        jnp.dot(tokens, kv_weight, preferred_element_type=jnp.float32).astype(jnp.bfloat16),
        "seq",
        scatter_dimension=0,
        tiled=True,
    ).astype(jnp.float32)
    encoded, scales = encode(
        rotate(summed.reshape(per_device, head_blocks, head_size), sign_rows, matrix)
    )
    slot_index = slot_numbers(owners[0, :, 0], seq_count, slots)
    slot_total = seq_count * slots
    send_values = (
        jnp.zeros((slot_total, head_blocks, head_size), jnp.bfloat16).at[slot_index].set(encoded)
    )
    send_scales = jnp.zeros((slot_total, head_blocks), jnp.bfloat16).at[slot_index].set(scales)
    send_codes = jnp.zeros((slot_total,), jnp.int32).at[slot_index].set(requests[0] + 1)
    got_values, got_scales, arrived_codes = (
        lax.all_to_all(send_values, "seq", split_axis=0, concat_axis=0, tiled=True),
        lax.all_to_all(send_scales, "seq", split_axis=0, concat_axis=0, tiled=True),
        lax.all_to_all(send_codes, "seq", split_axis=0, concat_axis=0, tiled=True),
    )
    arrived = decode(got_values, got_scales)
    query = queries[0, 0]
    request_count = query.shape[0]
    group = query.shape[1] // (kv_heads * head_size)
    query_blocks = query.astype(jnp.float32).reshape(request_count, kv_heads, group, head_size)
    query_rot = rotate(query_blocks, sign_rows[:kv_heads][:, None, :], matrix).astype(jnp.bfloat16)
    local_cache = kv_cache[0, 0]
    cache_span = local_cache.shape[1]
    local_cache = local_cache.reshape(request_count, cache_span, head_blocks, head_size)
    score_scale = 1.0 / math.sqrt(head_size)
    lowest = -1e30
    highest = lax.Precision.HIGHEST
    score_cache = (
        jnp.einsum(
            "rkgd,rckd->rkgc",
            query_rot,
            local_cache[:, :, :kv_heads],
            preferred_element_type=jnp.float32,
        )
        * score_scale
    )
    score_new = (
        jnp.einsum(
            "rkgd,nkd->rkgn", query_rot, arrived[:, :kv_heads], preferred_element_type=jnp.float32
        )
        * score_scale
    )
    positions = lax.axis_index("tp") * cache_span + lax.iota(jnp.int32, cache_span)
    mask_cache = (positions[None, :] < lengths[0, 0][:, None])[:, None, None, :]
    match = arrived_codes[None, :] == (lax.iota(jnp.int32, request_count) + 1)[:, None]
    mask_new = match[:, None, None, :]
    top = jnp.maximum(
        jnp.max(jnp.where(mask_cache, score_cache, lowest), axis=-1),
        jnp.max(jnp.where(mask_new, score_new, lowest), axis=-1),
    )
    probs_cache = jnp.where(mask_cache, jnp.exp(score_cache - top[..., None]), 0.0)
    probs_new = jnp.where(mask_new, jnp.exp(score_new - top[..., None]), 0.0)
    total = jnp.sum(probs_cache, axis=-1) + jnp.sum(probs_new, axis=-1)
    mixed = jnp.einsum(
        "rkgc,rckd->rkgd",
        probs_cache,
        local_cache[:, :, kv_heads:].astype(jnp.float32),
        precision=highest,
    )
    mixed = mixed + jnp.einsum(
        "rkgn,nkd->rkgd", probs_new, arrived[:, kv_heads:].astype(jnp.float32), precision=highest
    )
    shared_top = lax.pmax(top, "tp")
    factor = jnp.exp(top - shared_top)
    total, mixed = (
        lax.psum((total * factor).astype(jnp.bfloat16), "tp").astype(jnp.float32),
        lax.psum((mixed * factor[..., None]).astype(jnp.bfloat16), "tp").astype(jnp.float32),
    )
    mixed = mixed / total[..., None]
    output = rotate(mixed, 1.0, matrix) * sign_rows[kv_heads:][None, :, None, :]
    return output.reshape(1, 1, request_count, group * kv_heads * head_size).astype(jnp.bfloat16)


def solution(mesh):
    placed = (
        P(("groups", "tp", "section"), "seq"),
        P("seq", None),
        P(("groups", "tp", "section"), "seq", None),
        P(("groups", "tp", "section"), "seq"),
        P(),
        P(("groups", "seq"), "section", None, None),
        P(("groups", "seq"), "section", None, "tp", None),
        P(("groups", "seq"), "section", None),
    )
    return jax.shard_map(
        on_device,
        mesh=mesh,
        in_specs=placed,
        out_specs=P(("groups", "seq"), "section", None, None),
        check_vma=False,
    )
```

profile of v0, /device:TPU:0, one launch (start us, length us, event | category | flops | bytes accessed | tf_op | source)
XLA Modules:
  0.0 114.8 jit_solution(6240723388200547971)
XLA Ops:
  6.5 0.8 add_bitcast_fusion
  7.3 0.7 fusion.57
  8.2 0.8 select_reduce_fusion.2
  9.0 0.7 fusion.61
  9.7 0.8 scatter_custom_fusion
  11.1 6.3 %all-to-all-start = ((s32[4,32,1]{1,2,0:T(1,128)}), s32[4,32,1]{1,2,0:T(1,128)S(1)}, u32[]{:S(2)}, u32[]{:S(2)}) async-start(s32[4,32,1]{1,2,0:T(1,128)} %bitcast.10), calls=%async_computation | async-start | bytes 4096 | tf_op jit(solution)/shard_map/all_to_all | solution.py:72
  17.4 6.5 %convolution_convert_fusion = bf16[256,1024]{1,0:T(8,128)(2,1)} fusion(bf16[256,4096]{1,0:T(8,128)(2,1)S(1)} %copy-done, bf16[4096,1024]{1,0:T(8,128)(2,1)} %param.9), kind=kOutput, calls=%fused_computation.3 | convolution fusion | flops 2147745792 | bytes 11010048 | tf_op jit(solution)/shard_map/dot_general | solution.py:54
  24.2 3.9 %copy.29 = bf16[1,1,8,128,1024]{3,4,2,1,0:T(8,128)(2,1)} copy(bf16[1,1,8,128,1024]{4,3,2,1,0:T(8,128)(2,1)} %param.14) | data formatting | bytes 4194304 | tf_op args[6]
  28.9 18.4 %reduce-scatter.2.cloned.1.call-done = bf16[64,1024]{1,0:T(8,128)(2,1)} async-done(((bf16[256,1024]{1,0:T(8,128)(2,1)}), bf16[64,1024]{1,0:T(8,128)(2,1)}) %reduce-scatter.2.cloned.1.call-update) | async-done | bytes 131088 | tf_op jit(solution)/shard_map/reduce_scatter | solution.py:53
  47.3 0.9 convert_bitcast_fusion
  48.3 0.8 abs_reduce_fusion
  49.2 0.8 scatter_custom_fusion.2
  50.0 0.7 reshape.190
  50.7 3.2 %all-to-all-start.2 = ((bf16[4,2,128]{2,1,0:T(2,128)(2,1)}), bf16[4,2,128]{2,1,0:T(2,128)(2,1)S(1)}, u32[]{:S(2)}, u32[]{:S(2)}) async-start(bf16[4,2,128]{2,1,0:T(2,128)(2,1)} %reshape.190), calls=%async_computation.3 | async-start | bytes 4096 | tf_op jit(solution)/shard_map/all_to_all | solution.py:71
  54.1 0.8 broadcast_in_dim.55
  54.8 6.6 %scatter_fusion = bf16[128,8,128]{2,1,0:T(8,128)(2,1)} fusion(bf16[128,8,128]{2,1,0:T(8,128)(2,1)} %broadcast_in_dim.55, s32[64]{0:T(128)S(1)} %fusion.61, bf16[64,8,128]{2,1,0:T(8,128)(2,1)S(1)} %divide_convert_fusion), kind=kCustom, calls=%fused_computation.1 | custom fusion | bytes 393472 | tf_op jit(solution)/shard_map/scatter | solution.py:65
  61.4 5.0 %all-to-all-start.1 = ((bf16[128,8,128]{2,1,0:T(8,128)(2,1)}), bf16[128,8,128]{2,1,0:T(8,128)(2,1)S(1)}, u32[]{:S(2)}, u32[]{:S(2)}) async-start(bf16[128,8,128]{2,1,0:T(8,128)(2,1)} %scatter_fusion), calls=%async_computation.2 | async-start | bytes 524288 | tf_op jit(solution)/shard_map/all_to_all | solution.py:70
  66.4 1.7 %select_reduce_fusion.1 = (f32[8,4,8]{2,1,0:T(4,128)S(1)}, f32[8,4,8,128]{3,2,1,0:T(8,128)S(1)}) fusion(pred[8,128]{1,0:T(8,128)(4,1)S(1)} %broadcast_compare_fusion.1, bf16[8,4,8,128]{3,2,1,0:T(8,128)(2,1)S(1)} %fusion.3, bf16[8,128,8,128]{1,3,2,0:T(8,128)(2,1)} %bitcast.60), kind=kOutput, calls=%fused_computation.31 | convolution fusion | flops 8486656 | bytes 1247232 | tf_op jit(solution)/shard_map/rkgd,rckd->rkgc/dot_general | solution.py:87
  69.6 3.6 %all-to-all-done.1 = bf16[128,8,128]{2,1,0:T(8,128)(2,1)S(1)} async-done(((bf16[128,8,128]{2,1,0:T(8,128)(2,1)}), bf16[128,8,128]{2,1,0:T(8,128)(2,1)S(1)}, u32[]{:S(2)}, u32[]{:S(2)}) %all-to-all-start.1) | async-done | bytes 262176 | tf_op jit(solution)/shard_map/all_to_all | solution.py:70
  73.7 8.0 %pmax.7 = f32[8,4,8]{2,1,0:T(4,128)S(1)} all-reduce(f32[8,4,8]{2,1,0:T(4,128)S(1)} %max.9), channel_id=1, replica_groups=mesh['groups'=2,'seq'=4,'tp'=2,'section'=2] {'tp'}, use_global_device_ids=true, to_apply=%region_9.10 | all-reduce | flops 256 | bytes 2048 | tf_op jit(solution)/shard_map/pmax | solution.py:121
  82.3 3.6 %fusion.2 = bf16[8,4,8,128]{3,2,1,0:T(8,128)(2,1)} fusion(f32[8,4,8,128]{3,2,1,0:T(8,128)S(1)} %convolution_bitcast_fusion, bf16[8,128,8,128]{1,3,2,0:T(8,128)(2,1)} %bitcast.61, f32[8,4,8,128]{3,2,1,0:T(8,128)S(1)} %get-tuple-element.14, f32[8,4,8]{2,1,0:T(4,128)S(1)} %get-tuple-element.8, f32[8,4,8]{2,1,0:T(4,128)S(1)} %max.9, ...), kind=kOutput, calls=%fused_computation.13 | convolution fusion | flops 50495488 | bytes 1379328 | tf_op jit(solution)/shard_map/rkgc,rckd->rkgd/dot_general | solution.py:112
  86.0 5.0 %psum.15 = bf16[8,4,8]{2,1,0:T(4,128)(2,1)S(1)} all-reduce(bf16[8,4,8]{2,1,0:T(4,128)(2,1)S(1)} %get-tuple-element.7), channel_id=1, replica_groups=mesh['groups'=2,'seq'=4,'tp'=2,'section'=2] {'tp'}, use_global_device_ids=true, to_apply=%region_13.14 | all-reduce | flops 256 | bytes 1024 | tf_op jit(solution)/shard_map/psum | solution.py:124
  91.0 14.8 %all-reduce.2.cloned.1.call-done = bf16[8,4,8,128]{3,2,1,0:T(8,128)(2,1)} async-done(((bf16[8,4,8,128]{3,2,1,0:T(8,128)(2,1)}), bf16[8,4,8,128]{3,2,1,0:T(8,128)(2,1)}) %all-reduce.2.cloned.1.call-update) | async-done | bytes 65552 | tf_op jit(solution)/shard_map/psum | solution.py:125
  105.8 1.5 %fusion.4 = bf16[8,4,8,128]{3,2,1,0:T(8,128)(2,1)S(1)} fusion(bf16[8,4,8,128]{3,2,1,0:T(8,128)(2,1)} %all-reduce.2.cloned.1.call-done, f32[4,128]{1,0:T(4,128)S(1)} %get-tuple-element.9, f32[8,4,8]{2,1,0:T(4,128)S(1)} %convert_element_type.105, s32[128]{0:T(128)S(1)} %get-tuple-element.17, s32[128]{0:T(128)S(1)} %get-tuple-element.29, ...), kind=kOutput, calls=%fused_computation.15 | convolution fusion | flops 53460992 | bytes 141056 | tf_op jit(solution)/shard_map/...h,hk->...k/dot_general | solution.py:19
  (52 shorter events, 5.2 us)
Async XLA Ops:
  6.5 10.9 %copy-start = (bf16[256,4096]{1,0:T(8,128)(2,1)S(1)}, bf16[256,4096]{1,0:T(8,128)(2,1)}, u32[]{:S(2)}) copy-start(bf16[256,4096]{1,0:T(8,128)(2,1)} %param.8) | copy-start | bytes 6291460
  11.1 39.6 %all-to-all-start = ((s32[4,32,1]{1,2,0:T(1,128)}), s32[4,32,1]{1,2,0:T(1,128)S(1)}, u32[]{:S(2)}, u32[]{:S(2)}) async-start(s32[4,32,1]{1,2,0:T(1,128)} %bitcast.10), calls=%async_computation | async-start | bytes 4096 | tf_op jit(solution)/shard_map/all_to_all | solution.py:72
  17.4 6.7 %copy-start.1 = (bf16[1,1,8,4096]{3,2,1,0:T(8,128)(2,1)S(1)}, bf16[1,1,8,4096]{3,2,1,0:T(8,128)(2,1)}, u32[]{:S(2)}) copy-start(bf16[1,1,8,4096]{3,2,1,0:T(8,128)(2,1)} %param.13) | copy-start | bytes 196612
  17.4 29.9 %reduce-scatter.2.cloned.1.call-start = ((), (), s32[]{:S(2)}) async-start(), calls=%async_computation.4 | async-start | bytes 655360 | tf_op jit(solution)/shard_map/reduce_scatter | solution.py:53
  24.2 4.0 %copy-start.3 = (s32[1,1,8]{2,1,0:T(1,128)S(1)}, s32[1,1,8]{2,1,0:T(1,128)}, u32[]{:S(2)}) copy-start(s32[1,1,8]{2,1,0:T(1,128)} %param.15) | copy-start | bytes 100
  24.2 4.0 %copy-start.2 = (s32[8,128]{1,0:T(8,128)S(1)}, s32[8,128]{1,0:T(8,128)}, u32[]{:S(2)}) copy-start(s32[8,128]{1,0:T(8,128)} %param.12) | copy-start | bytes 12292
  50.7 10.7 %all-to-all-start.2 = ((bf16[4,2,128]{2,1,0:T(2,128)(2,1)}), bf16[4,2,128]{2,1,0:T(2,128)(2,1)S(1)}, u32[]{:S(2)}, u32[]{:S(2)}) async-start(bf16[4,2,128]{2,1,0:T(2,128)(2,1)} %reshape.190), calls=%async_computation.3 | async-start | bytes 4096 | tf_op jit(solution)/shard_map/all_to_all | solution.py:71
  61.4 11.8 %all-to-all-start.1 = ((bf16[128,8,128]{2,1,0:T(8,128)(2,1)}), bf16[128,8,128]{2,1,0:T(8,128)(2,1)S(1)}, u32[]{:S(2)}, u32[]{:S(2)}) async-start(bf16[128,8,128]{2,1,0:T(8,128)(2,1)} %scatter_fusion), calls=%async_computation.2 | async-start | bytes 524288 | tf_op jit(solution)/shard_map/all_to_all | solution.py:70
  66.4 39.4 %all-reduce.2.cloned.1.call-start = ((), (), s32[]{:S(2)}) async-start(), calls=%async_computation.5 | async-start | bytes 131072 | tf_op jit(solution)/shard_map/psum | solution.py:125
Sparse Core Ops, SparseCore 0:
  24.1 23.1 reduce-scatter.1
  86.1 19.6 all-reduce.1
where the time goes:
time: 116 us; the launch traced here: 115 us
  waiting for transfers between devices  36.9 us (32%)
  matrix products  15.4 us (13%)
  local copies, waits for them, and re-layouts  14.9 us (13%)
  starting transfers between devices  14.6 us (13%)
  between operations  13.6 us (12%)
  blocking collectives  13 us (11%)
  other arithmetic  6.39 us (6%)
    reduce_scatter x1, waiting for transfers between devices, on_device(): lax.psum_scatter(jnp.dot(tokens, kv_weight, preferred_element_type=jnp.fl...  18.4 us
    psum x1, waiting for transfers between devices, on_device(): lax.psum((mixed * factor[..., None]).astype(jnp.bfloat16), 'tp')  14.8 us
    pmax x1, blocking collectives, on_device(): shared_top = lax.pmax(top, 'tp')  8.02 us
    scatter x1, local copies, waits for them, and re-layouts, on_device(): jnp.zeros((slot_total, head_blocks, head_size), jnp.bfloat16).at[slot_index]  6.56 us
    dot_general x1, matrix products, on_device(): jnp.dot(tokens, kv_weight, preferred_element_type=jnp.float32)  6.54 us
    all_to_all x1, starting transfers between devices, on_device(): lax.all_to_all(send_codes, 'seq', split_axis=0, concat_axis=0, tiled=True)  6.32 us
    all_to_all x1, starting transfers between devices, on_device(): lax.all_to_all(send_values, 'seq', split_axis=0, concat_axis=0, tiled=True)  5.02 us
    psum x1, blocking collectives, on_device(): lax.psum((total * factor).astype(jnp.bfloat16), 'tp').astype(jnp.float32)  5.01 us
  transfers between devices with their start and end apart: 5, of which 3 were waited for; matrix products, arithmetic and copies ran while one was open for 22% of the time, Pallas kernels for 0%

commit v1 on v0

--- a/solution.py
+++ b/solution.py
@@ -1,9 +1,359 @@
+import functools
 import math
 
 import jax
 import jax.numpy as jnp
 from jax import lax
+from jax.experimental import pallas as pl
+from jax.experimental.pallas import tpu as pltpu
 from jax.sharding import PartitionSpec as P
+
+LOWEST = -1e30
+VMEM_LIMIT = 48 * 1024 * 1024
+NT = (((1,), (1,)), ((), ()))
+
+
+def params():
+    return pltpu.CompilerParams(vmem_limit_bytes=VMEM_LIMIT)
+
+
+def hadamard_tile(order):
+    rows = lax.broadcasted_iota(jnp.int32, (order, order), 0)
+    cols = lax.broadcasted_iota(jnp.int32, (order, order), 1)
+    common = rows & cols
+    parity = jnp.zeros((order, order), jnp.int32)
+    for bit_number in range(order.bit_length() - 1):
+        parity = parity ^ (common >> bit_number)
+    return (1 - 2 * (parity & 1)).astype(jnp.float32).astype(jnp.bfloat16)
+
+
+def project_kernel(tokens_ref, weight_ref, out_ref, acc_ref):
+    step = pl.program_id(0)
+    part = jnp.dot(tokens_ref[...], weight_ref[...], preferred_element_type=jnp.float32)
+
+    @pl.when(step == 0)
+    def _():
+        acc_ref[...] = part
+
+    @pl.when(step > 0)
+    def _():
+        acc_ref[...] += part
+
+    @pl.when(step == pl.num_programs(0) - 1)
+    def _():
+        out_ref[...] = acc_ref[...].astype(out_ref.dtype)
+
+
+def project(tokens, weight):
+    rows, features = tokens.shape
+    width = weight.shape[1]
+    block = min(512, features)
+    return pl.pallas_call(
+        project_kernel,
+        grid=(features // block,),
+        in_specs=[
+            pl.BlockSpec((rows, block), lambda i: (0, i)),
+            pl.BlockSpec((block, width), lambda i: (i, 0)),
+        ],
+        out_specs=pl.BlockSpec((rows, width), lambda i: (0, 0)),
+        out_shape=jax.ShapeDtypeStruct((rows, width), jnp.bfloat16),
+        scratch_shapes=[pltpu.VMEM((rows, width), jnp.float32)],
+        compiler_params=params(),
+        cost_estimate=pl.CostEstimate(
+            flops=2 * rows * features * width,
+            bytes_accessed=2 * (rows * features + features * width),
+            transcendentals=0,
+        ),
+        name="project",
+    )(tokens, weight)
+
+
+def cache_kernel(heads, lengths_ref, query_ref, keys_ref, values_ref, signs_ref, mixed_ref, stats_ref):
+    requests, span, size = keys_ref.shape
+    group = query_ref.shape[1] // size
+    head = pl.program_id(0)
+    matrix = hadamard_tile(size)
+    norm = 1.0 / math.sqrt(size)
+    key_sign = (2 * signs_ref[pl.ds(head, 1), :] - 1).astype(jnp.float32)
+    value_sign = (2 * signs_ref[pl.ds(heads + head, 1), :] - 1).astype(jnp.float32)
+    query = query_ref[...].astype(jnp.float32)
+    query = jnp.concatenate([query[:, g * size : (g + 1) * size] for g in range(group)], axis=0)
+    query = (query * key_sign).astype(jnp.bfloat16)
+    rotated = (jnp.dot(query, matrix, preferred_element_type=jnp.float32) * norm).astype(jnp.bfloat16)
+    keys = keys_ref[...].reshape(requests * span, size)
+    scores = lax.dot_general(rotated, keys, NT, preferred_element_type=jnp.float32) * norm
+    shape = scores.shape
+    row_request = lax.broadcasted_iota(jnp.int32, shape, 0) % requests
+    lane = lax.broadcasted_iota(jnp.int32, shape, 1)
+    position = lax.axis_index("tp") * span + lane % span
+    limit = jnp.concatenate(
+        [jnp.full((1, span), lengths_ref[0, 0, r], jnp.int32) for r in range(requests)], axis=1
+    )
+    live = (row_request == lane // span) & (position < limit)
+    top = jnp.max(jnp.where(live, scores, LOWEST), axis=1, keepdims=True)
+    probs = jnp.where(live, jnp.exp(scores - top), 0.0)
+    total = jnp.sum(probs, axis=1, keepdims=True)
+    values = values_ref[...].reshape(requests * span, size)
+    mixed = jnp.dot(probs.astype(jnp.bfloat16), values, preferred_element_type=jnp.float32)
+    high = mixed.astype(jnp.bfloat16)
+    low = (mixed - high.astype(jnp.float32)).astype(jnp.bfloat16)
+    plain = jnp.dot(high, matrix, preferred_element_type=jnp.float32)
+    plain = plain + jnp.dot(low, matrix, preferred_element_type=jnp.float32)
+    plain = plain * (value_sign * norm)
+
+    @pl.when(head == 0)
+    def _():
+        stats_ref[...] = jnp.zeros_like(stats_ref)
+
+    columns = lax.broadcasted_iota(jnp.int32, (requests, stats_ref.shape[1]), 1)
+    for g in range(group):
+        rows = slice(g * requests, (g + 1) * requests)
+        mixed_ref[:, g * size : (g + 1) * size] = plain[rows]
+        here = columns == head * group + g
+        stats_ref[:requests, :] = jnp.where(here, top[rows], stats_ref[:requests, :])
+        stats_ref[requests:, :] = jnp.where(here, total[rows], stats_ref[requests:, :])
+
+
+def cache_part(lengths, query, cache, signs):
+    requests, span, width = cache.shape
+    blocks, size = signs.shape
+    heads = blocks // 2
+    columns = query.shape[1] // heads
+    return pl.pallas_call(
+        functools.partial(cache_kernel, heads),
+        grid=(heads,),
+        in_specs=[
+            pl.BlockSpec(memory_space=pltpu.SMEM),
+            pl.BlockSpec((requests, columns), lambda k: (0, k)),
+            pl.BlockSpec((requests, span, size), lambda k: (0, 0, k)),
+            pl.BlockSpec((requests, span, size), lambda k: (0, 0, heads + k)),
+            pl.BlockSpec((blocks, size), lambda k: (0, 0)),
+        ],
+        out_specs=[
+            pl.BlockSpec((requests, columns), lambda k: (0, k)),
+            pl.BlockSpec((2 * requests, 128), lambda k: (0, 0)),
+        ],
+        out_shape=[
+            jax.ShapeDtypeStruct(query.shape, jnp.float32),
+            jax.ShapeDtypeStruct((2 * requests, 128), jnp.float32),
+        ],
+        compiler_params=params(),
+        cost_estimate=pl.CostEstimate(
+            flops=4 * requests * query.shape[1] * requests * span,
+            bytes_accessed=2 * requests * span * width,
+            transcendentals=requests * span * requests * columns // size * heads,
+        ),
+        name="cache_part",
+    )(lengths, query, cache, cache, signs)
+
+
+def code_row(message_refs, start, requests):
+    code = sum(ref[0:1, start:].astype(jnp.float32) for ref in message_refs).astype(jnp.int32)
+    me = lax.axis_index("seq")
+    return ((code // requests) ^ me) * requests + code % requests
+
+
+def score_kernel(heads, partial_ref, *refs):
+    message_refs, (scores_ref, code_ref) = refs[:-2], refs[-2:]
+    requests = message_refs[0].shape[0]
+    size = partial_ref.shape[1] // heads
+    tokens = partial_ref.shape[0]
+    start = message_refs[0].shape[1] - tokens
+    group = start // (heads * size)
+    code = code_row(message_refs, start, requests)
+    code_ref[...] = jnp.broadcast_to(code, code_ref.shape)
+    span = len(message_refs) * requests
+    here = lax.broadcasted_iota(jnp.int32, (span, tokens), 0) == code
+    queries = [ref[:, :start].astype(jnp.float32) for ref in message_refs]
+    for k in range(heads):
+        rows = []
+        for g in range(group):
+            at = (k * group + g) * size
+            rows += [query[:, at : at + size] for query in queries]
+        query = jnp.concatenate(rows, axis=0).astype(jnp.bfloat16)
+        keys = partial_ref[:, k * size : (k + 1) * size]
+        scores = lax.dot_general(query, keys, NT, preferred_element_type=jnp.float32)
+        lines = [
+            jnp.sum(jnp.where(here, scores[g * span : (g + 1) * span], 0.0), axis=0, keepdims=True)
+            for g in range(group)
+        ]
+        scores_ref[k * group : (k + 1) * group, :] = jnp.concatenate(lines, axis=0) * (
+            1.0 / math.sqrt(size)
+        )
+
+
+def partial_scores(heads, width, partials, messages):
+    tokens = partials.shape[0]
+    size = width // heads
+    query_heads = (messages[0].shape[1] - tokens) // size
+    return pl.pallas_call(
+        functools.partial(score_kernel, heads),
+        grid=(1,),
+        in_specs=[pl.BlockSpec((tokens, width), lambda i: (0, 0))]
+        + [pl.BlockSpec(m.shape, lambda i: (0, 0)) for m in messages],
+        out_specs=[
+            pl.BlockSpec((query_heads, tokens), lambda i: (0, 0)),
+            pl.BlockSpec((8, tokens), lambda i: (0, 0)),
+        ],
+        out_shape=[
+            jax.ShapeDtypeStruct((query_heads, tokens), jnp.float32),
+            jax.ShapeDtypeStruct((8, tokens), jnp.int32),
+        ],
+        compiler_params=params(),
+        name="partial_scores",
+    )(partials, *messages)
+
+
+def mix_kernel(heads, count, code_ref, values_ref, cache_stats_ref, *refs):
+    score_refs = refs[:count]
+    mixed_refs = refs[count : 2 * count]
+    new_stats_ref, stats_ref = refs[2 * count :]
+    tokens = values_ref.shape[0]
+    size = values_ref.shape[1] // heads
+    requests = stats_ref.shape[0] // 2
+    group = score_refs[0].shape[0] // heads
+    span = count * requests
+    here = lax.broadcasted_iota(jnp.int32, (span, tokens), 0) == code_ref[0:1, :]
+    parts = [ref[...] for ref in score_refs]
+    while len(parts) > 1:
+        parts = [parts[i] + parts[i + 1] for i in range(0, len(parts), 2)]
+    scores = parts[0]
+    columns = lax.broadcasted_iota(jnp.int32, (requests, stats_ref.shape[1]), 1)
+    tops = jnp.full(columns.shape, 0.0, jnp.float32)
+    totals = jnp.zeros(columns.shape, jnp.float32)
+    mixed = []
+    for k in range(heads):
+        weights = []
+        for g in range(group):
+            row = k * group + g
+            line = jnp.broadcast_to(scores[row : row + 1, :], (span, tokens))
+            top = jnp.max(jnp.where(here, line, LOWEST), axis=1, keepdims=True)
+            probs = jnp.where(here, jnp.exp(line - top), 0.0)
+            total = jnp.sum(probs, axis=1, keepdims=True)
+            weights.append(probs)
+            tops = jnp.where(columns == row, top[:requests], tops)
+            totals = jnp.where(columns == row, total[:requests], totals)
+        weights = jnp.concatenate(weights, axis=0).astype(jnp.bfloat16)
+        values = values_ref[:, k * size : (k + 1) * size]
+        mixed.append(jnp.dot(weights, values, preferred_element_type=jnp.float32))
+    half = heads // 2
+    for k in range(half):
+        for g in range(group):
+            at = (k * group + g) * size
+            for d in range(count):
+                rows = slice(g * span + d * requests, g * span + (d + 1) * requests)
+                pair = jnp.concatenate([mixed[k][rows], mixed[k + half][rows]], axis=0)
+                mixed_refs[d][:, at : at + size] = pair.astype(jnp.bfloat16)
+    new_stats_ref[:requests, :] = tops
+    new_stats_ref[requests:, :] = totals
+    cache_tops = cache_stats_ref[:requests, :]
+    both = jnp.maximum(cache_tops, tops)
+    stats_ref[:requests, :] = both
+    stats_ref[requests:, :] = cache_stats_ref[requests:, :] * jnp.exp(cache_tops - both) + totals * jnp.exp(
+        tops - both
+    )
+
+
+def mix(heads, width, code, partials, cache_stats, scores):
+    count = len(scores)
+    tokens = partials.shape[0]
+    requests = cache_stats.shape[0] // 2
+    columns = scores[0].shape[0] * (width // heads) // 2
+    whole = lambda shape: pl.BlockSpec(shape, lambda i: (0, 0))
+    return pl.pallas_call(
+        functools.partial(mix_kernel, heads, count),
+        grid=(1,),
+        in_specs=[
+            whole(code.shape),
+            pl.BlockSpec((tokens, width), lambda i: (0, 1)),
+            whole(cache_stats.shape),
+        ]
+        + [whole(s.shape) for s in scores],
+        out_specs=[whole((2 * requests, columns))] * count + [whole(cache_stats.shape)] * 2,
+        out_shape=[jax.ShapeDtypeStruct((2 * requests, columns), jnp.bfloat16)] * count
+        + [jax.ShapeDtypeStruct(cache_stats.shape, jnp.float32)] * 2,
+        compiler_params=params(),
+        name="mix",
+    )(code, partials, cache_stats, *scores)
+
+
+def merge_kernel(count, size, cache_ref, cache_stats_ref, new_stats_ref, stats_ref, other_ref, *refs):
+    mixed_refs, out_ref = refs[:count], refs[count]
+    requests = cache_ref.shape[0]
+    half = out_ref.shape[1] // 2
+    top = stats_ref[:requests, :]
+    other_top = other_ref[:requests, :]
+    both = jnp.maximum(top, other_top)
+    total = stats_ref[requests:, :] * jnp.exp(top - both) + other_ref[requests:, :] * jnp.exp(
+        other_top - both
+    )
+    inverse = 1.0 / total
+    cache_factor = jnp.exp(cache_stats_ref[:requests, :] - both) * inverse
+    new_factor = jnp.exp(new_stats_ref[:requests, :] - both) * inverse
+    for at in range(0, half, size):
+        new = sum(ref[:, at : at + size].astype(jnp.float32) for ref in mixed_refs)
+        pair = []
+        for side in range(2):
+            head = (side * half + at) // size
+            column = slice(side * half + at, side * half + at + size)
+            pair.append(
+                cache_ref[:, column] * cache_factor[:, head : head + 1]
+                + new[side * requests : (side + 1) * requests] * new_factor[:, head : head + 1]
+            )
+        out_ref[:, at : at + size] = pair[0].astype(out_ref.dtype)
+        out_ref[:, half + at : half + at + size] = pair[1].astype(out_ref.dtype)
+
+
+def merge(size, cache_mixed, cache_stats, new_stats, stats, other, mixed):
+    whole = lambda shape: pl.BlockSpec(shape, lambda i: (0, 0))
+    inputs = [cache_mixed, cache_stats, new_stats, stats, other] + list(mixed)
+    return pl.pallas_call(
+        functools.partial(merge_kernel, len(mixed), size),
+        grid=(1,),
+        in_specs=[whole(x.shape) for x in inputs],
+        out_specs=whole(cache_mixed.shape),
+        out_shape=jax.ShapeDtypeStruct(cache_mixed.shape, jnp.bfloat16),
+        compiler_params=params(),
+        name="merge",
+    )(*inputs)
+
+
+def from_partner(x, axis, distance):
+    count = lax.axis_size(axis)
+    return lax.ppermute(x, axis, [(i, i ^ distance) for i in range(count)])
+
+
+def on_device(tokens, kv_weight, owners, requests, signs, queries, kv_cache, lengths):
+    seq_count = lax.axis_size("seq")
+    blocks, size = signs.shape
+    heads = blocks // 2
+    width = heads * size
+    query = queries[0, 0]
+    request_count, columns = query.shape
+    per_device = owners.shape[1]
+    token_count = tokens.shape[0]
+    code = owners[0, :, 0] * request_count + requests[0]
+    spread = jnp.where(
+        lax.iota(jnp.int32, token_count) // per_device == lax.axis_index("seq"),
+        jnp.tile(code, seq_count),
+        0,
+    ).astype(jnp.bfloat16)
+    message = jnp.concatenate(
+        [query, jnp.broadcast_to(spread[None], (request_count, token_count))], axis=1
+    )
+    messages = [message] + [from_partner(message, "seq", d) for d in range(1, seq_count)]
+    partials = project(tokens, kv_weight)
+    cache_mixed, cache_stats = cache_part(lengths, query, kv_cache[0, 0], signs)
+    scores, relative = partial_scores(heads, width, partials, messages)
+    scores = [scores] + [from_partner(scores, "seq", d) for d in range(1, seq_count)]
+    results = mix(heads, width, relative, partials, cache_stats, scores)
+    mixed, (new_stats, stats) = results[:seq_count], results[seq_count:]
+    other = from_partner(stats, "tp", 1)
+    mixed = [mixed[0]] + [from_partner(mixed[d], "seq", d) for d in range(1, seq_count)]
+    own = merge(size, cache_mixed, cache_stats, new_stats, stats, other, mixed)
+    far = from_partner(own, "tp", 1)
+    output = (own.astype(jnp.float32) + far.astype(jnp.float32)).astype(jnp.bfloat16)
+    return output.reshape(1, 1, request_count, columns)
 
 
 def hadamard(order):
@@ -41,7 +391,7 @@
     return targets * room + within
 
 
-def on_device(tokens, kv_weight, owners, requests, signs, queries, kv_cache, lengths):
+def on_device_long(tokens, kv_weight, owners, requests, signs, queries, kv_cache, lengths):
     seq_count = lax.axis_size("seq")
     per_device = owners.shape[1]
     slots = max(2, (2 * per_device + seq_count - 1) // seq_count)
@@ -140,8 +490,9 @@
         P(("groups", "seq"), "section", None, "tp", None),
         P(("groups", "seq"), "section", None),
     )
+    short = mesh.shape["seq"] == 4 and mesh.shape["tp"] == 2
     return jax.shard_map(
-        on_device,
+        on_device if short else on_device_long,
         mesh=mesh,
         in_specs=placed,
         out_specs=P(("groups", "seq"), "section", None, None),

time: 116 us -> 42.5 us (0.37)
  waiting for transfers between devices: 36.9 us -> 7.25 us
  matrix products: 15.4 us -> 0 us
  between operations: 13.6 us -> 0.11 us
  local copies, waits for them, and re-layouts: 14.9 us -> 1.71 us
  Pallas kernels: 0 us -> 13.1 us
  blocking collectives: 13 us -> 0 us
  other arithmetic: 6.39 us -> 2.23 us
  starting transfers between devices: 14.6 us -> 17.8 us
    reduce_scatter x1 -> x0, waiting for transfers between devices: 18.4 us -> none  [on_device(): lax.psum_scatter(jnp.dot(tokens, kv_weight, preferred_element_type=jnp.fl...]
    ppermute x0 -> x11, starting transfers between devices: none -> 17.8 us  [from_partner(): return lax.ppermute(x, axis, [(i, i ^ distance) for i in range(count)])]
    dot_general x8 -> x0, matrix products: 15.4 us -> none  [the longest x1 6.54 us: on_device(): jnp.dot(tokens, kv_weight, preferred_element_type=jnp.float32)]
    psum x1 -> x0, waiting for transfers between devices: 14.8 us -> none  [on_device(): lax.psum((mixed * factor[..., None]).astype(jnp.bfloat16), 'tp')]
    all_to_all x3 -> x0, starting transfers between devices: 14.6 us -> none  [the longest x1 6.32 us: on_device(): lax.all_to_all(send_codes, 'seq', split_axis=0, concat_axis=0, tiled=True)]
    pallas_call x0 -> x5, Pallas kernels: none -> 13.1 us  [the longest x1 8.12 us: project(): pl.pallas_call(project_kernel, grid=(features // block,), in_specs=[pl.Bl...]
    pmax x1 -> x0, blocking collectives: 8.02 us -> none  [on_device(): shared_top = lax.pmax(top, 'tp')]
    scatter x2 -> x0, local copies, waits for them, and re-layouts: 7.33 us -> none  [the longest x1 6.56 us: on_device(): jnp.zeros((slot_total, head_blocks, head_size), jnp.bfloat16).at[slot_index]]
  transfers between devices with their start and end apart: 5 -> 11, of which waited for: 3 -> 4; matrix products, arithmetic and copies ran while one was open for 22% -> 0% of each run, Pallas kernels for 0% -> 29%
where the time goes in v1:
time: 42.5 us; the launch traced here: 42.2 us
  starting transfers between devices  17.8 us (42%)
  Pallas kernels  13.1 us (31%)
  waiting for transfers between devices  7.25 us (17%)
  other arithmetic  2.23 us (5%)
  local copies, waits for them, and re-layouts  1.71 us (4%)
    ppermute x11, starting transfers between devices, from_partner(): return lax.ppermute(x, axis, [(i, i ^ distance) for i in range(count)])  17.8 us
    pallas_call x1, Pallas kernels, project(): pl.pallas_call(project_kernel, grid=(features // block,), in_specs=[pl.Bl...  8.12 us
    ppermute x11, waiting for transfers between devices, from_partner(): return lax.ppermute(x, axis, [(i, i ^ distance) for i in range(count)])  7.25 us
    pallas_call x1, Pallas kernels, cache_part(): pl.pallas_call(functools.partial(cache_kernel, heads), grid=(heads,), in_...  4.07 us
    unnamed x10, local copies, waits for them, and re-layouts  1.61 us
    concatenate x1, other arithmetic, on_device(): jnp.concatenate([query, jnp.broadcast_to(spread[None], (request_count, to...  0.9 us
  transfers between devices with their start and end apart: 11, of which 4 were waited for; matrix products, arithmetic and copies ran while one was open for 0% of the time, Pallas kernels for 29%

profile of v1, /device:TPU:0, one launch (start us, length us, event | category | flops | bytes accessed | tf_op | source)
XLA Modules:
  0.0 42.2 jit_solution(16843550640112974797)
XLA Ops:
  0.0 0.7 %fusion.2 = s32[64]{0:T(128)S(1)} fusion(s32[1,64]{1,0:T(1,128)} %param.11, s32[1,64,1]{1,2,0:T(1,128)} %param.10), kind=kLoop, calls=%fused_computation.10 | loop fusion | flops 128 | bytes 768 | tf_op jit(solution)/shard_map/tile | solution.py:338
  0.7 0.1 tile.13
  0.8 0.0 copy-start.3
  0.8 0.9 %pad_maximum_fusion.refs_0_ = bf16[8,4352]{1,0:T(8,128)(2,1)S(1)} fusion(bf16[8,4096]{1,0:T(8,128)(2,1)} %bitcast.12, bf16[4352]{0:T(1024)(128)(2,1)S(1)} %pad.1.clone), kind=kLoop, calls=%fused_computation.1 | loop fusion | flops 139264 | bytes 143872 | tf_op jit(solution)/shard_map/concatenate | solution.py:341
  1.7 5.1 %collective-permute-start.2 = (bf16[8,4352]{1,0:T(8,128)(2,1)S(1)}, bf16[8,4352]{1,0:T(8,128)(2,1)S(1)}, u32[]{:S(2)}, u32[]{:S(2)}) collective-permute-start(bf16[8,4352]{1,0:T(8,128)(2,1)S(1)} %pad_maximum_fusion.refs_0_), channel_id=1, source_target_pairs={{0,12},{4,8},{8,4},{12,0},{1,13},{5,9},{9,5},{13,1},{2,14},{6,10},... | collective-permute-start | bytes 208904 | tf_op jit(solution)/shard_map/ppermute | solution.py:323
  6.8 0.6 %collective-permute-start = (bf16[8,4352]{1,0:T(8,128)(2,1)S(1)}, bf16[8,4352]{1,0:T(8,128)(2,1)S(1)}, u32[]{:S(2)}, u32[]{:S(2)}) collective-permute-start(bf16[8,4352]{1,0:T(8,128)(2,1)S(1)} %pad_maximum_fusion.refs_0_), channel_id=1, source_target_pairs={{0,4},{4,0},{8,12},{12,8},{1,5},{5,1},{9,13},{13,9},{2,6},{6,2},{1... | collective-permute-start | bytes 208904 | tf_op jit(solution)/shard_map/ppermute | solution.py:323
  7.5 1.6 %copy-done.1 = bf16[256,4096]{1,0:T(8,128)(2,1)S(1)} copy-done((bf16[256,4096]{1,0:T(8,128)(2,1)S(1)}, bf16[256,4096]{1,0:T(8,128)(2,1)}, u32[]{:S(2)}) %copy-start.1) | copy-done | bytes 2097176
  9.1 8.1 %project.1.partial_ref.values_ref = bf16[256,1024]{1,0:T(8,128)(2,1)S(1)} custom-call(bf16[256,4096]{1,0:T(8,128)(2,1)S(1)} %copy-done.1, bf16[4096,1024]{1,0:T(8,128)(2,1)} %weight_ref.1), custom_call_target="tpu_custom_call" | custom-call | flops 2147483648 | bytes 10485760 | tf_op jit(solution)/shard_map/project/pallas_call | solution.py:51
  17.2 0.3 partial_scores.1
  17.6 3.8 %collective-permute-start.5 = (f32[32,256]{1,0:T(8,128)S(1)}, f32[32,256]{1,0:T(8,128)S(1)}, u32[]{:S(2)}, u32[]{:S(2)}) collective-permute-start(f32[32,256]{1,0:T(8,128)S(1)} %get-tuple-element.18.refs_0_), channel_id=1, source_target_pairs={{0,12},{4,8},{8,4},{12,0},{1,13},{5,9},{9,5},{13,1},{2,14},{6,10},... | collective-permute-start | bytes 98312 | tf_op jit(solution)/shard_map/ppermute | solution.py:323
  21.4 0.6 %collective-permute-start.3 = (f32[32,256]{1,0:T(8,128)S(1)}, f32[32,256]{1,0:T(8,128)S(1)}, u32[]{:S(2)}, u32[]{:S(2)}) collective-permute-start(f32[32,256]{1,0:T(8,128)S(1)} %get-tuple-element.18.refs_0_), channel_id=1, source_target_pairs={{0,4},{4,0},{8,12},{12,8},{1,5},{5,1},{9,13},{13,9},{2,6},{6,2},{1... | collective-permute-start | bytes 98312 | tf_op jit(solution)/shard_map/ppermute | solution.py:323
  22.0 4.1 %cache_part.1 = (f32[8,4096]{1,0:T(8,128)S(1)}, f32[16,128]{1,0:T(8,128)S(1)}) custom-call(s32[1,1,8]{2,1,0:T(1,128)S(1)} %copy-done.4, bf16[8,4096]{1,0:T(8,128)(2,1)S(1)} %bitcast.13, bf16[8,128,1024]{2,1,0:T(8,128)(2,1)S(1)} %bitcast.10, bf16[8,128,1024]{2,1,0:T(8,128)(2,1)S(1)} %bitcast.11, s32[8,128]{1,0:T(8,128)S(1)} %copy-done.3), custom_call_target="tpu_custom_call" | custom-call | flops 134217728 | bytes 2097152 | tf_op jit(solution)/shard_map/cache_part/pallas_call | solution.py:122
  26.1 0.1 collective-permute-done.4.refs_2_
  26.2 0.4 mix.1
  26.6 1.4 %collective-permute-start.7 = (bf16[16,2048]{1,0:T(8,128)(2,1)S(1)}, bf16[16,2048]{1,0:T(8,128)(2,1)S(1)}, u32[]{:S(2)}, u32[]{:S(2)}) collective-permute-start(bf16[16,2048]{1,0:T(8,128)(2,1)S(1)} %get-tuple-element.22), channel_id=1, source_target_pairs={{0,4},{4,0},{8,12},{12,8},{1,5},{5,1},{9,13},{13,9},{2,6},{6,2},{1... | collective-permute-start | bytes 196616 | tf_op jit(solution)/shard_map/ppermute | solution.py:323
  28.0 2.9 %collective-permute-start.8 = (bf16[16,2048]{1,0:T(8,128)(2,1)S(1)}, bf16[16,2048]{1,0:T(8,128)(2,1)S(1)}, u32[]{:S(2)}, u32[]{:S(2)}) collective-permute-start(bf16[16,2048]{1,0:T(8,128)(2,1)S(1)} %get-tuple-element.23), channel_id=1, source_target_pairs={{0,8},{4,12},{8,0},{12,4},{1,9},{5,13},{9,1},{13,5},{2,10},{6,14},... | collective-permute-start | bytes 196616 | tf_op jit(solution)/shard_map/ppermute | solution.py:323
  30.9 0.1 collective-permute-start.9
  31.1 1.6 %collective-permute-start.6 = (f32[16,128]{1,0:T(8,128)S(1)}, f32[16,128]{1,0:T(8,128)S(1)}, u32[]{:S(2)}, u32[]{:S(2)}) collective-permute-start(f32[16,128]{1,0:T(8,128)S(1)} %get-tuple-element.20.stats_ref), channel_id=1, source_target_pairs={{0,2},{2,0},{1,3},{3,1},{4,6},{6,4},{5,7},{7,5},{8,10},{10,8},{9,1... | collective-permute-start | bytes 24584 | tf_op jit(solution)/shard_map/ppermute | solution.py:323
  32.6 2.1 %collective-permute-done.6.other_ref = f32[16,128]{1,0:T(8,128)S(1)} collective-permute-done((f32[16,128]{1,0:T(8,128)S(1)}, f32[16,128]{1,0:T(8,128)S(1)}, u32[]{:S(2)}, u32[]{:S(2)}) %collective-permute-start.6) | collective-permute-done | bytes 8224 | tf_op jit(solution)/shard_map/ppermute | solution.py:323
  34.7 2.3 %collective-permute-done.9.refs_3_ = bf16[16,2048]{1,0:T(8,128)(2,1)S(1)} collective-permute-done((bf16[16,2048]{1,0:T(8,128)(2,1)S(1)}, bf16[16,2048]{1,0:T(8,128)(2,1)S(1)}, u32[]{:S(2)}, u32[]{:S(2)}) %collective-permute-start.9) | collective-permute-done | bytes 65568 | tf_op jit(solution)/shard_map/ppermute | solution.py:323
  37.0 0.2 merge.1
  37.2 1.5 %collective-permute-start.10 = (bf16[8,4096]{1,0:T(8,128)(2,1)S(1)}, bf16[8,4096]{1,0:T(8,128)(2,1)S(1)}, u32[]{:S(2)}, u32[]{:S(2)}) collective-permute-start(bf16[8,4096]{1,0:T(8,128)(2,1)S(1)} %merge.1), channel_id=1, source_target_pairs={{0,2},{2,0},{1,3},{3,1},{4,6},{6,4},{5,7},{7,5},{8,10},{10,8},{9,1... | collective-permute-start | bytes 196616 | tf_op jit(solution)/shard_map/ppermute | solution.py:323
  38.7 2.8 %collective-permute-done.10 = bf16[8,4096]{1,0:T(8,128)(2,1)S(1)} collective-permute-done((bf16[8,4096]{1,0:T(8,128)(2,1)S(1)}, bf16[8,4096]{1,0:T(8,128)(2,1)S(1)}, u32[]{:S(2)}, u32[]{:S(2)}) %collective-permute-start.10) | collective-permute-done | bytes 65568 | tf_op jit(solution)/shard_map/ppermute | solution.py:323
  41.5 0.6 %fusion = bf16[1,1,8,4096]{3,2,1,0:T(8,128)(2,1)} fusion(bf16[8,4096]{1,0:T(8,128)(2,1)S(1)} %collective-permute-done.10, bf16[8,4096]{1,0:T(8,128)(2,1)S(1)} %merge.1), kind=kLoop, calls=%fused_computation.2 | loop fusion | flops 131072 | bytes 196608 | tf_op jit(solution)/shard_map/reshape | solution.py:356
  (20 shorter events, 0.1 us)
Async XLA Ops:
  0.8 21.2 %copy-start.2 = (bf16[1,1,8,4096]{3,2,1,0:T(8,128)(2,1)S(1)}, bf16[1,1,8,4096]{3,2,1,0:T(8,128)(2,1)}, u32[]{:S(2)}) copy-start(bf16[1,1,8,4096]{3,2,1,0:T(8,128)(2,1)} %param.13) | copy-start | bytes 196612
  0.8 21.2 %copy-start.3 = (s32[8,128]{1,0:T(8,128)S(1)}, s32[8,128]{1,0:T(8,128)}, u32[]{:S(2)}) copy-start(s32[8,128]{1,0:T(8,128)} %signs_ref.1) | copy-start | bytes 12292
  0.8 21.2 %copy-start.4 = (s32[1,1,8]{2,1,0:T(1,128)S(1)}, s32[1,1,8]{2,1,0:T(1,128)}, u32[]{:S(2)}) copy-start(s32[1,1,8]{2,1,0:T(1,128)} %lengths_ref.1) | copy-start | bytes 100
  1.7 15.5 %collective-permute-start.2 = (bf16[8,4352]{1,0:T(8,128)(2,1)S(1)}, bf16[8,4352]{1,0:T(8,128)(2,1)S(1)}, u32[]{:S(2)}, u32[]{:S(2)}) collective-permute-start(bf16[8,4352]{1,0:T(8,128)(2,1)S(1)} %pad_maximum_fusion.refs_0_), channel_id=1, source_target_pairs={{0,12},{4,8},{8,4},{12,0},{1,13},{5,9},{9,5},{13,1},{2,14},{6,10},... | collective-permute-start | bytes 208904 | tf_op jit(solution)/shard_map/ppermute | solution.py:323
  6.8 10.4 %collective-permute-start.1 = (bf16[8,4352]{1,0:T(8,128)(2,1)S(1)}, bf16[8,4352]{1,0:T(8,128)(2,1)S(1)}, u32[]{:S(2)}, u32[]{:S(2)}) collective-permute-start(bf16[8,4352]{1,0:T(8,128)(2,1)S(1)} %pad_maximum_fusion.refs_0_), channel_id=1, source_target_pairs={{0,8},{4,12},{8,0},{12,4},{1,9},{5,13},{9,1},{13,5},{2,10},{6,14},... | collective-permute-start | bytes 208904 | tf_op jit(solution)/shard_map/ppermute | solution.py:323
  6.8 10.4 %collective-permute-start = (bf16[8,4352]{1,0:T(8,128)(2,1)S(1)}, bf16[8,4352]{1,0:T(8,128)(2,1)S(1)}, u32[]{:S(2)}, u32[]{:S(2)}) collective-permute-start(bf16[8,4352]{1,0:T(8,128)(2,1)S(1)} %pad_maximum_fusion.refs_0_), channel_id=1, source_target_pairs={{0,4},{4,0},{8,12},{12,8},{1,5},{5,1},{9,13},{13,9},{2,6},{6,2},{1... | collective-permute-start | bytes 208904 | tf_op jit(solution)/shard_map/ppermute | solution.py:323
  7.5 1.6 %copy-start.1 = (bf16[256,4096]{1,0:T(8,128)(2,1)S(1)}, bf16[256,4096]{1,0:T(8,128)(2,1)}, u32[]{:S(2)}) copy-start(bf16[256,4096]{1,0:T(8,128)(2,1)} %tokens_ref.1) | copy-start | bytes 6291460
  9.1 13.0 %copy-start = (bf16[1,1,8,128,1024]{4,3,2,1,0:T(8,128)(2,1)S(1)}, bf16[1,1,8,128,1024]{4,3,2,1,0:T(8,128)(2,1)}, u32[]{:S(2)}) copy-start(bf16[1,1,8,128,1024]{4,3,2,1,0:T(8,128)(2,1)} %param.14) | copy-start | bytes 6291460
  17.6 8.6 %collective-permute-start.5 = (f32[32,256]{1,0:T(8,128)S(1)}, f32[32,256]{1,0:T(8,128)S(1)}, u32[]{:S(2)}, u32[]{:S(2)}) collective-permute-start(f32[32,256]{1,0:T(8,128)S(1)} %get-tuple-element.18.refs_0_), channel_id=1, source_target_pairs={{0,12},{4,8},{8,4},{12,0},{1,13},{5,9},{9,5},{13,1},{2,14},{6,10},... | collective-permute-start | bytes 98312 | tf_op jit(solution)/shard_map/ppermute | solution.py:323
  21.4 4.8 %collective-permute-start.4 = (f32[32,256]{1,0:T(8,128)S(1)}, f32[32,256]{1,0:T(8,128)S(1)}, u32[]{:S(2)}, u32[]{:S(2)}) collective-permute-start(f32[32,256]{1,0:T(8,128)S(1)} %get-tuple-element.18.refs_0_), channel_id=1, source_target_pairs={{0,8},{4,12},{8,0},{12,4},{1,9},{5,13},{9,1},{13,5},{2,10},{6,14},... | collective-permute-start | bytes 98312 | tf_op jit(solution)/shard_map/ppermute | solution.py:323
  21.4 4.8 %collective-permute-start.3 = (f32[32,256]{1,0:T(8,128)S(1)}, f32[32,256]{1,0:T(8,128)S(1)}, u32[]{:S(2)}, u32[]{:S(2)}) collective-permute-start(f32[32,256]{1,0:T(8,128)S(1)} %get-tuple-element.18.refs_0_), channel_id=1, source_target_pairs={{0,4},{4,0},{8,12},{12,8},{1,5},{5,1},{9,13},{13,9},{2,6},{6,2},{1... | collective-permute-start | bytes 98312 | tf_op jit(solution)/shard_map/ppermute | solution.py:323
  26.6 8.1 %collective-permute-start.7 = (bf16[16,2048]{1,0:T(8,128)(2,1)S(1)}, bf16[16,2048]{1,0:T(8,128)(2,1)S(1)}, u32[]{:S(2)}, u32[]{:S(2)}) collective-permute-start(bf16[16,2048]{1,0:T(8,128)(2,1)S(1)} %get-tuple-element.22), channel_id=1, source_target_pairs={{0,4},{4,0},{8,12},{12,8},{1,5},{5,1},{9,13},{13,9},{2,6},{6,2},{1... | collective-permute-start | bytes 196616 | tf_op jit(solution)/shard_map/ppermute | solution.py:323
  28.0 6.7 %collective-permute-start.8 = (bf16[16,2048]{1,0:T(8,128)(2,1)S(1)}, bf16[16,2048]{1,0:T(8,128)(2,1)S(1)}, u32[]{:S(2)}, u32[]{:S(2)}) collective-permute-start(bf16[16,2048]{1,0:T(8,128)(2,1)S(1)} %get-tuple-element.23), channel_id=1, source_target_pairs={{0,8},{4,12},{8,0},{12,4},{1,9},{5,13},{9,1},{13,5},{2,10},{6,14},... | collective-permute-start | bytes 196616 | tf_op jit(solution)/shard_map/ppermute | solution.py:323
  30.9 6.1 %collective-permute-start.9 = (bf16[16,2048]{1,0:T(8,128)(2,1)S(1)}, bf16[16,2048]{1,0:T(8,128)(2,1)S(1)}, u32[]{:S(2)}, u32[]{:S(2)}) collective-permute-start(bf16[16,2048]{1,0:T(8,128)(2,1)S(1)} %get-tuple-element.24), channel_id=1, source_target_pairs={{0,12},{4,8},{8,4},{12,0},{1,13},{5,9},{9,5},{13,1},{2,14},{6,10},... | collective-permute-start | bytes 196616 | tf_op jit(solution)/shard_map/ppermute | solution.py:323
  31.1 3.7 %collective-permute-start.6 = (f32[16,128]{1,0:T(8,128)S(1)}, f32[16,128]{1,0:T(8,128)S(1)}, u32[]{:S(2)}, u32[]{:S(2)}) collective-permute-start(f32[16,128]{1,0:T(8,128)S(1)} %get-tuple-element.20.stats_ref), channel_id=1, source_target_pairs={{0,2},{2,0},{1,3},{3,1},{4,6},{6,4},{5,7},{7,5},{8,10},{10,8},{9,1... | collective-permute-start | bytes 24584 | tf_op jit(solution)/shard_map/ppermute | solution.py:323
  37.2 4.3 %collective-permute-start.10 = (bf16[8,4096]{1,0:T(8,128)(2,1)S(1)}, bf16[8,4096]{1,0:T(8,128)(2,1)S(1)}, u32[]{:S(2)}, u32[]{:S(2)}) collective-permute-start(bf16[8,4096]{1,0:T(8,128)(2,1)S(1)} %merge.1), channel_id=1, source_target_pairs={{0,2},{2,0},{1,3},{3,1},{4,6},{6,4},{5,7},{7,5},{8,10},{10,8},{9,1... | collective-permute-start | bytes 196616 | tf_op jit(solution)/shard_map/ppermute | solution.py:323

commit v2 on v0

--- a/solution.py
+++ b/solution.py
@@ -1,9 +1,407 @@
+import functools
 import math
 
 import jax
 import jax.numpy as jnp
 from jax import lax
+from jax.experimental import pallas as pl
+from jax.experimental.pallas import tpu as pltpu
 from jax.sharding import PartitionSpec as P
+
+LOWEST = -1e30
+MIB = 1024 * 1024
+NT = (((1,), (1,)), ((), ()))
+
+
+def params(mib=32):
+    return pltpu.CompilerParams(vmem_limit_bytes=mib * MIB)
+
+
+def in_hbm(x):
+    return pltpu.with_memory_space_constraint(x, pltpu.HBM)
+
+
+def hadamard_tile(order):
+    rows = lax.broadcasted_iota(jnp.int32, (order, order), 0)
+    cols = lax.broadcasted_iota(jnp.int32, (order, order), 1)
+    common = rows & cols
+    parity = jnp.zeros((order, order), jnp.int32)
+    for bit_number in range(order.bit_length() - 1):
+        parity = parity ^ (common >> bit_number)
+    return (1 - 2 * (parity & 1)).astype(jnp.float32).astype(jnp.bfloat16)
+
+
+def project_kernel(tokens_ref, weight_ref, out_ref, tokens_buf, weight_buf, acc_ref, sems):
+    steps, block, width = weight_buf.shape
+    copies = []
+    for step in range(steps):
+        span = slice(step * block, (step + 1) * block)
+        pair = (
+            pltpu.make_async_copy(tokens_ref.at[:, span], tokens_buf.at[step], sems.at[0, step]),
+            pltpu.make_async_copy(weight_ref.at[span, :], weight_buf.at[step], sems.at[1, step]),
+        )
+        for copy in pair:
+            copy.start()
+        copies.append(pair)
+    for step in range(steps):
+        for copy in copies[step]:
+            copy.wait()
+        part = jnp.dot(tokens_buf[step], weight_buf[step], preferred_element_type=jnp.float32)
+        if step == 0:
+            acc_ref[...] = part
+        elif step < steps - 1:
+            acc_ref[...] += part
+        else:
+            out_ref[...] = (acc_ref[...] + part).astype(out_ref.dtype)
+
+
+def project(tokens, weight):
+    rows, features = tokens.shape
+    width = weight.shape[1]
+    block = min(512, features // 2)
+    steps = features // block
+    return pl.pallas_call(
+        project_kernel,
+        in_specs=[pl.BlockSpec(memory_space=pl.ANY)] * 2,
+        out_specs=pl.BlockSpec(memory_space=pltpu.VMEM),
+        out_shape=jax.ShapeDtypeStruct((rows, width), jnp.bfloat16),
+        scratch_shapes=[
+            pltpu.VMEM((steps, rows, block), jnp.bfloat16),
+            pltpu.VMEM((steps, block, width), jnp.bfloat16),
+            pltpu.VMEM((rows, width), jnp.float32),
+            pltpu.SemaphoreType.DMA((2, steps)),
+        ],
+        compiler_params=params(48),
+        cost_estimate=pl.CostEstimate(
+            flops=2 * rows * features * width,
+            bytes_accessed=2 * (rows * features + features * width),
+            transcendentals=0,
+        ),
+        name="project",
+    )(in_hbm(tokens), in_hbm(weight))
+
+
+def message_kernel(query_ref, owners_ref, requests_ref, out_ref, query_buf, owners_buf, requests_buf, sems):
+    requests, columns = query_ref.shape
+    per_device = owners_ref.shape[1]
+    tokens = out_ref.shape[1] - columns
+    copies = [
+        pltpu.make_async_copy(source, target, sems.at[i])
+        for i, (source, target) in enumerate(
+            ((query_ref, query_buf), (owners_ref, owners_buf), (requests_ref, requests_buf))
+        )
+    ]
+    for copy in copies:
+        copy.start()
+    for copy in copies:
+        copy.wait()
+    out_ref[:, :columns] = query_buf[...]
+    code = (owners_buf[...] * requests + requests_buf[...]).astype(jnp.float32)
+    spread = jnp.concatenate([code] * (tokens // per_device), axis=1)
+    spread = jnp.broadcast_to(spread, (requests, tokens))
+    start = lax.axis_index("seq") * per_device
+    lane = lax.broadcasted_iota(jnp.int32, spread.shape, 1)
+    mine = (lane >= start) & (lane < start + per_device)
+    out_ref[:, columns:] = jnp.where(mine, spread, 0.0).astype(out_ref.dtype)
+
+
+def make_message(query, owners, requests, tokens):
+    count, columns = query.shape
+    return pl.pallas_call(
+        message_kernel,
+        in_specs=[pl.BlockSpec(memory_space=pl.ANY)] * 3,
+        out_specs=pl.BlockSpec(memory_space=pltpu.VMEM),
+        out_shape=jax.ShapeDtypeStruct((count, columns + tokens), query.dtype),
+        scratch_shapes=[
+            pltpu.VMEM(query.shape, query.dtype),
+            pltpu.VMEM(owners.shape, owners.dtype),
+            pltpu.VMEM(requests.shape, requests.dtype),
+            pltpu.SemaphoreType.DMA((3,)),
+        ],
+        compiler_params=params(48),
+        name="make_message",
+    )(in_hbm(query), in_hbm(owners), in_hbm(requests))
+
+
+def cache_kernel(
+    lengths_ref, query_ref, cache_ref, signs_ref, tops_ref, totals_ref, mixed_ref, stats_ref, factor_ref, order_ref
+):
+    requests, span, _ = cache_ref.shape
+    blocks, size = signs_ref.shape
+    heads = blocks // 2
+    count = query_ref.shape[1] // size
+    group = count // heads
+    norm = 1.0 / math.sqrt(size)
+    matrix = hadamard_tile(size)
+    signs = (2 * signs_ref[...] - 1).astype(jnp.float32)
+    query = query_ref[...].astype(jnp.float32)
+    query = jnp.concatenate(
+        [query[:, h * size : (h + 1) * size] * signs[h // group : h // group + 1] for h in range(count)], axis=0
+    )
+    rotated = jnp.dot(query.astype(jnp.bfloat16), matrix, preferred_element_type=jnp.float32) * norm
+    order_ref[0] = rotated
+    position = lax.axis_index("tp") * span + lax.broadcasted_iota(jnp.int32, (group, span), 1)
+    mixed = []
+    for r in range(requests):
+        rows = order_ref[0, pl.ds(r, count, stride=requests), :]
+        live = position < lengths_ref[0, 0, r]
+        for k in range(heads):
+            keys = cache_ref[r, :, k * size : (k + 1) * size]
+            values = cache_ref[r, :, (heads + k) * size : (heads + k + 1) * size]
+            here = rows[k * group : (k + 1) * group].astype(jnp.bfloat16)
+            scores = lax.dot_general(here, keys, NT, preferred_element_type=jnp.float32) * norm
+            top = jnp.max(jnp.where(live, scores, LOWEST), axis=1, keepdims=True)
+            probs = jnp.where(live, jnp.exp(scores - top), 0.0)
+            total = jnp.sum(probs, axis=1, keepdims=True)
+            mixed.append(jnp.dot(probs.astype(jnp.bfloat16), values, preferred_element_type=jnp.float32))
+            at = slice(r * count + k * group, r * count + (k + 1) * group)
+            order_ref[1, at, :] = jnp.broadcast_to(top, (group, size))
+            order_ref[2, at, :] = jnp.broadcast_to(total, (group, size))
+    mixed = jnp.concatenate(mixed, axis=0)
+    high = mixed.astype(jnp.bfloat16)
+    low = (mixed - high.astype(jnp.float32)).astype(jnp.bfloat16)
+    plain = jnp.dot(high, matrix, preferred_element_type=jnp.float32)
+    order_ref[3] = plain + jnp.dot(low, matrix, preferred_element_type=jnp.float32)
+    lane = lax.broadcasted_iota(jnp.int32, stats_ref.shape, 1)
+    stats = jnp.zeros(stats_ref.shape, jnp.float32)
+    for h in range(count):
+        pick = pl.ds(h, requests, stride=count)
+        k = heads + h // group
+        top = order_ref[1, pick, :]
+        column = slice(h * size, (h + 1) * size)
+        new_top = tops_ref[:, column]
+        both = jnp.maximum(top, new_top)
+        cache_factor = jnp.exp(top - both)
+        new_factor = jnp.exp(new_top - both)
+        total = order_ref[2, pick, :] * cache_factor + totals_ref[:, column] * new_factor
+        factor_ref[:, column] = new_factor
+        mixed_ref[:, column] = order_ref[3, pick, :] * (cache_factor * (signs[k : k + 1] * norm))
+        for start, value in ((0, both), (3 * count, total)):
+            for part in range(3):
+                piece = value.astype(jnp.bfloat16).astype(jnp.float32)
+                value = value - piece
+                stats = jnp.where(lane == start + part * count + h, jnp.tile(piece, (1, 2)), stats)
+    stats_ref[...] = stats.astype(jnp.bfloat16)
+
+
+def cache_part(lengths, query, cache, signs, tops, totals):
+    requests, span, width = cache.shape
+    size = signs.shape[1]
+    columns = query.shape[1]
+    vmem = pl.BlockSpec(memory_space=pltpu.VMEM)
+    return pl.pallas_call(
+        cache_kernel,
+        in_specs=[pl.BlockSpec(memory_space=pltpu.SMEM)] + [vmem] * 5,
+        out_shape=[
+            jax.ShapeDtypeStruct(query.shape, jnp.float32),
+            jax.ShapeDtypeStruct((requests, 2 * size), jnp.bfloat16),
+            jax.ShapeDtypeStruct(query.shape, jnp.float32),
+        ],
+        scratch_shapes=[pltpu.VMEM((4, requests * columns // size, size), jnp.float32)],
+        compiler_params=params(),
+        cost_estimate=pl.CostEstimate(
+            flops=4 * span * requests * columns,
+            bytes_accessed=2 * requests * span * width,
+            transcendentals=span * requests * columns // size,
+        ),
+        name="cache_part",
+    )(lengths, query, cache, signs, tops, totals)
+
+
+def code_row(message_refs, start, requests):
+    code = sum(ref[0:1, start:].astype(jnp.float32) for ref in message_refs).astype(jnp.int32)
+    me = lax.axis_index("seq")
+    return ((code // requests) ^ me) * requests + code % requests
+
+
+def score_kernel(heads, partial_ref, *refs):
+    message_refs, (scores_ref, code_ref) = refs[:-2], refs[-2:]
+    requests = message_refs[0].shape[0]
+    size = partial_ref.shape[1] // heads
+    tokens = partial_ref.shape[0]
+    start = message_refs[0].shape[1] - tokens
+    group = start // (heads * size)
+    code = code_row(message_refs, start, requests)
+    code_ref[...] = jnp.broadcast_to(code, code_ref.shape)
+    span = len(message_refs) * requests
+    here = lax.broadcasted_iota(jnp.int32, (span, tokens), 0) == code
+    queries = [ref[:, :start].astype(jnp.float32) for ref in message_refs]
+    for k in range(heads):
+        rows = []
+        for g in range(group):
+            at = (k * group + g) * size
+            rows += [query[:, at : at + size] for query in queries]
+        query = jnp.concatenate(rows, axis=0).astype(jnp.bfloat16)
+        keys = partial_ref[:, k * size : (k + 1) * size]
+        scores = lax.dot_general(query, keys, NT, preferred_element_type=jnp.float32)
+        lines = [
+            jnp.sum(jnp.where(here, scores[g * span : (g + 1) * span], 0.0), axis=0, keepdims=True)
+            for g in range(group)
+        ]
+        scores_ref[k * group : (k + 1) * group, :] = jnp.concatenate(lines, axis=0) * (
+            1.0 / math.sqrt(size)
+        )
+
+
+def partial_scores(heads, width, partials, messages):
+    tokens = partials.shape[0]
+    size = width // heads
+    query_heads = (messages[0].shape[1] - tokens) // size
+    return pl.pallas_call(
+        functools.partial(score_kernel, heads),
+        grid=(1,),
+        in_specs=[pl.BlockSpec((tokens, width), lambda i: (0, 0))]
+        + [pl.BlockSpec(m.shape, lambda i: (0, 0)) for m in messages],
+        out_specs=[
+            pl.BlockSpec((query_heads, tokens), lambda i: (0, 0)),
+            pl.BlockSpec((8, tokens), lambda i: (0, 0)),
+        ],
+        out_shape=[
+            jax.ShapeDtypeStruct((query_heads, tokens), jnp.float32),
+            jax.ShapeDtypeStruct((8, tokens), jnp.int32),
+        ],
+        compiler_params=params(),
+        name="partial_scores",
+    )(partials, *messages)
+
+
+def mix_kernel(heads, count, code_ref, values_ref, *refs):
+    score_refs = refs[:count]
+    mixed_refs = refs[count : 2 * count]
+    tops_ref, totals_ref = refs[2 * count :]
+    tokens = values_ref.shape[0]
+    size = values_ref.shape[1] // heads
+    requests = tops_ref.shape[0]
+    group = score_refs[0].shape[0] // heads
+    span = count * requests
+    here = lax.broadcasted_iota(jnp.int32, (span, tokens), 0) == code_ref[0:1, :]
+    parts = [ref[...] for ref in score_refs]
+    while len(parts) > 1:
+        parts = [parts[i] + parts[i + 1] for i in range(0, len(parts), 2)]
+    scores = parts[0]
+    mixed = []
+    for k in range(heads):
+        weights = []
+        for g in range(group):
+            row = k * group + g
+            line = jnp.broadcast_to(scores[row : row + 1, :], (span, tokens))
+            top = jnp.max(jnp.where(here, line, LOWEST), axis=1, keepdims=True)
+            probs = jnp.where(here, jnp.exp(line - top), 0.0)
+            total = jnp.sum(probs, axis=1, keepdims=True)
+            weights.append(probs)
+            column = slice(row * size, (row + 1) * size)
+            tops_ref[:, column] = jnp.broadcast_to(top[:requests], (requests, size))
+            totals_ref[:, column] = jnp.broadcast_to(total[:requests], (requests, size))
+        weights = jnp.concatenate(weights, axis=0).astype(jnp.bfloat16)
+        values = values_ref[:, k * size : (k + 1) * size]
+        mixed.append(jnp.dot(weights, values, preferred_element_type=jnp.float32))
+    half = heads // 2
+    for k in range(half):
+        for g in range(group):
+            at = (k * group + g) * size
+            for d in range(count):
+                rows = slice(g * span + d * requests, g * span + (d + 1) * requests)
+                pair = jnp.concatenate([mixed[k][rows], mixed[k + half][rows]], axis=0)
+                mixed_refs[d][:, at : at + size] = pair.astype(jnp.bfloat16)
+
+
+def mix(heads, width, requests, code, partials, scores):
+    count = len(scores)
+    tokens = partials.shape[0]
+    columns = scores[0].shape[0] * (width // heads)
+    whole = lambda shape: pl.BlockSpec(shape, lambda i: (0, 0))
+    return pl.pallas_call(
+        functools.partial(mix_kernel, heads, count),
+        grid=(1,),
+        in_specs=[whole(code.shape), pl.BlockSpec((tokens, width), lambda i: (0, 1))]
+        + [whole(s.shape) for s in scores],
+        out_specs=[whole((2 * requests, columns // 2))] * count + [whole((requests, columns))] * 2,
+        out_shape=[jax.ShapeDtypeStruct((2 * requests, columns // 2), jnp.bfloat16)] * count
+        + [jax.ShapeDtypeStruct((requests, columns), jnp.float32)] * 2,
+        compiler_params=params(),
+        name="mix",
+    )(code, partials, *scores)
+
+
+def merge_kernel(count, cache_ref, stats_ref, factor_ref, *refs):
+    mixed_refs, out_ref = refs[:count], refs[count]
+    requests, columns = cache_ref.shape
+    half = columns // 2
+    new = sum(ref[...].astype(jnp.float32) for ref in mixed_refs)
+    for side in range(2):
+        at = slice(side * half, (side + 1) * half)
+        own = cache_ref[:, at] + new[side * requests : (side + 1) * requests] * factor_ref[:, at]
+        out_ref[:, at] = own.astype(out_ref.dtype)
+    out_ref[:, columns:] = stats_ref[...]
+
+
+def merge(cache_mixed, stats, factor, mixed):
+    requests, columns = cache_mixed.shape
+    return pl.pallas_call(
+        functools.partial(merge_kernel, len(mixed)),
+        out_shape=jax.ShapeDtypeStruct((requests, columns + stats.shape[1]), jnp.bfloat16),
+        compiler_params=params(),
+        name="merge",
+    )(cache_mixed, stats, factor, *mixed)
+
+
+def finish_kernel(own_ref, far_ref, out_ref):
+    requests, columns = out_ref.shape
+    first = lax.axis_index("tp") == 0
+    own, far = own_ref[...].astype(jnp.float32), far_ref[...].astype(jnp.float32)
+    low, high = jnp.where(first, own, far), jnp.where(first, far, own)
+    count = (own.shape[1] - columns) // 8
+    size = columns // count
+
+    def read(message, start):
+        at = columns + start * count
+        parts = [message[:, at + part * count : at + (part + 1) * count] for part in range(3)]
+        return parts[0] + parts[1] + parts[2]
+
+    low_top, high_top = read(low, 0), read(high, 0)
+    both = jnp.maximum(low_top, high_top)
+    low_factor, high_factor = jnp.exp(low_top - both), jnp.exp(high_top - both)
+    inverse = 1.0 / (read(low, 3) * low_factor + read(high, 3) * high_factor)
+    low_factor, high_factor = low_factor * inverse, high_factor * inverse
+    for h in range(count):
+        at = slice(h * size, (h + 1) * size)
+        out = low[:, at] * low_factor[:, h : h + 1] + high[:, at] * high_factor[:, h : h + 1]
+        out_ref[:, at] = out.astype(out_ref.dtype)
+
+
+def finish(own, far, columns):
+    return pl.pallas_call(
+        finish_kernel,
+        out_shape=jax.ShapeDtypeStruct((own.shape[0], columns), jnp.bfloat16),
+        compiler_params=params(),
+        name="finish",
+    )(own, far)
+
+
+def from_partner(x, axis, distance):
+    count = lax.axis_size(axis)
+    return lax.ppermute(x, axis, [(i, i ^ distance) for i in range(count)])
+
+
+def on_device(tokens, kv_weight, owners, requests, signs, queries, kv_cache, lengths):
+    seq_count = lax.axis_size("seq")
+    blocks, size = signs.shape
+    heads = blocks // 2
+    width = heads * size
+    query = queries[0, 0]
+    request_count, columns = query.shape
+    message = make_message(query, owners[:, :, 0], requests, tokens.shape[0])
+    messages = [message] + [from_partner(message, "seq", d) for d in range(1, seq_count)]
+    partials = project(tokens, kv_weight)
+    scores, code = partial_scores(heads, width, partials, messages)
+    scores = [scores] + [from_partner(scores, "seq", d) for d in range(1, seq_count)]
+    results = mix(heads, width, request_count, code, partials, scores)
+    mixed, (tops, totals) = results[:seq_count], results[seq_count:]
+    mixed = [mixed[0]] + [from_partner(mixed[d], "seq", d) for d in range(1, seq_count)]
+    cache_mixed, stats, factor = cache_part(lengths, query, kv_cache[0, 0], signs, tops, totals)
+    own = merge(cache_mixed, stats, factor, mixed)
+    far = from_partner(own, "tp", 1)
+    return finish(own, far, columns).reshape(1, 1, request_count, columns)
 
 
 def hadamard(order):
@@ -41,7 +439,7 @@
     return targets * room + within
 
 
-def on_device(tokens, kv_weight, owners, requests, signs, queries, kv_cache, lengths):
+def on_device_long(tokens, kv_weight, owners, requests, signs, queries, kv_cache, lengths):
     seq_count = lax.axis_size("seq")
     per_device = owners.shape[1]
     slots = max(2, (2 * per_device + seq_count - 1) // seq_count)
@@ -140,8 +538,9 @@
         P(("groups", "seq"), "section", None, "tp", None),
         P(("groups", "seq"), "section", None),
     )
+    short = mesh.shape["seq"] == 4 and mesh.shape["tp"] == 2
     return jax.shard_map(
-        on_device,
+        on_device if short else on_device_long,
         mesh=mesh,
         in_specs=placed,
         out_specs=P(("groups", "seq"), "section", None, None),

time: 116 us -> 39.6 us (0.34)
  waiting for transfers between devices: 36.9 us -> 7.02 us
  Pallas kernels: 0 us -> 16.1 us
  matrix products: 15.4 us -> 0 us
  local copies, waits for them, and re-layouts: 14.9 us -> 0.02 us
  between operations: 13.6 us -> 0.11 us
  blocking collectives: 13 us -> 0 us
  other arithmetic: 6.39 us -> 0 us
  starting transfers between devices: 14.6 us -> 16.2 us
    reduce_scatter x1 -> x0, waiting for transfers between devices: 18.4 us -> none  [on_device(): lax.psum_scatter(jnp.dot(tokens, kv_weight, preferred_element_type=jnp.fl...]
    ppermute x0 -> x10, starting transfers between devices: none -> 16.2 us  [from_partner(): return lax.ppermute(x, axis, [(i, i ^ distance) for i in range(count)])]
    pallas_call x0 -> x7, Pallas kernels: none -> 16.1 us  [the longest x1 8.55 us: cache_part(): pl.pallas_call(cache_kernel, in_specs=[pl.BlockSpec(memory_space=pltpu.SM...]
    dot_general x8 -> x0, matrix products: 15.4 us -> none  [the longest x1 6.54 us: on_device(): jnp.dot(tokens, kv_weight, preferred_element_type=jnp.float32)]
    psum x1 -> x0, waiting for transfers between devices: 14.8 us -> none  [on_device(): lax.psum((mixed * factor[..., None]).astype(jnp.bfloat16), 'tp')]
    all_to_all x3 -> x0, starting transfers between devices: 14.6 us -> none  [the longest x1 6.32 us: on_device(): lax.all_to_all(send_codes, 'seq', split_axis=0, concat_axis=0, tiled=True)]
    pmax x1 -> x0, blocking collectives: 8.02 us -> none  [on_device(): shared_top = lax.pmax(top, 'tp')]
    scatter x2 -> x0, local copies, waits for them, and re-layouts: 7.33 us -> none  [the longest x1 6.56 us: on_device(): jnp.zeros((slot_total, head_blocks, head_size), jnp.bfloat16).at[slot_index]]
  transfers between devices with their start and end apart: 5 -> 10, of which waited for: 3 -> 4; matrix products, arithmetic and copies ran while one was open for 22% -> 0% of each run, Pallas kernels for 0% -> 34%
where the time goes in v2:
time: 39.6 us; the launch traced here: 39.4 us
  starting transfers between devices  16.2 us (41%)
  Pallas kernels  16.1 us (41%)
  waiting for transfers between devices  7.02 us (18%)
    ppermute x10, starting transfers between devices, from_partner(): return lax.ppermute(x, axis, [(i, i ^ distance) for i in range(count)])  16.2 us
    pallas_call x1, Pallas kernels, cache_part(): pl.pallas_call(cache_kernel, in_specs=[pl.BlockSpec(memory_space=pltpu.SM...  8.55 us
    ppermute x10, waiting for transfers between devices, from_partner(): return lax.ppermute(x, axis, [(i, i ^ distance) for i in range(count)])  7.02 us
    pallas_call x1, Pallas kernels, project(): pl.pallas_call(project_kernel, in_specs=[pl.BlockSpec(memory_space=pl.ANY...  4.74 us
    pallas_call x1, Pallas kernels, finish(): pl.pallas_call(finish_kernel, out_shape=jax.ShapeDtypeStruct((own.shape[0...  1.04 us
    pallas_call x1, Pallas kernels, make_message(): pl.pallas_call(message_kernel, in_specs=[pl.BlockSpec(memory_space=pl.ANY...  0.95 us
  transfers between devices with their start and end apart: 10, of which 4 were waited for; matrix products, arithmetic and copies ran while one was open for 0% of the time, Pallas kernels for 34%

profile of v2, /device:TPU:0, one launch (start us, length us, event | category | flops | bytes accessed | tf_op | source)
XLA Modules:
  0.0 39.4 jit_solution(4128365373983236456)
XLA Ops:
  0.0 0.9 %make_message.1.refs_0_ = bf16[8,4352]{1,0:T(8,128)(2,1)S(1)} custom-call(bf16[8,4096]{1,0:T(8,128)(2,1)} %bitcast.5, s32[1,64]{1,0:T(1,128)} %bitcast.7, s32[1,64]{1,0:T(1,128)} %requests_ref.1), custom_call_target="tpu_custom_call" | custom-call | tf_op jit(solution)/shard_map/make_message/pallas_call | solution.py:110
  1.0 0.0 copy-start.1
  1.0 0.0 copy-start.2
  1.0 0.0 copy-start.3
  1.0 5.1 %collective-permute-start.2 = (bf16[8,4352]{1,0:T(8,128)(2,1)S(1)}, bf16[8,4352]{1,0:T(8,128)(2,1)S(1)}, u32[]{:S(2)}, u32[]{:S(2)}) collective-permute-start(bf16[8,4352]{1,0:T(8,128)(2,1)S(1)} %make_message.1.refs_0_), channel_id=1, source_target_pairs={{0,12},{4,8},{8,4},{12,0},{1,13},{5,9},{9,5},{13,1},{2,14},{6,10},... | collective-permute-start | bytes 208904 | tf_op jit(solution)/shard_map/ppermute | solution.py:383
  6.1 0.0 collective-permute-start.1
  6.1 0.6 %collective-permute-start = (bf16[8,4352]{1,0:T(8,128)(2,1)S(1)}, bf16[8,4352]{1,0:T(8,128)(2,1)S(1)}, u32[]{:S(2)}, u32[]{:S(2)}) collective-permute-start(bf16[8,4352]{1,0:T(8,128)(2,1)S(1)} %make_message.1.refs_0_), channel_id=1, source_target_pairs={{0,4},{4,0},{8,12},{12,8},{1,5},{5,1},{9,13},{13,9},{2,6},{6,2},{1... | collective-permute-start | bytes 208904 | tf_op jit(solution)/shard_map/ppermute | solution.py:383
  6.8 4.7 %project.1.partial_ref.values_ref = bf16[256,1024]{1,0:T(8,128)(2,1)S(1)} custom-call(bf16[256,4096]{1,0:T(8,128)(2,1)} %tokens_ref.1, bf16[4096,1024]{1,0:T(8,128)(2,1)} %weight_ref.1), custom_call_target="tpu_custom_call" | custom-call | flops 2147483648 | bytes 10485760 | tf_op jit(solution)/shard_map/project/pallas_call | solution.py:63
  11.5 0.0 collective-permute-done.2.refs_3_
  11.5 0.5 %collective-permute-done.1.refs_2_ = bf16[8,4352]{1,0:T(8,128)(2,1)S(1)} collective-permute-done((bf16[8,4352]{1,0:T(8,128)(2,1)S(1)}, bf16[8,4352]{1,0:T(8,128)(2,1)S(1)}, u32[]{:S(2)}, u32[]{:S(2)}) %collective-permute-start.1) | collective-permute-done | bytes 69664 | tf_op jit(solution)/shard_map/ppermute | solution.py:383
  12.0 0.3 partial_scores.1
  12.4 3.3 %collective-permute-start.5 = (f32[32,256]{1,0:T(8,128)S(1)}, f32[32,256]{1,0:T(8,128)S(1)}, u32[]{:S(2)}, u32[]{:S(2)}) collective-permute-start(f32[32,256]{1,0:T(8,128)S(1)} %get-tuple-element.17.refs_0_), channel_id=1, source_target_pairs={{0,12},{4,8},{8,4},{12,0},{1,13},{5,9},{9,5},{13,1},{2,14},{6,10},... | collective-permute-start | bytes 98312 | tf_op jit(solution)/shard_map/ppermute | solution.py:383
  15.7 1.1 %collective-permute-start.3 = (f32[32,256]{1,0:T(8,128)S(1)}, f32[32,256]{1,0:T(8,128)S(1)}, u32[]{:S(2)}, u32[]{:S(2)}) collective-permute-start(f32[32,256]{1,0:T(8,128)S(1)} %get-tuple-element.17.refs_0_), channel_id=1, source_target_pairs={{0,4},{4,0},{8,12},{12,8},{1,5},{5,1},{9,13},{13,9},{2,6},{6,2},{1... | collective-permute-start | bytes 98312 | tf_op jit(solution)/shard_map/ppermute | solution.py:383
  16.8 1.3 %collective-permute-done.5.refs_3_ = f32[32,256]{1,0:T(8,128)S(1)} collective-permute-done((f32[32,256]{1,0:T(8,128)S(1)}, f32[32,256]{1,0:T(8,128)S(1)}, u32[]{:S(2)}, u32[]{:S(2)}) %collective-permute-start.5) | collective-permute-done | bytes 32800 | tf_op jit(solution)/shard_map/ppermute | solution.py:383
  18.2 2.3 %collective-permute-done.4.refs_2_ = f32[32,256]{1,0:T(8,128)S(1)} collective-permute-done((f32[32,256]{1,0:T(8,128)S(1)}, f32[32,256]{1,0:T(8,128)S(1)}, u32[]{:S(2)}, u32[]{:S(2)}) %collective-permute-start.4) | collective-permute-done | bytes 32800 | tf_op jit(solution)/shard_map/ppermute | solution.py:383
  20.5 0.4 %mix.1 = (bf16[16,2048]{1,0:T(8,128)(2,1)S(1)}, bf16[16,2048]{1,0:T(8,128)(2,1)S(1)}, bf16[16,2048]{1,0:T(8,128)(2,1)S(1)}, bf16[16,2048]{1,0:T(8,128)(2,1)S(1)}...) custom-call(s32[8,256]{1,0:T(8,128)S(1)} %get-tuple-element.16.code_ref, ...), custom_call_target="tpu_custom_call" | custom-call | tf_op jit(solution)/shard_map/mix/pallas_call | solution.py:313
  20.9 0.3 collective-permute-start.6
  21.2 1.9 %collective-permute-start.7 = (bf16[16,2048]{1,0:T(8,128)(2,1)S(1)}, bf16[16,2048]{1,0:T(8,128)(2,1)S(1)}, u32[]{:S(2)}, u32[]{:S(2)}) collective-permute-start(bf16[16,2048]{1,0:T(8,128)(2,1)S(1)} %get-tuple-element.25), channel_id=1, source_target_pairs={{0,8},{4,12},{8,0},{12,4},{1,9},{5,13},{9,1},{13,5},{2,10},{6,14},... | collective-permute-start | bytes 196616 | tf_op jit(solution)/shard_map/ppermute | solution.py:383
  23.1 2.3 %collective-permute-start.8 = (bf16[16,2048]{1,0:T(8,128)(2,1)S(1)}, bf16[16,2048]{1,0:T(8,128)(2,1)S(1)}, u32[]{:S(2)}, u32[]{:S(2)}) collective-permute-start(bf16[16,2048]{1,0:T(8,128)(2,1)S(1)} %get-tuple-element.26), channel_id=1, source_target_pairs={{0,12},{4,8},{8,4},{12,0},{1,13},{5,9},{9,5},{13,1},{2,14},{6,10},... | collective-permute-start | bytes 196616 | tf_op jit(solution)/shard_map/ppermute | solution.py:383
  25.4 8.5 %cache_part.1 = (f32[8,4096]{1,0:T(8,128)S(1)}, bf16[8,256]{1,0:T(8,128)(2,1)S(1)}, f32[8,4096]{1,0:T(8,128)S(1)}) custom-call(s32[1,1,8]{2,1,0:T(1,128)S(1)} %copy-done.3, bf16[8,4096]{1,0:T(8,128)(2,1)S(1)} %bitcast.6, bf16[8,128,1024]{2,1,0:T(8,128)(2,1)S(1)} %bitcast.4, s32[8,128]{1,0:T(8,128)S(1)} %copy-done.2, ...), custom_call_target="tpu_custom_call" | custom-call | flops 16777216 | bytes 2097152 | tf_op jit(solution)/shard_map/cache_part/pallas_call | solution.py:192
  34.0 0.1 merge.1.own_ref
  34.0 1.6 %collective-permute-start.9 = (bf16[8,4352]{1,0:T(8,128)(2,1)S(1)}, bf16[8,4352]{1,0:T(8,128)(2,1)S(1)}, u32[]{:S(2)}, u32[]{:S(2)}) collective-permute-start(bf16[8,4352]{1,0:T(8,128)(2,1)S(1)} %merge.1.own_ref), channel_id=1, source_target_pairs={{0,2},{2,0},{1,3},{3,1},{4,6},{6,4},{5,7},{7,5},{8,10},{10,8},{9,1... | collective-permute-start | bytes 208904 | tf_op jit(solution)/shard_map/ppermute | solution.py:383
  35.6 2.8 %collective-permute-done.9.far_ref = bf16[8,4352]{1,0:T(8,128)(2,1)S(1)} collective-permute-done((bf16[8,4352]{1,0:T(8,128)(2,1)S(1)}, bf16[8,4352]{1,0:T(8,128)(2,1)S(1)}, u32[]{:S(2)}, u32[]{:S(2)}) %collective-permute-start.9) | collective-permute-done | bytes 69664 | tf_op jit(solution)/shard_map/ppermute | solution.py:383
  38.4 1.0 %finish.1 = bf16[8,4096]{1,0:T(8,128)(2,1)} custom-call(bf16[8,4352]{1,0:T(8,128)(2,1)S(1)} %merge.1.own_ref, bf16[8,4352]{1,0:T(8,128)(2,1)S(1)} %collective-permute-done.9.far_ref), custom_call_target="tpu_custom_call" | custom-call | tf_op jit(solution)/shard_map/finish/pallas_call | solution.py:373
  (11 shorter events, 0.0 us)
Async XLA Ops:
  1.0 24.4 %copy-start.1 = (bf16[1,1,8,4096]{3,2,1,0:T(8,128)(2,1)S(1)}, bf16[1,1,8,4096]{3,2,1,0:T(8,128)(2,1)}, u32[]{:S(2)}) copy-start(bf16[1,1,8,4096]{3,2,1,0:T(8,128)(2,1)} %param.13) | copy-start | bytes 196612
  1.0 24.4 %copy-start.2 = (s32[8,128]{1,0:T(8,128)S(1)}, s32[8,128]{1,0:T(8,128)}, u32[]{:S(2)}) copy-start(s32[8,128]{1,0:T(8,128)} %signs_ref.1) | copy-start | bytes 12292
  1.0 24.4 %copy-start.3 = (s32[1,1,8]{2,1,0:T(1,128)S(1)}, s32[1,1,8]{2,1,0:T(1,128)}, u32[]{:S(2)}) copy-start(s32[1,1,8]{2,1,0:T(1,128)} %lengths_ref.1) | copy-start | bytes 100
  1.0 10.5 %collective-permute-start.2 = (bf16[8,4352]{1,0:T(8,128)(2,1)S(1)}, bf16[8,4352]{1,0:T(8,128)(2,1)S(1)}, u32[]{:S(2)}, u32[]{:S(2)}) collective-permute-start(bf16[8,4352]{1,0:T(8,128)(2,1)S(1)} %make_message.1.refs_0_), channel_id=1, source_target_pairs={{0,12},{4,8},{8,4},{12,0},{1,13},{5,9},{9,5},{13,1},{2,14},{6,10},... | collective-permute-start | bytes 208904 | tf_op jit(solution)/shard_map/ppermute | solution.py:383
  6.1 5.9 %collective-permute-start.1 = (bf16[8,4352]{1,0:T(8,128)(2,1)S(1)}, bf16[8,4352]{1,0:T(8,128)(2,1)S(1)}, u32[]{:S(2)}, u32[]{:S(2)}) collective-permute-start(bf16[8,4352]{1,0:T(8,128)(2,1)S(1)} %make_message.1.refs_0_), channel_id=1, source_target_pairs={{0,8},{4,12},{8,0},{12,4},{1,9},{5,13},{9,1},{13,5},{2,10},{6,14},... | collective-permute-start | bytes 208904 | tf_op jit(solution)/shard_map/ppermute | solution.py:383
  6.1 5.9 %collective-permute-start = (bf16[8,4352]{1,0:T(8,128)(2,1)S(1)}, bf16[8,4352]{1,0:T(8,128)(2,1)S(1)}, u32[]{:S(2)}, u32[]{:S(2)}) collective-permute-start(bf16[8,4352]{1,0:T(8,128)(2,1)S(1)} %make_message.1.refs_0_), channel_id=1, source_target_pairs={{0,4},{4,0},{8,12},{12,8},{1,5},{5,1},{9,13},{13,9},{2,6},{6,2},{1... | collective-permute-start | bytes 208904 | tf_op jit(solution)/shard_map/ppermute | solution.py:383
  6.8 18.6 %copy-start = (bf16[1,1,8,128,1024]{4,3,2,1,0:T(8,128)(2,1)S(1)}, bf16[1,1,8,128,1024]{4,3,2,1,0:T(8,128)(2,1)}, u32[]{:S(2)}) copy-start(bf16[1,1,8,128,1024]{4,3,2,1,0:T(8,128)(2,1)} %param.14) | copy-start | bytes 6291460
  12.4 5.8 %collective-permute-start.5 = (f32[32,256]{1,0:T(8,128)S(1)}, f32[32,256]{1,0:T(8,128)S(1)}, u32[]{:S(2)}, u32[]{:S(2)}) collective-permute-start(f32[32,256]{1,0:T(8,128)S(1)} %get-tuple-element.17.refs_0_), channel_id=1, source_target_pairs={{0,12},{4,8},{8,4},{12,0},{1,13},{5,9},{9,5},{13,1},{2,14},{6,10},... | collective-permute-start | bytes 98312 | tf_op jit(solution)/shard_map/ppermute | solution.py:383
  15.7 4.8 %collective-permute-start.4 = (f32[32,256]{1,0:T(8,128)S(1)}, f32[32,256]{1,0:T(8,128)S(1)}, u32[]{:S(2)}, u32[]{:S(2)}) collective-permute-start(f32[32,256]{1,0:T(8,128)S(1)} %get-tuple-element.17.refs_0_), channel_id=1, source_target_pairs={{0,8},{4,12},{8,0},{12,4},{1,9},{5,13},{9,1},{13,5},{2,10},{6,14},... | collective-permute-start | bytes 98312 | tf_op jit(solution)/shard_map/ppermute | solution.py:383
  15.7 4.8 %collective-permute-start.3 = (f32[32,256]{1,0:T(8,128)S(1)}, f32[32,256]{1,0:T(8,128)S(1)}, u32[]{:S(2)}, u32[]{:S(2)}) collective-permute-start(f32[32,256]{1,0:T(8,128)S(1)} %get-tuple-element.17.refs_0_), channel_id=1, source_target_pairs={{0,4},{4,0},{8,12},{12,8},{1,5},{5,1},{9,13},{13,9},{2,6},{6,2},{1... | collective-permute-start | bytes 98312 | tf_op jit(solution)/shard_map/ppermute | solution.py:383
  20.9 13.0 %collective-permute-start.6 = (bf16[16,2048]{1,0:T(8,128)(2,1)S(1)}, bf16[16,2048]{1,0:T(8,128)(2,1)S(1)}, u32[]{:S(2)}, u32[]{:S(2)}) collective-permute-start(bf16[16,2048]{1,0:T(8,128)(2,1)S(1)} %get-tuple-element.24), channel_id=1, source_target_pairs={{0,4},{4,0},{8,12},{12,8},{1,5},{5,1},{9,13},{13,9},{2,6},{6,2},{1... | collective-permute-start | bytes 196616 | tf_op jit(solution)/shard_map/ppermute | solution.py:383
  21.2 12.7 %collective-permute-start.7 = (bf16[16,2048]{1,0:T(8,128)(2,1)S(1)}, bf16[16,2048]{1,0:T(8,128)(2,1)S(1)}, u32[]{:S(2)}, u32[]{:S(2)}) collective-permute-start(bf16[16,2048]{1,0:T(8,128)(2,1)S(1)} %get-tuple-element.25), channel_id=1, source_target_pairs={{0,8},{4,12},{8,0},{12,4},{1,9},{5,13},{9,1},{13,5},{2,10},{6,14},... | collective-permute-start | bytes 196616 | tf_op jit(solution)/shard_map/ppermute | solution.py:383
  23.1 10.9 %collective-permute-start.8 = (bf16[16,2048]{1,0:T(8,128)(2,1)S(1)}, bf16[16,2048]{1,0:T(8,128)(2,1)S(1)}, u32[]{:S(2)}, u32[]{:S(2)}) collective-permute-start(bf16[16,2048]{1,0:T(8,128)(2,1)S(1)} %get-tuple-element.26), channel_id=1, source_target_pairs={{0,12},{4,8},{8,4},{12,0},{1,13},{5,9},{9,5},{13,1},{2,14},{6,10},... | collective-permute-start | bytes 196616 | tf_op jit(solution)/shard_map/ppermute | solution.py:383
  34.0 4.4 %collective-permute-start.9 = (bf16[8,4352]{1,0:T(8,128)(2,1)S(1)}, bf16[8,4352]{1,0:T(8,128)(2,1)S(1)}, u32[]{:S(2)}, u32[]{:S(2)}) collective-permute-start(bf16[8,4352]{1,0:T(8,128)(2,1)S(1)} %merge.1.own_ref), channel_id=1, source_target_pairs={{0,2},{2,0},{1,3},{3,1},{4,6},{6,4},{5,7},{7,5},{8,10},{10,8},{9,1... | collective-permute-start | bytes 208904 | tf_op jit(solution)/shard_map/ppermute | solution.py:383

commit v3 on v2

--- a/solution.py
+++ b/solution.py
@@ -124,11 +124,12 @@
 
 
 def cache_kernel(
-    lengths_ref, query_ref, cache_ref, signs_ref, tops_ref, totals_ref, mixed_ref, stats_ref, factor_ref, order_ref
+    lengths_ref, query_ref, cache_ref, signs_ref, mixed_ref, tops_ref, totals_ref, query_buf, top_buf, total_buf, mixed_buf
 ):
     requests, span, _ = cache_ref.shape
     blocks, size = signs_ref.shape
     heads = blocks // 2
+    width = heads * size
     count = query_ref.shape[1] // size
     group = count // heads
     norm = 1.0 / math.sqrt(size)
@@ -138,66 +139,63 @@
     query = jnp.concatenate(
         [query[:, h * size : (h + 1) * size] * signs[h // group : h // group + 1] for h in range(count)], axis=0
     )
-    rotated = jnp.dot(query.astype(jnp.bfloat16), matrix, preferred_element_type=jnp.float32) * norm
-    order_ref[0] = rotated
-    position = lax.axis_index("tp") * span + lax.broadcasted_iota(jnp.int32, (group, span), 1)
+    query_buf[...] = jnp.dot(query.astype(jnp.bfloat16), matrix, preferred_element_type=jnp.float32) * norm
+    rows = 2 * count
+    kv_head = lax.broadcasted_iota(jnp.int32, (rows, width), 0) // group & (heads - 1)
+    own_head = kv_head == lax.broadcasted_iota(jnp.int32, (rows, width), 1) // size
+    first = lax.broadcasted_iota(jnp.int32, (rows, span), 0) < count
+    position = lax.axis_index("tp") * span + lax.broadcasted_iota(jnp.int32, (rows, span), 1)
+    pairs = range(0, requests, 2)
+    scores = []
+    for r in pairs:
+        both = [query_buf[pl.ds(r + i, count, stride=requests), :] for i in range(2)]
+        wide = jnp.concatenate([jnp.concatenate(both, axis=0)] * heads, axis=1)
+        wide = jnp.where(own_head, wide, 0.0).astype(jnp.bfloat16)
+        keys = cache_ref[r : r + 2, :, :width].reshape(2 * span, width)
+        scores.append(lax.dot_general(wide, keys, NT, preferred_element_type=jnp.float32))
+    probs = []
+    for r, score in zip(pairs, scores):
+        score = jnp.where(first, score[:, :span], score[:, span:]) * norm
+        live = position < jnp.where(first, lengths_ref[0, 0, r], lengths_ref[0, 0, r + 1])
+        top = jnp.max(jnp.where(live, score, LOWEST), axis=1, keepdims=True)
+        prob = jnp.where(live, jnp.exp(score - top), 0.0)
+        total = jnp.sum(prob, axis=1, keepdims=True)
+        at = slice(r * count, (r + 2) * count)
+        top_buf[at, :] = jnp.broadcast_to(top, (rows, size))
+        total_buf[at, :] = jnp.broadcast_to(total, (rows, size))
+        probs.append(
+            jnp.concatenate([jnp.where(first, prob, 0.0), jnp.where(first, 0.0, prob)], axis=1).astype(jnp.bfloat16)
+        )
     mixed = []
-    for r in range(requests):
-        rows = order_ref[0, pl.ds(r, count, stride=requests), :]
-        live = position < lengths_ref[0, 0, r]
-        for k in range(heads):
-            keys = cache_ref[r, :, k * size : (k + 1) * size]
-            values = cache_ref[r, :, (heads + k) * size : (heads + k + 1) * size]
-            here = rows[k * group : (k + 1) * group].astype(jnp.bfloat16)
-            scores = lax.dot_general(here, keys, NT, preferred_element_type=jnp.float32) * norm
-            top = jnp.max(jnp.where(live, scores, LOWEST), axis=1, keepdims=True)
-            probs = jnp.where(live, jnp.exp(scores - top), 0.0)
-            total = jnp.sum(probs, axis=1, keepdims=True)
-            mixed.append(jnp.dot(probs.astype(jnp.bfloat16), values, preferred_element_type=jnp.float32))
-            at = slice(r * count + k * group, r * count + (k + 1) * group)
-            order_ref[1, at, :] = jnp.broadcast_to(top, (group, size))
-            order_ref[2, at, :] = jnp.broadcast_to(total, (group, size))
+    for r, prob in zip(pairs, probs):
+        values = cache_ref[r : r + 2, :, width:].reshape(2 * span, width)
+        wide = jnp.dot(prob, values, preferred_element_type=jnp.float32)
+        wide = jnp.where(own_head, wide, 0.0)
+        mixed.append(sum(wide[:, k * size : (k + 1) * size] for k in range(heads)))
     mixed = jnp.concatenate(mixed, axis=0)
     high = mixed.astype(jnp.bfloat16)
     low = (mixed - high.astype(jnp.float32)).astype(jnp.bfloat16)
     plain = jnp.dot(high, matrix, preferred_element_type=jnp.float32)
-    order_ref[3] = plain + jnp.dot(low, matrix, preferred_element_type=jnp.float32)
-    lane = lax.broadcasted_iota(jnp.int32, stats_ref.shape, 1)
-    stats = jnp.zeros(stats_ref.shape, jnp.float32)
+    mixed_buf[...] = plain + jnp.dot(low, matrix, preferred_element_type=jnp.float32)
     for h in range(count):
         pick = pl.ds(h, requests, stride=count)
+        column = slice(h * size, (h + 1) * size)
         k = heads + h // group
-        top = order_ref[1, pick, :]
-        column = slice(h * size, (h + 1) * size)
-        new_top = tops_ref[:, column]
-        both = jnp.maximum(top, new_top)
-        cache_factor = jnp.exp(top - both)
-        new_factor = jnp.exp(new_top - both)
-        total = order_ref[2, pick, :] * cache_factor + totals_ref[:, column] * new_factor
-        factor_ref[:, column] = new_factor
-        mixed_ref[:, column] = order_ref[3, pick, :] * (cache_factor * (signs[k : k + 1] * norm))
-        for start, value in ((0, both), (3 * count, total)):
-            for part in range(3):
-                piece = value.astype(jnp.bfloat16).astype(jnp.float32)
-                value = value - piece
-                stats = jnp.where(lane == start + part * count + h, jnp.tile(piece, (1, 2)), stats)
-    stats_ref[...] = stats.astype(jnp.bfloat16)
-
-
-def cache_part(lengths, query, cache, signs, tops, totals):
+        mixed_ref[:, column] = mixed_buf[pick, :] * (signs[k : k + 1] * norm)
+        tops_ref[:, column] = top_buf[pick, :]
+        totals_ref[:, column] = total_buf[pick, :]
+
+
+def cache_part(lengths, query, cache, signs):
     requests, span, width = cache.shape
     size = signs.shape[1]
     columns = query.shape[1]
     vmem = pl.BlockSpec(memory_space=pltpu.VMEM)
     return pl.pallas_call(
         cache_kernel,
-        in_specs=[pl.BlockSpec(memory_space=pltpu.SMEM)] + [vmem] * 5,
-        out_shape=[
-            jax.ShapeDtypeStruct(query.shape, jnp.float32),
-            jax.ShapeDtypeStruct((requests, 2 * size), jnp.bfloat16),
-            jax.ShapeDtypeStruct(query.shape, jnp.float32),
-        ],
-        scratch_shapes=[pltpu.VMEM((4, requests * columns // size, size), jnp.float32)],
+        in_specs=[pl.BlockSpec(memory_space=pltpu.SMEM)] + [vmem] * 3,
+        out_shape=[jax.ShapeDtypeStruct(query.shape, jnp.float32)] * 3,
+        scratch_shapes=[pltpu.VMEM((requests * columns // size, size), jnp.float32)] * 4,
         compiler_params=params(),
         cost_estimate=pl.CostEstimate(
             flops=4 * span * requests * columns,
@@ -205,7 +203,45 @@
             transcendentals=span * requests * columns // size,
         ),
         name="cache_part",
-    )(lengths, query, cache, signs, tops, totals)
+    )(lengths, query, cache, signs)
+
+
+def stats_kernel(top_ref, total_ref, new_top_ref, new_total_ref, cache_ref, cache_out_ref, factor_ref, stats_ref):
+    requests, columns = top_ref.shape
+    size = 128
+    count = columns // size
+    top, new_top = top_ref[...], new_top_ref[...]
+    both = jnp.maximum(top, new_top)
+    cache_factor = jnp.exp(top - both)
+    new_factor = jnp.exp(new_top - both)
+    cache_out_ref[...] = cache_ref[...] * cache_factor
+    factor_ref[...] = new_factor
+    total = total_ref[...] * cache_factor + new_total_ref[...] * new_factor
+    lane = lax.broadcasted_iota(jnp.int32, (requests, size), 1)
+    packed = []
+    for value in (both, total):
+        narrow = jnp.zeros((requests, size), jnp.float32)
+        for h in range(count):
+            narrow = jnp.where(lane % count == h, value[:, h * size : (h + 1) * size], narrow)
+        high = narrow.astype(jnp.bfloat16).astype(jnp.float32)
+        middle = (narrow - high).astype(jnp.bfloat16).astype(jnp.float32)
+        low = narrow - high - middle
+        packed.append(jnp.where(lane < count, high, jnp.where(lane < 2 * count, middle, low)))
+    stats_ref[...] = jnp.concatenate(packed, axis=1).astype(jnp.bfloat16)
+
+
+def combine_stats(tops, totals, new_tops, new_totals, cache_mixed):
+    shape = tops.shape
+    return pl.pallas_call(
+        stats_kernel,
+        out_shape=[
+            jax.ShapeDtypeStruct(shape, jnp.float32),
+            jax.ShapeDtypeStruct(shape, jnp.float32),
+            jax.ShapeDtypeStruct((shape[0], 256), jnp.bfloat16),
+        ],
+        compiler_params=params(),
+        name="combine_stats",
+    )(tops, totals, new_tops, new_totals, cache_mixed)
 
 
 def code_row(message_refs, start, requests):
@@ -265,20 +301,28 @@
     )(partials, *messages)
 
 
-def mix_kernel(heads, count, code_ref, values_ref, *refs):
-    score_refs = refs[:count]
-    mixed_refs = refs[count : 2 * count]
-    tops_ref, totals_ref = refs[2 * count :]
+def add_kernel(left_ref, right_ref, out_ref):
+    out_ref[...] = left_ref[...] + right_ref[...]
+
+
+def add(left, right):
+    return pl.pallas_call(
+        add_kernel,
+        out_shape=jax.ShapeDtypeStruct(left.shape, left.dtype),
+        compiler_params=params(),
+        name="add",
+    )(left, right)
+
+
+def mix_kernel(heads, count, code_ref, values_ref, near_ref, far_ref, *refs):
+    mixed_refs, (tops_ref, totals_ref) = refs[:count], refs[count:]
     tokens = values_ref.shape[0]
     size = values_ref.shape[1] // heads
     requests = tops_ref.shape[0]
-    group = score_refs[0].shape[0] // heads
+    group = near_ref.shape[0] // heads
     span = count * requests
     here = lax.broadcasted_iota(jnp.int32, (span, tokens), 0) == code_ref[0:1, :]
-    parts = [ref[...] for ref in score_refs]
-    while len(parts) > 1:
-        parts = [parts[i] + parts[i + 1] for i in range(0, len(parts), 2)]
-    scores = parts[0]
+    scores = near_ref[...] + far_ref[...]
     mixed = []
     for k in range(heads):
         weights = []
@@ -305,8 +349,7 @@
                 mixed_refs[d][:, at : at + size] = pair.astype(jnp.bfloat16)
 
 
-def mix(heads, width, requests, code, partials, scores):
-    count = len(scores)
+def mix(heads, width, requests, count, code, partials, scores):
     tokens = partials.shape[0]
     columns = scores[0].shape[0] * (width // heads)
     whole = lambda shape: pl.BlockSpec(shape, lambda i: (0, 0))
@@ -350,18 +393,18 @@
     first = lax.axis_index("tp") == 0
     own, far = own_ref[...].astype(jnp.float32), far_ref[...].astype(jnp.float32)
     low, high = jnp.where(first, own, far), jnp.where(first, far, own)
-    count = (own.shape[1] - columns) // 8
-    size = columns // count
+    size = 128
+    count = columns // size
 
     def read(message, start):
-        at = columns + start * count
+        at = columns + start * size
         parts = [message[:, at + part * count : at + (part + 1) * count] for part in range(3)]
         return parts[0] + parts[1] + parts[2]
 
     low_top, high_top = read(low, 0), read(high, 0)
     both = jnp.maximum(low_top, high_top)
     low_factor, high_factor = jnp.exp(low_top - both), jnp.exp(high_top - both)
-    inverse = 1.0 / (read(low, 3) * low_factor + read(high, 3) * high_factor)
+    inverse = 1.0 / (read(low, 1) * low_factor + read(high, 1) * high_factor)
     low_factor, high_factor = low_factor * inverse, high_factor * inverse
     for h in range(count):
         at = slice(h * size, (h + 1) * size)
@@ -394,11 +437,16 @@
     messages = [message] + [from_partner(message, "seq", d) for d in range(1, seq_count)]
     partials = project(tokens, kv_weight)
     scores, code = partial_scores(heads, width, partials, messages)
-    scores = [scores] + [from_partner(scores, "seq", d) for d in range(1, seq_count)]
-    results = mix(heads, width, request_count, code, partials, scores)
-    mixed, (tops, totals) = results[:seq_count], results[seq_count:]
+    distance = 1
+    while distance < seq_count // 2:
+        scores = add(scores, from_partner(scores, "seq", distance))
+        distance *= 2
+    scores = (scores, from_partner(scores, "seq", distance))
+    cache_mixed, tops, totals = cache_part(lengths, query, kv_cache[0, 0], signs)
+    results = mix(heads, width, request_count, seq_count, code, partials, scores)
+    mixed, (new_tops, new_totals) = results[:seq_count], results[seq_count:]
     mixed = [mixed[0]] + [from_partner(mixed[d], "seq", d) for d in range(1, seq_count)]
-    cache_mixed, stats, factor = cache_part(lengths, query, kv_cache[0, 0], signs, tops, totals)
+    cache_mixed, factor, stats = combine_stats(tops, totals, new_tops, new_totals, cache_mixed)
     own = merge(cache_mixed, stats, factor, mixed)
     far = from_partner(own, "tp", 1)
     return finish(own, far, columns).reshape(1, 1, request_count, columns)

time: 39.6 us -> 37 us (0.934)
  Pallas kernels: 16.1 us -> 9.07 us
  waiting for transfers between devices: 7.02 us -> 13.2 us
  starting transfers between devices: 16.2 us -> 14.5 us
    pallas_call x1, Pallas kernels: 8.55 us -> 1.61 us  [cache_part(): pl.pallas_call(cache_kernel, in_specs=[pl.BlockSpec(memory_space=pltpu.SM...]
    ppermute x10 -> x9, waiting for transfers between devices: 7.02 us -> 13.2 us  [from_partner(): return lax.ppermute(x, axis, [(i, i ^ distance) for i in range(count)])]
    ppermute x10 -> x9, starting transfers between devices: 16.2 us -> 14.5 us  [from_partner(): return lax.ppermute(x, axis, [(i, i ^ distance) for i in range(count)])]
  transfers between devices with their start and end apart: 10 -> 9, of which waited for: 4 -> 6; matrix products, arithmetic and copies ran while one was open for 0% -> 0% of each run, Pallas kernels for 34% -> 17%
where the time goes in v3:
time: 37 us; the launch traced here: 36.8 us
  starting transfers between devices  14.5 us (39%)
  waiting for transfers between devices  13.2 us (36%)
  Pallas kernels  9.07 us (25%)
    ppermute x9, starting transfers between devices, from_partner(): return lax.ppermute(x, axis, [(i, i ^ distance) for i in range(count)])  14.5 us
    ppermute x9, waiting for transfers between devices, from_partner(): return lax.ppermute(x, axis, [(i, i ^ distance) for i in range(count)])  13.2 us
    pallas_call x1, Pallas kernels, project(): pl.pallas_call(project_kernel, in_specs=[pl.BlockSpec(memory_space=pl.ANY...  4.74 us
    pallas_call x1, Pallas kernels, cache_part(): pl.pallas_call(cache_kernel, in_specs=[pl.BlockSpec(memory_space=pltpu.SM...  1.61 us
    pallas_call x1, Pallas kernels, make_message(): pl.pallas_call(message_kernel, in_specs=[pl.BlockSpec(memory_space=pl.ANY...  0.95 us
    pallas_call x1, Pallas kernels, finish(): pl.pallas_call(finish_kernel, out_shape=jax.ShapeDtypeStruct((own.shape[0...  0.9 us
  transfers between devices with their start and end apart: 9, of which 6 were waited for; matrix products, arithmetic and copies ran while one was open for 0% of the time, Pallas kernels for 17%

profile of v3, /device:TPU:0, one launch (start us, length us, event | category | flops | bytes accessed | tf_op | source)
XLA Modules:
  0.0 36.8 jit_solution(11545892061484661443)
XLA Ops:
  0.0 0.9 %make_message.1.refs_0_ = bf16[8,4352]{1,0:T(8,128)(2,1)S(1)} custom-call(bf16[8,4096]{1,0:T(8,128)(2,1)} %bitcast.5, s32[1,64]{1,0:T(1,128)} %bitcast.7, s32[1,64]{1,0:T(1,128)} %requests_ref.1), custom_call_target="tpu_custom_call" | custom-call | tf_op jit(solution)/shard_map/make_message/pallas_call | solution.py:110
  1.0 0.0 copy-start.2
  1.0 0.0 copy-start.3
  1.0 3.1 %collective-permute-start = (bf16[8,4352]{1,0:T(8,128)(2,1)S(1)}, bf16[8,4352]{1,0:T(8,128)(2,1)S(1)}, u32[]{:S(2)}, u32[]{:S(2)}) collective-permute-start(bf16[8,4352]{1,0:T(8,128)(2,1)S(1)} %make_message.1.refs_0_), channel_id=1, source_target_pairs={{0,4},{4,0},{8,12},{12,8},{1,5},{5,1},{9,13},{13,9},{2,6},{6,2},{1... | collective-permute-start | bytes 208904 | tf_op jit(solution)/shard_map/ppermute | solution.py:426
  4.1 2.6 %collective-permute-start.1 = (bf16[8,4352]{1,0:T(8,128)(2,1)S(1)}, bf16[8,4352]{1,0:T(8,128)(2,1)S(1)}, u32[]{:S(2)}, u32[]{:S(2)}) collective-permute-start(bf16[8,4352]{1,0:T(8,128)(2,1)S(1)} %make_message.1.refs_0_), channel_id=1, source_target_pairs={{0,8},{4,12},{8,0},{12,4},{1,9},{5,13},{9,1},{13,5},{2,10},{6,14},... | collective-permute-start | bytes 208904 | tf_op jit(solution)/shard_map/ppermute | solution.py:426
  6.7 4.7 %project.1.partial_ref.values_ref = bf16[256,1024]{1,0:T(8,128)(2,1)S(1)} custom-call(bf16[256,4096]{1,0:T(8,128)(2,1)} %tokens_ref.1, bf16[4096,1024]{1,0:T(8,128)(2,1)} %weight_ref.1), custom_call_target="tpu_custom_call" | custom-call | flops 2147483648 | bytes 10485760 | tf_op jit(solution)/shard_map/project/pallas_call | solution.py:63
  11.4 0.2 collective-permute-done.1.refs_2_
  11.6 1.3 %collective-permute-done.2.refs_3_ = bf16[8,4352]{1,0:T(8,128)(2,1)S(1)} collective-permute-done((bf16[8,4352]{1,0:T(8,128)(2,1)S(1)}, bf16[8,4352]{1,0:T(8,128)(2,1)S(1)}, u32[]{:S(2)}, u32[]{:S(2)}) %collective-permute-start.2) | collective-permute-done | bytes 69664 | tf_op jit(solution)/shard_map/ppermute | solution.py:426
  12.9 0.3 partial_scores.1
  13.2 0.8 %collective-permute-start.3 = (f32[32,256]{1,0:T(8,128)S(1)}, f32[32,256]{1,0:T(8,128)S(1)}, u32[]{:S(2)}, u32[]{:S(2)}) collective-permute-start(f32[32,256]{1,0:T(8,128)S(1)} %get-tuple-element.22.left_ref), channel_id=1, source_target_pairs={{0,4},{4,0},{8,12},{12,8},{1,5},{5,1},{9,13},{13,9},{2,6},{6,2},{1... | collective-permute-start | bytes 98312 | tf_op jit(solution)/shard_map/ppermute | solution.py:426
  14.1 3.1 %collective-permute-done.3.right_ref = f32[32,256]{1,0:T(8,128)S(1)} collective-permute-done((f32[32,256]{1,0:T(8,128)S(1)}, f32[32,256]{1,0:T(8,128)S(1)}, u32[]{:S(2)}, u32[]{:S(2)}) %collective-permute-start.3) | collective-permute-done | bytes 32800 | tf_op jit(solution)/shard_map/ppermute | solution.py:426
  17.2 1.9 %collective-permute-start.4 = (f32[32,256]{1,0:T(8,128)S(1)}, f32[32,256]{1,0:T(8,128)S(1)}, u32[]{:S(2)}, u32[]{:S(2)}) collective-permute-start(f32[32,256]{1,0:T(8,128)S(1)} %add.1.near_ref), channel_id=1, source_target_pairs={{0,8},{4,12},{8,0},{12,4},{1,9},{5,13},{9,1},{13,5},{2,10},{6,14},... | collective-permute-start | bytes 98312 | tf_op jit(solution)/shard_map/ppermute | solution.py:426
  19.1 3.2 %collective-permute-done.4.far_ref = f32[32,256]{1,0:T(8,128)S(1)} collective-permute-done((f32[32,256]{1,0:T(8,128)S(1)}, f32[32,256]{1,0:T(8,128)S(1)}, u32[]{:S(2)}, u32[]{:S(2)}) %collective-permute-start.4) | collective-permute-done | bytes 32800 | tf_op jit(solution)/shard_map/ppermute | solution.py:426
  22.4 0.4 %mix.1 = (bf16[16,2048]{1,0:T(8,128)(2,1)S(1)}, bf16[16,2048]{1,0:T(8,128)(2,1)S(1)}, bf16[16,2048]{1,0:T(8,128)(2,1)S(1)}, bf16[16,2048]{1,0:T(8,128)(2,1)S(1)}...) custom-call(s32[8,256]{1,0:T(8,128)S(1)} %get-tuple-element.21.code_ref, ...), custom_call_target="tpu_custom_call" | custom-call | tf_op jit(solution)/shard_map/mix/pallas_call | solution.py:356
  22.8 0.6 %collective-permute-start.5 = (bf16[16,2048]{1,0:T(8,128)(2,1)S(1)}, bf16[16,2048]{1,0:T(8,128)(2,1)S(1)}, u32[]{:S(2)}, u32[]{:S(2)}) collective-permute-start(bf16[16,2048]{1,0:T(8,128)(2,1)S(1)} %get-tuple-element.30), channel_id=1, source_target_pairs={{0,4},{4,0},{8,12},{12,8},{1,5},{5,1},{9,13},{13,9},{2,6},{6,2},{1... | collective-permute-start | bytes 196616 | tf_op jit(solution)/shard_map/ppermute | solution.py:426
  23.4 2.1 %collective-permute-start.6 = (bf16[16,2048]{1,0:T(8,128)(2,1)S(1)}, bf16[16,2048]{1,0:T(8,128)(2,1)S(1)}, u32[]{:S(2)}, u32[]{:S(2)}) collective-permute-start(bf16[16,2048]{1,0:T(8,128)(2,1)S(1)} %get-tuple-element.31), channel_id=1, source_target_pairs={{0,8},{4,12},{8,0},{12,4},{1,9},{5,13},{9,1},{13,5},{2,10},{6,14},... | collective-permute-start | bytes 196616 | tf_op jit(solution)/shard_map/ppermute | solution.py:426
  25.4 1.8 %collective-permute-start.7 = (bf16[16,2048]{1,0:T(8,128)(2,1)S(1)}, bf16[16,2048]{1,0:T(8,128)(2,1)S(1)}, u32[]{:S(2)}, u32[]{:S(2)}) collective-permute-start(bf16[16,2048]{1,0:T(8,128)(2,1)S(1)} %get-tuple-element.32), channel_id=1, source_target_pairs={{0,12},{4,8},{8,4},{12,0},{1,13},{5,9},{9,5},{13,1},{2,14},{6,10},... | collective-permute-start | bytes 196616 | tf_op jit(solution)/shard_map/ppermute | solution.py:426
  27.2 1.6 %cache_part.1 = (f32[8,4096]{1,0:T(8,128)S(1)}, f32[8,4096]{1,0:T(8,128)S(1)}, f32[8,4096]{1,0:T(8,128)S(1)}) custom-call(s32[1,1,8]{2,1,0:T(1,128)S(1)} %copy-done.3, bf16[8,4096]{1,0:T(8,128)(2,1)S(1)} %bitcast.6, bf16[8,128,1024]{2,1,0:T(8,128)(2,1)S(1)} %bitcast.4, s32[8,128]{1,0:T(8,128)S(1)} %copy-done.2), custom_call_target="tpu_custom_call" | custom-call | flops 16777216 | bytes 2097152 | tf_op jit(solution)/shard_map/cache_part/pallas_call | solution.py:194
  28.9 0.1 combine_stats.1
  29.0 2.5 %collective-permute-done.7.refs_3_ = bf16[16,2048]{1,0:T(8,128)(2,1)S(1)} collective-permute-done((bf16[16,2048]{1,0:T(8,128)(2,1)S(1)}, bf16[16,2048]{1,0:T(8,128)(2,1)S(1)}, u32[]{:S(2)}, u32[]{:S(2)}) %collective-permute-start.7) | collective-permute-done | bytes 65568 | tf_op jit(solution)/shard_map/ppermute | solution.py:426
  31.5 0.1 merge.1.own_ref
  31.6 1.6 %collective-permute-start.8 = (bf16[8,4352]{1,0:T(8,128)(2,1)S(1)}, bf16[8,4352]{1,0:T(8,128)(2,1)S(1)}, u32[]{:S(2)}, u32[]{:S(2)}) collective-permute-start(bf16[8,4352]{1,0:T(8,128)(2,1)S(1)} %merge.1.own_ref), channel_id=1, source_target_pairs={{0,2},{2,0},{1,3},{3,1},{4,6},{6,4},{5,7},{7,5},{8,10},{10,8},{9,1... | collective-permute-start | bytes 208904 | tf_op jit(solution)/shard_map/ppermute | solution.py:426
  33.1 2.8 %collective-permute-done.8.far_ref = bf16[8,4352]{1,0:T(8,128)(2,1)S(1)} collective-permute-done((bf16[8,4352]{1,0:T(8,128)(2,1)S(1)}, bf16[8,4352]{1,0:T(8,128)(2,1)S(1)}, u32[]{:S(2)}, u32[]{:S(2)}) %collective-permute-start.8) | collective-permute-done | bytes 69664 | tf_op jit(solution)/shard_map/ppermute | solution.py:426
  35.9 0.9 %finish.1 = bf16[8,4096]{1,0:T(8,128)(2,1)} custom-call(bf16[8,4352]{1,0:T(8,128)(2,1)S(1)} %merge.1.own_ref, bf16[8,4352]{1,0:T(8,128)(2,1)S(1)} %collective-permute-done.8.far_ref), custom_call_target="tpu_custom_call" | custom-call | tf_op jit(solution)/shard_map/finish/pallas_call | solution.py:416
  (11 shorter events, 0.0 us)
Async XLA Ops:
  1.0 26.3 %copy-start.1 = (bf16[1,1,8,4096]{3,2,1,0:T(8,128)(2,1)S(1)}, bf16[1,1,8,4096]{3,2,1,0:T(8,128)(2,1)}, u32[]{:S(2)}) copy-start(bf16[1,1,8,4096]{3,2,1,0:T(8,128)(2,1)} %param.13) | copy-start | bytes 196612
  1.0 26.3 %copy-start.2 = (s32[8,128]{1,0:T(8,128)S(1)}, s32[8,128]{1,0:T(8,128)}, u32[]{:S(2)}) copy-start(s32[8,128]{1,0:T(8,128)} %signs_ref.1) | copy-start | bytes 12292
  1.0 26.3 %copy-start.3 = (s32[1,1,8]{2,1,0:T(1,128)S(1)}, s32[1,1,8]{2,1,0:T(1,128)}, u32[]{:S(2)}) copy-start(s32[1,1,8]{2,1,0:T(1,128)} %lengths_ref.1) | copy-start | bytes 100
  1.0 10.4 %collective-permute-start = (bf16[8,4352]{1,0:T(8,128)(2,1)S(1)}, bf16[8,4352]{1,0:T(8,128)(2,1)S(1)}, u32[]{:S(2)}, u32[]{:S(2)}) collective-permute-start(bf16[8,4352]{1,0:T(8,128)(2,1)S(1)} %make_message.1.refs_0_), channel_id=1, source_target_pairs={{0,4},{4,0},{8,12},{12,8},{1,5},{5,1},{9,13},{13,9},{2,6},{6,2},{1... | collective-permute-start | bytes 208904 | tf_op jit(solution)/shard_map/ppermute | solution.py:426
  4.1 7.5 %collective-permute-start.1 = (bf16[8,4352]{1,0:T(8,128)(2,1)S(1)}, bf16[8,4352]{1,0:T(8,128)(2,1)S(1)}, u32[]{:S(2)}, u32[]{:S(2)}) collective-permute-start(bf16[8,4352]{1,0:T(8,128)(2,1)S(1)} %make_message.1.refs_0_), channel_id=1, source_target_pairs={{0,8},{4,12},{8,0},{12,4},{1,9},{5,13},{9,1},{13,5},{2,10},{6,14},... | collective-permute-start | bytes 208904 | tf_op jit(solution)/shard_map/ppermute | solution.py:426
  6.7 6.2 %collective-permute-start.2 = (bf16[8,4352]{1,0:T(8,128)(2,1)S(1)}, bf16[8,4352]{1,0:T(8,128)(2,1)S(1)}, u32[]{:S(2)}, u32[]{:S(2)}) collective-permute-start(bf16[8,4352]{1,0:T(8,128)(2,1)S(1)} %make_message.1.refs_0_), channel_id=1, source_target_pairs={{0,12},{4,8},{8,4},{12,0},{1,13},{5,9},{9,5},{13,1},{2,14},{6,10},... | collective-permute-start | bytes 208904 | tf_op jit(solution)/shard_map/ppermute | solution.py:426
  6.7 20.6 %copy-start = (bf16[1,1,8,128,1024]{4,3,2,1,0:T(8,128)(2,1)S(1)}, bf16[1,1,8,128,1024]{4,3,2,1,0:T(8,128)(2,1)}, u32[]{:S(2)}) copy-start(bf16[1,1,8,128,1024]{4,3,2,1,0:T(8,128)(2,1)} %param.14) | copy-start | bytes 6291460
  13.2 4.0 %collective-permute-start.3 = (f32[32,256]{1,0:T(8,128)S(1)}, f32[32,256]{1,0:T(8,128)S(1)}, u32[]{:S(2)}, u32[]{:S(2)}) collective-permute-start(f32[32,256]{1,0:T(8,128)S(1)} %get-tuple-element.22.left_ref), channel_id=1, source_target_pairs={{0,4},{4,0},{8,12},{12,8},{1,5},{5,1},{9,13},{13,9},{2,6},{6,2},{1... | collective-permute-start | bytes 98312 | tf_op jit(solution)/shard_map/ppermute | solution.py:426
  17.2 5.2 %collective-permute-start.4 = (f32[32,256]{1,0:T(8,128)S(1)}, f32[32,256]{1,0:T(8,128)S(1)}, u32[]{:S(2)}, u32[]{:S(2)}) collective-permute-start(f32[32,256]{1,0:T(8,128)S(1)} %add.1.near_ref), channel_id=1, source_target_pairs={{0,8},{4,12},{8,0},{12,4},{1,9},{5,13},{9,1},{13,5},{2,10},{6,14},... | collective-permute-start | bytes 98312 | tf_op jit(solution)/shard_map/ppermute | solution.py:426
  22.8 6.2 %collective-permute-start.5 = (bf16[16,2048]{1,0:T(8,128)(2,1)S(1)}, bf16[16,2048]{1,0:T(8,128)(2,1)S(1)}, u32[]{:S(2)}, u32[]{:S(2)}) collective-permute-start(bf16[16,2048]{1,0:T(8,128)(2,1)S(1)} %get-tuple-element.30), channel_id=1, source_target_pairs={{0,4},{4,0},{8,12},{12,8},{1,5},{5,1},{9,13},{13,9},{2,6},{6,2},{1... | collective-permute-start | bytes 196616 | tf_op jit(solution)/shard_map/ppermute | solution.py:426
  23.4 5.6 %collective-permute-start.6 = (bf16[16,2048]{1,0:T(8,128)(2,1)S(1)}, bf16[16,2048]{1,0:T(8,128)(2,1)S(1)}, u32[]{:S(2)}, u32[]{:S(2)}) collective-permute-start(bf16[16,2048]{1,0:T(8,128)(2,1)S(1)} %get-tuple-element.31), channel_id=1, source_target_pairs={{0,8},{4,12},{8,0},{12,4},{1,9},{5,13},{9,1},{13,5},{2,10},{6,14},... | collective-permute-start | bytes 196616 | tf_op jit(solution)/shard_map/ppermute | solution.py:426
  25.4 6.1 %collective-permute-start.7 = (bf16[16,2048]{1,0:T(8,128)(2,1)S(1)}, bf16[16,2048]{1,0:T(8,128)(2,1)S(1)}, u32[]{:S(2)}, u32[]{:S(2)}) collective-permute-start(bf16[16,2048]{1,0:T(8,128)(2,1)S(1)} %get-tuple-element.32), channel_id=1, source_target_pairs={{0,12},{4,8},{8,4},{12,0},{1,13},{5,9},{9,5},{13,1},{2,14},{6,10},... | collective-permute-start | bytes 196616 | tf_op jit(solution)/shard_map/ppermute | solution.py:426
  31.6 4.4 %collective-permute-start.8 = (bf16[8,4352]{1,0:T(8,128)(2,1)S(1)}, bf16[8,4352]{1,0:T(8,128)(2,1)S(1)}, u32[]{:S(2)}, u32[]{:S(2)}) collective-permute-start(bf16[8,4352]{1,0:T(8,128)(2,1)S(1)} %merge.1.own_ref), channel_id=1, source_target_pairs={{0,2},{2,0},{1,3},{3,1},{4,6},{6,4},{5,7},{7,5},{8,10},{10,8},{9,1... | collective-permute-start | bytes 208904 | tf_op jit(solution)/shard_map/ppermute | solution.py:426

commit v4 on v3

--- a/solution.py
+++ b/solution.py
@@ -19,6 +19,10 @@
 
 def in_hbm(x):
     return pltpu.with_memory_space_constraint(x, pltpu.HBM)
+
+
+def in_vmem(x):
+    return pltpu.with_memory_space_constraint(x, pltpu.VMEM)
 
 
 def hadamard_tile(order):
@@ -31,54 +35,26 @@
     return (1 - 2 * (parity & 1)).astype(jnp.float32).astype(jnp.bfloat16)
 
 
-def project_kernel(tokens_ref, weight_ref, out_ref, tokens_buf, weight_buf, acc_ref, sems):
-    steps, block, width = weight_buf.shape
-    copies = []
-    for step in range(steps):
-        span = slice(step * block, (step + 1) * block)
-        pair = (
-            pltpu.make_async_copy(tokens_ref.at[:, span], tokens_buf.at[step], sems.at[0, step]),
-            pltpu.make_async_copy(weight_ref.at[span, :], weight_buf.at[step], sems.at[1, step]),
-        )
-        for copy in pair:
-            copy.start()
-        copies.append(pair)
-    for step in range(steps):
-        for copy in copies[step]:
-            copy.wait()
-        part = jnp.dot(tokens_buf[step], weight_buf[step], preferred_element_type=jnp.float32)
-        if step == 0:
-            acc_ref[...] = part
-        elif step < steps - 1:
-            acc_ref[...] += part
-        else:
-            out_ref[...] = (acc_ref[...] + part).astype(out_ref.dtype)
+def project_kernel(tokens_ref, weight_ref, out_ref):
+    out_ref[...] = jnp.dot(tokens_ref[...], weight_ref[...], preferred_element_type=jnp.float32).astype(out_ref.dtype)
 
 
 def project(tokens, weight):
     rows, features = tokens.shape
     width = weight.shape[1]
-    block = min(512, features // 2)
-    steps = features // block
     return pl.pallas_call(
         project_kernel,
-        in_specs=[pl.BlockSpec(memory_space=pl.ANY)] * 2,
+        in_specs=[pl.BlockSpec(memory_space=pltpu.VMEM)] * 2,
         out_specs=pl.BlockSpec(memory_space=pltpu.VMEM),
         out_shape=jax.ShapeDtypeStruct((rows, width), jnp.bfloat16),
-        scratch_shapes=[
-            pltpu.VMEM((steps, rows, block), jnp.bfloat16),
-            pltpu.VMEM((steps, block, width), jnp.bfloat16),
-            pltpu.VMEM((rows, width), jnp.float32),
-            pltpu.SemaphoreType.DMA((2, steps)),
-        ],
-        compiler_params=params(48),
+        compiler_params=params(32),
         cost_estimate=pl.CostEstimate(
             flops=2 * rows * features * width,
             bytes_accessed=2 * (rows * features + features * width),
             transcendentals=0,
         ),
         name="project",
-    )(in_hbm(tokens), in_hbm(weight))
+    )(in_vmem(tokens), in_vmem(weight))
 
 
 def message_kernel(query_ref, owners_ref, requests_ref, out_ref, query_buf, owners_buf, requests_buf, sems):
@@ -118,7 +94,8 @@
             pltpu.VMEM(requests.shape, requests.dtype),
             pltpu.SemaphoreType.DMA((3,)),
         ],
-        compiler_params=params(48),
+        compiler_params=params(16),
+        cost_estimate=pl.CostEstimate(flops=10**11, bytes_accessed=10**4, transcendentals=0),
         name="make_message",
     )(in_hbm(query), in_hbm(owners), in_hbm(requests))
 

time: 37 us -> 36.7 us (level)
  Pallas kernels: 9.07 us -> 6.78 us
  waiting for transfers between devices: 13.2 us -> 15 us
    pallas_call x1, Pallas kernels: 4.74 us -> 2.32 us  [project(): pl.pallas_call(project_kernel, in_specs=[pl.BlockSpec(memory_space=pltpu....]
    ppermute x9, waiting for transfers between devices: 13.2 us -> 15 us  [from_partner(): return lax.ppermute(x, axis, [(i, i ^ distance) for i in range(count)])]
  transfers between devices with their start and end apart: 9 -> 9, of which waited for: 6 -> 6; matrix products, arithmetic and copies ran while one was open for 0% -> 0% of each run, Pallas kernels for 17% -> 11%
where the time goes in v4:
time: 36.7 us; the launch traced here: 36.6 us
  waiting for transfers between devices  15 us (41%)
  starting transfers between devices  14.6 us (40%)
  Pallas kernels  6.78 us (18%)
    ppermute x9, waiting for transfers between devices, from_partner(): return lax.ppermute(x, axis, [(i, i ^ distance) for i in range(count)])  15 us
    ppermute x9, starting transfers between devices, from_partner(): return lax.ppermute(x, axis, [(i, i ^ distance) for i in range(count)])  14.6 us
    pallas_call x1, Pallas kernels, project(): pl.pallas_call(project_kernel, in_specs=[pl.BlockSpec(memory_space=pltpu....  2.32 us
    pallas_call x1, Pallas kernels, cache_part(): pl.pallas_call(cache_kernel, in_specs=[pl.BlockSpec(memory_space=pltpu.SM...  1.61 us
    pallas_call x1, Pallas kernels, make_message(): pl.pallas_call(message_kernel, in_specs=[pl.BlockSpec(memory_space=pl.ANY...  1.1 us
    pallas_call x1, Pallas kernels, finish(): pl.pallas_call(finish_kernel, out_shape=jax.ShapeDtypeStruct((own.shape[0...  0.9 us
  transfers between devices with their start and end apart: 9, of which 6 were waited for; matrix products, arithmetic and copies ran while one was open for 0% of the time, Pallas kernels for 11%

profile of v4, /device:TPU:0, one launch (start us, length us, event | category | flops | bytes accessed | tf_op | source)
XLA Modules:
  0.0 36.6 jit_solution(10784488294762385166)
XLA Ops:
  0.0 1.1 %make_message.1.refs_0_ = bf16[8,4352]{1,0:T(8,128)(2,1)S(1)} custom-call(bf16[8,4096]{1,0:T(8,128)(2,1)} %bitcast.7, s32[1,64]{1,0:T(1,128)} %bitcast.9, s32[1,64]{1,0:T(1,128)} %requests_ref.1), custom_call_target="tpu_custom_call" | custom-call | flops 99999997952 | bytes 10000 | tf_op jit(solution)/shard_map/make_message/pallas_call | solution.py:86
  1.1 0.0 copy-start.3
  1.1 0.0 copy-start.4
  1.1 3.1 %collective-permute-start = (bf16[8,4352]{1,0:T(8,128)(2,1)S(1)}, bf16[8,4352]{1,0:T(8,128)(2,1)S(1)}, u32[]{:S(2)}, u32[]{:S(2)}) collective-permute-start(bf16[8,4352]{1,0:T(8,128)(2,1)S(1)} %make_message.1.refs_0_), channel_id=1, source_target_pairs={{0,4},{4,0},{8,12},{12,8},{1,5},{5,1},{9,13},{13,9},{2,6},{6,2},{1... | collective-permute-start | bytes 208904 | tf_op jit(solution)/shard_map/ppermute | solution.py:403
  4.2 2.6 %collective-permute-start.1 = (bf16[8,4352]{1,0:T(8,128)(2,1)S(1)}, bf16[8,4352]{1,0:T(8,128)(2,1)S(1)}, u32[]{:S(2)}, u32[]{:S(2)}) collective-permute-start(bf16[8,4352]{1,0:T(8,128)(2,1)S(1)} %make_message.1.refs_0_), channel_id=1, source_target_pairs={{0,8},{4,12},{8,0},{12,4},{1,9},{5,13},{9,1},{13,5},{2,10},{6,14},... | collective-permute-start | bytes 208904 | tf_op jit(solution)/shard_map/ppermute | solution.py:403
  6.9 0.0 copy-start
  6.9 2.3 %project.1.partial_ref.values_ref = bf16[256,1024]{1,0:T(8,128)(2,1)S(1)} custom-call(bf16[256,4096]{1,0:T(8,128)(2,1)S(1)} %copy-done.1, bf16[4096,1024]{1,0:T(8,128)(2,1)S(1)} %bitcast.5), custom_call_target="tpu_custom_call" | custom-call | flops 2147483648 | bytes 10485760 | tf_op jit(solution)/shard_map/project/pallas_call | solution.py:45
  9.2 2.6 %collective-permute-done.1.refs_2_ = bf16[8,4352]{1,0:T(8,128)(2,1)S(1)} collective-permute-done((bf16[8,4352]{1,0:T(8,128)(2,1)S(1)}, bf16[8,4352]{1,0:T(8,128)(2,1)S(1)}, u32[]{:S(2)}, u32[]{:S(2)}) %collective-permute-start.1) | collective-permute-done | bytes 69664 | tf_op jit(solution)/shard_map/ppermute | solution.py:403
  11.8 1.3 %collective-permute-done.2.refs_3_ = bf16[8,4352]{1,0:T(8,128)(2,1)S(1)} collective-permute-done((bf16[8,4352]{1,0:T(8,128)(2,1)S(1)}, bf16[8,4352]{1,0:T(8,128)(2,1)S(1)}, u32[]{:S(2)}, u32[]{:S(2)}) %collective-permute-start.2) | collective-permute-done | bytes 69664 | tf_op jit(solution)/shard_map/ppermute | solution.py:403
  13.0 0.3 partial_scores.1
  13.4 0.8 %collective-permute-start.3 = (f32[32,256]{1,0:T(8,128)S(1)}, f32[32,256]{1,0:T(8,128)S(1)}, u32[]{:S(2)}, u32[]{:S(2)}) collective-permute-start(f32[32,256]{1,0:T(8,128)S(1)} %get-tuple-element.22.left_ref), channel_id=1, source_target_pairs={{0,4},{4,0},{8,12},{12,8},{1,5},{5,1},{9,13},{13,9},{2,6},{6,2},{1... | collective-permute-start | bytes 98312 | tf_op jit(solution)/shard_map/ppermute | solution.py:403
  14.2 3.1 %collective-permute-done.3.right_ref = f32[32,256]{1,0:T(8,128)S(1)} collective-permute-done((f32[32,256]{1,0:T(8,128)S(1)}, f32[32,256]{1,0:T(8,128)S(1)}, u32[]{:S(2)}, u32[]{:S(2)}) %collective-permute-start.3) | collective-permute-done | bytes 32800 | tf_op jit(solution)/shard_map/ppermute | solution.py:403
  17.4 2.1 %collective-permute-start.4 = (f32[32,256]{1,0:T(8,128)S(1)}, f32[32,256]{1,0:T(8,128)S(1)}, u32[]{:S(2)}, u32[]{:S(2)}) collective-permute-start(f32[32,256]{1,0:T(8,128)S(1)} %add.1.near_ref), channel_id=1, source_target_pairs={{0,8},{4,12},{8,0},{12,4},{1,9},{5,13},{9,1},{13,5},{2,10},{6,14},... | collective-permute-start | bytes 98312 | tf_op jit(solution)/shard_map/ppermute | solution.py:403
  19.4 3.1 %collective-permute-done.4.far_ref = f32[32,256]{1,0:T(8,128)S(1)} collective-permute-done((f32[32,256]{1,0:T(8,128)S(1)}, f32[32,256]{1,0:T(8,128)S(1)}, u32[]{:S(2)}, u32[]{:S(2)}) %collective-permute-start.4) | collective-permute-done | bytes 32800 | tf_op jit(solution)/shard_map/ppermute | solution.py:403
  22.5 0.4 %mix.1 = (bf16[16,2048]{1,0:T(8,128)(2,1)S(1)}, bf16[16,2048]{1,0:T(8,128)(2,1)S(1)}, bf16[16,2048]{1,0:T(8,128)(2,1)S(1)}, bf16[16,2048]{1,0:T(8,128)(2,1)S(1)}...) custom-call(s32[8,256]{1,0:T(8,128)S(1)} %get-tuple-element.21.code_ref, ...), custom_call_target="tpu_custom_call" | custom-call | tf_op jit(solution)/shard_map/mix/pallas_call | solution.py:333
  22.9 0.6 %collective-permute-start.5 = (bf16[16,2048]{1,0:T(8,128)(2,1)S(1)}, bf16[16,2048]{1,0:T(8,128)(2,1)S(1)}, u32[]{:S(2)}, u32[]{:S(2)}) collective-permute-start(bf16[16,2048]{1,0:T(8,128)(2,1)S(1)} %get-tuple-element.30), channel_id=1, source_target_pairs={{0,4},{4,0},{8,12},{12,8},{1,5},{5,1},{9,13},{13,9},{2,6},{6,2},{1... | collective-permute-start | bytes 196616 | tf_op jit(solution)/shard_map/ppermute | solution.py:403
  23.5 1.7 %collective-permute-start.6 = (bf16[16,2048]{1,0:T(8,128)(2,1)S(1)}, bf16[16,2048]{1,0:T(8,128)(2,1)S(1)}, u32[]{:S(2)}, u32[]{:S(2)}) collective-permute-start(bf16[16,2048]{1,0:T(8,128)(2,1)S(1)} %get-tuple-element.31), channel_id=1, source_target_pairs={{0,8},{4,12},{8,0},{12,4},{1,9},{5,13},{9,1},{13,5},{2,10},{6,14},... | collective-permute-start | bytes 196616 | tf_op jit(solution)/shard_map/ppermute | solution.py:403
  25.2 2.2 %collective-permute-start.7 = (bf16[16,2048]{1,0:T(8,128)(2,1)S(1)}, bf16[16,2048]{1,0:T(8,128)(2,1)S(1)}, u32[]{:S(2)}, u32[]{:S(2)}) collective-permute-start(bf16[16,2048]{1,0:T(8,128)(2,1)S(1)} %get-tuple-element.32), channel_id=1, source_target_pairs={{0,12},{4,8},{8,4},{12,0},{1,13},{5,9},{9,5},{13,1},{2,14},{6,10},... | collective-permute-start | bytes 196616 | tf_op jit(solution)/shard_map/ppermute | solution.py:403
  27.4 1.6 %cache_part.1 = (f32[8,4096]{1,0:T(8,128)S(1)}, f32[8,4096]{1,0:T(8,128)S(1)}, f32[8,4096]{1,0:T(8,128)S(1)}) custom-call(s32[1,1,8]{2,1,0:T(1,128)S(1)} %copy-done.4, bf16[8,4096]{1,0:T(8,128)(2,1)S(1)} %bitcast.8, bf16[8,128,1024]{2,1,0:T(8,128)(2,1)S(1)} %bitcast.6, s32[8,128]{1,0:T(8,128)S(1)} %copy-done.3), custom_call_target="tpu_custom_call" | custom-call | flops 16777216 | bytes 2097152 | tf_op jit(solution)/shard_map/cache_part/pallas_call | solution.py:171
  29.0 0.1 combine_stats.1
  29.1 2.1 %collective-permute-done.7.refs_3_ = bf16[16,2048]{1,0:T(8,128)(2,1)S(1)} collective-permute-done((bf16[16,2048]{1,0:T(8,128)(2,1)S(1)}, bf16[16,2048]{1,0:T(8,128)(2,1)S(1)}, u32[]{:S(2)}, u32[]{:S(2)}) %collective-permute-start.7) | collective-permute-done | bytes 65568 | tf_op jit(solution)/shard_map/ppermute | solution.py:403
  31.3 1.6 %collective-permute-start.8 = (bf16[8,4352]{1,0:T(8,128)(2,1)S(1)}, bf16[8,4352]{1,0:T(8,128)(2,1)S(1)}, u32[]{:S(2)}, u32[]{:S(2)}) collective-permute-start(bf16[8,4352]{1,0:T(8,128)(2,1)S(1)} %merge.1.own_ref), channel_id=1, source_target_pairs={{0,2},{2,0},{1,3},{3,1},{4,6},{6,4},{5,7},{7,5},{8,10},{10,8},{9,1... | collective-permute-start | bytes 208904 | tf_op jit(solution)/shard_map/ppermute | solution.py:403
  32.9 2.8 %collective-permute-done.8.far_ref = bf16[8,4352]{1,0:T(8,128)(2,1)S(1)} collective-permute-done((bf16[8,4352]{1,0:T(8,128)(2,1)S(1)}, bf16[8,4352]{1,0:T(8,128)(2,1)S(1)}, u32[]{:S(2)}, u32[]{:S(2)}) %collective-permute-start.8) | collective-permute-done | bytes 69664 | tf_op jit(solution)/shard_map/ppermute | solution.py:403
  35.7 0.9 %finish.1 = bf16[8,4096]{1,0:T(8,128)(2,1)} custom-call(bf16[8,4352]{1,0:T(8,128)(2,1)S(1)} %merge.1.own_ref, bf16[8,4352]{1,0:T(8,128)(2,1)S(1)} %collective-permute-done.8.far_ref), custom_call_target="tpu_custom_call" | custom-call | tf_op jit(solution)/shard_map/finish/pallas_call | solution.py:393
  (18 shorter events, 0.1 us)
Async XLA Ops:
  0.0 6.8 %slice-start = ((s8[8388608]{0:T(1024)(128)(4,1)}), s8[4194304]{0:T(1024)(128)(4,1)S(1)}, s32[]{:S(2)}) async-start(s8[8388608]{0:T(1024)(128)(4,1)} %bitcast.4), calls=%async_computation | async-start | bytes 8388608
  0.0 6.8 %slice-start.1 = ((s8[8388608]{0:T(1024)(128)(4,1)}), s8[4194304]{0:T(1024)(128)(4,1)S(1)}, s32[]{:S(2)}) async-start(s8[8388608]{0:T(1024)(128)(4,1)} %bitcast.4), calls=%async_computation.1 | async-start | bytes 8388608
  0.0 6.8 %copy-start.1 = (bf16[256,4096]{1,0:T(8,128)(2,1)S(1)}, bf16[256,4096]{1,0:T(8,128)(2,1)}, u32[]{:S(2)}) copy-start(bf16[256,4096]{1,0:T(8,128)(2,1)} %tokens_ref.1) | copy-start | bytes 6291460
  1.1 26.3 %copy-start.2 = (bf16[1,1,8,4096]{3,2,1,0:T(8,128)(2,1)S(1)}, bf16[1,1,8,4096]{3,2,1,0:T(8,128)(2,1)}, u32[]{:S(2)}) copy-start(bf16[1,1,8,4096]{3,2,1,0:T(8,128)(2,1)} %param.13) | copy-start | bytes 196612
  1.1 26.3 %copy-start.3 = (s32[8,128]{1,0:T(8,128)S(1)}, s32[8,128]{1,0:T(8,128)}, u32[]{:S(2)}) copy-start(s32[8,128]{1,0:T(8,128)} %signs_ref.1) | copy-start | bytes 12292
  1.1 26.3 %copy-start.4 = (s32[1,1,8]{2,1,0:T(1,128)S(1)}, s32[1,1,8]{2,1,0:T(1,128)}, u32[]{:S(2)}) copy-start(s32[1,1,8]{2,1,0:T(1,128)} %lengths_ref.1) | copy-start | bytes 100
  1.1 8.1 %collective-permute-start = (bf16[8,4352]{1,0:T(8,128)(2,1)S(1)}, bf16[8,4352]{1,0:T(8,128)(2,1)S(1)}, u32[]{:S(2)}, u32[]{:S(2)}) collective-permute-start(bf16[8,4352]{1,0:T(8,128)(2,1)S(1)} %make_message.1.refs_0_), channel_id=1, source_target_pairs={{0,4},{4,0},{8,12},{12,8},{1,5},{5,1},{9,13},{13,9},{2,6},{6,2},{1... | collective-permute-start | bytes 208904 | tf_op jit(solution)/shard_map/ppermute | solution.py:403
  4.2 7.5 %collective-permute-start.1 = (bf16[8,4352]{1,0:T(8,128)(2,1)S(1)}, bf16[8,4352]{1,0:T(8,128)(2,1)S(1)}, u32[]{:S(2)}, u32[]{:S(2)}) collective-permute-start(bf16[8,4352]{1,0:T(8,128)(2,1)S(1)} %make_message.1.refs_0_), channel_id=1, source_target_pairs={{0,8},{4,12},{8,0},{12,4},{1,9},{5,13},{9,1},{13,5},{2,10},{6,14},... | collective-permute-start | bytes 208904 | tf_op jit(solution)/shard_map/ppermute | solution.py:403
  6.8 6.2 %collective-permute-start.2 = (bf16[8,4352]{1,0:T(8,128)(2,1)S(1)}, bf16[8,4352]{1,0:T(8,128)(2,1)S(1)}, u32[]{:S(2)}, u32[]{:S(2)}) collective-permute-start(bf16[8,4352]{1,0:T(8,128)(2,1)S(1)} %make_message.1.refs_0_), channel_id=1, source_target_pairs={{0,12},{4,8},{8,4},{12,0},{1,13},{5,9},{9,5},{13,1},{2,14},{6,10},... | collective-permute-start | bytes 208904 | tf_op jit(solution)/shard_map/ppermute | solution.py:403
  6.9 20.5 %copy-start = (bf16[1,1,8,128,1024]{4,3,2,1,0:T(8,128)(2,1)S(1)}, bf16[1,1,8,128,1024]{4,3,2,1,0:T(8,128)(2,1)}, u32[]{:S(2)}) copy-start(bf16[1,1,8,128,1024]{4,3,2,1,0:T(8,128)(2,1)} %param.14) | copy-start | bytes 6291460
  13.4 4.0 %collective-permute-start.3 = (f32[32,256]{1,0:T(8,128)S(1)}, f32[32,256]{1,0:T(8,128)S(1)}, u32[]{:S(2)}, u32[]{:S(2)}) collective-permute-start(f32[32,256]{1,0:T(8,128)S(1)} %get-tuple-element.22.left_ref), channel_id=1, source_target_pairs={{0,4},{4,0},{8,12},{12,8},{1,5},{5,1},{9,13},{13,9},{2,6},{6,2},{1... | collective-permute-start | bytes 98312 | tf_op jit(solution)/shard_map/ppermute | solution.py:403
  17.4 5.2 %collective-permute-start.4 = (f32[32,256]{1,0:T(8,128)S(1)}, f32[32,256]{1,0:T(8,128)S(1)}, u32[]{:S(2)}, u32[]{:S(2)}) collective-permute-start(f32[32,256]{1,0:T(8,128)S(1)} %add.1.near_ref), channel_id=1, source_target_pairs={{0,8},{4,12},{8,0},{12,4},{1,9},{5,13},{9,1},{13,5},{2,10},{6,14},... | collective-permute-start | bytes 98312 | tf_op jit(solution)/shard_map/ppermute | solution.py:403
  22.9 6.2 %collective-permute-start.5 = (bf16[16,2048]{1,0:T(8,128)(2,1)S(1)}, bf16[16,2048]{1,0:T(8,128)(2,1)S(1)}, u32[]{:S(2)}, u32[]{:S(2)}) collective-permute-start(bf16[16,2048]{1,0:T(8,128)(2,1)S(1)} %get-tuple-element.30), channel_id=1, source_target_pairs={{0,4},{4,0},{8,12},{12,8},{1,5},{5,1},{9,13},{13,9},{2,6},{6,2},{1... | collective-permute-start | bytes 196616 | tf_op jit(solution)/shard_map/ppermute | solution.py:403
  23.5 5.6 %collective-permute-start.6 = (bf16[16,2048]{1,0:T(8,128)(2,1)S(1)}, bf16[16,2048]{1,0:T(8,128)(2,1)S(1)}, u32[]{:S(2)}, u32[]{:S(2)}) collective-permute-start(bf16[16,2048]{1,0:T(8,128)(2,1)S(1)} %get-tuple-element.31), channel_id=1, source_target_pairs={{0,8},{4,12},{8,0},{12,4},{1,9},{5,13},{9,1},{13,5},{2,10},{6,14},... | collective-permute-start | bytes 196616 | tf_op jit(solution)/shard_map/ppermute | solution.py:403
  25.2 6.1 %collective-permute-start.7 = (bf16[16,2048]{1,0:T(8,128)(2,1)S(1)}, bf16[16,2048]{1,0:T(8,128)(2,1)S(1)}, u32[]{:S(2)}, u32[]{:S(2)}) collective-permute-start(bf16[16,2048]{1,0:T(8,128)(2,1)S(1)} %get-tuple-element.32), channel_id=1, source_target_pairs={{0,12},{4,8},{8,4},{12,0},{1,13},{5,9},{9,5},{13,1},{2,14},{6,10},... | collective-permute-start | bytes 196616 | tf_op jit(solution)/shard_map/ppermute | solution.py:403
  31.3 4.4 %collective-permute-start.8 = (bf16[8,4352]{1,0:T(8,128)(2,1)S(1)}, bf16[8,4352]{1,0:T(8,128)(2,1)S(1)}, u32[]{:S(2)}, u32[]{:S(2)}) collective-permute-start(bf16[8,4352]{1,0:T(8,128)(2,1)S(1)} %merge.1.own_ref), channel_id=1, source_target_pairs={{0,2},{2,0},{1,3},{3,1},{4,6},{6,4},{5,7},{7,5},{8,10},{10,8},{9,1... | collective-permute-start | bytes 208904 | tf_op jit(solution)/shard_map/ppermute | solution.py:403

commit v5 on v4

--- a/solution.py
+++ b/solution.py
@@ -33,6 +33,10 @@
     for bit_number in range(order.bit_length() - 1):
         parity = parity ^ (common >> bit_number)
     return (1 - 2 * (parity & 1)).astype(jnp.float32).astype(jnp.bfloat16)
+
+
+def far_first(blocks):
+    return [blocks[0]] + list(blocks[:0:-1])
 
 
 def project_kernel(tokens_ref, weight_ref, out_ref):
@@ -60,7 +64,6 @@
 def message_kernel(query_ref, owners_ref, requests_ref, out_ref, query_buf, owners_buf, requests_buf, sems):
     requests, columns = query_ref.shape
     per_device = owners_ref.shape[1]
-    tokens = out_ref.shape[1] - columns
     copies = [
         pltpu.make_async_copy(source, target, sems.at[i])
         for i, (source, target) in enumerate(
@@ -73,21 +76,19 @@
         copy.wait()
     out_ref[:, :columns] = query_buf[...]
     code = (owners_buf[...] * requests + requests_buf[...]).astype(jnp.float32)
-    spread = jnp.concatenate([code] * (tokens // per_device), axis=1)
-    spread = jnp.broadcast_to(spread, (requests, tokens))
-    start = lax.axis_index("seq") * per_device
-    lane = lax.broadcasted_iota(jnp.int32, spread.shape, 1)
-    mine = (lane >= start) & (lane < start + per_device)
-    out_ref[:, columns:] = jnp.where(mine, spread, 0.0).astype(out_ref.dtype)
-
-
-def make_message(query, owners, requests, tokens):
+    spare = jnp.zeros((1, out_ref.shape[1] - columns - per_device), jnp.float32)
+    code = jnp.concatenate([code, spare], axis=1)
+    out_ref[:, columns:] = jnp.broadcast_to(code, (requests, code.shape[1])).astype(out_ref.dtype)
+
+
+def make_message(query, owners, requests):
     count, columns = query.shape
+    lanes = -(-owners.shape[1] // 128) * 128
     return pl.pallas_call(
         message_kernel,
         in_specs=[pl.BlockSpec(memory_space=pl.ANY)] * 3,
         out_specs=pl.BlockSpec(memory_space=pltpu.VMEM),
-        out_shape=jax.ShapeDtypeStruct((count, columns + tokens), query.dtype),
+        out_shape=jax.ShapeDtypeStruct((count, columns + lanes), query.dtype),
         scratch_shapes=[
             pltpu.VMEM(query.shape, query.dtype),
             pltpu.VMEM(owners.shape, owners.dtype),
@@ -221,20 +222,22 @@
     )(tops, totals, new_tops, new_totals, cache_mixed)
 
 
-def code_row(message_refs, start, requests):
-    code = sum(ref[0:1, start:].astype(jnp.float32) for ref in message_refs).astype(jnp.int32)
+def code_row(message_refs, start, requests, tokens):
+    count = len(message_refs)
     me = lax.axis_index("seq")
+    pieces = [ref[0:1, start : start + tokens // count].astype(jnp.float32) for ref in message_refs]
+    row = [sum(jnp.where(me ^ d == at, pieces[d], 0.0) for d in range(count)) for at in range(count)]
+    code = jnp.concatenate(row, axis=1).astype(jnp.int32)
     return ((code // requests) ^ me) * requests + code % requests
 
 
-def score_kernel(heads, partial_ref, *refs):
-    message_refs, (scores_ref, code_ref) = refs[:-2], refs[-2:]
+def score_kernel(heads, start, partial_ref, *refs):
+    message_refs, (scores_ref, code_ref) = far_first(refs[:-2]), refs[-2:]
     requests = message_refs[0].shape[0]
     size = partial_ref.shape[1] // heads
     tokens = partial_ref.shape[0]
-    start = message_refs[0].shape[1] - tokens
     group = start // (heads * size)
-    code = code_row(message_refs, start, requests)
+    code = code_row(message_refs, start, requests, tokens)
     code_ref[...] = jnp.broadcast_to(code, code_ref.shape)
     span = len(message_refs) * requests
     here = lax.broadcasted_iota(jnp.int32, (span, tokens), 0) == code
@@ -256,12 +259,12 @@
         )
 
 
-def partial_scores(heads, width, partials, messages):
+def partial_scores(heads, width, columns, partials, messages):
     tokens = partials.shape[0]
     size = width // heads
-    query_heads = (messages[0].shape[1] - tokens) // size
-    return pl.pallas_call(
-        functools.partial(score_kernel, heads),
+    query_heads = columns // size
+    return pl.pallas_call(
+        functools.partial(score_kernel, heads, columns),
         grid=(1,),
         in_specs=[pl.BlockSpec((tokens, width), lambda i: (0, 0))]
         + [pl.BlockSpec(m.shape, lambda i: (0, 0)) for m in messages],
@@ -275,31 +278,23 @@
         ],
         compiler_params=params(),
         name="partial_scores",
-    )(partials, *messages)
-
-
-def add_kernel(left_ref, right_ref, out_ref):
-    out_ref[...] = left_ref[...] + right_ref[...]
-
-
-def add(left, right):
-    return pl.pallas_call(
-        add_kernel,
-        out_shape=jax.ShapeDtypeStruct(left.shape, left.dtype),
-        compiler_params=params(),
-        name="add",
-    )(left, right)
-
-
-def mix_kernel(heads, count, code_ref, values_ref, near_ref, far_ref, *refs):
-    mixed_refs, (tops_ref, totals_ref) = refs[:count], refs[count:]
+    )(partials, *far_first(messages))
+
+
+def mix_kernel(heads, count, code_ref, values_ref, *refs):
+    score_refs = far_first(refs[:count])
+    mixed_refs = refs[count : 2 * count]
+    tops_ref, totals_ref = refs[2 * count :]
     tokens = values_ref.shape[0]
     size = values_ref.shape[1] // heads
     requests = tops_ref.shape[0]
-    group = near_ref.shape[0] // heads
+    group = score_refs[0].shape[0] // heads
     span = count * requests
     here = lax.broadcasted_iota(jnp.int32, (span, tokens), 0) == code_ref[0:1, :]
-    scores = near_ref[...] + far_ref[...]
+    parts = [ref[...] for ref in score_refs]
+    while len(parts) > 1:
+        parts = [parts[i] + parts[i + 1] for i in range(0, len(parts), 2)]
+    scores = parts[0]
     mixed = []
     for k in range(heads):
         weights = []
@@ -326,7 +321,8 @@
                 mixed_refs[d][:, at : at + size] = pair.astype(jnp.bfloat16)
 
 
-def mix(heads, width, requests, count, code, partials, scores):
+def mix(heads, width, requests, code, partials, scores):
+    count = len(scores)
     tokens = partials.shape[0]
     columns = scores[0].shape[0] * (width // heads)
     whole = lambda shape: pl.BlockSpec(shape, lambda i: (0, 0))
@@ -340,7 +336,7 @@
         + [jax.ShapeDtypeStruct((requests, columns), jnp.float32)] * 2,
         compiler_params=params(),
         name="mix",
-    )(code, partials, *scores)
+    )(code, partials, *far_first(scores))
 
 
 def merge_kernel(count, cache_ref, stats_ref, factor_ref, *refs):
@@ -362,7 +358,7 @@
         out_shape=jax.ShapeDtypeStruct((requests, columns + stats.shape[1]), jnp.bfloat16),
         compiler_params=params(),
         name="merge",
-    )(cache_mixed, stats, factor, *mixed)
+    )(cache_mixed, stats, factor, *far_first(mixed))
 
 
 def finish_kernel(own_ref, far_ref, out_ref):
@@ -403,6 +399,10 @@
     return lax.ppermute(x, axis, [(i, i ^ distance) for i in range(count)])
 
 
+def exchange(blocks):
+    return [blocks[0]] + [from_partner(blocks[d], "seq", d) for d in range(1, len(blocks))]
+
+
 def on_device(tokens, kv_weight, owners, requests, signs, queries, kv_cache, lengths):
     seq_count = lax.axis_size("seq")
     blocks, size = signs.shape
@@ -410,19 +410,15 @@
     width = heads * size
     query = queries[0, 0]
     request_count, columns = query.shape
-    message = make_message(query, owners[:, :, 0], requests, tokens.shape[0])
-    messages = [message] + [from_partner(message, "seq", d) for d in range(1, seq_count)]
+    message = make_message(query, owners[:, :, 0], requests)
+    messages = exchange([message] * seq_count)
     partials = project(tokens, kv_weight)
-    scores, code = partial_scores(heads, width, partials, messages)
-    distance = 1
-    while distance < seq_count // 2:
-        scores = add(scores, from_partner(scores, "seq", distance))
-        distance *= 2
-    scores = (scores, from_partner(scores, "seq", distance))
+    scores, code = partial_scores(heads, width, columns, partials, messages)
+    scores = exchange([scores] * seq_count)
     cache_mixed, tops, totals = cache_part(lengths, query, kv_cache[0, 0], signs)
-    results = mix(heads, width, request_count, seq_count, code, partials, scores)
+    results = mix(heads, width, request_count, code, partials, scores)
     mixed, (new_tops, new_totals) = results[:seq_count], results[seq_count:]
-    mixed = [mixed[0]] + [from_partner(mixed[d], "seq", d) for d in range(1, seq_count)]
+    mixed = exchange(mixed)
     cache_mixed, factor, stats = combine_stats(tops, totals, new_tops, new_totals, cache_mixed)
     own = merge(cache_mixed, stats, factor, mixed)
     far = from_partner(own, "tp", 1)

time: 36.7 us -> 33.5 us (0.913)
  waiting for transfers between devices: 15 us -> 10.3 us
  starting transfers between devices: 14.6 us -> 16.2 us
    ppermute x9 -> x10, waiting for transfers between devices: 15 us -> 10.3 us  [from_partner(): return lax.ppermute(x, axis, [(i, i ^ distance) for i in range(count)])]
    ppermute x9 -> x10, starting transfers between devices: 14.6 us -> 16.2 us  [from_partner(): return lax.ppermute(x, axis, [(i, i ^ distance) for i in range(count)])]
  transfers between devices with their start and end apart: 9 -> 10, of which waited for: 6 -> 5; matrix products, arithmetic and copies ran while one was open for 0% -> 0% of each run, Pallas kernels for 11% -> 12%
where the time goes in v5:
time: 33.5 us; the launch traced here: 33.3 us
  starting transfers between devices  16.2 us (48%)
  waiting for transfers between devices  10.3 us (31%)
  Pallas kernels  6.71 us (20%)
    ppermute x10, starting transfers between devices, from_partner(): return lax.ppermute(x, axis, [(i, i ^ distance) for i in range(count)])  16.2 us
    ppermute x10, waiting for transfers between devices, from_partner(): return lax.ppermute(x, axis, [(i, i ^ distance) for i in range(count)])  10.3 us
    pallas_call x1, Pallas kernels, project(): pl.pallas_call(project_kernel, in_specs=[pl.BlockSpec(memory_space=pltpu....  2.32 us
    pallas_call x1, Pallas kernels, cache_part(): pl.pallas_call(cache_kernel, in_specs=[pl.BlockSpec(memory_space=pltpu.SM...  1.61 us
    pallas_call x1, Pallas kernels, make_message(): pl.pallas_call(message_kernel, in_specs=[pl.BlockSpec(memory_space=pl.ANY...  1.03 us
    pallas_call x1, Pallas kernels, finish(): pl.pallas_call(finish_kernel, out_shape=jax.ShapeDtypeStruct((own.shape[0...  0.9 us
  transfers between devices with their start and end apart: 10, of which 5 were waited for; matrix products, arithmetic and copies ran while one was open for 0% of the time, Pallas kernels for 12%

profile of v5, /device:TPU:0, one launch (start us, length us, event | category | flops | bytes accessed | tf_op | source)
XLA Modules:
  0.0 33.3 jit_solution(879065799933323063)
XLA Ops:
  0.0 1.0 %make_message.1.refs_0_ = bf16[8,4224]{1,0:T(8,128)(2,1)S(1)} custom-call(bf16[8,4096]{1,0:T(8,128)(2,1)} %bitcast.7, s32[1,64]{1,0:T(1,128)} %bitcast.9, s32[1,64]{1,0:T(1,128)} %requests_ref.1), custom_call_target="tpu_custom_call" | custom-call | flops 99999997952 | bytes 10000 | tf_op jit(solution)/shard_map/make_message/pallas_call | solution.py:87
  1.0 0.0 copy-start.2
  1.1 0.0 copy-start.3
  1.1 0.0 copy-start.4
  1.1 5.1 %collective-permute-start = (bf16[8,4224]{1,0:T(8,128)(2,1)S(1)}, bf16[8,4224]{1,0:T(8,128)(2,1)S(1)}, u32[]{:S(2)}, u32[]{:S(2)}) collective-permute-start(bf16[8,4224]{1,0:T(8,128)(2,1)S(1)} %make_message.1.refs_0_), channel_id=1, source_target_pairs={{0,12},{4,8},{8,4},{12,0},{1,13},{5,9},{9,5},{13,1},{2,14},{6,10},... | collective-permute-start | bytes 202760 | tf_op jit(solution)/shard_map/ppermute | solution.py:399
  6.2 0.6 %collective-permute-start.2 = (bf16[8,4224]{1,0:T(8,128)(2,1)S(1)}, bf16[8,4224]{1,0:T(8,128)(2,1)S(1)}, u32[]{:S(2)}, u32[]{:S(2)}) collective-permute-start(bf16[8,4224]{1,0:T(8,128)(2,1)S(1)} %make_message.1.refs_0_), channel_id=1, source_target_pairs={{0,4},{4,0},{8,12},{12,8},{1,5},{5,1},{9,13},{13,9},{2,6},{6,2},{1... | collective-permute-start | bytes 202760 | tf_op jit(solution)/shard_map/ppermute | solution.py:399
  6.9 0.0 copy-start
  6.9 2.3 %project.1.partial_ref.values_ref = bf16[256,1024]{1,0:T(8,128)(2,1)S(1)} custom-call(bf16[256,4096]{1,0:T(8,128)(2,1)S(1)} %copy-done.1, bf16[4096,1024]{1,0:T(8,128)(2,1)S(1)} %bitcast.5), custom_call_target="tpu_custom_call" | custom-call | flops 2147483648 | bytes 10485760 | tf_op jit(solution)/shard_map/project/pallas_call | solution.py:49
  9.2 2.7 %collective-permute-done.1.refs_2_ = bf16[8,4224]{1,0:T(8,128)(2,1)S(1)} collective-permute-done((bf16[8,4224]{1,0:T(8,128)(2,1)S(1)}, bf16[8,4224]{1,0:T(8,128)(2,1)S(1)}, u32[]{:S(2)}, u32[]{:S(2)}) %collective-permute-start.1) | collective-permute-done | bytes 67616 | tf_op jit(solution)/shard_map/ppermute | solution.py:399
  12.0 0.3 partial_scores.1
  12.3 2.8 %collective-permute-start.3 = (f32[32,256]{1,0:T(8,128)S(1)}, f32[32,256]{1,0:T(8,128)S(1)}, u32[]{:S(2)}, u32[]{:S(2)}) collective-permute-start(f32[32,256]{1,0:T(8,128)S(1)} %get-tuple-element.22.refs_0_), channel_id=1, source_target_pairs={{0,12},{4,8},{8,4},{12,0},{1,13},{5,9},{9,5},{13,1},{2,14},{6,10},... | collective-permute-start | bytes 98312 | tf_op jit(solution)/shard_map/ppermute | solution.py:399
  15.1 1.7 %collective-permute-start.5 = (f32[32,256]{1,0:T(8,128)S(1)}, f32[32,256]{1,0:T(8,128)S(1)}, u32[]{:S(2)}, u32[]{:S(2)}) collective-permute-start(f32[32,256]{1,0:T(8,128)S(1)} %get-tuple-element.22.refs_0_), channel_id=1, source_target_pairs={{0,4},{4,0},{8,12},{12,8},{1,5},{5,1},{9,13},{13,9},{2,6},{6,2},{1... | collective-permute-start | bytes 98312 | tf_op jit(solution)/shard_map/ppermute | solution.py:399
  16.7 1.4 %collective-permute-done.3.refs_1_ = f32[32,256]{1,0:T(8,128)S(1)} collective-permute-done((f32[32,256]{1,0:T(8,128)S(1)}, f32[32,256]{1,0:T(8,128)S(1)}, u32[]{:S(2)}, u32[]{:S(2)}) %collective-permute-start.3) | collective-permute-done | bytes 32800 | tf_op jit(solution)/shard_map/ppermute | solution.py:399
  18.2 1.7 %collective-permute-done.4.refs_2_ = f32[32,256]{1,0:T(8,128)S(1)} collective-permute-done((f32[32,256]{1,0:T(8,128)S(1)}, f32[32,256]{1,0:T(8,128)S(1)}, u32[]{:S(2)}, u32[]{:S(2)}) %collective-permute-start.4) | collective-permute-done | bytes 32800 | tf_op jit(solution)/shard_map/ppermute | solution.py:399
  19.9 0.4 %mix.1 = (bf16[16,2048]{1,0:T(8,128)(2,1)S(1)}, bf16[16,2048]{1,0:T(8,128)(2,1)S(1)}, bf16[16,2048]{1,0:T(8,128)(2,1)S(1)}, bf16[16,2048]{1,0:T(8,128)(2,1)S(1)}...) custom-call(s32[8,256]{1,0:T(8,128)S(1)} %get-tuple-element.21.code_ref, ...), custom_call_target="tpu_custom_call" | custom-call | tf_op jit(solution)/shard_map/mix/pallas_call | solution.py:329
  20.3 1.8 %collective-permute-start.6 = (bf16[16,2048]{1,0:T(8,128)(2,1)S(1)}, bf16[16,2048]{1,0:T(8,128)(2,1)S(1)}, u32[]{:S(2)}, u32[]{:S(2)}) collective-permute-start(bf16[16,2048]{1,0:T(8,128)(2,1)S(1)} %get-tuple-element.30), channel_id=1, source_target_pairs={{0,12},{4,8},{8,4},{12,0},{1,13},{5,9},{9,5},{13,1},{2,14},{6,10},... | collective-permute-start | bytes 196616 | tf_op jit(solution)/shard_map/ppermute | solution.py:399
  22.1 0.4 %collective-permute-start.7 = (bf16[16,2048]{1,0:T(8,128)(2,1)S(1)}, bf16[16,2048]{1,0:T(8,128)(2,1)S(1)}, u32[]{:S(2)}, u32[]{:S(2)}) collective-permute-start(bf16[16,2048]{1,0:T(8,128)(2,1)S(1)} %get-tuple-element.31), channel_id=1, source_target_pairs={{0,8},{4,12},{8,0},{12,4},{1,9},{5,13},{9,1},{13,5},{2,10},{6,14},... | collective-permute-start | bytes 196616 | tf_op jit(solution)/shard_map/ppermute | solution.py:399
  22.6 2.2 %collective-permute-start.8 = (bf16[16,2048]{1,0:T(8,128)(2,1)S(1)}, bf16[16,2048]{1,0:T(8,128)(2,1)S(1)}, u32[]{:S(2)}, u32[]{:S(2)}) collective-permute-start(bf16[16,2048]{1,0:T(8,128)(2,1)S(1)} %get-tuple-element.32), channel_id=1, source_target_pairs={{0,4},{4,0},{8,12},{12,8},{1,5},{5,1},{9,13},{13,9},{2,6},{6,2},{1... | collective-permute-start | bytes 196616 | tf_op jit(solution)/shard_map/ppermute | solution.py:399
  24.8 1.6 %cache_part.1 = (f32[8,4096]{1,0:T(8,128)S(1)}, f32[8,4096]{1,0:T(8,128)S(1)}, f32[8,4096]{1,0:T(8,128)S(1)}) custom-call(s32[1,1,8]{2,1,0:T(1,128)S(1)} %copy-done.4, bf16[8,4096]{1,0:T(8,128)(2,1)S(1)} %bitcast.8, bf16[8,128,1024]{2,1,0:T(8,128)(2,1)S(1)} %bitcast.6, s32[8,128]{1,0:T(8,128)S(1)} %copy-done.3), custom_call_target="tpu_custom_call" | custom-call | flops 16777216 | bytes 2097152 | tf_op jit(solution)/shard_map/cache_part/pallas_call | solution.py:172
  26.4 0.1 combine_stats.1
  26.5 1.5 %collective-permute-done.7.refs_2_ = bf16[16,2048]{1,0:T(8,128)(2,1)S(1)} collective-permute-done((bf16[16,2048]{1,0:T(8,128)(2,1)S(1)}, bf16[16,2048]{1,0:T(8,128)(2,1)S(1)}, u32[]{:S(2)}, u32[]{:S(2)}) %collective-permute-start.7) | collective-permute-done | bytes 65568 | tf_op jit(solution)/shard_map/ppermute | solution.py:399
  28.1 1.6 %collective-permute-start.9 = (bf16[8,4352]{1,0:T(8,128)(2,1)S(1)}, bf16[8,4352]{1,0:T(8,128)(2,1)S(1)}, u32[]{:S(2)}, u32[]{:S(2)}) collective-permute-start(bf16[8,4352]{1,0:T(8,128)(2,1)S(1)} %merge.1.own_ref), channel_id=1, source_target_pairs={{0,2},{2,0},{1,3},{3,1},{4,6},{6,4},{5,7},{7,5},{8,10},{10,8},{9,1... | collective-permute-start | bytes 208904 | tf_op jit(solution)/shard_map/ppermute | solution.py:399
  29.6 2.8 %collective-permute-done.9.far_ref = bf16[8,4352]{1,0:T(8,128)(2,1)S(1)} collective-permute-done((bf16[8,4352]{1,0:T(8,128)(2,1)S(1)}, bf16[8,4352]{1,0:T(8,128)(2,1)S(1)}, u32[]{:S(2)}, u32[]{:S(2)}) %collective-permute-start.9) | collective-permute-done | bytes 69664 | tf_op jit(solution)/shard_map/ppermute | solution.py:399
  32.4 0.9 %finish.1 = bf16[8,4096]{1,0:T(8,128)(2,1)} custom-call(bf16[8,4352]{1,0:T(8,128)(2,1)S(1)} %merge.1.own_ref, bf16[8,4352]{1,0:T(8,128)(2,1)S(1)} %collective-permute-done.9.far_ref), custom_call_target="tpu_custom_call" | custom-call | tf_op jit(solution)/shard_map/finish/pallas_call | solution.py:389
  (19 shorter events, 0.1 us)
Async XLA Ops:
  0.0 6.8 %slice-start = ((s8[8388608]{0:T(1024)(128)(4,1)}), s8[4194304]{0:T(1024)(128)(4,1)S(1)}, s32[]{:S(2)}) async-start(s8[8388608]{0:T(1024)(128)(4,1)} %bitcast.4), calls=%async_computation | async-start | bytes 8388608
  0.0 6.8 %slice-start.1 = ((s8[8388608]{0:T(1024)(128)(4,1)}), s8[4194304]{0:T(1024)(128)(4,1)S(1)}, s32[]{:S(2)}) async-start(s8[8388608]{0:T(1024)(128)(4,1)} %bitcast.4), calls=%async_computation.1 | async-start | bytes 8388608
  0.0 6.8 %copy-start.1 = (bf16[256,4096]{1,0:T(8,128)(2,1)S(1)}, bf16[256,4096]{1,0:T(8,128)(2,1)}, u32[]{:S(2)}) copy-start(bf16[256,4096]{1,0:T(8,128)(2,1)} %tokens_ref.1) | copy-start | bytes 6291460
  1.0 23.7 %copy-start.2 = (bf16[1,1,8,4096]{3,2,1,0:T(8,128)(2,1)S(1)}, bf16[1,1,8,4096]{3,2,1,0:T(8,128)(2,1)}, u32[]{:S(2)}) copy-start(bf16[1,1,8,4096]{3,2,1,0:T(8,128)(2,1)} %param.13) | copy-start | bytes 196612
  1.1 23.7 %copy-start.3 = (s32[8,128]{1,0:T(8,128)S(1)}, s32[8,128]{1,0:T(8,128)}, u32[]{:S(2)}) copy-start(s32[8,128]{1,0:T(8,128)} %signs_ref.1) | copy-start | bytes 12292
  1.1 23.7 %copy-start.4 = (s32[1,1,8]{2,1,0:T(1,128)S(1)}, s32[1,1,8]{2,1,0:T(1,128)}, u32[]{:S(2)}) copy-start(s32[1,1,8]{2,1,0:T(1,128)} %lengths_ref.1) | copy-start | bytes 100
  1.1 8.1 %collective-permute-start = (bf16[8,4224]{1,0:T(8,128)(2,1)S(1)}, bf16[8,4224]{1,0:T(8,128)(2,1)S(1)}, u32[]{:S(2)}, u32[]{:S(2)}) collective-permute-start(bf16[8,4224]{1,0:T(8,128)(2,1)S(1)} %make_message.1.refs_0_), channel_id=1, source_target_pairs={{0,12},{4,8},{8,4},{12,0},{1,13},{5,9},{9,5},{13,1},{2,14},{6,10},... | collective-permute-start | bytes 202760 | tf_op jit(solution)/shard_map/ppermute | solution.py:399
  6.2 5.8 %collective-permute-start.1 = (bf16[8,4224]{1,0:T(8,128)(2,1)S(1)}, bf16[8,4224]{1,0:T(8,128)(2,1)S(1)}, u32[]{:S(2)}, u32[]{:S(2)}) collective-permute-start(bf16[8,4224]{1,0:T(8,128)(2,1)S(1)} %make_message.1.refs_0_), channel_id=1, source_target_pairs={{0,8},{4,12},{8,0},{12,4},{1,9},{5,13},{9,1},{13,5},{2,10},{6,14},... | collective-permute-start | bytes 202760 | tf_op jit(solution)/shard_map/ppermute | solution.py:399
  6.2 5.8 %collective-permute-start.2 = (bf16[8,4224]{1,0:T(8,128)(2,1)S(1)}, bf16[8,4224]{1,0:T(8,128)(2,1)S(1)}, u32[]{:S(2)}, u32[]{:S(2)}) collective-permute-start(bf16[8,4224]{1,0:T(8,128)(2,1)S(1)} %make_message.1.refs_0_), channel_id=1, source_target_pairs={{0,4},{4,0},{8,12},{12,8},{1,5},{5,1},{9,13},{13,9},{2,6},{6,2},{1... | collective-permute-start | bytes 202760 | tf_op jit(solution)/shard_map/ppermute | solution.py:399
  6.9 17.9 %copy-start = (bf16[1,1,8,128,1024]{4,3,2,1,0:T(8,128)(2,1)S(1)}, bf16[1,1,8,128,1024]{4,3,2,1,0:T(8,128)(2,1)}, u32[]{:S(2)}) copy-start(bf16[1,1,8,128,1024]{4,3,2,1,0:T(8,128)(2,1)} %param.14) | copy-start | bytes 6291460
  12.3 5.9 %collective-permute-start.3 = (f32[32,256]{1,0:T(8,128)S(1)}, f32[32,256]{1,0:T(8,128)S(1)}, u32[]{:S(2)}, u32[]{:S(2)}) collective-permute-start(f32[32,256]{1,0:T(8,128)S(1)} %get-tuple-element.22.refs_0_), channel_id=1, source_target_pairs={{0,12},{4,8},{8,4},{12,0},{1,13},{5,9},{9,5},{13,1},{2,14},{6,10},... | collective-permute-start | bytes 98312 | tf_op jit(solution)/shard_map/ppermute | solution.py:399
  15.1 4.8 %collective-permute-start.4 = (f32[32,256]{1,0:T(8,128)S(1)}, f32[32,256]{1,0:T(8,128)S(1)}, u32[]{:S(2)}, u32[]{:S(2)}) collective-permute-start(f32[32,256]{1,0:T(8,128)S(1)} %get-tuple-element.22.refs_0_), channel_id=1, source_target_pairs={{0,8},{4,12},{8,0},{12,4},{1,9},{5,13},{9,1},{13,5},{2,10},{6,14},... | collective-permute-start | bytes 98312 | tf_op jit(solution)/shard_map/ppermute | solution.py:399
  15.1 4.8 %collective-permute-start.5 = (f32[32,256]{1,0:T(8,128)S(1)}, f32[32,256]{1,0:T(8,128)S(1)}, u32[]{:S(2)}, u32[]{:S(2)}) collective-permute-start(f32[32,256]{1,0:T(8,128)S(1)} %get-tuple-element.22.refs_0_), channel_id=1, source_target_pairs={{0,4},{4,0},{8,12},{12,8},{1,5},{5,1},{9,13},{13,9},{2,6},{6,2},{1... | collective-permute-start | bytes 98312 | tf_op jit(solution)/shard_map/ppermute | solution.py:399
  20.3 6.2 %collective-permute-start.6 = (bf16[16,2048]{1,0:T(8,128)(2,1)S(1)}, bf16[16,2048]{1,0:T(8,128)(2,1)S(1)}, u32[]{:S(2)}, u32[]{:S(2)}) collective-permute-start(bf16[16,2048]{1,0:T(8,128)(2,1)S(1)} %get-tuple-element.30), channel_id=1, source_target_pairs={{0,12},{4,8},{8,4},{12,0},{1,13},{5,9},{9,5},{13,1},{2,14},{6,10},... | collective-permute-start | bytes 196616 | tf_op jit(solution)/shard_map/ppermute | solution.py:399
  22.1 5.9 %collective-permute-start.7 = (bf16[16,2048]{1,0:T(8,128)(2,1)S(1)}, bf16[16,2048]{1,0:T(8,128)(2,1)S(1)}, u32[]{:S(2)}, u32[]{:S(2)}) collective-permute-start(bf16[16,2048]{1,0:T(8,128)(2,1)S(1)} %get-tuple-element.31), channel_id=1, source_target_pairs={{0,8},{4,12},{8,0},{12,4},{1,9},{5,13},{9,1},{13,5},{2,10},{6,14},... | collective-permute-start | bytes 196616 | tf_op jit(solution)/shard_map/ppermute | solution.py:399
  22.6 5.4 %collective-permute-start.8 = (bf16[16,2048]{1,0:T(8,128)(2,1)S(1)}, bf16[16,2048]{1,0:T(8,128)(2,1)S(1)}, u32[]{:S(2)}, u32[]{:S(2)}) collective-permute-start(bf16[16,2048]{1,0:T(8,128)(2,1)S(1)} %get-tuple-element.32), channel_id=1, source_target_pairs={{0,4},{4,0},{8,12},{12,8},{1,5},{5,1},{9,13},{13,9},{2,6},{6,2},{1... | collective-permute-start | bytes 196616 | tf_op jit(solution)/shard_map/ppermute | solution.py:399
  28.1 4.4 %collective-permute-start.9 = (bf16[8,4352]{1,0:T(8,128)(2,1)S(1)}, bf16[8,4352]{1,0:T(8,128)(2,1)S(1)}, u32[]{:S(2)}, u32[]{:S(2)}) collective-permute-start(bf16[8,4352]{1,0:T(8,128)(2,1)S(1)} %merge.1.own_ref), channel_id=1, source_target_pairs={{0,2},{2,0},{1,3},{3,1},{4,6},{6,4},{5,7},{7,5},{8,10},{10,8},{9,1... | collective-permute-start | bytes 208904 | tf_op jit(solution)/shard_map/ppermute | solution.py:399

commit v6 on v5

--- a/solution.py
+++ b/solution.py
@@ -35,8 +35,17 @@
     return (1 - 2 * (parity & 1)).astype(jnp.float32).astype(jnp.bfloat16)
 
 
-def far_first(blocks):
-    return [blocks[0]] + list(blocks[:0:-1])
+QUERY_ORDER = (3, 2, 1)
+SCORE_ORDER = (2, 3, 1)
+MIXED_ORDER = (3, 1, 2)
+
+
+def arranged(blocks, order):
+    return [blocks[0]] + [blocks[d] for d in order]
+
+
+def by_distance(refs, order):
+    return [refs[0]] + [refs[1 + order.index(d)] for d in range(1, len(refs))]
 
 
 def project_kernel(tokens_ref, weight_ref, out_ref):
@@ -232,7 +241,7 @@
 
 
 def score_kernel(heads, start, partial_ref, *refs):
-    message_refs, (scores_ref, code_ref) = far_first(refs[:-2]), refs[-2:]
+    message_refs, (scores_ref, code_ref) = by_distance(refs[:-2], QUERY_ORDER), refs[-2:]
     requests = message_refs[0].shape[0]
     size = partial_ref.shape[1] // heads
     tokens = partial_ref.shape[0]
@@ -278,11 +287,11 @@
         ],
         compiler_params=params(),
         name="partial_scores",
-    )(partials, *far_first(messages))
+    )(partials, *arranged(messages, QUERY_ORDER))
 
 
 def mix_kernel(heads, count, code_ref, values_ref, *refs):
-    score_refs = far_first(refs[:count])
+    score_refs = by_distance(refs[:count], SCORE_ORDER)
     mixed_refs = refs[count : 2 * count]
     tops_ref, totals_ref = refs[2 * count :]
     tokens = values_ref.shape[0]
@@ -336,7 +345,7 @@
         + [jax.ShapeDtypeStruct((requests, columns), jnp.float32)] * 2,
         compiler_params=params(),
         name="mix",
-    )(code, partials, *far_first(scores))
+    )(code, partials, *arranged(scores, SCORE_ORDER))
 
 
 def merge_kernel(count, cache_ref, stats_ref, factor_ref, *refs):
@@ -358,7 +367,7 @@
         out_shape=jax.ShapeDtypeStruct((requests, columns + stats.shape[1]), jnp.bfloat16),
         compiler_params=params(),
         name="merge",
-    )(cache_mixed, stats, factor, *far_first(mixed))
+    )(cache_mixed, stats, factor, *arranged(mixed, MIXED_ORDER))
 
 
 def finish_kernel(own_ref, far_ref, out_ref):

time: 33.5 us -> 33.3 us (level)
  starting transfers between devices: 16.2 us -> 15.3 us
  waiting for transfers between devices: 10.3 us -> 11 us
    ppermute x10, starting transfers between devices: 16.2 us -> 15.3 us  [from_partner(): return lax.ppermute(x, axis, [(i, i ^ distance) for i in range(count)])]
    ppermute x10, waiting for transfers between devices: 10.3 us -> 11 us  [from_partner(): return lax.ppermute(x, axis, [(i, i ^ distance) for i in range(count)])]
  transfers between devices with their start and end apart: 10 -> 10, of which waited for: 5 -> 6; matrix products, arithmetic and copies ran while one was open for 0% -> 0% of each run, Pallas kernels for 12% -> 12%
where the time goes in v6:
time: 33.3 us; the launch traced here: 33.1 us
  starting transfers between devices  15.3 us (46%)
  waiting for transfers between devices  11 us (33%)
  Pallas kernels  6.71 us (20%)
    ppermute x10, starting transfers between devices, from_partner(): return lax.ppermute(x, axis, [(i, i ^ distance) for i in range(count)])  15.3 us
    ppermute x10, waiting for transfers between devices, from_partner(): return lax.ppermute(x, axis, [(i, i ^ distance) for i in range(count)])  11 us
    pallas_call x1, Pallas kernels, project(): pl.pallas_call(project_kernel, in_specs=[pl.BlockSpec(memory_space=pltpu....  2.32 us
    pallas_call x1, Pallas kernels, cache_part(): pl.pallas_call(cache_kernel, in_specs=[pl.BlockSpec(memory_space=pltpu.SM...  1.61 us
    pallas_call x1, Pallas kernels, make_message(): pl.pallas_call(message_kernel, in_specs=[pl.BlockSpec(memory_space=pl.ANY...  1.03 us
    pallas_call x1, Pallas kernels, finish(): pl.pallas_call(finish_kernel, out_shape=jax.ShapeDtypeStruct((own.shape[0...  0.9 us
  transfers between devices with their start and end apart: 10, of which 6 were waited for; matrix products, arithmetic and copies ran while one was open for 0% of the time, Pallas kernels for 12%

profile of v6, /device:TPU:0, one launch (start us, length us, event | category | flops | bytes accessed | tf_op | source)
XLA Modules:
  0.0 33.1 jit_solution(713125563395535200)
XLA Ops:
  0.0 1.0 %make_message.1.refs_0_ = bf16[8,4224]{1,0:T(8,128)(2,1)S(1)} custom-call(bf16[8,4096]{1,0:T(8,128)(2,1)} %bitcast.7, s32[1,64]{1,0:T(1,128)} %bitcast.9, s32[1,64]{1,0:T(1,128)} %requests_ref.1), custom_call_target="tpu_custom_call" | custom-call | flops 99999997952 | bytes 10000 | tf_op jit(solution)/shard_map/make_message/pallas_call | solution.py:96
  1.0 0.0 copy-start.2
  1.1 0.0 copy-start.3
  1.1 5.1 %collective-permute-start = (bf16[8,4224]{1,0:T(8,128)(2,1)S(1)}, bf16[8,4224]{1,0:T(8,128)(2,1)S(1)}, u32[]{:S(2)}, u32[]{:S(2)}) collective-permute-start(bf16[8,4224]{1,0:T(8,128)(2,1)S(1)} %make_message.1.refs_0_), channel_id=1, source_target_pairs={{0,12},{4,8},{8,4},{12,0},{1,13},{5,9},{9,5},{13,1},{2,14},{6,10},... | collective-permute-start | bytes 202760 | tf_op jit(solution)/shard_map/ppermute | solution.py:408
  6.2 0.6 %collective-permute-start.2 = (bf16[8,4224]{1,0:T(8,128)(2,1)S(1)}, bf16[8,4224]{1,0:T(8,128)(2,1)S(1)}, u32[]{:S(2)}, u32[]{:S(2)}) collective-permute-start(bf16[8,4224]{1,0:T(8,128)(2,1)S(1)} %make_message.1.refs_0_), channel_id=1, source_target_pairs={{0,4},{4,0},{8,12},{12,8},{1,5},{5,1},{9,13},{13,9},{2,6},{6,2},{1... | collective-permute-start | bytes 202760 | tf_op jit(solution)/shard_map/ppermute | solution.py:408
  6.9 2.3 %project.1.partial_ref.values_ref = bf16[256,1024]{1,0:T(8,128)(2,1)S(1)} custom-call(bf16[256,4096]{1,0:T(8,128)(2,1)S(1)} %copy-done.1, bf16[4096,1024]{1,0:T(8,128)(2,1)S(1)} %bitcast.5), custom_call_target="tpu_custom_call" | custom-call | flops 2147483648 | bytes 10485760 | tf_op jit(solution)/shard_map/project/pallas_call | solution.py:58
  9.2 2.7 %collective-permute-done.1.refs_2_ = bf16[8,4224]{1,0:T(8,128)(2,1)S(1)} collective-permute-done((bf16[8,4224]{1,0:T(8,128)(2,1)S(1)}, bf16[8,4224]{1,0:T(8,128)(2,1)S(1)}, u32[]{:S(2)}, u32[]{:S(2)}) %collective-permute-start.1) | collective-permute-done | bytes 67616 | tf_op jit(solution)/shard_map/ppermute | solution.py:408
  12.0 0.3 partial_scores.1
  12.3 1.5 %collective-permute-start.3 = (f32[32,256]{1,0:T(8,128)S(1)}, f32[32,256]{1,0:T(8,128)S(1)}, u32[]{:S(2)}, u32[]{:S(2)}) collective-permute-start(f32[32,256]{1,0:T(8,128)S(1)} %get-tuple-element.22.refs_0_), channel_id=1, source_target_pairs={{0,8},{4,12},{8,0},{12,4},{1,9},{5,13},{9,1},{13,5},{2,10},{6,14},... | collective-permute-start | bytes 98312 | tf_op jit(solution)/shard_map/ppermute | solution.py:408
  13.8 2.0 %collective-permute-start.4 = (f32[32,256]{1,0:T(8,128)S(1)}, f32[32,256]{1,0:T(8,128)S(1)}, u32[]{:S(2)}, u32[]{:S(2)}) collective-permute-start(f32[32,256]{1,0:T(8,128)S(1)} %get-tuple-element.22.refs_0_), channel_id=1, source_target_pairs={{0,12},{4,8},{8,4},{12,0},{1,13},{5,9},{9,5},{13,1},{2,14},{6,10},... | collective-permute-start | bytes 98312 | tf_op jit(solution)/shard_map/ppermute | solution.py:408
  15.8 0.1 collective-permute-start.5
  15.8 1.4 %collective-permute-done.3.refs_1_ = f32[32,256]{1,0:T(8,128)S(1)} collective-permute-done((f32[32,256]{1,0:T(8,128)S(1)}, f32[32,256]{1,0:T(8,128)S(1)}, u32[]{:S(2)}, u32[]{:S(2)}) %collective-permute-start.3) | collective-permute-done | bytes 32800 | tf_op jit(solution)/shard_map/ppermute | solution.py:408
  17.2 2.3 %collective-permute-done.4.refs_2_ = f32[32,256]{1,0:T(8,128)S(1)} collective-permute-done((f32[32,256]{1,0:T(8,128)S(1)}, f32[32,256]{1,0:T(8,128)S(1)}, u32[]{:S(2)}, u32[]{:S(2)}) %collective-permute-start.4) | collective-permute-done | bytes 32800 | tf_op jit(solution)/shard_map/ppermute | solution.py:408
  19.5 0.3 %collective-permute-done.5.refs_3_ = f32[32,256]{1,0:T(8,128)S(1)} collective-permute-done((f32[32,256]{1,0:T(8,128)S(1)}, f32[32,256]{1,0:T(8,128)S(1)}, u32[]{:S(2)}, u32[]{:S(2)}) %collective-permute-start.5) | collective-permute-done | bytes 32800 | tf_op jit(solution)/shard_map/ppermute | solution.py:408
  19.9 0.4 %mix.1 = (bf16[16,2048]{1,0:T(8,128)(2,1)S(1)}, bf16[16,2048]{1,0:T(8,128)(2,1)S(1)}, bf16[16,2048]{1,0:T(8,128)(2,1)S(1)}, bf16[16,2048]{1,0:T(8,128)(2,1)S(1)}...) custom-call(s32[8,256]{1,0:T(8,128)S(1)} %get-tuple-element.21.code_ref, ...), custom_call_target="tpu_custom_call" | custom-call | tf_op jit(solution)/shard_map/mix/pallas_call | solution.py:338
  20.3 2.0 %collective-permute-start.6 = (bf16[16,2048]{1,0:T(8,128)(2,1)S(1)}, bf16[16,2048]{1,0:T(8,128)(2,1)S(1)}, u32[]{:S(2)}, u32[]{:S(2)}) collective-permute-start(bf16[16,2048]{1,0:T(8,128)(2,1)S(1)} %get-tuple-element.30), channel_id=1, source_target_pairs={{0,12},{4,8},{8,4},{12,0},{1,13},{5,9},{9,5},{13,1},{2,14},{6,10},... | collective-permute-start | bytes 196616 | tf_op jit(solution)/shard_map/ppermute | solution.py:408
  22.3 2.4 %collective-permute-start.8 = (bf16[16,2048]{1,0:T(8,128)(2,1)S(1)}, bf16[16,2048]{1,0:T(8,128)(2,1)S(1)}, u32[]{:S(2)}, u32[]{:S(2)}) collective-permute-start(bf16[16,2048]{1,0:T(8,128)(2,1)S(1)} %get-tuple-element.32), channel_id=1, source_target_pairs={{0,8},{4,12},{8,0},{12,4},{1,9},{5,13},{9,1},{13,5},{2,10},{6,14},... | collective-permute-start | bytes 196616 | tf_op jit(solution)/shard_map/ppermute | solution.py:408
  24.7 1.6 %cache_part.1 = (f32[8,4096]{1,0:T(8,128)S(1)}, f32[8,4096]{1,0:T(8,128)S(1)}, f32[8,4096]{1,0:T(8,128)S(1)}) custom-call(s32[1,1,8]{2,1,0:T(1,128)S(1)} %copy-done.4, bf16[8,4096]{1,0:T(8,128)(2,1)S(1)} %bitcast.8, bf16[8,128,1024]{2,1,0:T(8,128)(2,1)S(1)} %bitcast.6, s32[8,128]{1,0:T(8,128)S(1)} %copy-done.3), custom_call_target="tpu_custom_call" | custom-call | flops 16777216 | bytes 2097152 | tf_op jit(solution)/shard_map/cache_part/pallas_call | solution.py:181
  26.4 0.1 combine_stats.1
  26.4 0.0 collective-permute-done.6.refs_1_
  26.5 1.3 %collective-permute-done.7.refs_2_ = bf16[16,2048]{1,0:T(8,128)(2,1)S(1)} collective-permute-done((bf16[16,2048]{1,0:T(8,128)(2,1)S(1)}, bf16[16,2048]{1,0:T(8,128)(2,1)S(1)}, u32[]{:S(2)}, u32[]{:S(2)}) %collective-permute-start.7) | collective-permute-done | bytes 65568 | tf_op jit(solution)/shard_map/ppermute | solution.py:408
  27.9 1.6 %collective-permute-start.9 = (bf16[8,4352]{1,0:T(8,128)(2,1)S(1)}, bf16[8,4352]{1,0:T(8,128)(2,1)S(1)}, u32[]{:S(2)}, u32[]{:S(2)}) collective-permute-start(bf16[8,4352]{1,0:T(8,128)(2,1)S(1)} %merge.1.own_ref), channel_id=1, source_target_pairs={{0,2},{2,0},{1,3},{3,1},{4,6},{6,4},{5,7},{7,5},{8,10},{10,8},{9,1... | collective-permute-start | bytes 208904 | tf_op jit(solution)/shard_map/ppermute | solution.py:408
  29.4 2.8 %collective-permute-done.9.far_ref = bf16[8,4352]{1,0:T(8,128)(2,1)S(1)} collective-permute-done((bf16[8,4352]{1,0:T(8,128)(2,1)S(1)}, bf16[8,4352]{1,0:T(8,128)(2,1)S(1)}, u32[]{:S(2)}, u32[]{:S(2)}) %collective-permute-start.9) | collective-permute-done | bytes 69664 | tf_op jit(solution)/shard_map/ppermute | solution.py:408
  32.2 0.9 %finish.1 = bf16[8,4096]{1,0:T(8,128)(2,1)} custom-call(bf16[8,4352]{1,0:T(8,128)(2,1)S(1)} %merge.1.own_ref, bf16[8,4352]{1,0:T(8,128)(2,1)S(1)} %collective-permute-done.9.far_ref), custom_call_target="tpu_custom_call" | custom-call | tf_op jit(solution)/shard_map/finish/pallas_call | solution.py:398
  (19 shorter events, 0.1 us)
Async XLA Ops:
  0.0 6.8 %slice-start = ((s8[8388608]{0:T(1024)(128)(4,1)}), s8[4194304]{0:T(1024)(128)(4,1)S(1)}, s32[]{:S(2)}) async-start(s8[8388608]{0:T(1024)(128)(4,1)} %bitcast.4), calls=%async_computation | async-start | bytes 8388608
  0.0 6.8 %slice-start.1 = ((s8[8388608]{0:T(1024)(128)(4,1)}), s8[4194304]{0:T(1024)(128)(4,1)S(1)}, s32[]{:S(2)}) async-start(s8[8388608]{0:T(1024)(128)(4,1)} %bitcast.4), calls=%async_computation.1 | async-start | bytes 8388608
  0.0 6.8 %copy-start.1 = (bf16[256,4096]{1,0:T(8,128)(2,1)S(1)}, bf16[256,4096]{1,0:T(8,128)(2,1)}, u32[]{:S(2)}) copy-start(bf16[256,4096]{1,0:T(8,128)(2,1)} %tokens_ref.1) | copy-start | bytes 6291460
  1.0 23.7 %copy-start.2 = (bf16[1,1,8,4096]{3,2,1,0:T(8,128)(2,1)S(1)}, bf16[1,1,8,4096]{3,2,1,0:T(8,128)(2,1)}, u32[]{:S(2)}) copy-start(bf16[1,1,8,4096]{3,2,1,0:T(8,128)(2,1)} %param.13) | copy-start | bytes 196612
  1.1 23.7 %copy-start.3 = (s32[8,128]{1,0:T(8,128)S(1)}, s32[8,128]{1,0:T(8,128)}, u32[]{:S(2)}) copy-start(s32[8,128]{1,0:T(8,128)} %signs_ref.1) | copy-start | bytes 12292
  1.1 23.7 %copy-start.4 = (s32[1,1,8]{2,1,0:T(1,128)S(1)}, s32[1,1,8]{2,1,0:T(1,128)}, u32[]{:S(2)}) copy-start(s32[1,1,8]{2,1,0:T(1,128)} %lengths_ref.1) | copy-start | bytes 100
  1.1 8.1 %collective-permute-start = (bf16[8,4224]{1,0:T(8,128)(2,1)S(1)}, bf16[8,4224]{1,0:T(8,128)(2,1)S(1)}, u32[]{:S(2)}, u32[]{:S(2)}) collective-permute-start(bf16[8,4224]{1,0:T(8,128)(2,1)S(1)} %make_message.1.refs_0_), channel_id=1, source_target_pairs={{0,12},{4,8},{8,4},{12,0},{1,13},{5,9},{9,5},{13,1},{2,14},{6,10},... | collective-permute-start | bytes 202760 | tf_op jit(solution)/shard_map/ppermute | solution.py:408
  6.2 5.8 %collective-permute-start.1 = (bf16[8,4224]{1,0:T(8,128)(2,1)S(1)}, bf16[8,4224]{1,0:T(8,128)(2,1)S(1)}, u32[]{:S(2)}, u32[]{:S(2)}) collective-permute-start(bf16[8,4224]{1,0:T(8,128)(2,1)S(1)} %make_message.1.refs_0_), channel_id=1, source_target_pairs={{0,8},{4,12},{8,0},{12,4},{1,9},{5,13},{9,1},{13,5},{2,10},{6,14},... | collective-permute-start | bytes 202760 | tf_op jit(solution)/shard_map/ppermute | solution.py:408
  6.2 5.8 %collective-permute-start.2 = (bf16[8,4224]{1,0:T(8,128)(2,1)S(1)}, bf16[8,4224]{1,0:T(8,128)(2,1)S(1)}, u32[]{:S(2)}, u32[]{:S(2)}) collective-permute-start(bf16[8,4224]{1,0:T(8,128)(2,1)S(1)} %make_message.1.refs_0_), channel_id=1, source_target_pairs={{0,4},{4,0},{8,12},{12,8},{1,5},{5,1},{9,13},{13,9},{2,6},{6,2},{1... | collective-permute-start | bytes 202760 | tf_op jit(solution)/shard_map/ppermute | solution.py:408
  6.9 17.9 %copy-start = (bf16[1,1,8,128,1024]{4,3,2,1,0:T(8,128)(2,1)S(1)}, bf16[1,1,8,128,1024]{4,3,2,1,0:T(8,128)(2,1)}, u32[]{:S(2)}) copy-start(bf16[1,1,8,128,1024]{4,3,2,1,0:T(8,128)(2,1)} %param.14) | copy-start | bytes 6291460
  12.3 4.9 %collective-permute-start.3 = (f32[32,256]{1,0:T(8,128)S(1)}, f32[32,256]{1,0:T(8,128)S(1)}, u32[]{:S(2)}, u32[]{:S(2)}) collective-permute-start(f32[32,256]{1,0:T(8,128)S(1)} %get-tuple-element.22.refs_0_), channel_id=1, source_target_pairs={{0,8},{4,12},{8,0},{12,4},{1,9},{5,13},{9,1},{13,5},{2,10},{6,14},... | collective-permute-start | bytes 98312 | tf_op jit(solution)/shard_map/ppermute | solution.py:408
  13.8 5.7 %collective-permute-start.4 = (f32[32,256]{1,0:T(8,128)S(1)}, f32[32,256]{1,0:T(8,128)S(1)}, u32[]{:S(2)}, u32[]{:S(2)}) collective-permute-start(f32[32,256]{1,0:T(8,128)S(1)} %get-tuple-element.22.refs_0_), channel_id=1, source_target_pairs={{0,12},{4,8},{8,4},{12,0},{1,13},{5,9},{9,5},{13,1},{2,14},{6,10},... | collective-permute-start | bytes 98312 | tf_op jit(solution)/shard_map/ppermute | solution.py:408
  15.8 4.1 %collective-permute-start.5 = (f32[32,256]{1,0:T(8,128)S(1)}, f32[32,256]{1,0:T(8,128)S(1)}, u32[]{:S(2)}, u32[]{:S(2)}) collective-permute-start(f32[32,256]{1,0:T(8,128)S(1)} %get-tuple-element.22.refs_0_), channel_id=1, source_target_pairs={{0,4},{4,0},{8,12},{12,8},{1,5},{5,1},{9,13},{13,9},{2,6},{6,2},{1... | collective-permute-start | bytes 98312 | tf_op jit(solution)/shard_map/ppermute | solution.py:408
  20.3 6.2 %collective-permute-start.6 = (bf16[16,2048]{1,0:T(8,128)(2,1)S(1)}, bf16[16,2048]{1,0:T(8,128)(2,1)S(1)}, u32[]{:S(2)}, u32[]{:S(2)}) collective-permute-start(bf16[16,2048]{1,0:T(8,128)(2,1)S(1)} %get-tuple-element.30), channel_id=1, source_target_pairs={{0,12},{4,8},{8,4},{12,0},{1,13},{5,9},{9,5},{13,1},{2,14},{6,10},... | collective-permute-start | bytes 196616 | tf_op jit(solution)/shard_map/ppermute | solution.py:408
  22.3 5.5 %collective-permute-start.7 = (bf16[16,2048]{1,0:T(8,128)(2,1)S(1)}, bf16[16,2048]{1,0:T(8,128)(2,1)S(1)}, u32[]{:S(2)}, u32[]{:S(2)}) collective-permute-start(bf16[16,2048]{1,0:T(8,128)(2,1)S(1)} %get-tuple-element.31), channel_id=1, source_target_pairs={{0,4},{4,0},{8,12},{12,8},{1,5},{5,1},{9,13},{13,9},{2,6},{6,2},{1... | collective-permute-start | bytes 196616 | tf_op jit(solution)/shard_map/ppermute | solution.py:408
  22.3 5.5 %collective-permute-start.8 = (bf16[16,2048]{1,0:T(8,128)(2,1)S(1)}, bf16[16,2048]{1,0:T(8,128)(2,1)S(1)}, u32[]{:S(2)}, u32[]{:S(2)}) collective-permute-start(bf16[16,2048]{1,0:T(8,128)(2,1)S(1)} %get-tuple-element.32), channel_id=1, source_target_pairs={{0,8},{4,12},{8,0},{12,4},{1,9},{5,13},{9,1},{13,5},{2,10},{6,14},... | collective-permute-start | bytes 196616 | tf_op jit(solution)/shard_map/ppermute | solution.py:408
  27.9 4.4 %collective-permute-start.9 = (bf16[8,4352]{1,0:T(8,128)(2,1)S(1)}, bf16[8,4352]{1,0:T(8,128)(2,1)S(1)}, u32[]{:S(2)}, u32[]{:S(2)}) collective-permute-start(bf16[8,4352]{1,0:T(8,128)(2,1)S(1)} %merge.1.own_ref), channel_id=1, source_target_pairs={{0,2},{2,0},{1,3},{3,1},{4,6},{6,4},{5,7},{7,5},{8,10},{10,8},{9,1... | collective-permute-start | bytes 208904 | tf_op jit(solution)/shard_map/ppermute | solution.py:408

commit v7 on v6

--- a/solution.py
+++ b/solution.py
@@ -36,8 +36,7 @@
 
 
 QUERY_ORDER = (3, 2, 1)
-SCORE_ORDER = (2, 3, 1)
-MIXED_ORDER = (3, 1, 2)
+MIXED_ORDER = (3, 2, 1)
 
 
 def arranged(blocks, order):
@@ -263,9 +262,9 @@
             jnp.sum(jnp.where(here, scores[g * span : (g + 1) * span], 0.0), axis=0, keepdims=True)
             for g in range(group)
         ]
-        scores_ref[k * group : (k + 1) * group, :] = jnp.concatenate(lines, axis=0) * (
-            1.0 / math.sqrt(size)
-        )
+        block = jnp.concatenate(lines, axis=0) * (1.0 / math.sqrt(size))
+        for d in range(len(message_refs)):
+            scores_ref[d, k * group : (k + 1) * group, :] = block
 
 
 def partial_scores(heads, width, columns, partials, messages):
@@ -278,11 +277,11 @@
         in_specs=[pl.BlockSpec((tokens, width), lambda i: (0, 0))]
         + [pl.BlockSpec(m.shape, lambda i: (0, 0)) for m in messages],
         out_specs=[
-            pl.BlockSpec((query_heads, tokens), lambda i: (0, 0)),
+            pl.BlockSpec((len(messages), query_heads, tokens), lambda i: (0, 0, 0)),
             pl.BlockSpec((8, tokens), lambda i: (0, 0)),
         ],
         out_shape=[
-            jax.ShapeDtypeStruct((query_heads, tokens), jnp.float32),
+            jax.ShapeDtypeStruct((len(messages), query_heads, tokens), jnp.float32),
             jax.ShapeDtypeStruct((8, tokens), jnp.int32),
         ],
         compiler_params=params(),
@@ -290,20 +289,16 @@
     )(partials, *arranged(messages, QUERY_ORDER))
 
 
-def mix_kernel(heads, count, code_ref, values_ref, *refs):
-    score_refs = by_distance(refs[:count], SCORE_ORDER)
-    mixed_refs = refs[count : 2 * count]
-    tops_ref, totals_ref = refs[2 * count :]
+def mix_kernel(heads, code_ref, values_ref, scores_ref, *refs):
+    mixed_refs, (tops_ref, totals_ref) = refs[:-2], refs[-2:]
+    count = scores_ref.shape[0]
     tokens = values_ref.shape[0]
     size = values_ref.shape[1] // heads
     requests = tops_ref.shape[0]
-    group = score_refs[0].shape[0] // heads
+    group = scores_ref.shape[1] // heads
     span = count * requests
     here = lax.broadcasted_iota(jnp.int32, (span, tokens), 0) == code_ref[0:1, :]
-    parts = [ref[...] for ref in score_refs]
-    while len(parts) > 1:
-        parts = [parts[i] + parts[i + 1] for i in range(0, len(parts), 2)]
-    scores = parts[0]
+    scores = jnp.sum(scores_ref[...], axis=0)
     mixed = []
     for k in range(heads):
         weights = []
@@ -331,21 +326,21 @@
 
 
 def mix(heads, width, requests, code, partials, scores):
-    count = len(scores)
+    count = scores.shape[0]
     tokens = partials.shape[0]
-    columns = scores[0].shape[0] * (width // heads)
+    columns = scores.shape[1] * (width // heads)
     whole = lambda shape: pl.BlockSpec(shape, lambda i: (0, 0))
     return pl.pallas_call(
-        functools.partial(mix_kernel, heads, count),
+        functools.partial(mix_kernel, heads),
         grid=(1,),
         in_specs=[whole(code.shape), pl.BlockSpec((tokens, width), lambda i: (0, 1))]
-        + [whole(s.shape) for s in scores],
+        + [pl.BlockSpec(scores.shape, lambda i: (0, 0, 0))],
         out_specs=[whole((2 * requests, columns // 2))] * count + [whole((requests, columns))] * 2,
         out_shape=[jax.ShapeDtypeStruct((2 * requests, columns // 2), jnp.bfloat16)] * count
         + [jax.ShapeDtypeStruct((requests, columns), jnp.float32)] * 2,
         compiler_params=params(),
         name="mix",
-    )(code, partials, *arranged(scores, SCORE_ORDER))
+    )(code, partials, scores)
 
 
 def merge_kernel(count, cache_ref, stats_ref, factor_ref, *refs):
@@ -423,7 +418,7 @@
     messages = exchange([message] * seq_count)
     partials = project(tokens, kv_weight)
     scores, code = partial_scores(heads, width, columns, partials, messages)
-    scores = exchange([scores] * seq_count)
+    scores = lax.all_to_all(scores, "seq", split_axis=0, concat_axis=0, tiled=True)
     cache_mixed, tops, totals = cache_part(lengths, query, kv_cache[0, 0], signs)
     results = mix(heads, width, request_count, code, partials, scores)
     mixed, (new_tops, new_totals) = results[:seq_count], results[seq_count:]

time: 33.3 us -> 35.6 us (1.069)
  blocking collectives: 0 us -> 9.71 us
  waiting for transfers between devices: 11 us -> 7.12 us
  starting transfers between devices: 15.3 us -> 11.8 us
    all_to_all x0 -> x1, blocking collectives: none -> 9.71 us  [on_device(): lax.all_to_all(scores, 'seq', split_axis=0, concat_axis=0, tiled=True)]
    ppermute x10 -> x7, waiting for transfers between devices: 11 us -> 7.12 us  [from_partner(): return lax.ppermute(x, axis, [(i, i ^ distance) for i in range(count)])]
    ppermute x10 -> x7, starting transfers between devices: 15.3 us -> 11.8 us  [from_partner(): return lax.ppermute(x, axis, [(i, i ^ distance) for i in range(count)])]
  transfers between devices with their start and end apart: 10 -> 7, of which waited for: 6 -> 4; matrix products, arithmetic and copies ran while one was open for 0% -> 0% of each run, Pallas kernels for 12% -> 11%
where the time goes in v7:
time: 35.6 us; the launch traced here: 35.5 us
  starting transfers between devices  11.8 us (33%)
  blocking collectives  9.71 us (27%)
  waiting for transfers between devices  7.12 us (20%)
  Pallas kernels  6.71 us (19%)
    ppermute x7, starting transfers between devices, from_partner(): return lax.ppermute(x, axis, [(i, i ^ distance) for i in range(count)])  11.8 us
    all_to_all x1, blocking collectives, on_device(): lax.all_to_all(scores, 'seq', split_axis=0, concat_axis=0, tiled=True)  9.71 us
    ppermute x7, waiting for transfers between devices, from_partner(): return lax.ppermute(x, axis, [(i, i ^ distance) for i in range(count)])  7.12 us
    pallas_call x1, Pallas kernels, project(): pl.pallas_call(project_kernel, in_specs=[pl.BlockSpec(memory_space=pltpu....  2.32 us
    pallas_call x1, Pallas kernels, cache_part(): pl.pallas_call(cache_kernel, in_specs=[pl.BlockSpec(memory_space=pltpu.SM...  1.61 us
    pallas_call x1, Pallas kernels, make_message(): pl.pallas_call(message_kernel, in_specs=[pl.BlockSpec(memory_space=pl.ANY...  1.03 us
    pallas_call x1, Pallas kernels, finish(): pl.pallas_call(finish_kernel, out_shape=jax.ShapeDtypeStruct((own.shape[0...  0.9 us
  transfers between devices with their start and end apart: 7, of which 4 were waited for; matrix products, arithmetic and copies ran while one was open for 0% of the time, Pallas kernels for 11%

profile of v7, /device:TPU:0, one launch (start us, length us, event | category | flops | bytes accessed | tf_op | source)
XLA Modules:
  0.0 35.5 jit_solution(12492798774707827980)
XLA Ops:
  0.0 1.0 %make_message.1.refs_0_ = bf16[8,4224]{1,0:T(8,128)(2,1)S(1)} custom-call(bf16[8,4096]{1,0:T(8,128)(2,1)} %bitcast.7, s32[1,64]{1,0:T(1,128)} %bitcast.9, s32[1,64]{1,0:T(1,128)} %requests_ref.1), custom_call_target="tpu_custom_call" | custom-call | flops 99999997952 | bytes 10000 | tf_op jit(solution)/shard_map/make_message/pallas_call | solution.py:95
  1.0 0.0 copy-start.2
  1.1 0.0 copy-start.3
  1.1 0.0 copy-start.4
  1.1 5.1 %collective-permute-start = (bf16[8,4224]{1,0:T(8,128)(2,1)S(1)}, bf16[8,4224]{1,0:T(8,128)(2,1)S(1)}, u32[]{:S(2)}, u32[]{:S(2)}) collective-permute-start(bf16[8,4224]{1,0:T(8,128)(2,1)S(1)} %make_message.1.refs_0_), channel_id=1, source_target_pairs={{0,12},{4,8},{8,4},{12,0},{1,13},{5,9},{9,5},{13,1},{2,14},{6,10},... | collective-permute-start | bytes 202760 | tf_op jit(solution)/shard_map/ppermute | solution.py:403
  6.2 0.0 collective-permute-start.1
  6.2 0.6 %collective-permute-start.2 = (bf16[8,4224]{1,0:T(8,128)(2,1)S(1)}, bf16[8,4224]{1,0:T(8,128)(2,1)S(1)}, u32[]{:S(2)}, u32[]{:S(2)}) collective-permute-start(bf16[8,4224]{1,0:T(8,128)(2,1)S(1)} %make_message.1.refs_0_), channel_id=1, source_target_pairs={{0,4},{4,0},{8,12},{12,8},{1,5},{5,1},{9,13},{13,9},{2,6},{6,2},{1... | collective-permute-start | bytes 202760 | tf_op jit(solution)/shard_map/ppermute | solution.py:403
  6.9 0.0 copy-start
  6.9 2.3 %project.1.partial_ref.values_ref = bf16[256,1024]{1,0:T(8,128)(2,1)S(1)} custom-call(bf16[256,4096]{1,0:T(8,128)(2,1)S(1)} %copy-done.1, bf16[4096,1024]{1,0:T(8,128)(2,1)S(1)} %bitcast.5), custom_call_target="tpu_custom_call" | custom-call | flops 2147483648 | bytes 10485760 | tf_op jit(solution)/shard_map/project/pallas_call | solution.py:57
  9.2 0.0 collective-permute-done.refs_1_
  9.2 2.7 %collective-permute-done.1.refs_2_ = bf16[8,4224]{1,0:T(8,128)(2,1)S(1)} collective-permute-done((bf16[8,4224]{1,0:T(8,128)(2,1)S(1)}, bf16[8,4224]{1,0:T(8,128)(2,1)S(1)}, u32[]{:S(2)}, u32[]{:S(2)}) %collective-permute-start.1) | collective-permute-done | bytes 67616 | tf_op jit(solution)/shard_map/ppermute | solution.py:403
  12.0 0.3 partial_scores.1
  12.3 9.7 %all_to_all.5.scores_ref = f32[4,32,256]{2,1,0:T(8,128)S(1)} all-to-all(f32[4,32,256]{2,1,0:T(8,128)S(1)} %get-tuple-element.22), channel_id=1, replica_groups=mesh['groups'=2,'seq'=4,'tp'=2,'section'=2] {'seq'}, dimensions={0} | all-to-all | bytes 262144 | tf_op jit(solution)/shard_map/all_to_all | solution.py:421
  22.0 0.4 %mix.1 = (bf16[16,2048]{1,0:T(8,128)(2,1)S(1)}, bf16[16,2048]{1,0:T(8,128)(2,1)S(1)}, bf16[16,2048]{1,0:T(8,128)(2,1)S(1)}, bf16[16,2048]{1,0:T(8,128)(2,1)S(1)}...) custom-call(s32[8,256]{1,0:T(8,128)S(1)} %get-tuple-element.21.code_ref, ...), custom_call_target="tpu_custom_call" | custom-call | tf_op jit(solution)/shard_map/mix/pallas_call | solution.py:333
  22.4 1.5 %collective-permute-start.3 = (bf16[16,2048]{1,0:T(8,128)(2,1)S(1)}, bf16[16,2048]{1,0:T(8,128)(2,1)S(1)}, u32[]{:S(2)}, u32[]{:S(2)}) collective-permute-start(bf16[16,2048]{1,0:T(8,128)(2,1)S(1)} %get-tuple-element.30), channel_id=1, source_target_pairs={{0,12},{4,8},{8,4},{12,0},{1,13},{5,9},{9,5},{13,1},{2,14},{6,10},... | collective-permute-start | bytes 196616 | tf_op jit(solution)/shard_map/ppermute | solution.py:403
  23.9 1.3 %collective-permute-start.4 = (bf16[16,2048]{1,0:T(8,128)(2,1)S(1)}, bf16[16,2048]{1,0:T(8,128)(2,1)S(1)}, u32[]{:S(2)}, u32[]{:S(2)}) collective-permute-start(bf16[16,2048]{1,0:T(8,128)(2,1)S(1)} %get-tuple-element.31), channel_id=1, source_target_pairs={{0,8},{4,12},{8,0},{12,4},{1,9},{5,13},{9,1},{13,5},{2,10},{6,14},... | collective-permute-start | bytes 196616 | tf_op jit(solution)/shard_map/ppermute | solution.py:403
  25.2 1.7 %collective-permute-start.5 = (bf16[16,2048]{1,0:T(8,128)(2,1)S(1)}, bf16[16,2048]{1,0:T(8,128)(2,1)S(1)}, u32[]{:S(2)}, u32[]{:S(2)}) collective-permute-start(bf16[16,2048]{1,0:T(8,128)(2,1)S(1)} %get-tuple-element.32), channel_id=1, source_target_pairs={{0,4},{4,0},{8,12},{12,8},{1,5},{5,1},{9,13},{13,9},{2,6},{6,2},{1... | collective-permute-start | bytes 196616 | tf_op jit(solution)/shard_map/ppermute | solution.py:403
  26.9 1.6 %cache_part.1 = (f32[8,4096]{1,0:T(8,128)S(1)}, f32[8,4096]{1,0:T(8,128)S(1)}, f32[8,4096]{1,0:T(8,128)S(1)}) custom-call(s32[1,1,8]{2,1,0:T(1,128)S(1)} %copy-done.4, bf16[8,4096]{1,0:T(8,128)(2,1)S(1)} %bitcast.8, bf16[8,128,1024]{2,1,0:T(8,128)(2,1)S(1)} %bitcast.6, s32[8,128]{1,0:T(8,128)S(1)} %copy-done.3), custom_call_target="tpu_custom_call" | custom-call | flops 16777216 | bytes 2097152 | tf_op jit(solution)/shard_map/cache_part/pallas_call | solution.py:180
  28.5 0.1 combine_stats.1
  28.6 1.5 %collective-permute-done.4.refs_2_ = bf16[16,2048]{1,0:T(8,128)(2,1)S(1)} collective-permute-done((bf16[16,2048]{1,0:T(8,128)(2,1)S(1)}, bf16[16,2048]{1,0:T(8,128)(2,1)S(1)}, u32[]{:S(2)}, u32[]{:S(2)}) %collective-permute-start.4) | collective-permute-done | bytes 65568 | tf_op jit(solution)/shard_map/ppermute | solution.py:403
  30.0 0.1 collective-permute-done.5.refs_3_
  30.2 1.6 %collective-permute-start.6 = (bf16[8,4352]{1,0:T(8,128)(2,1)S(1)}, bf16[8,4352]{1,0:T(8,128)(2,1)S(1)}, u32[]{:S(2)}, u32[]{:S(2)}) collective-permute-start(bf16[8,4352]{1,0:T(8,128)(2,1)S(1)} %merge.1.own_ref), channel_id=1, source_target_pairs={{0,2},{2,0},{1,3},{3,1},{4,6},{6,4},{5,7},{7,5},{8,10},{10,8},{9,1... | collective-permute-start | bytes 208904 | tf_op jit(solution)/shard_map/ppermute | solution.py:403
  31.7 2.8 %collective-permute-done.6.far_ref = bf16[8,4352]{1,0:T(8,128)(2,1)S(1)} collective-permute-done((bf16[8,4352]{1,0:T(8,128)(2,1)S(1)}, bf16[8,4352]{1,0:T(8,128)(2,1)S(1)}, u32[]{:S(2)}, u32[]{:S(2)}) %collective-permute-start.6) | collective-permute-done | bytes 69664 | tf_op jit(solution)/shard_map/ppermute | solution.py:403
  34.6 0.9 %finish.1 = bf16[8,4096]{1,0:T(8,128)(2,1)} custom-call(bf16[8,4352]{1,0:T(8,128)(2,1)S(1)} %merge.1.own_ref, bf16[8,4352]{1,0:T(8,128)(2,1)S(1)} %collective-permute-done.6.far_ref), custom_call_target="tpu_custom_call" | custom-call | tf_op jit(solution)/shard_map/finish/pallas_call | solution.py:393
  (14 shorter events, 0.1 us)
Async XLA Ops:
  0.0 6.8 %slice-start = ((s8[8388608]{0:T(1024)(128)(4,1)}), s8[4194304]{0:T(1024)(128)(4,1)S(1)}, s32[]{:S(2)}) async-start(s8[8388608]{0:T(1024)(128)(4,1)} %bitcast.4), calls=%async_computation.1 | async-start | bytes 8388608
  0.0 6.8 %slice-start.1 = ((s8[8388608]{0:T(1024)(128)(4,1)}), s8[4194304]{0:T(1024)(128)(4,1)S(1)}, s32[]{:S(2)}) async-start(s8[8388608]{0:T(1024)(128)(4,1)} %bitcast.4), calls=%async_computation.2 | async-start | bytes 8388608
  0.0 6.8 %copy-start.1 = (bf16[256,4096]{1,0:T(8,128)(2,1)S(1)}, bf16[256,4096]{1,0:T(8,128)(2,1)}, u32[]{:S(2)}) copy-start(bf16[256,4096]{1,0:T(8,128)(2,1)} %tokens_ref.1) | copy-start | bytes 6291460
  1.0 25.8 %copy-start.2 = (bf16[1,1,8,4096]{3,2,1,0:T(8,128)(2,1)S(1)}, bf16[1,1,8,4096]{3,2,1,0:T(8,128)(2,1)}, u32[]{:S(2)}) copy-start(bf16[1,1,8,4096]{3,2,1,0:T(8,128)(2,1)} %param.13) | copy-start | bytes 196612
  1.1 25.8 %copy-start.3 = (s32[8,128]{1,0:T(8,128)S(1)}, s32[8,128]{1,0:T(8,128)}, u32[]{:S(2)}) copy-start(s32[8,128]{1,0:T(8,128)} %signs_ref.1) | copy-start | bytes 12292
  1.1 25.8 %copy-start.4 = (s32[1,1,8]{2,1,0:T(1,128)S(1)}, s32[1,1,8]{2,1,0:T(1,128)}, u32[]{:S(2)}) copy-start(s32[1,1,8]{2,1,0:T(1,128)} %lengths_ref.1) | copy-start | bytes 100
  1.1 8.1 %collective-permute-start = (bf16[8,4224]{1,0:T(8,128)(2,1)S(1)}, bf16[8,4224]{1,0:T(8,128)(2,1)S(1)}, u32[]{:S(2)}, u32[]{:S(2)}) collective-permute-start(bf16[8,4224]{1,0:T(8,128)(2,1)S(1)} %make_message.1.refs_0_), channel_id=1, source_target_pairs={{0,12},{4,8},{8,4},{12,0},{1,13},{5,9},{9,5},{13,1},{2,14},{6,10},... | collective-permute-start | bytes 202760 | tf_op jit(solution)/shard_map/ppermute | solution.py:403
  6.2 5.8 %collective-permute-start.1 = (bf16[8,4224]{1,0:T(8,128)(2,1)S(1)}, bf16[8,4224]{1,0:T(8,128)(2,1)S(1)}, u32[]{:S(2)}, u32[]{:S(2)}) collective-permute-start(bf16[8,4224]{1,0:T(8,128)(2,1)S(1)} %make_message.1.refs_0_), channel_id=1, source_target_pairs={{0,8},{4,12},{8,0},{12,4},{1,9},{5,13},{9,1},{13,5},{2,10},{6,14},... | collective-permute-start | bytes 202760 | tf_op jit(solution)/shard_map/ppermute | solution.py:403
  6.2 5.8 %collective-permute-start.2 = (bf16[8,4224]{1,0:T(8,128)(2,1)S(1)}, bf16[8,4224]{1,0:T(8,128)(2,1)S(1)}, u32[]{:S(2)}, u32[]{:S(2)}) collective-permute-start(bf16[8,4224]{1,0:T(8,128)(2,1)S(1)} %make_message.1.refs_0_), channel_id=1, source_target_pairs={{0,4},{4,0},{8,12},{12,8},{1,5},{5,1},{9,13},{13,9},{2,6},{6,2},{1... | collective-permute-start | bytes 202760 | tf_op jit(solution)/shard_map/ppermute | solution.py:403
  6.9 20.0 %copy-start = (bf16[1,1,8,128,1024]{4,3,2,1,0:T(8,128)(2,1)S(1)}, bf16[1,1,8,128,1024]{4,3,2,1,0:T(8,128)(2,1)}, u32[]{:S(2)}) copy-start(bf16[1,1,8,128,1024]{4,3,2,1,0:T(8,128)(2,1)} %param.14) | copy-start | bytes 6291460
  22.4 6.2 %collective-permute-start.3 = (bf16[16,2048]{1,0:T(8,128)(2,1)S(1)}, bf16[16,2048]{1,0:T(8,128)(2,1)S(1)}, u32[]{:S(2)}, u32[]{:S(2)}) collective-permute-start(bf16[16,2048]{1,0:T(8,128)(2,1)S(1)} %get-tuple-element.30), channel_id=1, source_target_pairs={{0,12},{4,8},{8,4},{12,0},{1,13},{5,9},{9,5},{13,1},{2,14},{6,10},... | collective-permute-start | bytes 196616 | tf_op jit(solution)/shard_map/ppermute | solution.py:403
  23.9 6.2 %collective-permute-start.4 = (bf16[16,2048]{1,0:T(8,128)(2,1)S(1)}, bf16[16,2048]{1,0:T(8,128)(2,1)S(1)}, u32[]{:S(2)}, u32[]{:S(2)}) collective-permute-start(bf16[16,2048]{1,0:T(8,128)(2,1)S(1)} %get-tuple-element.31), channel_id=1, source_target_pairs={{0,8},{4,12},{8,0},{12,4},{1,9},{5,13},{9,1},{13,5},{2,10},{6,14},... | collective-permute-start | bytes 196616 | tf_op jit(solution)/shard_map/ppermute | solution.py:403
  25.2 4.9 %collective-permute-start.5 = (bf16[16,2048]{1,0:T(8,128)(2,1)S(1)}, bf16[16,2048]{1,0:T(8,128)(2,1)S(1)}, u32[]{:S(2)}, u32[]{:S(2)}) collective-permute-start(bf16[16,2048]{1,0:T(8,128)(2,1)S(1)} %get-tuple-element.32), channel_id=1, source_target_pairs={{0,4},{4,0},{8,12},{12,8},{1,5},{5,1},{9,13},{13,9},{2,6},{6,2},{1... | collective-permute-start | bytes 196616 | tf_op jit(solution)/shard_map/ppermute | solution.py:403
  30.2 4.4 %collective-permute-start.6 = (bf16[8,4352]{1,0:T(8,128)(2,1)S(1)}, bf16[8,4352]{1,0:T(8,128)(2,1)S(1)}, u32[]{:S(2)}, u32[]{:S(2)}) collective-permute-start(bf16[8,4352]{1,0:T(8,128)(2,1)S(1)} %merge.1.own_ref), channel_id=1, source_target_pairs={{0,2},{2,0},{1,3},{3,1},{4,6},{6,4},{5,7},{7,5},{8,10},{10,8},{9,1... | collective-permute-start | bytes 208904 | tf_op jit(solution)/shard_map/ppermute | solution.py:403

commit v8 on v6

--- a/solution.py
+++ b/solution.py
@@ -37,7 +37,7 @@
 
 QUERY_ORDER = (3, 2, 1)
 SCORE_ORDER = (2, 3, 1)
-MIXED_ORDER = (3, 1, 2)
+MIXED_ORDER = (3, 2, 1)
 
 
 def arranged(blocks, order):

time: 33.3 us -> 33.3 us (level)
  no operation moved by 1% of the time
where the time goes in v8:
time: 33.3 us; the launch traced here: 33.1 us
  starting transfers between devices  15.3 us (46%)
  waiting for transfers between devices  11 us (33%)
  Pallas kernels  6.71 us (20%)
    ppermute x10, starting transfers between devices, from_partner(): return lax.ppermute(x, axis, [(i, i ^ distance) for i in range(count)])  15.3 us
    ppermute x10, waiting for transfers between devices, from_partner(): return lax.ppermute(x, axis, [(i, i ^ distance) for i in range(count)])  11 us
    pallas_call x1, Pallas kernels, project(): pl.pallas_call(project_kernel, in_specs=[pl.BlockSpec(memory_space=pltpu....  2.32 us
    pallas_call x1, Pallas kernels, cache_part(): pl.pallas_call(cache_kernel, in_specs=[pl.BlockSpec(memory_space=pltpu.SM...  1.61 us
    pallas_call x1, Pallas kernels, make_message(): pl.pallas_call(message_kernel, in_specs=[pl.BlockSpec(memory_space=pl.ANY...  1.03 us
    pallas_call x1, Pallas kernels, finish(): pl.pallas_call(finish_kernel, out_shape=jax.ShapeDtypeStruct((own.shape[0...  0.9 us
  transfers between devices with their start and end apart: 10, of which 6 were waited for; matrix products, arithmetic and copies ran while one was open for 0% of the time, Pallas kernels for 12%

profile of v8, /device:TPU:0, one launch (start us, length us, event | category | flops | bytes accessed | tf_op | source)
XLA Modules:
  0.0 33.1 jit_solution(2441458657605122651)
XLA Ops:
  0.0 1.0 %make_message.1.refs_0_ = bf16[8,4224]{1,0:T(8,128)(2,1)S(1)} custom-call(bf16[8,4096]{1,0:T(8,128)(2,1)} %bitcast.7, s32[1,64]{1,0:T(1,128)} %bitcast.9, s32[1,64]{1,0:T(1,128)} %requests_ref.1), custom_call_target="tpu_custom_call" | custom-call | flops 99999997952 | bytes 10000 | tf_op jit(solution)/shard_map/make_message/pallas_call | solution.py:96
  1.0 0.0 copy-start.2
  1.1 0.0 copy-start.3
  1.1 0.0 copy-start.4
  1.1 5.1 %collective-permute-start = (bf16[8,4224]{1,0:T(8,128)(2,1)S(1)}, bf16[8,4224]{1,0:T(8,128)(2,1)S(1)}, u32[]{:S(2)}, u32[]{:S(2)}) collective-permute-start(bf16[8,4224]{1,0:T(8,128)(2,1)S(1)} %make_message.1.refs_0_), channel_id=1, source_target_pairs={{0,12},{4,8},{8,4},{12,0},{1,13},{5,9},{9,5},{13,1},{2,14},{6,10},... | collective-permute-start | bytes 202760 | tf_op jit(solution)/shard_map/ppermute | solution.py:408
  6.2 0.6 %collective-permute-start.2 = (bf16[8,4224]{1,0:T(8,128)(2,1)S(1)}, bf16[8,4224]{1,0:T(8,128)(2,1)S(1)}, u32[]{:S(2)}, u32[]{:S(2)}) collective-permute-start(bf16[8,4224]{1,0:T(8,128)(2,1)S(1)} %make_message.1.refs_0_), channel_id=1, source_target_pairs={{0,4},{4,0},{8,12},{12,8},{1,5},{5,1},{9,13},{13,9},{2,6},{6,2},{1... | collective-permute-start | bytes 202760 | tf_op jit(solution)/shard_map/ppermute | solution.py:408
  6.9 2.3 %project.1.partial_ref.values_ref = bf16[256,1024]{1,0:T(8,128)(2,1)S(1)} custom-call(bf16[256,4096]{1,0:T(8,128)(2,1)S(1)} %copy-done.1, bf16[4096,1024]{1,0:T(8,128)(2,1)S(1)} %bitcast.5), custom_call_target="tpu_custom_call" | custom-call | flops 2147483648 | bytes 10485760 | tf_op jit(solution)/shard_map/project/pallas_call | solution.py:58
  9.2 2.7 %collective-permute-done.1.refs_2_ = bf16[8,4224]{1,0:T(8,128)(2,1)S(1)} collective-permute-done((bf16[8,4224]{1,0:T(8,128)(2,1)S(1)}, bf16[8,4224]{1,0:T(8,128)(2,1)S(1)}, u32[]{:S(2)}, u32[]{:S(2)}) %collective-permute-start.1) | collective-permute-done | bytes 67616 | tf_op jit(solution)/shard_map/ppermute | solution.py:408
  12.0 0.3 partial_scores.1
  12.3 1.5 %collective-permute-start.3 = (f32[32,256]{1,0:T(8,128)S(1)}, f32[32,256]{1,0:T(8,128)S(1)}, u32[]{:S(2)}, u32[]{:S(2)}) collective-permute-start(f32[32,256]{1,0:T(8,128)S(1)} %get-tuple-element.22.refs_0_), channel_id=1, source_target_pairs={{0,8},{4,12},{8,0},{12,4},{1,9},{5,13},{9,1},{13,5},{2,10},{6,14},... | collective-permute-start | bytes 98312 | tf_op jit(solution)/shard_map/ppermute | solution.py:408
  13.8 2.0 %collective-permute-start.4 = (f32[32,256]{1,0:T(8,128)S(1)}, f32[32,256]{1,0:T(8,128)S(1)}, u32[]{:S(2)}, u32[]{:S(2)}) collective-permute-start(f32[32,256]{1,0:T(8,128)S(1)} %get-tuple-element.22.refs_0_), channel_id=1, source_target_pairs={{0,12},{4,8},{8,4},{12,0},{1,13},{5,9},{9,5},{13,1},{2,14},{6,10},... | collective-permute-start | bytes 98312 | tf_op jit(solution)/shard_map/ppermute | solution.py:408
  15.8 0.1 collective-permute-start.5
  15.8 1.4 %collective-permute-done.3.refs_1_ = f32[32,256]{1,0:T(8,128)S(1)} collective-permute-done((f32[32,256]{1,0:T(8,128)S(1)}, f32[32,256]{1,0:T(8,128)S(1)}, u32[]{:S(2)}, u32[]{:S(2)}) %collective-permute-start.3) | collective-permute-done | bytes 32800 | tf_op jit(solution)/shard_map/ppermute | solution.py:408
  17.2 2.3 %collective-permute-done.4.refs_2_ = f32[32,256]{1,0:T(8,128)S(1)} collective-permute-done((f32[32,256]{1,0:T(8,128)S(1)}, f32[32,256]{1,0:T(8,128)S(1)}, u32[]{:S(2)}, u32[]{:S(2)}) %collective-permute-start.4) | collective-permute-done | bytes 32800 | tf_op jit(solution)/shard_map/ppermute | solution.py:408
  19.5 0.3 %collective-permute-done.5.refs_3_ = f32[32,256]{1,0:T(8,128)S(1)} collective-permute-done((f32[32,256]{1,0:T(8,128)S(1)}, f32[32,256]{1,0:T(8,128)S(1)}, u32[]{:S(2)}, u32[]{:S(2)}) %collective-permute-start.5) | collective-permute-done | bytes 32800 | tf_op jit(solution)/shard_map/ppermute | solution.py:408
  19.9 0.4 %mix.1 = (bf16[16,2048]{1,0:T(8,128)(2,1)S(1)}, bf16[16,2048]{1,0:T(8,128)(2,1)S(1)}, bf16[16,2048]{1,0:T(8,128)(2,1)S(1)}, bf16[16,2048]{1,0:T(8,128)(2,1)S(1)}...) custom-call(s32[8,256]{1,0:T(8,128)S(1)} %get-tuple-element.21.code_ref, ...), custom_call_target="tpu_custom_call" | custom-call | tf_op jit(solution)/shard_map/mix/pallas_call | solution.py:338
  20.3 2.0 %collective-permute-start.6 = (bf16[16,2048]{1,0:T(8,128)(2,1)S(1)}, bf16[16,2048]{1,0:T(8,128)(2,1)S(1)}, u32[]{:S(2)}, u32[]{:S(2)}) collective-permute-start(bf16[16,2048]{1,0:T(8,128)(2,1)S(1)} %get-tuple-element.30), channel_id=1, source_target_pairs={{0,12},{4,8},{8,4},{12,0},{1,13},{5,9},{9,5},{13,1},{2,14},{6,10},... | collective-permute-start | bytes 196616 | tf_op jit(solution)/shard_map/ppermute | solution.py:408
  22.3 2.4 %collective-permute-start.8 = (bf16[16,2048]{1,0:T(8,128)(2,1)S(1)}, bf16[16,2048]{1,0:T(8,128)(2,1)S(1)}, u32[]{:S(2)}, u32[]{:S(2)}) collective-permute-start(bf16[16,2048]{1,0:T(8,128)(2,1)S(1)} %get-tuple-element.32), channel_id=1, source_target_pairs={{0,4},{4,0},{8,12},{12,8},{1,5},{5,1},{9,13},{13,9},{2,6},{6,2},{1... | collective-permute-start | bytes 196616 | tf_op jit(solution)/shard_map/ppermute | solution.py:408
  24.7 1.6 %cache_part.1 = (f32[8,4096]{1,0:T(8,128)S(1)}, f32[8,4096]{1,0:T(8,128)S(1)}, f32[8,4096]{1,0:T(8,128)S(1)}) custom-call(s32[1,1,8]{2,1,0:T(1,128)S(1)} %copy-done.4, bf16[8,4096]{1,0:T(8,128)(2,1)S(1)} %bitcast.8, bf16[8,128,1024]{2,1,0:T(8,128)(2,1)S(1)} %bitcast.6, s32[8,128]{1,0:T(8,128)S(1)} %copy-done.3), custom_call_target="tpu_custom_call" | custom-call | flops 16777216 | bytes 2097152 | tf_op jit(solution)/shard_map/cache_part/pallas_call | solution.py:181
  26.4 0.1 combine_stats.1
  26.5 1.4 %collective-permute-done.7.refs_2_ = bf16[16,2048]{1,0:T(8,128)(2,1)S(1)} collective-permute-done((bf16[16,2048]{1,0:T(8,128)(2,1)S(1)}, bf16[16,2048]{1,0:T(8,128)(2,1)S(1)}, u32[]{:S(2)}, u32[]{:S(2)}) %collective-permute-start.7) | collective-permute-done | bytes 65568 | tf_op jit(solution)/shard_map/ppermute | solution.py:408
  27.9 1.6 %collective-permute-start.9 = (bf16[8,4352]{1,0:T(8,128)(2,1)S(1)}, bf16[8,4352]{1,0:T(8,128)(2,1)S(1)}, u32[]{:S(2)}, u32[]{:S(2)}) collective-permute-start(bf16[8,4352]{1,0:T(8,128)(2,1)S(1)} %merge.1.own_ref), channel_id=1, source_target_pairs={{0,2},{2,0},{1,3},{3,1},{4,6},{6,4},{5,7},{7,5},{8,10},{10,8},{9,1... | collective-permute-start | bytes 208904 | tf_op jit(solution)/shard_map/ppermute | solution.py:408
  29.4 2.8 %collective-permute-done.9.far_ref = bf16[8,4352]{1,0:T(8,128)(2,1)S(1)} collective-permute-done((bf16[8,4352]{1,0:T(8,128)(2,1)S(1)}, bf16[8,4352]{1,0:T(8,128)(2,1)S(1)}, u32[]{:S(2)}, u32[]{:S(2)}) %collective-permute-start.9) | collective-permute-done | bytes 69664 | tf_op jit(solution)/shard_map/ppermute | solution.py:408
  32.2 0.9 %finish.1 = bf16[8,4096]{1,0:T(8,128)(2,1)} custom-call(bf16[8,4352]{1,0:T(8,128)(2,1)S(1)} %merge.1.own_ref, bf16[8,4352]{1,0:T(8,128)(2,1)S(1)} %collective-permute-done.9.far_ref), custom_call_target="tpu_custom_call" | custom-call | tf_op jit(solution)/shard_map/finish/pallas_call | solution.py:398
  (19 shorter events, 0.1 us)
Async XLA Ops:
  0.0 6.8 %slice-start = ((s8[8388608]{0:T(1024)(128)(4,1)}), s8[4194304]{0:T(1024)(128)(4,1)S(1)}, s32[]{:S(2)}) async-start(s8[8388608]{0:T(1024)(128)(4,1)} %bitcast.4), calls=%async_computation | async-start | bytes 8388608
  0.0 6.8 %slice-start.1 = ((s8[8388608]{0:T(1024)(128)(4,1)}), s8[4194304]{0:T(1024)(128)(4,1)S(1)}, s32[]{:S(2)}) async-start(s8[8388608]{0:T(1024)(128)(4,1)} %bitcast.4), calls=%async_computation.1 | async-start | bytes 8388608
  0.0 6.8 %copy-start.1 = (bf16[256,4096]{1,0:T(8,128)(2,1)S(1)}, bf16[256,4096]{1,0:T(8,128)(2,1)}, u32[]{:S(2)}) copy-start(bf16[256,4096]{1,0:T(8,128)(2,1)} %tokens_ref.1) | copy-start | bytes 6291460
  1.0 23.7 %copy-start.2 = (bf16[1,1,8,4096]{3,2,1,0:T(8,128)(2,1)S(1)}, bf16[1,1,8,4096]{3,2,1,0:T(8,128)(2,1)}, u32[]{:S(2)}) copy-start(bf16[1,1,8,4096]{3,2,1,0:T(8,128)(2,1)} %param.13) | copy-start | bytes 196612
  1.1 23.7 %copy-start.3 = (s32[8,128]{1,0:T(8,128)S(1)}, s32[8,128]{1,0:T(8,128)}, u32[]{:S(2)}) copy-start(s32[8,128]{1,0:T(8,128)} %signs_ref.1) | copy-start | bytes 12292
  1.1 23.7 %copy-start.4 = (s32[1,1,8]{2,1,0:T(1,128)S(1)}, s32[1,1,8]{2,1,0:T(1,128)}, u32[]{:S(2)}) copy-start(s32[1,1,8]{2,1,0:T(1,128)} %lengths_ref.1) | copy-start | bytes 100
  1.1 8.1 %collective-permute-start = (bf16[8,4224]{1,0:T(8,128)(2,1)S(1)}, bf16[8,4224]{1,0:T(8,128)(2,1)S(1)}, u32[]{:S(2)}, u32[]{:S(2)}) collective-permute-start(bf16[8,4224]{1,0:T(8,128)(2,1)S(1)} %make_message.1.refs_0_), channel_id=1, source_target_pairs={{0,12},{4,8},{8,4},{12,0},{1,13},{5,9},{9,5},{13,1},{2,14},{6,10},... | collective-permute-start | bytes 202760 | tf_op jit(solution)/shard_map/ppermute | solution.py:408
  6.2 5.8 %collective-permute-start.1 = (bf16[8,4224]{1,0:T(8,128)(2,1)S(1)}, bf16[8,4224]{1,0:T(8,128)(2,1)S(1)}, u32[]{:S(2)}, u32[]{:S(2)}) collective-permute-start(bf16[8,4224]{1,0:T(8,128)(2,1)S(1)} %make_message.1.refs_0_), channel_id=1, source_target_pairs={{0,8},{4,12},{8,0},{12,4},{1,9},{5,13},{9,1},{13,5},{2,10},{6,14},... | collective-permute-start | bytes 202760 | tf_op jit(solution)/shard_map/ppermute | solution.py:408
  6.2 5.8 %collective-permute-start.2 = (bf16[8,4224]{1,0:T(8,128)(2,1)S(1)}, bf16[8,4224]{1,0:T(8,128)(2,1)S(1)}, u32[]{:S(2)}, u32[]{:S(2)}) collective-permute-start(bf16[8,4224]{1,0:T(8,128)(2,1)S(1)} %make_message.1.refs_0_), channel_id=1, source_target_pairs={{0,4},{4,0},{8,12},{12,8},{1,5},{5,1},{9,13},{13,9},{2,6},{6,2},{1... | collective-permute-start | bytes 202760 | tf_op jit(solution)/shard_map/ppermute | solution.py:408
  6.9 17.9 %copy-start = (bf16[1,1,8,128,1024]{4,3,2,1,0:T(8,128)(2,1)S(1)}, bf16[1,1,8,128,1024]{4,3,2,1,0:T(8,128)(2,1)}, u32[]{:S(2)}) copy-start(bf16[1,1,8,128,1024]{4,3,2,1,0:T(8,128)(2,1)} %param.14) | copy-start | bytes 6291460
  12.3 4.9 %collective-permute-start.3 = (f32[32,256]{1,0:T(8,128)S(1)}, f32[32,256]{1,0:T(8,128)S(1)}, u32[]{:S(2)}, u32[]{:S(2)}) collective-permute-start(f32[32,256]{1,0:T(8,128)S(1)} %get-tuple-element.22.refs_0_), channel_id=1, source_target_pairs={{0,8},{4,12},{8,0},{12,4},{1,9},{5,13},{9,1},{13,5},{2,10},{6,14},... | collective-permute-start | bytes 98312 | tf_op jit(solution)/shard_map/ppermute | solution.py:408
  13.8 5.7 %collective-permute-start.4 = (f32[32,256]{1,0:T(8,128)S(1)}, f32[32,256]{1,0:T(8,128)S(1)}, u32[]{:S(2)}, u32[]{:S(2)}) collective-permute-start(f32[32,256]{1,0:T(8,128)S(1)} %get-tuple-element.22.refs_0_), channel_id=1, source_target_pairs={{0,12},{4,8},{8,4},{12,0},{1,13},{5,9},{9,5},{13,1},{2,14},{6,10},... | collective-permute-start | bytes 98312 | tf_op jit(solution)/shard_map/ppermute | solution.py:408
  15.8 4.1 %collective-permute-start.5 = (f32[32,256]{1,0:T(8,128)S(1)}, f32[32,256]{1,0:T(8,128)S(1)}, u32[]{:S(2)}, u32[]{:S(2)}) collective-permute-start(f32[32,256]{1,0:T(8,128)S(1)} %get-tuple-element.22.refs_0_), channel_id=1, source_target_pairs={{0,4},{4,0},{8,12},{12,8},{1,5},{5,1},{9,13},{13,9},{2,6},{6,2},{1... | collective-permute-start | bytes 98312 | tf_op jit(solution)/shard_map/ppermute | solution.py:408
  20.3 6.2 %collective-permute-start.6 = (bf16[16,2048]{1,0:T(8,128)(2,1)S(1)}, bf16[16,2048]{1,0:T(8,128)(2,1)S(1)}, u32[]{:S(2)}, u32[]{:S(2)}) collective-permute-start(bf16[16,2048]{1,0:T(8,128)(2,1)S(1)} %get-tuple-element.30), channel_id=1, source_target_pairs={{0,12},{4,8},{8,4},{12,0},{1,13},{5,9},{9,5},{13,1},{2,14},{6,10},... | collective-permute-start | bytes 196616 | tf_op jit(solution)/shard_map/ppermute | solution.py:408
  22.3 5.5 %collective-permute-start.7 = (bf16[16,2048]{1,0:T(8,128)(2,1)S(1)}, bf16[16,2048]{1,0:T(8,128)(2,1)S(1)}, u32[]{:S(2)}, u32[]{:S(2)}) collective-permute-start(bf16[16,2048]{1,0:T(8,128)(2,1)S(1)} %get-tuple-element.31), channel_id=1, source_target_pairs={{0,8},{4,12},{8,0},{12,4},{1,9},{5,13},{9,1},{13,5},{2,10},{6,14},... | collective-permute-start | bytes 196616 | tf_op jit(solution)/shard_map/ppermute | solution.py:408
  22.3 5.5 %collective-permute-start.8 = (bf16[16,2048]{1,0:T(8,128)(2,1)S(1)}, bf16[16,2048]{1,0:T(8,128)(2,1)S(1)}, u32[]{:S(2)}, u32[]{:S(2)}) collective-permute-start(bf16[16,2048]{1,0:T(8,128)(2,1)S(1)} %get-tuple-element.32), channel_id=1, source_target_pairs={{0,4},{4,0},{8,12},{12,8},{1,5},{5,1},{9,13},{13,9},{2,6},{6,2},{1... | collective-permute-start | bytes 196616 | tf_op jit(solution)/shard_map/ppermute | solution.py:408
  27.9 4.4 %collective-permute-start.9 = (bf16[8,4352]{1,0:T(8,128)(2,1)S(1)}, bf16[8,4352]{1,0:T(8,128)(2,1)S(1)}, u32[]{:S(2)}, u32[]{:S(2)}) collective-permute-start(bf16[8,4352]{1,0:T(8,128)(2,1)S(1)} %merge.1.own_ref), channel_id=1, source_target_pairs={{0,2},{2,0},{1,3},{3,1},{4,6},{6,4},{5,7},{7,5},{8,10},{10,8},{9,1... | collective-permute-start | bytes 208904 | tf_op jit(solution)/shard_map/ppermute | solution.py:408

commit v9 on v0

--- a/solution.py
+++ b/solution.py
@@ -1,9 +1,526 @@
+import functools
 import math
 
 import jax
 import jax.numpy as jnp
 from jax import lax
+from jax.experimental import pallas as pl
+from jax.experimental.pallas import tpu as pltpu
 from jax.sharding import PartitionSpec as P
+
+LOWEST = -1e30
+MIB = 1024 * 1024
+NT = (((1,), (1,)), ((), ()))
+
+
+def params(mib=32):
+    return pltpu.CompilerParams(vmem_limit_bytes=mib * MIB)
+
+
+def in_hbm(x):
+    return pltpu.with_memory_space_constraint(x, pltpu.HBM)
+
+
+def hadamard_tile(order):
+    rows = lax.broadcasted_iota(jnp.int32, (order, order), 0)
+    cols = lax.broadcasted_iota(jnp.int32, (order, order), 1)
+    common = rows & cols
+    parity = jnp.zeros((order, order), jnp.int32)
+    for bit_number in range(order.bit_length() - 1):
+        parity = parity ^ (common >> bit_number)
+    return (1 - 2 * (parity & 1)).astype(jnp.float32).astype(jnp.bfloat16)
+
+
+QUERY_ORDER = (1, 3, 2)
+MIXED_ORDER = (3, 2, 1)
+
+
+def arranged(blocks, order):
+    return [blocks[0]] + [blocks[d] for d in order]
+
+
+def by_distance(refs, order):
+    return [refs[0]] + [refs[1 + order.index(d)] for d in range(1, len(refs))]
+
+
+def side():
+    return lax.axis_index("seq") & 1
+
+
+def start_all(copies):
+    for copy in copies:
+        copy.start()
+    return copies
+
+
+def accumulate(tokens_ref, weight_buf, acc_ref, copies):
+    steps, block, _ = weight_buf.shape
+    for step in range(steps):
+        for copy in copies[step]:
+            copy.wait()
+        tokens = tokens_ref[:, step * block : (step + 1) * block]
+        part = jnp.dot(tokens, weight_buf[step], preferred_element_type=jnp.float32)
+        acc_ref[...] = part if step == 0 else acc_ref[...] + part
+
+
+def halves(acc_ref):
+    width = acc_ref.shape[1] // 2
+    mine = pl.multiple_of(side() * width, width)
+    other = pl.multiple_of((1 - side()) * width, width)
+    return acc_ref[:, pl.ds(mine, width)], acc_ref[:, pl.ds(other, width)]
+
+
+def keys_kernel(
+    query_ref, owners_ref, requests_ref, tokens_ref, weight_ref,
+    tokens_out, own_ref, near_ref, same_ref, other_ref,
+    query_buf, owners_buf, requests_buf, weight_buf, acc_ref, small_sems, sems,
+):
+    requests, columns = query_ref.shape
+    per_device = owners_ref.shape[1]
+    rows = tokens_ref.shape[0]
+    steps, block, width = weight_buf.shape
+    half = columns // 2
+    small = start_all(
+        [
+            pltpu.make_async_copy(query_ref, query_buf, small_sems.at[0]),
+            pltpu.make_async_copy(owners_ref, owners_buf, small_sems.at[1]),
+            pltpu.make_async_copy(requests_ref, requests_buf, small_sems.at[2]),
+        ]
+    )
+    copies = []
+    for step in range(steps):
+        span = slice(step * block, (step + 1) * block)
+        copies.append(
+            start_all(
+                [
+                    pltpu.make_async_copy(tokens_ref.at[:, span], tokens_out.at[:, span], sems.at[0, step]),
+                    pltpu.make_async_copy(weight_ref.at[span, :width], weight_buf.at[step], sems.at[1, step]),
+                ]
+            )
+        )
+    for copy in small:
+        copy.wait()
+    code = (owners_buf[...] * requests + requests_buf[...]).astype(jnp.float32)
+    near_width = near_ref.shape[1]
+    spare = jnp.zeros((1, near_width - per_device), jnp.float32)
+    code = jnp.broadcast_to(jnp.concatenate([code, spare], axis=1), (2 * requests, near_width))
+    lanes = same_ref.shape[1] - half
+    mine = pl.multiple_of(side() * half, half)
+    other = pl.multiple_of((1 - side()) * half, half)
+    same_ref[:, :half] = query_buf[:, pl.ds(mine, half)]
+    same_ref[:, half:] = code[:requests, :lanes].astype(same_ref.dtype)
+    far_query = query_buf[:, pl.ds(other, half)]
+    other_ref[:, :half] = far_query
+    other_ref[:, half:] = code[:requests, :lanes].astype(same_ref.dtype)
+    stacked = far_query.astype(jnp.float32)
+    stacked = jnp.concatenate([stacked[:, at : at + near_width] for at in range(0, half, near_width)], axis=0)
+    near_ref[rows : rows + stacked.shape[0], :] = stacked.astype(near_ref.dtype)
+    near_ref[rows + stacked.shape[0] :, :] = code.astype(near_ref.dtype)
+    accumulate(tokens_out, weight_buf, acc_ref, copies)
+    kept, sent = halves(acc_ref)
+    own_ref[...] = kept.astype(own_ref.dtype)
+    near_ref[:rows, :] = sent.astype(near_ref.dtype)
+
+
+def project_keys(query, owners, requests, tokens, weight):
+    count, columns = query.shape
+    rows, features = tokens.shape
+    width = weight.shape[1] // 2
+    block = min(512, features // 2)
+    steps = features // block
+    half = columns // 2
+    lanes = -(-owners.shape[1] // 128) * 128
+    near_rows = rows + count * half // (width // 2) + 2 * count
+    vmem = pl.BlockSpec(memory_space=pltpu.VMEM)
+    return pl.pallas_call(
+        keys_kernel,
+        in_specs=[pl.BlockSpec(memory_space=pl.ANY)] * 5,
+        out_specs=[vmem] * 5,
+        out_shape=[
+            jax.ShapeDtypeStruct(tokens.shape, tokens.dtype),
+            jax.ShapeDtypeStruct((rows, width // 2), jnp.bfloat16),
+            jax.ShapeDtypeStruct((near_rows, width // 2), jnp.bfloat16),
+            jax.ShapeDtypeStruct((count, half + lanes), query.dtype),
+            jax.ShapeDtypeStruct((count, half + lanes), query.dtype),
+        ],
+        scratch_shapes=[
+            pltpu.VMEM(query.shape, query.dtype),
+            pltpu.VMEM(owners.shape, owners.dtype),
+            pltpu.VMEM(requests.shape, requests.dtype),
+            pltpu.VMEM((steps, block, width), weight.dtype),
+            pltpu.VMEM((rows, width), jnp.float32),
+            pltpu.SemaphoreType.DMA((3,)),
+            pltpu.SemaphoreType.DMA((2, steps)),
+        ],
+        compiler_params=params(),
+        name="project_keys",
+    )(in_hbm(query), in_hbm(owners), in_hbm(requests), in_hbm(tokens), in_hbm(weight))
+
+
+def values_kernel(tokens_ref, weight_ref, own_ref, near_ref, weight_buf, acc_ref, sems):
+    steps, block, width = weight_buf.shape
+    copies = []
+    for step in range(steps):
+        span = slice(step * block, (step + 1) * block)
+        copies.append(
+            start_all([pltpu.make_async_copy(weight_ref.at[span, width:], weight_buf.at[step], sems.at[step])])
+        )
+    accumulate(tokens_ref, weight_buf, acc_ref, copies)
+    kept, sent = halves(acc_ref)
+    own_ref[...] = kept.astype(own_ref.dtype)
+    near_ref[...] = sent.astype(near_ref.dtype)
+
+
+def project_values(tokens, weight):
+    rows, features = tokens.shape
+    width = weight.shape[1] // 2
+    block = min(512, features // 2)
+    steps = features // block
+    vmem = pl.BlockSpec(memory_space=pltpu.VMEM)
+    return pl.pallas_call(
+        values_kernel,
+        in_specs=[vmem, pl.BlockSpec(memory_space=pl.ANY)],
+        out_specs=[vmem] * 2,
+        out_shape=[jax.ShapeDtypeStruct((rows, width // 2), jnp.bfloat16)] * 2,
+        scratch_shapes=[
+            pltpu.VMEM((steps, block, width), weight.dtype),
+            pltpu.VMEM((rows, width), jnp.float32),
+            pltpu.SemaphoreType.DMA((steps,)),
+        ],
+        compiler_params=params(),
+        cost_estimate=pl.CostEstimate(
+            flops=2 * rows * features * width,
+            bytes_accessed=2 * features * width,
+            transcendentals=0,
+        ),
+        name="project_values",
+    )(tokens, in_hbm(weight))
+
+
+def cache_kernel(
+    lengths_ref, query_ref, cache_ref, signs_ref, mixed_ref, tops_ref, totals_ref, query_buf, top_buf, total_buf, mixed_buf
+):
+    requests, span, _ = cache_ref.shape
+    blocks, size = signs_ref.shape
+    heads = blocks // 2
+    width = heads * size
+    count = query_ref.shape[1] // size
+    group = count // heads
+    norm = 1.0 / math.sqrt(size)
+    matrix = hadamard_tile(size)
+    signs = (2 * signs_ref[...] - 1).astype(jnp.float32)
+    query = query_ref[...].astype(jnp.float32)
+    query = jnp.concatenate(
+        [query[:, h * size : (h + 1) * size] * signs[h // group : h // group + 1] for h in range(count)], axis=0
+    )
+    query_buf[...] = jnp.dot(query.astype(jnp.bfloat16), matrix, preferred_element_type=jnp.float32) * norm
+    rows = 2 * count
+    kv_head = lax.broadcasted_iota(jnp.int32, (rows, width), 0) // group & (heads - 1)
+    own_head = kv_head == lax.broadcasted_iota(jnp.int32, (rows, width), 1) // size
+    first = lax.broadcasted_iota(jnp.int32, (rows, span), 0) < count
+    position = lax.axis_index("tp") * span + lax.broadcasted_iota(jnp.int32, (rows, span), 1)
+    pairs = range(0, requests, 2)
+    scores = []
+    for r in pairs:
+        both = [query_buf[pl.ds(r + i, count, stride=requests), :] for i in range(2)]
+        wide = jnp.concatenate([jnp.concatenate(both, axis=0)] * heads, axis=1)
+        wide = jnp.where(own_head, wide, 0.0).astype(jnp.bfloat16)
+        keys = cache_ref[r : r + 2, :, :width].reshape(2 * span, width)
+        scores.append(lax.dot_general(wide, keys, NT, preferred_element_type=jnp.float32))
+    probs = []
+    for r, score in zip(pairs, scores):
+        score = jnp.where(first, score[:, :span], score[:, span:]) * norm
+        live = position < jnp.where(first, lengths_ref[0, 0, r], lengths_ref[0, 0, r + 1])
+        top = jnp.max(jnp.where(live, score, LOWEST), axis=1, keepdims=True)
+        prob = jnp.where(live, jnp.exp(score - top), 0.0)
+        total = jnp.sum(prob, axis=1, keepdims=True)
+        at = slice(r * count, (r + 2) * count)
+        top_buf[at, :] = jnp.broadcast_to(top, (rows, size))
+        total_buf[at, :] = jnp.broadcast_to(total, (rows, size))
+        probs.append(
+            jnp.concatenate([jnp.where(first, prob, 0.0), jnp.where(first, 0.0, prob)], axis=1).astype(jnp.bfloat16)
+        )
+    mixed = []
+    for r, prob in zip(pairs, probs):
+        values = cache_ref[r : r + 2, :, width:].reshape(2 * span, width)
+        wide = jnp.dot(prob, values, preferred_element_type=jnp.float32)
+        wide = jnp.where(own_head, wide, 0.0)
+        mixed.append(sum(wide[:, k * size : (k + 1) * size] for k in range(heads)))
+    mixed = jnp.concatenate(mixed, axis=0)
+    high = mixed.astype(jnp.bfloat16)
+    low = (mixed - high.astype(jnp.float32)).astype(jnp.bfloat16)
+    plain = jnp.dot(high, matrix, preferred_element_type=jnp.float32)
+    mixed_buf[...] = plain + jnp.dot(low, matrix, preferred_element_type=jnp.float32)
+    for h in range(count):
+        pick = pl.ds(h, requests, stride=count)
+        k = h // group
+        at = slice(k * requests, (k + 1) * requests)
+        column = slice(h % group * size, (h % group + 1) * size)
+        mixed_ref[at, column] = mixed_buf[pick, :] * (signs[heads + k : heads + k + 1] * norm)
+        tops_ref[at, column] = top_buf[pick, :]
+        totals_ref[at, column] = total_buf[pick, :]
+
+
+def cache_part(lengths, query, cache, signs):
+    requests, span, width = cache.shape
+    size = signs.shape[1]
+    heads = signs.shape[0] // 2
+    columns = query.shape[1]
+    vmem = pl.BlockSpec(memory_space=pltpu.VMEM)
+    return pl.pallas_call(
+        cache_kernel,
+        in_specs=[pl.BlockSpec(memory_space=pltpu.SMEM)] + [vmem] * 3,
+        out_shape=[jax.ShapeDtypeStruct((heads * requests, columns // heads), jnp.float32)] * 3,
+        scratch_shapes=[pltpu.VMEM((requests * columns // size, size), jnp.float32)] * 4,
+        compiler_params=params(),
+        cost_estimate=pl.CostEstimate(
+            flops=4 * span * requests * columns,
+            bytes_accessed=2 * requests * span * width,
+            transcendentals=span * requests * columns // size,
+        ),
+        name="cache_part",
+    )(lengths, query, cache, signs)
+
+
+def score_kernel(heads, keys_ref, own_ref, *refs):
+    message_refs, (scores_ref, code_ref) = by_distance((own_ref,) + refs[:-2], QUERY_ORDER), refs[-2:]
+    near_ref = message_refs[1]
+    requests = own_ref.shape[0]
+    tokens, width = keys_ref.shape
+    size = width // heads
+    count = len(message_refs)
+    half = scores_ref.shape[0] * size
+    group = scores_ref.shape[0] // heads
+    stacked = near_ref[tokens:, :].astype(jnp.float32)
+    spread = requests * half // width
+    near_query = jnp.concatenate(
+        [stacked[at * requests : (at + 1) * requests] for at in range(half // width)], axis=1
+    )
+    queries, codes = [], []
+    for d, ref in enumerate(message_refs):
+        if d == 1:
+            queries.append(near_query)
+            codes.append(stacked[spread : spread + 1, : tokens // count])
+        else:
+            queries.append(ref[:, :half].astype(jnp.float32))
+            codes.append(ref[0:1, half : half + tokens // count].astype(jnp.float32))
+    me = lax.axis_index("seq")
+    row = [sum(jnp.where(me ^ d == at, codes[d], 0.0) for d in range(count)) for at in range(count)]
+    code = jnp.concatenate(row, axis=1).astype(jnp.int32)
+    code = ((code // requests) ^ me) * requests + code % requests
+    code_ref[...] = jnp.broadcast_to(code, code_ref.shape)
+    span = count * requests
+    here = lax.broadcasted_iota(jnp.int32, (span, tokens), 0) == code
+    for k in range(heads):
+        rows = []
+        for g in range(group):
+            at = (k * group + g) * size
+            rows += [query[:, at : at + size] for query in queries]
+        query = jnp.concatenate(rows, axis=0).astype(jnp.bfloat16)
+        columns = slice(k * size, (k + 1) * size)
+        scores = lax.dot_general(query, keys_ref[:, columns], NT, preferred_element_type=jnp.float32)
+        scores = scores + lax.dot_general(
+            query, near_ref[:tokens, columns], NT, preferred_element_type=jnp.float32
+        )
+        lines = [
+            jnp.sum(jnp.where(here, scores[g * span : (g + 1) * span], 0.0), axis=0, keepdims=True)
+            for g in range(group)
+        ]
+        scores_ref[k * group : (k + 1) * group, :] = jnp.concatenate(lines, axis=0) * (
+            1.0 / math.sqrt(size)
+        )
+
+
+def pair_scores(heads, half, keys, messages):
+    tokens, width = keys.shape
+    return pl.pallas_call(
+        functools.partial(score_kernel, heads),
+        out_shape=[
+            jax.ShapeDtypeStruct((half * heads // width, tokens), jnp.float32),
+            jax.ShapeDtypeStruct((8, tokens), jnp.int32),
+        ],
+        compiler_params=params(),
+        name="pair_scores",
+    )(keys, *arranged(messages, QUERY_ORDER))
+
+
+def packed(value, group, size):
+    lane = lax.broadcasted_iota(jnp.int32, (value.shape[0], size), 1)
+    narrow = jnp.zeros(lane.shape, jnp.float32)
+    for g in range(group):
+        narrow = jnp.where(lane % group == g, value[:, g * size : (g + 1) * size], narrow)
+    high = narrow.astype(jnp.bfloat16).astype(jnp.float32)
+    middle = (narrow - high).astype(jnp.bfloat16).astype(jnp.float32)
+    return jnp.where(lane < group, high, jnp.where(lane < 2 * group, middle, narrow - high - middle))
+
+
+def packed_stats(tops, totals, group):
+    size = tops.shape[1] // group
+    lane = lax.broadcasted_iota(jnp.int32, (tops.shape[0], size), 1)
+    totals = pltpu.roll(packed(totals, group, size), 3 * group, 1)
+    return jnp.where(lane < 3 * group, packed(tops, group, size), totals)
+
+
+def unpacked_stats(stats, group):
+    parts = [stats[:, at * group : (at + 1) * group] for at in range(6)]
+    return parts[0] + parts[1] + parts[2], parts[3] + parts[4] + parts[5]
+
+
+def broad(narrow, size):
+    rows, group = narrow.shape
+    return jnp.concatenate([jnp.broadcast_to(narrow[:, g : g + 1], (rows, size)) for g in range(group)], axis=1)
+
+
+def mix_kernel(heads, count, requests, code_ref, own_ref, near_ref, scores_ref, far_scores_ref, *refs):
+    mixed_refs, (tops_ref, totals_ref) = refs[:count], refs[count:]
+    tokens, width = own_ref.shape
+    size = width // heads
+    group = scores_ref.shape[0] // heads
+    span = count * requests
+    here = lax.broadcasted_iota(jnp.int32, (span, tokens), 0) == code_ref[0:1, :]
+    scores = scores_ref[...] + far_scores_ref[...]
+    mixed, tops, totals = [], [], []
+    for k in range(heads):
+        weights = []
+        for g in range(group):
+            row = k * group + g
+            line = jnp.broadcast_to(scores[row : row + 1, :], (span, tokens))
+            top = jnp.max(jnp.where(here, line, LOWEST), axis=1, keepdims=True)
+            probs = jnp.where(here, jnp.exp(line - top), 0.0)
+            weights.append(probs)
+            tops.append(jnp.broadcast_to(top, (span, size)))
+            totals.append(jnp.broadcast_to(jnp.sum(probs, axis=1, keepdims=True), (span, size)))
+        weights = jnp.concatenate(weights, axis=0).astype(jnp.bfloat16)
+        columns = slice(k * size, (k + 1) * size)
+        sums = jnp.dot(weights, own_ref[:, columns], preferred_element_type=jnp.float32)
+        mixed.append(sums + jnp.dot(weights, near_ref[:, columns], preferred_element_type=jnp.float32))
+
+    def block(parts, d):
+        rows = slice(d * requests, (d + 1) * requests)
+        lines = [
+            jnp.concatenate([parts[k * group + g][rows] for g in range(group)], axis=1) for k in range(heads)
+        ]
+        return jnp.concatenate(lines, axis=0)
+
+    pieces = [mixed[k][g * span : (g + 1) * span] for k in range(heads) for g in range(group)]
+    for d in range(count):
+        mixed_refs[d][:, : group * size] = block(pieces, d).astype(jnp.bfloat16)
+    stats = packed_stats(block(tops, 1), block(totals, 1), group)
+    mixed_refs[1][:, group * size :] = stats.astype(jnp.bfloat16)
+    tops_ref[...] = block(tops, 0)
+    totals_ref[...] = block(totals, 0)
+
+
+def mix(heads, count, requests, code, values, near_values, scores, far_scores):
+    size = values.shape[1] // heads
+    columns = scores.shape[0] // heads * size
+    shape = (heads * requests, columns)
+    wide = (heads * requests, columns + size)
+    return pl.pallas_call(
+        functools.partial(mix_kernel, heads, count, requests),
+        out_shape=[jax.ShapeDtypeStruct(wide if d == 1 else shape, jnp.bfloat16) for d in range(count)]
+        + [jax.ShapeDtypeStruct(shape, jnp.float32)] * 2,
+        compiler_params=params(),
+        name="mix",
+    )(code, values, near_values, scores, far_scores)
+
+
+def merge_kernel(cache_ref, top_ref, total_ref, new_top_ref, new_total_ref, *refs):
+    mixed_refs, out_ref = by_distance(refs[:-1], MIXED_ORDER), refs[-1]
+    rows, columns = new_top_ref.shape
+    size = out_ref.shape[1] - columns
+    group = columns // size
+    near = mixed_refs[1][...].astype(jnp.float32)
+    near_top, near_total = unpacked_stats(near[:, columns:], group)
+    own = mixed_refs[0][...].astype(jnp.float32) + mixed_refs[2][...].astype(jnp.float32)
+    other = near[:, :columns] + mixed_refs[3][...].astype(jnp.float32)
+    parts = (
+        (side(), own, new_top_ref[...], new_total_ref[...]),
+        (1 - side(), other, broad(near_top, size), broad(near_total, size)),
+    )
+    for place, new, new_top, new_total in parts:
+        at = pl.ds(pl.multiple_of(place * rows, rows), rows)
+        top = top_ref[at, :]
+        both = jnp.maximum(top, new_top)
+        cache_factor = jnp.exp(top - both)
+        new_factor = jnp.exp(new_top - both)
+        out_ref[at, :columns] = (cache_ref[at, :] * cache_factor + new * new_factor).astype(out_ref.dtype)
+        total = total_ref[at, :] * cache_factor + new_total * new_factor
+        out_ref[at, columns:] = packed_stats(both, total, group).astype(out_ref.dtype)
+
+
+def merge(size, cache_mixed, tops, totals, new_tops, new_totals, mixed):
+    rows, columns = cache_mixed.shape
+    return pl.pallas_call(
+        merge_kernel,
+        out_shape=jax.ShapeDtypeStruct((rows, columns + size), jnp.bfloat16),
+        compiler_params=params(),
+        name="merge",
+    )(cache_mixed, tops, totals, new_tops, new_totals, *arranged(mixed, MIXED_ORDER))
+
+
+def finish_kernel(own_ref, far_ref, out_ref):
+    requests = out_ref.shape[0]
+    rows, wide = own_ref.shape
+    heads = rows // requests
+    columns = out_ref.shape[1] // heads
+    size = wide - columns
+    group = columns // size
+    first = lax.axis_index("tp") == 0
+    own, far = own_ref[...].astype(jnp.float32), far_ref[...].astype(jnp.float32)
+    low, high = jnp.where(first, own, far), jnp.where(first, far, own)
+    low_top, low_total = unpacked_stats(low[:, columns:], group)
+    high_top, high_total = unpacked_stats(high[:, columns:], group)
+    both = jnp.maximum(low_top, high_top)
+    low_factor, high_factor = jnp.exp(low_top - both), jnp.exp(high_top - both)
+    inverse = 1.0 / (low_total * low_factor + high_total * high_factor)
+    low_factor, high_factor = low_factor * inverse, high_factor * inverse
+    for g in range(group):
+        at = slice(g * size, (g + 1) * size)
+        out = low[:, at] * low_factor[:, g : g + 1] + high[:, at] * high_factor[:, g : g + 1]
+        for k in range(heads):
+            column = slice((k * group + g) * size, (k * group + g + 1) * size)
+            out_ref[:, column] = out[k * requests : (k + 1) * requests].astype(out_ref.dtype)
+
+
+def finish(requests, own, far, columns):
+    return pl.pallas_call(
+        finish_kernel,
+        out_shape=jax.ShapeDtypeStruct((requests, columns), jnp.bfloat16),
+        compiler_params=params(),
+        name="finish",
+    )(own, far)
+
+
+def from_partner(x, axis, distance):
+    count = lax.axis_size(axis)
+    return lax.ppermute(x, axis, [(i, i ^ distance) for i in range(count)])
+
+
+def on_device(tokens, kv_weight, owners, requests, signs, queries, kv_cache, lengths):
+    seq_count = lax.axis_size("seq")
+    blocks, size = signs.shape
+    kept_heads = blocks // 4
+    query = queries[0, 0]
+    request_count, columns = query.shape
+    tokens, keys, near, same, other = project_keys(query, owners[:, :, 0], requests, tokens, kv_weight)
+    messages = [
+        same,
+        from_partner(near, "seq", 1),
+        from_partner(same, "seq", 2),
+        from_partner(other, "seq", 3),
+    ]
+    values, far_values = project_values(tokens, kv_weight)
+    near_values = from_partner(far_values, "seq", 1)
+    scores, code = pair_scores(kept_heads, columns // 2, keys, messages)
+    far_scores = from_partner(scores, "seq", 2)
+    results = mix(kept_heads, seq_count, request_count, code, values, near_values, scores, far_scores)
+    mixed, (new_tops, new_totals) = results[:seq_count], results[seq_count:]
+    mixed = [mixed[0]] + [from_partner(mixed[d], "seq", d) for d in range(1, seq_count)]
+    cache_mixed, tops, totals = cache_part(lengths, query, kv_cache[0, 0], signs)
+    own = merge(size, cache_mixed, tops, totals, new_tops, new_totals, mixed)
+    far = from_partner(own, "tp", 1)
+    return finish(request_count, own, far, columns).reshape(1, 1, request_count, columns)
 
 
 def hadamard(order):
@@ -41,7 +558,7 @@
     return targets * room + within
 
 
-def on_device(tokens, kv_weight, owners, requests, signs, queries, kv_cache, lengths):
+def on_device_long(tokens, kv_weight, owners, requests, signs, queries, kv_cache, lengths):
     seq_count = lax.axis_size("seq")
     per_device = owners.shape[1]
     slots = max(2, (2 * per_device + seq_count - 1) // seq_count)
@@ -140,8 +657,9 @@
         P(("groups", "seq"), "section", None, "tp", None),
         P(("groups", "seq"), "section", None),
     )
+    short = mesh.shape["seq"] == 4 and mesh.shape["tp"] == 2
     return jax.shard_map(
-        on_device,
+        on_device if short else on_device_long,
         mesh=mesh,
         in_specs=placed,
         out_specs=P(("groups", "seq"), "section", None, None),

time: 116 us -> 36.8 us (0.32)
  waiting for transfers between devices: 36.9 us -> 13 us
  matrix products: 15.4 us -> 0 us
  local copies, waits for them, and re-layouts: 14.9 us -> 0.01 us
  between operations: 13.6 us -> 0.07 us
  blocking collectives: 13 us -> 0 us
  Pallas kernels: 0 us -> 10.9 us
  other arithmetic: 6.39 us -> 0 us
  starting transfers between devices: 14.6 us -> 12.7 us
    reduce_scatter x1 -> x0, waiting for transfers between devices: 18.4 us -> none  [on_device(): lax.psum_scatter(jnp.dot(tokens, kv_weight, preferred_element_type=jnp.fl...]
    dot_general x8 -> x0, matrix products: 15.4 us -> none  [the longest x1 6.54 us: on_device(): jnp.dot(tokens, kv_weight, preferred_element_type=jnp.float32)]
    psum x1 -> x0, waiting for transfers between devices: 14.8 us -> none  [on_device(): lax.psum((mixed * factor[..., None]).astype(jnp.bfloat16), 'tp')]
    all_to_all x3 -> x0, starting transfers between devices: 14.6 us -> none  [the longest x1 6.32 us: on_device(): lax.all_to_all(send_codes, 'seq', split_axis=0, concat_axis=0, tiled=True)]
    ppermute x0 -> x9, waiting for transfers between devices: none -> 13 us  [from_partner(): return lax.ppermute(x, axis, [(i, i ^ distance) for i in range(count)])]
    ppermute x0 -> x9, starting transfers between devices: none -> 12.7 us  [from_partner(): return lax.ppermute(x, axis, [(i, i ^ distance) for i in range(count)])]
    pallas_call x0 -> x7, Pallas kernels: none -> 10.9 us  [the longest x1 4.32 us: project_keys(): pl.pallas_call(keys_kernel, in_specs=[pl.BlockSpec(memory_space=pl.ANY)]...]
    pmax x1 -> x0, blocking collectives: 8.02 us -> none  [on_device(): shared_top = lax.pmax(top, 'tp')]
  transfers between devices with their start and end apart: 5 -> 9, of which waited for: 3 -> 6; matrix products, arithmetic and copies ran while one was open for 22% -> 0% of each run, Pallas kernels for 0% -> 13%
where the time goes in v9:
time: 36.8 us; the launch traced here: 36.6 us
  waiting for transfers between devices  13 us (35%)
  starting transfers between devices  12.7 us (35%)
  Pallas kernels  10.9 us (30%)
    ppermute x9, waiting for transfers between devices, from_partner(): return lax.ppermute(x, axis, [(i, i ^ distance) for i in range(count)])  13 us
    ppermute x9, starting transfers between devices, from_partner(): return lax.ppermute(x, axis, [(i, i ^ distance) for i in range(count)])  12.7 us
    pallas_call x1, Pallas kernels, project_keys(): pl.pallas_call(keys_kernel, in_specs=[pl.BlockSpec(memory_space=pl.ANY)]...  4.32 us
    pallas_call x1, Pallas kernels, project_values(): pl.pallas_call(values_kernel, in_specs=[vmem, pl.BlockSpec(memory_space=p...  2.97 us
    pallas_call x1, Pallas kernels, cache_part(): pl.pallas_call(cache_kernel, in_specs=[pl.BlockSpec(memory_space=pltpu.SM...  1.61 us
    pallas_call x1, Pallas kernels, finish(): pl.pallas_call(finish_kernel, out_shape=jax.ShapeDtypeStruct((requests, c...  1.01 us
  transfers between devices with their start and end apart: 9, of which 6 were waited for; matrix products, arithmetic and copies ran while one was open for 0% of the time, Pallas kernels for 13%

profile of v9, /device:TPU:0, one launch (start us, length us, event | category | flops | bytes accessed | tf_op | source)
XLA Modules:
  0.0 36.6 jit_solution(8936962375451421861)
XLA Ops:
  0.0 4.3 %project_keys.1 = (bf16[256,4096]{1,0:T(8,128)(2,1)S(1)}, bf16[256,256]{1,0:T(8,128)(2,1)S(1)}, bf16[336,256]{1,0:T(8,128)(2,1)S(1)}, bf16[8,2176]{1,0:T(8,128)(2,1)S(1)}, bf16[8,2176]{1,0:T(8,128)(2,1)S(1)}) custom-call(bf16[8,4096]{1,0:T(8,128)(2,1)} %bitcast.5, s32[1,64]{1,0:T(1,128)} %bitcast.7, s32[1,64]{1,0:T(1,128)} %requests_ref.1, ...), custom_call_target="tpu_custom_call" | custom-call | tf_op jit(solution)/shard_map/project_keys/pallas_call | solution.py:135
  4.3 3.1 %collective-permute-start = (bf16[336,256]{1,0:T(8,128)(2,1)S(1)}, bf16[336,256]{1,0:T(8,128)(2,1)S(1)}, u32[]{:S(2)}, u32[]{:S(2)}) collective-permute-start(bf16[336,256]{1,0:T(8,128)(2,1)S(1)} %get-tuple-element.28), channel_id=1, source_target_pairs={{0,4},{4,0},{8,12},{12,8},{1,5},{5,1},{9,13},{13,9},{2,6},{6,2},{1... | collective-permute-start | bytes 516104 | tf_op jit(solution)/shard_map/ppermute | solution.py:497
  7.4 3.0 %project_values.1 = (bf16[256,256]{1,0:T(8,128)(2,1)S(1)}, bf16[256,256]{1,0:T(8,128)(2,1)S(1)}) custom-call(bf16[256,4096]{1,0:T(8,128)(2,1)S(1)} %get-tuple-element.31.tokens_ref, bf16[4096,1024]{1,0:T(8,128)(2,1)} %weight_ref.3), custom_call_target="tpu_custom_call" | custom-call | flops 1073741824 | bytes 4194304 | tf_op jit(solution)/shard_map/project_values/pallas_call | solution.py:180
  10.4 0.1 collective-permute-start.3
  10.5 3.0 %collective-permute-start.2 = (bf16[8,2176]{1,0:T(8,128)(2,1)S(1)}, bf16[8,2176]{1,0:T(8,128)(2,1)S(1)}, u32[]{:S(2)}, u32[]{:S(2)}) collective-permute-start(bf16[8,2176]{1,0:T(8,128)(2,1)S(1)} %get-tuple-element.27.own_ref), channel_id=1, source_target_pairs={{0,8},{4,12},{8,0},{12,4},{1,9},{5,13},{9,1},{13,5},{2,10},{6,14},... | collective-permute-start | bytes 104456 | tf_op jit(solution)/shard_map/ppermute | solution.py:497
  13.5 1.3 %collective-permute-start.1 = (bf16[8,2176]{1,0:T(8,128)(2,1)S(1)}, bf16[8,2176]{1,0:T(8,128)(2,1)S(1)}, u32[]{:S(2)}, u32[]{:S(2)}) collective-permute-start(bf16[8,2176]{1,0:T(8,128)(2,1)S(1)} %get-tuple-element.29), channel_id=1, source_target_pairs={{0,12},{4,8},{8,4},{12,0},{1,13},{5,9},{9,5},{13,1},{2,14},{6,10},... | collective-permute-start | bytes 104456 | tf_op jit(solution)/shard_map/ppermute | solution.py:497
  14.9 0.7 %collective-permute-done.2.refs_2_ = bf16[8,2176]{1,0:T(8,128)(2,1)S(1)} collective-permute-done((bf16[8,2176]{1,0:T(8,128)(2,1)S(1)}, bf16[8,2176]{1,0:T(8,128)(2,1)S(1)}, u32[]{:S(2)}, u32[]{:S(2)}) %collective-permute-start.2) | collective-permute-done | bytes 34848 | tf_op jit(solution)/shard_map/ppermute | solution.py:497
  15.5 3.7 %collective-permute-done.1.refs_1_ = bf16[8,2176]{1,0:T(8,128)(2,1)S(1)} collective-permute-done((bf16[8,2176]{1,0:T(8,128)(2,1)S(1)}, bf16[8,2176]{1,0:T(8,128)(2,1)S(1)}, u32[]{:S(2)}, u32[]{:S(2)}) %collective-permute-start.1) | collective-permute-done | bytes 34848 | tf_op jit(solution)/shard_map/ppermute | solution.py:497
  19.2 0.0 collective-permute-done.refs_0_
  19.2 0.3 pair_scores.1
  19.6 0.1 collective-permute-start.4
  19.6 0.0 collective-permute-done.3.near_ref
  19.6 4.6 %collective-permute-done.4.far_scores_ref = f32[16,256]{1,0:T(8,128)S(1)} collective-permute-done((f32[16,256]{1,0:T(8,128)S(1)}, f32[16,256]{1,0:T(8,128)S(1)}, u32[]{:S(2)}, u32[]{:S(2)}) %collective-permute-start.4) | collective-permute-done | bytes 16416 | tf_op jit(solution)/shard_map/ppermute | solution.py:497
  24.3 0.4 mix.1
  24.6 0.2 collective-permute-start.7
  24.9 1.3 %collective-permute-start.5 = (bf16[16,1024]{1,0:T(8,128)(2,1)S(1)}, bf16[16,1024]{1,0:T(8,128)(2,1)S(1)}, u32[]{:S(2)}, u32[]{:S(2)}) collective-permute-start(bf16[16,1024]{1,0:T(8,128)(2,1)S(1)} %get-tuple-element.38), channel_id=1, source_target_pairs={{0,12},{4,8},{8,4},{12,0},{1,13},{5,9},{9,5},{13,1},{2,14},{6,10},... | collective-permute-start | bytes 98312 | tf_op jit(solution)/shard_map/ppermute | solution.py:497
  26.2 2.0 %collective-permute-start.6 = (bf16[16,1024]{1,0:T(8,128)(2,1)S(1)}, bf16[16,1024]{1,0:T(8,128)(2,1)S(1)}, u32[]{:S(2)}, u32[]{:S(2)}) collective-permute-start(bf16[16,1024]{1,0:T(8,128)(2,1)S(1)} %get-tuple-element.39), channel_id=1, source_target_pairs={{0,8},{4,12},{8,0},{12,4},{1,9},{5,13},{9,1},{13,5},{2,10},{6,14},... | collective-permute-start | bytes 98312 | tf_op jit(solution)/shard_map/ppermute | solution.py:497
  28.2 1.6 %cache_part.1 = (f32[32,1024]{1,0:T(8,128)S(1)}, f32[32,1024]{1,0:T(8,128)S(1)}, f32[32,1024]{1,0:T(8,128)S(1)}) custom-call(s32[1,1,8]{2,1,0:T(1,128)S(1)} %copy-done.3, bf16[8,4096]{1,0:T(8,128)(2,1)S(1)} %bitcast.6, bf16[8,128,1024]{2,1,0:T(8,128)(2,1)S(1)} %bitcast.4, s32[8,128]{1,0:T(8,128)S(1)} %copy-done.2), custom_call_target="tpu_custom_call" | custom-call | flops 16777216 | bytes 2097152 | tf_op jit(solution)/shard_map/cache_part/pallas_call | solution.py:270
  29.8 0.7 %collective-permute-done.5.refs_1_ = bf16[16,1024]{1,0:T(8,128)(2,1)S(1)} collective-permute-done((bf16[16,1024]{1,0:T(8,128)(2,1)S(1)}, bf16[16,1024]{1,0:T(8,128)(2,1)S(1)}, u32[]{:S(2)}, u32[]{:S(2)}) %collective-permute-start.5) | collective-permute-done | bytes 32800 | tf_op jit(solution)/shard_map/ppermute | solution.py:497
  30.6 0.4 %collective-permute-done.6.refs_2_ = bf16[16,1024]{1,0:T(8,128)(2,1)S(1)} collective-permute-done((bf16[16,1024]{1,0:T(8,128)(2,1)S(1)}, bf16[16,1024]{1,0:T(8,128)(2,1)S(1)}, u32[]{:S(2)}, u32[]{:S(2)}) %collective-permute-start.6) | collective-permute-done | bytes 32800 | tf_op jit(solution)/shard_map/ppermute | solution.py:497
  31.0 0.3 merge.1.own_ref
  31.3 1.5 %collective-permute-start.8 = (bf16[32,1152]{1,0:T(8,128)(2,1)S(1)}, bf16[32,1152]{1,0:T(8,128)(2,1)S(1)}, u32[]{:S(2)}, u32[]{:S(2)}) collective-permute-start(bf16[32,1152]{1,0:T(8,128)(2,1)S(1)} %merge.1.own_ref), channel_id=1, source_target_pairs={{0,2},{2,0},{1,3},{3,1},{4,6},{6,4},{5,7},{7,5},{8,10},{10,8},{9,1... | collective-permute-start | bytes 221192 | tf_op jit(solution)/shard_map/ppermute | solution.py:497
  32.8 2.9 %collective-permute-done.8.far_ref = bf16[32,1152]{1,0:T(8,128)(2,1)S(1)} collective-permute-done((bf16[32,1152]{1,0:T(8,128)(2,1)S(1)}, bf16[32,1152]{1,0:T(8,128)(2,1)S(1)}, u32[]{:S(2)}, u32[]{:S(2)}) %collective-permute-start.8) | collective-permute-done | bytes 73760 | tf_op jit(solution)/shard_map/ppermute | solution.py:497
  35.6 1.0 %finish.1 = bf16[8,4096]{1,0:T(8,128)(2,1)} custom-call(bf16[32,1152]{1,0:T(8,128)(2,1)S(1)} %merge.1.own_ref, bf16[32,1152]{1,0:T(8,128)(2,1)S(1)} %collective-permute-done.8.far_ref), custom_call_target="tpu_custom_call" | custom-call | tf_op jit(solution)/shard_map/finish/pallas_call | solution.py:487
  (9 shorter events, 0.0 us)
Async XLA Ops:
  4.3 14.9 %collective-permute-start = (bf16[336,256]{1,0:T(8,128)(2,1)S(1)}, bf16[336,256]{1,0:T(8,128)(2,1)S(1)}, u32[]{:S(2)}, u32[]{:S(2)}) collective-permute-start(bf16[336,256]{1,0:T(8,128)(2,1)S(1)} %get-tuple-element.28), channel_id=1, source_target_pairs={{0,4},{4,0},{8,12},{12,8},{1,5},{5,1},{9,13},{13,9},{2,6},{6,2},{1... | collective-permute-start | bytes 516104 | tf_op jit(solution)/shard_map/ppermute | solution.py:497
  7.4 20.8 %copy-start = (bf16[1,1,8,128,1024]{4,3,2,1,0:T(8,128)(2,1)S(1)}, bf16[1,1,8,128,1024]{4,3,2,1,0:T(8,128)(2,1)}, u32[]{:S(2)}) copy-start(bf16[1,1,8,128,1024]{4,3,2,1,0:T(8,128)(2,1)} %param.14) | copy-start | bytes 6291460
  7.4 20.8 %copy-start.1 = (bf16[1,1,8,4096]{3,2,1,0:T(8,128)(2,1)S(1)}, bf16[1,1,8,4096]{3,2,1,0:T(8,128)(2,1)}, u32[]{:S(2)}) copy-start(bf16[1,1,8,4096]{3,2,1,0:T(8,128)(2,1)} %param.13) | copy-start | bytes 196612
  7.4 20.8 %copy-start.2 = (s32[8,128]{1,0:T(8,128)S(1)}, s32[8,128]{1,0:T(8,128)}, u32[]{:S(2)}) copy-start(s32[8,128]{1,0:T(8,128)} %signs_ref.1) | copy-start | bytes 12292
  7.4 20.8 %copy-start.3 = (s32[1,1,8]{2,1,0:T(1,128)S(1)}, s32[1,1,8]{2,1,0:T(1,128)}, u32[]{:S(2)}) copy-start(s32[1,1,8]{2,1,0:T(1,128)} %lengths_ref.1) | copy-start | bytes 100
  10.4 9.2 %collective-permute-start.3 = (bf16[256,256]{1,0:T(8,128)(2,1)S(1)}, bf16[256,256]{1,0:T(8,128)(2,1)S(1)}, u32[]{:S(2)}, u32[]{:S(2)}) collective-permute-start(bf16[256,256]{1,0:T(8,128)(2,1)S(1)} %get-tuple-element.33), channel_id=1, source_target_pairs={{0,4},{4,0},{8,12},{12,8},{1,5},{5,1},{9,13},{13,9},{2,6},{6,2},{1... | collective-permute-start | bytes 393224 | tf_op jit(solution)/shard_map/ppermute | solution.py:497
  10.5 5.0 %collective-permute-start.2 = (bf16[8,2176]{1,0:T(8,128)(2,1)S(1)}, bf16[8,2176]{1,0:T(8,128)(2,1)S(1)}, u32[]{:S(2)}, u32[]{:S(2)}) collective-permute-start(bf16[8,2176]{1,0:T(8,128)(2,1)S(1)} %get-tuple-element.27.own_ref), channel_id=1, source_target_pairs={{0,8},{4,12},{8,0},{12,4},{1,9},{5,13},{9,1},{13,5},{2,10},{6,14},... | collective-permute-start | bytes 104456 | tf_op jit(solution)/shard_map/ppermute | solution.py:497
  13.5 5.7 %collective-permute-start.1 = (bf16[8,2176]{1,0:T(8,128)(2,1)S(1)}, bf16[8,2176]{1,0:T(8,128)(2,1)S(1)}, u32[]{:S(2)}, u32[]{:S(2)}) collective-permute-start(bf16[8,2176]{1,0:T(8,128)(2,1)S(1)} %get-tuple-element.29), channel_id=1, source_target_pairs={{0,12},{4,8},{8,4},{12,0},{1,13},{5,9},{9,5},{13,1},{2,14},{6,10},... | collective-permute-start | bytes 104456 | tf_op jit(solution)/shard_map/ppermute | solution.py:497
  19.6 4.7 %collective-permute-start.4 = (f32[16,256]{1,0:T(8,128)S(1)}, f32[16,256]{1,0:T(8,128)S(1)}, u32[]{:S(2)}, u32[]{:S(2)}) collective-permute-start(f32[16,256]{1,0:T(8,128)S(1)} %get-tuple-element.34.scores_ref), channel_id=1, source_target_pairs={{0,8},{4,12},{8,0},{12,4},{1,9},{5,13},{9,1},{13,5},{2,10},{6,14},... | collective-permute-start | bytes 49160 | tf_op jit(solution)/shard_map/ppermute | solution.py:497
  24.6 6.4 %collective-permute-start.7 = (bf16[16,1152]{1,0:T(8,128)(2,1)S(1)}, bf16[16,1152]{1,0:T(8,128)(2,1)S(1)}, u32[]{:S(2)}, u32[]{:S(2)}) collective-permute-start(bf16[16,1152]{1,0:T(8,128)(2,1)S(1)} %get-tuple-element.40), channel_id=1, source_target_pairs={{0,4},{4,0},{8,12},{12,8},{1,5},{5,1},{9,13},{13,9},{2,6},{6,2},{1... | collective-permute-start | bytes 110600 | tf_op jit(solution)/shard_map/ppermute | solution.py:497
  24.9 5.7 %collective-permute-start.5 = (bf16[16,1024]{1,0:T(8,128)(2,1)S(1)}, bf16[16,1024]{1,0:T(8,128)(2,1)S(1)}, u32[]{:S(2)}, u32[]{:S(2)}) collective-permute-start(bf16[16,1024]{1,0:T(8,128)(2,1)S(1)} %get-tuple-element.38), channel_id=1, source_target_pairs={{0,12},{4,8},{8,4},{12,0},{1,13},{5,9},{9,5},{13,1},{2,14},{6,10},... | collective-permute-start | bytes 98312 | tf_op jit(solution)/shard_map/ppermute | solution.py:497
  26.2 4.8 %collective-permute-start.6 = (bf16[16,1024]{1,0:T(8,128)(2,1)S(1)}, bf16[16,1024]{1,0:T(8,128)(2,1)S(1)}, u32[]{:S(2)}, u32[]{:S(2)}) collective-permute-start(bf16[16,1024]{1,0:T(8,128)(2,1)S(1)} %get-tuple-element.39), channel_id=1, source_target_pairs={{0,8},{4,12},{8,0},{12,4},{1,9},{5,13},{9,1},{13,5},{2,10},{6,14},... | collective-permute-start | bytes 98312 | tf_op jit(solution)/shard_map/ppermute | solution.py:497
  31.3 4.4 %collective-permute-start.8 = (bf16[32,1152]{1,0:T(8,128)(2,1)S(1)}, bf16[32,1152]{1,0:T(8,128)(2,1)S(1)}, u32[]{:S(2)}, u32[]{:S(2)}) collective-permute-start(bf16[32,1152]{1,0:T(8,128)(2,1)S(1)} %merge.1.own_ref), channel_id=1, source_target_pairs={{0,2},{2,0},{1,3},{3,1},{4,6},{6,4},{5,7},{7,5},{8,10},{10,8},{9,1... | collective-permute-start | bytes 221192 | tf_op jit(solution)/shard_map/ppermute | solution.py:497

commit v10 on v9

--- a/solution.py
+++ b/solution.py
@@ -19,6 +19,10 @@
 
 def in_hbm(x):
     return pltpu.with_memory_space_constraint(x, pltpu.HBM)
+
+
+def in_vmem(x):
+    return pltpu.with_memory_space_constraint(x, pltpu.VMEM)
 
 
 def hadamard_tile(order):
@@ -31,7 +35,8 @@
     return (1 - 2 * (parity & 1)).astype(jnp.float32).astype(jnp.bfloat16)
 
 
-QUERY_ORDER = (1, 3, 2)
+QUERY_ORDER = (3, 2, 1)
+SCORE_ORDER = (1, 3, 2)
 MIXED_ORDER = (3, 2, 1)
 
 
@@ -47,154 +52,77 @@
     return lax.axis_index("seq") & 1
 
 
-def start_all(copies):
+def project_kernel(tokens_ref, weight_ref, keys_ref, own_ref, near_ref, acc_ref):
+    width = keys_ref.shape[1]
+    half = own_ref.shape[1]
+    keys_ref[...] = jnp.dot(
+        tokens_ref[...], weight_ref[:, :width], preferred_element_type=jnp.float32
+    ).astype(keys_ref.dtype)
+    acc_ref[...] = jnp.dot(tokens_ref[...], weight_ref[:, width:], preferred_element_type=jnp.float32)
+    mine = pl.multiple_of(side() * half, half)
+    other = pl.multiple_of((1 - side()) * half, half)
+    own_ref[...] = acc_ref[:, pl.ds(mine, half)].astype(own_ref.dtype)
+    near_ref[...] = acc_ref[:, pl.ds(other, half)].astype(near_ref.dtype)
+
+
+def project(tokens, weight):
+    rows, features = tokens.shape
+    width = weight.shape[1] // 2
+    vmem = pl.BlockSpec(memory_space=pltpu.VMEM)
+    return pl.pallas_call(
+        project_kernel,
+        in_specs=[vmem] * 2,
+        out_specs=[vmem] * 3,
+        out_shape=[jax.ShapeDtypeStruct((rows, columns), jnp.bfloat16) for columns in (width, width // 2, width // 2)],
+        scratch_shapes=[pltpu.VMEM((rows, width), jnp.float32)],
+        compiler_params=params(32),
+        cost_estimate=pl.CostEstimate(
+            flops=4 * rows * features * width,
+            bytes_accessed=2 * (rows * features + 2 * features * width),
+            transcendentals=0,
+        ),
+        name="project",
+    )(in_vmem(tokens), in_vmem(weight))
+
+
+def message_kernel(query_ref, owners_ref, requests_ref, out_ref, query_buf, owners_buf, requests_buf, sems):
+    requests, columns = query_ref.shape
+    per_device = owners_ref.shape[1]
+    copies = [
+        pltpu.make_async_copy(source, target, sems.at[i])
+        for i, (source, target) in enumerate(
+            ((query_ref, query_buf), (owners_ref, owners_buf), (requests_ref, requests_buf))
+        )
+    ]
     for copy in copies:
         copy.start()
-    return copies
-
-
-def accumulate(tokens_ref, weight_buf, acc_ref, copies):
-    steps, block, _ = weight_buf.shape
-    for step in range(steps):
-        for copy in copies[step]:
-            copy.wait()
-        tokens = tokens_ref[:, step * block : (step + 1) * block]
-        part = jnp.dot(tokens, weight_buf[step], preferred_element_type=jnp.float32)
-        acc_ref[...] = part if step == 0 else acc_ref[...] + part
-
-
-def halves(acc_ref):
-    width = acc_ref.shape[1] // 2
-    mine = pl.multiple_of(side() * width, width)
-    other = pl.multiple_of((1 - side()) * width, width)
-    return acc_ref[:, pl.ds(mine, width)], acc_ref[:, pl.ds(other, width)]
-
-
-def keys_kernel(
-    query_ref, owners_ref, requests_ref, tokens_ref, weight_ref,
-    tokens_out, own_ref, near_ref, same_ref, other_ref,
-    query_buf, owners_buf, requests_buf, weight_buf, acc_ref, small_sems, sems,
-):
-    requests, columns = query_ref.shape
-    per_device = owners_ref.shape[1]
-    rows = tokens_ref.shape[0]
-    steps, block, width = weight_buf.shape
-    half = columns // 2
-    small = start_all(
-        [
-            pltpu.make_async_copy(query_ref, query_buf, small_sems.at[0]),
-            pltpu.make_async_copy(owners_ref, owners_buf, small_sems.at[1]),
-            pltpu.make_async_copy(requests_ref, requests_buf, small_sems.at[2]),
-        ]
-    )
-    copies = []
-    for step in range(steps):
-        span = slice(step * block, (step + 1) * block)
-        copies.append(
-            start_all(
-                [
-                    pltpu.make_async_copy(tokens_ref.at[:, span], tokens_out.at[:, span], sems.at[0, step]),
-                    pltpu.make_async_copy(weight_ref.at[span, :width], weight_buf.at[step], sems.at[1, step]),
-                ]
-            )
-        )
-    for copy in small:
+    for copy in copies:
         copy.wait()
+    out_ref[:, :columns] = query_buf[...]
     code = (owners_buf[...] * requests + requests_buf[...]).astype(jnp.float32)
-    near_width = near_ref.shape[1]
-    spare = jnp.zeros((1, near_width - per_device), jnp.float32)
-    code = jnp.broadcast_to(jnp.concatenate([code, spare], axis=1), (2 * requests, near_width))
-    lanes = same_ref.shape[1] - half
-    mine = pl.multiple_of(side() * half, half)
-    other = pl.multiple_of((1 - side()) * half, half)
-    same_ref[:, :half] = query_buf[:, pl.ds(mine, half)]
-    same_ref[:, half:] = code[:requests, :lanes].astype(same_ref.dtype)
-    far_query = query_buf[:, pl.ds(other, half)]
-    other_ref[:, :half] = far_query
-    other_ref[:, half:] = code[:requests, :lanes].astype(same_ref.dtype)
-    stacked = far_query.astype(jnp.float32)
-    stacked = jnp.concatenate([stacked[:, at : at + near_width] for at in range(0, half, near_width)], axis=0)
-    near_ref[rows : rows + stacked.shape[0], :] = stacked.astype(near_ref.dtype)
-    near_ref[rows + stacked.shape[0] :, :] = code.astype(near_ref.dtype)
-    accumulate(tokens_out, weight_buf, acc_ref, copies)
-    kept, sent = halves(acc_ref)
-    own_ref[...] = kept.astype(own_ref.dtype)
-    near_ref[:rows, :] = sent.astype(near_ref.dtype)
-
-
-def project_keys(query, owners, requests, tokens, weight):
+    spare = jnp.zeros((1, out_ref.shape[1] - columns - per_device), jnp.float32)
+    code = jnp.concatenate([code, spare], axis=1)
+    out_ref[:, columns:] = jnp.broadcast_to(code, (requests, code.shape[1])).astype(out_ref.dtype)
+
+
+def make_message(query, owners, requests):
     count, columns = query.shape
-    rows, features = tokens.shape
-    width = weight.shape[1] // 2
-    block = min(512, features // 2)
-    steps = features // block
-    half = columns // 2
     lanes = -(-owners.shape[1] // 128) * 128
-    near_rows = rows + count * half // (width // 2) + 2 * count
-    vmem = pl.BlockSpec(memory_space=pltpu.VMEM)
     return pl.pallas_call(
-        keys_kernel,
-        in_specs=[pl.BlockSpec(memory_space=pl.ANY)] * 5,
-        out_specs=[vmem] * 5,
-        out_shape=[
-            jax.ShapeDtypeStruct(tokens.shape, tokens.dtype),
-            jax.ShapeDtypeStruct((rows, width // 2), jnp.bfloat16),
-            jax.ShapeDtypeStruct((near_rows, width // 2), jnp.bfloat16),
-            jax.ShapeDtypeStruct((count, half + lanes), query.dtype),
-            jax.ShapeDtypeStruct((count, half + lanes), query.dtype),
-        ],
+        message_kernel,
+        in_specs=[pl.BlockSpec(memory_space=pl.ANY)] * 3,
+        out_specs=pl.BlockSpec(memory_space=pltpu.VMEM),
+        out_shape=jax.ShapeDtypeStruct((count, columns + lanes), query.dtype),
         scratch_shapes=[
             pltpu.VMEM(query.shape, query.dtype),
             pltpu.VMEM(owners.shape, owners.dtype),
             pltpu.VMEM(requests.shape, requests.dtype),
-            pltpu.VMEM((steps, block, width), weight.dtype),
-            pltpu.VMEM((rows, width), jnp.float32),
             pltpu.SemaphoreType.DMA((3,)),
-            pltpu.SemaphoreType.DMA((2, steps)),
         ],
-        compiler_params=params(),
-        name="project_keys",
-    )(in_hbm(query), in_hbm(owners), in_hbm(requests), in_hbm(tokens), in_hbm(weight))
-
-
-def values_kernel(tokens_ref, weight_ref, own_ref, near_ref, weight_buf, acc_ref, sems):
-    steps, block, width = weight_buf.shape
-    copies = []
-    for step in range(steps):
-        span = slice(step * block, (step + 1) * block)
-        copies.append(
-            start_all([pltpu.make_async_copy(weight_ref.at[span, width:], weight_buf.at[step], sems.at[step])])
-        )
-    accumulate(tokens_ref, weight_buf, acc_ref, copies)
-    kept, sent = halves(acc_ref)
-    own_ref[...] = kept.astype(own_ref.dtype)
-    near_ref[...] = sent.astype(near_ref.dtype)
-
-
-def project_values(tokens, weight):
-    rows, features = tokens.shape
-    width = weight.shape[1] // 2
-    block = min(512, features // 2)
-    steps = features // block
-    vmem = pl.BlockSpec(memory_space=pltpu.VMEM)
-    return pl.pallas_call(
-        values_kernel,
-        in_specs=[vmem, pl.BlockSpec(memory_space=pl.ANY)],
-        out_specs=[vmem] * 2,
-        out_shape=[jax.ShapeDtypeStruct((rows, width // 2), jnp.bfloat16)] * 2,
-        scratch_shapes=[
-            pltpu.VMEM((steps, block, width), weight.dtype),
-            pltpu.VMEM((rows, width), jnp.float32),
-            pltpu.SemaphoreType.DMA((steps,)),
-        ],
-        compiler_params=params(),
-        cost_estimate=pl.CostEstimate(
-            flops=2 * rows * features * width,
-            bytes_accessed=2 * features * width,
-            transcendentals=0,
-        ),
-        name="project_values",
-    )(tokens, in_hbm(weight))
+        compiler_params=params(16),
+        cost_estimate=pl.CostEstimate(flops=10**11, bytes_accessed=10**4, transcendentals=0),
+        name="make_message",
+    )(in_hbm(query), in_hbm(owners), in_hbm(requests))
 
 
 def cache_kernel(
@@ -282,46 +210,36 @@
     )(lengths, query, cache, signs)
 
 
-def score_kernel(heads, keys_ref, own_ref, *refs):
-    message_refs, (scores_ref, code_ref) = by_distance((own_ref,) + refs[:-2], QUERY_ORDER), refs[-2:]
-    near_ref = message_refs[1]
-    requests = own_ref.shape[0]
+def code_row(message_refs, start, requests, tokens):
+    count = len(message_refs)
+    me = lax.axis_index("seq")
+    pieces = [ref[0:1, start : start + tokens // count].astype(jnp.float32) for ref in message_refs]
+    row = [sum(jnp.where(me ^ d == at, pieces[d], 0.0) for d in range(count)) for at in range(count)]
+    code = jnp.concatenate(row, axis=1).astype(jnp.int32)
+    return ((code // requests) ^ me) * requests + code % requests
+
+
+def score_kernel(heads, start, keys_ref, values_ref, *refs):
+    message_refs, refs = by_distance(refs[:-5], QUERY_ORDER), refs[-5:]
+    scores_ref, same_ref, other_ref, near_ref, code_ref = refs
+    requests = message_refs[0].shape[0]
     tokens, width = keys_ref.shape
     size = width // heads
-    count = len(message_refs)
-    half = scores_ref.shape[0] * size
-    group = scores_ref.shape[0] // heads
-    stacked = near_ref[tokens:, :].astype(jnp.float32)
-    spread = requests * half // width
-    near_query = jnp.concatenate(
-        [stacked[at * requests : (at + 1) * requests] for at in range(half // width)], axis=1
-    )
-    queries, codes = [], []
-    for d, ref in enumerate(message_refs):
-        if d == 1:
-            queries.append(near_query)
-            codes.append(stacked[spread : spread + 1, : tokens // count])
-        else:
-            queries.append(ref[:, :half].astype(jnp.float32))
-            codes.append(ref[0:1, half : half + tokens // count].astype(jnp.float32))
-    me = lax.axis_index("seq")
-    row = [sum(jnp.where(me ^ d == at, codes[d], 0.0) for d in range(count)) for at in range(count)]
-    code = jnp.concatenate(row, axis=1).astype(jnp.int32)
-    code = ((code // requests) ^ me) * requests + code % requests
+    group = start // width
+    half = same_ref.shape[0]
+    code = code_row(message_refs, start, requests, tokens)
     code_ref[...] = jnp.broadcast_to(code, code_ref.shape)
-    span = count * requests
+    span = len(message_refs) * requests
     here = lax.broadcasted_iota(jnp.int32, (span, tokens), 0) == code
+    queries = [ref[:, :start].astype(jnp.float32) for ref in message_refs]
     for k in range(heads):
         rows = []
         for g in range(group):
             at = (k * group + g) * size
             rows += [query[:, at : at + size] for query in queries]
         query = jnp.concatenate(rows, axis=0).astype(jnp.bfloat16)
-        columns = slice(k * size, (k + 1) * size)
-        scores = lax.dot_general(query, keys_ref[:, columns], NT, preferred_element_type=jnp.float32)
-        scores = scores + lax.dot_general(
-            query, near_ref[:tokens, columns], NT, preferred_element_type=jnp.float32
-        )
+        keys = keys_ref[:, k * size : (k + 1) * size]
+        scores = lax.dot_general(query, keys, NT, preferred_element_type=jnp.float32)
         lines = [
             jnp.sum(jnp.where(here, scores[g * span : (g + 1) * span], 0.0), axis=0, keepdims=True)
             for g in range(group)
@@ -329,19 +247,34 @@
         scores_ref[k * group : (k + 1) * group, :] = jnp.concatenate(lines, axis=0) * (
             1.0 / math.sqrt(size)
         )
-
-
-def pair_scores(heads, half, keys, messages):
+    same_ref[...] = scores_ref[pl.ds(pl.multiple_of(side() * half, half), half), :]
+    other = scores_ref[pl.ds(pl.multiple_of((1 - side()) * half, half), half), :]
+    other_ref[...] = other
+    near_ref[:tokens, :] = values_ref[...]
+    for part in range(3):
+        piece = other.astype(near_ref.dtype)
+        near_ref[tokens + part * half : tokens + (part + 1) * half, :] = piece
+        other = other - piece.astype(jnp.float32)
+
+
+def partial_scores(heads, columns, keys, values, messages):
     tokens, width = keys.shape
+    query_heads = columns * heads // width
+    vmem = pl.BlockSpec(memory_space=pltpu.VMEM)
     return pl.pallas_call(
-        functools.partial(score_kernel, heads),
+        functools.partial(score_kernel, heads, columns),
+        in_specs=[vmem] * (2 + len(messages)),
+        out_specs=[vmem] * 5,
         out_shape=[
-            jax.ShapeDtypeStruct((half * heads // width, tokens), jnp.float32),
+            jax.ShapeDtypeStruct((query_heads, tokens), jnp.float32),
+            jax.ShapeDtypeStruct((query_heads // 2, tokens), jnp.float32),
+            jax.ShapeDtypeStruct((query_heads // 2, tokens), jnp.float32),
+            jax.ShapeDtypeStruct((tokens + 3 * query_heads // 2, values.shape[1]), values.dtype),
             jax.ShapeDtypeStruct((8, tokens), jnp.int32),
         ],
         compiler_params=params(),
-        name="pair_scores",
-    )(keys, *arranged(messages, QUERY_ORDER))
+        name="partial_scores",
+    )(keys, values, *arranged(messages, QUERY_ORDER))[1:]
 
 
 def packed(value, group, size):
@@ -371,14 +304,20 @@
     return jnp.concatenate([jnp.broadcast_to(narrow[:, g : g + 1], (rows, size)) for g in range(group)], axis=1)
 
 
-def mix_kernel(heads, count, requests, code_ref, own_ref, near_ref, scores_ref, far_scores_ref, *refs):
-    mixed_refs, (tops_ref, totals_ref) = refs[:count], refs[count:]
+def mix_kernel(heads, count, requests, code_ref, own_ref, *refs):
+    score_refs = by_distance(refs[:count], SCORE_ORDER)
+    mixed_refs, (tops_ref, totals_ref) = refs[count : 2 * count], refs[2 * count :]
     tokens, width = own_ref.shape
     size = width // heads
-    group = scores_ref.shape[0] // heads
+    group = score_refs[0].shape[0] // heads
     span = count * requests
     here = lax.broadcasted_iota(jnp.int32, (span, tokens), 0) == code_ref[0:1, :]
-    scores = scores_ref[...] + far_scores_ref[...]
+    near_ref, half = score_refs[1], score_refs[0].shape[0]
+    parts = [
+        near_ref[tokens + part * half : tokens + (part + 1) * half, :].astype(jnp.float32) for part in range(3)
+    ]
+    near_scores = (parts[0] + parts[1]) + parts[2]
+    scores = (score_refs[0][...] + score_refs[2][...]) + (near_scores + score_refs[3][...])
     mixed, tops, totals = [], [], []
     for k in range(heads):
         weights = []
@@ -393,7 +332,7 @@
         weights = jnp.concatenate(weights, axis=0).astype(jnp.bfloat16)
         columns = slice(k * size, (k + 1) * size)
         sums = jnp.dot(weights, own_ref[:, columns], preferred_element_type=jnp.float32)
-        mixed.append(sums + jnp.dot(weights, near_ref[:, columns], preferred_element_type=jnp.float32))
+        mixed.append(sums + jnp.dot(weights, near_ref[:tokens, columns], preferred_element_type=jnp.float32))
 
     def block(parts, d):
         rows = slice(d * requests, (d + 1) * requests)
@@ -411,9 +350,10 @@
     totals_ref[...] = block(totals, 0)
 
 
-def mix(heads, count, requests, code, values, near_values, scores, far_scores):
+def mix(heads, requests, code, values, scores):
+    count = len(scores)
     size = values.shape[1] // heads
-    columns = scores.shape[0] // heads * size
+    columns = scores[0].shape[0] // heads * size
     shape = (heads * requests, columns)
     wide = (heads * requests, columns + size)
     return pl.pallas_call(
@@ -422,7 +362,7 @@
         + [jax.ShapeDtypeStruct(shape, jnp.float32)] * 2,
         compiler_params=params(),
         name="mix",
-    )(code, values, near_values, scores, far_scores)
+    )(code, values, *arranged(scores, SCORE_ORDER))
 
 
 def merge_kernel(cache_ref, top_ref, total_ref, new_top_ref, new_total_ref, *refs):
@@ -497,26 +437,24 @@
     return lax.ppermute(x, axis, [(i, i ^ distance) for i in range(count)])
 
 
+def exchange(blocks):
+    return [blocks[0]] + [from_partner(blocks[d], "seq", d) for d in range(1, len(blocks))]
+
+
 def on_device(tokens, kv_weight, owners, requests, signs, queries, kv_cache, lengths):
     seq_count = lax.axis_size("seq")
     blocks, size = signs.shape
-    kept_heads = blocks // 4
+    heads = blocks // 2
     query = queries[0, 0]
     request_count, columns = query.shape
-    tokens, keys, near, same, other = project_keys(query, owners[:, :, 0], requests, tokens, kv_weight)
-    messages = [
-        same,
-        from_partner(near, "seq", 1),
-        from_partner(same, "seq", 2),
-        from_partner(other, "seq", 3),
-    ]
-    values, far_values = project_values(tokens, kv_weight)
-    near_values = from_partner(far_values, "seq", 1)
-    scores, code = pair_scores(kept_heads, columns // 2, keys, messages)
-    far_scores = from_partner(scores, "seq", 2)
-    results = mix(kept_heads, seq_count, request_count, code, values, near_values, scores, far_scores)
+    message = make_message(query, owners[:, :, 0], requests)
+    messages = exchange([message] * seq_count)
+    keys, values, far_values = project(tokens, kv_weight)
+    same, other, near, code = partial_scores(heads, columns, keys, far_values, messages)
+    scores = exchange([same, near, same, other])
+    results = mix(heads // 2, request_count, code, values, scores)
     mixed, (new_tops, new_totals) = results[:seq_count], results[seq_count:]
-    mixed = [mixed[0]] + [from_partner(mixed[d], "seq", d) for d in range(1, seq_count)]
+    mixed = exchange(mixed)
     cache_mixed, tops, totals = cache_part(lengths, query, kv_cache[0, 0], signs)
     own = merge(size, cache_mixed, tops, totals, new_tops, new_totals, mixed)
     far = from_partner(own, "tp", 1)

time: 36.8 us -> 34.5 us (0.938)
  Pallas kernels: 10.9 us -> 7.63 us
  starting transfers between devices: 12.7 us -> 15.2 us
  waiting for transfers between devices: 13 us -> 11.4 us
    pallas_call x3, Pallas kernels: 7.59 us -> 4.36 us  [the longest x1 2.4 us: project(): pl.pallas_call(project_kernel, in_specs=[vmem] * 2, out_specs=[vmem] * 3,...]
    ppermute x9 -> x10, starting transfers between devices: 12.7 us -> 15.2 us  [from_partner(): return lax.ppermute(x, axis, [(i, i ^ distance) for i in range(count)])]
    ppermute x9 -> x10, waiting for transfers between devices: 13 us -> 11.4 us  [from_partner(): return lax.ppermute(x, axis, [(i, i ^ distance) for i in range(count)])]
  transfers between devices with their start and end apart: 9 -> 10, of which waited for: 6 -> 6; matrix products, arithmetic and copies ran while one was open for 0% -> 0% of each run, Pallas kernels for 13% -> 12%
where the time goes in v10:
time: 34.5 us; the launch traced here: 34.3 us
  starting transfers between devices  15.2 us (44%)
  waiting for transfers between devices  11.4 us (33%)
  Pallas kernels  7.63 us (22%)
    ppermute x10, starting transfers between devices, from_partner(): return lax.ppermute(x, axis, [(i, i ^ distance) for i in range(count)])  15.2 us
    ppermute x10, waiting for transfers between devices, from_partner(): return lax.ppermute(x, axis, [(i, i ^ distance) for i in range(count)])  11.4 us
    pallas_call x1, Pallas kernels, project(): pl.pallas_call(project_kernel, in_specs=[vmem] * 2, out_specs=[vmem] * 3,...  2.4 us
    pallas_call x1, Pallas kernels, cache_part(): pl.pallas_call(cache_kernel, in_specs=[pl.BlockSpec(memory_space=pltpu.SM...  1.61 us
    pallas_call x1, Pallas kernels, make_message(): pl.pallas_call(message_kernel, in_specs=[pl.BlockSpec(memory_space=pl.ANY...  1.03 us
    pallas_call x1, Pallas kernels, finish(): pl.pallas_call(finish_kernel, out_shape=jax.ShapeDtypeStruct((requests, c...  1.01 us
    pallas_call x1, Pallas kernels, partial_scores(): pl.pallas_call(functools.partial(score_kernel, heads, columns), in_specs=...  0.92 us
  transfers between devices with their start and end apart: 10, of which 6 were waited for; matrix products, arithmetic and copies ran while one was open for 0% of the time, Pallas kernels for 12%

profile of v10, /device:TPU:0, one launch (start us, length us, event | category | flops | bytes accessed | tf_op | source)
XLA Modules:
  0.0 34.3 jit_solution(12697006927408328027)
XLA Ops:
  0.0 1.0 %make_message.1.refs_0_ = bf16[8,4224]{1,0:T(8,128)(2,1)S(1)} custom-call(bf16[8,4096]{1,0:T(8,128)(2,1)} %bitcast.7, s32[1,64]{1,0:T(1,128)} %bitcast.9, s32[1,64]{1,0:T(1,128)} %requests_ref.1), custom_call_target="tpu_custom_call" | custom-call | flops 99999997952 | bytes 10000 | tf_op jit(solution)/shard_map/make_message/pallas_call | solution.py:111
  1.0 0.0 copy-start.2
  1.1 0.0 copy-start.3
  1.1 5.1 %collective-permute-start = (bf16[8,4224]{1,0:T(8,128)(2,1)S(1)}, bf16[8,4224]{1,0:T(8,128)(2,1)S(1)}, u32[]{:S(2)}, u32[]{:S(2)}) collective-permute-start(bf16[8,4224]{1,0:T(8,128)(2,1)S(1)} %make_message.1.refs_0_), channel_id=1, source_target_pairs={{0,12},{4,8},{8,4},{12,0},{1,13},{5,9},{9,5},{13,1},{2,14},{6,10},... | collective-permute-start | bytes 202760 | tf_op jit(solution)/shard_map/ppermute | solution.py:437
  6.2 0.6 %collective-permute-start.2 = (bf16[8,4224]{1,0:T(8,128)(2,1)S(1)}, bf16[8,4224]{1,0:T(8,128)(2,1)S(1)}, u32[]{:S(2)}, u32[]{:S(2)}) collective-permute-start(bf16[8,4224]{1,0:T(8,128)(2,1)S(1)} %make_message.1.refs_0_), channel_id=1, source_target_pairs={{0,4},{4,0},{8,12},{12,8},{1,5},{5,1},{9,13},{13,9},{2,6},{6,2},{1... | collective-permute-start | bytes 202760 | tf_op jit(solution)/shard_map/ppermute | solution.py:437
  6.9 2.4 %project.1 = (bf16[256,512]{1,0:T(8,128)(2,1)S(1)}, bf16[256,256]{1,0:T(8,128)(2,1)S(1)}, bf16[256,256]{1,0:T(8,128)(2,1)S(1)}) custom-call(bf16[256,4096]{1,0:T(8,128)(2,1)S(1)} %copy-done, bf16[4096,1024]{1,0:T(8,128)(2,1)S(1)} %bitcast.5), custom_call_target="tpu_custom_call" | custom-call | flops 2147483648 | bytes 10485760 | tf_op jit(solution)/shard_map/project/pallas_call | solution.py:72
  9.3 2.7 %collective-permute-done.1.refs_2_ = bf16[8,4224]{1,0:T(8,128)(2,1)S(1)} collective-permute-done((bf16[8,4224]{1,0:T(8,128)(2,1)S(1)}, bf16[8,4224]{1,0:T(8,128)(2,1)S(1)}, u32[]{:S(2)}, u32[]{:S(2)}) %collective-permute-start.1) | collective-permute-done | bytes 67616 | tf_op jit(solution)/shard_map/ppermute | solution.py:437
  12.0 0.9 %partial_scores.1 = (f32[32,256]{1,0:T(8,128)}, f32[16,256]{1,0:T(8,128)S(1)}, f32[16,256]{1,0:T(8,128)S(1)}, bf16[304,256]{1,0:T(8,128)(2,1)S(1)}, s32[8,256]{1,0:T(8,128)S(1)}) custom-call(bf16[256,512]{1,0:T(8,128)(2,1)S(1)} %get-tuple-element.24.keys_ref, bf16[256,256]{1,0:T(8,128)(2,1)S(1)} %get-tuple-element.25.values_ref, ...), custom_call_target="tpu_custom_call" | custom-call | tf_op jit(solution)/shard_map/partial_scores/pallas_call | solution.py:264
  12.9 1.1 %collective-permute-start.3 = (bf16[304,256]{1,0:T(8,128)(2,1)S(1)}, bf16[304,256]{1,0:T(8,128)(2,1)S(1)}, u32[]{:S(2)}, u32[]{:S(2)}) collective-permute-start(bf16[304,256]{1,0:T(8,128)(2,1)S(1)} %get-tuple-element.29), channel_id=1, source_target_pairs={{0,4},{4,0},{8,12},{12,8},{1,5},{5,1},{9,13},{13,9},{2,6},{6,2},{1... | collective-permute-start | bytes 466952 | tf_op jit(solution)/shard_map/ppermute | solution.py:437
  13.9 2.2 %collective-permute-start.5 = (f32[16,256]{1,0:T(8,128)S(1)}, f32[16,256]{1,0:T(8,128)S(1)}, u32[]{:S(2)}, u32[]{:S(2)}) collective-permute-start(f32[16,256]{1,0:T(8,128)S(1)} %get-tuple-element.28.refs_0_), channel_id=1, source_target_pairs={{0,8},{4,12},{8,0},{12,4},{1,9},{5,13},{9,1},{13,5},{2,10},{6,14},... | collective-permute-start | bytes 49160 | tf_op jit(solution)/shard_map/ppermute | solution.py:437
  16.2 1.1 %collective-permute-start.4 = (f32[16,256]{1,0:T(8,128)S(1)}, f32[16,256]{1,0:T(8,128)S(1)}, u32[]{:S(2)}, u32[]{:S(2)}) collective-permute-start(f32[16,256]{1,0:T(8,128)S(1)} %get-tuple-element.30), channel_id=1, source_target_pairs={{0,12},{4,8},{8,4},{12,0},{1,13},{5,9},{9,5},{13,1},{2,14},{6,10},... | collective-permute-start | bytes 49160 | tf_op jit(solution)/shard_map/ppermute | solution.py:437
  17.3 1.5 %collective-permute-done.5.refs_3_ = f32[16,256]{1,0:T(8,128)S(1)} collective-permute-done((f32[16,256]{1,0:T(8,128)S(1)}, f32[16,256]{1,0:T(8,128)S(1)}, u32[]{:S(2)}, u32[]{:S(2)}) %collective-permute-start.5) | collective-permute-done | bytes 16416 | tf_op jit(solution)/shard_map/ppermute | solution.py:437
  18.8 3.0 %collective-permute-done.4.refs_2_ = f32[16,256]{1,0:T(8,128)S(1)} collective-permute-done((f32[16,256]{1,0:T(8,128)S(1)}, f32[16,256]{1,0:T(8,128)S(1)}, u32[]{:S(2)}, u32[]{:S(2)}) %collective-permute-start.4) | collective-permute-done | bytes 16416 | tf_op jit(solution)/shard_map/ppermute | solution.py:437
  21.7 0.4 %mix.1 = (bf16[16,1024]{1,0:T(8,128)(2,1)S(1)}, bf16[16,1152]{1,0:T(8,128)(2,1)S(1)}, bf16[16,1024]{1,0:T(8,128)(2,1)S(1)}, bf16[16,1024]{1,0:T(8,128)(2,1)S(1)}...) custom-call(s32[8,256]{1,0:T(8,128)S(1)} %get-tuple-element.26.code_ref, ...), custom_call_target="tpu_custom_call" | custom-call | tf_op jit(solution)/shard_map/mix/pallas_call | solution.py:359
  22.1 0.1 collective-permute-start.8
  22.2 1.2 %collective-permute-start.6 = (bf16[16,1024]{1,0:T(8,128)(2,1)S(1)}, bf16[16,1024]{1,0:T(8,128)(2,1)S(1)}, u32[]{:S(2)}, u32[]{:S(2)}) collective-permute-start(bf16[16,1024]{1,0:T(8,128)(2,1)S(1)} %get-tuple-element.34), channel_id=1, source_target_pairs={{0,12},{4,8},{8,4},{12,0},{1,13},{5,9},{9,5},{13,1},{2,14},{6,10},... | collective-permute-start | bytes 98312 | tf_op jit(solution)/shard_map/ppermute | solution.py:437
  23.3 2.3 %collective-permute-start.7 = (bf16[16,1024]{1,0:T(8,128)(2,1)S(1)}, bf16[16,1024]{1,0:T(8,128)(2,1)S(1)}, u32[]{:S(2)}, u32[]{:S(2)}) collective-permute-start(bf16[16,1024]{1,0:T(8,128)(2,1)S(1)} %get-tuple-element.35), channel_id=1, source_target_pairs={{0,8},{4,12},{8,0},{12,4},{1,9},{5,13},{9,1},{13,5},{2,10},{6,14},... | collective-permute-start | bytes 98312 | tf_op jit(solution)/shard_map/ppermute | solution.py:437
  25.7 1.6 %cache_part.1 = (f32[32,1024]{1,0:T(8,128)S(1)}, f32[32,1024]{1,0:T(8,128)S(1)}, f32[32,1024]{1,0:T(8,128)S(1)}) custom-call(s32[1,1,8]{2,1,0:T(1,128)S(1)} %copy-done.4, bf16[8,4096]{1,0:T(8,128)(2,1)S(1)} %bitcast.8, bf16[8,128,1024]{2,1,0:T(8,128)(2,1)S(1)} %bitcast.6, s32[8,128]{1,0:T(8,128)S(1)} %copy-done.3), custom_call_target="tpu_custom_call" | custom-call | flops 16777216 | bytes 2097152 | tf_op jit(solution)/shard_map/cache_part/pallas_call | solution.py:198
  27.3 0.7 %collective-permute-done.6.refs_1_ = bf16[16,1024]{1,0:T(8,128)(2,1)S(1)} collective-permute-done((bf16[16,1024]{1,0:T(8,128)(2,1)S(1)}, bf16[16,1024]{1,0:T(8,128)(2,1)S(1)}, u32[]{:S(2)}, u32[]{:S(2)}) %collective-permute-start.6) | collective-permute-done | bytes 32800 | tf_op jit(solution)/shard_map/ppermute | solution.py:437
  28.0 0.7 %collective-permute-done.7.refs_2_ = bf16[16,1024]{1,0:T(8,128)(2,1)S(1)} collective-permute-done((bf16[16,1024]{1,0:T(8,128)(2,1)S(1)}, bf16[16,1024]{1,0:T(8,128)(2,1)S(1)}, u32[]{:S(2)}, u32[]{:S(2)}) %collective-permute-start.7) | collective-permute-done | bytes 32800 | tf_op jit(solution)/shard_map/ppermute | solution.py:437
  28.7 0.3 merge.1.own_ref
  28.9 1.5 %collective-permute-start.9 = (bf16[32,1152]{1,0:T(8,128)(2,1)S(1)}, bf16[32,1152]{1,0:T(8,128)(2,1)S(1)}, u32[]{:S(2)}, u32[]{:S(2)}) collective-permute-start(bf16[32,1152]{1,0:T(8,128)(2,1)S(1)} %merge.1.own_ref), channel_id=1, source_target_pairs={{0,2},{2,0},{1,3},{3,1},{4,6},{6,4},{5,7},{7,5},{8,10},{10,8},{9,1... | collective-permute-start | bytes 221192 | tf_op jit(solution)/shard_map/ppermute | solution.py:437
  30.4 2.9 %collective-permute-done.9.far_ref = bf16[32,1152]{1,0:T(8,128)(2,1)S(1)} collective-permute-done((bf16[32,1152]{1,0:T(8,128)(2,1)S(1)}, bf16[32,1152]{1,0:T(8,128)(2,1)S(1)}, u32[]{:S(2)}, u32[]{:S(2)}) %collective-permute-start.9) | collective-permute-done | bytes 73760 | tf_op jit(solution)/shard_map/ppermute | solution.py:437
  33.3 1.0 %finish.1 = bf16[8,4096]{1,0:T(8,128)(2,1)} custom-call(bf16[32,1152]{1,0:T(8,128)(2,1)S(1)} %merge.1.own_ref, bf16[32,1152]{1,0:T(8,128)(2,1)S(1)} %collective-permute-done.9.far_ref), custom_call_target="tpu_custom_call" | custom-call | tf_op jit(solution)/shard_map/finish/pallas_call | solution.py:427
  (18 shorter events, 0.0 us)
Async XLA Ops:
  0.0 6.8 %slice-start = ((s8[8388608]{0:T(1024)(128)(4,1)}), s8[4194304]{0:T(1024)(128)(4,1)S(1)}, s32[]{:S(2)}) async-start(s8[8388608]{0:T(1024)(128)(4,1)} %bitcast.4), calls=%async_computation | async-start | bytes 8388608
  0.0 6.8 %slice-start.1 = ((s8[8388608]{0:T(1024)(128)(4,1)}), s8[4194304]{0:T(1024)(128)(4,1)S(1)}, s32[]{:S(2)}) async-start(s8[8388608]{0:T(1024)(128)(4,1)} %bitcast.4), calls=%async_computation.1 | async-start | bytes 8388608
  0.0 6.8 %copy-start = (bf16[256,4096]{1,0:T(8,128)(2,1)S(1)}, bf16[256,4096]{1,0:T(8,128)(2,1)}, u32[]{:S(2)}) copy-start(bf16[256,4096]{1,0:T(8,128)(2,1)} %tokens_ref.1) | copy-start | bytes 6291460
  1.0 24.6 %copy-start.2 = (bf16[1,1,8,4096]{3,2,1,0:T(8,128)(2,1)S(1)}, bf16[1,1,8,4096]{3,2,1,0:T(8,128)(2,1)}, u32[]{:S(2)}) copy-start(bf16[1,1,8,4096]{3,2,1,0:T(8,128)(2,1)} %param.13) | copy-start | bytes 196612
  1.1 24.6 %copy-start.3 = (s32[8,128]{1,0:T(8,128)S(1)}, s32[8,128]{1,0:T(8,128)}, u32[]{:S(2)}) copy-start(s32[8,128]{1,0:T(8,128)} %signs_ref.1) | copy-start | bytes 12292
  1.1 24.6 %copy-start.4 = (s32[1,1,8]{2,1,0:T(1,128)S(1)}, s32[1,1,8]{2,1,0:T(1,128)}, u32[]{:S(2)}) copy-start(s32[1,1,8]{2,1,0:T(1,128)} %lengths_ref.1) | copy-start | bytes 100
  1.1 8.2 %collective-permute-start = (bf16[8,4224]{1,0:T(8,128)(2,1)S(1)}, bf16[8,4224]{1,0:T(8,128)(2,1)S(1)}, u32[]{:S(2)}, u32[]{:S(2)}) collective-permute-start(bf16[8,4224]{1,0:T(8,128)(2,1)S(1)} %make_message.1.refs_0_), channel_id=1, source_target_pairs={{0,12},{4,8},{8,4},{12,0},{1,13},{5,9},{9,5},{13,1},{2,14},{6,10},... | collective-permute-start | bytes 202760 | tf_op jit(solution)/shard_map/ppermute | solution.py:437
  6.2 5.8 %collective-permute-start.1 = (bf16[8,4224]{1,0:T(8,128)(2,1)S(1)}, bf16[8,4224]{1,0:T(8,128)(2,1)S(1)}, u32[]{:S(2)}, u32[]{:S(2)}) collective-permute-start(bf16[8,4224]{1,0:T(8,128)(2,1)S(1)} %make_message.1.refs_0_), channel_id=1, source_target_pairs={{0,8},{4,12},{8,0},{12,4},{1,9},{5,13},{9,1},{13,5},{2,10},{6,14},... | collective-permute-start | bytes 202760 | tf_op jit(solution)/shard_map/ppermute | solution.py:437
  6.2 5.8 %collective-permute-start.2 = (bf16[8,4224]{1,0:T(8,128)(2,1)S(1)}, bf16[8,4224]{1,0:T(8,128)(2,1)S(1)}, u32[]{:S(2)}, u32[]{:S(2)}) collective-permute-start(bf16[8,4224]{1,0:T(8,128)(2,1)S(1)} %make_message.1.refs_0_), channel_id=1, source_target_pairs={{0,4},{4,0},{8,12},{12,8},{1,5},{5,1},{9,13},{13,9},{2,6},{6,2},{1... | collective-permute-start | bytes 202760 | tf_op jit(solution)/shard_map/ppermute | solution.py:437
  6.9 18.8 %copy-start.1 = (bf16[1,1,8,128,1024]{4,3,2,1,0:T(8,128)(2,1)S(1)}, bf16[1,1,8,128,1024]{4,3,2,1,0:T(8,128)(2,1)}, u32[]{:S(2)}) copy-start(bf16[1,1,8,128,1024]{4,3,2,1,0:T(8,128)(2,1)} %param.14) | copy-start | bytes 6291460
  12.9 8.8 %collective-permute-start.3 = (bf16[304,256]{1,0:T(8,128)(2,1)S(1)}, bf16[304,256]{1,0:T(8,128)(2,1)S(1)}, u32[]{:S(2)}, u32[]{:S(2)}) collective-permute-start(bf16[304,256]{1,0:T(8,128)(2,1)S(1)} %get-tuple-element.29), channel_id=1, source_target_pairs={{0,4},{4,0},{8,12},{12,8},{1,5},{5,1},{9,13},{13,9},{2,6},{6,2},{1... | collective-permute-start | bytes 466952 | tf_op jit(solution)/shard_map/ppermute | solution.py:437
  13.9 4.8 %collective-permute-start.5 = (f32[16,256]{1,0:T(8,128)S(1)}, f32[16,256]{1,0:T(8,128)S(1)}, u32[]{:S(2)}, u32[]{:S(2)}) collective-permute-start(f32[16,256]{1,0:T(8,128)S(1)} %get-tuple-element.28.refs_0_), channel_id=1, source_target_pairs={{0,8},{4,12},{8,0},{12,4},{1,9},{5,13},{9,1},{13,5},{2,10},{6,14},... | collective-permute-start | bytes 49160 | tf_op jit(solution)/shard_map/ppermute | solution.py:437
  16.2 5.5 %collective-permute-start.4 = (f32[16,256]{1,0:T(8,128)S(1)}, f32[16,256]{1,0:T(8,128)S(1)}, u32[]{:S(2)}, u32[]{:S(2)}) collective-permute-start(f32[16,256]{1,0:T(8,128)S(1)} %get-tuple-element.30), channel_id=1, source_target_pairs={{0,12},{4,8},{8,4},{12,0},{1,13},{5,9},{9,5},{13,1},{2,14},{6,10},... | collective-permute-start | bytes 49160 | tf_op jit(solution)/shard_map/ppermute | solution.py:437
  22.1 6.6 %collective-permute-start.8 = (bf16[16,1152]{1,0:T(8,128)(2,1)S(1)}, bf16[16,1152]{1,0:T(8,128)(2,1)S(1)}, u32[]{:S(2)}, u32[]{:S(2)}) collective-permute-start(bf16[16,1152]{1,0:T(8,128)(2,1)S(1)} %get-tuple-element.36), channel_id=1, source_target_pairs={{0,4},{4,0},{8,12},{12,8},{1,5},{5,1},{9,13},{13,9},{2,6},{6,2},{1... | collective-permute-start | bytes 110600 | tf_op jit(solution)/shard_map/ppermute | solution.py:437
  22.2 5.8 %collective-permute-start.6 = (bf16[16,1024]{1,0:T(8,128)(2,1)S(1)}, bf16[16,1024]{1,0:T(8,128)(2,1)S(1)}, u32[]{:S(2)}, u32[]{:S(2)}) collective-permute-start(bf16[16,1024]{1,0:T(8,128)(2,1)S(1)} %get-tuple-element.34), channel_id=1, source_target_pairs={{0,12},{4,8},{8,4},{12,0},{1,13},{5,9},{9,5},{13,1},{2,14},{6,10},... | collective-permute-start | bytes 98312 | tf_op jit(solution)/shard_map/ppermute | solution.py:437
  23.3 5.3 %collective-permute-start.7 = (bf16[16,1024]{1,0:T(8,128)(2,1)S(1)}, bf16[16,1024]{1,0:T(8,128)(2,1)S(1)}, u32[]{:S(2)}, u32[]{:S(2)}) collective-permute-start(bf16[16,1024]{1,0:T(8,128)(2,1)S(1)} %get-tuple-element.35), channel_id=1, source_target_pairs={{0,8},{4,12},{8,0},{12,4},{1,9},{5,13},{9,1},{13,5},{2,10},{6,14},... | collective-permute-start | bytes 98312 | tf_op jit(solution)/shard_map/ppermute | solution.py:437
  28.9 4.4 %collective-permute-start.9 = (bf16[32,1152]{1,0:T(8,128)(2,1)S(1)}, bf16[32,1152]{1,0:T(8,128)(2,1)S(1)}, u32[]{:S(2)}, u32[]{:S(2)}) collective-permute-start(bf16[32,1152]{1,0:T(8,128)(2,1)S(1)} %merge.1.own_ref), channel_id=1, source_target_pairs={{0,2},{2,0},{1,3},{3,1},{4,6},{6,4},{5,7},{7,5},{8,10},{10,8},{9,1... | collective-permute-start | bytes 221192 | tf_op jit(solution)/shard_map/ppermute | solution.py:437

commit v11 on v10

--- a/solution.py
+++ b/solution.py
@@ -36,7 +36,7 @@
 
 
 QUERY_ORDER = (3, 2, 1)
-SCORE_ORDER = (1, 3, 2)
+SCORE_ORDER = (2, 3, 1)
 MIXED_ORDER = (3, 2, 1)
 
 
@@ -219,9 +219,9 @@
     return ((code // requests) ^ me) * requests + code % requests
 
 
-def score_kernel(heads, start, keys_ref, values_ref, *refs):
-    message_refs, refs = by_distance(refs[:-5], QUERY_ORDER), refs[-5:]
-    scores_ref, same_ref, other_ref, near_ref, code_ref = refs
+def score_kernel(heads, start, keys_ref, *refs):
+    message_refs, refs = by_distance(refs[:-4], QUERY_ORDER), refs[-4:]
+    same_ref, other_ref, code_ref, scores_ref = refs
     requests = message_refs[0].shape[0]
     tokens, width = keys_ref.shape
     size = width // heads
@@ -248,33 +248,27 @@
             1.0 / math.sqrt(size)
         )
     same_ref[...] = scores_ref[pl.ds(pl.multiple_of(side() * half, half), half), :]
-    other = scores_ref[pl.ds(pl.multiple_of((1 - side()) * half, half), half), :]
-    other_ref[...] = other
-    near_ref[:tokens, :] = values_ref[...]
-    for part in range(3):
-        piece = other.astype(near_ref.dtype)
-        near_ref[tokens + part * half : tokens + (part + 1) * half, :] = piece
-        other = other - piece.astype(jnp.float32)
-
-
-def partial_scores(heads, columns, keys, values, messages):
+    other_ref[...] = scores_ref[pl.ds(pl.multiple_of((1 - side()) * half, half), half), :]
+
+
+def partial_scores(heads, columns, keys, messages):
     tokens, width = keys.shape
     query_heads = columns * heads // width
     vmem = pl.BlockSpec(memory_space=pltpu.VMEM)
     return pl.pallas_call(
         functools.partial(score_kernel, heads, columns),
-        in_specs=[vmem] * (2 + len(messages)),
-        out_specs=[vmem] * 5,
+        in_specs=[vmem] * (1 + len(messages)),
+        out_specs=[vmem] * 3,
         out_shape=[
-            jax.ShapeDtypeStruct((query_heads, tokens), jnp.float32),
             jax.ShapeDtypeStruct((query_heads // 2, tokens), jnp.float32),
             jax.ShapeDtypeStruct((query_heads // 2, tokens), jnp.float32),
-            jax.ShapeDtypeStruct((tokens + 3 * query_heads // 2, values.shape[1]), values.dtype),
             jax.ShapeDtypeStruct((8, tokens), jnp.int32),
         ],
+        scratch_shapes=[pltpu.VMEM((query_heads, tokens), jnp.float32)],
         compiler_params=params(),
+        cost_estimate=pl.CostEstimate(flops=10**11, bytes_accessed=10**4, transcendentals=0),
         name="partial_scores",
-    )(keys, values, *arranged(messages, QUERY_ORDER))[1:]
+    )(keys, *arranged(messages, QUERY_ORDER))
 
 
 def packed(value, group, size):
@@ -304,7 +298,7 @@
     return jnp.concatenate([jnp.broadcast_to(narrow[:, g : g + 1], (rows, size)) for g in range(group)], axis=1)
 
 
-def mix_kernel(heads, count, requests, code_ref, own_ref, *refs):
+def mix_kernel(heads, count, requests, code_ref, own_ref, near_ref, *refs):
     score_refs = by_distance(refs[:count], SCORE_ORDER)
     mixed_refs, (tops_ref, totals_ref) = refs[count : 2 * count], refs[2 * count :]
     tokens, width = own_ref.shape
@@ -312,12 +306,7 @@
     group = score_refs[0].shape[0] // heads
     span = count * requests
     here = lax.broadcasted_iota(jnp.int32, (span, tokens), 0) == code_ref[0:1, :]
-    near_ref, half = score_refs[1], score_refs[0].shape[0]
-    parts = [
-        near_ref[tokens + part * half : tokens + (part + 1) * half, :].astype(jnp.float32) for part in range(3)
-    ]
-    near_scores = (parts[0] + parts[1]) + parts[2]
-    scores = (score_refs[0][...] + score_refs[2][...]) + (near_scores + score_refs[3][...])
+    scores = (score_refs[0][...] + score_refs[2][...]) + (score_refs[1][...] + score_refs[3][...])
     mixed, tops, totals = [], [], []
     for k in range(heads):
         weights = []
@@ -332,7 +321,7 @@
         weights = jnp.concatenate(weights, axis=0).astype(jnp.bfloat16)
         columns = slice(k * size, (k + 1) * size)
         sums = jnp.dot(weights, own_ref[:, columns], preferred_element_type=jnp.float32)
-        mixed.append(sums + jnp.dot(weights, near_ref[:tokens, columns], preferred_element_type=jnp.float32))
+        mixed.append(sums + jnp.dot(weights, near_ref[:, columns], preferred_element_type=jnp.float32))
 
     def block(parts, d):
         rows = slice(d * requests, (d + 1) * requests)
@@ -350,7 +339,7 @@
     totals_ref[...] = block(totals, 0)
 
 
-def mix(heads, requests, code, values, scores):
+def mix(heads, requests, code, values, near_values, scores):
     count = len(scores)
     size = values.shape[1] // heads
     columns = scores[0].shape[0] // heads * size
@@ -362,7 +351,7 @@
         + [jax.ShapeDtypeStruct(shape, jnp.float32)] * 2,
         compiler_params=params(),
         name="mix",
-    )(code, values, *arranged(scores, SCORE_ORDER))
+    )(code, values, near_values, *arranged(scores, SCORE_ORDER))
 
 
 def merge_kernel(cache_ref, top_ref, total_ref, new_top_ref, new_total_ref, *refs):
@@ -450,9 +439,10 @@
     message = make_message(query, owners[:, :, 0], requests)
     messages = exchange([message] * seq_count)
     keys, values, far_values = project(tokens, kv_weight)
-    same, other, near, code = partial_scores(heads, columns, keys, far_values, messages)
-    scores = exchange([same, near, same, other])
-    results = mix(heads // 2, request_count, code, values, scores)
+    near_values = from_partner(far_values, "seq", 1)
+    same, other, code = partial_scores(heads, columns, keys, messages)
+    scores = exchange([same, other, same, other])
+    results = mix(heads // 2, request_count, code, values, near_values, scores)
     mixed, (new_tops, new_totals) = results[:seq_count], results[seq_count:]
     mixed = exchange(mixed)
     cache_mixed, tops, totals = cache_part(lengths, query, kv_cache[0, 0], signs)

time: 34.5 us -> 33.8 us (0.980)
  waiting for transfers between devices: 11.4 us -> 10.5 us
  starting transfers between devices: 15.2 us -> 16 us
  Pallas kernels: 7.63 us -> 7.03 us
    ppermute x10 -> x11, waiting for transfers between devices: 11.4 us -> 10.5 us  [from_partner(): return lax.ppermute(x, axis, [(i, i ^ distance) for i in range(count)])]
    ppermute x10 -> x11, starting transfers between devices: 15.2 us -> 16 us  [from_partner(): return lax.ppermute(x, axis, [(i, i ^ distance) for i in range(count)])]
    pallas_call x1, Pallas kernels: 0.92 us -> 0.32 us  [partial_scores(): pl.pallas_call(functools.partial(score_kernel, heads, columns), in_specs=...]
  transfers between devices with their start and end apart: 10 -> 11, of which waited for: 6 -> 7; matrix products, arithmetic and copies ran while one was open for 0% -> 0% of each run, Pallas kernels for 12% -> 13%
where the time goes in v11:
time: 33.8 us; the launch traced here: 33.6 us
  starting transfers between devices  16 us (47%)
  waiting for transfers between devices  10.5 us (31%)
  Pallas kernels  7.03 us (21%)
    ppermute x11, starting transfers between devices, from_partner(): return lax.ppermute(x, axis, [(i, i ^ distance) for i in range(count)])  16 us
    ppermute x11, waiting for transfers between devices, from_partner(): return lax.ppermute(x, axis, [(i, i ^ distance) for i in range(count)])  10.5 us
    pallas_call x1, Pallas kernels, project(): pl.pallas_call(project_kernel, in_specs=[vmem] * 2, out_specs=[vmem] * 3,...  2.4 us
    pallas_call x1, Pallas kernels, cache_part(): pl.pallas_call(cache_kernel, in_specs=[pl.BlockSpec(memory_space=pltpu.SM...  1.62 us
    pallas_call x1, Pallas kernels, make_message(): pl.pallas_call(message_kernel, in_specs=[pl.BlockSpec(memory_space=pl.ANY...  1.03 us
    pallas_call x1, Pallas kernels, finish(): pl.pallas_call(finish_kernel, out_shape=jax.ShapeDtypeStruct((requests, c...  1.01 us
  transfers between devices with their start and end apart: 11, of which 7 were waited for; matrix products, arithmetic and copies ran while one was open for 0% of the time, Pallas kernels for 13%

profile of v11, /device:TPU:0, one launch (start us, length us, event | category | flops | bytes accessed | tf_op | source)
XLA Modules:
  0.0 33.6 jit_solution(13176679299138175348)
XLA Ops:
  0.0 1.0 %make_message.1.refs_0_ = bf16[8,4224]{1,0:T(8,128)(2,1)S(1)} custom-call(bf16[8,4096]{1,0:T(8,128)(2,1)} %bitcast.7, s32[1,64]{1,0:T(1,128)} %bitcast.9, s32[1,64]{1,0:T(1,128)} %requests_ref.1), custom_call_target="tpu_custom_call" | custom-call | flops 99999997952 | bytes 10000 | tf_op jit(solution)/shard_map/make_message/pallas_call | solution.py:111
  1.0 5.1 %collective-permute-start = (bf16[8,4224]{1,0:T(8,128)(2,1)S(1)}, bf16[8,4224]{1,0:T(8,128)(2,1)S(1)}, u32[]{:S(2)}, u32[]{:S(2)}) collective-permute-start(bf16[8,4224]{1,0:T(8,128)(2,1)S(1)} %make_message.1.refs_0_), channel_id=1, source_target_pairs={{0,12},{4,8},{8,4},{12,0},{1,13},{5,9},{9,5},{13,1},{2,14},{6,10},... | collective-permute-start | bytes 202760 | tf_op jit(solution)/shard_map/ppermute | solution.py:426
  6.2 0.6 %collective-permute-start.2 = (bf16[8,4224]{1,0:T(8,128)(2,1)S(1)}, bf16[8,4224]{1,0:T(8,128)(2,1)S(1)}, u32[]{:S(2)}, u32[]{:S(2)}) collective-permute-start(bf16[8,4224]{1,0:T(8,128)(2,1)S(1)} %make_message.1.refs_0_), channel_id=1, source_target_pairs={{0,4},{4,0},{8,12},{12,8},{1,5},{5,1},{9,13},{13,9},{2,6},{6,2},{1... | collective-permute-start | bytes 202760 | tf_op jit(solution)/shard_map/ppermute | solution.py:426
  6.8 2.4 %project.1 = (bf16[256,512]{1,0:T(8,128)(2,1)S(1)}, bf16[256,256]{1,0:T(8,128)(2,1)S(1)}, bf16[256,256]{1,0:T(8,128)(2,1)S(1)}) custom-call(bf16[256,4096]{1,0:T(8,128)(2,1)S(1)} %copy-done, bf16[4096,1024]{1,0:T(8,128)(2,1)S(1)} %bitcast.5), custom_call_target="tpu_custom_call" | custom-call | flops 2147483648 | bytes 10485760 | tf_op jit(solution)/shard_map/project/pallas_call | solution.py:72
  9.2 1.5 %collective-permute-start.3 = (bf16[256,256]{1,0:T(8,128)(2,1)S(1)}, bf16[256,256]{1,0:T(8,128)(2,1)S(1)}, u32[]{:S(2)}, u32[]{:S(2)}) collective-permute-start(bf16[256,256]{1,0:T(8,128)(2,1)S(1)} %get-tuple-element.26), channel_id=1, source_target_pairs={{0,4},{4,0},{8,12},{12,8},{1,5},{5,1},{9,13},{13,9},{2,6},{6,2},{1... | collective-permute-start | bytes 393224 | tf_op jit(solution)/shard_map/ppermute | solution.py:426
  10.7 1.3 %collective-permute-done.1.refs_2_ = bf16[8,4224]{1,0:T(8,128)(2,1)S(1)} collective-permute-done((bf16[8,4224]{1,0:T(8,128)(2,1)S(1)}, bf16[8,4224]{1,0:T(8,128)(2,1)S(1)}, u32[]{:S(2)}, u32[]{:S(2)}) %collective-permute-start.1) | collective-permute-done | bytes 67616 | tf_op jit(solution)/shard_map/ppermute | solution.py:426
  12.0 0.0 copy-start.4
  12.0 0.3 partial_scores.1
  12.4 1.7 %collective-permute-start.4 = (f32[16,256]{1,0:T(8,128)S(1)}, f32[16,256]{1,0:T(8,128)S(1)}, u32[]{:S(2)}, u32[]{:S(2)}) collective-permute-start(f32[16,256]{1,0:T(8,128)S(1)} %get-tuple-element.27.refs_0_), channel_id=1, source_target_pairs={{0,8},{4,12},{8,0},{12,4},{1,9},{5,13},{9,1},{13,5},{2,10},{6,14},... | collective-permute-start | bytes 49160 | tf_op jit(solution)/shard_map/ppermute | solution.py:426
  14.1 2.0 %collective-permute-start.5 = (f32[16,256]{1,0:T(8,128)S(1)}, f32[16,256]{1,0:T(8,128)S(1)}, u32[]{:S(2)}, u32[]{:S(2)}) collective-permute-start(f32[16,256]{1,0:T(8,128)S(1)} %get-tuple-element.28), channel_id=1, source_target_pairs={{0,12},{4,8},{8,4},{12,0},{1,13},{5,9},{9,5},{13,1},{2,14},{6,10},... | collective-permute-start | bytes 49160 | tf_op jit(solution)/shard_map/ppermute | solution.py:426
  16.1 1.1 %collective-permute-done.4.refs_1_ = f32[16,256]{1,0:T(8,128)S(1)} collective-permute-done((f32[16,256]{1,0:T(8,128)S(1)}, f32[16,256]{1,0:T(8,128)S(1)}, u32[]{:S(2)}, u32[]{:S(2)}) %collective-permute-start.4) | collective-permute-done | bytes 16416 | tf_op jit(solution)/shard_map/ppermute | solution.py:426
  17.2 2.4 %collective-permute-done.5.refs_2_ = f32[16,256]{1,0:T(8,128)S(1)} collective-permute-done((f32[16,256]{1,0:T(8,128)S(1)}, f32[16,256]{1,0:T(8,128)S(1)}, u32[]{:S(2)}, u32[]{:S(2)}) %collective-permute-start.5) | collective-permute-done | bytes 16416 | tf_op jit(solution)/shard_map/ppermute | solution.py:426
  19.6 0.2 collective-permute-done.6.refs_3_
  19.8 0.4 %mix.1 = (bf16[16,1024]{1,0:T(8,128)(2,1)S(1)}, bf16[16,1152]{1,0:T(8,128)(2,1)S(1)}, bf16[16,1024]{1,0:T(8,128)(2,1)S(1)}, bf16[16,1024]{1,0:T(8,128)(2,1)S(1)}...) custom-call(s32[8,256]{1,0:T(8,128)S(1)} %get-tuple-element.24.code_ref, ...), custom_call_target="tpu_custom_call" | custom-call | tf_op jit(solution)/shard_map/mix/pallas_call | solution.py:348
  20.2 0.2 collective-permute-start.9
  20.5 2.4 %collective-permute-start.7 = (bf16[16,1024]{1,0:T(8,128)(2,1)S(1)}, bf16[16,1024]{1,0:T(8,128)(2,1)S(1)}, u32[]{:S(2)}, u32[]{:S(2)}) collective-permute-start(bf16[16,1024]{1,0:T(8,128)(2,1)S(1)} %get-tuple-element.32), channel_id=1, source_target_pairs={{0,12},{4,8},{8,4},{12,0},{1,13},{5,9},{9,5},{13,1},{2,14},{6,10},... | collective-permute-start | bytes 98312 | tf_op jit(solution)/shard_map/ppermute | solution.py:426
  22.9 0.9 %collective-permute-start.8 = (bf16[16,1024]{1,0:T(8,128)(2,1)S(1)}, bf16[16,1024]{1,0:T(8,128)(2,1)S(1)}, u32[]{:S(2)}, u32[]{:S(2)}) collective-permute-start(bf16[16,1024]{1,0:T(8,128)(2,1)S(1)} %get-tuple-element.33), channel_id=1, source_target_pairs={{0,8},{4,12},{8,0},{12,4},{1,9},{5,13},{9,1},{13,5},{2,10},{6,14},... | collective-permute-start | bytes 98312 | tf_op jit(solution)/shard_map/ppermute | solution.py:426
  23.8 1.6 %cache_part.1 = (f32[32,1024]{1,0:T(8,128)S(1)}, f32[32,1024]{1,0:T(8,128)S(1)}, f32[32,1024]{1,0:T(8,128)S(1)}) custom-call(s32[1,1,8]{2,1,0:T(1,128)S(1)} %copy-done.4, bf16[8,4096]{1,0:T(8,128)(2,1)S(1)} %bitcast.8, bf16[8,128,1024]{2,1,0:T(8,128)(2,1)S(1)} %bitcast.6, s32[8,128]{1,0:T(8,128)S(1)} %copy-done.3), custom_call_target="tpu_custom_call" | custom-call | flops 16777216 | bytes 2097152 | tf_op jit(solution)/shard_map/cache_part/pallas_call | solution.py:198
  25.4 0.8 %collective-permute-done.7.refs_1_ = bf16[16,1024]{1,0:T(8,128)(2,1)S(1)} collective-permute-done((bf16[16,1024]{1,0:T(8,128)(2,1)S(1)}, bf16[16,1024]{1,0:T(8,128)(2,1)S(1)}, u32[]{:S(2)}, u32[]{:S(2)}) %collective-permute-start.7) | collective-permute-done | bytes 32800 | tf_op jit(solution)/shard_map/ppermute | solution.py:426
  26.2 1.8 %collective-permute-done.8.refs_2_ = bf16[16,1024]{1,0:T(8,128)(2,1)S(1)} collective-permute-done((bf16[16,1024]{1,0:T(8,128)(2,1)S(1)}, bf16[16,1024]{1,0:T(8,128)(2,1)S(1)}, u32[]{:S(2)}, u32[]{:S(2)}) %collective-permute-start.8) | collective-permute-done | bytes 32800 | tf_op jit(solution)/shard_map/ppermute | solution.py:426
  28.0 0.3 merge.1.own_ref
  28.3 1.5 %collective-permute-start.10 = (bf16[32,1152]{1,0:T(8,128)(2,1)S(1)}, bf16[32,1152]{1,0:T(8,128)(2,1)S(1)}, u32[]{:S(2)}, u32[]{:S(2)}) collective-permute-start(bf16[32,1152]{1,0:T(8,128)(2,1)S(1)} %merge.1.own_ref), channel_id=1, source_target_pairs={{0,2},{2,0},{1,3},{3,1},{4,6},{6,4},{5,7},{7,5},{8,10},{10,8},{9,1... | collective-permute-start | bytes 221192 | tf_op jit(solution)/shard_map/ppermute | solution.py:426
  29.8 2.9 %collective-permute-done.10.far_ref = bf16[32,1152]{1,0:T(8,128)(2,1)S(1)} collective-permute-done((bf16[32,1152]{1,0:T(8,128)(2,1)S(1)}, bf16[32,1152]{1,0:T(8,128)(2,1)S(1)}, u32[]{:S(2)}, u32[]{:S(2)}) %collective-permute-start.10) | collective-permute-done | bytes 73760 | tf_op jit(solution)/shard_map/ppermute | solution.py:426
  32.6 1.0 %finish.1 = bf16[8,4096]{1,0:T(8,128)(2,1)} custom-call(bf16[32,1152]{1,0:T(8,128)(2,1)S(1)} %merge.1.own_ref, bf16[32,1152]{1,0:T(8,128)(2,1)S(1)} %collective-permute-done.10.far_ref), custom_call_target="tpu_custom_call" | custom-call | tf_op jit(solution)/shard_map/finish/pallas_call | solution.py:416
  (20 shorter events, 0.0 us)
Async XLA Ops:
  0.0 6.8 %slice-start = ((s8[8388608]{0:T(1024)(128)(4,1)}), s8[4194304]{0:T(1024)(128)(4,1)S(1)}, s32[]{:S(2)}) async-start(s8[8388608]{0:T(1024)(128)(4,1)} %bitcast.4), calls=%async_computation | async-start | bytes 8388608
  0.0 6.8 %slice-start.1 = ((s8[8388608]{0:T(1024)(128)(4,1)}), s8[4194304]{0:T(1024)(128)(4,1)S(1)}, s32[]{:S(2)}) async-start(s8[8388608]{0:T(1024)(128)(4,1)} %bitcast.4), calls=%async_computation.1 | async-start | bytes 8388608
  0.0 6.8 %copy-start = (bf16[256,4096]{1,0:T(8,128)(2,1)S(1)}, bf16[256,4096]{1,0:T(8,128)(2,1)}, u32[]{:S(2)}) copy-start(bf16[256,4096]{1,0:T(8,128)(2,1)} %tokens_ref.1) | copy-start | bytes 6291460
  1.0 9.6 %collective-permute-start = (bf16[8,4224]{1,0:T(8,128)(2,1)S(1)}, bf16[8,4224]{1,0:T(8,128)(2,1)S(1)}, u32[]{:S(2)}, u32[]{:S(2)}) collective-permute-start(bf16[8,4224]{1,0:T(8,128)(2,1)S(1)} %make_message.1.refs_0_), channel_id=1, source_target_pairs={{0,12},{4,8},{8,4},{12,0},{1,13},{5,9},{9,5},{13,1},{2,14},{6,10},... | collective-permute-start | bytes 202760 | tf_op jit(solution)/shard_map/ppermute | solution.py:426
  6.2 5.8 %collective-permute-start.1 = (bf16[8,4224]{1,0:T(8,128)(2,1)S(1)}, bf16[8,4224]{1,0:T(8,128)(2,1)S(1)}, u32[]{:S(2)}, u32[]{:S(2)}) collective-permute-start(bf16[8,4224]{1,0:T(8,128)(2,1)S(1)} %make_message.1.refs_0_), channel_id=1, source_target_pairs={{0,8},{4,12},{8,0},{12,4},{1,9},{5,13},{9,1},{13,5},{2,10},{6,14},... | collective-permute-start | bytes 202760 | tf_op jit(solution)/shard_map/ppermute | solution.py:426
  6.2 5.8 %collective-permute-start.2 = (bf16[8,4224]{1,0:T(8,128)(2,1)S(1)}, bf16[8,4224]{1,0:T(8,128)(2,1)S(1)}, u32[]{:S(2)}, u32[]{:S(2)}) collective-permute-start(bf16[8,4224]{1,0:T(8,128)(2,1)S(1)} %make_message.1.refs_0_), channel_id=1, source_target_pairs={{0,4},{4,0},{8,12},{12,8},{1,5},{5,1},{9,13},{13,9},{2,6},{6,2},{1... | collective-permute-start | bytes 202760 | tf_op jit(solution)/shard_map/ppermute | solution.py:426
  9.2 10.6 %collective-permute-start.3 = (bf16[256,256]{1,0:T(8,128)(2,1)S(1)}, bf16[256,256]{1,0:T(8,128)(2,1)S(1)}, u32[]{:S(2)}, u32[]{:S(2)}) collective-permute-start(bf16[256,256]{1,0:T(8,128)(2,1)S(1)} %get-tuple-element.26), channel_id=1, source_target_pairs={{0,4},{4,0},{8,12},{12,8},{1,5},{5,1},{9,13},{13,9},{2,6},{6,2},{1... | collective-permute-start | bytes 393224 | tf_op jit(solution)/shard_map/ppermute | solution.py:426
  12.0 11.8 %copy-start.1 = (bf16[1,1,8,128,1024]{4,3,2,1,0:T(8,128)(2,1)S(1)}, bf16[1,1,8,128,1024]{4,3,2,1,0:T(8,128)(2,1)}, u32[]{:S(2)}) copy-start(bf16[1,1,8,128,1024]{4,3,2,1,0:T(8,128)(2,1)} %param.14) | copy-start | bytes 6291460
  12.0 11.8 %copy-start.2 = (bf16[1,1,8,4096]{3,2,1,0:T(8,128)(2,1)S(1)}, bf16[1,1,8,4096]{3,2,1,0:T(8,128)(2,1)}, u32[]{:S(2)}) copy-start(bf16[1,1,8,4096]{3,2,1,0:T(8,128)(2,1)} %param.13) | copy-start | bytes 196612
  12.0 11.8 %copy-start.3 = (s32[8,128]{1,0:T(8,128)S(1)}, s32[8,128]{1,0:T(8,128)}, u32[]{:S(2)}) copy-start(s32[8,128]{1,0:T(8,128)} %signs_ref.1) | copy-start | bytes 12292
  12.0 11.8 %copy-start.4 = (s32[1,1,8]{2,1,0:T(1,128)S(1)}, s32[1,1,8]{2,1,0:T(1,128)}, u32[]{:S(2)}) copy-start(s32[1,1,8]{2,1,0:T(1,128)} %lengths_ref.1) | copy-start | bytes 100
  12.4 4.9 %collective-permute-start.4 = (f32[16,256]{1,0:T(8,128)S(1)}, f32[16,256]{1,0:T(8,128)S(1)}, u32[]{:S(2)}, u32[]{:S(2)}) collective-permute-start(f32[16,256]{1,0:T(8,128)S(1)} %get-tuple-element.27.refs_0_), channel_id=1, source_target_pairs={{0,8},{4,12},{8,0},{12,4},{1,9},{5,13},{9,1},{13,5},{2,10},{6,14},... | collective-permute-start | bytes 49160 | tf_op jit(solution)/shard_map/ppermute | solution.py:426
  14.1 5.5 %collective-permute-start.5 = (f32[16,256]{1,0:T(8,128)S(1)}, f32[16,256]{1,0:T(8,128)S(1)}, u32[]{:S(2)}, u32[]{:S(2)}) collective-permute-start(f32[16,256]{1,0:T(8,128)S(1)} %get-tuple-element.28), channel_id=1, source_target_pairs={{0,12},{4,8},{8,4},{12,0},{1,13},{5,9},{9,5},{13,1},{2,14},{6,10},... | collective-permute-start | bytes 49160 | tf_op jit(solution)/shard_map/ppermute | solution.py:426
  16.1 3.7 %collective-permute-start.6 = (f32[16,256]{1,0:T(8,128)S(1)}, f32[16,256]{1,0:T(8,128)S(1)}, u32[]{:S(2)}, u32[]{:S(2)}) collective-permute-start(f32[16,256]{1,0:T(8,128)S(1)} %get-tuple-element.28), channel_id=1, source_target_pairs={{0,4},{4,0},{8,12},{12,8},{1,5},{5,1},{9,13},{13,9},{2,6},{6,2},{1... | collective-permute-start | bytes 49160 | tf_op jit(solution)/shard_map/ppermute | solution.py:426
  20.2 7.8 %collective-permute-start.9 = (bf16[16,1152]{1,0:T(8,128)(2,1)S(1)}, bf16[16,1152]{1,0:T(8,128)(2,1)S(1)}, u32[]{:S(2)}, u32[]{:S(2)}) collective-permute-start(bf16[16,1152]{1,0:T(8,128)(2,1)S(1)} %get-tuple-element.34), channel_id=1, source_target_pairs={{0,4},{4,0},{8,12},{12,8},{1,5},{5,1},{9,13},{13,9},{2,6},{6,2},{1... | collective-permute-start | bytes 110600 | tf_op jit(solution)/shard_map/ppermute | solution.py:426
  20.5 5.7 %collective-permute-start.7 = (bf16[16,1024]{1,0:T(8,128)(2,1)S(1)}, bf16[16,1024]{1,0:T(8,128)(2,1)S(1)}, u32[]{:S(2)}, u32[]{:S(2)}) collective-permute-start(bf16[16,1024]{1,0:T(8,128)(2,1)S(1)} %get-tuple-element.32), channel_id=1, source_target_pairs={{0,12},{4,8},{8,4},{12,0},{1,13},{5,9},{9,5},{13,1},{2,14},{6,10},... | collective-permute-start | bytes 98312 | tf_op jit(solution)/shard_map/ppermute | solution.py:426
  22.9 5.1 %collective-permute-start.8 = (bf16[16,1024]{1,0:T(8,128)(2,1)S(1)}, bf16[16,1024]{1,0:T(8,128)(2,1)S(1)}, u32[]{:S(2)}, u32[]{:S(2)}) collective-permute-start(bf16[16,1024]{1,0:T(8,128)(2,1)S(1)} %get-tuple-element.33), channel_id=1, source_target_pairs={{0,8},{4,12},{8,0},{12,4},{1,9},{5,13},{9,1},{13,5},{2,10},{6,14},... | collective-permute-start | bytes 98312 | tf_op jit(solution)/shard_map/ppermute | solution.py:426
  28.3 4.4 %collective-permute-start.10 = (bf16[32,1152]{1,0:T(8,128)(2,1)S(1)}, bf16[32,1152]{1,0:T(8,128)(2,1)S(1)}, u32[]{:S(2)}, u32[]{:S(2)}) collective-permute-start(bf16[32,1152]{1,0:T(8,128)(2,1)S(1)} %merge.1.own_ref), channel_id=1, source_target_pairs={{0,2},{2,0},{1,3},{3,1},{4,6},{6,4},{5,7},{7,5},{8,10},{10,8},{9,1... | collective-permute-start | bytes 221192 | tf_op jit(solution)/shard_map/ppermute | solution.py:426

commit v12 on v11

--- a/solution.py
+++ b/solution.py
@@ -36,7 +36,7 @@
 
 
 QUERY_ORDER = (3, 2, 1)
-SCORE_ORDER = (2, 3, 1)
+SCORE_ORDER = (3, 2, 1)
 MIXED_ORDER = (3, 2, 1)
 
 
@@ -333,8 +333,8 @@
     pieces = [mixed[k][g * span : (g + 1) * span] for k in range(heads) for g in range(group)]
     for d in range(count):
         mixed_refs[d][:, : group * size] = block(pieces, d).astype(jnp.bfloat16)
-    stats = packed_stats(block(tops, 1), block(totals, 1), group)
-    mixed_refs[1][:, group * size :] = stats.astype(jnp.bfloat16)
+    stats = packed_stats(block(tops, 3), block(totals, 3), group)
+    mixed_refs[3][:, group * size :] = stats.astype(jnp.bfloat16)
     tops_ref[...] = block(tops, 0)
     totals_ref[...] = block(totals, 0)
 
@@ -347,7 +347,7 @@
     wide = (heads * requests, columns + size)
     return pl.pallas_call(
         functools.partial(mix_kernel, heads, count, requests),
-        out_shape=[jax.ShapeDtypeStruct(wide if d == 1 else shape, jnp.bfloat16) for d in range(count)]
+        out_shape=[jax.ShapeDtypeStruct(wide if d == 3 else shape, jnp.bfloat16) for d in range(count)]
         + [jax.ShapeDtypeStruct(shape, jnp.float32)] * 2,
         compiler_params=params(),
         name="mix",
@@ -359,13 +359,13 @@
     rows, columns = new_top_ref.shape
     size = out_ref.shape[1] - columns
     group = columns // size
-    near = mixed_refs[1][...].astype(jnp.float32)
-    near_top, near_total = unpacked_stats(near[:, columns:], group)
+    far = mixed_refs[3][...].astype(jnp.float32)
+    far_top, far_total = unpacked_stats(far[:, columns:], group)
     own = mixed_refs[0][...].astype(jnp.float32) + mixed_refs[2][...].astype(jnp.float32)
-    other = near[:, :columns] + mixed_refs[3][...].astype(jnp.float32)
+    other = mixed_refs[1][...].astype(jnp.float32) + far[:, :columns]
     parts = (
         (side(), own, new_top_ref[...], new_total_ref[...]),
-        (1 - side(), other, broad(near_top, size), broad(near_total, size)),
+        (1 - side(), other, broad(far_top, size), broad(far_total, size)),
     )
     for place, new, new_top, new_total in parts:
         at = pl.ds(pl.multiple_of(place * rows, rows), rows)

time: 33.8 us -> 32.6 us (0.964)
  waiting for transfers between devices: 10.5 us -> 7.66 us
  starting transfers between devices: 16 us -> 17.6 us
    ppermute x11, waiting for transfers between devices: 10.5 us -> 7.66 us  [from_partner(): return lax.ppermute(x, axis, [(i, i ^ distance) for i in range(count)])]
    ppermute x11, starting transfers between devices: 16 us -> 17.6 us  [from_partner(): return lax.ppermute(x, axis, [(i, i ^ distance) for i in range(count)])]
  transfers between devices with their start and end apart: 11 -> 11, of which waited for: 7 -> 6; matrix products, arithmetic and copies ran while one was open for 0% -> 0% of each run, Pallas kernels for 13% -> 13%
where the time goes in v12:
time: 32.6 us; the launch traced here: 32.4 us
  starting transfers between devices  17.6 us (54%)
  waiting for transfers between devices  7.66 us (23%)
  Pallas kernels  7.04 us (22%)
    ppermute x11, starting transfers between devices, from_partner(): return lax.ppermute(x, axis, [(i, i ^ distance) for i in range(count)])  17.6 us
    ppermute x11, waiting for transfers between devices, from_partner(): return lax.ppermute(x, axis, [(i, i ^ distance) for i in range(count)])  7.66 us
    pallas_call x1, Pallas kernels, project(): pl.pallas_call(project_kernel, in_specs=[vmem] * 2, out_specs=[vmem] * 3,...  2.4 us
    pallas_call x1, Pallas kernels, cache_part(): pl.pallas_call(cache_kernel, in_specs=[pl.BlockSpec(memory_space=pltpu.SM...  1.61 us
    pallas_call x1, Pallas kernels, make_message(): pl.pallas_call(message_kernel, in_specs=[pl.BlockSpec(memory_space=pl.ANY...  1.03 us
    pallas_call x1, Pallas kernels, finish(): pl.pallas_call(finish_kernel, out_shape=jax.ShapeDtypeStruct((requests, c...  1.01 us
  transfers between devices with their start and end apart: 11, of which 6 were waited for; matrix products, arithmetic and copies ran while one was open for 0% of the time, Pallas kernels for 13%

profile of v12, /device:TPU:0, one launch (start us, length us, event | category | flops | bytes accessed | tf_op | source)
XLA Modules:
  0.0 32.4 jit_solution(5084409523946404355)
XLA Ops:
  0.0 1.0 %make_message.1.refs_0_ = bf16[8,4224]{1,0:T(8,128)(2,1)S(1)} custom-call(bf16[8,4096]{1,0:T(8,128)(2,1)} %bitcast.7, s32[1,64]{1,0:T(1,128)} %bitcast.9, s32[1,64]{1,0:T(1,128)} %requests_ref.1), custom_call_target="tpu_custom_call" | custom-call | flops 99999997952 | bytes 10000 | tf_op jit(solution)/shard_map/make_message/pallas_call | solution.py:111
  1.0 5.1 %collective-permute-start = (bf16[8,4224]{1,0:T(8,128)(2,1)S(1)}, bf16[8,4224]{1,0:T(8,128)(2,1)S(1)}, u32[]{:S(2)}, u32[]{:S(2)}) collective-permute-start(bf16[8,4224]{1,0:T(8,128)(2,1)S(1)} %make_message.1.refs_0_), channel_id=1, source_target_pairs={{0,12},{4,8},{8,4},{12,0},{1,13},{5,9},{9,5},{13,1},{2,14},{6,10},... | collective-permute-start | bytes 202760 | tf_op jit(solution)/shard_map/ppermute | solution.py:426
  6.2 0.6 %collective-permute-start.2 = (bf16[8,4224]{1,0:T(8,128)(2,1)S(1)}, bf16[8,4224]{1,0:T(8,128)(2,1)S(1)}, u32[]{:S(2)}, u32[]{:S(2)}) collective-permute-start(bf16[8,4224]{1,0:T(8,128)(2,1)S(1)} %make_message.1.refs_0_), channel_id=1, source_target_pairs={{0,4},{4,0},{8,12},{12,8},{1,5},{5,1},{9,13},{13,9},{2,6},{6,2},{1... | collective-permute-start | bytes 202760 | tf_op jit(solution)/shard_map/ppermute | solution.py:426
  6.8 2.4 %project.1 = (bf16[256,512]{1,0:T(8,128)(2,1)S(1)}, bf16[256,256]{1,0:T(8,128)(2,1)S(1)}, bf16[256,256]{1,0:T(8,128)(2,1)S(1)}) custom-call(bf16[256,4096]{1,0:T(8,128)(2,1)S(1)} %copy-done, bf16[4096,1024]{1,0:T(8,128)(2,1)S(1)} %bitcast.5), custom_call_target="tpu_custom_call" | custom-call | flops 2147483648 | bytes 10485760 | tf_op jit(solution)/shard_map/project/pallas_call | solution.py:72
  9.2 1.5 %collective-permute-start.3 = (bf16[256,256]{1,0:T(8,128)(2,1)S(1)}, bf16[256,256]{1,0:T(8,128)(2,1)S(1)}, u32[]{:S(2)}, u32[]{:S(2)}) collective-permute-start(bf16[256,256]{1,0:T(8,128)(2,1)S(1)} %get-tuple-element.26), channel_id=1, source_target_pairs={{0,4},{4,0},{8,12},{12,8},{1,5},{5,1},{9,13},{13,9},{2,6},{6,2},{1... | collective-permute-start | bytes 393224 | tf_op jit(solution)/shard_map/ppermute | solution.py:426
  10.7 1.3 %collective-permute-done.1.refs_2_ = bf16[8,4224]{1,0:T(8,128)(2,1)S(1)} collective-permute-done((bf16[8,4224]{1,0:T(8,128)(2,1)S(1)}, bf16[8,4224]{1,0:T(8,128)(2,1)S(1)}, u32[]{:S(2)}, u32[]{:S(2)}) %collective-permute-start.1) | collective-permute-done | bytes 67616 | tf_op jit(solution)/shard_map/ppermute | solution.py:426
  12.0 0.0 copy-start.4
  12.0 0.3 partial_scores.1
  12.4 2.7 %collective-permute-start.4 = (f32[16,256]{1,0:T(8,128)S(1)}, f32[16,256]{1,0:T(8,128)S(1)}, u32[]{:S(2)}, u32[]{:S(2)}) collective-permute-start(f32[16,256]{1,0:T(8,128)S(1)} %get-tuple-element.28), channel_id=1, source_target_pairs={{0,12},{4,8},{8,4},{12,0},{1,13},{5,9},{9,5},{13,1},{2,14},{6,10},... | collective-permute-start | bytes 49160 | tf_op jit(solution)/shard_map/ppermute | solution.py:426
  15.1 0.1 collective-permute-start.5
  15.2 1.6 %collective-permute-start.6 = (f32[16,256]{1,0:T(8,128)S(1)}, f32[16,256]{1,0:T(8,128)S(1)}, u32[]{:S(2)}, u32[]{:S(2)}) collective-permute-start(f32[16,256]{1,0:T(8,128)S(1)} %get-tuple-element.28), channel_id=1, source_target_pairs={{0,4},{4,0},{8,12},{12,8},{1,5},{5,1},{9,13},{13,9},{2,6},{6,2},{1... | collective-permute-start | bytes 49160 | tf_op jit(solution)/shard_map/ppermute | solution.py:426
  16.8 1.2 %collective-permute-done.4.refs_1_ = f32[16,256]{1,0:T(8,128)S(1)} collective-permute-done((f32[16,256]{1,0:T(8,128)S(1)}, f32[16,256]{1,0:T(8,128)S(1)}, u32[]{:S(2)}, u32[]{:S(2)}) %collective-permute-start.4) | collective-permute-done | bytes 16416 | tf_op jit(solution)/shard_map/ppermute | solution.py:426
  18.0 1.7 %collective-permute-done.5.refs_2_ = f32[16,256]{1,0:T(8,128)S(1)} collective-permute-done((f32[16,256]{1,0:T(8,128)S(1)}, f32[16,256]{1,0:T(8,128)S(1)}, u32[]{:S(2)}, u32[]{:S(2)}) %collective-permute-start.5) | collective-permute-done | bytes 16416 | tf_op jit(solution)/shard_map/ppermute | solution.py:426
  19.7 0.4 %mix.1 = (bf16[16,1024]{1,0:T(8,128)(2,1)S(1)}, bf16[16,1024]{1,0:T(8,128)(2,1)S(1)}, bf16[16,1024]{1,0:T(8,128)(2,1)S(1)}, bf16[16,1152]{1,0:T(8,128)(2,1)S(1)}...) custom-call(s32[8,256]{1,0:T(8,128)S(1)} %get-tuple-element.24.code_ref, ...), custom_call_target="tpu_custom_call" | custom-call | tf_op jit(solution)/shard_map/mix/pallas_call | solution.py:348
  20.1 1.5 %collective-permute-start.7 = (bf16[16,1152]{1,0:T(8,128)(2,1)S(1)}, bf16[16,1152]{1,0:T(8,128)(2,1)S(1)}, u32[]{:S(2)}, u32[]{:S(2)}) collective-permute-start(bf16[16,1152]{1,0:T(8,128)(2,1)S(1)} %get-tuple-element.32), channel_id=1, source_target_pairs={{0,12},{4,8},{8,4},{12,0},{1,13},{5,9},{9,5},{13,1},{2,14},{6,10},... | collective-permute-start | bytes 110600 | tf_op jit(solution)/shard_map/ppermute | solution.py:426
  21.6 0.9 %collective-permute-start.8 = (bf16[16,1024]{1,0:T(8,128)(2,1)S(1)}, bf16[16,1024]{1,0:T(8,128)(2,1)S(1)}, u32[]{:S(2)}, u32[]{:S(2)}) collective-permute-start(bf16[16,1024]{1,0:T(8,128)(2,1)S(1)} %get-tuple-element.33), channel_id=1, source_target_pairs={{0,8},{4,12},{8,0},{12,4},{1,9},{5,13},{9,1},{13,5},{2,10},{6,14},... | collective-permute-start | bytes 98312 | tf_op jit(solution)/shard_map/ppermute | solution.py:426
  22.5 2.1 %collective-permute-start.9 = (bf16[16,1024]{1,0:T(8,128)(2,1)S(1)}, bf16[16,1024]{1,0:T(8,128)(2,1)S(1)}, u32[]{:S(2)}, u32[]{:S(2)}) collective-permute-start(bf16[16,1024]{1,0:T(8,128)(2,1)S(1)} %get-tuple-element.34), channel_id=1, source_target_pairs={{0,4},{4,0},{8,12},{12,8},{1,5},{5,1},{9,13},{13,9},{2,6},{6,2},{1... | collective-permute-start | bytes 98312 | tf_op jit(solution)/shard_map/ppermute | solution.py:426
  24.6 1.6 %cache_part.1 = (f32[32,1024]{1,0:T(8,128)S(1)}, f32[32,1024]{1,0:T(8,128)S(1)}, f32[32,1024]{1,0:T(8,128)S(1)}) custom-call(s32[1,1,8]{2,1,0:T(1,128)S(1)} %copy-done.4, bf16[8,4096]{1,0:T(8,128)(2,1)S(1)} %bitcast.8, bf16[8,128,1024]{2,1,0:T(8,128)(2,1)S(1)} %bitcast.6, s32[8,128]{1,0:T(8,128)S(1)} %copy-done.3), custom_call_target="tpu_custom_call" | custom-call | flops 16777216 | bytes 2097152 | tf_op jit(solution)/shard_map/cache_part/pallas_call | solution.py:198
  26.2 0.3 collective-permute-done.8.refs_2_
  26.5 0.3 collective-permute-done.9.refs_3_
  26.8 0.3 merge.1.own_ref
  27.1 1.5 %collective-permute-start.10 = (bf16[32,1152]{1,0:T(8,128)(2,1)S(1)}, bf16[32,1152]{1,0:T(8,128)(2,1)S(1)}, u32[]{:S(2)}, u32[]{:S(2)}) collective-permute-start(bf16[32,1152]{1,0:T(8,128)(2,1)S(1)} %merge.1.own_ref), channel_id=1, source_target_pairs={{0,2},{2,0},{1,3},{3,1},{4,6},{6,4},{5,7},{7,5},{8,10},{10,8},{9,1... | collective-permute-start | bytes 221192 | tf_op jit(solution)/shard_map/ppermute | solution.py:426
  28.6 2.9 %collective-permute-done.10.far_ref = bf16[32,1152]{1,0:T(8,128)(2,1)S(1)} collective-permute-done((bf16[32,1152]{1,0:T(8,128)(2,1)S(1)}, bf16[32,1152]{1,0:T(8,128)(2,1)S(1)}, u32[]{:S(2)}, u32[]{:S(2)}) %collective-permute-start.10) | collective-permute-done | bytes 73760 | tf_op jit(solution)/shard_map/ppermute | solution.py:426
  31.4 1.0 %finish.1 = bf16[8,4096]{1,0:T(8,128)(2,1)} custom-call(bf16[32,1152]{1,0:T(8,128)(2,1)S(1)} %merge.1.own_ref, bf16[32,1152]{1,0:T(8,128)(2,1)S(1)} %collective-permute-done.10.far_ref), custom_call_target="tpu_custom_call" | custom-call | tf_op jit(solution)/shard_map/finish/pallas_call | solution.py:416
  (20 shorter events, 0.0 us)
Async XLA Ops:
  0.0 6.8 %slice-start = ((s8[8388608]{0:T(1024)(128)(4,1)}), s8[4194304]{0:T(1024)(128)(4,1)S(1)}, s32[]{:S(2)}) async-start(s8[8388608]{0:T(1024)(128)(4,1)} %bitcast.4), calls=%async_computation | async-start | bytes 8388608
  0.0 6.8 %slice-start.1 = ((s8[8388608]{0:T(1024)(128)(4,1)}), s8[4194304]{0:T(1024)(128)(4,1)S(1)}, s32[]{:S(2)}) async-start(s8[8388608]{0:T(1024)(128)(4,1)} %bitcast.4), calls=%async_computation.1 | async-start | bytes 8388608
  0.0 6.8 %copy-start = (bf16[256,4096]{1,0:T(8,128)(2,1)S(1)}, bf16[256,4096]{1,0:T(8,128)(2,1)}, u32[]{:S(2)}) copy-start(bf16[256,4096]{1,0:T(8,128)(2,1)} %tokens_ref.1) | copy-start | bytes 6291460
  1.0 9.6 %collective-permute-start = (bf16[8,4224]{1,0:T(8,128)(2,1)S(1)}, bf16[8,4224]{1,0:T(8,128)(2,1)S(1)}, u32[]{:S(2)}, u32[]{:S(2)}) collective-permute-start(bf16[8,4224]{1,0:T(8,128)(2,1)S(1)} %make_message.1.refs_0_), channel_id=1, source_target_pairs={{0,12},{4,8},{8,4},{12,0},{1,13},{5,9},{9,5},{13,1},{2,14},{6,10},... | collective-permute-start | bytes 202760 | tf_op jit(solution)/shard_map/ppermute | solution.py:426
  6.2 5.8 %collective-permute-start.1 = (bf16[8,4224]{1,0:T(8,128)(2,1)S(1)}, bf16[8,4224]{1,0:T(8,128)(2,1)S(1)}, u32[]{:S(2)}, u32[]{:S(2)}) collective-permute-start(bf16[8,4224]{1,0:T(8,128)(2,1)S(1)} %make_message.1.refs_0_), channel_id=1, source_target_pairs={{0,8},{4,12},{8,0},{12,4},{1,9},{5,13},{9,1},{13,5},{2,10},{6,14},... | collective-permute-start | bytes 202760 | tf_op jit(solution)/shard_map/ppermute | solution.py:426
  6.2 5.8 %collective-permute-start.2 = (bf16[8,4224]{1,0:T(8,128)(2,1)S(1)}, bf16[8,4224]{1,0:T(8,128)(2,1)S(1)}, u32[]{:S(2)}, u32[]{:S(2)}) collective-permute-start(bf16[8,4224]{1,0:T(8,128)(2,1)S(1)} %make_message.1.refs_0_), channel_id=1, source_target_pairs={{0,4},{4,0},{8,12},{12,8},{1,5},{5,1},{9,13},{13,9},{2,6},{6,2},{1... | collective-permute-start | bytes 202760 | tf_op jit(solution)/shard_map/ppermute | solution.py:426
  9.2 10.5 %collective-permute-start.3 = (bf16[256,256]{1,0:T(8,128)(2,1)S(1)}, bf16[256,256]{1,0:T(8,128)(2,1)S(1)}, u32[]{:S(2)}, u32[]{:S(2)}) collective-permute-start(bf16[256,256]{1,0:T(8,128)(2,1)S(1)} %get-tuple-element.26), channel_id=1, source_target_pairs={{0,4},{4,0},{8,12},{12,8},{1,5},{5,1},{9,13},{13,9},{2,6},{6,2},{1... | collective-permute-start | bytes 393224 | tf_op jit(solution)/shard_map/ppermute | solution.py:426
  12.0 12.5 %copy-start.1 = (bf16[1,1,8,128,1024]{4,3,2,1,0:T(8,128)(2,1)S(1)}, bf16[1,1,8,128,1024]{4,3,2,1,0:T(8,128)(2,1)}, u32[]{:S(2)}) copy-start(bf16[1,1,8,128,1024]{4,3,2,1,0:T(8,128)(2,1)} %param.14) | copy-start | bytes 6291460
  12.0 12.5 %copy-start.2 = (bf16[1,1,8,4096]{3,2,1,0:T(8,128)(2,1)S(1)}, bf16[1,1,8,4096]{3,2,1,0:T(8,128)(2,1)}, u32[]{:S(2)}) copy-start(bf16[1,1,8,4096]{3,2,1,0:T(8,128)(2,1)} %param.13) | copy-start | bytes 196612
  12.0 12.5 %copy-start.3 = (s32[8,128]{1,0:T(8,128)S(1)}, s32[8,128]{1,0:T(8,128)}, u32[]{:S(2)}) copy-start(s32[8,128]{1,0:T(8,128)} %signs_ref.1) | copy-start | bytes 12292
  12.0 12.5 %copy-start.4 = (s32[1,1,8]{2,1,0:T(1,128)S(1)}, s32[1,1,8]{2,1,0:T(1,128)}, u32[]{:S(2)}) copy-start(s32[1,1,8]{2,1,0:T(1,128)} %lengths_ref.1) | copy-start | bytes 100
  12.4 5.6 %collective-permute-start.4 = (f32[16,256]{1,0:T(8,128)S(1)}, f32[16,256]{1,0:T(8,128)S(1)}, u32[]{:S(2)}, u32[]{:S(2)}) collective-permute-start(f32[16,256]{1,0:T(8,128)S(1)} %get-tuple-element.28), channel_id=1, source_target_pairs={{0,12},{4,8},{8,4},{12,0},{1,13},{5,9},{9,5},{13,1},{2,14},{6,10},... | collective-permute-start | bytes 49160 | tf_op jit(solution)/shard_map/ppermute | solution.py:426
  15.1 4.6 %collective-permute-start.5 = (f32[16,256]{1,0:T(8,128)S(1)}, f32[16,256]{1,0:T(8,128)S(1)}, u32[]{:S(2)}, u32[]{:S(2)}) collective-permute-start(f32[16,256]{1,0:T(8,128)S(1)} %get-tuple-element.27.refs_0_), channel_id=1, source_target_pairs={{0,8},{4,12},{8,0},{12,4},{1,9},{5,13},{9,1},{13,5},{2,10},{6,14},... | collective-permute-start | bytes 49160 | tf_op jit(solution)/shard_map/ppermute | solution.py:426
  15.2 4.5 %collective-permute-start.6 = (f32[16,256]{1,0:T(8,128)S(1)}, f32[16,256]{1,0:T(8,128)S(1)}, u32[]{:S(2)}, u32[]{:S(2)}) collective-permute-start(f32[16,256]{1,0:T(8,128)S(1)} %get-tuple-element.28), channel_id=1, source_target_pairs={{0,4},{4,0},{8,12},{12,8},{1,5},{5,1},{9,13},{13,9},{2,6},{6,2},{1... | collective-permute-start | bytes 49160 | tf_op jit(solution)/shard_map/ppermute | solution.py:426
  20.1 6.7 %collective-permute-start.7 = (bf16[16,1152]{1,0:T(8,128)(2,1)S(1)}, bf16[16,1152]{1,0:T(8,128)(2,1)S(1)}, u32[]{:S(2)}, u32[]{:S(2)}) collective-permute-start(bf16[16,1152]{1,0:T(8,128)(2,1)S(1)} %get-tuple-element.32), channel_id=1, source_target_pairs={{0,12},{4,8},{8,4},{12,0},{1,13},{5,9},{9,5},{13,1},{2,14},{6,10},... | collective-permute-start | bytes 110600 | tf_op jit(solution)/shard_map/ppermute | solution.py:426
  21.6 4.8 %collective-permute-start.8 = (bf16[16,1024]{1,0:T(8,128)(2,1)S(1)}, bf16[16,1024]{1,0:T(8,128)(2,1)S(1)}, u32[]{:S(2)}, u32[]{:S(2)}) collective-permute-start(bf16[16,1024]{1,0:T(8,128)(2,1)S(1)} %get-tuple-element.33), channel_id=1, source_target_pairs={{0,8},{4,12},{8,0},{12,4},{1,9},{5,13},{9,1},{13,5},{2,10},{6,14},... | collective-permute-start | bytes 98312 | tf_op jit(solution)/shard_map/ppermute | solution.py:426
  22.5 4.3 %collective-permute-start.9 = (bf16[16,1024]{1,0:T(8,128)(2,1)S(1)}, bf16[16,1024]{1,0:T(8,128)(2,1)S(1)}, u32[]{:S(2)}, u32[]{:S(2)}) collective-permute-start(bf16[16,1024]{1,0:T(8,128)(2,1)S(1)} %get-tuple-element.34), channel_id=1, source_target_pairs={{0,4},{4,0},{8,12},{12,8},{1,5},{5,1},{9,13},{13,9},{2,6},{6,2},{1... | collective-permute-start | bytes 98312 | tf_op jit(solution)/shard_map/ppermute | solution.py:426
  27.1 4.4 %collective-permute-start.10 = (bf16[32,1152]{1,0:T(8,128)(2,1)S(1)}, bf16[32,1152]{1,0:T(8,128)(2,1)S(1)}, u32[]{:S(2)}, u32[]{:S(2)}) collective-permute-start(bf16[32,1152]{1,0:T(8,128)(2,1)S(1)} %merge.1.own_ref), channel_id=1, source_target_pairs={{0,2},{2,0},{1,3},{3,1},{4,6},{6,4},{5,7},{7,5},{8,10},{10,8},{9,1... | collective-permute-start | bytes 221192 | tf_op jit(solution)/shard_map/ppermute | solution.py:426

commit v13 on v12

--- a/solution.py
+++ b/solution.py
@@ -35,9 +35,8 @@
     return (1 - 2 * (parity & 1)).astype(jnp.float32).astype(jnp.bfloat16)
 
 
-QUERY_ORDER = (3, 2, 1)
+QUERY_ORDER = (1, 2, 3)
 SCORE_ORDER = (3, 2, 1)
-MIXED_ORDER = (3, 2, 1)
 
 
 def arranged(blocks, order):
@@ -48,21 +47,12 @@
     return [refs[0]] + [refs[1 + order.index(d)] for d in range(1, len(refs))]
 
 
-def side():
-    return lax.axis_index("seq") & 1
-
-
-def project_kernel(tokens_ref, weight_ref, keys_ref, own_ref, near_ref, acc_ref):
+def project_kernel(tokens_ref, weight_ref, keys_ref, values_ref):
     width = keys_ref.shape[1]
-    half = own_ref.shape[1]
-    keys_ref[...] = jnp.dot(
-        tokens_ref[...], weight_ref[:, :width], preferred_element_type=jnp.float32
-    ).astype(keys_ref.dtype)
-    acc_ref[...] = jnp.dot(tokens_ref[...], weight_ref[:, width:], preferred_element_type=jnp.float32)
-    mine = pl.multiple_of(side() * half, half)
-    other = pl.multiple_of((1 - side()) * half, half)
-    own_ref[...] = acc_ref[:, pl.ds(mine, half)].astype(own_ref.dtype)
-    near_ref[...] = acc_ref[:, pl.ds(other, half)].astype(near_ref.dtype)
+    for out_ref, columns in ((keys_ref, slice(0, width)), (values_ref, slice(width, 2 * width))):
+        out_ref[...] = jnp.dot(
+            tokens_ref[...], weight_ref[:, columns], preferred_element_type=jnp.float32
+        ).astype(out_ref.dtype)
 
 
 def project(tokens, weight):
@@ -72,9 +62,8 @@
     return pl.pallas_call(
         project_kernel,
         in_specs=[vmem] * 2,
-        out_specs=[vmem] * 3,
-        out_shape=[jax.ShapeDtypeStruct((rows, columns), jnp.bfloat16) for columns in (width, width // 2, width // 2)],
-        scratch_shapes=[pltpu.VMEM((rows, width), jnp.float32)],
+        out_specs=[vmem] * 2,
+        out_shape=[jax.ShapeDtypeStruct((rows, width), jnp.bfloat16)] * 2,
         compiler_params=params(32),
         cost_estimate=pl.CostEstimate(
             flops=4 * rows * features * width,
@@ -126,7 +115,7 @@
 
 
 def cache_kernel(
-    lengths_ref, query_ref, cache_ref, signs_ref, mixed_ref, tops_ref, totals_ref, query_buf, top_buf, total_buf, mixed_buf
+    lengths_ref, query_ref, cache_ref, signs_ref, mixed_ref, stats_ref, query_buf, top_buf, total_buf, mixed_buf
 ):
     requests, span, _ = cache_ref.shape
     blocks, size = signs_ref.shape
@@ -179,26 +168,32 @@
     low = (mixed - high.astype(jnp.float32)).astype(jnp.bfloat16)
     plain = jnp.dot(high, matrix, preferred_element_type=jnp.float32)
     mixed_buf[...] = plain + jnp.dot(low, matrix, preferred_element_type=jnp.float32)
+    lane = lax.broadcasted_iota(jnp.int32, (requests, stats_ref.shape[1]), 1)
+    tops = jnp.full(lane.shape, 0.0, jnp.float32)
+    totals = jnp.ones(lane.shape, jnp.float32)
     for h in range(count):
         pick = pl.ds(h, requests, stride=count)
-        k = h // group
-        at = slice(k * requests, (k + 1) * requests)
-        column = slice(h % group * size, (h % group + 1) * size)
-        mixed_ref[at, column] = mixed_buf[pick, :] * (signs[heads + k : heads + k + 1] * norm)
-        tops_ref[at, column] = top_buf[pick, :]
-        totals_ref[at, column] = total_buf[pick, :]
+        column = slice(h * size, (h + 1) * size)
+        k = heads + h // group
+        mixed_ref[:, column] = mixed_buf[pick, :] * (signs[k : k + 1] * norm)
+        tops = jnp.where(lane == h, top_buf[pick, :], tops)
+        totals = jnp.where(lane == h, total_buf[pick, :], totals)
+    stats_ref[:requests, :] = tops
+    stats_ref[requests:, :] = totals
 
 
 def cache_part(lengths, query, cache, signs):
     requests, span, width = cache.shape
     size = signs.shape[1]
-    heads = signs.shape[0] // 2
     columns = query.shape[1]
     vmem = pl.BlockSpec(memory_space=pltpu.VMEM)
     return pl.pallas_call(
         cache_kernel,
         in_specs=[pl.BlockSpec(memory_space=pltpu.SMEM)] + [vmem] * 3,
-        out_shape=[jax.ShapeDtypeStruct((heads * requests, columns // heads), jnp.float32)] * 3,
+        out_shape=[
+            jax.ShapeDtypeStruct(query.shape, jnp.float32),
+            jax.ShapeDtypeStruct((2 * requests, size), jnp.float32),
+        ],
         scratch_shapes=[pltpu.VMEM((requests * columns // size, size), jnp.float32)] * 4,
         compiler_params=params(),
         cost_estimate=pl.CostEstimate(
@@ -220,13 +215,11 @@
 
 
 def score_kernel(heads, start, keys_ref, *refs):
-    message_refs, refs = by_distance(refs[:-4], QUERY_ORDER), refs[-4:]
-    same_ref, other_ref, code_ref, scores_ref = refs
+    message_refs, (scores_ref, code_ref) = by_distance(refs[:-2], QUERY_ORDER), refs[-2:]
     requests = message_refs[0].shape[0]
     tokens, width = keys_ref.shape
     size = width // heads
     group = start // width
-    half = same_ref.shape[0]
     code = code_row(message_refs, start, requests, tokens)
     code_ref[...] = jnp.broadcast_to(code, code_ref.shape)
     span = len(message_refs) * requests
@@ -247,178 +240,131 @@
         scores_ref[k * group : (k + 1) * group, :] = jnp.concatenate(lines, axis=0) * (
             1.0 / math.sqrt(size)
         )
-    same_ref[...] = scores_ref[pl.ds(pl.multiple_of(side() * half, half), half), :]
-    other_ref[...] = scores_ref[pl.ds(pl.multiple_of((1 - side()) * half, half), half), :]
 
 
 def partial_scores(heads, columns, keys, messages):
     tokens, width = keys.shape
-    query_heads = columns * heads // width
-    vmem = pl.BlockSpec(memory_space=pltpu.VMEM)
     return pl.pallas_call(
         functools.partial(score_kernel, heads, columns),
-        in_specs=[vmem] * (1 + len(messages)),
-        out_specs=[vmem] * 3,
         out_shape=[
-            jax.ShapeDtypeStruct((query_heads // 2, tokens), jnp.float32),
-            jax.ShapeDtypeStruct((query_heads // 2, tokens), jnp.float32),
+            jax.ShapeDtypeStruct((columns * heads // width, tokens), jnp.float32),
             jax.ShapeDtypeStruct((8, tokens), jnp.int32),
         ],
-        scratch_shapes=[pltpu.VMEM((query_heads, tokens), jnp.float32)],
         compiler_params=params(),
         cost_estimate=pl.CostEstimate(flops=10**11, bytes_accessed=10**4, transcendentals=0),
         name="partial_scores",
     )(keys, *arranged(messages, QUERY_ORDER))
 
 
-def packed(value, group, size):
-    lane = lax.broadcasted_iota(jnp.int32, (value.shape[0], size), 1)
-    narrow = jnp.zeros(lane.shape, jnp.float32)
-    for g in range(group):
-        narrow = jnp.where(lane % group == g, value[:, g * size : (g + 1) * size], narrow)
-    high = narrow.astype(jnp.bfloat16).astype(jnp.float32)
-    middle = (narrow - high).astype(jnp.bfloat16).astype(jnp.float32)
-    return jnp.where(lane < group, high, jnp.where(lane < 2 * group, middle, narrow - high - middle))
-
-
-def packed_stats(tops, totals, group):
-    size = tops.shape[1] // group
-    lane = lax.broadcasted_iota(jnp.int32, (tops.shape[0], size), 1)
-    totals = pltpu.roll(packed(totals, group, size), 3 * group, 1)
-    return jnp.where(lane < 3 * group, packed(tops, group, size), totals)
-
-
-def unpacked_stats(stats, group):
-    parts = [stats[:, at * group : (at + 1) * group] for at in range(6)]
-    return parts[0] + parts[1] + parts[2], parts[3] + parts[4] + parts[5]
-
-
-def broad(narrow, size):
-    rows, group = narrow.shape
-    return jnp.concatenate([jnp.broadcast_to(narrow[:, g : g + 1], (rows, size)) for g in range(group)], axis=1)
-
-
-def mix_kernel(heads, count, requests, code_ref, own_ref, near_ref, *refs):
-    score_refs = by_distance(refs[:count], SCORE_ORDER)
-    mixed_refs, (tops_ref, totals_ref) = refs[count : 2 * count], refs[2 * count :]
-    tokens, width = own_ref.shape
+def mix_kernel(heads, requests, code_ref, values_ref, near_ref, cache_stats_ref, *refs):
+    score_refs, (own_ref, far_ref, new_stats_ref, stats_ref) = refs[:4], refs[4:]
+    own, after, across, before = [ref[...] for ref in score_refs]
+    scores = (own + across) + (before + after)
+    tokens, width = values_ref.shape
     size = width // heads
-    group = score_refs[0].shape[0] // heads
-    span = count * requests
-    here = lax.broadcasted_iota(jnp.int32, (span, tokens), 0) == code_ref[0:1, :]
-    scores = (score_refs[0][...] + score_refs[2][...]) + (score_refs[1][...] + score_refs[3][...])
-    mixed, tops, totals = [], [], []
+    group = scores.shape[0] // heads
+    span = 2 * requests
+    row = lax.broadcasted_iota(jnp.int32, (span, tokens), 0)
+    here = jnp.where(row < requests, row, row + requests) == code_ref[0:1, :]
+    lane = lax.broadcasted_iota(jnp.int32, (requests, stats_ref.shape[1]), 1)
+    tops = jnp.full(lane.shape, 0.0, jnp.float32)
+    totals = jnp.zeros(lane.shape, jnp.float32)
     for k in range(heads):
         weights = []
         for g in range(group):
-            row = k * group + g
-            line = jnp.broadcast_to(scores[row : row + 1, :], (span, tokens))
+            h = k * group + g
+            line = jnp.broadcast_to(scores[h : h + 1, :], (span, tokens))
             top = jnp.max(jnp.where(here, line, LOWEST), axis=1, keepdims=True)
             probs = jnp.where(here, jnp.exp(line - top), 0.0)
+            total = jnp.sum(probs, axis=1, keepdims=True)
             weights.append(probs)
-            tops.append(jnp.broadcast_to(top, (span, size)))
-            totals.append(jnp.broadcast_to(jnp.sum(probs, axis=1, keepdims=True), (span, size)))
+            tops = jnp.where(lane == h, top[:requests], tops)
+            totals = jnp.where(lane == h, total[:requests], totals)
         weights = jnp.concatenate(weights, axis=0).astype(jnp.bfloat16)
         columns = slice(k * size, (k + 1) * size)
-        sums = jnp.dot(weights, own_ref[:, columns], preferred_element_type=jnp.float32)
-        mixed.append(sums + jnp.dot(weights, near_ref[:, columns], preferred_element_type=jnp.float32))
-
-    def block(parts, d):
-        rows = slice(d * requests, (d + 1) * requests)
-        lines = [
-            jnp.concatenate([parts[k * group + g][rows] for g in range(group)], axis=1) for k in range(heads)
-        ]
-        return jnp.concatenate(lines, axis=0)
-
-    pieces = [mixed[k][g * span : (g + 1) * span] for k in range(heads) for g in range(group)]
-    for d in range(count):
-        mixed_refs[d][:, : group * size] = block(pieces, d).astype(jnp.bfloat16)
-    stats = packed_stats(block(tops, 3), block(totals, 3), group)
-    mixed_refs[3][:, group * size :] = stats.astype(jnp.bfloat16)
-    tops_ref[...] = block(tops, 0)
-    totals_ref[...] = block(totals, 0)
-
-
-def mix(heads, requests, code, values, near_values, scores):
-    count = len(scores)
+        mixed = jnp.dot(weights, values_ref[:, columns], preferred_element_type=jnp.float32)
+        mixed = mixed + jnp.dot(weights, near_ref[:, columns], preferred_element_type=jnp.float32)
+        for g in range(group):
+            at = slice((k * group + g) * size, (k * group + g + 1) * size)
+            own_ref[:, at] = mixed[g * span : g * span + requests]
+            far_ref[:, at] = mixed[g * span + requests : (g + 1) * span].astype(far_ref.dtype)
+    new_stats_ref[...] = tops
+    cache_tops = cache_stats_ref[:requests, :]
+    both = jnp.maximum(cache_tops, tops)
+    stats_ref[:requests, :] = both
+    stats_ref[requests:, :] = cache_stats_ref[requests:, :] * jnp.exp(cache_tops - both) + totals * jnp.exp(
+        tops - both
+    )
+
+
+def mix(heads, code, values, near_values, cache_stats, scores):
+    requests, lanes = cache_stats.shape[0] // 2, cache_stats.shape[1]
     size = values.shape[1] // heads
-    columns = scores[0].shape[0] // heads * size
-    shape = (heads * requests, columns)
-    wide = (heads * requests, columns + size)
-    return pl.pallas_call(
-        functools.partial(mix_kernel, heads, count, requests),
-        out_shape=[jax.ShapeDtypeStruct(wide if d == 3 else shape, jnp.bfloat16) for d in range(count)]
-        + [jax.ShapeDtypeStruct(shape, jnp.float32)] * 2,
+    shape = (requests, scores[0].shape[0] * size)
+    return pl.pallas_call(
+        functools.partial(mix_kernel, heads, requests),
+        out_shape=[
+            jax.ShapeDtypeStruct(shape, jnp.float32),
+            jax.ShapeDtypeStruct(shape, jnp.bfloat16),
+            jax.ShapeDtypeStruct((requests, lanes), jnp.float32),
+            jax.ShapeDtypeStruct(cache_stats.shape, jnp.float32),
+        ],
         compiler_params=params(),
         name="mix",
-    )(code, values, near_values, *arranged(scores, SCORE_ORDER))
-
-
-def merge_kernel(cache_ref, top_ref, total_ref, new_top_ref, new_total_ref, *refs):
-    mixed_refs, out_ref = by_distance(refs[:-1], MIXED_ORDER), refs[-1]
-    rows, columns = new_top_ref.shape
-    size = out_ref.shape[1] - columns
-    group = columns // size
-    far = mixed_refs[3][...].astype(jnp.float32)
-    far_top, far_total = unpacked_stats(far[:, columns:], group)
-    own = mixed_refs[0][...].astype(jnp.float32) + mixed_refs[2][...].astype(jnp.float32)
-    other = mixed_refs[1][...].astype(jnp.float32) + far[:, :columns]
-    parts = (
-        (side(), own, new_top_ref[...], new_total_ref[...]),
-        (1 - side(), other, broad(far_top, size), broad(far_total, size)),
-    )
-    for place, new, new_top, new_total in parts:
-        at = pl.ds(pl.multiple_of(place * rows, rows), rows)
-        top = top_ref[at, :]
-        both = jnp.maximum(top, new_top)
-        cache_factor = jnp.exp(top - both)
-        new_factor = jnp.exp(new_top - both)
-        out_ref[at, :columns] = (cache_ref[at, :] * cache_factor + new * new_factor).astype(out_ref.dtype)
-        total = total_ref[at, :] * cache_factor + new_total * new_factor
-        out_ref[at, columns:] = packed_stats(both, total, group).astype(out_ref.dtype)
-
-
-def merge(size, cache_mixed, tops, totals, new_tops, new_totals, mixed):
-    rows, columns = cache_mixed.shape
+    )(code, values, near_values, cache_stats, *arranged(scores, SCORE_ORDER))
+
+
+def weigh_kernel(cache_ref, own_ref, cache_stats_ref, new_stats_ref, stats_ref, other_ref, base_ref, factor_ref):
+    requests, columns = cache_ref.shape
+    size = cache_stats_ref.shape[1]
+    top, other_top = stats_ref[:requests, :], other_ref[:requests, :]
+    both = jnp.maximum(top, other_top)
+    total = stats_ref[requests:, :] * jnp.exp(top - both)
+    total = total + other_ref[requests:, :] * jnp.exp(other_top - both)
+    inverse = 1.0 / total
+    cache_factor = jnp.exp(cache_stats_ref[:requests, :] - both) * inverse
+    new_factor = jnp.exp(new_stats_ref[...] - both) * inverse
+    for h in range(columns // size):
+        at = slice(h * size, (h + 1) * size)
+        factor = jnp.broadcast_to(new_factor[:, h : h + 1], (requests, size))
+        factor_ref[:, at] = factor
+        base_ref[:, at] = cache_ref[:, at] * cache_factor[:, h : h + 1] + own_ref[:, at] * factor
+
+
+def weigh(cache_mixed, own, cache_stats, new_stats, stats, other):
+    return pl.pallas_call(
+        weigh_kernel,
+        out_shape=[jax.ShapeDtypeStruct(own.shape, jnp.float32)] * 2,
+        compiler_params=params(),
+        name="weigh",
+    )(cache_mixed, own, cache_stats, new_stats, stats, other)
+
+
+def merge_kernel(base_ref, factor_ref, far_ref, out_ref):
+    out = base_ref[...] + far_ref[...].astype(jnp.float32) * factor_ref[...]
+    out_ref[...] = out.astype(out_ref.dtype)
+
+
+def merge(base, factor, far):
     return pl.pallas_call(
         merge_kernel,
-        out_shape=jax.ShapeDtypeStruct((rows, columns + size), jnp.bfloat16),
+        out_shape=jax.ShapeDtypeStruct(far.shape, far.dtype),
         compiler_params=params(),
         name="merge",
-    )(cache_mixed, tops, totals, new_tops, new_totals, *arranged(mixed, MIXED_ORDER))
-
-
-def finish_kernel(own_ref, far_ref, out_ref):
-    requests = out_ref.shape[0]
-    rows, wide = own_ref.shape
-    heads = rows // requests
-    columns = out_ref.shape[1] // heads
-    size = wide - columns
-    group = columns // size
-    first = lax.axis_index("tp") == 0
-    own, far = own_ref[...].astype(jnp.float32), far_ref[...].astype(jnp.float32)
-    low, high = jnp.where(first, own, far), jnp.where(first, far, own)
-    low_top, low_total = unpacked_stats(low[:, columns:], group)
-    high_top, high_total = unpacked_stats(high[:, columns:], group)
-    both = jnp.maximum(low_top, high_top)
-    low_factor, high_factor = jnp.exp(low_top - both), jnp.exp(high_top - both)
-    inverse = 1.0 / (low_total * low_factor + high_total * high_factor)
-    low_factor, high_factor = low_factor * inverse, high_factor * inverse
-    for g in range(group):
-        at = slice(g * size, (g + 1) * size)
-        out = low[:, at] * low_factor[:, g : g + 1] + high[:, at] * high_factor[:, g : g + 1]
-        for k in range(heads):
-            column = slice((k * group + g) * size, (k * group + g + 1) * size)
-            out_ref[:, column] = out[k * requests : (k + 1) * requests].astype(out_ref.dtype)
-
-
-def finish(requests, own, far, columns):
+    )(base, factor, far)
+
+
+def finish_kernel(own_ref, other_ref, out_ref):
+    out_ref[...] = (own_ref[...].astype(jnp.float32) + other_ref[...].astype(jnp.float32)).astype(out_ref.dtype)
+
+
+def finish(own, other):
     return pl.pallas_call(
         finish_kernel,
-        out_shape=jax.ShapeDtypeStruct((requests, columns), jnp.bfloat16),
+        out_shape=jax.ShapeDtypeStruct(own.shape, own.dtype),
         compiler_params=params(),
         name="finish",
-    )(own, far)
+    )(own, other)
 
 
 def from_partner(x, axis, distance):
@@ -426,29 +372,29 @@
     return lax.ppermute(x, axis, [(i, i ^ distance) for i in range(count)])
 
 
-def exchange(blocks):
-    return [blocks[0]] + [from_partner(blocks[d], "seq", d) for d in range(1, len(blocks))]
+def from_behind(x, axis, distance):
+    count = lax.axis_size(axis)
+    return lax.ppermute(x, axis, [(i, (i + distance) % count) for i in range(count)])
 
 
 def on_device(tokens, kv_weight, owners, requests, signs, queries, kv_cache, lengths):
     seq_count = lax.axis_size("seq")
-    blocks, size = signs.shape
-    heads = blocks // 2
+    heads = signs.shape[0] // 2
     query = queries[0, 0]
     request_count, columns = query.shape
     message = make_message(query, owners[:, :, 0], requests)
-    messages = exchange([message] * seq_count)
-    keys, values, far_values = project(tokens, kv_weight)
-    near_values = from_partner(far_values, "seq", 1)
-    same, other, code = partial_scores(heads, columns, keys, messages)
-    scores = exchange([same, other, same, other])
-    results = mix(heads // 2, request_count, code, values, near_values, scores)
-    mixed, (new_tops, new_totals) = results[:seq_count], results[seq_count:]
-    mixed = exchange(mixed)
-    cache_mixed, tops, totals = cache_part(lengths, query, kv_cache[0, 0], signs)
-    own = merge(size, cache_mixed, tops, totals, new_tops, new_totals, mixed)
-    far = from_partner(own, "tp", 1)
-    return finish(request_count, own, far, columns).reshape(1, 1, request_count, columns)
+    messages = [message] + [from_partner(message, "seq", d) for d in range(1, seq_count)]
+    keys, values = project(tokens, kv_weight)
+    near_values = from_partner(values, "seq", 1)
+    scores, code = partial_scores(heads, columns, keys, messages)
+    scores = [scores] + [from_behind(scores, "seq", d) for d in range(1, seq_count)]
+    cache_mixed, cache_stats = cache_part(lengths, query, kv_cache[0, 0], signs)
+    own, far, new_stats, stats = mix(heads, code, values, near_values, cache_stats, scores)
+    far = from_partner(far, "seq", 2)
+    other = from_partner(stats, "tp", 1)
+    base, factor = weigh(cache_mixed, own, cache_stats, new_stats, stats, other)
+    share = merge(base, factor, far)
+    return finish(share, from_partner(share, "tp", 1)).reshape(1, 1, request_count, columns)
 
 
 def hadamard(order):

time: 32.6 us -> 30.7 us (0.942)
  starting transfers between devices: 17.6 us -> 16.3 us
  Pallas kernels: 7.04 us -> 6.5 us
    ppermute x11 -> x7, starting transfers between devices: 17.6 us -> 11.8 us  [from_partner(): return lax.ppermute(x, axis, [(i, i ^ distance) for i in range(count)])]
    ppermute x0 -> x3, starting transfers between devices: none -> 4.52 us  [from_behind(): lax.ppermute(x, axis, [(i, (i + distance) % count) for i in range(count)])]
    ppermute x11 -> x7, waiting for transfers between devices: 7.66 us -> 6.26 us  [from_partner(): return lax.ppermute(x, axis, [(i, i ^ distance) for i in range(count)])]
    ppermute x0 -> x3, waiting for transfers between devices: none -> 1.38 us  [from_behind(): lax.ppermute(x, axis, [(i, (i + distance) % count) for i in range(count)])]
    pallas_call x5 -> x6, Pallas kernels: 4.4 us -> 3.87 us  [the longest x1 2.32 us: project(): pl.pallas_call(project_kernel, in_specs=[vmem] * 2, out_specs=[vmem] * 2,...]
  transfers between devices with their start and end apart: 11 -> 10, of which waited for: 6 -> 4; matrix products, arithmetic and copies ran while one was open for 0% -> 0% of each run, Pallas kernels for 13% -> 14%
where the time goes in v13:
time: 30.7 us; the launch traced here: 30.6 us
  starting transfers between devices  16.3 us (53%)
  waiting for transfers between devices  7.64 us (25%)
  Pallas kernels  6.5 us (21%)
    ppermute x7, starting transfers between devices, from_partner(): return lax.ppermute(x, axis, [(i, i ^ distance) for i in range(count)])  11.8 us
    ppermute x7, waiting for transfers between devices, from_partner(): return lax.ppermute(x, axis, [(i, i ^ distance) for i in range(count)])  6.26 us
    ppermute x3, starting transfers between devices, from_behind(): lax.ppermute(x, axis, [(i, (i + distance) % count) for i in range(count)])  4.52 us
    pallas_call x1, Pallas kernels, project(): pl.pallas_call(project_kernel, in_specs=[vmem] * 2, out_specs=[vmem] * 2,...  2.32 us
    pallas_call x1, Pallas kernels, cache_part(): pl.pallas_call(cache_kernel, in_specs=[pl.BlockSpec(memory_space=pltpu.SM...  1.6 us
    ppermute x3, waiting for transfers between devices, from_behind(): lax.ppermute(x, axis, [(i, (i + distance) % count) for i in range(count)])  1.38 us
    pallas_call x1, Pallas kernels, make_message(): pl.pallas_call(message_kernel, in_specs=[pl.BlockSpec(memory_space=pl.ANY...  1.03 us
    pallas_call x1, Pallas kernels, finish(): pl.pallas_call(finish_kernel, out_shape=jax.ShapeDtypeStruct(own.shape, o...  0.65 us
  transfers between devices with their start and end apart: 10, of which 4 were waited for; matrix products, arithmetic and copies ran while one was open for 0% of the time, Pallas kernels for 14%

profile of v13, /device:TPU:0, one launch (start us, length us, event | category | flops | bytes accessed | tf_op | source)
XLA Modules:
  0.0 30.6 jit_solution(3027395407764241761)
XLA Ops:
  0.0 1.0 %make_message.1.refs_0_ = bf16[8,4224]{1,0:T(8,128)(2,1)S(1)} custom-call(bf16[8,4096]{1,0:T(8,128)(2,1)} %bitcast.7, s32[1,64]{1,0:T(1,128)} %bitcast.9, s32[1,64]{1,0:T(1,128)} %requests_ref.1), custom_call_target="tpu_custom_call" | custom-call | flops 99999997952 | bytes 10000 | tf_op jit(solution)/shard_map/make_message/pallas_call | solution.py:100
  1.0 5.1 %collective-permute-start.2 = (bf16[8,4224]{1,0:T(8,128)(2,1)S(1)}, bf16[8,4224]{1,0:T(8,128)(2,1)S(1)}, u32[]{:S(2)}, u32[]{:S(2)}) collective-permute-start(bf16[8,4224]{1,0:T(8,128)(2,1)S(1)} %make_message.1.refs_0_), channel_id=1, source_target_pairs={{0,12},{4,8},{8,4},{12,0},{1,13},{5,9},{9,5},{13,1},{2,14},{6,10},... | collective-permute-start | bytes 202760 | tf_op jit(solution)/shard_map/ppermute | solution.py:372
  6.2 0.0 collective-permute-start.1
  6.2 0.6 %collective-permute-start = (bf16[8,4224]{1,0:T(8,128)(2,1)S(1)}, bf16[8,4224]{1,0:T(8,128)(2,1)S(1)}, u32[]{:S(2)}, u32[]{:S(2)}) collective-permute-start(bf16[8,4224]{1,0:T(8,128)(2,1)S(1)} %make_message.1.refs_0_), channel_id=1, source_target_pairs={{0,4},{4,0},{8,12},{12,8},{1,5},{5,1},{9,13},{13,9},{2,6},{6,2},{1... | collective-permute-start | bytes 202760 | tf_op jit(solution)/shard_map/ppermute | solution.py:372
  6.8 2.3 %project.1 = (bf16[256,512]{1,0:T(8,128)(2,1)S(1)}, bf16[256,512]{1,0:T(8,128)(2,1)S(1)}) custom-call(bf16[256,4096]{1,0:T(8,128)(2,1)S(1)} %copy-done, bf16[4096,1024]{1,0:T(8,128)(2,1)S(1)} %bitcast.5), custom_call_target="tpu_custom_call" | custom-call | flops 2147483648 | bytes 10485760 | tf_op jit(solution)/shard_map/project/pallas_call | solution.py:62
  9.1 1.5 %collective-permute-start.3 = (bf16[256,512]{1,0:T(8,128)(2,1)S(1)}, bf16[256,512]{1,0:T(8,128)(2,1)S(1)}, u32[]{:S(2)}, u32[]{:S(2)}) collective-permute-start(bf16[256,512]{1,0:T(8,128)(2,1)S(1)} %get-tuple-element.20.values_ref), channel_id=1, source_target_pairs={{0,4},{4,0},{8,12},{12,8},{1,5},{5,1},{9,13},{13,9},{2,6},{6,2},{1... | collective-permute-start | bytes 786440 | tf_op jit(solution)/shard_map/ppermute | solution.py:372
  10.6 0.0 collective-permute-done.2.refs_3_
  10.6 1.4 %collective-permute-done.1.refs_2_ = bf16[8,4224]{1,0:T(8,128)(2,1)S(1)} collective-permute-done((bf16[8,4224]{1,0:T(8,128)(2,1)S(1)}, bf16[8,4224]{1,0:T(8,128)(2,1)S(1)}, u32[]{:S(2)}, u32[]{:S(2)}) %collective-permute-start.1) | collective-permute-done | bytes 67616 | tf_op jit(solution)/shard_map/ppermute | solution.py:372
  12.0 0.0 collective-permute-done.refs_1_
  12.0 0.0 copy-start.4
  12.0 0.3 %partial_scores.1 = (f32[32,256]{1,0:T(8,128)S(1)}, s32[8,256]{1,0:T(8,128)S(1)}) custom-call(bf16[256,512]{1,0:T(8,128)(2,1)S(1)} %get-tuple-element.18.keys_ref, bf16[8,4224]{1,0:T(8,128)(2,1)S(1)} %make_message.1.refs_0_, bf16[8,4224]{1,0:T(8,128)(2,1)S(1)} %collective-permute-done.refs_1_, bf16[8,4224]{1,0:T(8,128)(2,1)S(1)} %collective-permute-done.1.refs_2_, ...), custom_call_target="tpu_custom_call" | custom-call | flops 99999997952 | bytes 10000 | tf_op jit(solution)/shard_map/partial_scores/pallas_call | solution.py:247
  12.4 1.5 %collective-permute-start.6 = (f32[32,256]{1,0:T(8,128)S(1)}, f32[32,256]{1,0:T(8,128)S(1)}, u32[]{:S(2)}, u32[]{:S(2)}) collective-permute-start(f32[32,256]{1,0:T(8,128)S(1)} %get-tuple-element.22.refs_0_), channel_id=1, source_target_pairs={{0,4},{4,8},{8,12},{12,0},{1,5},{5,9},{9,13},{13,1},{2,6},{6,10},{... | collective-permute-start | bytes 98312 | tf_op jit(solution)/shard_map/ppermute | solution.py:377
  13.8 1.8 %collective-permute-start.5 = (f32[32,256]{1,0:T(8,128)S(1)}, f32[32,256]{1,0:T(8,128)S(1)}, u32[]{:S(2)}, u32[]{:S(2)}) collective-permute-start(f32[32,256]{1,0:T(8,128)S(1)} %get-tuple-element.22.refs_0_), channel_id=1, source_target_pairs={{0,8},{4,12},{8,0},{12,4},{1,9},{5,13},{9,1},{13,5},{2,10},{6,14},... | collective-permute-start | bytes 98312 | tf_op jit(solution)/shard_map/ppermute | solution.py:377
  15.6 1.3 %collective-permute-start.4 = (f32[32,256]{1,0:T(8,128)S(1)}, f32[32,256]{1,0:T(8,128)S(1)}, u32[]{:S(2)}, u32[]{:S(2)}) collective-permute-start(f32[32,256]{1,0:T(8,128)S(1)} %get-tuple-element.22.refs_0_), channel_id=1, source_target_pairs={{0,12},{4,0},{8,4},{12,8},{1,13},{5,1},{9,5},{13,9},{2,14},{6,2},{... | collective-permute-start | bytes 98312 | tf_op jit(solution)/shard_map/ppermute | solution.py:377
  16.9 1.6 %cache_part.1 = (f32[8,4096]{1,0:T(8,128)S(1)}, f32[16,128]{1,0:T(8,128)S(1)}) custom-call(s32[1,1,8]{2,1,0:T(1,128)S(1)} %copy-done.4, bf16[8,4096]{1,0:T(8,128)(2,1)S(1)} %bitcast.8, bf16[8,128,1024]{2,1,0:T(8,128)(2,1)S(1)} %bitcast.6, s32[8,128]{1,0:T(8,128)S(1)} %copy-done.3), custom_call_target="tpu_custom_call" | custom-call | flops 16777216 | bytes 2097152 | tf_op jit(solution)/shard_map/cache_part/pallas_call | solution.py:190
  18.5 1.4 %collective-permute-done.6.refs_3_ = f32[32,256]{1,0:T(8,128)S(1)} collective-permute-done((f32[32,256]{1,0:T(8,128)S(1)}, f32[32,256]{1,0:T(8,128)S(1)}, u32[]{:S(2)}, u32[]{:S(2)}) %collective-permute-start.6) | collective-permute-done | bytes 32800 | tf_op jit(solution)/shard_map/ppermute | solution.py:377
  19.9 0.4 %mix.1 = (f32[8,4096]{1,0:T(8,128)S(1)}, bf16[8,4096]{1,0:T(8,128)(2,1)S(1)}, f32[8,128]{1,0:T(8,128)S(1)}, f32[16,128]{1,0:T(8,128)S(1)}) custom-call(s32[8,256]{1,0:T(8,128)S(1)} %get-tuple-element.19.code_ref, bf16[256,512]{1,0:T(8,128)(2,1)S(1)} %get-tuple-element.20.values_ref, bf16[256,512]{1,0:T(8,128)(2,1)S(1)} %collective-permute-done.3.near_ref, ...), custom_call_target="tpu_custom_call" | custom-call | tf_op jit(solution)/shard_map/mix/pallas_call | solution.py:304
  20.3 1.4 %collective-permute-start.8 = (bf16[8,4096]{1,0:T(8,128)(2,1)S(1)}, bf16[8,4096]{1,0:T(8,128)(2,1)S(1)}, u32[]{:S(2)}, u32[]{:S(2)}) collective-permute-start(bf16[8,4096]{1,0:T(8,128)(2,1)S(1)} %get-tuple-element.28), channel_id=1, source_target_pairs={{0,8},{4,12},{8,0},{12,4},{1,9},{5,13},{9,1},{13,5},{2,10},{6,14},... | collective-permute-start | bytes 196616 | tf_op jit(solution)/shard_map/ppermute | solution.py:372
  21.7 1.5 %collective-permute-start.7 = (f32[16,128]{1,0:T(8,128)S(1)}, f32[16,128]{1,0:T(8,128)S(1)}, u32[]{:S(2)}, u32[]{:S(2)}) collective-permute-start(f32[16,128]{1,0:T(8,128)S(1)} %get-tuple-element.25.stats_ref), channel_id=1, source_target_pairs={{0,2},{2,0},{1,3},{3,1},{4,6},{6,4},{5,7},{7,5},{8,10},{10,8},{9,1... | collective-permute-start | bytes 24584 | tf_op jit(solution)/shard_map/ppermute | solution.py:372
  23.2 2.2 %collective-permute-done.7.other_ref = f32[16,128]{1,0:T(8,128)S(1)} collective-permute-done((f32[16,128]{1,0:T(8,128)S(1)}, f32[16,128]{1,0:T(8,128)S(1)}, u32[]{:S(2)}, u32[]{:S(2)}) %collective-permute-start.7) | collective-permute-done | bytes 8224 | tf_op jit(solution)/shard_map/ppermute | solution.py:372
  25.4 0.2 weigh.1
  25.6 1.6 %collective-permute-start.9 = (bf16[8,4096]{1,0:T(8,128)(2,1)S(1)}, bf16[8,4096]{1,0:T(8,128)(2,1)S(1)}, u32[]{:S(2)}, u32[]{:S(2)}) collective-permute-start(bf16[8,4096]{1,0:T(8,128)(2,1)S(1)} %merge.1.own_ref), channel_id=1, source_target_pairs={{0,2},{2,0},{1,3},{3,1},{4,6},{6,4},{5,7},{7,5},{8,10},{10,8},{9,1... | collective-permute-start | bytes 196616 | tf_op jit(solution)/shard_map/ppermute | solution.py:372
  27.2 2.7 %collective-permute-done.9.other_ref = bf16[8,4096]{1,0:T(8,128)(2,1)S(1)} collective-permute-done((bf16[8,4096]{1,0:T(8,128)(2,1)S(1)}, bf16[8,4096]{1,0:T(8,128)(2,1)S(1)}, u32[]{:S(2)}, u32[]{:S(2)}) %collective-permute-start.9) | collective-permute-done | bytes 65568 | tf_op jit(solution)/shard_map/ppermute | solution.py:372
  29.9 0.6 %finish.1 = bf16[8,4096]{1,0:T(8,128)(2,1)} custom-call(bf16[8,4096]{1,0:T(8,128)(2,1)S(1)} %merge.1.own_ref, bf16[8,4096]{1,0:T(8,128)(2,1)S(1)} %collective-permute-done.9.other_ref), custom_call_target="tpu_custom_call" | custom-call | tf_op jit(solution)/shard_map/finish/pallas_call | solution.py:362
  (19 shorter events, 0.1 us)
Async XLA Ops:
  0.0 6.8 %slice-start = ((s8[8388608]{0:T(1024)(128)(4,1)}), s8[4194304]{0:T(1024)(128)(4,1)S(1)}, s32[]{:S(2)}) async-start(s8[8388608]{0:T(1024)(128)(4,1)} %bitcast.4), calls=%async_computation | async-start | bytes 8388608
  0.0 6.8 %slice-start.1 = ((s8[8388608]{0:T(1024)(128)(4,1)}), s8[4194304]{0:T(1024)(128)(4,1)S(1)}, s32[]{:S(2)}) async-start(s8[8388608]{0:T(1024)(128)(4,1)} %bitcast.4), calls=%async_computation.1 | async-start | bytes 8388608
  0.0 6.8 %copy-start = (bf16[256,4096]{1,0:T(8,128)(2,1)S(1)}, bf16[256,4096]{1,0:T(8,128)(2,1)}, u32[]{:S(2)}) copy-start(bf16[256,4096]{1,0:T(8,128)(2,1)} %tokens_ref.1) | copy-start | bytes 6291460
  1.0 9.6 %collective-permute-start.2 = (bf16[8,4224]{1,0:T(8,128)(2,1)S(1)}, bf16[8,4224]{1,0:T(8,128)(2,1)S(1)}, u32[]{:S(2)}, u32[]{:S(2)}) collective-permute-start(bf16[8,4224]{1,0:T(8,128)(2,1)S(1)} %make_message.1.refs_0_), channel_id=1, source_target_pairs={{0,12},{4,8},{8,4},{12,0},{1,13},{5,9},{9,5},{13,1},{2,14},{6,10},... | collective-permute-start | bytes 202760 | tf_op jit(solution)/shard_map/ppermute | solution.py:372
  6.2 5.8 %collective-permute-start.1 = (bf16[8,4224]{1,0:T(8,128)(2,1)S(1)}, bf16[8,4224]{1,0:T(8,128)(2,1)S(1)}, u32[]{:S(2)}, u32[]{:S(2)}) collective-permute-start(bf16[8,4224]{1,0:T(8,128)(2,1)S(1)} %make_message.1.refs_0_), channel_id=1, source_target_pairs={{0,8},{4,12},{8,0},{12,4},{1,9},{5,13},{9,1},{13,5},{2,10},{6,14},... | collective-permute-start | bytes 202760 | tf_op jit(solution)/shard_map/ppermute | solution.py:372
  6.2 5.8 %collective-permute-start = (bf16[8,4224]{1,0:T(8,128)(2,1)S(1)}, bf16[8,4224]{1,0:T(8,128)(2,1)S(1)}, u32[]{:S(2)}, u32[]{:S(2)}) collective-permute-start(bf16[8,4224]{1,0:T(8,128)(2,1)S(1)} %make_message.1.refs_0_), channel_id=1, source_target_pairs={{0,4},{4,0},{8,12},{12,8},{1,5},{5,1},{9,13},{13,9},{2,6},{6,2},{1... | collective-permute-start | bytes 202760 | tf_op jit(solution)/shard_map/ppermute | solution.py:372
  9.1 10.7 %collective-permute-start.3 = (bf16[256,512]{1,0:T(8,128)(2,1)S(1)}, bf16[256,512]{1,0:T(8,128)(2,1)S(1)}, u32[]{:S(2)}, u32[]{:S(2)}) collective-permute-start(bf16[256,512]{1,0:T(8,128)(2,1)S(1)} %get-tuple-element.20.values_ref), channel_id=1, source_target_pairs={{0,4},{4,0},{8,12},{12,8},{1,5},{5,1},{9,13},{13,9},{2,6},{6,2},{1... | collective-permute-start | bytes 786440 | tf_op jit(solution)/shard_map/ppermute | solution.py:372
  12.0 4.9 %copy-start.1 = (bf16[1,1,8,128,1024]{4,3,2,1,0:T(8,128)(2,1)S(1)}, bf16[1,1,8,128,1024]{4,3,2,1,0:T(8,128)(2,1)}, u32[]{:S(2)}) copy-start(bf16[1,1,8,128,1024]{4,3,2,1,0:T(8,128)(2,1)} %param.14) | copy-start | bytes 6291460
  12.0 4.9 %copy-start.2 = (bf16[1,1,8,4096]{3,2,1,0:T(8,128)(2,1)S(1)}, bf16[1,1,8,4096]{3,2,1,0:T(8,128)(2,1)}, u32[]{:S(2)}) copy-start(bf16[1,1,8,4096]{3,2,1,0:T(8,128)(2,1)} %param.13) | copy-start | bytes 196612
  12.0 4.9 %copy-start.3 = (s32[8,128]{1,0:T(8,128)S(1)}, s32[8,128]{1,0:T(8,128)}, u32[]{:S(2)}) copy-start(s32[8,128]{1,0:T(8,128)} %signs_ref.1) | copy-start | bytes 12292
  12.0 4.9 %copy-start.4 = (s32[1,1,8]{2,1,0:T(1,128)S(1)}, s32[1,1,8]{2,1,0:T(1,128)}, u32[]{:S(2)}) copy-start(s32[1,1,8]{2,1,0:T(1,128)} %lengths_ref.1) | copy-start | bytes 100
  12.4 7.5 %collective-permute-start.6 = (f32[32,256]{1,0:T(8,128)S(1)}, f32[32,256]{1,0:T(8,128)S(1)}, u32[]{:S(2)}, u32[]{:S(2)}) collective-permute-start(f32[32,256]{1,0:T(8,128)S(1)} %get-tuple-element.22.refs_0_), channel_id=1, source_target_pairs={{0,4},{4,8},{8,12},{12,0},{1,5},{5,9},{9,13},{13,1},{2,6},{6,10},{... | collective-permute-start | bytes 98312 | tf_op jit(solution)/shard_map/ppermute | solution.py:377
  13.8 6.1 %collective-permute-start.5 = (f32[32,256]{1,0:T(8,128)S(1)}, f32[32,256]{1,0:T(8,128)S(1)}, u32[]{:S(2)}, u32[]{:S(2)}) collective-permute-start(f32[32,256]{1,0:T(8,128)S(1)} %get-tuple-element.22.refs_0_), channel_id=1, source_target_pairs={{0,8},{4,12},{8,0},{12,4},{1,9},{5,13},{9,1},{13,5},{2,10},{6,14},... | collective-permute-start | bytes 98312 | tf_op jit(solution)/shard_map/ppermute | solution.py:377
  15.6 4.3 %collective-permute-start.4 = (f32[32,256]{1,0:T(8,128)S(1)}, f32[32,256]{1,0:T(8,128)S(1)}, u32[]{:S(2)}, u32[]{:S(2)}) collective-permute-start(f32[32,256]{1,0:T(8,128)S(1)} %get-tuple-element.22.refs_0_), channel_id=1, source_target_pairs={{0,12},{4,0},{8,4},{12,8},{1,13},{5,1},{9,5},{13,9},{2,14},{6,2},{... | collective-permute-start | bytes 98312 | tf_op jit(solution)/shard_map/ppermute | solution.py:377
  20.3 5.3 %collective-permute-start.8 = (bf16[8,4096]{1,0:T(8,128)(2,1)S(1)}, bf16[8,4096]{1,0:T(8,128)(2,1)S(1)}, u32[]{:S(2)}, u32[]{:S(2)}) collective-permute-start(bf16[8,4096]{1,0:T(8,128)(2,1)S(1)} %get-tuple-element.28), channel_id=1, source_target_pairs={{0,8},{4,12},{8,0},{12,4},{1,9},{5,13},{9,1},{13,5},{2,10},{6,14},... | collective-permute-start | bytes 196616 | tf_op jit(solution)/shard_map/ppermute | solution.py:372
  21.7 3.7 %collective-permute-start.7 = (f32[16,128]{1,0:T(8,128)S(1)}, f32[16,128]{1,0:T(8,128)S(1)}, u32[]{:S(2)}, u32[]{:S(2)}) collective-permute-start(f32[16,128]{1,0:T(8,128)S(1)} %get-tuple-element.25.stats_ref), channel_id=1, source_target_pairs={{0,2},{2,0},{1,3},{3,1},{4,6},{6,4},{5,7},{7,5},{8,10},{10,8},{9,1... | collective-permute-start | bytes 24584 | tf_op jit(solution)/shard_map/ppermute | solution.py:372
  25.6 4.3 %collective-permute-start.9 = (bf16[8,4096]{1,0:T(8,128)(2,1)S(1)}, bf16[8,4096]{1,0:T(8,128)(2,1)S(1)}, u32[]{:S(2)}, u32[]{:S(2)}) collective-permute-start(bf16[8,4096]{1,0:T(8,128)(2,1)S(1)} %merge.1.own_ref), channel_id=1, source_target_pairs={{0,2},{2,0},{1,3},{3,1},{4,6},{6,4},{5,7},{7,5},{8,10},{10,8},{9,1... | collective-permute-start | bytes 196616 | tf_op jit(solution)/shard_map/ppermute | solution.py:372

commit v14 on v13

--- a/solution.py
+++ b/solution.py
@@ -47,31 +47,30 @@
     return [refs[0]] + [refs[1 + order.index(d)] for d in range(1, len(refs))]
 
 
-def project_kernel(tokens_ref, weight_ref, keys_ref, values_ref):
-    width = keys_ref.shape[1]
-    for out_ref, columns in ((keys_ref, slice(0, width)), (values_ref, slice(width, 2 * width))):
-        out_ref[...] = jnp.dot(
-            tokens_ref[...], weight_ref[:, columns], preferred_element_type=jnp.float32
-        ).astype(out_ref.dtype)
-
-
-def project(tokens, weight):
+def project_kernel(tokens_ref, weight_ref, out_ref, *, first):
+    width = out_ref.shape[1]
+    columns = slice(first, first + width)
+    product = jnp.dot(tokens_ref[...], weight_ref[:, columns], preferred_element_type=jnp.float32)
+    out_ref[...] = product.astype(out_ref.dtype)
+
+
+def project(tokens, weight, part, name):
     rows, features = tokens.shape
     width = weight.shape[1] // 2
     vmem = pl.BlockSpec(memory_space=pltpu.VMEM)
     return pl.pallas_call(
-        project_kernel,
+        functools.partial(project_kernel, first=part * width),
         in_specs=[vmem] * 2,
-        out_specs=[vmem] * 2,
-        out_shape=[jax.ShapeDtypeStruct((rows, width), jnp.bfloat16)] * 2,
+        out_specs=vmem,
+        out_shape=jax.ShapeDtypeStruct((rows, width), jnp.bfloat16),
         compiler_params=params(32),
         cost_estimate=pl.CostEstimate(
-            flops=4 * rows * features * width,
-            bytes_accessed=2 * (rows * features + 2 * features * width),
+            flops=2 * rows * features * width,
+            bytes_accessed=2 * (rows * features + features * width),
             transcendentals=0,
         ),
-        name="project",
-    )(in_vmem(tokens), in_vmem(weight))
+        name=name,
+    )(tokens, weight)
 
 
 def message_kernel(query_ref, owners_ref, requests_ref, out_ref, query_buf, owners_buf, requests_buf, sems):
@@ -384,8 +383,10 @@
     request_count, columns = query.shape
     message = make_message(query, owners[:, :, 0], requests)
     messages = [message] + [from_partner(message, "seq", d) for d in range(1, seq_count)]
-    keys, values = project(tokens, kv_weight)
+    tokens, kv_weight = in_vmem(tokens), in_vmem(kv_weight)
+    values = project(tokens, kv_weight, 1, "project_values")
     near_values = from_partner(values, "seq", 1)
+    keys = project(tokens, kv_weight, 0, "project_keys")
     scores, code = partial_scores(heads, columns, keys, messages)
     scores = [scores] + [from_behind(scores, "seq", d) for d in range(1, seq_count)]
     cache_mixed, cache_stats = cache_part(lengths, query, kv_cache[0, 0], signs)

time: 30.7 us -> 31.4 us (1.023)
  waiting for transfers between devices: 7.64 us -> 8.03 us
    ppermute x7, waiting for transfers between devices: 6.26 us -> 6.97 us  [from_partner(): return lax.ppermute(x, axis, [(i, i ^ distance) for i in range(count)])]
    ppermute x3, waiting for transfers between devices: 1.38 us -> 1.06 us  [from_behind(): lax.ppermute(x, axis, [(i, (i + distance) % count) for i in range(count)])]
    pallas_call x1 -> x2, Pallas kernels: 2.32 us -> 2.48 us  [project(): pl.pallas_call(functools.partial(project_kernel, first=part * width), in_...]
  transfers between devices with their start and end apart: 10 -> 10, of which waited for: 4 -> 7; matrix products, arithmetic and copies ran while one was open for 0% -> 0% of each run, Pallas kernels for 14% -> 15%
where the time goes in v14:
time: 31.4 us; the launch traced here: 31.3 us
  starting transfers between devices  16.5 us (53%)
  waiting for transfers between devices  8.03 us (26%)
  Pallas kernels  6.64 us (21%)
    ppermute x7, starting transfers between devices, from_partner(): return lax.ppermute(x, axis, [(i, i ^ distance) for i in range(count)])  11.6 us
    ppermute x7, waiting for transfers between devices, from_partner(): return lax.ppermute(x, axis, [(i, i ^ distance) for i in range(count)])  6.97 us
    ppermute x3, starting transfers between devices, from_behind(): lax.ppermute(x, axis, [(i, (i + distance) % count) for i in range(count)])  4.83 us
    pallas_call x2, Pallas kernels, project(): pl.pallas_call(functools.partial(project_kernel, first=part * width), in_...  2.48 us
    pallas_call x1, Pallas kernels, cache_part(): pl.pallas_call(cache_kernel, in_specs=[pl.BlockSpec(memory_space=pltpu.SM...  1.6 us
    ppermute x3, waiting for transfers between devices, from_behind(): lax.ppermute(x, axis, [(i, (i + distance) % count) for i in range(count)])  1.06 us
    pallas_call x1, Pallas kernels, make_message(): pl.pallas_call(message_kernel, in_specs=[pl.BlockSpec(memory_space=pl.ANY...  1.03 us
    pallas_call x1, Pallas kernels, finish(): pl.pallas_call(finish_kernel, out_shape=jax.ShapeDtypeStruct(own.shape, o...  0.65 us
  transfers between devices with their start and end apart: 10, of which 7 were waited for; matrix products, arithmetic and copies ran while one was open for 0% of the time, Pallas kernels for 15%

profile of v14, /device:TPU:0, one launch (start us, length us, event | category | flops | bytes accessed | tf_op | source)
XLA Modules:
  0.0 31.3 jit_solution(1113832533616373907)
XLA Ops:
  0.0 1.0 %make_message.1.refs_0_ = bf16[8,4224]{1,0:T(8,128)(2,1)S(1)} custom-call(bf16[8,4096]{1,0:T(8,128)(2,1)} %bitcast.7, s32[1,64]{1,0:T(1,128)} %bitcast.9, s32[1,64]{1,0:T(1,128)} %requests_ref.1), custom_call_target="tpu_custom_call" | custom-call | flops 99999997952 | bytes 10000 | tf_op jit(solution)/shard_map/make_message/pallas_call | solution.py:99
  1.0 5.1 %collective-permute-start.2 = (bf16[8,4224]{1,0:T(8,128)(2,1)S(1)}, bf16[8,4224]{1,0:T(8,128)(2,1)S(1)}, u32[]{:S(2)}, u32[]{:S(2)}) collective-permute-start(bf16[8,4224]{1,0:T(8,128)(2,1)S(1)} %make_message.1.refs_0_), channel_id=1, source_target_pairs={{0,12},{4,8},{8,4},{12,0},{1,13},{5,9},{9,5},{13,1},{2,14},{6,10},... | collective-permute-start | bytes 202760 | tf_op jit(solution)/shard_map/ppermute | solution.py:371
  6.2 0.6 %collective-permute-start = (bf16[8,4224]{1,0:T(8,128)(2,1)S(1)}, bf16[8,4224]{1,0:T(8,128)(2,1)S(1)}, u32[]{:S(2)}, u32[]{:S(2)}) collective-permute-start(bf16[8,4224]{1,0:T(8,128)(2,1)S(1)} %make_message.1.refs_0_), channel_id=1, source_target_pairs={{0,4},{4,0},{8,12},{12,8},{1,5},{5,1},{9,13},{13,9},{2,6},{6,2},{1... | collective-permute-start | bytes 202760 | tf_op jit(solution)/shard_map/ppermute | solution.py:371
  6.8 1.2 %project_values.1.values_ref = bf16[256,512]{1,0:T(8,128)(2,1)S(1)} custom-call(bf16[256,4096]{1,0:T(8,128)(2,1)S(1)} %copy-done, bf16[4096,1024]{1,0:T(8,128)(2,1)S(1)} %bitcast.5), custom_call_target="tpu_custom_call" | custom-call | flops 1073741824 | bytes 6291456 | tf_op jit(solution)/shard_map/project_values/pallas_call | solution.py:61
  8.1 1.5 %collective-permute-start.3 = (bf16[256,512]{1,0:T(8,128)(2,1)S(1)}, bf16[256,512]{1,0:T(8,128)(2,1)S(1)}, u32[]{:S(2)}, u32[]{:S(2)}) collective-permute-start(bf16[256,512]{1,0:T(8,128)(2,1)S(1)} %project_values.1.values_ref), channel_id=1, source_target_pairs={{0,4},{4,0},{8,12},{12,8},{1,5},{5,1},{9,13},{13,9},{2,6},{6,2},{1... | collective-permute-start | bytes 786440 | tf_op jit(solution)/shard_map/ppermute | solution.py:371
  9.5 1.2 %project_keys.1.keys_ref = bf16[256,512]{1,0:T(8,128)(2,1)S(1)} custom-call(bf16[256,4096]{1,0:T(8,128)(2,1)S(1)} %copy-done, bf16[4096,1024]{1,0:T(8,128)(2,1)S(1)} %bitcast.5), custom_call_target="tpu_custom_call" | custom-call | flops 1073741824 | bytes 6291456 | tf_op jit(solution)/shard_map/project_keys/pallas_call | solution.py:61
  10.8 1.2 %collective-permute-done.1.refs_2_ = bf16[8,4224]{1,0:T(8,128)(2,1)S(1)} collective-permute-done((bf16[8,4224]{1,0:T(8,128)(2,1)S(1)}, bf16[8,4224]{1,0:T(8,128)(2,1)S(1)}, u32[]{:S(2)}, u32[]{:S(2)}) %collective-permute-start.1) | collective-permute-done | bytes 67616 | tf_op jit(solution)/shard_map/ppermute | solution.py:371
  12.0 0.1 collective-permute-done.refs_1_
  12.2 0.3 partial_scores.1
  12.5 2.0 %collective-permute-start.6 = (f32[32,256]{1,0:T(8,128)S(1)}, f32[32,256]{1,0:T(8,128)S(1)}, u32[]{:S(2)}, u32[]{:S(2)}) collective-permute-start(f32[32,256]{1,0:T(8,128)S(1)} %get-tuple-element.18.refs_0_), channel_id=1, source_target_pairs={{0,4},{4,8},{8,12},{12,0},{1,5},{5,9},{9,13},{13,1},{2,6},{6,10},{... | collective-permute-start | bytes 98312 | tf_op jit(solution)/shard_map/ppermute | solution.py:376
  14.5 1.1 %collective-permute-start.5 = (f32[32,256]{1,0:T(8,128)S(1)}, f32[32,256]{1,0:T(8,128)S(1)}, u32[]{:S(2)}, u32[]{:S(2)}) collective-permute-start(f32[32,256]{1,0:T(8,128)S(1)} %get-tuple-element.18.refs_0_), channel_id=1, source_target_pairs={{0,8},{4,12},{8,0},{12,4},{1,9},{5,13},{9,1},{13,5},{2,10},{6,14},... | collective-permute-start | bytes 98312 | tf_op jit(solution)/shard_map/ppermute | solution.py:376
  15.6 1.7 %collective-permute-start.4 = (f32[32,256]{1,0:T(8,128)S(1)}, f32[32,256]{1,0:T(8,128)S(1)}, u32[]{:S(2)}, u32[]{:S(2)}) collective-permute-start(f32[32,256]{1,0:T(8,128)S(1)} %get-tuple-element.18.refs_0_), channel_id=1, source_target_pairs={{0,12},{4,0},{8,4},{12,8},{1,13},{5,1},{9,5},{13,9},{2,14},{6,2},{... | collective-permute-start | bytes 98312 | tf_op jit(solution)/shard_map/ppermute | solution.py:376
  17.3 1.6 %cache_part.1 = (f32[8,4096]{1,0:T(8,128)S(1)}, f32[16,128]{1,0:T(8,128)S(1)}) custom-call(s32[1,1,8]{2,1,0:T(1,128)S(1)} %copy-done.4, bf16[8,4096]{1,0:T(8,128)(2,1)S(1)} %bitcast.8, bf16[8,128,1024]{2,1,0:T(8,128)(2,1)S(1)} %bitcast.6, s32[8,128]{1,0:T(8,128)S(1)} %copy-done.3), custom_call_target="tpu_custom_call" | custom-call | flops 16777216 | bytes 2097152 | tf_op jit(solution)/shard_map/cache_part/pallas_call | solution.py:189
  18.9 0.7 %collective-permute-done.6.refs_3_ = f32[32,256]{1,0:T(8,128)S(1)} collective-permute-done((f32[32,256]{1,0:T(8,128)S(1)}, f32[32,256]{1,0:T(8,128)S(1)}, u32[]{:S(2)}, u32[]{:S(2)}) %collective-permute-start.6) | collective-permute-done | bytes 32800 | tf_op jit(solution)/shard_map/ppermute | solution.py:376
  19.6 0.3 %collective-permute-done.5.refs_2_ = f32[32,256]{1,0:T(8,128)S(1)} collective-permute-done((f32[32,256]{1,0:T(8,128)S(1)}, f32[32,256]{1,0:T(8,128)S(1)}, u32[]{:S(2)}, u32[]{:S(2)}) %collective-permute-start.5) | collective-permute-done | bytes 32800 | tf_op jit(solution)/shard_map/ppermute | solution.py:376
  20.0 0.4 %mix.1 = (f32[8,4096]{1,0:T(8,128)S(1)}, bf16[8,4096]{1,0:T(8,128)(2,1)S(1)}, f32[8,128]{1,0:T(8,128)S(1)}, f32[16,128]{1,0:T(8,128)S(1)}) custom-call(s32[8,256]{1,0:T(8,128)S(1)} %get-tuple-element.16.code_ref, bf16[256,512]{1,0:T(8,128)(2,1)S(1)} %project_values.1.values_ref, bf16[256,512]{1,0:T(8,128)(2,1)S(1)} %collective-permute-done.3.near_ref, ...), custom_call_target="tpu_custom_call" | custom-call | tf_op jit(solution)/shard_map/mix/pallas_call | solution.py:303
  20.4 1.4 %collective-permute-start.8 = (bf16[8,4096]{1,0:T(8,128)(2,1)S(1)}, bf16[8,4096]{1,0:T(8,128)(2,1)S(1)}, u32[]{:S(2)}, u32[]{:S(2)}) collective-permute-start(bf16[8,4096]{1,0:T(8,128)(2,1)S(1)} %get-tuple-element.24), channel_id=1, source_target_pairs={{0,8},{4,12},{8,0},{12,4},{1,9},{5,13},{9,1},{13,5},{2,10},{6,14},... | collective-permute-start | bytes 196616 | tf_op jit(solution)/shard_map/ppermute | solution.py:371
  21.7 1.5 %collective-permute-start.7 = (f32[16,128]{1,0:T(8,128)S(1)}, f32[16,128]{1,0:T(8,128)S(1)}, u32[]{:S(2)}, u32[]{:S(2)}) collective-permute-start(f32[16,128]{1,0:T(8,128)S(1)} %get-tuple-element.21.stats_ref), channel_id=1, source_target_pairs={{0,2},{2,0},{1,3},{3,1},{4,6},{6,4},{5,7},{7,5},{8,10},{10,8},{9,1... | collective-permute-start | bytes 24584 | tf_op jit(solution)/shard_map/ppermute | solution.py:371
  23.2 2.2 %collective-permute-done.7.other_ref = f32[16,128]{1,0:T(8,128)S(1)} collective-permute-done((f32[16,128]{1,0:T(8,128)S(1)}, f32[16,128]{1,0:T(8,128)S(1)}, u32[]{:S(2)}, u32[]{:S(2)}) %collective-permute-start.7) | collective-permute-done | bytes 8224 | tf_op jit(solution)/shard_map/ppermute | solution.py:371
  25.4 0.2 weigh.1
  25.6 0.7 %collective-permute-done.8.far_ref = bf16[8,4096]{1,0:T(8,128)(2,1)S(1)} collective-permute-done((bf16[8,4096]{1,0:T(8,128)(2,1)S(1)}, bf16[8,4096]{1,0:T(8,128)(2,1)S(1)}, u32[]{:S(2)}, u32[]{:S(2)}) %collective-permute-start.8) | collective-permute-done | bytes 65568 | tf_op jit(solution)/shard_map/ppermute | solution.py:371
  26.3 1.6 %collective-permute-start.9 = (bf16[8,4096]{1,0:T(8,128)(2,1)S(1)}, bf16[8,4096]{1,0:T(8,128)(2,1)S(1)}, u32[]{:S(2)}, u32[]{:S(2)}) collective-permute-start(bf16[8,4096]{1,0:T(8,128)(2,1)S(1)} %merge.1.own_ref), channel_id=1, source_target_pairs={{0,2},{2,0},{1,3},{3,1},{4,6},{6,4},{5,7},{7,5},{8,10},{10,8},{9,1... | collective-permute-start | bytes 196616 | tf_op jit(solution)/shard_map/ppermute | solution.py:371
  27.9 2.8 %collective-permute-done.9.other_ref = bf16[8,4096]{1,0:T(8,128)(2,1)S(1)} collective-permute-done((bf16[8,4096]{1,0:T(8,128)(2,1)S(1)}, bf16[8,4096]{1,0:T(8,128)(2,1)S(1)}, u32[]{:S(2)}, u32[]{:S(2)}) %collective-permute-start.9) | collective-permute-done | bytes 65568 | tf_op jit(solution)/shard_map/ppermute | solution.py:371
  30.6 0.6 %finish.1 = bf16[8,4096]{1,0:T(8,128)(2,1)} custom-call(bf16[8,4096]{1,0:T(8,128)(2,1)S(1)} %merge.1.own_ref, bf16[8,4096]{1,0:T(8,128)(2,1)S(1)} %collective-permute-done.9.other_ref), custom_call_target="tpu_custom_call" | custom-call | tf_op jit(solution)/shard_map/finish/pallas_call | solution.py:361
  (20 shorter events, 0.1 us)
Async XLA Ops:
  0.0 6.8 %slice-start = ((s8[8388608]{0:T(1024)(128)(4,1)}), s8[4194304]{0:T(1024)(128)(4,1)S(1)}, s32[]{:S(2)}) async-start(s8[8388608]{0:T(1024)(128)(4,1)} %bitcast.4), calls=%async_computation | async-start | bytes 8388608
  0.0 6.8 %slice-start.1 = ((s8[8388608]{0:T(1024)(128)(4,1)}), s8[4194304]{0:T(1024)(128)(4,1)S(1)}, s32[]{:S(2)}) async-start(s8[8388608]{0:T(1024)(128)(4,1)} %bitcast.4), calls=%async_computation.1 | async-start | bytes 8388608
  0.0 6.8 %copy-start = (bf16[256,4096]{1,0:T(8,128)(2,1)S(1)}, bf16[256,4096]{1,0:T(8,128)(2,1)}, u32[]{:S(2)}) copy-start(bf16[256,4096]{1,0:T(8,128)(2,1)} %tokens_ref.3) | copy-start | bytes 6291460
  1.0 9.8 %collective-permute-start.2 = (bf16[8,4224]{1,0:T(8,128)(2,1)S(1)}, bf16[8,4224]{1,0:T(8,128)(2,1)S(1)}, u32[]{:S(2)}, u32[]{:S(2)}) collective-permute-start(bf16[8,4224]{1,0:T(8,128)(2,1)S(1)} %make_message.1.refs_0_), channel_id=1, source_target_pairs={{0,12},{4,8},{8,4},{12,0},{1,13},{5,9},{9,5},{13,1},{2,14},{6,10},... | collective-permute-start | bytes 202760 | tf_op jit(solution)/shard_map/ppermute | solution.py:371
  6.2 5.9 %collective-permute-start.1 = (bf16[8,4224]{1,0:T(8,128)(2,1)S(1)}, bf16[8,4224]{1,0:T(8,128)(2,1)S(1)}, u32[]{:S(2)}, u32[]{:S(2)}) collective-permute-start(bf16[8,4224]{1,0:T(8,128)(2,1)S(1)} %make_message.1.refs_0_), channel_id=1, source_target_pairs={{0,8},{4,12},{8,0},{12,4},{1,9},{5,13},{9,1},{13,5},{2,10},{6,14},... | collective-permute-start | bytes 202760 | tf_op jit(solution)/shard_map/ppermute | solution.py:371
  6.2 6.0 %collective-permute-start = (bf16[8,4224]{1,0:T(8,128)(2,1)S(1)}, bf16[8,4224]{1,0:T(8,128)(2,1)S(1)}, u32[]{:S(2)}, u32[]{:S(2)}) collective-permute-start(bf16[8,4224]{1,0:T(8,128)(2,1)S(1)} %make_message.1.refs_0_), channel_id=1, source_target_pairs={{0,4},{4,0},{8,12},{12,8},{1,5},{5,1},{9,13},{13,9},{2,6},{6,2},{1... | collective-permute-start | bytes 202760 | tf_op jit(solution)/shard_map/ppermute | solution.py:371
  8.1 11.9 %collective-permute-start.3 = (bf16[256,512]{1,0:T(8,128)(2,1)S(1)}, bf16[256,512]{1,0:T(8,128)(2,1)S(1)}, u32[]{:S(2)}, u32[]{:S(2)}) collective-permute-start(bf16[256,512]{1,0:T(8,128)(2,1)S(1)} %project_values.1.values_ref), channel_id=1, source_target_pairs={{0,4},{4,0},{8,12},{12,8},{1,5},{5,1},{9,13},{13,9},{2,6},{6,2},{1... | collective-permute-start | bytes 786440 | tf_op jit(solution)/shard_map/ppermute | solution.py:371
  10.8 6.5 %copy-start.1 = (bf16[1,1,8,128,1024]{4,3,2,1,0:T(8,128)(2,1)S(1)}, bf16[1,1,8,128,1024]{4,3,2,1,0:T(8,128)(2,1)}, u32[]{:S(2)}) copy-start(bf16[1,1,8,128,1024]{4,3,2,1,0:T(8,128)(2,1)} %param.14) | copy-start | bytes 6291460
  10.8 6.5 %copy-start.2 = (bf16[1,1,8,4096]{3,2,1,0:T(8,128)(2,1)S(1)}, bf16[1,1,8,4096]{3,2,1,0:T(8,128)(2,1)}, u32[]{:S(2)}) copy-start(bf16[1,1,8,4096]{3,2,1,0:T(8,128)(2,1)} %param.13) | copy-start | bytes 196612
  10.8 6.5 %copy-start.3 = (s32[8,128]{1,0:T(8,128)S(1)}, s32[8,128]{1,0:T(8,128)}, u32[]{:S(2)}) copy-start(s32[8,128]{1,0:T(8,128)} %signs_ref.1) | copy-start | bytes 12292
  10.8 6.5 %copy-start.4 = (s32[1,1,8]{2,1,0:T(1,128)S(1)}, s32[1,1,8]{2,1,0:T(1,128)}, u32[]{:S(2)}) copy-start(s32[1,1,8]{2,1,0:T(1,128)} %lengths_ref.1) | copy-start | bytes 100
  12.5 7.2 %collective-permute-start.6 = (f32[32,256]{1,0:T(8,128)S(1)}, f32[32,256]{1,0:T(8,128)S(1)}, u32[]{:S(2)}, u32[]{:S(2)}) collective-permute-start(f32[32,256]{1,0:T(8,128)S(1)} %get-tuple-element.18.refs_0_), channel_id=1, source_target_pairs={{0,4},{4,8},{8,12},{12,0},{1,5},{5,9},{9,13},{13,1},{2,6},{6,10},{... | collective-permute-start | bytes 98312 | tf_op jit(solution)/shard_map/ppermute | solution.py:376
  14.5 5.5 %collective-permute-start.5 = (f32[32,256]{1,0:T(8,128)S(1)}, f32[32,256]{1,0:T(8,128)S(1)}, u32[]{:S(2)}, u32[]{:S(2)}) collective-permute-start(f32[32,256]{1,0:T(8,128)S(1)} %get-tuple-element.18.refs_0_), channel_id=1, source_target_pairs={{0,8},{4,12},{8,0},{12,4},{1,9},{5,13},{9,1},{13,5},{2,10},{6,14},... | collective-permute-start | bytes 98312 | tf_op jit(solution)/shard_map/ppermute | solution.py:376
  15.6 4.4 %collective-permute-start.4 = (f32[32,256]{1,0:T(8,128)S(1)}, f32[32,256]{1,0:T(8,128)S(1)}, u32[]{:S(2)}, u32[]{:S(2)}) collective-permute-start(f32[32,256]{1,0:T(8,128)S(1)} %get-tuple-element.18.refs_0_), channel_id=1, source_target_pairs={{0,12},{4,0},{8,4},{12,8},{1,13},{5,1},{9,5},{13,9},{2,14},{6,2},{... | collective-permute-start | bytes 98312 | tf_op jit(solution)/shard_map/ppermute | solution.py:376
  20.4 5.9 %collective-permute-start.8 = (bf16[8,4096]{1,0:T(8,128)(2,1)S(1)}, bf16[8,4096]{1,0:T(8,128)(2,1)S(1)}, u32[]{:S(2)}, u32[]{:S(2)}) collective-permute-start(bf16[8,4096]{1,0:T(8,128)(2,1)S(1)} %get-tuple-element.24), channel_id=1, source_target_pairs={{0,8},{4,12},{8,0},{12,4},{1,9},{5,13},{9,1},{13,5},{2,10},{6,14},... | collective-permute-start | bytes 196616 | tf_op jit(solution)/shard_map/ppermute | solution.py:371
  21.7 3.7 %collective-permute-start.7 = (f32[16,128]{1,0:T(8,128)S(1)}, f32[16,128]{1,0:T(8,128)S(1)}, u32[]{:S(2)}, u32[]{:S(2)}) collective-permute-start(f32[16,128]{1,0:T(8,128)S(1)} %get-tuple-element.21.stats_ref), channel_id=1, source_target_pairs={{0,2},{2,0},{1,3},{3,1},{4,6},{6,4},{5,7},{7,5},{8,10},{10,8},{9,1... | collective-permute-start | bytes 24584 | tf_op jit(solution)/shard_map/ppermute | solution.py:371
  26.3 4.3 %collective-permute-start.9 = (bf16[8,4096]{1,0:T(8,128)(2,1)S(1)}, bf16[8,4096]{1,0:T(8,128)(2,1)S(1)}, u32[]{:S(2)}, u32[]{:S(2)}) collective-permute-start(bf16[8,4096]{1,0:T(8,128)(2,1)S(1)} %merge.1.own_ref), channel_id=1, source_target_pairs={{0,2},{2,0},{1,3},{3,1},{4,6},{6,4},{5,7},{7,5},{8,10},{10,8},{9,1... | collective-permute-start | bytes 196616 | tf_op jit(solution)/shard_map/ppermute | solution.py:371

commit v15 on v13

--- a/solution.py
+++ b/solution.py
@@ -74,24 +74,23 @@
     )(in_vmem(tokens), in_vmem(weight))
 
 
-def message_kernel(query_ref, owners_ref, requests_ref, out_ref, query_buf, owners_buf, requests_buf, sems):
+def message_kernel(query_ref, owners_ref, requests_ref, out_ref, owners_buf, requests_buf, sems):
     requests, columns = query_ref.shape
     per_device = owners_ref.shape[1]
     copies = [
-        pltpu.make_async_copy(source, target, sems.at[i])
-        for i, (source, target) in enumerate(
-            ((query_ref, query_buf), (owners_ref, owners_buf), (requests_ref, requests_buf))
-        )
+        pltpu.make_async_copy(query_ref, out_ref.at[:, :columns], sems.at[0]),
+        pltpu.make_async_copy(owners_ref, owners_buf, sems.at[1]),
+        pltpu.make_async_copy(requests_ref, requests_buf, sems.at[2]),
     ]
     for copy in copies:
         copy.start()
-    for copy in copies:
-        copy.wait()
-    out_ref[:, :columns] = query_buf[...]
+    copies[1].wait()
+    copies[2].wait()
     code = (owners_buf[...] * requests + requests_buf[...]).astype(jnp.float32)
     spare = jnp.zeros((1, out_ref.shape[1] - columns - per_device), jnp.float32)
     code = jnp.concatenate([code, spare], axis=1)
     out_ref[:, columns:] = jnp.broadcast_to(code, (requests, code.shape[1])).astype(out_ref.dtype)
+    copies[0].wait()
 
 
 def make_message(query, owners, requests):
@@ -103,7 +102,6 @@
         out_specs=pl.BlockSpec(memory_space=pltpu.VMEM),
         out_shape=jax.ShapeDtypeStruct((count, columns + lanes), query.dtype),
         scratch_shapes=[
-            pltpu.VMEM(query.shape, query.dtype),
             pltpu.VMEM(owners.shape, owners.dtype),
             pltpu.VMEM(requests.shape, requests.dtype),
             pltpu.SemaphoreType.DMA((3,)),
@@ -237,9 +235,8 @@
             jnp.sum(jnp.where(here, scores[g * span : (g + 1) * span], 0.0), axis=0, keepdims=True)
             for g in range(group)
         ]
-        scores_ref[k * group : (k + 1) * group, :] = jnp.concatenate(lines, axis=0) * (
-            1.0 / math.sqrt(size)
-        )
+        lines = jnp.concatenate(lines, axis=0) * (1.0 / math.sqrt(size))
+        scores_ref[k * group : (k + 1) * group, :] = lines.astype(scores_ref.dtype)
 
 
 def partial_scores(heads, columns, keys, messages):
@@ -247,7 +244,7 @@
     return pl.pallas_call(
         functools.partial(score_kernel, heads, columns),
         out_shape=[
-            jax.ShapeDtypeStruct((columns * heads // width, tokens), jnp.float32),
+            jax.ShapeDtypeStruct((columns * heads // width, tokens), jnp.bfloat16),
             jax.ShapeDtypeStruct((8, tokens), jnp.int32),
         ],
         compiler_params=params(),
@@ -258,7 +255,7 @@
 
 def mix_kernel(heads, requests, code_ref, values_ref, near_ref, cache_stats_ref, *refs):
     score_refs, (own_ref, far_ref, new_stats_ref, stats_ref) = refs[:4], refs[4:]
-    own, after, across, before = [ref[...] for ref in score_refs]
+    own, after, across, before = [ref[...].astype(jnp.float32) for ref in score_refs]
     scores = (own + across) + (before + after)
     tokens, width = values_ref.shape
     size = width // heads
@@ -273,9 +270,9 @@
         weights = []
         for g in range(group):
             h = k * group + g
-            line = jnp.broadcast_to(scores[h : h + 1, :], (span, tokens))
-            top = jnp.max(jnp.where(here, line, LOWEST), axis=1, keepdims=True)
-            probs = jnp.where(here, jnp.exp(line - top), 0.0)
+            line = jnp.where(here, jnp.broadcast_to(scores[h : h + 1, :], (span, tokens)), LOWEST)
+            top = jnp.maximum(jnp.max(line, axis=1, keepdims=True), 0.1 * LOWEST)
+            probs = jnp.exp(line - top)
             total = jnp.sum(probs, axis=1, keepdims=True)
             weights.append(probs)
             tops = jnp.where(lane == h, top[:requests], tops)

time: 30.7 us -> 31.7 us (1.033)
  waiting for transfers between devices: 7.64 us -> 10.7 us
  starting transfers between devices: 16.3 us -> 14.3 us
    ppermute x7, waiting for transfers between devices: 6.26 us -> 8.32 us  [from_partner(): return lax.ppermute(x, axis, [(i, i ^ distance) for i in range(count)])]
    ppermute x7, starting transfers between devices: 11.8 us -> 10.6 us  [from_partner(): return lax.ppermute(x, axis, [(i, i ^ distance) for i in range(count)])]
    ppermute x3, waiting for transfers between devices: 1.38 us -> 2.34 us  [from_behind(): lax.ppermute(x, axis, [(i, (i + distance) % count) for i in range(count)])]
    ppermute x3, starting transfers between devices: 4.52 us -> 3.66 us  [from_behind(): lax.ppermute(x, axis, [(i, (i + distance) % count) for i in range(count)])]
  transfers between devices with their start and end apart: 10 -> 10, of which waited for: 4 -> 7; matrix products, arithmetic and copies ran while one was open for 0% -> 0% of each run, Pallas kernels for 14% -> 14%
where the time goes in v15:
time: 31.7 us; the launch traced here: 31.5 us
  starting transfers between devices  14.3 us (45%)
  waiting for transfers between devices  10.7 us (34%)
  Pallas kernels  6.48 us (20%)
    ppermute x7, starting transfers between devices, from_partner(): return lax.ppermute(x, axis, [(i, i ^ distance) for i in range(count)])  10.6 us
    ppermute x7, waiting for transfers between devices, from_partner(): return lax.ppermute(x, axis, [(i, i ^ distance) for i in range(count)])  8.32 us
    ppermute x3, starting transfers between devices, from_behind(): lax.ppermute(x, axis, [(i, (i + distance) % count) for i in range(count)])  3.66 us
    ppermute x3, waiting for transfers between devices, from_behind(): lax.ppermute(x, axis, [(i, (i + distance) % count) for i in range(count)])  2.34 us
    pallas_call x1, Pallas kernels, project(): pl.pallas_call(project_kernel, in_specs=[vmem] * 2, out_specs=[vmem] * 2,...  2.32 us
    pallas_call x1, Pallas kernels, cache_part(): pl.pallas_call(cache_kernel, in_specs=[pl.BlockSpec(memory_space=pltpu.SM...  1.6 us
    pallas_call x1, Pallas kernels, make_message(): pl.pallas_call(message_kernel, in_specs=[pl.BlockSpec(memory_space=pl.ANY...  1.01 us
    pallas_call x1, Pallas kernels, finish(): pl.pallas_call(finish_kernel, out_shape=jax.ShapeDtypeStruct(own.shape, o...  0.65 us
  transfers between devices with their start and end apart: 10, of which 7 were waited for; matrix products, arithmetic and copies ran while one was open for 0% of the time, Pallas kernels for 14%

profile of v15, /device:TPU:0, one launch (start us, length us, event | category | flops | bytes accessed | tf_op | source)
XLA Modules:
  0.0 31.5 jit_solution(11989765190068260402)
XLA Ops:
  0.0 1.0 %make_message.1.refs_0_ = bf16[8,4224]{1,0:T(8,128)(2,1)S(1)} custom-call(bf16[8,4096]{1,0:T(8,128)(2,1)} %bitcast.7, s32[1,64]{1,0:T(1,128)} %bitcast.9, s32[1,64]{1,0:T(1,128)} %requests_ref.1), custom_call_target="tpu_custom_call" | custom-call | flops 99999997952 | bytes 10000 | tf_op jit(solution)/shard_map/make_message/pallas_call | solution.py:99
  1.0 3.1 %collective-permute-start = (bf16[8,4224]{1,0:T(8,128)(2,1)S(1)}, bf16[8,4224]{1,0:T(8,128)(2,1)S(1)}, u32[]{:S(2)}, u32[]{:S(2)}) collective-permute-start(bf16[8,4224]{1,0:T(8,128)(2,1)S(1)} %make_message.1.refs_0_), channel_id=1, source_target_pairs={{0,4},{4,0},{8,12},{12,8},{1,5},{5,1},{9,13},{13,9},{2,6},{6,2},{1... | collective-permute-start | bytes 202760 | tf_op jit(solution)/shard_map/ppermute | solution.py:369
  4.1 2.6 %collective-permute-start.1 = (bf16[8,4224]{1,0:T(8,128)(2,1)S(1)}, bf16[8,4224]{1,0:T(8,128)(2,1)S(1)}, u32[]{:S(2)}, u32[]{:S(2)}) collective-permute-start(bf16[8,4224]{1,0:T(8,128)(2,1)S(1)} %make_message.1.refs_0_), channel_id=1, source_target_pairs={{0,8},{4,12},{8,0},{12,4},{1,9},{5,13},{9,1},{13,5},{2,10},{6,14},... | collective-permute-start | bytes 202760 | tf_op jit(solution)/shard_map/ppermute | solution.py:369
  6.7 2.3 %project.1 = (bf16[256,512]{1,0:T(8,128)(2,1)S(1)}, bf16[256,512]{1,0:T(8,128)(2,1)S(1)}) custom-call(bf16[256,4096]{1,0:T(8,128)(2,1)S(1)} %copy-done, bf16[4096,1024]{1,0:T(8,128)(2,1)S(1)} %bitcast.5), custom_call_target="tpu_custom_call" | custom-call | flops 2147483648 | bytes 10485760 | tf_op jit(solution)/shard_map/project/pallas_call | solution.py:62
  9.1 0.9 %collective-permute-start.3 = (bf16[256,512]{1,0:T(8,128)(2,1)S(1)}, bf16[256,512]{1,0:T(8,128)(2,1)S(1)}, u32[]{:S(2)}, u32[]{:S(2)}) collective-permute-start(bf16[256,512]{1,0:T(8,128)(2,1)S(1)} %get-tuple-element.20.values_ref), channel_id=1, source_target_pairs={{0,4},{4,0},{8,12},{12,8},{1,5},{5,1},{9,13},{13,9},{2,6},{6,2},{1... | collective-permute-start | bytes 786440 | tf_op jit(solution)/shard_map/ppermute | solution.py:369
  10.0 1.5 %collective-permute-done.1.refs_2_ = bf16[8,4224]{1,0:T(8,128)(2,1)S(1)} collective-permute-done((bf16[8,4224]{1,0:T(8,128)(2,1)S(1)}, bf16[8,4224]{1,0:T(8,128)(2,1)S(1)}, u32[]{:S(2)}, u32[]{:S(2)}) %collective-permute-start.1) | collective-permute-done | bytes 67616 | tf_op jit(solution)/shard_map/ppermute | solution.py:369
  11.5 1.4 %collective-permute-done.2.refs_3_ = bf16[8,4224]{1,0:T(8,128)(2,1)S(1)} collective-permute-done((bf16[8,4224]{1,0:T(8,128)(2,1)S(1)}, bf16[8,4224]{1,0:T(8,128)(2,1)S(1)}, u32[]{:S(2)}, u32[]{:S(2)}) %collective-permute-start.2) | collective-permute-done | bytes 67616 | tf_op jit(solution)/shard_map/ppermute | solution.py:369
  13.0 0.3 partial_scores.1
  13.3 1.8 %collective-permute-start.4 = (bf16[32,256]{1,0:T(8,128)(2,1)S(1)}, bf16[32,256]{1,0:T(8,128)(2,1)S(1)}, u32[]{:S(2)}, u32[]{:S(2)}) collective-permute-start(bf16[32,256]{1,0:T(8,128)(2,1)S(1)} %get-tuple-element.22.refs_0_), channel_id=1, source_target_pairs={{0,12},{4,0},{8,4},{12,8},{1,13},{5,1},{9,5},{13,9},{2,14},{6,2},{... | collective-permute-start | bytes 49160 | tf_op jit(solution)/shard_map/ppermute | solution.py:374
  15.1 0.2 collective-permute-start.5
  15.4 1.6 %collective-permute-start.6 = (bf16[32,256]{1,0:T(8,128)(2,1)S(1)}, bf16[32,256]{1,0:T(8,128)(2,1)S(1)}, u32[]{:S(2)}, u32[]{:S(2)}) collective-permute-start(bf16[32,256]{1,0:T(8,128)(2,1)S(1)} %get-tuple-element.22.refs_0_), channel_id=1, source_target_pairs={{0,4},{4,8},{8,12},{12,0},{1,5},{5,9},{9,13},{13,1},{2,6},{6,10},{... | collective-permute-start | bytes 49160 | tf_op jit(solution)/shard_map/ppermute | solution.py:374
  17.0 1.6 %cache_part.1 = (f32[8,4096]{1,0:T(8,128)S(1)}, f32[16,128]{1,0:T(8,128)S(1)}) custom-call(s32[1,1,8]{2,1,0:T(1,128)S(1)} %copy-done.4, bf16[8,4096]{1,0:T(8,128)(2,1)S(1)} %bitcast.8, bf16[8,128,1024]{2,1,0:T(8,128)(2,1)S(1)} %bitcast.6, s32[8,128]{1,0:T(8,128)S(1)} %copy-done.3), custom_call_target="tpu_custom_call" | custom-call | flops 16777216 | bytes 2097152 | tf_op jit(solution)/shard_map/cache_part/pallas_call | solution.py:188
  18.6 0.0 collective-permute-done.4.refs_1_
  18.6 1.2 %collective-permute-done.5.refs_2_ = bf16[32,256]{1,0:T(8,128)(2,1)S(1)} collective-permute-done((bf16[32,256]{1,0:T(8,128)(2,1)S(1)}, bf16[32,256]{1,0:T(8,128)(2,1)S(1)}, u32[]{:S(2)}, u32[]{:S(2)}) %collective-permute-start.5) | collective-permute-done | bytes 16416 | tf_op jit(solution)/shard_map/ppermute | solution.py:374
  19.8 1.1 %collective-permute-done.6.refs_3_ = bf16[32,256]{1,0:T(8,128)(2,1)S(1)} collective-permute-done((bf16[32,256]{1,0:T(8,128)(2,1)S(1)}, bf16[32,256]{1,0:T(8,128)(2,1)S(1)}, u32[]{:S(2)}, u32[]{:S(2)}) %collective-permute-start.6) | collective-permute-done | bytes 16416 | tf_op jit(solution)/shard_map/ppermute | solution.py:374
  20.9 0.4 %mix.1 = (f32[8,4096]{1,0:T(8,128)S(1)}, bf16[8,4096]{1,0:T(8,128)(2,1)S(1)}, f32[8,128]{1,0:T(8,128)S(1)}, f32[16,128]{1,0:T(8,128)S(1)}) custom-call(s32[8,256]{1,0:T(8,128)S(1)} %get-tuple-element.19.code_ref, bf16[256,512]{1,0:T(8,128)(2,1)S(1)} %get-tuple-element.20.values_ref, bf16[256,512]{1,0:T(8,128)(2,1)S(1)} %collective-permute-done.3.near_ref, ...), custom_call_target="tpu_custom_call" | custom-call | tf_op jit(solution)/shard_map/mix/pallas_call | solution.py:301
  21.3 1.0 %collective-permute-start.8 = (bf16[8,4096]{1,0:T(8,128)(2,1)S(1)}, bf16[8,4096]{1,0:T(8,128)(2,1)S(1)}, u32[]{:S(2)}, u32[]{:S(2)}) collective-permute-start(bf16[8,4096]{1,0:T(8,128)(2,1)S(1)} %get-tuple-element.28), channel_id=1, source_target_pairs={{0,8},{4,12},{8,0},{12,4},{1,9},{5,13},{9,1},{13,5},{2,10},{6,14},... | collective-permute-start | bytes 196616 | tf_op jit(solution)/shard_map/ppermute | solution.py:369
  22.3 1.5 %collective-permute-start.7 = (f32[16,128]{1,0:T(8,128)S(1)}, f32[16,128]{1,0:T(8,128)S(1)}, u32[]{:S(2)}, u32[]{:S(2)}) collective-permute-start(f32[16,128]{1,0:T(8,128)S(1)} %get-tuple-element.25.stats_ref), channel_id=1, source_target_pairs={{0,2},{2,0},{1,3},{3,1},{4,6},{6,4},{5,7},{7,5},{8,10},{10,8},{9,1... | collective-permute-start | bytes 24584 | tf_op jit(solution)/shard_map/ppermute | solution.py:369
  23.7 2.2 %collective-permute-done.7.other_ref = f32[16,128]{1,0:T(8,128)S(1)} collective-permute-done((f32[16,128]{1,0:T(8,128)S(1)}, f32[16,128]{1,0:T(8,128)S(1)}, u32[]{:S(2)}, u32[]{:S(2)}) %collective-permute-start.7) | collective-permute-done | bytes 8224 | tf_op jit(solution)/shard_map/ppermute | solution.py:369
  25.9 0.2 weigh.1
  26.1 0.4 %collective-permute-done.8.far_ref = bf16[8,4096]{1,0:T(8,128)(2,1)S(1)} collective-permute-done((bf16[8,4096]{1,0:T(8,128)(2,1)S(1)}, bf16[8,4096]{1,0:T(8,128)(2,1)S(1)}, u32[]{:S(2)}, u32[]{:S(2)}) %collective-permute-start.8) | collective-permute-done | bytes 65568 | tf_op jit(solution)/shard_map/ppermute | solution.py:369
  26.6 1.6 %collective-permute-start.9 = (bf16[8,4096]{1,0:T(8,128)(2,1)S(1)}, bf16[8,4096]{1,0:T(8,128)(2,1)S(1)}, u32[]{:S(2)}, u32[]{:S(2)}) collective-permute-start(bf16[8,4096]{1,0:T(8,128)(2,1)S(1)} %merge.1.own_ref), channel_id=1, source_target_pairs={{0,2},{2,0},{1,3},{3,1},{4,6},{6,4},{5,7},{7,5},{8,10},{10,8},{9,1... | collective-permute-start | bytes 196616 | tf_op jit(solution)/shard_map/ppermute | solution.py:369
  28.1 2.8 %collective-permute-done.9.other_ref = bf16[8,4096]{1,0:T(8,128)(2,1)S(1)} collective-permute-done((bf16[8,4096]{1,0:T(8,128)(2,1)S(1)}, bf16[8,4096]{1,0:T(8,128)(2,1)S(1)}, u32[]{:S(2)}, u32[]{:S(2)}) %collective-permute-start.9) | collective-permute-done | bytes 65568 | tf_op jit(solution)/shard_map/ppermute | solution.py:369
  30.9 0.6 %finish.1 = bf16[8,4096]{1,0:T(8,128)(2,1)} custom-call(bf16[8,4096]{1,0:T(8,128)(2,1)S(1)} %merge.1.own_ref, bf16[8,4096]{1,0:T(8,128)(2,1)S(1)} %collective-permute-done.9.other_ref), custom_call_target="tpu_custom_call" | custom-call | tf_op jit(solution)/shard_map/finish/pallas_call | solution.py:359
  (19 shorter events, 0.1 us)
Async XLA Ops:
  0.0 6.7 %slice-start = ((s8[8388608]{0:T(1024)(128)(4,1)}), s8[4194304]{0:T(1024)(128)(4,1)S(1)}, s32[]{:S(2)}) async-start(s8[8388608]{0:T(1024)(128)(4,1)} %bitcast.4), calls=%async_computation | async-start | bytes 8388608
  0.0 6.7 %slice-start.1 = ((s8[8388608]{0:T(1024)(128)(4,1)}), s8[4194304]{0:T(1024)(128)(4,1)S(1)}, s32[]{:S(2)}) async-start(s8[8388608]{0:T(1024)(128)(4,1)} %bitcast.4), calls=%async_computation.1 | async-start | bytes 8388608
  0.0 6.7 %copy-start = (bf16[256,4096]{1,0:T(8,128)(2,1)S(1)}, bf16[256,4096]{1,0:T(8,128)(2,1)}, u32[]{:S(2)}) copy-start(bf16[256,4096]{1,0:T(8,128)(2,1)} %tokens_ref.1) | copy-start | bytes 6291460
  1.0 9.0 %collective-permute-start = (bf16[8,4224]{1,0:T(8,128)(2,1)S(1)}, bf16[8,4224]{1,0:T(8,128)(2,1)S(1)}, u32[]{:S(2)}, u32[]{:S(2)}) collective-permute-start(bf16[8,4224]{1,0:T(8,128)(2,1)S(1)} %make_message.1.refs_0_), channel_id=1, source_target_pairs={{0,4},{4,0},{8,12},{12,8},{1,5},{5,1},{9,13},{13,9},{2,6},{6,2},{1... | collective-permute-start | bytes 202760 | tf_op jit(solution)/shard_map/ppermute | solution.py:369
  4.1 7.4 %collective-permute-start.1 = (bf16[8,4224]{1,0:T(8,128)(2,1)S(1)}, bf16[8,4224]{1,0:T(8,128)(2,1)S(1)}, u32[]{:S(2)}, u32[]{:S(2)}) collective-permute-start(bf16[8,4224]{1,0:T(8,128)(2,1)S(1)} %make_message.1.refs_0_), channel_id=1, source_target_pairs={{0,8},{4,12},{8,0},{12,4},{1,9},{5,13},{9,1},{13,5},{2,10},{6,14},... | collective-permute-start | bytes 202760 | tf_op jit(solution)/shard_map/ppermute | solution.py:369
  6.7 6.2 %collective-permute-start.2 = (bf16[8,4224]{1,0:T(8,128)(2,1)S(1)}, bf16[8,4224]{1,0:T(8,128)(2,1)S(1)}, u32[]{:S(2)}, u32[]{:S(2)}) collective-permute-start(bf16[8,4224]{1,0:T(8,128)(2,1)S(1)} %make_message.1.refs_0_), channel_id=1, source_target_pairs={{0,12},{4,8},{8,4},{12,0},{1,13},{5,9},{9,5},{13,1},{2,14},{6,10},... | collective-permute-start | bytes 202760 | tf_op jit(solution)/shard_map/ppermute | solution.py:369
  9.1 11.8 %collective-permute-start.3 = (bf16[256,512]{1,0:T(8,128)(2,1)S(1)}, bf16[256,512]{1,0:T(8,128)(2,1)S(1)}, u32[]{:S(2)}, u32[]{:S(2)}) collective-permute-start(bf16[256,512]{1,0:T(8,128)(2,1)S(1)} %get-tuple-element.20.values_ref), channel_id=1, source_target_pairs={{0,4},{4,0},{8,12},{12,8},{1,5},{5,1},{9,13},{13,9},{2,6},{6,2},{1... | collective-permute-start | bytes 786440 | tf_op jit(solution)/shard_map/ppermute | solution.py:369
  13.0 4.0 %copy-start.1 = (bf16[1,1,8,128,1024]{4,3,2,1,0:T(8,128)(2,1)S(1)}, bf16[1,1,8,128,1024]{4,3,2,1,0:T(8,128)(2,1)}, u32[]{:S(2)}) copy-start(bf16[1,1,8,128,1024]{4,3,2,1,0:T(8,128)(2,1)} %param.14) | copy-start | bytes 6291460
  13.0 4.0 %copy-start.2 = (bf16[1,1,8,4096]{3,2,1,0:T(8,128)(2,1)S(1)}, bf16[1,1,8,4096]{3,2,1,0:T(8,128)(2,1)}, u32[]{:S(2)}) copy-start(bf16[1,1,8,4096]{3,2,1,0:T(8,128)(2,1)} %param.13) | copy-start | bytes 196612
  13.0 4.0 %copy-start.3 = (s32[8,128]{1,0:T(8,128)S(1)}, s32[8,128]{1,0:T(8,128)}, u32[]{:S(2)}) copy-start(s32[8,128]{1,0:T(8,128)} %signs_ref.1) | copy-start | bytes 12292
  13.0 4.0 %copy-start.4 = (s32[1,1,8]{2,1,0:T(1,128)S(1)}, s32[1,1,8]{2,1,0:T(1,128)}, u32[]{:S(2)}) copy-start(s32[1,1,8]{2,1,0:T(1,128)} %lengths_ref.1) | copy-start | bytes 100
  13.3 5.3 %collective-permute-start.4 = (bf16[32,256]{1,0:T(8,128)(2,1)S(1)}, bf16[32,256]{1,0:T(8,128)(2,1)S(1)}, u32[]{:S(2)}, u32[]{:S(2)}) collective-permute-start(bf16[32,256]{1,0:T(8,128)(2,1)S(1)} %get-tuple-element.22.refs_0_), channel_id=1, source_target_pairs={{0,12},{4,0},{8,4},{12,8},{1,13},{5,1},{9,5},{13,9},{2,14},{6,2},{... | collective-permute-start | bytes 49160 | tf_op jit(solution)/shard_map/ppermute | solution.py:374
  15.1 4.6 %collective-permute-start.5 = (bf16[32,256]{1,0:T(8,128)(2,1)S(1)}, bf16[32,256]{1,0:T(8,128)(2,1)S(1)}, u32[]{:S(2)}, u32[]{:S(2)}) collective-permute-start(bf16[32,256]{1,0:T(8,128)(2,1)S(1)} %get-tuple-element.22.refs_0_), channel_id=1, source_target_pairs={{0,8},{4,12},{8,0},{12,4},{1,9},{5,13},{9,1},{13,5},{2,10},{6,14},... | collective-permute-start | bytes 49160 | tf_op jit(solution)/shard_map/ppermute | solution.py:374
  15.4 5.5 %collective-permute-start.6 = (bf16[32,256]{1,0:T(8,128)(2,1)S(1)}, bf16[32,256]{1,0:T(8,128)(2,1)S(1)}, u32[]{:S(2)}, u32[]{:S(2)}) collective-permute-start(bf16[32,256]{1,0:T(8,128)(2,1)S(1)} %get-tuple-element.22.refs_0_), channel_id=1, source_target_pairs={{0,4},{4,8},{8,12},{12,0},{1,5},{5,9},{9,13},{13,1},{2,6},{6,10},{... | collective-permute-start | bytes 49160 | tf_op jit(solution)/shard_map/ppermute | solution.py:374
  21.3 5.2 %collective-permute-start.8 = (bf16[8,4096]{1,0:T(8,128)(2,1)S(1)}, bf16[8,4096]{1,0:T(8,128)(2,1)S(1)}, u32[]{:S(2)}, u32[]{:S(2)}) collective-permute-start(bf16[8,4096]{1,0:T(8,128)(2,1)S(1)} %get-tuple-element.28), channel_id=1, source_target_pairs={{0,8},{4,12},{8,0},{12,4},{1,9},{5,13},{9,1},{13,5},{2,10},{6,14},... | collective-permute-start | bytes 196616 | tf_op jit(solution)/shard_map/ppermute | solution.py:369
  22.3 3.7 %collective-permute-start.7 = (f32[16,128]{1,0:T(8,128)S(1)}, f32[16,128]{1,0:T(8,128)S(1)}, u32[]{:S(2)}, u32[]{:S(2)}) collective-permute-start(f32[16,128]{1,0:T(8,128)S(1)} %get-tuple-element.25.stats_ref), channel_id=1, source_target_pairs={{0,2},{2,0},{1,3},{3,1},{4,6},{6,4},{5,7},{7,5},{8,10},{10,8},{9,1... | collective-permute-start | bytes 24584 | tf_op jit(solution)/shard_map/ppermute | solution.py:369
  26.6 4.3 %collective-permute-start.9 = (bf16[8,4096]{1,0:T(8,128)(2,1)S(1)}, bf16[8,4096]{1,0:T(8,128)(2,1)S(1)}, u32[]{:S(2)}, u32[]{:S(2)}) collective-permute-start(bf16[8,4096]{1,0:T(8,128)(2,1)S(1)} %merge.1.own_ref), channel_id=1, source_target_pairs={{0,2},{2,0},{1,3},{3,1},{4,6},{6,4},{5,7},{7,5},{8,10},{10,8},{9,1... | collective-permute-start | bytes 196616 | tf_op jit(solution)/shard_map/ppermute | solution.py:369

commit v16 on v15

--- a/solution.py
+++ b/solution.py
@@ -35,8 +35,8 @@
     return (1 - 2 * (parity & 1)).astype(jnp.float32).astype(jnp.bfloat16)
 
 
-QUERY_ORDER = (1, 2, 3)
-SCORE_ORDER = (3, 2, 1)
+QUERY_ORDER = (3, 2, 1)
+SCORE_ORDER = (1, 2, 3)
 
 
 def arranged(blocks, order):
@@ -255,7 +255,7 @@
 
 def mix_kernel(heads, requests, code_ref, values_ref, near_ref, cache_stats_ref, *refs):
     score_refs, (own_ref, far_ref, new_stats_ref, stats_ref) = refs[:4], refs[4:]
-    own, after, across, before = [ref[...].astype(jnp.float32) for ref in score_refs]
+    own, before, across, after = [ref[...].astype(jnp.float32) for ref in score_refs]
     scores = (own + across) + (before + after)
     tokens, width = values_ref.shape
     size = width // heads

time: 31.7 us -> 30.1 us (0.950)
  waiting for transfers between devices: 10.7 us -> 7.4 us
  starting transfers between devices: 14.3 us -> 16 us
    ppermute x7, waiting for transfers between devices: 8.32 us -> 6.55 us  [from_partner(): return lax.ppermute(x, axis, [(i, i ^ distance) for i in range(count)])]
    ppermute x3, waiting for transfers between devices: 2.34 us -> 0.85 us  [from_behind(): lax.ppermute(x, axis, [(i, (i + distance) % count) for i in range(count)])]
    ppermute x3, starting transfers between devices: 3.66 us -> 4.52 us  [from_behind(): lax.ppermute(x, axis, [(i, (i + distance) % count) for i in range(count)])]
    ppermute x7, starting transfers between devices: 10.6 us -> 11.5 us  [from_partner(): return lax.ppermute(x, axis, [(i, i ^ distance) for i in range(count)])]
  transfers between devices with their start and end apart: 10 -> 10, of which waited for: 7 -> 6; matrix products, arithmetic and copies ran while one was open for 0% -> 0% of each run, Pallas kernels for 14% -> 15%
where the time goes in v16:
time: 30.1 us; the launch traced here: 30 us
  starting transfers between devices  16 us (53%)
  waiting for transfers between devices  7.4 us (25%)
  Pallas kernels  6.47 us (21%)
    ppermute x7, starting transfers between devices, from_partner(): return lax.ppermute(x, axis, [(i, i ^ distance) for i in range(count)])  11.5 us
    ppermute x7, waiting for transfers between devices, from_partner(): return lax.ppermute(x, axis, [(i, i ^ distance) for i in range(count)])  6.55 us
    ppermute x3, starting transfers between devices, from_behind(): lax.ppermute(x, axis, [(i, (i + distance) % count) for i in range(count)])  4.52 us
    pallas_call x1, Pallas kernels, project(): pl.pallas_call(project_kernel, in_specs=[vmem] * 2, out_specs=[vmem] * 2,...  2.32 us
    pallas_call x1, Pallas kernels, cache_part(): pl.pallas_call(cache_kernel, in_specs=[pl.BlockSpec(memory_space=pltpu.SM...  1.6 us
    pallas_call x1, Pallas kernels, make_message(): pl.pallas_call(message_kernel, in_specs=[pl.BlockSpec(memory_space=pl.ANY...  1.01 us
    ppermute x3, waiting for transfers between devices, from_behind(): lax.ppermute(x, axis, [(i, (i + distance) % count) for i in range(count)])  0.85 us
    pallas_call x1, Pallas kernels, finish(): pl.pallas_call(finish_kernel, out_shape=jax.ShapeDtypeStruct(own.shape, o...  0.65 us
  transfers between devices with their start and end apart: 10, of which 6 were waited for; matrix products, arithmetic and copies ran while one was open for 0% of the time, Pallas kernels for 15%

profile of v16, /device:TPU:0, one launch (start us, length us, event | category | flops | bytes accessed | tf_op | source)
XLA Modules:
  0.0 30.0 jit_solution(7483718044823757095)
XLA Ops:
  0.0 1.0 %make_message.1.refs_0_ = bf16[8,4224]{1,0:T(8,128)(2,1)S(1)} custom-call(bf16[8,4096]{1,0:T(8,128)(2,1)} %bitcast.7, s32[1,64]{1,0:T(1,128)} %bitcast.9, s32[1,64]{1,0:T(1,128)} %requests_ref.1), custom_call_target="tpu_custom_call" | custom-call | flops 99999997952 | bytes 10000 | tf_op jit(solution)/shard_map/make_message/pallas_call | solution.py:99
  1.0 5.1 %collective-permute-start = (bf16[8,4224]{1,0:T(8,128)(2,1)S(1)}, bf16[8,4224]{1,0:T(8,128)(2,1)S(1)}, u32[]{:S(2)}, u32[]{:S(2)}) collective-permute-start(bf16[8,4224]{1,0:T(8,128)(2,1)S(1)} %make_message.1.refs_0_), channel_id=1, source_target_pairs={{0,12},{4,8},{8,4},{12,0},{1,13},{5,9},{9,5},{13,1},{2,14},{6,10},... | collective-permute-start | bytes 202760 | tf_op jit(solution)/shard_map/ppermute | solution.py:369
  6.2 0.0 collective-permute-start.1
  6.2 0.6 %collective-permute-start.2 = (bf16[8,4224]{1,0:T(8,128)(2,1)S(1)}, bf16[8,4224]{1,0:T(8,128)(2,1)S(1)}, u32[]{:S(2)}, u32[]{:S(2)}) collective-permute-start(bf16[8,4224]{1,0:T(8,128)(2,1)S(1)} %make_message.1.refs_0_), channel_id=1, source_target_pairs={{0,4},{4,0},{8,12},{12,8},{1,5},{5,1},{9,13},{13,9},{2,6},{6,2},{1... | collective-permute-start | bytes 202760 | tf_op jit(solution)/shard_map/ppermute | solution.py:369
  6.8 2.3 %project.1 = (bf16[256,512]{1,0:T(8,128)(2,1)S(1)}, bf16[256,512]{1,0:T(8,128)(2,1)S(1)}) custom-call(bf16[256,4096]{1,0:T(8,128)(2,1)S(1)} %copy-done, bf16[4096,1024]{1,0:T(8,128)(2,1)S(1)} %bitcast.5), custom_call_target="tpu_custom_call" | custom-call | flops 2147483648 | bytes 10485760 | tf_op jit(solution)/shard_map/project/pallas_call | solution.py:62
  9.1 1.5 %collective-permute-start.3 = (bf16[256,512]{1,0:T(8,128)(2,1)S(1)}, bf16[256,512]{1,0:T(8,128)(2,1)S(1)}, u32[]{:S(2)}, u32[]{:S(2)}) collective-permute-start(bf16[256,512]{1,0:T(8,128)(2,1)S(1)} %get-tuple-element.20.values_ref), channel_id=1, source_target_pairs={{0,4},{4,0},{8,12},{12,8},{1,5},{5,1},{9,13},{13,9},{2,6},{6,2},{1... | collective-permute-start | bytes 786440 | tf_op jit(solution)/shard_map/ppermute | solution.py:369
  10.6 1.4 %collective-permute-done.1.refs_2_ = bf16[8,4224]{1,0:T(8,128)(2,1)S(1)} collective-permute-done((bf16[8,4224]{1,0:T(8,128)(2,1)S(1)}, bf16[8,4224]{1,0:T(8,128)(2,1)S(1)}, u32[]{:S(2)}, u32[]{:S(2)}) %collective-permute-start.1) | collective-permute-done | bytes 67616 | tf_op jit(solution)/shard_map/ppermute | solution.py:369
  12.0 0.0 copy-start.4
  12.0 0.3 %partial_scores.1 = (bf16[32,256]{1,0:T(8,128)(2,1)S(1)}, s32[8,256]{1,0:T(8,128)S(1)}) custom-call(bf16[256,512]{1,0:T(8,128)(2,1)S(1)} %get-tuple-element.18.keys_ref, bf16[8,4224]{1,0:T(8,128)(2,1)S(1)} %make_message.1.refs_0_, bf16[8,4224]{1,0:T(8,128)(2,1)S(1)} %collective-permute-done.refs_1_, bf16[8,4224]{1,0:T(8,128)(2,1)S(1)} %collective-permute-done.1.refs_2_, ...), custom_call_target="tpu_custom_call" | custom-call | flops 99999997952 | bytes 10000 | tf_op jit(solution)/shard_map/partial_scores/pallas_call | solution.py:244
  12.3 1.5 %collective-permute-start.4 = (bf16[32,256]{1,0:T(8,128)(2,1)S(1)}, bf16[32,256]{1,0:T(8,128)(2,1)S(1)}, u32[]{:S(2)}, u32[]{:S(2)}) collective-permute-start(bf16[32,256]{1,0:T(8,128)(2,1)S(1)} %get-tuple-element.22.refs_0_), channel_id=1, source_target_pairs={{0,4},{4,8},{8,12},{12,0},{1,5},{5,9},{9,13},{13,1},{2,6},{6,10},{... | collective-permute-start | bytes 49160 | tf_op jit(solution)/shard_map/ppermute | solution.py:374
  13.8 1.8 %collective-permute-start.5 = (bf16[32,256]{1,0:T(8,128)(2,1)S(1)}, bf16[32,256]{1,0:T(8,128)(2,1)S(1)}, u32[]{:S(2)}, u32[]{:S(2)}) collective-permute-start(bf16[32,256]{1,0:T(8,128)(2,1)S(1)} %get-tuple-element.22.refs_0_), channel_id=1, source_target_pairs={{0,8},{4,12},{8,0},{12,4},{1,9},{5,13},{9,1},{13,5},{2,10},{6,14},... | collective-permute-start | bytes 49160 | tf_op jit(solution)/shard_map/ppermute | solution.py:374
  15.6 1.3 %collective-permute-start.6 = (bf16[32,256]{1,0:T(8,128)(2,1)S(1)}, bf16[32,256]{1,0:T(8,128)(2,1)S(1)}, u32[]{:S(2)}, u32[]{:S(2)}) collective-permute-start(bf16[32,256]{1,0:T(8,128)(2,1)S(1)} %get-tuple-element.22.refs_0_), channel_id=1, source_target_pairs={{0,12},{4,0},{8,4},{12,8},{1,13},{5,1},{9,5},{13,9},{2,14},{6,2},{... | collective-permute-start | bytes 49160 | tf_op jit(solution)/shard_map/ppermute | solution.py:374
  16.9 1.6 %cache_part.1 = (f32[8,4096]{1,0:T(8,128)S(1)}, f32[16,128]{1,0:T(8,128)S(1)}) custom-call(s32[1,1,8]{2,1,0:T(1,128)S(1)} %copy-done.4, bf16[8,4096]{1,0:T(8,128)(2,1)S(1)} %bitcast.8, bf16[8,128,1024]{2,1,0:T(8,128)(2,1)S(1)} %bitcast.6, s32[8,128]{1,0:T(8,128)S(1)} %copy-done.3), custom_call_target="tpu_custom_call" | custom-call | flops 16777216 | bytes 2097152 | tf_op jit(solution)/shard_map/cache_part/pallas_call | solution.py:188
  18.5 0.6 %collective-permute-done.4.refs_1_ = bf16[32,256]{1,0:T(8,128)(2,1)S(1)} collective-permute-done((bf16[32,256]{1,0:T(8,128)(2,1)S(1)}, bf16[32,256]{1,0:T(8,128)(2,1)S(1)}, u32[]{:S(2)}, u32[]{:S(2)}) %collective-permute-start.4) | collective-permute-done | bytes 16416 | tf_op jit(solution)/shard_map/ppermute | solution.py:374
  19.1 0.2 collective-permute-done.6.refs_3_
  19.3 0.4 %mix.1 = (f32[8,4096]{1,0:T(8,128)S(1)}, bf16[8,4096]{1,0:T(8,128)(2,1)S(1)}, f32[8,128]{1,0:T(8,128)S(1)}, f32[16,128]{1,0:T(8,128)S(1)}) custom-call(s32[8,256]{1,0:T(8,128)S(1)} %get-tuple-element.19.code_ref, bf16[256,512]{1,0:T(8,128)(2,1)S(1)} %get-tuple-element.20.values_ref, bf16[256,512]{1,0:T(8,128)(2,1)S(1)} %collective-permute-done.3.near_ref, ...), custom_call_target="tpu_custom_call" | custom-call | tf_op jit(solution)/shard_map/mix/pallas_call | solution.py:301
  19.7 1.2 %collective-permute-start.8 = (bf16[8,4096]{1,0:T(8,128)(2,1)S(1)}, bf16[8,4096]{1,0:T(8,128)(2,1)S(1)}, u32[]{:S(2)}, u32[]{:S(2)}) collective-permute-start(bf16[8,4096]{1,0:T(8,128)(2,1)S(1)} %get-tuple-element.28), channel_id=1, source_target_pairs={{0,8},{4,12},{8,0},{12,4},{1,9},{5,13},{9,1},{13,5},{2,10},{6,14},... | collective-permute-start | bytes 196616 | tf_op jit(solution)/shard_map/ppermute | solution.py:369
  20.9 1.5 %collective-permute-start.7 = (f32[16,128]{1,0:T(8,128)S(1)}, f32[16,128]{1,0:T(8,128)S(1)}, u32[]{:S(2)}, u32[]{:S(2)}) collective-permute-start(f32[16,128]{1,0:T(8,128)S(1)} %get-tuple-element.25.stats_ref), channel_id=1, source_target_pairs={{0,2},{2,0},{1,3},{3,1},{4,6},{6,4},{5,7},{7,5},{8,10},{10,8},{9,1... | collective-permute-start | bytes 24584 | tf_op jit(solution)/shard_map/ppermute | solution.py:369
  22.4 2.2 %collective-permute-done.7.other_ref = f32[16,128]{1,0:T(8,128)S(1)} collective-permute-done((f32[16,128]{1,0:T(8,128)S(1)}, f32[16,128]{1,0:T(8,128)S(1)}, u32[]{:S(2)}, u32[]{:S(2)}) %collective-permute-start.7) | collective-permute-done | bytes 8224 | tf_op jit(solution)/shard_map/ppermute | solution.py:369
  24.6 0.2 weigh.1
  24.7 0.2 collective-permute-done.8.far_ref
  25.0 1.6 %collective-permute-start.9 = (bf16[8,4096]{1,0:T(8,128)(2,1)S(1)}, bf16[8,4096]{1,0:T(8,128)(2,1)S(1)}, u32[]{:S(2)}, u32[]{:S(2)}) collective-permute-start(bf16[8,4096]{1,0:T(8,128)(2,1)S(1)} %merge.1.own_ref), channel_id=1, source_target_pairs={{0,2},{2,0},{1,3},{3,1},{4,6},{6,4},{5,7},{7,5},{8,10},{10,8},{9,1... | collective-permute-start | bytes 196616 | tf_op jit(solution)/shard_map/ppermute | solution.py:369
  26.5 2.8 %collective-permute-done.9.other_ref = bf16[8,4096]{1,0:T(8,128)(2,1)S(1)} collective-permute-done((bf16[8,4096]{1,0:T(8,128)(2,1)S(1)}, bf16[8,4096]{1,0:T(8,128)(2,1)S(1)}, u32[]{:S(2)}, u32[]{:S(2)}) %collective-permute-start.9) | collective-permute-done | bytes 65568 | tf_op jit(solution)/shard_map/ppermute | solution.py:369
  29.3 0.6 %finish.1 = bf16[8,4096]{1,0:T(8,128)(2,1)} custom-call(bf16[8,4096]{1,0:T(8,128)(2,1)S(1)} %merge.1.own_ref, bf16[8,4096]{1,0:T(8,128)(2,1)S(1)} %collective-permute-done.9.other_ref), custom_call_target="tpu_custom_call" | custom-call | tf_op jit(solution)/shard_map/finish/pallas_call | solution.py:359
  (19 shorter events, 0.1 us)
Async XLA Ops:
  0.0 6.8 %slice-start = ((s8[8388608]{0:T(1024)(128)(4,1)}), s8[4194304]{0:T(1024)(128)(4,1)S(1)}, s32[]{:S(2)}) async-start(s8[8388608]{0:T(1024)(128)(4,1)} %bitcast.4), calls=%async_computation | async-start | bytes 8388608
  0.0 6.8 %slice-start.1 = ((s8[8388608]{0:T(1024)(128)(4,1)}), s8[4194304]{0:T(1024)(128)(4,1)S(1)}, s32[]{:S(2)}) async-start(s8[8388608]{0:T(1024)(128)(4,1)} %bitcast.4), calls=%async_computation.1 | async-start | bytes 8388608
  0.0 6.8 %copy-start = (bf16[256,4096]{1,0:T(8,128)(2,1)S(1)}, bf16[256,4096]{1,0:T(8,128)(2,1)}, u32[]{:S(2)}) copy-start(bf16[256,4096]{1,0:T(8,128)(2,1)} %tokens_ref.1) | copy-start | bytes 6291460
  1.0 9.6 %collective-permute-start = (bf16[8,4224]{1,0:T(8,128)(2,1)S(1)}, bf16[8,4224]{1,0:T(8,128)(2,1)S(1)}, u32[]{:S(2)}, u32[]{:S(2)}) collective-permute-start(bf16[8,4224]{1,0:T(8,128)(2,1)S(1)} %make_message.1.refs_0_), channel_id=1, source_target_pairs={{0,12},{4,8},{8,4},{12,0},{1,13},{5,9},{9,5},{13,1},{2,14},{6,10},... | collective-permute-start | bytes 202760 | tf_op jit(solution)/shard_map/ppermute | solution.py:369
  6.2 5.8 %collective-permute-start.1 = (bf16[8,4224]{1,0:T(8,128)(2,1)S(1)}, bf16[8,4224]{1,0:T(8,128)(2,1)S(1)}, u32[]{:S(2)}, u32[]{:S(2)}) collective-permute-start(bf16[8,4224]{1,0:T(8,128)(2,1)S(1)} %make_message.1.refs_0_), channel_id=1, source_target_pairs={{0,8},{4,12},{8,0},{12,4},{1,9},{5,13},{9,1},{13,5},{2,10},{6,14},... | collective-permute-start | bytes 202760 | tf_op jit(solution)/shard_map/ppermute | solution.py:369
  6.2 5.8 %collective-permute-start.2 = (bf16[8,4224]{1,0:T(8,128)(2,1)S(1)}, bf16[8,4224]{1,0:T(8,128)(2,1)S(1)}, u32[]{:S(2)}, u32[]{:S(2)}) collective-permute-start(bf16[8,4224]{1,0:T(8,128)(2,1)S(1)} %make_message.1.refs_0_), channel_id=1, source_target_pairs={{0,4},{4,0},{8,12},{12,8},{1,5},{5,1},{9,13},{13,9},{2,6},{6,2},{1... | collective-permute-start | bytes 202760 | tf_op jit(solution)/shard_map/ppermute | solution.py:369
  9.1 10.2 %collective-permute-start.3 = (bf16[256,512]{1,0:T(8,128)(2,1)S(1)}, bf16[256,512]{1,0:T(8,128)(2,1)S(1)}, u32[]{:S(2)}, u32[]{:S(2)}) collective-permute-start(bf16[256,512]{1,0:T(8,128)(2,1)S(1)} %get-tuple-element.20.values_ref), channel_id=1, source_target_pairs={{0,4},{4,0},{8,12},{12,8},{1,5},{5,1},{9,13},{13,9},{2,6},{6,2},{1... | collective-permute-start | bytes 786440 | tf_op jit(solution)/shard_map/ppermute | solution.py:369
  12.0 4.9 %copy-start.1 = (bf16[1,1,8,128,1024]{4,3,2,1,0:T(8,128)(2,1)S(1)}, bf16[1,1,8,128,1024]{4,3,2,1,0:T(8,128)(2,1)}, u32[]{:S(2)}) copy-start(bf16[1,1,8,128,1024]{4,3,2,1,0:T(8,128)(2,1)} %param.14) | copy-start | bytes 6291460
  12.0 4.9 %copy-start.2 = (bf16[1,1,8,4096]{3,2,1,0:T(8,128)(2,1)S(1)}, bf16[1,1,8,4096]{3,2,1,0:T(8,128)(2,1)}, u32[]{:S(2)}) copy-start(bf16[1,1,8,4096]{3,2,1,0:T(8,128)(2,1)} %param.13) | copy-start | bytes 196612
  12.0 4.9 %copy-start.3 = (s32[8,128]{1,0:T(8,128)S(1)}, s32[8,128]{1,0:T(8,128)}, u32[]{:S(2)}) copy-start(s32[8,128]{1,0:T(8,128)} %signs_ref.1) | copy-start | bytes 12292
  12.0 4.9 %copy-start.4 = (s32[1,1,8]{2,1,0:T(1,128)S(1)}, s32[1,1,8]{2,1,0:T(1,128)}, u32[]{:S(2)}) copy-start(s32[1,1,8]{2,1,0:T(1,128)} %lengths_ref.1) | copy-start | bytes 100
  12.3 6.8 %collective-permute-start.4 = (bf16[32,256]{1,0:T(8,128)(2,1)S(1)}, bf16[32,256]{1,0:T(8,128)(2,1)S(1)}, u32[]{:S(2)}, u32[]{:S(2)}) collective-permute-start(bf16[32,256]{1,0:T(8,128)(2,1)S(1)} %get-tuple-element.22.refs_0_), channel_id=1, source_target_pairs={{0,4},{4,8},{8,12},{12,0},{1,5},{5,9},{9,13},{13,1},{2,6},{6,10},{... | collective-permute-start | bytes 49160 | tf_op jit(solution)/shard_map/ppermute | solution.py:374
  13.8 5.3 %collective-permute-start.5 = (bf16[32,256]{1,0:T(8,128)(2,1)S(1)}, bf16[32,256]{1,0:T(8,128)(2,1)S(1)}, u32[]{:S(2)}, u32[]{:S(2)}) collective-permute-start(bf16[32,256]{1,0:T(8,128)(2,1)S(1)} %get-tuple-element.22.refs_0_), channel_id=1, source_target_pairs={{0,8},{4,12},{8,0},{12,4},{1,9},{5,13},{9,1},{13,5},{2,10},{6,14},... | collective-permute-start | bytes 49160 | tf_op jit(solution)/shard_map/ppermute | solution.py:374
  15.6 3.7 %collective-permute-start.6 = (bf16[32,256]{1,0:T(8,128)(2,1)S(1)}, bf16[32,256]{1,0:T(8,128)(2,1)S(1)}, u32[]{:S(2)}, u32[]{:S(2)}) collective-permute-start(bf16[32,256]{1,0:T(8,128)(2,1)S(1)} %get-tuple-element.22.refs_0_), channel_id=1, source_target_pairs={{0,12},{4,0},{8,4},{12,8},{1,13},{5,1},{9,5},{13,9},{2,14},{6,2},{... | collective-permute-start | bytes 49160 | tf_op jit(solution)/shard_map/ppermute | solution.py:374
  19.7 5.2 %collective-permute-start.8 = (bf16[8,4096]{1,0:T(8,128)(2,1)S(1)}, bf16[8,4096]{1,0:T(8,128)(2,1)S(1)}, u32[]{:S(2)}, u32[]{:S(2)}) collective-permute-start(bf16[8,4096]{1,0:T(8,128)(2,1)S(1)} %get-tuple-element.28), channel_id=1, source_target_pairs={{0,8},{4,12},{8,0},{12,4},{1,9},{5,13},{9,1},{13,5},{2,10},{6,14},... | collective-permute-start | bytes 196616 | tf_op jit(solution)/shard_map/ppermute | solution.py:369
  20.9 3.7 %collective-permute-start.7 = (f32[16,128]{1,0:T(8,128)S(1)}, f32[16,128]{1,0:T(8,128)S(1)}, u32[]{:S(2)}, u32[]{:S(2)}) collective-permute-start(f32[16,128]{1,0:T(8,128)S(1)} %get-tuple-element.25.stats_ref), channel_id=1, source_target_pairs={{0,2},{2,0},{1,3},{3,1},{4,6},{6,4},{5,7},{7,5},{8,10},{10,8},{9,1... | collective-permute-start | bytes 24584 | tf_op jit(solution)/shard_map/ppermute | solution.py:369
  25.0 4.3 %collective-permute-start.9 = (bf16[8,4096]{1,0:T(8,128)(2,1)S(1)}, bf16[8,4096]{1,0:T(8,128)(2,1)S(1)}, u32[]{:S(2)}, u32[]{:S(2)}) collective-permute-start(bf16[8,4096]{1,0:T(8,128)(2,1)S(1)} %merge.1.own_ref), channel_id=1, source_target_pairs={{0,2},{2,0},{1,3},{3,1},{4,6},{6,4},{5,7},{7,5},{8,10},{10,8},{9,1... | collective-permute-start | bytes 196616 | tf_op jit(solution)/shard_map/ppermute | solution.py:369

commit v17 on v15

--- a/solution.py
+++ b/solution.py
@@ -36,7 +36,14 @@
 
 
 QUERY_ORDER = (1, 2, 3)
-SCORE_ORDER = (3, 2, 1)
+SCORE_STEPS = (
+    (3, ((3, 0), (1, 2))),
+    (1, ((1, 0), (3, 2))),
+    (2, ((0, 2), (2, 0))),
+    (3, ((0, 3), (2, 1))),
+    (1, ((0, 1), (2, 3))),
+    (2, ((1, 3), (3, 1))),
+)
 
 
 def arranged(blocks, order):
@@ -254,9 +261,12 @@
 
 
 def mix_kernel(heads, requests, code_ref, values_ref, near_ref, cache_stats_ref, *refs):
-    score_refs, (own_ref, far_ref, new_stats_ref, stats_ref) = refs[:4], refs[4:]
-    own, after, across, before = [ref[...].astype(jnp.float32) for ref in score_refs]
-    scores = (own + across) + (before + after)
+    score_refs, (own_ref, far_ref, new_stats_ref, stats_ref) = refs[:-4], refs[-4:]
+    parts = [ref[...].astype(jnp.float32) for ref in score_refs]
+    by_xor = [parts[0]] + [
+        sum(part for part, (d, _) in zip(parts[:0:-1], SCORE_STEPS) if d == distance) for distance in (1, 2, 3)
+    ]
+    scores = (by_xor[0] + by_xor[2]) + (by_xor[1] + by_xor[3])
     tokens, width = values_ref.shape
     size = width // heads
     group = scores.shape[0] // heads
@@ -308,7 +318,7 @@
         ],
         compiler_params=params(),
         name="mix",
-    )(code, values, near_values, cache_stats, *arranged(scores, SCORE_ORDER))
+    )(code, values, near_values, cache_stats, scores[0], *scores[:0:-1])
 
 
 def weigh_kernel(cache_ref, own_ref, cache_stats_ref, new_stats_ref, stats_ref, other_ref, base_ref, factor_ref):
@@ -369,11 +379,6 @@
     return lax.ppermute(x, axis, [(i, i ^ distance) for i in range(count)])
 
 
-def from_behind(x, axis, distance):
-    count = lax.axis_size(axis)
-    return lax.ppermute(x, axis, [(i, (i + distance) % count) for i in range(count)])
-
-
 def on_device(tokens, kv_weight, owners, requests, signs, queries, kv_cache, lengths):
     seq_count = lax.axis_size("seq")
     heads = signs.shape[0] // 2
@@ -384,7 +389,7 @@
     keys, values = project(tokens, kv_weight)
     near_values = from_partner(values, "seq", 1)
     scores, code = partial_scores(heads, columns, keys, messages)
-    scores = [scores] + [from_behind(scores, "seq", d) for d in range(1, seq_count)]
+    scores = [scores] + [lax.ppermute(scores, "seq", pairs) for _, pairs in SCORE_STEPS]
     cache_mixed, cache_stats = cache_part(lengths, query, kv_cache[0, 0], signs)
     own, far, new_stats, stats = mix(heads, code, values, near_values, cache_stats, scores)
     far = from_partner(far, "seq", 2)

time: 31.7 us -> 36.6 us (1.15)
  starting transfers between devices: 14.3 us -> 22.6 us
  waiting for transfers between devices: 10.7 us -> 7.13 us
    ppermute x3 -> x6, starting transfers between devices: 3.66 us -> 11.7 us  [on_device(): lax.ppermute(scores, 'seq', pairs)]
    ppermute x3 -> x6, waiting for transfers between devices: 2.34 us -> 0.02 us  [on_device(): lax.ppermute(scores, 'seq', pairs)]
    ppermute x7, waiting for transfers between devices: 8.32 us -> 7.11 us  [from_partner(): return lax.ppermute(x, axis, [(i, i ^ distance) for i in range(count)])]
  transfers between devices with their start and end apart: 10 -> 13, of which waited for: 7 -> 4; matrix products, arithmetic and copies ran while one was open for 0% -> 0% of each run, Pallas kernels for 14% -> 12%
where the time goes in v17:
time: 36.6 us; the launch traced here: 36.4 us
  starting transfers between devices  22.6 us (62%)
  waiting for transfers between devices  7.13 us (19%)
  Pallas kernels  6.5 us (18%)
    ppermute x6, starting transfers between devices, on_device(): lax.ppermute(scores, 'seq', pairs)  11.7 us
    ppermute x7, starting transfers between devices, from_partner(): return lax.ppermute(x, axis, [(i, i ^ distance) for i in range(count)])  10.9 us
    ppermute x7, waiting for transfers between devices, from_partner(): return lax.ppermute(x, axis, [(i, i ^ distance) for i in range(count)])  7.11 us
    pallas_call x1, Pallas kernels, project(): pl.pallas_call(project_kernel, in_specs=[vmem] * 2, out_specs=[vmem] * 2,...  2.32 us
    pallas_call x1, Pallas kernels, cache_part(): pl.pallas_call(cache_kernel, in_specs=[pl.BlockSpec(memory_space=pltpu.SM...  1.6 us
    pallas_call x1, Pallas kernels, make_message(): pl.pallas_call(message_kernel, in_specs=[pl.BlockSpec(memory_space=pl.ANY...  1.01 us
  transfers between devices with their start and end apart: 13, of which 4 were waited for; matrix products, arithmetic and copies ran while one was open for 0% of the time, Pallas kernels for 12%

profile of v17, /device:TPU:0, one launch (start us, length us, event | category | flops | bytes accessed | tf_op | source)
XLA Modules:
  0.0 36.4 jit_solution(15358800823963504795)
XLA Ops:
  0.0 1.0 %make_message.1.refs_0_ = bf16[8,4224]{1,0:T(8,128)(2,1)S(1)} custom-call(bf16[8,4096]{1,0:T(8,128)(2,1)} %bitcast.7, s32[1,64]{1,0:T(1,128)} %bitcast.9, s32[1,64]{1,0:T(1,128)} %requests_ref.1), custom_call_target="tpu_custom_call" | custom-call | flops 99999997952 | bytes 10000 | tf_op jit(solution)/shard_map/make_message/pallas_call | solution.py:106
  1.0 5.1 %collective-permute-start.2 = (bf16[8,4224]{1,0:T(8,128)(2,1)S(1)}, bf16[8,4224]{1,0:T(8,128)(2,1)S(1)}, u32[]{:S(2)}, u32[]{:S(2)}) collective-permute-start(bf16[8,4224]{1,0:T(8,128)(2,1)S(1)} %make_message.1.refs_0_), channel_id=1, source_target_pairs={{0,12},{4,8},{8,4},{12,0},{1,13},{5,9},{9,5},{13,1},{2,14},{6,10},... | collective-permute-start | bytes 202760 | tf_op jit(solution)/shard_map/ppermute | solution.py:379
  6.2 0.6 %collective-permute-start = (bf16[8,4224]{1,0:T(8,128)(2,1)S(1)}, bf16[8,4224]{1,0:T(8,128)(2,1)S(1)}, u32[]{:S(2)}, u32[]{:S(2)}) collective-permute-start(bf16[8,4224]{1,0:T(8,128)(2,1)S(1)} %make_message.1.refs_0_), channel_id=1, source_target_pairs={{0,4},{4,0},{8,12},{12,8},{1,5},{5,1},{9,13},{13,9},{2,6},{6,2},{1... | collective-permute-start | bytes 202760 | tf_op jit(solution)/shard_map/ppermute | solution.py:379
  6.8 2.3 %project.1 = (bf16[256,512]{1,0:T(8,128)(2,1)S(1)}, bf16[256,512]{1,0:T(8,128)(2,1)S(1)}) custom-call(bf16[256,4096]{1,0:T(8,128)(2,1)S(1)} %copy-done, bf16[4096,1024]{1,0:T(8,128)(2,1)S(1)} %bitcast.5), custom_call_target="tpu_custom_call" | custom-call | flops 2147483648 | bytes 10485760 | tf_op jit(solution)/shard_map/project/pallas_call | solution.py:69
  9.1 1.5 %collective-permute-start.3 = (bf16[256,512]{1,0:T(8,128)(2,1)S(1)}, bf16[256,512]{1,0:T(8,128)(2,1)S(1)}, u32[]{:S(2)}, u32[]{:S(2)}) collective-permute-start(bf16[256,512]{1,0:T(8,128)(2,1)S(1)} %get-tuple-element.20.values_ref), channel_id=1, source_target_pairs={{0,4},{4,0},{8,12},{12,8},{1,5},{5,1},{9,13},{13,9},{2,6},{6,2},{1... | collective-permute-start | bytes 786440 | tf_op jit(solution)/shard_map/ppermute | solution.py:379
  10.6 1.4 %collective-permute-done.1.refs_2_ = bf16[8,4224]{1,0:T(8,128)(2,1)S(1)} collective-permute-done((bf16[8,4224]{1,0:T(8,128)(2,1)S(1)}, bf16[8,4224]{1,0:T(8,128)(2,1)S(1)}, u32[]{:S(2)}, u32[]{:S(2)}) %collective-permute-start.1) | collective-permute-done | bytes 67616 | tf_op jit(solution)/shard_map/ppermute | solution.py:379
  12.0 0.0 copy-start.4
  12.0 0.3 partial_scores.1
  12.3 1.4 %collective-permute-start.9 = (bf16[32,256]{1,0:T(8,128)(2,1)S(1)}, bf16[32,256]{1,0:T(8,128)(2,1)S(1)}, u32[]{:S(2)}, u32[]{:S(2)}) collective-permute-start(bf16[32,256]{1,0:T(8,128)(2,1)S(1)} %get-tuple-element.22.refs_0_), channel_id=1, source_target_pairs={{12,0},{4,8},{13,1},{5,9},{14,2},{6,10},{15,3},{7,11},{28,16},{20,... | collective-permute-start | bytes 49160 | tf_op jit(solution)/shard_map/ppermute | solution.py:392
  13.8 1.3 %collective-permute-start.8 = (bf16[32,256]{1,0:T(8,128)(2,1)S(1)}, bf16[32,256]{1,0:T(8,128)(2,1)S(1)}, u32[]{:S(2)}, u32[]{:S(2)}) collective-permute-start(bf16[32,256]{1,0:T(8,128)(2,1)S(1)} %get-tuple-element.22.refs_0_), channel_id=1, source_target_pairs={{4,0},{12,8},{5,1},{13,9},{6,2},{14,10},{7,3},{15,11},{20,16},{28,... | collective-permute-start | bytes 49160 | tf_op jit(solution)/shard_map/ppermute | solution.py:392
  15.1 3.5 %collective-permute-start.7 = (bf16[32,256]{1,0:T(8,128)(2,1)S(1)}, bf16[32,256]{1,0:T(8,128)(2,1)S(1)}, u32[]{:S(2)}, u32[]{:S(2)}) collective-permute-start(bf16[32,256]{1,0:T(8,128)(2,1)S(1)} %get-tuple-element.22.refs_0_), channel_id=1, source_target_pairs={{0,8},{8,0},{1,9},{9,1},{2,10},{10,2},{3,11},{11,3},{16,24},{24,16... | collective-permute-start | bytes 49160 | tf_op jit(solution)/shard_map/ppermute | solution.py:392
  18.5 3.5 %collective-permute-start.6 = (bf16[32,256]{1,0:T(8,128)(2,1)S(1)}, bf16[32,256]{1,0:T(8,128)(2,1)S(1)}, u32[]{:S(2)}, u32[]{:S(2)}) collective-permute-start(bf16[32,256]{1,0:T(8,128)(2,1)S(1)} %get-tuple-element.22.refs_0_), channel_id=1, source_target_pairs={{0,12},{8,4},{1,13},{9,5},{2,14},{10,6},{3,15},{11,7},{16,28},{24,... | collective-permute-start | bytes 49160 | tf_op jit(solution)/shard_map/ppermute | solution.py:392
  22.1 1.3 %collective-permute-start.5 = (bf16[32,256]{1,0:T(8,128)(2,1)S(1)}, bf16[32,256]{1,0:T(8,128)(2,1)S(1)}, u32[]{:S(2)}, u32[]{:S(2)}) collective-permute-start(bf16[32,256]{1,0:T(8,128)(2,1)S(1)} %get-tuple-element.22.refs_0_), channel_id=1, source_target_pairs={{0,4},{8,12},{1,5},{9,13},{2,6},{10,14},{3,7},{11,15},{16,20},{24,... | collective-permute-start | bytes 49160 | tf_op jit(solution)/shard_map/ppermute | solution.py:392
  23.4 0.7 %collective-permute-start.4 = (bf16[32,256]{1,0:T(8,128)(2,1)S(1)}, bf16[32,256]{1,0:T(8,128)(2,1)S(1)}, u32[]{:S(2)}, u32[]{:S(2)}) collective-permute-start(bf16[32,256]{1,0:T(8,128)(2,1)S(1)} %get-tuple-element.22.refs_0_), channel_id=1, source_target_pairs={{4,12},{12,4},{5,13},{13,5},{6,14},{14,6},{7,15},{15,7},{20,28},{2... | collective-permute-start | bytes 49160 | tf_op jit(solution)/shard_map/ppermute | solution.py:392
  24.1 1.6 %cache_part.1 = (f32[8,4096]{1,0:T(8,128)S(1)}, f32[16,128]{1,0:T(8,128)S(1)}) custom-call(s32[1,1,8]{2,1,0:T(1,128)S(1)} %copy-done.4, bf16[8,4096]{1,0:T(8,128)(2,1)S(1)} %bitcast.8, bf16[8,128,1024]{2,1,0:T(8,128)(2,1)S(1)} %bitcast.6, s32[8,128]{1,0:T(8,128)S(1)} %copy-done.3), custom_call_target="tpu_custom_call" | custom-call | flops 16777216 | bytes 2097152 | tf_op jit(solution)/shard_map/cache_part/pallas_call | solution.py:195
  25.8 0.4 %mix.1 = (f32[8,4096]{1,0:T(8,128)S(1)}, bf16[8,4096]{1,0:T(8,128)(2,1)S(1)}, f32[8,128]{1,0:T(8,128)S(1)}, f32[16,128]{1,0:T(8,128)S(1)}) custom-call(s32[8,256]{1,0:T(8,128)S(1)} %get-tuple-element.19.code_ref, bf16[256,512]{1,0:T(8,128)(2,1)S(1)} %get-tuple-element.20.values_ref, bf16[256,512]{1,0:T(8,128)(2,1)S(1)} %collective-permute-done.3.near_ref, ...), custom_call_target="tpu_custom_call" | custom-call | tf_op jit(solution)/shard_map/mix/pallas_call | solution.py:311
  26.2 0.6 %collective-permute-start.11 = (bf16[8,4096]{1,0:T(8,128)(2,1)S(1)}, bf16[8,4096]{1,0:T(8,128)(2,1)S(1)}, u32[]{:S(2)}, u32[]{:S(2)}) collective-permute-start(bf16[8,4096]{1,0:T(8,128)(2,1)S(1)} %get-tuple-element.28), channel_id=1, source_target_pairs={{0,8},{4,12},{8,0},{12,4},{1,9},{5,13},{9,1},{13,5},{2,10},{6,14},... | collective-permute-start | bytes 196616 | tf_op jit(solution)/shard_map/ppermute | solution.py:379
  26.8 1.5 %collective-permute-start.10 = (f32[16,128]{1,0:T(8,128)S(1)}, f32[16,128]{1,0:T(8,128)S(1)}, u32[]{:S(2)}, u32[]{:S(2)}) collective-permute-start(f32[16,128]{1,0:T(8,128)S(1)} %get-tuple-element.25.stats_ref), channel_id=1, source_target_pairs={{0,2},{2,0},{1,3},{3,1},{4,6},{6,4},{5,7},{7,5},{8,10},{10,8},{9,1... | collective-permute-start | bytes 24584 | tf_op jit(solution)/shard_map/ppermute | solution.py:379
  28.3 2.2 %collective-permute-done.10.other_ref = f32[16,128]{1,0:T(8,128)S(1)} collective-permute-done((f32[16,128]{1,0:T(8,128)S(1)}, f32[16,128]{1,0:T(8,128)S(1)}, u32[]{:S(2)}, u32[]{:S(2)}) %collective-permute-start.10) | collective-permute-done | bytes 8224 | tf_op jit(solution)/shard_map/ppermute | solution.py:379
  30.5 0.2 weigh.1
  30.6 0.8 %collective-permute-done.11.far_ref = bf16[8,4096]{1,0:T(8,128)(2,1)S(1)} collective-permute-done((bf16[8,4096]{1,0:T(8,128)(2,1)S(1)}, bf16[8,4096]{1,0:T(8,128)(2,1)S(1)}, u32[]{:S(2)}, u32[]{:S(2)}) %collective-permute-start.11) | collective-permute-done | bytes 65568 | tf_op jit(solution)/shard_map/ppermute | solution.py:379
  31.4 1.6 %collective-permute-start.12 = (bf16[8,4096]{1,0:T(8,128)(2,1)S(1)}, bf16[8,4096]{1,0:T(8,128)(2,1)S(1)}, u32[]{:S(2)}, u32[]{:S(2)}) collective-permute-start(bf16[8,4096]{1,0:T(8,128)(2,1)S(1)} %merge.1.own_ref), channel_id=1, source_target_pairs={{0,2},{2,0},{1,3},{3,1},{4,6},{6,4},{5,7},{7,5},{8,10},{10,8},{9,1... | collective-permute-start | bytes 196616 | tf_op jit(solution)/shard_map/ppermute | solution.py:379
  33.0 2.8 %collective-permute-done.12.other_ref = bf16[8,4096]{1,0:T(8,128)(2,1)S(1)} collective-permute-done((bf16[8,4096]{1,0:T(8,128)(2,1)S(1)}, bf16[8,4096]{1,0:T(8,128)(2,1)S(1)}, u32[]{:S(2)}, u32[]{:S(2)}) %collective-permute-start.12) | collective-permute-done | bytes 65568 | tf_op jit(solution)/shard_map/ppermute | solution.py:379
  35.8 0.6 %finish.1 = bf16[8,4096]{1,0:T(8,128)(2,1)} custom-call(bf16[8,4096]{1,0:T(8,128)(2,1)S(1)} %merge.1.own_ref, bf16[8,4096]{1,0:T(8,128)(2,1)S(1)} %collective-permute-done.12.other_ref), custom_call_target="tpu_custom_call" | custom-call | tf_op jit(solution)/shard_map/finish/pallas_call | solution.py:369
  (25 shorter events, 0.1 us)
Async XLA Ops:
  0.0 6.8 %slice-start = ((s8[8388608]{0:T(1024)(128)(4,1)}), s8[4194304]{0:T(1024)(128)(4,1)S(1)}, s32[]{:S(2)}) async-start(s8[8388608]{0:T(1024)(128)(4,1)} %bitcast.4), calls=%async_computation | async-start | bytes 8388608
  0.0 6.8 %slice-start.1 = ((s8[8388608]{0:T(1024)(128)(4,1)}), s8[4194304]{0:T(1024)(128)(4,1)S(1)}, s32[]{:S(2)}) async-start(s8[8388608]{0:T(1024)(128)(4,1)} %bitcast.4), calls=%async_computation.1 | async-start | bytes 8388608
  0.0 6.8 %copy-start = (bf16[256,4096]{1,0:T(8,128)(2,1)S(1)}, bf16[256,4096]{1,0:T(8,128)(2,1)}, u32[]{:S(2)}) copy-start(bf16[256,4096]{1,0:T(8,128)(2,1)} %tokens_ref.1) | copy-start | bytes 6291460
  1.0 9.6 %collective-permute-start.2 = (bf16[8,4224]{1,0:T(8,128)(2,1)S(1)}, bf16[8,4224]{1,0:T(8,128)(2,1)S(1)}, u32[]{:S(2)}, u32[]{:S(2)}) collective-permute-start(bf16[8,4224]{1,0:T(8,128)(2,1)S(1)} %make_message.1.refs_0_), channel_id=1, source_target_pairs={{0,12},{4,8},{8,4},{12,0},{1,13},{5,9},{9,5},{13,1},{2,14},{6,10},... | collective-permute-start | bytes 202760 | tf_op jit(solution)/shard_map/ppermute | solution.py:379
  6.2 5.8 %collective-permute-start.1 = (bf16[8,4224]{1,0:T(8,128)(2,1)S(1)}, bf16[8,4224]{1,0:T(8,128)(2,1)S(1)}, u32[]{:S(2)}, u32[]{:S(2)}) collective-permute-start(bf16[8,4224]{1,0:T(8,128)(2,1)S(1)} %make_message.1.refs_0_), channel_id=1, source_target_pairs={{0,8},{4,12},{8,0},{12,4},{1,9},{5,13},{9,1},{13,5},{2,10},{6,14},... | collective-permute-start | bytes 202760 | tf_op jit(solution)/shard_map/ppermute | solution.py:379
  6.2 5.8 %collective-permute-start = (bf16[8,4224]{1,0:T(8,128)(2,1)S(1)}, bf16[8,4224]{1,0:T(8,128)(2,1)S(1)}, u32[]{:S(2)}, u32[]{:S(2)}) collective-permute-start(bf16[8,4224]{1,0:T(8,128)(2,1)S(1)} %make_message.1.refs_0_), channel_id=1, source_target_pairs={{0,4},{4,0},{8,12},{12,8},{1,5},{5,1},{9,13},{13,9},{2,6},{6,2},{1... | collective-permute-start | bytes 202760 | tf_op jit(solution)/shard_map/ppermute | solution.py:379
  9.1 16.6 %collective-permute-start.3 = (bf16[256,512]{1,0:T(8,128)(2,1)S(1)}, bf16[256,512]{1,0:T(8,128)(2,1)S(1)}, u32[]{:S(2)}, u32[]{:S(2)}) collective-permute-start(bf16[256,512]{1,0:T(8,128)(2,1)S(1)} %get-tuple-element.20.values_ref), channel_id=1, source_target_pairs={{0,4},{4,0},{8,12},{12,8},{1,5},{5,1},{9,13},{13,9},{2,6},{6,2},{1... | collective-permute-start | bytes 786440 | tf_op jit(solution)/shard_map/ppermute | solution.py:379
  12.0 12.1 %copy-start.1 = (bf16[1,1,8,128,1024]{4,3,2,1,0:T(8,128)(2,1)S(1)}, bf16[1,1,8,128,1024]{4,3,2,1,0:T(8,128)(2,1)}, u32[]{:S(2)}) copy-start(bf16[1,1,8,128,1024]{4,3,2,1,0:T(8,128)(2,1)} %param.14) | copy-start | bytes 6291460
  12.0 12.1 %copy-start.2 = (bf16[1,1,8,4096]{3,2,1,0:T(8,128)(2,1)S(1)}, bf16[1,1,8,4096]{3,2,1,0:T(8,128)(2,1)}, u32[]{:S(2)}) copy-start(bf16[1,1,8,4096]{3,2,1,0:T(8,128)(2,1)} %param.13) | copy-start | bytes 196612
  12.0 12.1 %copy-start.3 = (s32[8,128]{1,0:T(8,128)S(1)}, s32[8,128]{1,0:T(8,128)}, u32[]{:S(2)}) copy-start(s32[8,128]{1,0:T(8,128)} %signs_ref.1) | copy-start | bytes 12292
  12.0 12.1 %copy-start.4 = (s32[1,1,8]{2,1,0:T(1,128)S(1)}, s32[1,1,8]{2,1,0:T(1,128)}, u32[]{:S(2)}) copy-start(s32[1,1,8]{2,1,0:T(1,128)} %lengths_ref.1) | copy-start | bytes 100
  12.3 9.8 %collective-permute-start.9 = (bf16[32,256]{1,0:T(8,128)(2,1)S(1)}, bf16[32,256]{1,0:T(8,128)(2,1)S(1)}, u32[]{:S(2)}, u32[]{:S(2)}) collective-permute-start(bf16[32,256]{1,0:T(8,128)(2,1)S(1)} %get-tuple-element.22.refs_0_), channel_id=1, source_target_pairs={{12,0},{4,8},{13,1},{5,9},{14,2},{6,10},{15,3},{7,11},{28,16},{20,... | collective-permute-start | bytes 49160 | tf_op jit(solution)/shard_map/ppermute | solution.py:392
  13.8 9.6 %collective-permute-start.8 = (bf16[32,256]{1,0:T(8,128)(2,1)S(1)}, bf16[32,256]{1,0:T(8,128)(2,1)S(1)}, u32[]{:S(2)}, u32[]{:S(2)}) collective-permute-start(bf16[32,256]{1,0:T(8,128)(2,1)S(1)} %get-tuple-element.22.refs_0_), channel_id=1, source_target_pairs={{4,0},{12,8},{5,1},{13,9},{6,2},{14,10},{7,3},{15,11},{20,16},{28,... | collective-permute-start | bytes 49160 | tf_op jit(solution)/shard_map/ppermute | solution.py:392
  15.1 10.7 %collective-permute-start.7 = (bf16[32,256]{1,0:T(8,128)(2,1)S(1)}, bf16[32,256]{1,0:T(8,128)(2,1)S(1)}, u32[]{:S(2)}, u32[]{:S(2)}) collective-permute-start(bf16[32,256]{1,0:T(8,128)(2,1)S(1)} %get-tuple-element.22.refs_0_), channel_id=1, source_target_pairs={{0,8},{8,0},{1,9},{9,1},{2,10},{10,2},{3,11},{11,3},{16,24},{24,16... | collective-permute-start | bytes 49160 | tf_op jit(solution)/shard_map/ppermute | solution.py:392
  18.5 7.2 %collective-permute-start.6 = (bf16[32,256]{1,0:T(8,128)(2,1)S(1)}, bf16[32,256]{1,0:T(8,128)(2,1)S(1)}, u32[]{:S(2)}, u32[]{:S(2)}) collective-permute-start(bf16[32,256]{1,0:T(8,128)(2,1)S(1)} %get-tuple-element.22.refs_0_), channel_id=1, source_target_pairs={{0,12},{8,4},{1,13},{9,5},{2,14},{10,6},{3,15},{11,7},{16,28},{24,... | collective-permute-start | bytes 49160 | tf_op jit(solution)/shard_map/ppermute | solution.py:392
  22.1 3.6 %collective-permute-start.5 = (bf16[32,256]{1,0:T(8,128)(2,1)S(1)}, bf16[32,256]{1,0:T(8,128)(2,1)S(1)}, u32[]{:S(2)}, u32[]{:S(2)}) collective-permute-start(bf16[32,256]{1,0:T(8,128)(2,1)S(1)} %get-tuple-element.22.refs_0_), channel_id=1, source_target_pairs={{0,4},{8,12},{1,5},{9,13},{2,6},{10,14},{3,7},{11,15},{16,20},{24,... | collective-permute-start | bytes 49160 | tf_op jit(solution)/shard_map/ppermute | solution.py:392
  23.4 2.3 %collective-permute-start.4 = (bf16[32,256]{1,0:T(8,128)(2,1)S(1)}, bf16[32,256]{1,0:T(8,128)(2,1)S(1)}, u32[]{:S(2)}, u32[]{:S(2)}) collective-permute-start(bf16[32,256]{1,0:T(8,128)(2,1)S(1)} %get-tuple-element.22.refs_0_), channel_id=1, source_target_pairs={{4,12},{12,4},{5,13},{13,5},{6,14},{14,6},{7,15},{15,7},{20,28},{2... | collective-permute-start | bytes 49160 | tf_op jit(solution)/shard_map/ppermute | solution.py:392
  26.2 5.2 %collective-permute-start.11 = (bf16[8,4096]{1,0:T(8,128)(2,1)S(1)}, bf16[8,4096]{1,0:T(8,128)(2,1)S(1)}, u32[]{:S(2)}, u32[]{:S(2)}) collective-permute-start(bf16[8,4096]{1,0:T(8,128)(2,1)S(1)} %get-tuple-element.28), channel_id=1, source_target_pairs={{0,8},{4,12},{8,0},{12,4},{1,9},{5,13},{9,1},{13,5},{2,10},{6,14},... | collective-permute-start | bytes 196616 | tf_op jit(solution)/shard_map/ppermute | solution.py:379
  26.8 3.7 %collective-permute-start.10 = (f32[16,128]{1,0:T(8,128)S(1)}, f32[16,128]{1,0:T(8,128)S(1)}, u32[]{:S(2)}, u32[]{:S(2)}) collective-permute-start(f32[16,128]{1,0:T(8,128)S(1)} %get-tuple-element.25.stats_ref), channel_id=1, source_target_pairs={{0,2},{2,0},{1,3},{3,1},{4,6},{6,4},{5,7},{7,5},{8,10},{10,8},{9,1... | collective-permute-start | bytes 24584 | tf_op jit(solution)/shard_map/ppermute | solution.py:379
  31.4 4.3 %collective-permute-start.12 = (bf16[8,4096]{1,0:T(8,128)(2,1)S(1)}, bf16[8,4096]{1,0:T(8,128)(2,1)S(1)}, u32[]{:S(2)}, u32[]{:S(2)}) collective-permute-start(bf16[8,4096]{1,0:T(8,128)(2,1)S(1)} %merge.1.own_ref), channel_id=1, source_target_pairs={{0,2},{2,0},{1,3},{3,1},{4,6},{6,4},{5,7},{7,5},{8,10},{10,8},{9,1... | collective-permute-start | bytes 196616 | tf_op jit(solution)/shard_map/ppermute | solution.py:379

commit v18 on v16

--- a/solution.py
+++ b/solution.py
@@ -74,23 +74,31 @@
     )(in_vmem(tokens), in_vmem(weight))
 
 
+def eighths(columns):
+    step = columns // 8
+    return [slice(at, at + step) for at in range(0, columns, step)]
+
+
 def message_kernel(query_ref, owners_ref, requests_ref, out_ref, owners_buf, requests_buf, sems):
     requests, columns = query_ref.shape
     per_device = owners_ref.shape[1]
-    copies = [
-        pltpu.make_async_copy(query_ref, out_ref.at[:, :columns], sems.at[0]),
-        pltpu.make_async_copy(owners_ref, owners_buf, sems.at[1]),
-        pltpu.make_async_copy(requests_ref, requests_buf, sems.at[2]),
+    small = [
+        pltpu.make_async_copy(owners_ref, owners_buf, sems.at[0]),
+        pltpu.make_async_copy(requests_ref, requests_buf, sems.at[1]),
     ]
-    for copy in copies:
+    copies = []
+    for i, span in enumerate(eighths(columns)):
+        copies.append(pltpu.make_async_copy(query_ref.at[:, span], out_ref.at[:, span], sems.at[2 + i]))
+    for copy in small + copies:
         copy.start()
-    copies[1].wait()
-    copies[2].wait()
+    for copy in small:
+        copy.wait()
     code = (owners_buf[...] * requests + requests_buf[...]).astype(jnp.float32)
     spare = jnp.zeros((1, out_ref.shape[1] - columns - per_device), jnp.float32)
     code = jnp.concatenate([code, spare], axis=1)
     out_ref[:, columns:] = jnp.broadcast_to(code, (requests, code.shape[1])).astype(out_ref.dtype)
-    copies[0].wait()
+    for copy in copies:
+        copy.wait()
 
 
 def make_message(query, owners, requests):
@@ -104,7 +112,7 @@
         scratch_shapes=[
             pltpu.VMEM(owners.shape, owners.dtype),
             pltpu.VMEM(requests.shape, requests.dtype),
-            pltpu.SemaphoreType.DMA((3,)),
+            pltpu.SemaphoreType.DMA((10,)),
         ],
         compiler_params=params(16),
         cost_estimate=pl.CostEstimate(flops=10**11, bytes_accessed=10**4, transcendentals=0),
@@ -351,14 +359,25 @@
     )(base, factor, far)
 
 
-def finish_kernel(own_ref, other_ref, out_ref):
-    out_ref[...] = (own_ref[...].astype(jnp.float32) + other_ref[...].astype(jnp.float32)).astype(out_ref.dtype)
+def finish_kernel(own_ref, other_ref, out_ref, out_buf, sems):
+    copies = []
+    for i, span in enumerate(eighths(own_ref.shape[1])):
+        total = own_ref[:, span].astype(jnp.float32) + other_ref[:, span].astype(jnp.float32)
+        out_buf[:, span] = total.astype(out_buf.dtype)
+        copies.append(pltpu.make_async_copy(out_buf.at[:, span], out_ref.at[:, span], sems.at[i]))
+        copies[-1].start()
+    for copy in copies:
+        copy.wait()
 
 
 def finish(own, other):
+    vmem = pl.BlockSpec(memory_space=pltpu.VMEM)
     return pl.pallas_call(
         finish_kernel,
+        in_specs=[vmem] * 2,
+        out_specs=pl.BlockSpec(memory_space=pl.ANY),
         out_shape=jax.ShapeDtypeStruct(own.shape, own.dtype),
+        scratch_shapes=[pltpu.VMEM(own.shape, own.dtype), pltpu.SemaphoreType.DMA((8,))],
         compiler_params=params(),
         name="finish",
     )(own, other)

time: 30.1 us -> 30.2 us (level)
  no operation moved by 1% of the time
where the time goes in v18:
time: 30.2 us; the launch traced here: 30 us
  starting transfers between devices  16 us (53%)
  waiting for transfers between devices  7.38 us (24%)
  Pallas kernels  6.54 us (22%)
    ppermute x7, starting transfers between devices, from_partner(): return lax.ppermute(x, axis, [(i, i ^ distance) for i in range(count)])  11.5 us
    ppermute x7, waiting for transfers between devices, from_partner(): return lax.ppermute(x, axis, [(i, i ^ distance) for i in range(count)])  6.53 us
    ppermute x3, starting transfers between devices, from_behind(): lax.ppermute(x, axis, [(i, (i + distance) % count) for i in range(count)])  4.52 us
    pallas_call x1, Pallas kernels, project(): pl.pallas_call(project_kernel, in_specs=[vmem] * 2, out_specs=[vmem] * 2,...  2.32 us
    pallas_call x1, Pallas kernels, cache_part(): pl.pallas_call(cache_kernel, in_specs=[pl.BlockSpec(memory_space=pltpu.SM...  1.6 us
    pallas_call x1, Pallas kernels, make_message(): pl.pallas_call(message_kernel, in_specs=[pl.BlockSpec(memory_space=pl.ANY...  1.03 us
    ppermute x3, waiting for transfers between devices, from_behind(): lax.ppermute(x, axis, [(i, (i + distance) % count) for i in range(count)])  0.85 us
    pallas_call x1, Pallas kernels, finish(): pl.pallas_call(finish_kernel, in_specs=[vmem] * 2, out_specs=pl.BlockSpec...  0.7 us
  transfers between devices with their start and end apart: 10, of which 6 were waited for; matrix products, arithmetic and copies ran while one was open for 0% of the time, Pallas kernels for 15%

profile of v18, /device:TPU:0, one launch (start us, length us, event | category | flops | bytes accessed | tf_op | source)
XLA Modules:
  0.0 30.0 jit_solution(13556528491188287212)
XLA Ops:
  0.0 1.0 %make_message.1.refs_0_ = bf16[8,4224]{1,0:T(8,128)(2,1)S(1)} custom-call(bf16[8,4096]{1,0:T(8,128)(2,1)} %bitcast.7, s32[1,64]{1,0:T(1,128)} %bitcast.9, s32[1,64]{1,0:T(1,128)} %requests_ref.1), custom_call_target="tpu_custom_call" | custom-call | flops 99999997952 | bytes 10000 | tf_op jit(solution)/shard_map/make_message/pallas_call | solution.py:107
  1.0 5.1 %collective-permute-start = (bf16[8,4224]{1,0:T(8,128)(2,1)S(1)}, bf16[8,4224]{1,0:T(8,128)(2,1)S(1)}, u32[]{:S(2)}, u32[]{:S(2)}) collective-permute-start(bf16[8,4224]{1,0:T(8,128)(2,1)S(1)} %make_message.1.refs_0_), channel_id=1, source_target_pairs={{0,12},{4,8},{8,4},{12,0},{1,13},{5,9},{9,5},{13,1},{2,14},{6,10},... | collective-permute-start | bytes 202760 | tf_op jit(solution)/shard_map/ppermute | solution.py:388
  6.2 0.0 collective-permute-start.1
  6.2 0.6 %collective-permute-start.2 = (bf16[8,4224]{1,0:T(8,128)(2,1)S(1)}, bf16[8,4224]{1,0:T(8,128)(2,1)S(1)}, u32[]{:S(2)}, u32[]{:S(2)}) collective-permute-start(bf16[8,4224]{1,0:T(8,128)(2,1)S(1)} %make_message.1.refs_0_), channel_id=1, source_target_pairs={{0,4},{4,0},{8,12},{12,8},{1,5},{5,1},{9,13},{13,9},{2,6},{6,2},{1... | collective-permute-start | bytes 202760 | tf_op jit(solution)/shard_map/ppermute | solution.py:388
  6.8 2.3 %project.1 = (bf16[256,512]{1,0:T(8,128)(2,1)S(1)}, bf16[256,512]{1,0:T(8,128)(2,1)S(1)}) custom-call(bf16[256,4096]{1,0:T(8,128)(2,1)S(1)} %copy-done, bf16[4096,1024]{1,0:T(8,128)(2,1)S(1)} %bitcast.5), custom_call_target="tpu_custom_call" | custom-call | flops 2147483648 | bytes 10485760 | tf_op jit(solution)/shard_map/project/pallas_call | solution.py:62
  9.1 1.5 %collective-permute-start.3 = (bf16[256,512]{1,0:T(8,128)(2,1)S(1)}, bf16[256,512]{1,0:T(8,128)(2,1)S(1)}, u32[]{:S(2)}, u32[]{:S(2)}) collective-permute-start(bf16[256,512]{1,0:T(8,128)(2,1)S(1)} %get-tuple-element.20.values_ref), channel_id=1, source_target_pairs={{0,4},{4,0},{8,12},{12,8},{1,5},{5,1},{9,13},{13,9},{2,6},{6,2},{1... | collective-permute-start | bytes 786440 | tf_op jit(solution)/shard_map/ppermute | solution.py:388
  10.6 1.4 %collective-permute-done.1.refs_2_ = bf16[8,4224]{1,0:T(8,128)(2,1)S(1)} collective-permute-done((bf16[8,4224]{1,0:T(8,128)(2,1)S(1)}, bf16[8,4224]{1,0:T(8,128)(2,1)S(1)}, u32[]{:S(2)}, u32[]{:S(2)}) %collective-permute-start.1) | collective-permute-done | bytes 67616 | tf_op jit(solution)/shard_map/ppermute | solution.py:388
  12.0 0.0 copy-start.4
  12.0 0.3 %partial_scores.1 = (bf16[32,256]{1,0:T(8,128)(2,1)S(1)}, s32[8,256]{1,0:T(8,128)S(1)}) custom-call(bf16[256,512]{1,0:T(8,128)(2,1)S(1)} %get-tuple-element.18.keys_ref, bf16[8,4224]{1,0:T(8,128)(2,1)S(1)} %make_message.1.refs_0_, bf16[8,4224]{1,0:T(8,128)(2,1)S(1)} %collective-permute-done.refs_1_, bf16[8,4224]{1,0:T(8,128)(2,1)S(1)} %collective-permute-done.1.refs_2_, ...), custom_call_target="tpu_custom_call" | custom-call | flops 99999997952 | bytes 10000 | tf_op jit(solution)/shard_map/partial_scores/pallas_call | solution.py:252
  12.4 1.5 %collective-permute-start.4 = (bf16[32,256]{1,0:T(8,128)(2,1)S(1)}, bf16[32,256]{1,0:T(8,128)(2,1)S(1)}, u32[]{:S(2)}, u32[]{:S(2)}) collective-permute-start(bf16[32,256]{1,0:T(8,128)(2,1)S(1)} %get-tuple-element.22.refs_0_), channel_id=1, source_target_pairs={{0,4},{4,8},{8,12},{12,0},{1,5},{5,9},{9,13},{13,1},{2,6},{6,10},{... | collective-permute-start | bytes 49160 | tf_op jit(solution)/shard_map/ppermute | solution.py:393
  13.8 1.8 %collective-permute-start.5 = (bf16[32,256]{1,0:T(8,128)(2,1)S(1)}, bf16[32,256]{1,0:T(8,128)(2,1)S(1)}, u32[]{:S(2)}, u32[]{:S(2)}) collective-permute-start(bf16[32,256]{1,0:T(8,128)(2,1)S(1)} %get-tuple-element.22.refs_0_), channel_id=1, source_target_pairs={{0,8},{4,12},{8,0},{12,4},{1,9},{5,13},{9,1},{13,5},{2,10},{6,14},... | collective-permute-start | bytes 49160 | tf_op jit(solution)/shard_map/ppermute | solution.py:393
  15.6 1.3 %collective-permute-start.6 = (bf16[32,256]{1,0:T(8,128)(2,1)S(1)}, bf16[32,256]{1,0:T(8,128)(2,1)S(1)}, u32[]{:S(2)}, u32[]{:S(2)}) collective-permute-start(bf16[32,256]{1,0:T(8,128)(2,1)S(1)} %get-tuple-element.22.refs_0_), channel_id=1, source_target_pairs={{0,12},{4,0},{8,4},{12,8},{1,13},{5,1},{9,5},{13,9},{2,14},{6,2},{... | collective-permute-start | bytes 49160 | tf_op jit(solution)/shard_map/ppermute | solution.py:393
  16.9 1.6 %cache_part.1 = (f32[8,4096]{1,0:T(8,128)S(1)}, f32[16,128]{1,0:T(8,128)S(1)}) custom-call(s32[1,1,8]{2,1,0:T(1,128)S(1)} %copy-done.4, bf16[8,4096]{1,0:T(8,128)(2,1)S(1)} %bitcast.8, bf16[8,128,1024]{2,1,0:T(8,128)(2,1)S(1)} %bitcast.6, s32[8,128]{1,0:T(8,128)S(1)} %copy-done.3), custom_call_target="tpu_custom_call" | custom-call | flops 16777216 | bytes 2097152 | tf_op jit(solution)/shard_map/cache_part/pallas_call | solution.py:196
  18.5 0.6 %collective-permute-done.4.refs_1_ = bf16[32,256]{1,0:T(8,128)(2,1)S(1)} collective-permute-done((bf16[32,256]{1,0:T(8,128)(2,1)S(1)}, bf16[32,256]{1,0:T(8,128)(2,1)S(1)}, u32[]{:S(2)}, u32[]{:S(2)}) %collective-permute-start.4) | collective-permute-done | bytes 16416 | tf_op jit(solution)/shard_map/ppermute | solution.py:393
  19.1 0.2 collective-permute-done.6.refs_3_
  19.3 0.4 %mix.1 = (f32[8,4096]{1,0:T(8,128)S(1)}, bf16[8,4096]{1,0:T(8,128)(2,1)S(1)}, f32[8,128]{1,0:T(8,128)S(1)}, f32[16,128]{1,0:T(8,128)S(1)}) custom-call(s32[8,256]{1,0:T(8,128)S(1)} %get-tuple-element.19.code_ref, bf16[256,512]{1,0:T(8,128)(2,1)S(1)} %get-tuple-element.20.values_ref, bf16[256,512]{1,0:T(8,128)(2,1)S(1)} %collective-permute-done.3.near_ref, ...), custom_call_target="tpu_custom_call" | custom-call | tf_op jit(solution)/shard_map/mix/pallas_call | solution.py:309
  19.7 1.2 %collective-permute-start.8 = (bf16[8,4096]{1,0:T(8,128)(2,1)S(1)}, bf16[8,4096]{1,0:T(8,128)(2,1)S(1)}, u32[]{:S(2)}, u32[]{:S(2)}) collective-permute-start(bf16[8,4096]{1,0:T(8,128)(2,1)S(1)} %get-tuple-element.28), channel_id=1, source_target_pairs={{0,8},{4,12},{8,0},{12,4},{1,9},{5,13},{9,1},{13,5},{2,10},{6,14},... | collective-permute-start | bytes 196616 | tf_op jit(solution)/shard_map/ppermute | solution.py:388
  20.9 1.5 %collective-permute-start.7 = (f32[16,128]{1,0:T(8,128)S(1)}, f32[16,128]{1,0:T(8,128)S(1)}, u32[]{:S(2)}, u32[]{:S(2)}) collective-permute-start(f32[16,128]{1,0:T(8,128)S(1)} %get-tuple-element.25.stats_ref), channel_id=1, source_target_pairs={{0,2},{2,0},{1,3},{3,1},{4,6},{6,4},{5,7},{7,5},{8,10},{10,8},{9,1... | collective-permute-start | bytes 24584 | tf_op jit(solution)/shard_map/ppermute | solution.py:388
  22.4 2.2 %collective-permute-done.7.other_ref = f32[16,128]{1,0:T(8,128)S(1)} collective-permute-done((f32[16,128]{1,0:T(8,128)S(1)}, f32[16,128]{1,0:T(8,128)S(1)}, u32[]{:S(2)}, u32[]{:S(2)}) %collective-permute-start.7) | collective-permute-done | bytes 8224 | tf_op jit(solution)/shard_map/ppermute | solution.py:388
  24.6 0.2 weigh.1
  24.8 0.2 collective-permute-done.8.far_ref
  25.0 1.6 %collective-permute-start.9 = (bf16[8,4096]{1,0:T(8,128)(2,1)S(1)}, bf16[8,4096]{1,0:T(8,128)(2,1)S(1)}, u32[]{:S(2)}, u32[]{:S(2)}) collective-permute-start(bf16[8,4096]{1,0:T(8,128)(2,1)S(1)} %merge.1.own_ref), channel_id=1, source_target_pairs={{0,2},{2,0},{1,3},{3,1},{4,6},{6,4},{5,7},{7,5},{8,10},{10,8},{9,1... | collective-permute-start | bytes 196616 | tf_op jit(solution)/shard_map/ppermute | solution.py:388
  26.6 2.8 %collective-permute-done.9.other_ref = bf16[8,4096]{1,0:T(8,128)(2,1)S(1)} collective-permute-done((bf16[8,4096]{1,0:T(8,128)(2,1)S(1)}, bf16[8,4096]{1,0:T(8,128)(2,1)S(1)}, u32[]{:S(2)}, u32[]{:S(2)}) %collective-permute-start.9) | collective-permute-done | bytes 65568 | tf_op jit(solution)/shard_map/ppermute | solution.py:388
  29.3 0.7 %finish.1 = bf16[8,4096]{1,0:T(8,128)(2,1)} custom-call(bf16[8,4096]{1,0:T(8,128)(2,1)S(1)} %merge.1.own_ref, bf16[8,4096]{1,0:T(8,128)(2,1)S(1)} %collective-permute-done.9.other_ref), custom_call_target="tpu_custom_call" | custom-call | tf_op jit(solution)/shard_map/finish/pallas_call | solution.py:375
  (19 shorter events, 0.1 us)
Async XLA Ops:
  0.0 6.8 %slice-start = ((s8[8388608]{0:T(1024)(128)(4,1)}), s8[4194304]{0:T(1024)(128)(4,1)S(1)}, s32[]{:S(2)}) async-start(s8[8388608]{0:T(1024)(128)(4,1)} %bitcast.4), calls=%async_computation | async-start | bytes 8388608
  0.0 6.8 %slice-start.1 = ((s8[8388608]{0:T(1024)(128)(4,1)}), s8[4194304]{0:T(1024)(128)(4,1)S(1)}, s32[]{:S(2)}) async-start(s8[8388608]{0:T(1024)(128)(4,1)} %bitcast.4), calls=%async_computation.1 | async-start | bytes 8388608
  0.0 6.8 %copy-start = (bf16[256,4096]{1,0:T(8,128)(2,1)S(1)}, bf16[256,4096]{1,0:T(8,128)(2,1)}, u32[]{:S(2)}) copy-start(bf16[256,4096]{1,0:T(8,128)(2,1)} %tokens_ref.1) | copy-start | bytes 6291460
  1.0 9.6 %collective-permute-start = (bf16[8,4224]{1,0:T(8,128)(2,1)S(1)}, bf16[8,4224]{1,0:T(8,128)(2,1)S(1)}, u32[]{:S(2)}, u32[]{:S(2)}) collective-permute-start(bf16[8,4224]{1,0:T(8,128)(2,1)S(1)} %make_message.1.refs_0_), channel_id=1, source_target_pairs={{0,12},{4,8},{8,4},{12,0},{1,13},{5,9},{9,5},{13,1},{2,14},{6,10},... | collective-permute-start | bytes 202760 | tf_op jit(solution)/shard_map/ppermute | solution.py:388
  6.2 5.8 %collective-permute-start.1 = (bf16[8,4224]{1,0:T(8,128)(2,1)S(1)}, bf16[8,4224]{1,0:T(8,128)(2,1)S(1)}, u32[]{:S(2)}, u32[]{:S(2)}) collective-permute-start(bf16[8,4224]{1,0:T(8,128)(2,1)S(1)} %make_message.1.refs_0_), channel_id=1, source_target_pairs={{0,8},{4,12},{8,0},{12,4},{1,9},{5,13},{9,1},{13,5},{2,10},{6,14},... | collective-permute-start | bytes 202760 | tf_op jit(solution)/shard_map/ppermute | solution.py:388
  6.2 5.8 %collective-permute-start.2 = (bf16[8,4224]{1,0:T(8,128)(2,1)S(1)}, bf16[8,4224]{1,0:T(8,128)(2,1)S(1)}, u32[]{:S(2)}, u32[]{:S(2)}) collective-permute-start(bf16[8,4224]{1,0:T(8,128)(2,1)S(1)} %make_message.1.refs_0_), channel_id=1, source_target_pairs={{0,4},{4,0},{8,12},{12,8},{1,5},{5,1},{9,13},{13,9},{2,6},{6,2},{1... | collective-permute-start | bytes 202760 | tf_op jit(solution)/shard_map/ppermute | solution.py:388
  9.1 10.2 %collective-permute-start.3 = (bf16[256,512]{1,0:T(8,128)(2,1)S(1)}, bf16[256,512]{1,0:T(8,128)(2,1)S(1)}, u32[]{:S(2)}, u32[]{:S(2)}) collective-permute-start(bf16[256,512]{1,0:T(8,128)(2,1)S(1)} %get-tuple-element.20.values_ref), channel_id=1, source_target_pairs={{0,4},{4,0},{8,12},{12,8},{1,5},{5,1},{9,13},{13,9},{2,6},{6,2},{1... | collective-permute-start | bytes 786440 | tf_op jit(solution)/shard_map/ppermute | solution.py:388
  12.0 4.9 %copy-start.1 = (bf16[1,1,8,128,1024]{4,3,2,1,0:T(8,128)(2,1)S(1)}, bf16[1,1,8,128,1024]{4,3,2,1,0:T(8,128)(2,1)}, u32[]{:S(2)}) copy-start(bf16[1,1,8,128,1024]{4,3,2,1,0:T(8,128)(2,1)} %param.14) | copy-start | bytes 6291460
  12.0 4.9 %copy-start.2 = (bf16[1,1,8,4096]{3,2,1,0:T(8,128)(2,1)S(1)}, bf16[1,1,8,4096]{3,2,1,0:T(8,128)(2,1)}, u32[]{:S(2)}) copy-start(bf16[1,1,8,4096]{3,2,1,0:T(8,128)(2,1)} %param.13) | copy-start | bytes 196612
  12.0 4.9 %copy-start.3 = (s32[8,128]{1,0:T(8,128)S(1)}, s32[8,128]{1,0:T(8,128)}, u32[]{:S(2)}) copy-start(s32[8,128]{1,0:T(8,128)} %signs_ref.1) | copy-start | bytes 12292
  12.0 4.9 %copy-start.4 = (s32[1,1,8]{2,1,0:T(1,128)S(1)}, s32[1,1,8]{2,1,0:T(1,128)}, u32[]{:S(2)}) copy-start(s32[1,1,8]{2,1,0:T(1,128)} %lengths_ref.1) | copy-start | bytes 100
  12.4 6.8 %collective-permute-start.4 = (bf16[32,256]{1,0:T(8,128)(2,1)S(1)}, bf16[32,256]{1,0:T(8,128)(2,1)S(1)}, u32[]{:S(2)}, u32[]{:S(2)}) collective-permute-start(bf16[32,256]{1,0:T(8,128)(2,1)S(1)} %get-tuple-element.22.refs_0_), channel_id=1, source_target_pairs={{0,4},{4,8},{8,12},{12,0},{1,5},{5,9},{9,13},{13,1},{2,6},{6,10},{... | collective-permute-start | bytes 49160 | tf_op jit(solution)/shard_map/ppermute | solution.py:393
  13.8 5.3 %collective-permute-start.5 = (bf16[32,256]{1,0:T(8,128)(2,1)S(1)}, bf16[32,256]{1,0:T(8,128)(2,1)S(1)}, u32[]{:S(2)}, u32[]{:S(2)}) collective-permute-start(bf16[32,256]{1,0:T(8,128)(2,1)S(1)} %get-tuple-element.22.refs_0_), channel_id=1, source_target_pairs={{0,8},{4,12},{8,0},{12,4},{1,9},{5,13},{9,1},{13,5},{2,10},{6,14},... | collective-permute-start | bytes 49160 | tf_op jit(solution)/shard_map/ppermute | solution.py:393
  15.6 3.7 %collective-permute-start.6 = (bf16[32,256]{1,0:T(8,128)(2,1)S(1)}, bf16[32,256]{1,0:T(8,128)(2,1)S(1)}, u32[]{:S(2)}, u32[]{:S(2)}) collective-permute-start(bf16[32,256]{1,0:T(8,128)(2,1)S(1)} %get-tuple-element.22.refs_0_), channel_id=1, source_target_pairs={{0,12},{4,0},{8,4},{12,8},{1,13},{5,1},{9,5},{13,9},{2,14},{6,2},{... | collective-permute-start | bytes 49160 | tf_op jit(solution)/shard_map/ppermute | solution.py:393
  19.7 5.2 %collective-permute-start.8 = (bf16[8,4096]{1,0:T(8,128)(2,1)S(1)}, bf16[8,4096]{1,0:T(8,128)(2,1)S(1)}, u32[]{:S(2)}, u32[]{:S(2)}) collective-permute-start(bf16[8,4096]{1,0:T(8,128)(2,1)S(1)} %get-tuple-element.28), channel_id=1, source_target_pairs={{0,8},{4,12},{8,0},{12,4},{1,9},{5,13},{9,1},{13,5},{2,10},{6,14},... | collective-permute-start | bytes 196616 | tf_op jit(solution)/shard_map/ppermute | solution.py:388
  20.9 3.7 %collective-permute-start.7 = (f32[16,128]{1,0:T(8,128)S(1)}, f32[16,128]{1,0:T(8,128)S(1)}, u32[]{:S(2)}, u32[]{:S(2)}) collective-permute-start(f32[16,128]{1,0:T(8,128)S(1)} %get-tuple-element.25.stats_ref), channel_id=1, source_target_pairs={{0,2},{2,0},{1,3},{3,1},{4,6},{6,4},{5,7},{7,5},{8,10},{10,8},{9,1... | collective-permute-start | bytes 24584 | tf_op jit(solution)/shard_map/ppermute | solution.py:388
  25.0 4.3 %collective-permute-start.9 = (bf16[8,4096]{1,0:T(8,128)(2,1)S(1)}, bf16[8,4096]{1,0:T(8,128)(2,1)S(1)}, u32[]{:S(2)}, u32[]{:S(2)}) collective-permute-start(bf16[8,4096]{1,0:T(8,128)(2,1)S(1)} %merge.1.own_ref), channel_id=1, source_target_pairs={{0,2},{2,0},{1,3},{3,1},{4,6},{6,4},{5,7},{7,5},{8,10},{10,8},{9,1... | collective-permute-start | bytes 196616 | tf_op jit(solution)/shard_map/ppermute | solution.py:388

commit v19 on v16

--- a/solution.py
+++ b/solution.py
@@ -37,6 +37,7 @@
 
 QUERY_ORDER = (3, 2, 1)
 SCORE_ORDER = (1, 2, 3)
+FINISH_PLACES = (2, 1, 0)
 
 
 def arranged(blocks, order):
@@ -253,19 +254,35 @@
     )(keys, *arranged(messages, QUERY_ORDER))
 
 
-def mix_kernel(heads, requests, code_ref, values_ref, near_ref, cache_stats_ref, *refs):
-    score_refs, (own_ref, far_ref, new_stats_ref, stats_ref) = refs[:4], refs[4:]
+def packed(value, count):
+    lane = lax.broadcasted_iota(jnp.int32, value.shape, 1)
+    high = value.astype(jnp.bfloat16).astype(jnp.float32)
+    middle = (value - high).astype(jnp.bfloat16).astype(jnp.float32)
+    low = value - high - middle
+    middle, low = pltpu.roll(middle, count, 1), pltpu.roll(low, 2 * count, 1)
+    return jnp.where(lane < count, high, jnp.where(lane < 2 * count, middle, low))
+
+
+def unpacked(message, at, count):
+    parts = [message[:, at + part * count : at + (part + 1) * count] for part in range(3)]
+    return parts[0] + parts[1] + parts[2]
+
+
+def mix_kernel(heads, requests, code_ref, values_ref, near_ref, cache_ref, cache_stats_ref, *refs):
+    score_refs, (share_ref, far_ref) = refs[:4], refs[4:]
     own, before, across, after = [ref[...].astype(jnp.float32) for ref in score_refs]
     scores = (own + across) + (before + after)
     tokens, width = values_ref.shape
     size = width // heads
-    group = scores.shape[0] // heads
+    count, columns = scores.shape[0], cache_ref.shape[1]
+    group = count // heads
     span = 2 * requests
     row = lax.broadcasted_iota(jnp.int32, (span, tokens), 0)
     here = jnp.where(row < requests, row, row + requests) == code_ref[0:1, :]
-    lane = lax.broadcasted_iota(jnp.int32, (requests, stats_ref.shape[1]), 1)
+    lane = lax.broadcasted_iota(jnp.int32, (requests, cache_stats_ref.shape[1]), 1)
     tops = jnp.full(lane.shape, 0.0, jnp.float32)
     totals = jnp.zeros(lane.shape, jnp.float32)
+    parts = []
     for k in range(heads):
         weights = []
         for g in range(group):
@@ -278,90 +295,86 @@
             tops = jnp.where(lane == h, top[:requests], tops)
             totals = jnp.where(lane == h, total[:requests], totals)
         weights = jnp.concatenate(weights, axis=0).astype(jnp.bfloat16)
-        columns = slice(k * size, (k + 1) * size)
-        mixed = jnp.dot(weights, values_ref[:, columns], preferred_element_type=jnp.float32)
-        mixed = mixed + jnp.dot(weights, near_ref[:, columns], preferred_element_type=jnp.float32)
+        part = slice(k * size, (k + 1) * size)
+        mixed = jnp.dot(weights, values_ref[:, part], preferred_element_type=jnp.float32)
+        mixed = mixed + jnp.dot(weights, near_ref[:, part], preferred_element_type=jnp.float32)
         for g in range(group):
             at = slice((k * group + g) * size, (k * group + g + 1) * size)
-            own_ref[:, at] = mixed[g * span : g * span + requests]
+            parts.append(mixed[g * span : g * span + requests])
             far_ref[:, at] = mixed[g * span + requests : (g + 1) * span].astype(far_ref.dtype)
-    new_stats_ref[...] = tops
     cache_tops = cache_stats_ref[:requests, :]
     both = jnp.maximum(cache_tops, tops)
-    stats_ref[:requests, :] = both
-    stats_ref[requests:, :] = cache_stats_ref[requests:, :] * jnp.exp(cache_tops - both) + totals * jnp.exp(
-        tops - both
-    )
-
-
-def mix(heads, code, values, near_values, cache_stats, scores):
+    cache_factor = jnp.exp(cache_tops - both)
+    new_factor = jnp.exp(tops - both)
+    total = cache_stats_ref[requests:, :] * cache_factor + totals * new_factor
+    for h, part in enumerate(parts):
+        at = slice(h * size, (h + 1) * size)
+        share = cache_ref[:, at] * cache_factor[:, h : h + 1] + part * new_factor[:, h : h + 1]
+        share_ref[:, at] = share.astype(share_ref.dtype)
+    lanes = cache_stats_ref.shape[1]
+    far_ref[:, columns:] = jnp.zeros((requests, 3 * lanes), far_ref.dtype)
+    for i, value in enumerate((both, total, new_factor)):
+        share_ref[:, columns + i * lanes : columns + (i + 1) * lanes] = packed(value, count).astype(share_ref.dtype)
+
+
+def mix(heads, code, values, near_values, cache_mixed, cache_stats, scores):
     requests, lanes = cache_stats.shape[0] // 2, cache_stats.shape[1]
-    size = values.shape[1] // heads
-    shape = (requests, scores[0].shape[0] * size)
+    columns = cache_mixed.shape[1]
     return pl.pallas_call(
         functools.partial(mix_kernel, heads, requests),
         out_shape=[
-            jax.ShapeDtypeStruct(shape, jnp.float32),
-            jax.ShapeDtypeStruct(shape, jnp.bfloat16),
-            jax.ShapeDtypeStruct((requests, lanes), jnp.float32),
-            jax.ShapeDtypeStruct(cache_stats.shape, jnp.float32),
-        ],
+            jax.ShapeDtypeStruct((requests, columns + 3 * lanes), jnp.bfloat16),
+        ]
+        * 2,
         compiler_params=params(),
         name="mix",
-    )(code, values, near_values, cache_stats, *arranged(scores, SCORE_ORDER))
-
-
-def weigh_kernel(cache_ref, own_ref, cache_stats_ref, new_stats_ref, stats_ref, other_ref, base_ref, factor_ref):
-    requests, columns = cache_ref.shape
-    size = cache_stats_ref.shape[1]
-    top, other_top = stats_ref[:requests, :], other_ref[:requests, :]
-    both = jnp.maximum(top, other_top)
-    total = stats_ref[requests:, :] * jnp.exp(top - both)
-    total = total + other_ref[requests:, :] * jnp.exp(other_top - both)
+    )(code, values, near_values, cache_mixed, cache_stats, *arranged(scores, SCORE_ORDER))
+
+
+def finish_kernel(count, own_ref, *refs):
+    out_ref = refs[-1]
+    other_ref, own_far_ref, other_far_ref = [refs[i] for i in FINISH_PLACES]
+    columns = out_ref.shape[1]
+    size = columns // count
+    lanes = (own_ref.shape[1] - columns) // 3
+    first = lax.axis_index("tp") == 0
+
+    def stats(ref):
+        message = ref[:, columns:].astype(jnp.float32)
+        return [unpacked(message, i * lanes, count) for i in range(3)]
+
+    own_top, own_total, own_new = stats(own_ref)
+    other_top, other_total, other_new = stats(other_ref)
+    both = jnp.maximum(own_top, other_top)
+    own_factor, other_factor = jnp.exp(own_top - both), jnp.exp(other_top - both)
+    own_total, other_total = own_total * own_factor, other_total * other_factor
+    total = jnp.where(first, own_total, other_total) + jnp.where(first, other_total, own_total)
     inverse = 1.0 / total
-    cache_factor = jnp.exp(cache_stats_ref[:requests, :] - both) * inverse
-    new_factor = jnp.exp(new_stats_ref[...] - both) * inverse
-    for h in range(columns // size):
+    sides = []
+    for ref, far_ref, factor, new in (
+        (own_ref, own_far_ref, own_factor, own_new),
+        (other_ref, other_far_ref, other_factor, other_new),
+    ):
+        factor = factor * inverse
+        sides.append((ref, far_ref, factor, factor * new))
+    for h in range(count):
         at = slice(h * size, (h + 1) * size)
-        factor = jnp.broadcast_to(new_factor[:, h : h + 1], (requests, size))
-        factor_ref[:, at] = factor
-        base_ref[:, at] = cache_ref[:, at] * cache_factor[:, h : h + 1] + own_ref[:, at] * factor
-
-
-def weigh(cache_mixed, own, cache_stats, new_stats, stats, other):
+        terms = [
+            ref[:, at].astype(jnp.float32) * factor[:, h : h + 1]
+            + far_ref[:, at].astype(jnp.float32) * far_factor[:, h : h + 1]
+            for ref, far_ref, factor, far_factor in sides
+        ]
+        out_ref[:, at] = (terms[0] + terms[1]).astype(out_ref.dtype)
+
+
+def finish(count, columns, own, other, own_far, other_far):
+    arrived = (other, own_far, other_far)
     return pl.pallas_call(
-        weigh_kernel,
-        out_shape=[jax.ShapeDtypeStruct(own.shape, jnp.float32)] * 2,
-        compiler_params=params(),
-        name="weigh",
-    )(cache_mixed, own, cache_stats, new_stats, stats, other)
-
-
-def merge_kernel(base_ref, factor_ref, far_ref, out_ref):
-    out = base_ref[...] + far_ref[...].astype(jnp.float32) * factor_ref[...]
-    out_ref[...] = out.astype(out_ref.dtype)
-
-
-def merge(base, factor, far):
-    return pl.pallas_call(
-        merge_kernel,
-        out_shape=jax.ShapeDtypeStruct(far.shape, far.dtype),
-        compiler_params=params(),
-        name="merge",
-    )(base, factor, far)
-
-
-def finish_kernel(own_ref, other_ref, out_ref):
-    out_ref[...] = (own_ref[...].astype(jnp.float32) + other_ref[...].astype(jnp.float32)).astype(out_ref.dtype)
-
-
-def finish(own, other):
-    return pl.pallas_call(
-        finish_kernel,
-        out_shape=jax.ShapeDtypeStruct(own.shape, own.dtype),
+        functools.partial(finish_kernel, count),
+        out_shape=jax.ShapeDtypeStruct((own.shape[0], columns), jnp.bfloat16),
         compiler_params=params(),
         name="finish",
-    )(own, other)
+    )(own, *[arrived[FINISH_PLACES.index(i)] for i in range(3)])
 
 
 def from_partner(x, axis, distance):
@@ -386,12 +399,17 @@
     scores, code = partial_scores(heads, columns, keys, messages)
     scores = [scores] + [from_behind(scores, "seq", d) for d in range(1, seq_count)]
     cache_mixed, cache_stats = cache_part(lengths, query, kv_cache[0, 0], signs)
-    own, far, new_stats, stats = mix(heads, code, values, near_values, cache_stats, scores)
-    far = from_partner(far, "seq", 2)
-    other = from_partner(stats, "tp", 1)
-    base, factor = weigh(cache_mixed, own, cache_stats, new_stats, stats, other)
-    share = merge(base, factor, far)
-    return finish(share, from_partner(share, "tp", 1)).reshape(1, 1, request_count, columns)
+    share, far = mix(heads, code, values, near_values, cache_mixed, cache_stats, scores)
+    far_pairs = [(i, i ^ 5) for i in range(2 * seq_count)]
+    output = finish(
+        columns // signs.shape[1],
+        columns,
+        share,
+        from_partner(share, "tp", 1),
+        from_partner(far, "seq", 2),
+        lax.ppermute(far, ("seq", "tp"), far_pairs),
+    )
+    return output.reshape(1, 1, request_count, columns)
 
 
 def hadamard(order):

time: 30.1 us -> 29.2 us (0.970)
  waiting for transfers between devices: 7.4 us -> 6.08 us
    ppermute x7 -> x6, waiting for transfers between devices: 6.55 us -> 2.53 us  [from_partner(): return lax.ppermute(x, axis, [(i, i ^ distance) for i in range(count)])]
    ppermute x0 -> x1, waiting for transfers between devices: none -> 2.7 us  [on_device(): lax.ppermute(far, ('seq', 'tp'), far_pairs)]
    ppermute x0 -> x1, starting transfers between devices: none -> 2.12 us  [on_device(): lax.ppermute(far, ('seq', 'tp'), far_pairs)]
    ppermute x7 -> x6, starting transfers between devices: 11.5 us -> 9.55 us  [from_partner(): return lax.ppermute(x, axis, [(i, i ^ distance) for i in range(count)])]
    pallas_call x3 -> x1, Pallas kernels: 0.86 us -> 0.99 us  [finish(): pl.pallas_call(functools.partial(finish_kernel, count), out_shape=jax.Sha...]
  transfers between devices with their start and end apart: 10 -> 10, of which waited for: 6 -> 5; matrix products, arithmetic and copies ran while one was open for 0% -> 0% of each run, Pallas kernels for 15% -> 15%
where the time goes in v19:
time: 29.2 us; the launch traced here: 29 us
  starting transfers between devices  16.2 us (55%)
  Pallas kernels  6.66 us (23%)
  waiting for transfers between devices  6.08 us (21%)
    ppermute x6, starting transfers between devices, from_partner(): return lax.ppermute(x, axis, [(i, i ^ distance) for i in range(count)])  9.55 us
    ppermute x3, starting transfers between devices, from_behind(): lax.ppermute(x, axis, [(i, (i + distance) % count) for i in range(count)])  4.52 us
    ppermute x1, waiting for transfers between devices, on_device(): lax.ppermute(far, ('seq', 'tp'), far_pairs)  2.7 us
    ppermute x6, waiting for transfers between devices, from_partner(): return lax.ppermute(x, axis, [(i, i ^ distance) for i in range(count)])  2.53 us
    pallas_call x1, Pallas kernels, project(): pl.pallas_call(project_kernel, in_specs=[vmem] * 2, out_specs=[vmem] * 2,...  2.32 us
    ppermute x1, starting transfers between devices, on_device(): lax.ppermute(far, ('seq', 'tp'), far_pairs)  2.12 us
    pallas_call x1, Pallas kernels, cache_part(): pl.pallas_call(cache_kernel, in_specs=[pl.BlockSpec(memory_space=pltpu.SM...  1.6 us
    pallas_call x1, Pallas kernels, make_message(): pl.pallas_call(message_kernel, in_specs=[pl.BlockSpec(memory_space=pl.ANY...  1.01 us
  transfers between devices with their start and end apart: 10, of which 5 were waited for; matrix products, arithmetic and copies ran while one was open for 0% of the time, Pallas kernels for 15%

profile of v19, /device:TPU:0, one launch (start us, length us, event | category | flops | bytes accessed | tf_op | source)
XLA Modules:
  0.0 29.0 jit_solution(10356010332642044706)
XLA Ops:
  0.0 1.0 %make_message.1.refs_0_ = bf16[8,4224]{1,0:T(8,128)(2,1)S(1)} custom-call(bf16[8,4096]{1,0:T(8,128)(2,1)} %bitcast.7, s32[1,64]{1,0:T(1,128)} %bitcast.9, s32[1,64]{1,0:T(1,128)} %requests_ref.1), custom_call_target="tpu_custom_call" | custom-call | flops 99999997952 | bytes 10000 | tf_op jit(solution)/shard_map/make_message/pallas_call | solution.py:100
  1.0 5.1 %collective-permute-start = (bf16[8,4224]{1,0:T(8,128)(2,1)S(1)}, bf16[8,4224]{1,0:T(8,128)(2,1)S(1)}, u32[]{:S(2)}, u32[]{:S(2)}) collective-permute-start(bf16[8,4224]{1,0:T(8,128)(2,1)S(1)} %make_message.1.refs_0_), channel_id=1, source_target_pairs={{0,12},{4,8},{8,4},{12,0},{1,13},{5,9},{9,5},{13,1},{2,14},{6,10},... | collective-permute-start | bytes 202760 | tf_op jit(solution)/shard_map/ppermute | solution.py:382
  6.2 0.0 collective-permute-start.1
  6.2 0.6 %collective-permute-start.2 = (bf16[8,4224]{1,0:T(8,128)(2,1)S(1)}, bf16[8,4224]{1,0:T(8,128)(2,1)S(1)}, u32[]{:S(2)}, u32[]{:S(2)}) collective-permute-start(bf16[8,4224]{1,0:T(8,128)(2,1)S(1)} %make_message.1.refs_0_), channel_id=1, source_target_pairs={{0,4},{4,0},{8,12},{12,8},{1,5},{5,1},{9,13},{13,9},{2,6},{6,2},{1... | collective-permute-start | bytes 202760 | tf_op jit(solution)/shard_map/ppermute | solution.py:382
  6.8 2.3 %project.1 = (bf16[256,512]{1,0:T(8,128)(2,1)S(1)}, bf16[256,512]{1,0:T(8,128)(2,1)S(1)}) custom-call(bf16[256,4096]{1,0:T(8,128)(2,1)S(1)} %copy-done, bf16[4096,1024]{1,0:T(8,128)(2,1)S(1)} %bitcast.5), custom_call_target="tpu_custom_call" | custom-call | flops 2147483648 | bytes 10485760 | tf_op jit(solution)/shard_map/project/pallas_call | solution.py:63
  9.1 1.5 %collective-permute-start.3 = (bf16[256,512]{1,0:T(8,128)(2,1)S(1)}, bf16[256,512]{1,0:T(8,128)(2,1)S(1)}, u32[]{:S(2)}, u32[]{:S(2)}) collective-permute-start(bf16[256,512]{1,0:T(8,128)(2,1)S(1)} %get-tuple-element.15.values_ref), channel_id=1, source_target_pairs={{0,4},{4,0},{8,12},{12,8},{1,5},{5,1},{9,13},{13,9},{2,6},{6,2},{1... | collective-permute-start | bytes 786440 | tf_op jit(solution)/shard_map/ppermute | solution.py:382
  10.6 0.0 collective-permute-done.refs_1_
  10.6 1.4 %collective-permute-done.1.refs_2_ = bf16[8,4224]{1,0:T(8,128)(2,1)S(1)} collective-permute-done((bf16[8,4224]{1,0:T(8,128)(2,1)S(1)}, bf16[8,4224]{1,0:T(8,128)(2,1)S(1)}, u32[]{:S(2)}, u32[]{:S(2)}) %collective-permute-start.1) | collective-permute-done | bytes 67616 | tf_op jit(solution)/shard_map/ppermute | solution.py:382
  12.0 0.0 collective-permute-done.2.refs_3_
  12.0 0.0 copy-start.4
  12.0 0.3 %partial_scores.1 = (bf16[32,256]{1,0:T(8,128)(2,1)S(1)}, s32[8,256]{1,0:T(8,128)S(1)}) custom-call(bf16[256,512]{1,0:T(8,128)(2,1)S(1)} %get-tuple-element.13.keys_ref, bf16[8,4224]{1,0:T(8,128)(2,1)S(1)} %make_message.1.refs_0_, bf16[8,4224]{1,0:T(8,128)(2,1)S(1)} %collective-permute-done.refs_1_, bf16[8,4224]{1,0:T(8,128)(2,1)S(1)} %collective-permute-done.1.refs_2_, ...), custom_call_target="tpu_custom_call" | custom-call | flops 99999997952 | bytes 10000 | tf_op jit(solution)/shard_map/partial_scores/pallas_call | solution.py:245
  12.3 1.5 %collective-permute-start.4 = (bf16[32,256]{1,0:T(8,128)(2,1)S(1)}, bf16[32,256]{1,0:T(8,128)(2,1)S(1)}, u32[]{:S(2)}, u32[]{:S(2)}) collective-permute-start(bf16[32,256]{1,0:T(8,128)(2,1)S(1)} %get-tuple-element.18.refs_0_), channel_id=1, source_target_pairs={{0,4},{4,8},{8,12},{12,0},{1,5},{5,9},{9,13},{13,1},{2,6},{6,10},{... | collective-permute-start | bytes 49160 | tf_op jit(solution)/shard_map/ppermute | solution.py:387
  13.8 1.8 %collective-permute-start.5 = (bf16[32,256]{1,0:T(8,128)(2,1)S(1)}, bf16[32,256]{1,0:T(8,128)(2,1)S(1)}, u32[]{:S(2)}, u32[]{:S(2)}) collective-permute-start(bf16[32,256]{1,0:T(8,128)(2,1)S(1)} %get-tuple-element.18.refs_0_), channel_id=1, source_target_pairs={{0,8},{4,12},{8,0},{12,4},{1,9},{5,13},{9,1},{13,5},{2,10},{6,14},... | collective-permute-start | bytes 49160 | tf_op jit(solution)/shard_map/ppermute | solution.py:387
  15.6 1.3 %collective-permute-start.6 = (bf16[32,256]{1,0:T(8,128)(2,1)S(1)}, bf16[32,256]{1,0:T(8,128)(2,1)S(1)}, u32[]{:S(2)}, u32[]{:S(2)}) collective-permute-start(bf16[32,256]{1,0:T(8,128)(2,1)S(1)} %get-tuple-element.18.refs_0_), channel_id=1, source_target_pairs={{0,12},{4,0},{8,4},{12,8},{1,13},{5,1},{9,5},{13,9},{2,14},{6,2},{... | collective-permute-start | bytes 49160 | tf_op jit(solution)/shard_map/ppermute | solution.py:387
  16.9 1.6 %cache_part.1 = (f32[8,4096]{1,0:T(8,128)S(1)}, f32[16,128]{1,0:T(8,128)S(1)}) custom-call(s32[1,1,8]{2,1,0:T(1,128)S(1)} %copy-done.4, bf16[8,4096]{1,0:T(8,128)(2,1)S(1)} %bitcast.8, bf16[8,128,1024]{2,1,0:T(8,128)(2,1)S(1)} %bitcast.6, s32[8,128]{1,0:T(8,128)S(1)} %copy-done.3), custom_call_target="tpu_custom_call" | custom-call | flops 16777216 | bytes 2097152 | tf_op jit(solution)/shard_map/cache_part/pallas_call | solution.py:189
  18.5 0.6 %collective-permute-done.4.refs_1_ = bf16[32,256]{1,0:T(8,128)(2,1)S(1)} collective-permute-done((bf16[32,256]{1,0:T(8,128)(2,1)S(1)}, bf16[32,256]{1,0:T(8,128)(2,1)S(1)}, u32[]{:S(2)}, u32[]{:S(2)}) %collective-permute-start.4) | collective-permute-done | bytes 16416 | tf_op jit(solution)/shard_map/ppermute | solution.py:387
  19.1 0.2 collective-permute-done.6.refs_3_
  19.3 0.4 %mix.1 = (bf16[8,4480]{1,0:T(8,128)(2,1)S(1)}, bf16[8,4480]{1,0:T(8,128)(2,1)S(1)}) custom-call(s32[8,256]{1,0:T(8,128)S(1)} %get-tuple-element.14.code_ref, bf16[256,512]{1,0:T(8,128)(2,1)S(1)} %get-tuple-element.15.values_ref, bf16[256,512]{1,0:T(8,128)(2,1)S(1)} %collective-permute-done.3.near_ref, f32[8,4096]{1,0:T(8,128)S(1)} %get-tuple-element.16.cache_ref, ...), custom_call_target="tpu_custom_call" | custom-call | tf_op jit(solution)/shard_map/mix/pallas_call | solution.py:323
  19.8 2.1 %collective-permute-start.7 = (bf16[8,4480]{1,0:T(8,128)(2,1)S(1)}, bf16[8,4480]{1,0:T(8,128)(2,1)S(1)}, u32[]{:S(2)}, u32[]{:S(2)}) collective-permute-start(bf16[8,4480]{1,0:T(8,128)(2,1)S(1)} %get-tuple-element.20), channel_id=1, source_target_pairs={{0,10},{2,8},{4,14},{6,12},{8,2},{10,0},{12,6},{14,4},{1,11},{3,9}... | collective-permute-start | bytes 215048 | tf_op jit(solution)/shard_map/ppermute | solution.py:410
  21.9 1.8 %collective-permute-start.8 = (bf16[8,4480]{1,0:T(8,128)(2,1)S(1)}, bf16[8,4480]{1,0:T(8,128)(2,1)S(1)}, u32[]{:S(2)}, u32[]{:S(2)}) collective-permute-start(bf16[8,4480]{1,0:T(8,128)(2,1)S(1)} %get-tuple-element.20), channel_id=1, source_target_pairs={{0,8},{4,12},{8,0},{12,4},{1,9},{5,13},{9,1},{13,5},{2,10},{6,14},... | collective-permute-start | bytes 215048 | tf_op jit(solution)/shard_map/ppermute | solution.py:382
  23.7 0.5 %collective-permute-start.9 = (bf16[8,4480]{1,0:T(8,128)(2,1)S(1)}, bf16[8,4480]{1,0:T(8,128)(2,1)S(1)}, u32[]{:S(2)}, u32[]{:S(2)}) collective-permute-start(bf16[8,4480]{1,0:T(8,128)(2,1)S(1)} %get-tuple-element.19.own_ref), channel_id=1, source_target_pairs={{0,2},{2,0},{1,3},{3,1},{4,6},{6,4},{5,7},{7,5},{8,10},{10,8},{9,1... | collective-permute-start | bytes 215048 | tf_op jit(solution)/shard_map/ppermute | solution.py:382
  24.2 2.7 %collective-permute-done.7.refs_0_ = bf16[8,4480]{1,0:T(8,128)(2,1)S(1)} collective-permute-done((bf16[8,4480]{1,0:T(8,128)(2,1)S(1)}, bf16[8,4480]{1,0:T(8,128)(2,1)S(1)}, u32[]{:S(2)}, u32[]{:S(2)}) %collective-permute-start.7) | collective-permute-done | bytes 71712 | tf_op jit(solution)/shard_map/ppermute | solution.py:410
  26.9 1.1 %collective-permute-done.8.refs_1_ = bf16[8,4480]{1,0:T(8,128)(2,1)S(1)} collective-permute-done((bf16[8,4480]{1,0:T(8,128)(2,1)S(1)}, bf16[8,4480]{1,0:T(8,128)(2,1)S(1)}, u32[]{:S(2)}, u32[]{:S(2)}) %collective-permute-start.8) | collective-permute-done | bytes 71712 | tf_op jit(solution)/shard_map/ppermute | solution.py:382
  28.0 1.0 %finish.1 = bf16[8,4096]{1,0:T(8,128)(2,1)} custom-call(bf16[8,4480]{1,0:T(8,128)(2,1)S(1)} %get-tuple-element.19.own_ref, bf16[8,4480]{1,0:T(8,128)(2,1)S(1)} %collective-permute-done.7.refs_0_, bf16[8,4480]{1,0:T(8,128)(2,1)S(1)} %collective-permute-done.8.refs_1_, bf16[8,4480]{1,0:T(8,128)(2,1)S(1)} %collective-permute-done.9.refs_2_), custom_call_target="tpu_custom_call" | custom-call | tf_op jit(solution)/shard_map/finish/pallas_call | solution.py:372
  (17 shorter events, 0.0 us)
Async XLA Ops:
  0.0 6.8 %slice-start = ((s8[8388608]{0:T(1024)(128)(4,1)}), s8[4194304]{0:T(1024)(128)(4,1)S(1)}, s32[]{:S(2)}) async-start(s8[8388608]{0:T(1024)(128)(4,1)} %bitcast.4), calls=%async_computation | async-start | bytes 8388608
  0.0 6.8 %slice-start.1 = ((s8[8388608]{0:T(1024)(128)(4,1)}), s8[4194304]{0:T(1024)(128)(4,1)S(1)}, s32[]{:S(2)}) async-start(s8[8388608]{0:T(1024)(128)(4,1)} %bitcast.4), calls=%async_computation.1 | async-start | bytes 8388608
  0.0 6.8 %copy-start = (bf16[256,4096]{1,0:T(8,128)(2,1)S(1)}, bf16[256,4096]{1,0:T(8,128)(2,1)}, u32[]{:S(2)}) copy-start(bf16[256,4096]{1,0:T(8,128)(2,1)} %tokens_ref.1) | copy-start | bytes 6291460
  1.0 9.6 %collective-permute-start = (bf16[8,4224]{1,0:T(8,128)(2,1)S(1)}, bf16[8,4224]{1,0:T(8,128)(2,1)S(1)}, u32[]{:S(2)}, u32[]{:S(2)}) collective-permute-start(bf16[8,4224]{1,0:T(8,128)(2,1)S(1)} %make_message.1.refs_0_), channel_id=1, source_target_pairs={{0,12},{4,8},{8,4},{12,0},{1,13},{5,9},{9,5},{13,1},{2,14},{6,10},... | collective-permute-start | bytes 202760 | tf_op jit(solution)/shard_map/ppermute | solution.py:382
  6.2 5.8 %collective-permute-start.1 = (bf16[8,4224]{1,0:T(8,128)(2,1)S(1)}, bf16[8,4224]{1,0:T(8,128)(2,1)S(1)}, u32[]{:S(2)}, u32[]{:S(2)}) collective-permute-start(bf16[8,4224]{1,0:T(8,128)(2,1)S(1)} %make_message.1.refs_0_), channel_id=1, source_target_pairs={{0,8},{4,12},{8,0},{12,4},{1,9},{5,13},{9,1},{13,5},{2,10},{6,14},... | collective-permute-start | bytes 202760 | tf_op jit(solution)/shard_map/ppermute | solution.py:382
  6.2 5.8 %collective-permute-start.2 = (bf16[8,4224]{1,0:T(8,128)(2,1)S(1)}, bf16[8,4224]{1,0:T(8,128)(2,1)S(1)}, u32[]{:S(2)}, u32[]{:S(2)}) collective-permute-start(bf16[8,4224]{1,0:T(8,128)(2,1)S(1)} %make_message.1.refs_0_), channel_id=1, source_target_pairs={{0,4},{4,0},{8,12},{12,8},{1,5},{5,1},{9,13},{13,9},{2,6},{6,2},{1... | collective-permute-start | bytes 202760 | tf_op jit(solution)/shard_map/ppermute | solution.py:382
  9.1 10.2 %collective-permute-start.3 = (bf16[256,512]{1,0:T(8,128)(2,1)S(1)}, bf16[256,512]{1,0:T(8,128)(2,1)S(1)}, u32[]{:S(2)}, u32[]{:S(2)}) collective-permute-start(bf16[256,512]{1,0:T(8,128)(2,1)S(1)} %get-tuple-element.15.values_ref), channel_id=1, source_target_pairs={{0,4},{4,0},{8,12},{12,8},{1,5},{5,1},{9,13},{13,9},{2,6},{6,2},{1... | collective-permute-start | bytes 786440 | tf_op jit(solution)/shard_map/ppermute | solution.py:382
  12.0 4.9 %copy-start.1 = (bf16[1,1,8,128,1024]{4,3,2,1,0:T(8,128)(2,1)S(1)}, bf16[1,1,8,128,1024]{4,3,2,1,0:T(8,128)(2,1)}, u32[]{:S(2)}) copy-start(bf16[1,1,8,128,1024]{4,3,2,1,0:T(8,128)(2,1)} %param.14) | copy-start | bytes 6291460
  12.0 4.9 %copy-start.2 = (bf16[1,1,8,4096]{3,2,1,0:T(8,128)(2,1)S(1)}, bf16[1,1,8,4096]{3,2,1,0:T(8,128)(2,1)}, u32[]{:S(2)}) copy-start(bf16[1,1,8,4096]{3,2,1,0:T(8,128)(2,1)} %param.13) | copy-start | bytes 196612
  12.0 4.9 %copy-start.3 = (s32[8,128]{1,0:T(8,128)S(1)}, s32[8,128]{1,0:T(8,128)}, u32[]{:S(2)}) copy-start(s32[8,128]{1,0:T(8,128)} %signs_ref.1) | copy-start | bytes 12292
  12.0 4.9 %copy-start.4 = (s32[1,1,8]{2,1,0:T(1,128)S(1)}, s32[1,1,8]{2,1,0:T(1,128)}, u32[]{:S(2)}) copy-start(s32[1,1,8]{2,1,0:T(1,128)} %lengths_ref.1) | copy-start | bytes 100
  12.3 6.8 %collective-permute-start.4 = (bf16[32,256]{1,0:T(8,128)(2,1)S(1)}, bf16[32,256]{1,0:T(8,128)(2,1)S(1)}, u32[]{:S(2)}, u32[]{:S(2)}) collective-permute-start(bf16[32,256]{1,0:T(8,128)(2,1)S(1)} %get-tuple-element.18.refs_0_), channel_id=1, source_target_pairs={{0,4},{4,8},{8,12},{12,0},{1,5},{5,9},{9,13},{13,1},{2,6},{6,10},{... | collective-permute-start | bytes 49160 | tf_op jit(solution)/shard_map/ppermute | solution.py:387
  13.8 5.3 %collective-permute-start.5 = (bf16[32,256]{1,0:T(8,128)(2,1)S(1)}, bf16[32,256]{1,0:T(8,128)(2,1)S(1)}, u32[]{:S(2)}, u32[]{:S(2)}) collective-permute-start(bf16[32,256]{1,0:T(8,128)(2,1)S(1)} %get-tuple-element.18.refs_0_), channel_id=1, source_target_pairs={{0,8},{4,12},{8,0},{12,4},{1,9},{5,13},{9,1},{13,5},{2,10},{6,14},... | collective-permute-start | bytes 49160 | tf_op jit(solution)/shard_map/ppermute | solution.py:387
  15.6 3.7 %collective-permute-start.6 = (bf16[32,256]{1,0:T(8,128)(2,1)S(1)}, bf16[32,256]{1,0:T(8,128)(2,1)S(1)}, u32[]{:S(2)}, u32[]{:S(2)}) collective-permute-start(bf16[32,256]{1,0:T(8,128)(2,1)S(1)} %get-tuple-element.18.refs_0_), channel_id=1, source_target_pairs={{0,12},{4,0},{8,4},{12,8},{1,13},{5,1},{9,5},{13,9},{2,14},{6,2},{... | collective-permute-start | bytes 49160 | tf_op jit(solution)/shard_map/ppermute | solution.py:387
  19.8 7.2 %collective-permute-start.7 = (bf16[8,4480]{1,0:T(8,128)(2,1)S(1)}, bf16[8,4480]{1,0:T(8,128)(2,1)S(1)}, u32[]{:S(2)}, u32[]{:S(2)}) collective-permute-start(bf16[8,4480]{1,0:T(8,128)(2,1)S(1)} %get-tuple-element.20), channel_id=1, source_target_pairs={{0,10},{2,8},{4,14},{6,12},{8,2},{10,0},{12,6},{14,4},{1,11},{3,9}... | collective-permute-start | bytes 215048 | tf_op jit(solution)/shard_map/ppermute | solution.py:410
  21.9 6.2 %collective-permute-start.8 = (bf16[8,4480]{1,0:T(8,128)(2,1)S(1)}, bf16[8,4480]{1,0:T(8,128)(2,1)S(1)}, u32[]{:S(2)}, u32[]{:S(2)}) collective-permute-start(bf16[8,4480]{1,0:T(8,128)(2,1)S(1)} %get-tuple-element.20), channel_id=1, source_target_pairs={{0,8},{4,12},{8,0},{12,4},{1,9},{5,13},{9,1},{13,5},{2,10},{6,14},... | collective-permute-start | bytes 215048 | tf_op jit(solution)/shard_map/ppermute | solution.py:382
  23.7 4.4 %collective-permute-start.9 = (bf16[8,4480]{1,0:T(8,128)(2,1)S(1)}, bf16[8,4480]{1,0:T(8,128)(2,1)S(1)}, u32[]{:S(2)}, u32[]{:S(2)}) collective-permute-start(bf16[8,4480]{1,0:T(8,128)(2,1)S(1)} %get-tuple-element.19.own_ref), channel_id=1, source_target_pairs={{0,2},{2,0},{1,3},{3,1},{4,6},{6,4},{5,7},{7,5},{8,10},{10,8},{9,1... | collective-permute-start | bytes 215048 | tf_op jit(solution)/shard_map/ppermute | solution.py:382

commit v20 on v19

--- a/solution.py
+++ b/solution.py
@@ -37,7 +37,7 @@
 
 QUERY_ORDER = (3, 2, 1)
 SCORE_ORDER = (1, 2, 3)
-FINISH_PLACES = (2, 1, 0)
+FINISH_PLACES = (2, 0, 1)
 
 
 def arranged(blocks, order):
@@ -254,18 +254,25 @@
     )(keys, *arranged(messages, QUERY_ORDER))
 
 
-def packed(value, count):
-    lane = lax.broadcasted_iota(jnp.int32, value.shape, 1)
-    high = value.astype(jnp.bfloat16).astype(jnp.float32)
-    middle = (value - high).astype(jnp.bfloat16).astype(jnp.float32)
-    low = value - high - middle
-    middle, low = pltpu.roll(middle, count, 1), pltpu.roll(low, 2 * count, 1)
-    return jnp.where(lane < count, high, jnp.where(lane < 2 * count, middle, low))
-
-
-def unpacked(message, at, count):
-    parts = [message[:, at + part * count : at + (part + 1) * count] for part in range(3)]
-    return parts[0] + parts[1] + parts[2]
+def packed(values, count):
+    rows, lanes = values[0].shape
+    lane = lax.broadcasted_iota(jnp.int32, (rows, lanes), 1)
+    tiles = [jnp.zeros((rows, lanes), jnp.float32)] * (8 * count // lanes)
+    slot = 0
+    for value, parts in zip(values, (3, 3, 2)):
+        for _ in range(parts):
+            piece = value.astype(jnp.bfloat16).astype(jnp.float32)
+            value = value - piece
+            tile, at = divmod(slot * count, lanes)
+            here = (lane >= at) & (lane < at + count)
+            tiles[tile] = jnp.where(here, pltpu.roll(piece, at, 1) if at else piece, tiles[tile])
+            slot += 1
+    return jnp.concatenate(tiles, axis=1)
+
+
+def unpacked(message, count):
+    parts = [message[:, at * count : (at + 1) * count] for at in range(8)]
+    return parts[0] + parts[1] + parts[2], parts[3] + parts[4] + parts[5], parts[6] + parts[7]
 
 
 def mix_kernel(heads, requests, code_ref, values_ref, near_ref, cache_ref, cache_stats_ref, *refs):
@@ -311,19 +318,17 @@
         at = slice(h * size, (h + 1) * size)
         share = cache_ref[:, at] * cache_factor[:, h : h + 1] + part * new_factor[:, h : h + 1]
         share_ref[:, at] = share.astype(share_ref.dtype)
-    lanes = cache_stats_ref.shape[1]
-    far_ref[:, columns:] = jnp.zeros((requests, 3 * lanes), far_ref.dtype)
-    for i, value in enumerate((both, total, new_factor)):
-        share_ref[:, columns + i * lanes : columns + (i + 1) * lanes] = packed(value, count).astype(share_ref.dtype)
+    far_ref[:, columns:] = jnp.zeros((requests, 8 * count), far_ref.dtype)
+    share_ref[:, columns:] = packed((both, total, new_factor), count).astype(share_ref.dtype)
 
 
 def mix(heads, code, values, near_values, cache_mixed, cache_stats, scores):
-    requests, lanes = cache_stats.shape[0] // 2, cache_stats.shape[1]
-    columns = cache_mixed.shape[1]
+    requests, columns = cache_mixed.shape
+    count = columns // (values.shape[1] // heads)
     return pl.pallas_call(
         functools.partial(mix_kernel, heads, requests),
         out_shape=[
-            jax.ShapeDtypeStruct((requests, columns + 3 * lanes), jnp.bfloat16),
+            jax.ShapeDtypeStruct((requests, columns + 8 * count), jnp.bfloat16),
         ]
         * 2,
         compiler_params=params(),
@@ -336,15 +341,9 @@
     other_ref, own_far_ref, other_far_ref = [refs[i] for i in FINISH_PLACES]
     columns = out_ref.shape[1]
     size = columns // count
-    lanes = (own_ref.shape[1] - columns) // 3
     first = lax.axis_index("tp") == 0
-
-    def stats(ref):
-        message = ref[:, columns:].astype(jnp.float32)
-        return [unpacked(message, i * lanes, count) for i in range(3)]
-
-    own_top, own_total, own_new = stats(own_ref)
-    other_top, other_total, other_new = stats(other_ref)
+    own_top, own_total, own_new = unpacked(own_ref[:, columns:].astype(jnp.float32), count)
+    other_top, other_total, other_new = unpacked(other_ref[:, columns:].astype(jnp.float32), count)
     both = jnp.maximum(own_top, other_top)
     own_factor, other_factor = jnp.exp(own_top - both), jnp.exp(other_top - both)
     own_total, other_total = own_total * own_factor, other_total * other_factor

time: 29.2 us -> 29.7 us (1.017)
  waiting for transfers between devices: 6.08 us -> 6.49 us
    ppermute x6, waiting for transfers between devices: 2.53 us -> 4.43 us  [from_partner(): return lax.ppermute(x, axis, [(i, i ^ distance) for i in range(count)])]
    ppermute x1, waiting for transfers between devices: 2.7 us -> 1.21 us  [on_device(): lax.ppermute(far, ('seq', 'tp'), far_pairs)]
    ppermute x6, starting transfers between devices: 9.55 us -> 8.95 us  [from_partner(): return lax.ppermute(x, axis, [(i, i ^ distance) for i in range(count)])]
    ppermute x1, starting transfers between devices: 2.12 us -> 2.72 us  [on_device(): lax.ppermute(far, ('seq', 'tp'), far_pairs)]
  transfers between devices with their start and end apart: 10 -> 10, of which waited for: 5 -> 6; matrix products, arithmetic and copies ran while one was open for 0% -> 0% of each run, Pallas kernels for 15% -> 14%
where the time goes in v20:
time: 29.7 us; the launch traced here: 29.6 us
  starting transfers between devices  16.2 us (55%)
  Pallas kernels  6.81 us (23%)
  waiting for transfers between devices  6.49 us (22%)
    ppermute x6, starting transfers between devices, from_partner(): return lax.ppermute(x, axis, [(i, i ^ distance) for i in range(count)])  8.95 us
    ppermute x3, starting transfers between devices, from_behind(): lax.ppermute(x, axis, [(i, (i + distance) % count) for i in range(count)])  4.52 us
    ppermute x6, waiting for transfers between devices, from_partner(): return lax.ppermute(x, axis, [(i, i ^ distance) for i in range(count)])  4.43 us
    ppermute x1, starting transfers between devices, on_device(): lax.ppermute(far, ('seq', 'tp'), far_pairs)  2.72 us
    pallas_call x1, Pallas kernels, project(): pl.pallas_call(project_kernel, in_specs=[vmem] * 2, out_specs=[vmem] * 2,...  2.32 us
    pallas_call x1, Pallas kernels, cache_part(): pl.pallas_call(cache_kernel, in_specs=[pl.BlockSpec(memory_space=pltpu.SM...  1.6 us
    ppermute x1, waiting for transfers between devices, on_device(): lax.ppermute(far, ('seq', 'tp'), far_pairs)  1.21 us
    pallas_call x1, Pallas kernels, finish(): pl.pallas_call(functools.partial(finish_kernel, count), out_shape=jax.Sha...  1.13 us
  transfers between devices with their start and end apart: 10, of which 6 were waited for; matrix products, arithmetic and copies ran while one was open for 0% of the time, Pallas kernels for 14%

profile of v20, /device:TPU:0, one launch (start us, length us, event | category | flops | bytes accessed | tf_op | source)
XLA Modules:
  0.0 29.6 jit_solution(7873944841467331094)
XLA Ops:
  0.0 1.0 %make_message.1.refs_0_ = bf16[8,4224]{1,0:T(8,128)(2,1)S(1)} custom-call(bf16[8,4096]{1,0:T(8,128)(2,1)} %bitcast.7, s32[1,64]{1,0:T(1,128)} %bitcast.9, s32[1,64]{1,0:T(1,128)} %requests_ref.1), custom_call_target="tpu_custom_call" | custom-call | flops 99999997952 | bytes 10000 | tf_op jit(solution)/shard_map/make_message/pallas_call | solution.py:100
  1.0 5.1 %collective-permute-start = (bf16[8,4224]{1,0:T(8,128)(2,1)S(1)}, bf16[8,4224]{1,0:T(8,128)(2,1)S(1)}, u32[]{:S(2)}, u32[]{:S(2)}) collective-permute-start(bf16[8,4224]{1,0:T(8,128)(2,1)S(1)} %make_message.1.refs_0_), channel_id=1, source_target_pairs={{0,12},{4,8},{8,4},{12,0},{1,13},{5,9},{9,5},{13,1},{2,14},{6,10},... | collective-permute-start | bytes 202760 | tf_op jit(solution)/shard_map/ppermute | solution.py:381
  6.2 0.6 %collective-permute-start.2 = (bf16[8,4224]{1,0:T(8,128)(2,1)S(1)}, bf16[8,4224]{1,0:T(8,128)(2,1)S(1)}, u32[]{:S(2)}, u32[]{:S(2)}) collective-permute-start(bf16[8,4224]{1,0:T(8,128)(2,1)S(1)} %make_message.1.refs_0_), channel_id=1, source_target_pairs={{0,4},{4,0},{8,12},{12,8},{1,5},{5,1},{9,13},{13,9},{2,6},{6,2},{1... | collective-permute-start | bytes 202760 | tf_op jit(solution)/shard_map/ppermute | solution.py:381
  6.8 2.3 %project.1 = (bf16[256,512]{1,0:T(8,128)(2,1)S(1)}, bf16[256,512]{1,0:T(8,128)(2,1)S(1)}) custom-call(bf16[256,4096]{1,0:T(8,128)(2,1)S(1)} %copy-done, bf16[4096,1024]{1,0:T(8,128)(2,1)S(1)} %bitcast.5), custom_call_target="tpu_custom_call" | custom-call | flops 2147483648 | bytes 10485760 | tf_op jit(solution)/shard_map/project/pallas_call | solution.py:63
  9.1 1.5 %collective-permute-start.3 = (bf16[256,512]{1,0:T(8,128)(2,1)S(1)}, bf16[256,512]{1,0:T(8,128)(2,1)S(1)}, u32[]{:S(2)}, u32[]{:S(2)}) collective-permute-start(bf16[256,512]{1,0:T(8,128)(2,1)S(1)} %get-tuple-element.15.values_ref), channel_id=1, source_target_pairs={{0,4},{4,0},{8,12},{12,8},{1,5},{5,1},{9,13},{13,9},{2,6},{6,2},{1... | collective-permute-start | bytes 786440 | tf_op jit(solution)/shard_map/ppermute | solution.py:381
  10.6 0.0 collective-permute-done.refs_1_
  10.6 1.4 %collective-permute-done.1.refs_2_ = bf16[8,4224]{1,0:T(8,128)(2,1)S(1)} collective-permute-done((bf16[8,4224]{1,0:T(8,128)(2,1)S(1)}, bf16[8,4224]{1,0:T(8,128)(2,1)S(1)}, u32[]{:S(2)}, u32[]{:S(2)}) %collective-permute-start.1) | collective-permute-done | bytes 67616 | tf_op jit(solution)/shard_map/ppermute | solution.py:381
  12.0 0.0 copy-start.4
  12.0 0.3 %partial_scores.1 = (bf16[32,256]{1,0:T(8,128)(2,1)S(1)}, s32[8,256]{1,0:T(8,128)S(1)}) custom-call(bf16[256,512]{1,0:T(8,128)(2,1)S(1)} %get-tuple-element.13.keys_ref, bf16[8,4224]{1,0:T(8,128)(2,1)S(1)} %make_message.1.refs_0_, bf16[8,4224]{1,0:T(8,128)(2,1)S(1)} %collective-permute-done.refs_1_, bf16[8,4224]{1,0:T(8,128)(2,1)S(1)} %collective-permute-done.1.refs_2_, ...), custom_call_target="tpu_custom_call" | custom-call | flops 99999997952 | bytes 10000 | tf_op jit(solution)/shard_map/partial_scores/pallas_call | solution.py:245
  12.3 1.5 %collective-permute-start.4 = (bf16[32,256]{1,0:T(8,128)(2,1)S(1)}, bf16[32,256]{1,0:T(8,128)(2,1)S(1)}, u32[]{:S(2)}, u32[]{:S(2)}) collective-permute-start(bf16[32,256]{1,0:T(8,128)(2,1)S(1)} %get-tuple-element.18.refs_0_), channel_id=1, source_target_pairs={{0,4},{4,8},{8,12},{12,0},{1,5},{5,9},{9,13},{13,1},{2,6},{6,10},{... | collective-permute-start | bytes 49160 | tf_op jit(solution)/shard_map/ppermute | solution.py:386
  13.8 1.8 %collective-permute-start.5 = (bf16[32,256]{1,0:T(8,128)(2,1)S(1)}, bf16[32,256]{1,0:T(8,128)(2,1)S(1)}, u32[]{:S(2)}, u32[]{:S(2)}) collective-permute-start(bf16[32,256]{1,0:T(8,128)(2,1)S(1)} %get-tuple-element.18.refs_0_), channel_id=1, source_target_pairs={{0,8},{4,12},{8,0},{12,4},{1,9},{5,13},{9,1},{13,5},{2,10},{6,14},... | collective-permute-start | bytes 49160 | tf_op jit(solution)/shard_map/ppermute | solution.py:386
  15.6 1.3 %collective-permute-start.6 = (bf16[32,256]{1,0:T(8,128)(2,1)S(1)}, bf16[32,256]{1,0:T(8,128)(2,1)S(1)}, u32[]{:S(2)}, u32[]{:S(2)}) collective-permute-start(bf16[32,256]{1,0:T(8,128)(2,1)S(1)} %get-tuple-element.18.refs_0_), channel_id=1, source_target_pairs={{0,12},{4,0},{8,4},{12,8},{1,13},{5,1},{9,5},{13,9},{2,14},{6,2},{... | collective-permute-start | bytes 49160 | tf_op jit(solution)/shard_map/ppermute | solution.py:386
  16.9 1.6 %cache_part.1 = (f32[8,4096]{1,0:T(8,128)S(1)}, f32[16,128]{1,0:T(8,128)S(1)}) custom-call(s32[1,1,8]{2,1,0:T(1,128)S(1)} %copy-done.4, bf16[8,4096]{1,0:T(8,128)(2,1)S(1)} %bitcast.8, bf16[8,128,1024]{2,1,0:T(8,128)(2,1)S(1)} %bitcast.6, s32[8,128]{1,0:T(8,128)S(1)} %copy-done.3), custom_call_target="tpu_custom_call" | custom-call | flops 16777216 | bytes 2097152 | tf_op jit(solution)/shard_map/cache_part/pallas_call | solution.py:189
  18.5 0.6 %collective-permute-done.4.refs_1_ = bf16[32,256]{1,0:T(8,128)(2,1)S(1)} collective-permute-done((bf16[32,256]{1,0:T(8,128)(2,1)S(1)}, bf16[32,256]{1,0:T(8,128)(2,1)S(1)}, u32[]{:S(2)}, u32[]{:S(2)}) %collective-permute-start.4) | collective-permute-done | bytes 16416 | tf_op jit(solution)/shard_map/ppermute | solution.py:386
  19.1 0.0 collective-permute-done.5.refs_2_
  19.1 0.2 collective-permute-done.6.refs_3_
  19.3 0.4 %mix.1 = (bf16[8,4352]{1,0:T(8,128)(2,1)S(1)}, bf16[8,4352]{1,0:T(8,128)(2,1)S(1)}) custom-call(s32[8,256]{1,0:T(8,128)S(1)} %get-tuple-element.14.code_ref, bf16[256,512]{1,0:T(8,128)(2,1)S(1)} %get-tuple-element.15.values_ref, bf16[256,512]{1,0:T(8,128)(2,1)S(1)} %collective-permute-done.3.near_ref, f32[8,4096]{1,0:T(8,128)S(1)} %get-tuple-element.16.cache_ref, ...), custom_call_target="tpu_custom_call" | custom-call | tf_op jit(solution)/shard_map/mix/pallas_call | solution.py:328
  19.8 1.2 %collective-permute-start.7 = (bf16[8,4352]{1,0:T(8,128)(2,1)S(1)}, bf16[8,4352]{1,0:T(8,128)(2,1)S(1)}, u32[]{:S(2)}, u32[]{:S(2)}) collective-permute-start(bf16[8,4352]{1,0:T(8,128)(2,1)S(1)} %get-tuple-element.20), channel_id=1, source_target_pairs={{0,8},{4,12},{8,0},{12,4},{1,9},{5,13},{9,1},{13,5},{2,10},{6,14},... | collective-permute-start | bytes 208904 | tf_op jit(solution)/shard_map/ppermute | solution.py:381
  21.0 2.7 %collective-permute-start.8 = (bf16[8,4352]{1,0:T(8,128)(2,1)S(1)}, bf16[8,4352]{1,0:T(8,128)(2,1)S(1)}, u32[]{:S(2)}, u32[]{:S(2)}) collective-permute-start(bf16[8,4352]{1,0:T(8,128)(2,1)S(1)} %get-tuple-element.20), channel_id=1, source_target_pairs={{0,10},{2,8},{4,14},{6,12},{8,2},{10,0},{12,6},{14,4},{1,11},{3,9}... | collective-permute-start | bytes 208904 | tf_op jit(solution)/shard_map/ppermute | solution.py:409
  23.7 0.5 %collective-permute-start.9 = (bf16[8,4352]{1,0:T(8,128)(2,1)S(1)}, bf16[8,4352]{1,0:T(8,128)(2,1)S(1)}, u32[]{:S(2)}, u32[]{:S(2)}) collective-permute-start(bf16[8,4352]{1,0:T(8,128)(2,1)S(1)} %get-tuple-element.19.own_ref), channel_id=1, source_target_pairs={{0,2},{2,0},{1,3},{3,1},{4,6},{6,4},{5,7},{7,5},{8,10},{10,8},{9,1... | collective-permute-start | bytes 208904 | tf_op jit(solution)/shard_map/ppermute | solution.py:381
  24.2 2.3 %collective-permute-done.7.refs_0_ = bf16[8,4352]{1,0:T(8,128)(2,1)S(1)} collective-permute-done((bf16[8,4352]{1,0:T(8,128)(2,1)S(1)}, bf16[8,4352]{1,0:T(8,128)(2,1)S(1)}, u32[]{:S(2)}, u32[]{:S(2)}) %collective-permute-start.7) | collective-permute-done | bytes 69664 | tf_op jit(solution)/shard_map/ppermute | solution.py:381
  26.5 1.2 %collective-permute-done.8.refs_1_ = bf16[8,4352]{1,0:T(8,128)(2,1)S(1)} collective-permute-done((bf16[8,4352]{1,0:T(8,128)(2,1)S(1)}, bf16[8,4352]{1,0:T(8,128)(2,1)S(1)}, u32[]{:S(2)}, u32[]{:S(2)}) %collective-permute-start.8) | collective-permute-done | bytes 69664 | tf_op jit(solution)/shard_map/ppermute | solution.py:409
  27.8 0.7 %collective-permute-done.9.refs_2_ = bf16[8,4352]{1,0:T(8,128)(2,1)S(1)} collective-permute-done((bf16[8,4352]{1,0:T(8,128)(2,1)S(1)}, bf16[8,4352]{1,0:T(8,128)(2,1)S(1)}, u32[]{:S(2)}, u32[]{:S(2)}) %collective-permute-start.9) | collective-permute-done | bytes 69664 | tf_op jit(solution)/shard_map/ppermute | solution.py:381
  28.5 1.1 %finish.1 = bf16[8,4096]{1,0:T(8,128)(2,1)} custom-call(bf16[8,4352]{1,0:T(8,128)(2,1)S(1)} %get-tuple-element.19.own_ref, bf16[8,4352]{1,0:T(8,128)(2,1)S(1)} %collective-permute-done.7.refs_0_, bf16[8,4352]{1,0:T(8,128)(2,1)S(1)} %collective-permute-done.8.refs_1_, bf16[8,4352]{1,0:T(8,128)(2,1)S(1)} %collective-permute-done.9.refs_2_), custom_call_target="tpu_custom_call" | custom-call | tf_op jit(solution)/shard_map/finish/pallas_call | solution.py:371
  (17 shorter events, 0.0 us)
Async XLA Ops:
  0.0 6.8 %slice-start = ((s8[8388608]{0:T(1024)(128)(4,1)}), s8[4194304]{0:T(1024)(128)(4,1)S(1)}, s32[]{:S(2)}) async-start(s8[8388608]{0:T(1024)(128)(4,1)} %bitcast.4), calls=%async_computation | async-start | bytes 8388608
  0.0 6.8 %slice-start.1 = ((s8[8388608]{0:T(1024)(128)(4,1)}), s8[4194304]{0:T(1024)(128)(4,1)S(1)}, s32[]{:S(2)}) async-start(s8[8388608]{0:T(1024)(128)(4,1)} %bitcast.4), calls=%async_computation.1 | async-start | bytes 8388608
  0.0 6.8 %copy-start = (bf16[256,4096]{1,0:T(8,128)(2,1)S(1)}, bf16[256,4096]{1,0:T(8,128)(2,1)}, u32[]{:S(2)}) copy-start(bf16[256,4096]{1,0:T(8,128)(2,1)} %tokens_ref.1) | copy-start | bytes 6291460
  1.0 9.6 %collective-permute-start = (bf16[8,4224]{1,0:T(8,128)(2,1)S(1)}, bf16[8,4224]{1,0:T(8,128)(2,1)S(1)}, u32[]{:S(2)}, u32[]{:S(2)}) collective-permute-start(bf16[8,4224]{1,0:T(8,128)(2,1)S(1)} %make_message.1.refs_0_), channel_id=1, source_target_pairs={{0,12},{4,8},{8,4},{12,0},{1,13},{5,9},{9,5},{13,1},{2,14},{6,10},... | collective-permute-start | bytes 202760 | tf_op jit(solution)/shard_map/ppermute | solution.py:381
  6.2 5.8 %collective-permute-start.1 = (bf16[8,4224]{1,0:T(8,128)(2,1)S(1)}, bf16[8,4224]{1,0:T(8,128)(2,1)S(1)}, u32[]{:S(2)}, u32[]{:S(2)}) collective-permute-start(bf16[8,4224]{1,0:T(8,128)(2,1)S(1)} %make_message.1.refs_0_), channel_id=1, source_target_pairs={{0,8},{4,12},{8,0},{12,4},{1,9},{5,13},{9,1},{13,5},{2,10},{6,14},... | collective-permute-start | bytes 202760 | tf_op jit(solution)/shard_map/ppermute | solution.py:381
  6.2 5.8 %collective-permute-start.2 = (bf16[8,4224]{1,0:T(8,128)(2,1)S(1)}, bf16[8,4224]{1,0:T(8,128)(2,1)S(1)}, u32[]{:S(2)}, u32[]{:S(2)}) collective-permute-start(bf16[8,4224]{1,0:T(8,128)(2,1)S(1)} %make_message.1.refs_0_), channel_id=1, source_target_pairs={{0,4},{4,0},{8,12},{12,8},{1,5},{5,1},{9,13},{13,9},{2,6},{6,2},{1... | collective-permute-start | bytes 202760 | tf_op jit(solution)/shard_map/ppermute | solution.py:381
  9.1 10.2 %collective-permute-start.3 = (bf16[256,512]{1,0:T(8,128)(2,1)S(1)}, bf16[256,512]{1,0:T(8,128)(2,1)S(1)}, u32[]{:S(2)}, u32[]{:S(2)}) collective-permute-start(bf16[256,512]{1,0:T(8,128)(2,1)S(1)} %get-tuple-element.15.values_ref), channel_id=1, source_target_pairs={{0,4},{4,0},{8,12},{12,8},{1,5},{5,1},{9,13},{13,9},{2,6},{6,2},{1... | collective-permute-start | bytes 786440 | tf_op jit(solution)/shard_map/ppermute | solution.py:381
  12.0 4.9 %copy-start.1 = (bf16[1,1,8,128,1024]{4,3,2,1,0:T(8,128)(2,1)S(1)}, bf16[1,1,8,128,1024]{4,3,2,1,0:T(8,128)(2,1)}, u32[]{:S(2)}) copy-start(bf16[1,1,8,128,1024]{4,3,2,1,0:T(8,128)(2,1)} %param.14) | copy-start | bytes 6291460
  12.0 4.9 %copy-start.2 = (bf16[1,1,8,4096]{3,2,1,0:T(8,128)(2,1)S(1)}, bf16[1,1,8,4096]{3,2,1,0:T(8,128)(2,1)}, u32[]{:S(2)}) copy-start(bf16[1,1,8,4096]{3,2,1,0:T(8,128)(2,1)} %param.13) | copy-start | bytes 196612
  12.0 4.9 %copy-start.3 = (s32[8,128]{1,0:T(8,128)S(1)}, s32[8,128]{1,0:T(8,128)}, u32[]{:S(2)}) copy-start(s32[8,128]{1,0:T(8,128)} %signs_ref.1) | copy-start | bytes 12292
  12.0 4.9 %copy-start.4 = (s32[1,1,8]{2,1,0:T(1,128)S(1)}, s32[1,1,8]{2,1,0:T(1,128)}, u32[]{:S(2)}) copy-start(s32[1,1,8]{2,1,0:T(1,128)} %lengths_ref.1) | copy-start | bytes 100
  12.3 6.8 %collective-permute-start.4 = (bf16[32,256]{1,0:T(8,128)(2,1)S(1)}, bf16[32,256]{1,0:T(8,128)(2,1)S(1)}, u32[]{:S(2)}, u32[]{:S(2)}) collective-permute-start(bf16[32,256]{1,0:T(8,128)(2,1)S(1)} %get-tuple-element.18.refs_0_), channel_id=1, source_target_pairs={{0,4},{4,8},{8,12},{12,0},{1,5},{5,9},{9,13},{13,1},{2,6},{6,10},{... | collective-permute-start | bytes 49160 | tf_op jit(solution)/shard_map/ppermute | solution.py:386
  13.8 5.3 %collective-permute-start.5 = (bf16[32,256]{1,0:T(8,128)(2,1)S(1)}, bf16[32,256]{1,0:T(8,128)(2,1)S(1)}, u32[]{:S(2)}, u32[]{:S(2)}) collective-permute-start(bf16[32,256]{1,0:T(8,128)(2,1)S(1)} %get-tuple-element.18.refs_0_), channel_id=1, source_target_pairs={{0,8},{4,12},{8,0},{12,4},{1,9},{5,13},{9,1},{13,5},{2,10},{6,14},... | collective-permute-start | bytes 49160 | tf_op jit(solution)/shard_map/ppermute | solution.py:386
  15.6 3.7 %collective-permute-start.6 = (bf16[32,256]{1,0:T(8,128)(2,1)S(1)}, bf16[32,256]{1,0:T(8,128)(2,1)S(1)}, u32[]{:S(2)}, u32[]{:S(2)}) collective-permute-start(bf16[32,256]{1,0:T(8,128)(2,1)S(1)} %get-tuple-element.18.refs_0_), channel_id=1, source_target_pairs={{0,12},{4,0},{8,4},{12,8},{1,13},{5,1},{9,5},{13,9},{2,14},{6,2},{... | collective-permute-start | bytes 49160 | tf_op jit(solution)/shard_map/ppermute | solution.py:386
  19.8 6.8 %collective-permute-start.7 = (bf16[8,4352]{1,0:T(8,128)(2,1)S(1)}, bf16[8,4352]{1,0:T(8,128)(2,1)S(1)}, u32[]{:S(2)}, u32[]{:S(2)}) collective-permute-start(bf16[8,4352]{1,0:T(8,128)(2,1)S(1)} %get-tuple-element.20), channel_id=1, source_target_pairs={{0,8},{4,12},{8,0},{12,4},{1,9},{5,13},{9,1},{13,5},{2,10},{6,14},... | collective-permute-start | bytes 208904 | tf_op jit(solution)/shard_map/ppermute | solution.py:381
  21.0 6.8 %collective-permute-start.8 = (bf16[8,4352]{1,0:T(8,128)(2,1)S(1)}, bf16[8,4352]{1,0:T(8,128)(2,1)S(1)}, u32[]{:S(2)}, u32[]{:S(2)}) collective-permute-start(bf16[8,4352]{1,0:T(8,128)(2,1)S(1)} %get-tuple-element.20), channel_id=1, source_target_pairs={{0,10},{2,8},{4,14},{6,12},{8,2},{10,0},{12,6},{14,4},{1,11},{3,9}... | collective-permute-start | bytes 208904 | tf_op jit(solution)/shard_map/ppermute | solution.py:409
  23.7 4.8 %collective-permute-start.9 = (bf16[8,4352]{1,0:T(8,128)(2,1)S(1)}, bf16[8,4352]{1,0:T(8,128)(2,1)S(1)}, u32[]{:S(2)}, u32[]{:S(2)}) collective-permute-start(bf16[8,4352]{1,0:T(8,128)(2,1)S(1)} %get-tuple-element.19.own_ref), channel_id=1, source_target_pairs={{0,2},{2,0},{1,3},{3,1},{4,6},{6,4},{5,7},{7,5},{8,10},{10,8},{9,1... | collective-permute-start | bytes 208904 | tf_op jit(solution)/shard_map/ppermute | solution.py:381

commit v21 on v19

--- a/solution.py
+++ b/solution.py
@@ -37,7 +37,7 @@
 
 QUERY_ORDER = (3, 2, 1)
 SCORE_ORDER = (1, 2, 3)
-FINISH_PLACES = (2, 1, 0)
+FINISH_PLACES = (2, 1, 0, 3)
 
 
 def arranged(blocks, order):
@@ -254,22 +254,8 @@
     )(keys, *arranged(messages, QUERY_ORDER))
 
 
-def packed(value, count):
-    lane = lax.broadcasted_iota(jnp.int32, value.shape, 1)
-    high = value.astype(jnp.bfloat16).astype(jnp.float32)
-    middle = (value - high).astype(jnp.bfloat16).astype(jnp.float32)
-    low = value - high - middle
-    middle, low = pltpu.roll(middle, count, 1), pltpu.roll(low, 2 * count, 1)
-    return jnp.where(lane < count, high, jnp.where(lane < 2 * count, middle, low))
-
-
-def unpacked(message, at, count):
-    parts = [message[:, at + part * count : at + (part + 1) * count] for part in range(3)]
-    return parts[0] + parts[1] + parts[2]
-
-
 def mix_kernel(heads, requests, code_ref, values_ref, near_ref, cache_ref, cache_stats_ref, *refs):
-    score_refs, (share_ref, far_ref) = refs[:4], refs[4:]
+    score_refs, (share_ref, far_ref, stats_ref) = refs[:4], refs[4:]
     own, before, across, after = [ref[...].astype(jnp.float32) for ref in score_refs]
     scores = (own + across) + (before + after)
     tokens, width = values_ref.shape
@@ -311,10 +297,7 @@
         at = slice(h * size, (h + 1) * size)
         share = cache_ref[:, at] * cache_factor[:, h : h + 1] + part * new_factor[:, h : h + 1]
         share_ref[:, at] = share.astype(share_ref.dtype)
-    lanes = cache_stats_ref.shape[1]
-    far_ref[:, columns:] = jnp.zeros((requests, 3 * lanes), far_ref.dtype)
-    for i, value in enumerate((both, total, new_factor)):
-        share_ref[:, columns + i * lanes : columns + (i + 1) * lanes] = packed(value, count).astype(share_ref.dtype)
+    stats_ref[...] = jnp.concatenate([both, total, new_factor], axis=0)
 
 
 def mix(heads, code, values, near_values, cache_mixed, cache_stats, scores):
@@ -323,28 +306,23 @@
     return pl.pallas_call(
         functools.partial(mix_kernel, heads, requests),
         out_shape=[
-            jax.ShapeDtypeStruct((requests, columns + 3 * lanes), jnp.bfloat16),
-        ]
-        * 2,
+            jax.ShapeDtypeStruct((requests, columns), jnp.bfloat16),
+            jax.ShapeDtypeStruct((requests, columns), jnp.bfloat16),
+            jax.ShapeDtypeStruct((3 * requests, lanes), jnp.float32),
+        ],
         compiler_params=params(),
         name="mix",
     )(code, values, near_values, cache_mixed, cache_stats, *arranged(scores, SCORE_ORDER))
 
 
-def finish_kernel(count, own_ref, *refs):
+def finish_kernel(own_ref, own_stats_ref, *refs):
     out_ref = refs[-1]
-    other_ref, own_far_ref, other_far_ref = [refs[i] for i in FINISH_PLACES]
-    columns = out_ref.shape[1]
-    size = columns // count
-    lanes = (own_ref.shape[1] - columns) // 3
+    other_ref, own_far_ref, other_far_ref, other_stats_ref = [refs[i] for i in FINISH_PLACES]
+    requests, columns = out_ref.shape
+    size = own_stats_ref.shape[1]
     first = lax.axis_index("tp") == 0
-
-    def stats(ref):
-        message = ref[:, columns:].astype(jnp.float32)
-        return [unpacked(message, i * lanes, count) for i in range(3)]
-
-    own_top, own_total, own_new = stats(own_ref)
-    other_top, other_total, other_new = stats(other_ref)
+    own_top, own_total, own_new = [own_stats_ref[i * requests : (i + 1) * requests, :] for i in range(3)]
+    other_top, other_total, other_new = [other_stats_ref[i * requests : (i + 1) * requests, :] for i in range(3)]
     both = jnp.maximum(own_top, other_top)
     own_factor, other_factor = jnp.exp(own_top - both), jnp.exp(other_top - both)
     own_total, other_total = own_total * own_factor, other_total * other_factor
@@ -357,7 +335,7 @@
     ):
         factor = factor * inverse
         sides.append((ref, far_ref, factor, factor * new))
-    for h in range(count):
+    for h in range(columns // size):
         at = slice(h * size, (h + 1) * size)
         terms = [
             ref[:, at].astype(jnp.float32) * factor[:, h : h + 1]
@@ -367,14 +345,14 @@
         out_ref[:, at] = (terms[0] + terms[1]).astype(out_ref.dtype)
 
 
-def finish(count, columns, own, other, own_far, other_far):
-    arrived = (other, own_far, other_far)
+def finish(own, own_stats, other, own_far, other_far, other_stats):
+    arrived = (other, own_far, other_far, other_stats)
     return pl.pallas_call(
-        functools.partial(finish_kernel, count),
-        out_shape=jax.ShapeDtypeStruct((own.shape[0], columns), jnp.bfloat16),
+        finish_kernel,
+        out_shape=jax.ShapeDtypeStruct(own.shape, own.dtype),
         compiler_params=params(),
         name="finish",
-    )(own, *[arrived[FINISH_PLACES.index(i)] for i in range(3)])
+    )(own, own_stats, *[arrived[FINISH_PLACES.index(i)] for i in range(4)])
 
 
 def from_partner(x, axis, distance):
@@ -399,15 +377,15 @@
     scores, code = partial_scores(heads, columns, keys, messages)
     scores = [scores] + [from_behind(scores, "seq", d) for d in range(1, seq_count)]
     cache_mixed, cache_stats = cache_part(lengths, query, kv_cache[0, 0], signs)
-    share, far = mix(heads, code, values, near_values, cache_mixed, cache_stats, scores)
+    share, far, stats = mix(heads, code, values, near_values, cache_mixed, cache_stats, scores)
     far_pairs = [(i, i ^ 5) for i in range(2 * seq_count)]
     output = finish(
-        columns // signs.shape[1],
-        columns,
         share,
+        stats,
         from_partner(share, "tp", 1),
         from_partner(far, "seq", 2),
         lax.ppermute(far, ("seq", "tp"), far_pairs),
+        from_partner(stats, "tp", 1),
     )
     return output.reshape(1, 1, request_count, columns)
 

time: 29.2 us -> 29.2 us (level)
  starting transfers between devices: 16.2 us -> 17.7 us
  waiting for transfers between devices: 6.08 us -> 4.64 us
    ppermute x1, waiting for transfers between devices: 2.7 us -> 0.01 us  [on_device(): lax.ppermute(far, ('seq', 'tp'), far_pairs)]
    ppermute x6 -> x7, starting transfers between devices: 9.55 us -> 11 us  [from_partner(): return lax.ppermute(x, axis, [(i, i ^ distance) for i in range(count)])]
    ppermute x6 -> x7, waiting for transfers between devices: 2.53 us -> 3.79 us  [from_partner(): return lax.ppermute(x, axis, [(i, i ^ distance) for i in range(count)])]
  transfers between devices with their start and end apart: 10 -> 11, of which waited for: 5 -> 4; matrix products, arithmetic and copies ran while one was open for 0% -> 0% of each run, Pallas kernels for 15% -> 15%
where the time goes in v21:
time: 29.2 us; the launch traced here: 29 us
  starting transfers between devices  17.7 us (61%)
  Pallas kernels  6.58 us (23%)
  waiting for transfers between devices  4.64 us (16%)
    ppermute x7, starting transfers between devices, from_partner(): return lax.ppermute(x, axis, [(i, i ^ distance) for i in range(count)])  11 us
    ppermute x3, starting transfers between devices, from_behind(): lax.ppermute(x, axis, [(i, (i + distance) % count) for i in range(count)])  4.52 us
    ppermute x7, waiting for transfers between devices, from_partner(): return lax.ppermute(x, axis, [(i, i ^ distance) for i in range(count)])  3.79 us
    pallas_call x1, Pallas kernels, project(): pl.pallas_call(project_kernel, in_specs=[vmem] * 2, out_specs=[vmem] * 2,...  2.32 us
    ppermute x1, starting transfers between devices, on_device(): lax.ppermute(far, ('seq', 'tp'), far_pairs)  2.12 us
    pallas_call x1, Pallas kernels, cache_part(): pl.pallas_call(cache_kernel, in_specs=[pl.BlockSpec(memory_space=pltpu.SM...  1.6 us
    pallas_call x1, Pallas kernels, make_message(): pl.pallas_call(message_kernel, in_specs=[pl.BlockSpec(memory_space=pl.ANY...  1.01 us
    pallas_call x1, Pallas kernels, finish(): pl.pallas_call(finish_kernel, out_shape=jax.ShapeDtypeStruct(own.shape, o...  0.91 us
  transfers between devices with their start and end apart: 11, of which 4 were waited for; matrix products, arithmetic and copies ran while one was open for 0% of the time, Pallas kernels for 15%

profile of v21, /device:TPU:0, one launch (start us, length us, event | category | flops | bytes accessed | tf_op | source)
XLA Modules:
  0.0 29.0 jit_solution(8258491023101366796)
XLA Ops:
  0.0 1.0 %make_message.1.refs_0_ = bf16[8,4224]{1,0:T(8,128)(2,1)S(1)} custom-call(bf16[8,4096]{1,0:T(8,128)(2,1)} %bitcast.7, s32[1,64]{1,0:T(1,128)} %bitcast.9, s32[1,64]{1,0:T(1,128)} %requests_ref.1), custom_call_target="tpu_custom_call" | custom-call | flops 99999997952 | bytes 10000 | tf_op jit(solution)/shard_map/make_message/pallas_call | solution.py:100
  1.0 5.1 %collective-permute-start = (bf16[8,4224]{1,0:T(8,128)(2,1)S(1)}, bf16[8,4224]{1,0:T(8,128)(2,1)S(1)}, u32[]{:S(2)}, u32[]{:S(2)}) collective-permute-start(bf16[8,4224]{1,0:T(8,128)(2,1)S(1)} %make_message.1.refs_0_), channel_id=1, source_target_pairs={{0,12},{4,8},{8,4},{12,0},{1,13},{5,9},{9,5},{13,1},{2,14},{6,10},... | collective-permute-start | bytes 202760 | tf_op jit(solution)/shard_map/ppermute | solution.py:360
  6.2 0.6 %collective-permute-start.2 = (bf16[8,4224]{1,0:T(8,128)(2,1)S(1)}, bf16[8,4224]{1,0:T(8,128)(2,1)S(1)}, u32[]{:S(2)}, u32[]{:S(2)}) collective-permute-start(bf16[8,4224]{1,0:T(8,128)(2,1)S(1)} %make_message.1.refs_0_), channel_id=1, source_target_pairs={{0,4},{4,0},{8,12},{12,8},{1,5},{5,1},{9,13},{13,9},{2,6},{6,2},{1... | collective-permute-start | bytes 202760 | tf_op jit(solution)/shard_map/ppermute | solution.py:360
  6.8 2.3 %project.1 = (bf16[256,512]{1,0:T(8,128)(2,1)S(1)}, bf16[256,512]{1,0:T(8,128)(2,1)S(1)}) custom-call(bf16[256,4096]{1,0:T(8,128)(2,1)S(1)} %copy-done, bf16[4096,1024]{1,0:T(8,128)(2,1)S(1)} %bitcast.5), custom_call_target="tpu_custom_call" | custom-call | flops 2147483648 | bytes 10485760 | tf_op jit(solution)/shard_map/project/pallas_call | solution.py:63
  9.1 1.5 %collective-permute-start.3 = (bf16[256,512]{1,0:T(8,128)(2,1)S(1)}, bf16[256,512]{1,0:T(8,128)(2,1)S(1)}, u32[]{:S(2)}, u32[]{:S(2)}) collective-permute-start(bf16[256,512]{1,0:T(8,128)(2,1)S(1)} %get-tuple-element.16.values_ref), channel_id=1, source_target_pairs={{0,4},{4,0},{8,12},{12,8},{1,5},{5,1},{9,13},{13,9},{2,6},{6,2},{1... | collective-permute-start | bytes 786440 | tf_op jit(solution)/shard_map/ppermute | solution.py:360
  10.6 1.4 %collective-permute-done.1.refs_2_ = bf16[8,4224]{1,0:T(8,128)(2,1)S(1)} collective-permute-done((bf16[8,4224]{1,0:T(8,128)(2,1)S(1)}, bf16[8,4224]{1,0:T(8,128)(2,1)S(1)}, u32[]{:S(2)}, u32[]{:S(2)}) %collective-permute-start.1) | collective-permute-done | bytes 67616 | tf_op jit(solution)/shard_map/ppermute | solution.py:360
  12.0 0.0 copy-start.4
  12.0 0.3 %partial_scores.1 = (bf16[32,256]{1,0:T(8,128)(2,1)S(1)}, s32[8,256]{1,0:T(8,128)S(1)}) custom-call(bf16[256,512]{1,0:T(8,128)(2,1)S(1)} %get-tuple-element.14.keys_ref, bf16[8,4224]{1,0:T(8,128)(2,1)S(1)} %make_message.1.refs_0_, bf16[8,4224]{1,0:T(8,128)(2,1)S(1)} %collective-permute-done.refs_1_, bf16[8,4224]{1,0:T(8,128)(2,1)S(1)} %collective-permute-done.1.refs_2_, ...), custom_call_target="tpu_custom_call" | custom-call | flops 99999997952 | bytes 10000 | tf_op jit(solution)/shard_map/partial_scores/pallas_call | solution.py:245
  12.3 1.5 %collective-permute-start.4 = (bf16[32,256]{1,0:T(8,128)(2,1)S(1)}, bf16[32,256]{1,0:T(8,128)(2,1)S(1)}, u32[]{:S(2)}, u32[]{:S(2)}) collective-permute-start(bf16[32,256]{1,0:T(8,128)(2,1)S(1)} %get-tuple-element.19.refs_0_), channel_id=1, source_target_pairs={{0,4},{4,8},{8,12},{12,0},{1,5},{5,9},{9,13},{13,1},{2,6},{6,10},{... | collective-permute-start | bytes 49160 | tf_op jit(solution)/shard_map/ppermute | solution.py:365
  13.8 1.8 %collective-permute-start.5 = (bf16[32,256]{1,0:T(8,128)(2,1)S(1)}, bf16[32,256]{1,0:T(8,128)(2,1)S(1)}, u32[]{:S(2)}, u32[]{:S(2)}) collective-permute-start(bf16[32,256]{1,0:T(8,128)(2,1)S(1)} %get-tuple-element.19.refs_0_), channel_id=1, source_target_pairs={{0,8},{4,12},{8,0},{12,4},{1,9},{5,13},{9,1},{13,5},{2,10},{6,14},... | collective-permute-start | bytes 49160 | tf_op jit(solution)/shard_map/ppermute | solution.py:365
  15.6 1.3 %collective-permute-start.6 = (bf16[32,256]{1,0:T(8,128)(2,1)S(1)}, bf16[32,256]{1,0:T(8,128)(2,1)S(1)}, u32[]{:S(2)}, u32[]{:S(2)}) collective-permute-start(bf16[32,256]{1,0:T(8,128)(2,1)S(1)} %get-tuple-element.19.refs_0_), channel_id=1, source_target_pairs={{0,12},{4,0},{8,4},{12,8},{1,13},{5,1},{9,5},{13,9},{2,14},{6,2},{... | collective-permute-start | bytes 49160 | tf_op jit(solution)/shard_map/ppermute | solution.py:365
  16.9 1.6 %cache_part.1 = (f32[8,4096]{1,0:T(8,128)S(1)}, f32[16,128]{1,0:T(8,128)S(1)}) custom-call(s32[1,1,8]{2,1,0:T(1,128)S(1)} %copy-done.4, bf16[8,4096]{1,0:T(8,128)(2,1)S(1)} %bitcast.8, bf16[8,128,1024]{2,1,0:T(8,128)(2,1)S(1)} %bitcast.6, s32[8,128]{1,0:T(8,128)S(1)} %copy-done.3), custom_call_target="tpu_custom_call" | custom-call | flops 16777216 | bytes 2097152 | tf_op jit(solution)/shard_map/cache_part/pallas_call | solution.py:189
  18.5 0.6 %collective-permute-done.4.refs_1_ = bf16[32,256]{1,0:T(8,128)(2,1)S(1)} collective-permute-done((bf16[32,256]{1,0:T(8,128)(2,1)S(1)}, bf16[32,256]{1,0:T(8,128)(2,1)S(1)}, u32[]{:S(2)}, u32[]{:S(2)}) %collective-permute-start.4) | collective-permute-done | bytes 16416 | tf_op jit(solution)/shard_map/ppermute | solution.py:365
  19.1 0.0 collective-permute-done.5.refs_2_
  19.1 0.2 collective-permute-done.6.refs_3_
  19.3 0.0 collective-permute-done.3.near_ref
  19.3 0.4 %mix.1 = (bf16[8,4096]{1,0:T(8,128)(2,1)S(1)}, bf16[8,4096]{1,0:T(8,128)(2,1)S(1)}, f32[24,128]{1,0:T(8,128)S(1)}) custom-call(s32[8,256]{1,0:T(8,128)S(1)} %get-tuple-element.15.code_ref, bf16[256,512]{1,0:T(8,128)(2,1)S(1)} %get-tuple-element.16.values_ref, bf16[256,512]{1,0:T(8,128)(2,1)S(1)} %collective-permute-done.3.near_ref, ...), custom_call_target="tpu_custom_call" | custom-call | tf_op jit(solution)/shard_map/mix/pallas_call | solution.py:306
  19.8 2.1 %collective-permute-start.7 = (bf16[8,4096]{1,0:T(8,128)(2,1)S(1)}, bf16[8,4096]{1,0:T(8,128)(2,1)S(1)}, u32[]{:S(2)}, u32[]{:S(2)}) collective-permute-start(bf16[8,4096]{1,0:T(8,128)(2,1)S(1)} %get-tuple-element.22), channel_id=1, source_target_pairs={{0,10},{2,8},{4,14},{6,12},{8,2},{10,0},{12,6},{14,4},{1,11},{3,9}... | collective-permute-start | bytes 196616 | tf_op jit(solution)/shard_map/ppermute | solution.py:387
  21.9 1.8 %collective-permute-start.8 = (bf16[8,4096]{1,0:T(8,128)(2,1)S(1)}, bf16[8,4096]{1,0:T(8,128)(2,1)S(1)}, u32[]{:S(2)}, u32[]{:S(2)}) collective-permute-start(bf16[8,4096]{1,0:T(8,128)(2,1)S(1)} %get-tuple-element.22), channel_id=1, source_target_pairs={{0,8},{4,12},{8,0},{12,4},{1,9},{5,13},{9,1},{13,5},{2,10},{6,14},... | collective-permute-start | bytes 196616 | tf_op jit(solution)/shard_map/ppermute | solution.py:360
  23.7 0.5 %collective-permute-start.9 = (bf16[8,4096]{1,0:T(8,128)(2,1)S(1)}, bf16[8,4096]{1,0:T(8,128)(2,1)S(1)}, u32[]{:S(2)}, u32[]{:S(2)}) collective-permute-start(bf16[8,4096]{1,0:T(8,128)(2,1)S(1)} %get-tuple-element.20.own_ref), channel_id=1, source_target_pairs={{0,2},{2,0},{1,3},{3,1},{4,6},{6,4},{5,7},{7,5},{8,10},{10,8},{9,1... | collective-permute-start | bytes 196616 | tf_op jit(solution)/shard_map/ppermute | solution.py:360
  24.2 1.5 %collective-permute-start.10 = (f32[24,128]{1,0:T(8,128)S(1)}, f32[24,128]{1,0:T(8,128)S(1)}, u32[]{:S(2)}, u32[]{:S(2)}) collective-permute-start(f32[24,128]{1,0:T(8,128)S(1)} %get-tuple-element.21.own_stats_ref), channel_id=1, source_target_pairs={{0,2},{2,0},{1,3},{3,1},{4,6},{6,4},{5,7},{7,5},{8,10},{10,8},{9,1... | collective-permute-start | bytes 36872 | tf_op jit(solution)/shard_map/ppermute | solution.py:360
  25.7 2.4 %collective-permute-done.10.refs_3_ = f32[24,128]{1,0:T(8,128)S(1)} collective-permute-done((f32[24,128]{1,0:T(8,128)S(1)}, f32[24,128]{1,0:T(8,128)S(1)}, u32[]{:S(2)}, u32[]{:S(2)}) %collective-permute-start.10) | collective-permute-done | bytes 12320 | tf_op jit(solution)/shard_map/ppermute | solution.py:360
  28.1 0.0 collective-permute-done.7.refs_0_
  28.1 0.9 %finish.1 = bf16[8,4096]{1,0:T(8,128)(2,1)} custom-call(bf16[8,4096]{1,0:T(8,128)(2,1)S(1)} %get-tuple-element.20.own_ref, f32[24,128]{1,0:T(8,128)S(1)} %get-tuple-element.21.own_stats_ref, bf16[8,4096]{1,0:T(8,128)(2,1)S(1)} %collective-permute-done.7.refs_0_, bf16[8,4096]{1,0:T(8,128)(2,1)S(1)} %collective-permute-done.8.refs_1_, ...), custom_call_target="tpu_custom_call" | custom-call | tf_op jit(solution)/shard_map/finish/pallas_call | solution.py:350
  (19 shorter events, 0.0 us)
Async XLA Ops:
  0.0 6.8 %slice-start = ((s8[8388608]{0:T(1024)(128)(4,1)}), s8[4194304]{0:T(1024)(128)(4,1)S(1)}, s32[]{:S(2)}) async-start(s8[8388608]{0:T(1024)(128)(4,1)} %bitcast.4), calls=%async_computation | async-start | bytes 8388608
  0.0 6.8 %slice-start.1 = ((s8[8388608]{0:T(1024)(128)(4,1)}), s8[4194304]{0:T(1024)(128)(4,1)S(1)}, s32[]{:S(2)}) async-start(s8[8388608]{0:T(1024)(128)(4,1)} %bitcast.4), calls=%async_computation.1 | async-start | bytes 8388608
  0.0 6.8 %copy-start = (bf16[256,4096]{1,0:T(8,128)(2,1)S(1)}, bf16[256,4096]{1,0:T(8,128)(2,1)}, u32[]{:S(2)}) copy-start(bf16[256,4096]{1,0:T(8,128)(2,1)} %tokens_ref.1) | copy-start | bytes 6291460
  1.0 9.6 %collective-permute-start = (bf16[8,4224]{1,0:T(8,128)(2,1)S(1)}, bf16[8,4224]{1,0:T(8,128)(2,1)S(1)}, u32[]{:S(2)}, u32[]{:S(2)}) collective-permute-start(bf16[8,4224]{1,0:T(8,128)(2,1)S(1)} %make_message.1.refs_0_), channel_id=1, source_target_pairs={{0,12},{4,8},{8,4},{12,0},{1,13},{5,9},{9,5},{13,1},{2,14},{6,10},... | collective-permute-start | bytes 202760 | tf_op jit(solution)/shard_map/ppermute | solution.py:360
  6.2 5.8 %collective-permute-start.1 = (bf16[8,4224]{1,0:T(8,128)(2,1)S(1)}, bf16[8,4224]{1,0:T(8,128)(2,1)S(1)}, u32[]{:S(2)}, u32[]{:S(2)}) collective-permute-start(bf16[8,4224]{1,0:T(8,128)(2,1)S(1)} %make_message.1.refs_0_), channel_id=1, source_target_pairs={{0,8},{4,12},{8,0},{12,4},{1,9},{5,13},{9,1},{13,5},{2,10},{6,14},... | collective-permute-start | bytes 202760 | tf_op jit(solution)/shard_map/ppermute | solution.py:360
  6.2 5.8 %collective-permute-start.2 = (bf16[8,4224]{1,0:T(8,128)(2,1)S(1)}, bf16[8,4224]{1,0:T(8,128)(2,1)S(1)}, u32[]{:S(2)}, u32[]{:S(2)}) collective-permute-start(bf16[8,4224]{1,0:T(8,128)(2,1)S(1)} %make_message.1.refs_0_), channel_id=1, source_target_pairs={{0,4},{4,0},{8,12},{12,8},{1,5},{5,1},{9,13},{13,9},{2,6},{6,2},{1... | collective-permute-start | bytes 202760 | tf_op jit(solution)/shard_map/ppermute | solution.py:360
  9.1 10.2 %collective-permute-start.3 = (bf16[256,512]{1,0:T(8,128)(2,1)S(1)}, bf16[256,512]{1,0:T(8,128)(2,1)S(1)}, u32[]{:S(2)}, u32[]{:S(2)}) collective-permute-start(bf16[256,512]{1,0:T(8,128)(2,1)S(1)} %get-tuple-element.16.values_ref), channel_id=1, source_target_pairs={{0,4},{4,0},{8,12},{12,8},{1,5},{5,1},{9,13},{13,9},{2,6},{6,2},{1... | collective-permute-start | bytes 786440 | tf_op jit(solution)/shard_map/ppermute | solution.py:360
  12.0 4.9 %copy-start.1 = (bf16[1,1,8,128,1024]{4,3,2,1,0:T(8,128)(2,1)S(1)}, bf16[1,1,8,128,1024]{4,3,2,1,0:T(8,128)(2,1)}, u32[]{:S(2)}) copy-start(bf16[1,1,8,128,1024]{4,3,2,1,0:T(8,128)(2,1)} %param.14) | copy-start | bytes 6291460
  12.0 4.9 %copy-start.2 = (bf16[1,1,8,4096]{3,2,1,0:T(8,128)(2,1)S(1)}, bf16[1,1,8,4096]{3,2,1,0:T(8,128)(2,1)}, u32[]{:S(2)}) copy-start(bf16[1,1,8,4096]{3,2,1,0:T(8,128)(2,1)} %param.13) | copy-start | bytes 196612
  12.0 4.9 %copy-start.3 = (s32[8,128]{1,0:T(8,128)S(1)}, s32[8,128]{1,0:T(8,128)}, u32[]{:S(2)}) copy-start(s32[8,128]{1,0:T(8,128)} %signs_ref.1) | copy-start | bytes 12292
  12.0 4.9 %copy-start.4 = (s32[1,1,8]{2,1,0:T(1,128)S(1)}, s32[1,1,8]{2,1,0:T(1,128)}, u32[]{:S(2)}) copy-start(s32[1,1,8]{2,1,0:T(1,128)} %lengths_ref.1) | copy-start | bytes 100
  12.3 6.8 %collective-permute-start.4 = (bf16[32,256]{1,0:T(8,128)(2,1)S(1)}, bf16[32,256]{1,0:T(8,128)(2,1)S(1)}, u32[]{:S(2)}, u32[]{:S(2)}) collective-permute-start(bf16[32,256]{1,0:T(8,128)(2,1)S(1)} %get-tuple-element.19.refs_0_), channel_id=1, source_target_pairs={{0,4},{4,8},{8,12},{12,0},{1,5},{5,9},{9,13},{13,1},{2,6},{6,10},{... | collective-permute-start | bytes 49160 | tf_op jit(solution)/shard_map/ppermute | solution.py:365
  13.8 5.3 %collective-permute-start.5 = (bf16[32,256]{1,0:T(8,128)(2,1)S(1)}, bf16[32,256]{1,0:T(8,128)(2,1)S(1)}, u32[]{:S(2)}, u32[]{:S(2)}) collective-permute-start(bf16[32,256]{1,0:T(8,128)(2,1)S(1)} %get-tuple-element.19.refs_0_), channel_id=1, source_target_pairs={{0,8},{4,12},{8,0},{12,4},{1,9},{5,13},{9,1},{13,5},{2,10},{6,14},... | collective-permute-start | bytes 49160 | tf_op jit(solution)/shard_map/ppermute | solution.py:365
  15.6 3.7 %collective-permute-start.6 = (bf16[32,256]{1,0:T(8,128)(2,1)S(1)}, bf16[32,256]{1,0:T(8,128)(2,1)S(1)}, u32[]{:S(2)}, u32[]{:S(2)}) collective-permute-start(bf16[32,256]{1,0:T(8,128)(2,1)S(1)} %get-tuple-element.19.refs_0_), channel_id=1, source_target_pairs={{0,12},{4,0},{8,4},{12,8},{1,13},{5,1},{9,5},{13,9},{2,14},{6,2},{... | collective-permute-start | bytes 49160 | tf_op jit(solution)/shard_map/ppermute | solution.py:365
  19.8 8.3 %collective-permute-start.7 = (bf16[8,4096]{1,0:T(8,128)(2,1)S(1)}, bf16[8,4096]{1,0:T(8,128)(2,1)S(1)}, u32[]{:S(2)}, u32[]{:S(2)}) collective-permute-start(bf16[8,4096]{1,0:T(8,128)(2,1)S(1)} %get-tuple-element.22), channel_id=1, source_target_pairs={{0,10},{2,8},{4,14},{6,12},{8,2},{10,0},{12,6},{14,4},{1,11},{3,9}... | collective-permute-start | bytes 196616 | tf_op jit(solution)/shard_map/ppermute | solution.py:387
  21.9 6.2 %collective-permute-start.8 = (bf16[8,4096]{1,0:T(8,128)(2,1)S(1)}, bf16[8,4096]{1,0:T(8,128)(2,1)S(1)}, u32[]{:S(2)}, u32[]{:S(2)}) collective-permute-start(bf16[8,4096]{1,0:T(8,128)(2,1)S(1)} %get-tuple-element.22), channel_id=1, source_target_pairs={{0,8},{4,12},{8,0},{12,4},{1,9},{5,13},{9,1},{13,5},{2,10},{6,14},... | collective-permute-start | bytes 196616 | tf_op jit(solution)/shard_map/ppermute | solution.py:360
  23.7 4.4 %collective-permute-start.9 = (bf16[8,4096]{1,0:T(8,128)(2,1)S(1)}, bf16[8,4096]{1,0:T(8,128)(2,1)S(1)}, u32[]{:S(2)}, u32[]{:S(2)}) collective-permute-start(bf16[8,4096]{1,0:T(8,128)(2,1)S(1)} %get-tuple-element.20.own_ref), channel_id=1, source_target_pairs={{0,2},{2,0},{1,3},{3,1},{4,6},{6,4},{5,7},{7,5},{8,10},{10,8},{9,1... | collective-permute-start | bytes 196616 | tf_op jit(solution)/shard_map/ppermute | solution.py:360
  24.2 3.9 %collective-permute-start.10 = (f32[24,128]{1,0:T(8,128)S(1)}, f32[24,128]{1,0:T(8,128)S(1)}, u32[]{:S(2)}, u32[]{:S(2)}) collective-permute-start(f32[24,128]{1,0:T(8,128)S(1)} %get-tuple-element.21.own_stats_ref), channel_id=1, source_target_pairs={{0,2},{2,0},{1,3},{3,1},{4,6},{6,4},{5,7},{7,5},{8,10},{10,8},{9,1... | collective-permute-start | bytes 36872 | tf_op jit(solution)/shard_map/ppermute | solution.py:360

commit v22 on v19

--- a/solution.py
+++ b/solution.py
@@ -37,7 +37,7 @@
 
 QUERY_ORDER = (3, 2, 1)
 SCORE_ORDER = (1, 2, 3)
-FINISH_PLACES = (2, 1, 0)
+FINISH_PLACES = (0, 1, 2)
 
 
 def arranged(blocks, order):
@@ -268,8 +268,12 @@
     return parts[0] + parts[1] + parts[2]
 
 
+def even_rank():
+    return lax.axis_index("seq") & 1 == 0
+
+
 def mix_kernel(heads, requests, code_ref, values_ref, near_ref, cache_ref, cache_stats_ref, *refs):
-    score_refs, (share_ref, far_ref) = refs[:4], refs[4:]
+    score_refs, (first_ref, far_ref, last_ref, share_ref) = refs[:4], refs[4:]
     own, before, across, after = [ref[...].astype(jnp.float32) for ref in score_refs]
     scores = (own + across) + (before + after)
     tokens, width = values_ref.shape
@@ -310,11 +314,15 @@
     for h, part in enumerate(parts):
         at = slice(h * size, (h + 1) * size)
         share = cache_ref[:, at] * cache_factor[:, h : h + 1] + part * new_factor[:, h : h + 1]
-        share_ref[:, at] = share.astype(share_ref.dtype)
+        share_ref[:, at] = share
     lanes = cache_stats_ref.shape[1]
     far_ref[:, columns:] = jnp.zeros((requests, 3 * lanes), far_ref.dtype)
     for i, value in enumerate((both, total, new_factor)):
-        share_ref[:, columns + i * lanes : columns + (i + 1) * lanes] = packed(value, count).astype(share_ref.dtype)
+        share_ref[:, columns + i * lanes : columns + (i + 1) * lanes] = packed(value, count)
+    share, far = share_ref[...], far_ref[...].astype(jnp.float32)
+    even = even_rank()
+    first_ref[...] = jnp.where(even, far, share).astype(first_ref.dtype)
+    last_ref[...] = jnp.where(even, share, far).astype(last_ref.dtype)
 
 
 def mix(heads, code, values, near_values, cache_mixed, cache_stats, scores):
@@ -325,56 +333,54 @@
         out_shape=[
             jax.ShapeDtypeStruct((requests, columns + 3 * lanes), jnp.bfloat16),
         ]
-        * 2,
+        * 3,
+        scratch_shapes=[pltpu.VMEM((requests, columns + 3 * lanes), jnp.float32)],
         compiler_params=params(),
         name="mix",
     )(code, values, near_values, cache_mixed, cache_stats, *arranged(scores, SCORE_ORDER))
 
 
-def finish_kernel(count, own_ref, *refs):
+def finish_kernel(count, own_first_ref, own_last_ref, *refs):
     out_ref = refs[-1]
-    other_ref, own_far_ref, other_far_ref = [refs[i] for i in FINISH_PLACES]
+    first_ref, own_far_ref, last_ref = [refs[i] for i in FINISH_PLACES]
     columns = out_ref.shape[1]
     size = columns // count
-    lanes = (own_ref.shape[1] - columns) // 3
-    first = lax.axis_index("tp") == 0
-
-    def stats(ref):
-        message = ref[:, columns:].astype(jnp.float32)
+    lanes = (own_far_ref.shape[1] - columns) // 3
+    even = even_rank()
+    column_zero = lax.axis_index("tp") == 0
+
+    def read(ref, other_ref, at):
+        return jnp.where(even, ref[:, at].astype(jnp.float32), other_ref[:, at].astype(jnp.float32))
+
+    def stats(ref, other_ref):
+        message = read(ref, other_ref, slice(columns, columns + 3 * lanes))
         return [unpacked(message, i * lanes, count) for i in range(3)]
 
-    own_top, own_total, own_new = stats(own_ref)
-    other_top, other_total, other_new = stats(other_ref)
+    own_top, own_total, own_new = stats(own_last_ref, own_first_ref)
+    other_top, other_total, other_new = stats(last_ref, first_ref)
     both = jnp.maximum(own_top, other_top)
     own_factor, other_factor = jnp.exp(own_top - both), jnp.exp(other_top - both)
     own_total, other_total = own_total * own_factor, other_total * other_factor
-    total = jnp.where(first, own_total, other_total) + jnp.where(first, other_total, own_total)
+    total = jnp.where(column_zero, own_total, other_total) + jnp.where(column_zero, other_total, own_total)
     inverse = 1.0 / total
-    sides = []
-    for ref, far_ref, factor, new in (
-        (own_ref, own_far_ref, own_factor, own_new),
-        (other_ref, other_far_ref, other_factor, other_new),
-    ):
-        factor = factor * inverse
-        sides.append((ref, far_ref, factor, factor * new))
+    own_factor, other_factor = own_factor * inverse, other_factor * inverse
+    own_new, other_new = own_factor * own_new, other_factor * other_new
     for h in range(count):
-        at = slice(h * size, (h + 1) * size)
-        terms = [
-            ref[:, at].astype(jnp.float32) * factor[:, h : h + 1]
-            + far_ref[:, at].astype(jnp.float32) * far_factor[:, h : h + 1]
-            for ref, far_ref, factor, far_factor in sides
-        ]
-        out_ref[:, at] = (terms[0] + terms[1]).astype(out_ref.dtype)
-
-
-def finish(count, columns, own, other, own_far, other_far):
-    arrived = (other, own_far, other_far)
+        at, lane = slice(h * size, (h + 1) * size), slice(h, h + 1)
+        own = read(own_last_ref, own_first_ref, at) * own_factor[:, lane]
+        own = own + own_far_ref[:, at].astype(jnp.float32) * own_new[:, lane]
+        other = read(last_ref, first_ref, at) * other_factor[:, lane]
+        other = other + read(first_ref, last_ref, at) * other_new[:, lane]
+        out_ref[:, at] = (own + other).astype(out_ref.dtype)
+
+
+def finish(count, columns, own_first, own_last, *arrived):
     return pl.pallas_call(
         functools.partial(finish_kernel, count),
-        out_shape=jax.ShapeDtypeStruct((own.shape[0], columns), jnp.bfloat16),
+        out_shape=jax.ShapeDtypeStruct((own_first.shape[0], columns), jnp.bfloat16),
         compiler_params=params(),
         name="finish",
-    )(own, *[arrived[FINISH_PLACES.index(i)] for i in range(3)])
+    )(own_first, own_last, *[arrived[FINISH_PLACES.index(i)] for i in range(3)])
 
 
 def from_partner(x, axis, distance):
@@ -399,15 +405,18 @@
     scores, code = partial_scores(heads, columns, keys, messages)
     scores = [scores] + [from_behind(scores, "seq", d) for d in range(1, seq_count)]
     cache_mixed, cache_stats = cache_part(lengths, query, kv_cache[0, 0], signs)
-    share, far = mix(heads, code, values, near_values, cache_mixed, cache_stats, scores)
-    far_pairs = [(i, i ^ 5) for i in range(2 * seq_count)]
+    first, far, last = mix(heads, code, values, near_values, cache_mixed, cache_stats, scores)
+    devices = range(2 * seq_count)
+    first_pairs = [(i, i ^ 1) if i & 2 else (i, i ^ 5) for i in devices]
+    last_pairs = [(i, i ^ 5) if i & 2 else (i, i ^ 1) for i in devices]
     output = finish(
         columns // signs.shape[1],
         columns,
-        share,
-        from_partner(share, "tp", 1),
+        first,
+        last,
+        lax.ppermute(first, ("seq", "tp"), first_pairs),
         from_partner(far, "seq", 2),
-        lax.ppermute(far, ("seq", "tp"), far_pairs),
+        lax.ppermute(last, ("seq", "tp"), last_pairs),
     )
     return output.reshape(1, 1, request_count, columns)
 

time: 29.2 us -> 29.3 us (level)
    ppermute x6 -> x5, waiting for transfers between devices: 2.53 us -> 3.57 us  [from_partner(): return lax.ppermute(x, axis, [(i, i ^ distance) for i in range(count)])]
    ppermute x1 -> x2, waiting for transfers between devices: 2.7 us -> 1.74 us  [the longest x1 1.74 us: on_device(): lax.ppermute(first, ('seq', 'tp'), first_pairs)]
    ppermute x1 -> x2, starting transfers between devices: 2.12 us -> 2.65 us  [the longest x1 2.12 us: on_device(): lax.ppermute(first, ('seq', 'tp'), first_pairs)]
    ppermute x6 -> x5, starting transfers between devices: 9.55 us -> 9.01 us  [from_partner(): return lax.ppermute(x, axis, [(i, i ^ distance) for i in range(count)])]
where the time goes in v22:
time: 29.3 us; the launch traced here: 29.1 us
  starting transfers between devices  16.2 us (55%)
  Pallas kernels  6.67 us (23%)
  waiting for transfers between devices  6.16 us (21%)
    ppermute x5, starting transfers between devices, from_partner(): return lax.ppermute(x, axis, [(i, i ^ distance) for i in range(count)])  9.01 us
    ppermute x3, starting transfers between devices, from_behind(): lax.ppermute(x, axis, [(i, (i + distance) % count) for i in range(count)])  4.52 us
    ppermute x5, waiting for transfers between devices, from_partner(): return lax.ppermute(x, axis, [(i, i ^ distance) for i in range(count)])  3.57 us
    pallas_call x1, Pallas kernels, project(): pl.pallas_call(project_kernel, in_specs=[vmem] * 2, out_specs=[vmem] * 2,...  2.32 us
    ppermute x1, starting transfers between devices, on_device(): lax.ppermute(first, ('seq', 'tp'), first_pairs)  2.12 us
    ppermute x1, waiting for transfers between devices, on_device(): lax.ppermute(first, ('seq', 'tp'), first_pairs)  1.74 us
    pallas_call x1, Pallas kernels, cache_part(): pl.pallas_call(cache_kernel, in_specs=[pl.BlockSpec(memory_space=pltpu.SM...  1.6 us
    pallas_call x1, Pallas kernels, make_message(): pl.pallas_call(message_kernel, in_specs=[pl.BlockSpec(memory_space=pl.ANY...  1.01 us
  transfers between devices with their start and end apart: 10, of which 5 were waited for; matrix products, arithmetic and copies ran while one was open for 0% of the time, Pallas kernels for 15%

profile of v22, /device:TPU:0, one launch (start us, length us, event | category | flops | bytes accessed | tf_op | source)
XLA Modules:
  0.0 29.1 jit_solution(16792240227180176347)
XLA Ops:
  0.0 1.0 %make_message.1.refs_0_ = bf16[8,4224]{1,0:T(8,128)(2,1)S(1)} custom-call(bf16[8,4096]{1,0:T(8,128)(2,1)} %bitcast.7, s32[1,64]{1,0:T(1,128)} %bitcast.9, s32[1,64]{1,0:T(1,128)} %requests_ref.1), custom_call_target="tpu_custom_call" | custom-call | flops 99999997952 | bytes 10000 | tf_op jit(solution)/shard_map/make_message/pallas_call | solution.py:100
  1.0 5.1 %collective-permute-start = (bf16[8,4224]{1,0:T(8,128)(2,1)S(1)}, bf16[8,4224]{1,0:T(8,128)(2,1)S(1)}, u32[]{:S(2)}, u32[]{:S(2)}) collective-permute-start(bf16[8,4224]{1,0:T(8,128)(2,1)S(1)} %make_message.1.refs_0_), channel_id=1, source_target_pairs={{0,12},{4,8},{8,4},{12,0},{1,13},{5,9},{9,5},{13,1},{2,14},{6,10},... | collective-permute-start | bytes 202760 | tf_op jit(solution)/shard_map/ppermute | solution.py:388
  6.2 0.0 collective-permute-start.1
  6.2 0.6 %collective-permute-start.2 = (bf16[8,4224]{1,0:T(8,128)(2,1)S(1)}, bf16[8,4224]{1,0:T(8,128)(2,1)S(1)}, u32[]{:S(2)}, u32[]{:S(2)}) collective-permute-start(bf16[8,4224]{1,0:T(8,128)(2,1)S(1)} %make_message.1.refs_0_), channel_id=1, source_target_pairs={{0,4},{4,0},{8,12},{12,8},{1,5},{5,1},{9,13},{13,9},{2,6},{6,2},{1... | collective-permute-start | bytes 202760 | tf_op jit(solution)/shard_map/ppermute | solution.py:388
  6.8 2.3 %project.1 = (bf16[256,512]{1,0:T(8,128)(2,1)S(1)}, bf16[256,512]{1,0:T(8,128)(2,1)S(1)}) custom-call(bf16[256,4096]{1,0:T(8,128)(2,1)S(1)} %copy-done, bf16[4096,1024]{1,0:T(8,128)(2,1)S(1)} %bitcast.5), custom_call_target="tpu_custom_call" | custom-call | flops 2147483648 | bytes 10485760 | tf_op jit(solution)/shard_map/project/pallas_call | solution.py:63
  9.1 1.5 %collective-permute-start.3 = (bf16[256,512]{1,0:T(8,128)(2,1)S(1)}, bf16[256,512]{1,0:T(8,128)(2,1)S(1)}, u32[]{:S(2)}, u32[]{:S(2)}) collective-permute-start(bf16[256,512]{1,0:T(8,128)(2,1)S(1)} %get-tuple-element.16.values_ref), channel_id=1, source_target_pairs={{0,4},{4,0},{8,12},{12,8},{1,5},{5,1},{9,13},{13,9},{2,6},{6,2},{1... | collective-permute-start | bytes 786440 | tf_op jit(solution)/shard_map/ppermute | solution.py:388
  10.6 1.4 %collective-permute-done.1.refs_2_ = bf16[8,4224]{1,0:T(8,128)(2,1)S(1)} collective-permute-done((bf16[8,4224]{1,0:T(8,128)(2,1)S(1)}, bf16[8,4224]{1,0:T(8,128)(2,1)S(1)}, u32[]{:S(2)}, u32[]{:S(2)}) %collective-permute-start.1) | collective-permute-done | bytes 67616 | tf_op jit(solution)/shard_map/ppermute | solution.py:388
  12.0 0.0 collective-permute-done.2.refs_3_
  12.0 0.0 copy-start.4
  12.0 0.3 %partial_scores.1 = (bf16[32,256]{1,0:T(8,128)(2,1)S(1)}, s32[8,256]{1,0:T(8,128)S(1)}) custom-call(bf16[256,512]{1,0:T(8,128)(2,1)S(1)} %get-tuple-element.14.keys_ref, bf16[8,4224]{1,0:T(8,128)(2,1)S(1)} %make_message.1.refs_0_, bf16[8,4224]{1,0:T(8,128)(2,1)S(1)} %collective-permute-done.refs_1_, bf16[8,4224]{1,0:T(8,128)(2,1)S(1)} %collective-permute-done.1.refs_2_, ...), custom_call_target="tpu_custom_call" | custom-call | flops 99999997952 | bytes 10000 | tf_op jit(solution)/shard_map/partial_scores/pallas_call | solution.py:245
  12.3 1.5 %collective-permute-start.4 = (bf16[32,256]{1,0:T(8,128)(2,1)S(1)}, bf16[32,256]{1,0:T(8,128)(2,1)S(1)}, u32[]{:S(2)}, u32[]{:S(2)}) collective-permute-start(bf16[32,256]{1,0:T(8,128)(2,1)S(1)} %get-tuple-element.19.refs_0_), channel_id=1, source_target_pairs={{0,4},{4,8},{8,12},{12,0},{1,5},{5,9},{9,13},{13,1},{2,6},{6,10},{... | collective-permute-start | bytes 49160 | tf_op jit(solution)/shard_map/ppermute | solution.py:393
  13.8 1.8 %collective-permute-start.5 = (bf16[32,256]{1,0:T(8,128)(2,1)S(1)}, bf16[32,256]{1,0:T(8,128)(2,1)S(1)}, u32[]{:S(2)}, u32[]{:S(2)}) collective-permute-start(bf16[32,256]{1,0:T(8,128)(2,1)S(1)} %get-tuple-element.19.refs_0_), channel_id=1, source_target_pairs={{0,8},{4,12},{8,0},{12,4},{1,9},{5,13},{9,1},{13,5},{2,10},{6,14},... | collective-permute-start | bytes 49160 | tf_op jit(solution)/shard_map/ppermute | solution.py:393
  15.6 1.3 %collective-permute-start.6 = (bf16[32,256]{1,0:T(8,128)(2,1)S(1)}, bf16[32,256]{1,0:T(8,128)(2,1)S(1)}, u32[]{:S(2)}, u32[]{:S(2)}) collective-permute-start(bf16[32,256]{1,0:T(8,128)(2,1)S(1)} %get-tuple-element.19.refs_0_), channel_id=1, source_target_pairs={{0,12},{4,0},{8,4},{12,8},{1,13},{5,1},{9,5},{13,9},{2,14},{6,2},{... | collective-permute-start | bytes 49160 | tf_op jit(solution)/shard_map/ppermute | solution.py:393
  16.9 1.6 %cache_part.1 = (f32[8,4096]{1,0:T(8,128)S(1)}, f32[16,128]{1,0:T(8,128)S(1)}) custom-call(s32[1,1,8]{2,1,0:T(1,128)S(1)} %copy-done.4, bf16[8,4096]{1,0:T(8,128)(2,1)S(1)} %bitcast.8, bf16[8,128,1024]{2,1,0:T(8,128)(2,1)S(1)} %bitcast.6, s32[8,128]{1,0:T(8,128)S(1)} %copy-done.3), custom_call_target="tpu_custom_call" | custom-call | flops 16777216 | bytes 2097152 | tf_op jit(solution)/shard_map/cache_part/pallas_call | solution.py:189
  18.5 0.6 %collective-permute-done.4.refs_1_ = bf16[32,256]{1,0:T(8,128)(2,1)S(1)} collective-permute-done((bf16[32,256]{1,0:T(8,128)(2,1)S(1)}, bf16[32,256]{1,0:T(8,128)(2,1)S(1)}, u32[]{:S(2)}, u32[]{:S(2)}) %collective-permute-start.4) | collective-permute-done | bytes 16416 | tf_op jit(solution)/shard_map/ppermute | solution.py:393
  19.1 0.0 collective-permute-done.5.refs_2_
  19.1 0.2 collective-permute-done.6.refs_3_
  19.3 0.4 %mix.1 = (bf16[8,4480]{1,0:T(8,128)(2,1)S(1)}, bf16[8,4480]{1,0:T(8,128)(2,1)S(1)}, bf16[8,4480]{1,0:T(8,128)(2,1)S(1)}) custom-call(s32[8,256]{1,0:T(8,128)S(1)} %get-tuple-element.15.code_ref, bf16[256,512]{1,0:T(8,128)(2,1)S(1)} %get-tuple-element.16.values_ref, bf16[256,512]{1,0:T(8,128)(2,1)S(1)} %collective-permute-done.3.near_ref, ...), custom_call_target="tpu_custom_call" | custom-call | tf_op jit(solution)/shard_map/mix/pallas_call | solution.py:331
  19.8 2.1 %collective-permute-start.7 = (bf16[8,4480]{1,0:T(8,128)(2,1)S(1)}, bf16[8,4480]{1,0:T(8,128)(2,1)S(1)}, u32[]{:S(2)}, u32[]{:S(2)}) collective-permute-start(bf16[8,4480]{1,0:T(8,128)(2,1)S(1)} %get-tuple-element.20.own_first_ref), channel_id=1, source_target_pairs={{0,10},{2,8},{4,6},{6,4},{8,2},{10,0},{12,14},{14,12},{1,11},{3,9}... | collective-permute-start | bytes 215048 | tf_op jit(solution)/shard_map/ppermute | solution.py:417
  21.9 1.8 %collective-permute-start.8 = (bf16[8,4480]{1,0:T(8,128)(2,1)S(1)}, bf16[8,4480]{1,0:T(8,128)(2,1)S(1)}, u32[]{:S(2)}, u32[]{:S(2)}) collective-permute-start(bf16[8,4480]{1,0:T(8,128)(2,1)S(1)} %get-tuple-element.22), channel_id=1, source_target_pairs={{0,8},{4,12},{8,0},{12,4},{1,9},{5,13},{9,1},{13,5},{2,10},{6,14},... | collective-permute-start | bytes 215048 | tf_op jit(solution)/shard_map/ppermute | solution.py:388
  23.7 0.5 %collective-permute-start.9 = (bf16[8,4480]{1,0:T(8,128)(2,1)S(1)}, bf16[8,4480]{1,0:T(8,128)(2,1)S(1)}, u32[]{:S(2)}, u32[]{:S(2)}) collective-permute-start(bf16[8,4480]{1,0:T(8,128)(2,1)S(1)} %get-tuple-element.21.own_last_ref), channel_id=1, source_target_pairs={{0,2},{2,0},{4,14},{6,12},{8,10},{10,8},{12,6},{14,4},{1,3},{3,1},... | collective-permute-start | bytes 215048 | tf_op jit(solution)/shard_map/ppermute | solution.py:419
  24.2 1.7 %collective-permute-done.7.refs_0_ = bf16[8,4480]{1,0:T(8,128)(2,1)S(1)} collective-permute-done((bf16[8,4480]{1,0:T(8,128)(2,1)S(1)}, bf16[8,4480]{1,0:T(8,128)(2,1)S(1)}, u32[]{:S(2)}, u32[]{:S(2)}) %collective-permute-start.7) | collective-permute-done | bytes 71712 | tf_op jit(solution)/shard_map/ppermute | solution.py:417
  26.0 2.2 %collective-permute-done.8.refs_1_ = bf16[8,4480]{1,0:T(8,128)(2,1)S(1)} collective-permute-done((bf16[8,4480]{1,0:T(8,128)(2,1)S(1)}, bf16[8,4480]{1,0:T(8,128)(2,1)S(1)}, u32[]{:S(2)}, u32[]{:S(2)}) %collective-permute-start.8) | collective-permute-done | bytes 71712 | tf_op jit(solution)/shard_map/ppermute | solution.py:388
  28.1 1.0 %finish.1 = bf16[8,4096]{1,0:T(8,128)(2,1)} custom-call(bf16[8,4480]{1,0:T(8,128)(2,1)S(1)} %get-tuple-element.20.own_first_ref, bf16[8,4480]{1,0:T(8,128)(2,1)S(1)} %get-tuple-element.21.own_last_ref, bf16[8,4480]{1,0:T(8,128)(2,1)S(1)} %collective-permute-done.7.refs_0_, bf16[8,4480]{1,0:T(8,128)(2,1)S(1)} %collective-permute-done.8.refs_1_, ...), custom_call_target="tpu_custom_call" | custom-call | tf_op jit(solution)/shard_map/finish/pallas_call | solution.py:378
  (17 shorter events, 0.0 us)
Async XLA Ops:
  0.0 6.8 %slice-start = ((s8[8388608]{0:T(1024)(128)(4,1)}), s8[4194304]{0:T(1024)(128)(4,1)S(1)}, s32[]{:S(2)}) async-start(s8[8388608]{0:T(1024)(128)(4,1)} %bitcast.4), calls=%async_computation | async-start | bytes 8388608
  0.0 6.8 %slice-start.1 = ((s8[8388608]{0:T(1024)(128)(4,1)}), s8[4194304]{0:T(1024)(128)(4,1)S(1)}, s32[]{:S(2)}) async-start(s8[8388608]{0:T(1024)(128)(4,1)} %bitcast.4), calls=%async_computation.1 | async-start | bytes 8388608
  0.0 6.8 %copy-start = (bf16[256,4096]{1,0:T(8,128)(2,1)S(1)}, bf16[256,4096]{1,0:T(8,128)(2,1)}, u32[]{:S(2)}) copy-start(bf16[256,4096]{1,0:T(8,128)(2,1)} %tokens_ref.1) | copy-start | bytes 6291460
  1.0 9.6 %collective-permute-start = (bf16[8,4224]{1,0:T(8,128)(2,1)S(1)}, bf16[8,4224]{1,0:T(8,128)(2,1)S(1)}, u32[]{:S(2)}, u32[]{:S(2)}) collective-permute-start(bf16[8,4224]{1,0:T(8,128)(2,1)S(1)} %make_message.1.refs_0_), channel_id=1, source_target_pairs={{0,12},{4,8},{8,4},{12,0},{1,13},{5,9},{9,5},{13,1},{2,14},{6,10},... | collective-permute-start | bytes 202760 | tf_op jit(solution)/shard_map/ppermute | solution.py:388
  6.2 5.8 %collective-permute-start.1 = (bf16[8,4224]{1,0:T(8,128)(2,1)S(1)}, bf16[8,4224]{1,0:T(8,128)(2,1)S(1)}, u32[]{:S(2)}, u32[]{:S(2)}) collective-permute-start(bf16[8,4224]{1,0:T(8,128)(2,1)S(1)} %make_message.1.refs_0_), channel_id=1, source_target_pairs={{0,8},{4,12},{8,0},{12,4},{1,9},{5,13},{9,1},{13,5},{2,10},{6,14},... | collective-permute-start | bytes 202760 | tf_op jit(solution)/shard_map/ppermute | solution.py:388
  6.2 5.8 %collective-permute-start.2 = (bf16[8,4224]{1,0:T(8,128)(2,1)S(1)}, bf16[8,4224]{1,0:T(8,128)(2,1)S(1)}, u32[]{:S(2)}, u32[]{:S(2)}) collective-permute-start(bf16[8,4224]{1,0:T(8,128)(2,1)S(1)} %make_message.1.refs_0_), channel_id=1, source_target_pairs={{0,4},{4,0},{8,12},{12,8},{1,5},{5,1},{9,13},{13,9},{2,6},{6,2},{1... | collective-permute-start | bytes 202760 | tf_op jit(solution)/shard_map/ppermute | solution.py:388
  9.1 10.2 %collective-permute-start.3 = (bf16[256,512]{1,0:T(8,128)(2,1)S(1)}, bf16[256,512]{1,0:T(8,128)(2,1)S(1)}, u32[]{:S(2)}, u32[]{:S(2)}) collective-permute-start(bf16[256,512]{1,0:T(8,128)(2,1)S(1)} %get-tuple-element.16.values_ref), channel_id=1, source_target_pairs={{0,4},{4,0},{8,12},{12,8},{1,5},{5,1},{9,13},{13,9},{2,6},{6,2},{1... | collective-permute-start | bytes 786440 | tf_op jit(solution)/shard_map/ppermute | solution.py:388
  12.0 4.9 %copy-start.1 = (bf16[1,1,8,128,1024]{4,3,2,1,0:T(8,128)(2,1)S(1)}, bf16[1,1,8,128,1024]{4,3,2,1,0:T(8,128)(2,1)}, u32[]{:S(2)}) copy-start(bf16[1,1,8,128,1024]{4,3,2,1,0:T(8,128)(2,1)} %param.14) | copy-start | bytes 6291460
  12.0 4.9 %copy-start.2 = (bf16[1,1,8,4096]{3,2,1,0:T(8,128)(2,1)S(1)}, bf16[1,1,8,4096]{3,2,1,0:T(8,128)(2,1)}, u32[]{:S(2)}) copy-start(bf16[1,1,8,4096]{3,2,1,0:T(8,128)(2,1)} %param.13) | copy-start | bytes 196612
  12.0 4.9 %copy-start.3 = (s32[8,128]{1,0:T(8,128)S(1)}, s32[8,128]{1,0:T(8,128)}, u32[]{:S(2)}) copy-start(s32[8,128]{1,0:T(8,128)} %signs_ref.1) | copy-start | bytes 12292
  12.0 4.9 %copy-start.4 = (s32[1,1,8]{2,1,0:T(1,128)S(1)}, s32[1,1,8]{2,1,0:T(1,128)}, u32[]{:S(2)}) copy-start(s32[1,1,8]{2,1,0:T(1,128)} %lengths_ref.1) | copy-start | bytes 100
  12.3 6.8 %collective-permute-start.4 = (bf16[32,256]{1,0:T(8,128)(2,1)S(1)}, bf16[32,256]{1,0:T(8,128)(2,1)S(1)}, u32[]{:S(2)}, u32[]{:S(2)}) collective-permute-start(bf16[32,256]{1,0:T(8,128)(2,1)S(1)} %get-tuple-element.19.refs_0_), channel_id=1, source_target_pairs={{0,4},{4,8},{8,12},{12,0},{1,5},{5,9},{9,13},{13,1},{2,6},{6,10},{... | collective-permute-start | bytes 49160 | tf_op jit(solution)/shard_map/ppermute | solution.py:393
  13.8 5.3 %collective-permute-start.5 = (bf16[32,256]{1,0:T(8,128)(2,1)S(1)}, bf16[32,256]{1,0:T(8,128)(2,1)S(1)}, u32[]{:S(2)}, u32[]{:S(2)}) collective-permute-start(bf16[32,256]{1,0:T(8,128)(2,1)S(1)} %get-tuple-element.19.refs_0_), channel_id=1, source_target_pairs={{0,8},{4,12},{8,0},{12,4},{1,9},{5,13},{9,1},{13,5},{2,10},{6,14},... | collective-permute-start | bytes 49160 | tf_op jit(solution)/shard_map/ppermute | solution.py:393
  15.6 3.7 %collective-permute-start.6 = (bf16[32,256]{1,0:T(8,128)(2,1)S(1)}, bf16[32,256]{1,0:T(8,128)(2,1)S(1)}, u32[]{:S(2)}, u32[]{:S(2)}) collective-permute-start(bf16[32,256]{1,0:T(8,128)(2,1)S(1)} %get-tuple-element.19.refs_0_), channel_id=1, source_target_pairs={{0,12},{4,0},{8,4},{12,8},{1,13},{5,1},{9,5},{13,9},{2,14},{6,2},{... | collective-permute-start | bytes 49160 | tf_op jit(solution)/shard_map/ppermute | solution.py:393
  19.8 6.2 %collective-permute-start.7 = (bf16[8,4480]{1,0:T(8,128)(2,1)S(1)}, bf16[8,4480]{1,0:T(8,128)(2,1)S(1)}, u32[]{:S(2)}, u32[]{:S(2)}) collective-permute-start(bf16[8,4480]{1,0:T(8,128)(2,1)S(1)} %get-tuple-element.20.own_first_ref), channel_id=1, source_target_pairs={{0,10},{2,8},{4,6},{6,4},{8,2},{10,0},{12,14},{14,12},{1,11},{3,9}... | collective-permute-start | bytes 215048 | tf_op jit(solution)/shard_map/ppermute | solution.py:417
  21.9 6.2 %collective-permute-start.8 = (bf16[8,4480]{1,0:T(8,128)(2,1)S(1)}, bf16[8,4480]{1,0:T(8,128)(2,1)S(1)}, u32[]{:S(2)}, u32[]{:S(2)}) collective-permute-start(bf16[8,4480]{1,0:T(8,128)(2,1)S(1)} %get-tuple-element.22), channel_id=1, source_target_pairs={{0,8},{4,12},{8,0},{12,4},{1,9},{5,13},{9,1},{13,5},{2,10},{6,14},... | collective-permute-start | bytes 215048 | tf_op jit(solution)/shard_map/ppermute | solution.py:388
  23.7 4.4 %collective-permute-start.9 = (bf16[8,4480]{1,0:T(8,128)(2,1)S(1)}, bf16[8,4480]{1,0:T(8,128)(2,1)S(1)}, u32[]{:S(2)}, u32[]{:S(2)}) collective-permute-start(bf16[8,4480]{1,0:T(8,128)(2,1)S(1)} %get-tuple-element.21.own_last_ref), channel_id=1, source_target_pairs={{0,2},{2,0},{4,14},{6,12},{8,10},{10,8},{12,6},{14,4},{1,3},{3,1},... | collective-permute-start | bytes 215048 | tf_op jit(solution)/shard_map/ppermute | solution.py:419

commit v23 on v19

--- a/solution.py
+++ b/solution.py
@@ -35,9 +35,9 @@
     return (1 - 2 * (parity & 1)).astype(jnp.float32).astype(jnp.bfloat16)
 
 
-QUERY_ORDER = (3, 2, 1)
-SCORE_ORDER = (1, 2, 3)
-FINISH_PLACES = (2, 1, 0)
+QUERY_ORDER = (1, 2, 3)
+SCORE_ORDER = (3, 2, 1)
+FINISH_PLACES = (1, 0, 2)
 
 
 def arranged(blocks, order):
@@ -75,7 +75,7 @@
     )(in_vmem(tokens), in_vmem(weight))
 
 
-def message_kernel(query_ref, owners_ref, requests_ref, out_ref, owners_buf, requests_buf, sems):
+def message_kernel(after_ref, query_ref, owners_ref, requests_ref, out_ref, owners_buf, requests_buf, sems):
     requests, columns = query_ref.shape
     per_device = owners_ref.shape[1]
     copies = [
@@ -94,12 +94,12 @@
     copies[0].wait()
 
 
-def make_message(query, owners, requests):
+def make_message(after, query, owners, requests):
     count, columns = query.shape
     lanes = -(-owners.shape[1] // 128) * 128
     return pl.pallas_call(
         message_kernel,
-        in_specs=[pl.BlockSpec(memory_space=pl.ANY)] * 3,
+        in_specs=[pl.BlockSpec(memory_space=pl.ANY)] * 4,
         out_specs=pl.BlockSpec(memory_space=pltpu.VMEM),
         out_shape=jax.ShapeDtypeStruct((count, columns + lanes), query.dtype),
         scratch_shapes=[
@@ -110,7 +110,7 @@
         compiler_params=params(16),
         cost_estimate=pl.CostEstimate(flops=10**11, bytes_accessed=10**4, transcendentals=0),
         name="make_message",
-    )(in_hbm(query), in_hbm(owners), in_hbm(requests))
+    )(after, in_hbm(query), in_hbm(owners), in_hbm(requests))
 
 
 def cache_kernel(
@@ -181,19 +181,76 @@
     stats_ref[requests:, :] = totals
 
 
-def cache_part(lengths, query, cache, signs):
+def early_kernel(
+    lengths_ref, query_ref, cache_ref, signs_ref, mixed_ref, stats_ref, lengths_in, query_in, cache_in, signs_in, sems, *bufs
+):
+    @pl.when(lax.axis_index("section") == 1)
+    def _():
+        places = (lengths_in, query_in, cache_in, signs_in)
+        copies = [
+            pltpu.make_async_copy(source, place, sems.at[i])
+            for i, (source, place) in enumerate(zip((lengths_ref, query_ref, cache_ref, signs_ref), places))
+        ]
+        for copy in copies:
+            copy.start()
+        for copy in copies:
+            copy.wait()
+        cache_kernel(lengths_in, query_in, cache_in, signs_in, mixed_ref, stats_ref, *bufs)
+
+
+def late_kernel(lengths_ref, query_ref, cache_ref, signs_ref, early_mixed, early_stats, mixed_ref, stats_ref, *bufs):
+    early = lax.axis_index("section") == 1
+
+    @pl.when(early)
+    def _():
+        mixed_ref[...] = early_mixed[...]
+        stats_ref[...] = early_stats[...]
+
+    @pl.when(jnp.logical_not(early))
+    def _():
+        cache_kernel(lengths_ref, query_ref, cache_ref, signs_ref, mixed_ref, stats_ref, *bufs)
+
+
+def cache_shapes(query, size):
+    requests, columns = query.shape
+    outputs = [
+        jax.ShapeDtypeStruct(query.shape, jnp.float32),
+        jax.ShapeDtypeStruct((2 * requests, size), jnp.float32),
+    ]
+    return outputs, [pltpu.VMEM((requests * columns // size, size), jnp.float32)] * 4
+
+
+def early_cache_part(lengths, query, cache, signs):
+    outputs, buffers = cache_shapes(query, signs.shape[1])
+    return pl.pallas_call(
+        early_kernel,
+        in_specs=[pl.BlockSpec(memory_space=pl.ANY)] * 4,
+        out_specs=[pl.BlockSpec(memory_space=pltpu.VMEM)] * 2,
+        out_shape=outputs,
+        scratch_shapes=[
+            pltpu.SMEM(lengths.shape, lengths.dtype),
+            pltpu.VMEM(query.shape, query.dtype),
+            pltpu.VMEM(cache.shape, cache.dtype),
+            pltpu.VMEM(signs.shape, signs.dtype),
+            pltpu.SemaphoreType.DMA((4,)),
+        ]
+        + buffers,
+        compiler_params=params(16),
+        name="early_cache_part",
+    )(in_hbm(lengths), in_hbm(query), in_hbm(cache), in_hbm(signs))
+
+
+def cache_part(lengths, query, cache, signs, early):
     requests, span, width = cache.shape
     size = signs.shape[1]
     columns = query.shape[1]
+    outputs, buffers = cache_shapes(query, size)
     vmem = pl.BlockSpec(memory_space=pltpu.VMEM)
     return pl.pallas_call(
-        cache_kernel,
-        in_specs=[pl.BlockSpec(memory_space=pltpu.SMEM)] + [vmem] * 3,
-        out_shape=[
-            jax.ShapeDtypeStruct(query.shape, jnp.float32),
-            jax.ShapeDtypeStruct((2 * requests, size), jnp.float32),
-        ],
-        scratch_shapes=[pltpu.VMEM((requests * columns // size, size), jnp.float32)] * 4,
+        late_kernel,
+        in_specs=[pl.BlockSpec(memory_space=pltpu.SMEM)] + [vmem] * 5,
+        out_shape=outputs,
+        scratch_shapes=buffers,
         compiler_params=params(),
         cost_estimate=pl.CostEstimate(
             flops=4 * span * requests * columns,
@@ -201,7 +258,7 @@
             transcendentals=span * requests * columns // size,
         ),
         name="cache_part",
-    )(lengths, query, cache, signs)
+    )(lengths, query, cache, signs, *early)
 
 
 def code_row(message_refs, start, requests, tokens):
@@ -270,7 +327,7 @@
 
 def mix_kernel(heads, requests, code_ref, values_ref, near_ref, cache_ref, cache_stats_ref, *refs):
     score_refs, (share_ref, far_ref) = refs[:4], refs[4:]
-    own, before, across, after = [ref[...].astype(jnp.float32) for ref in score_refs]
+    own, after, across, before = [ref[...].astype(jnp.float32) for ref in score_refs]
     scores = (own + across) + (before + after)
     tokens, width = values_ref.shape
     size = width // heads
@@ -331,8 +388,8 @@
     )(code, values, near_values, cache_mixed, cache_stats, *arranged(scores, SCORE_ORDER))
 
 
-def finish_kernel(count, own_ref, *refs):
-    out_ref = refs[-1]
+def finish_kernel(count, *refs):
+    own_ref, out_ref = refs[-2:]
     other_ref, own_far_ref, other_far_ref = [refs[i] for i in FINISH_PLACES]
     columns = out_ref.shape[1]
     size = columns // count
@@ -374,7 +431,7 @@
         out_shape=jax.ShapeDtypeStruct((own.shape[0], columns), jnp.bfloat16),
         compiler_params=params(),
         name="finish",
-    )(own, *[arrived[FINISH_PLACES.index(i)] for i in range(3)])
+    )(*[arrived[FINISH_PLACES.index(i)] for i in range(3)], own)
 
 
 def from_partner(x, axis, distance):
@@ -392,13 +449,14 @@
     heads = signs.shape[0] // 2
     query = queries[0, 0]
     request_count, columns = query.shape
-    message = make_message(query, owners[:, :, 0], requests)
+    early = early_cache_part(lengths, query, kv_cache[0, 0], signs)
+    message = make_message(early[1], query, owners[:, :, 0], requests)
     messages = [message] + [from_partner(message, "seq", d) for d in range(1, seq_count)]
     keys, values = project(tokens, kv_weight)
     near_values = from_partner(values, "seq", 1)
     scores, code = partial_scores(heads, columns, keys, messages)
     scores = [scores] + [from_behind(scores, "seq", d) for d in range(1, seq_count)]
-    cache_mixed, cache_stats = cache_part(lengths, query, kv_cache[0, 0], signs)
+    cache_mixed, cache_stats = cache_part(lengths, query, kv_cache[0, 0], signs, early)
     share, far = mix(heads, code, values, near_values, cache_mixed, cache_stats, scores)
     far_pairs = [(i, i ^ 5) for i in range(2 * seq_count)]
     output = finish(

time: 29.2 us -> 32.9 us (1.13)
  waiting for transfers between devices: 6.08 us -> 10.4 us
  starting transfers between devices: 16.2 us -> 15.6 us
    ppermute x1, waiting for transfers between devices: 2.7 us -> 5.56 us  [on_device(): lax.ppermute(far, ('seq', 'tp'), far_pairs)]
    ppermute x6, waiting for transfers between devices: 2.53 us -> 3.97 us  [from_partner(): return lax.ppermute(x, axis, [(i, i ^ distance) for i in range(count)])]
    ppermute x3, starting transfers between devices: 4.52 us -> 3.87 us  [from_behind(): lax.ppermute(x, axis, [(i, (i + distance) % count) for i in range(count)])]
    pallas_call x1 -> x2, Pallas kernels: 1.6 us -> 1.65 us  [the longest x1 1.61 us: cache_part(): pl.pallas_call(late_kernel, in_specs=[pl.BlockSpec(memory_space=pltpu.SME...]
  transfers between devices with their start and end apart: 10 -> 10, of which waited for: 5 -> 5; matrix products, arithmetic and copies ran while one was open for 0% -> 0% of each run, Pallas kernels for 15% -> 13%
where the time goes in v23:
time: 32.9 us; the launch traced here: 32.8 us
  starting transfers between devices  15.6 us (47%)
  waiting for transfers between devices  10.4 us (32%)
  Pallas kernels  6.72 us (20%)
    ppermute x6, starting transfers between devices, from_partner(): return lax.ppermute(x, axis, [(i, i ^ distance) for i in range(count)])  9.46 us
    ppermute x1, waiting for transfers between devices, on_device(): lax.ppermute(far, ('seq', 'tp'), far_pairs)  5.56 us
    ppermute x6, waiting for transfers between devices, from_partner(): return lax.ppermute(x, axis, [(i, i ^ distance) for i in range(count)])  3.97 us
    ppermute x3, starting transfers between devices, from_behind(): lax.ppermute(x, axis, [(i, (i + distance) % count) for i in range(count)])  3.87 us
    pallas_call x1, Pallas kernels, project(): pl.pallas_call(project_kernel, in_specs=[vmem] * 2, out_specs=[vmem] * 2,...  2.32 us
    ppermute x1, starting transfers between devices, on_device(): lax.ppermute(far, ('seq', 'tp'), far_pairs)  2.22 us
    pallas_call x1, Pallas kernels, cache_part(): pl.pallas_call(late_kernel, in_specs=[pl.BlockSpec(memory_space=pltpu.SME...  1.61 us
    pallas_call x1, Pallas kernels, make_message(): pl.pallas_call(message_kernel, in_specs=[pl.BlockSpec(memory_space=pl.ANY...  1.02 us
  transfers between devices with their start and end apart: 10, of which 5 were waited for; matrix products, arithmetic and copies ran while one was open for 0% of the time, Pallas kernels for 13%

profile of v23, /device:TPU:0, one launch (start us, length us, event | category | flops | bytes accessed | tf_op | source)
XLA Modules:
  0.0 32.8 jit_solution(4380460007290180850)
XLA Ops:
  0.0 0.0 slice-start
  0.1 0.0 copy-start.1
  0.1 1.0 %make_message.1.refs_0_ = bf16[8,4224]{1,0:T(8,128)(2,1)S(1)} custom-call(f32[16,128]{1,0:T(8,128)S(1)} %get-tuple-element.16.after_ref.early_stats, bf16[8,4096]{1,0:T(8,128)(2,1)} %bitcast.9, s32[1,64]{1,0:T(1,128)} %bitcast.11, s32[1,64]{1,0:T(1,128)} %requests_ref.1), custom_call_target="tpu_custom_call" | custom-call | flops 99999997952 | bytes 10000 | tf_op jit(solution)/shard_map/make_message/pallas_call | solution.py:100
  1.1 5.1 %collective-permute-start.2 = (bf16[8,4224]{1,0:T(8,128)(2,1)S(1)}, bf16[8,4224]{1,0:T(8,128)(2,1)S(1)}, u32[]{:S(2)}, u32[]{:S(2)}) collective-permute-start(bf16[8,4224]{1,0:T(8,128)(2,1)S(1)} %make_message.1.refs_0_), channel_id=1, source_target_pairs={{0,12},{4,8},{8,4},{12,0},{1,13},{5,9},{9,5},{13,1},{2,14},{6,10},... | collective-permute-start | bytes 202760 | tf_op jit(solution)/shard_map/ppermute | solution.py:439
  6.2 0.0 collective-permute-start.1
  6.2 0.6 %collective-permute-start = (bf16[8,4224]{1,0:T(8,128)(2,1)S(1)}, bf16[8,4224]{1,0:T(8,128)(2,1)S(1)}, u32[]{:S(2)}, u32[]{:S(2)}) collective-permute-start(bf16[8,4224]{1,0:T(8,128)(2,1)S(1)} %make_message.1.refs_0_), channel_id=1, source_target_pairs={{0,4},{4,0},{8,12},{12,8},{1,5},{5,1},{9,13},{13,9},{2,6},{6,2},{1... | collective-permute-start | bytes 202760 | tf_op jit(solution)/shard_map/ppermute | solution.py:439
  6.9 2.3 %project.1 = (bf16[256,512]{1,0:T(8,128)(2,1)S(1)}, bf16[256,512]{1,0:T(8,128)(2,1)S(1)}) custom-call(bf16[256,4096]{1,0:T(8,128)(2,1)S(1)} %copy-done.1, bf16[4096,1024]{1,0:T(8,128)(2,1)S(1)} %bitcast.5), custom_call_target="tpu_custom_call" | custom-call | flops 2147483648 | bytes 10485760 | tf_op jit(solution)/shard_map/project/pallas_call | solution.py:63
  9.2 1.5 %collective-permute-start.3 = (bf16[256,512]{1,0:T(8,128)(2,1)S(1)}, bf16[256,512]{1,0:T(8,128)(2,1)S(1)}, u32[]{:S(2)}, u32[]{:S(2)}) collective-permute-start(bf16[256,512]{1,0:T(8,128)(2,1)S(1)} %get-tuple-element.18.values_ref), channel_id=1, source_target_pairs={{0,4},{4,0},{8,12},{12,8},{1,5},{5,1},{9,13},{13,9},{2,6},{6,2},{1... | collective-permute-start | bytes 786440 | tf_op jit(solution)/shard_map/ppermute | solution.py:439
  10.7 2.4 %collective-permute-done.1.refs_2_ = bf16[8,4224]{1,0:T(8,128)(2,1)S(1)} collective-permute-done((bf16[8,4224]{1,0:T(8,128)(2,1)S(1)}, bf16[8,4224]{1,0:T(8,128)(2,1)S(1)}, u32[]{:S(2)}, u32[]{:S(2)}) %collective-permute-start.1) | collective-permute-done | bytes 67616 | tf_op jit(solution)/shard_map/ppermute | solution.py:439
  13.1 0.0 copy-start.4
  13.1 0.3 partial_scores.1
  13.4 0.1 collective-permute-start.6
  13.5 0.8 %collective-permute-start.5 = (bf16[32,256]{1,0:T(8,128)(2,1)S(1)}, bf16[32,256]{1,0:T(8,128)(2,1)S(1)}, u32[]{:S(2)}, u32[]{:S(2)}) collective-permute-start(bf16[32,256]{1,0:T(8,128)(2,1)S(1)} %get-tuple-element.22.refs_0_), channel_id=1, source_target_pairs={{0,8},{4,12},{8,0},{12,4},{1,9},{5,13},{9,1},{13,5},{2,10},{6,14},... | collective-permute-start | bytes 49160 | tf_op jit(solution)/shard_map/ppermute | solution.py:444
  14.3 3.0 %collective-permute-start.4 = (bf16[32,256]{1,0:T(8,128)(2,1)S(1)}, bf16[32,256]{1,0:T(8,128)(2,1)S(1)}, u32[]{:S(2)}, u32[]{:S(2)}) collective-permute-start(bf16[32,256]{1,0:T(8,128)(2,1)S(1)} %get-tuple-element.22.refs_0_), channel_id=1, source_target_pairs={{0,12},{4,0},{8,4},{12,8},{1,13},{5,1},{9,5},{13,9},{2,14},{6,2},{... | collective-permute-start | bytes 49160 | tf_op jit(solution)/shard_map/ppermute | solution.py:444
  17.3 1.6 %cache_part.1 = (f32[8,4096]{1,0:T(8,128)S(1)}, f32[16,128]{1,0:T(8,128)S(1)}) custom-call(s32[1,1,8]{2,1,0:T(1,128)S(1)} %copy-done.4, bf16[8,4096]{1,0:T(8,128)(2,1)S(1)} %bitcast.10, bf16[8,128,1024]{2,1,0:T(8,128)(2,1)S(1)} %bitcast.7, s32[8,128]{1,0:T(8,128)S(1)} %copy-done.3, f32[8,4096]{1,0:T(8,128)S(1)} %get-tuple-element.19.early_mixed, ...), custom_call_target="tpu_custom_call" | custom-call | flops 16777216 | bytes 2097152 | tf_op jit(solution)/shard_map/cache_part/pallas_call | solution.py:249
  18.9 0.6 %collective-permute-done.6.refs_3_ = bf16[32,256]{1,0:T(8,128)(2,1)S(1)} collective-permute-done((bf16[32,256]{1,0:T(8,128)(2,1)S(1)}, bf16[32,256]{1,0:T(8,128)(2,1)S(1)}, u32[]{:S(2)}, u32[]{:S(2)}) %collective-permute-start.6) | collective-permute-done | bytes 16416 | tf_op jit(solution)/shard_map/ppermute | solution.py:444
  19.6 0.2 collective-permute-done.4.refs_1_
  19.8 0.4 %mix.1 = (bf16[8,4480]{1,0:T(8,128)(2,1)S(1)}, bf16[8,4480]{1,0:T(8,128)(2,1)S(1)}) custom-call(s32[8,256]{1,0:T(8,128)S(1)} %get-tuple-element.17.code_ref, bf16[256,512]{1,0:T(8,128)(2,1)S(1)} %get-tuple-element.18.values_ref, bf16[256,512]{1,0:T(8,128)(2,1)S(1)} %collective-permute-done.3.near_ref, f32[8,4096]{1,0:T(8,128)S(1)} %get-tuple-element.20.cache_ref, ...), custom_call_target="tpu_custom_call" | custom-call | tf_op jit(solution)/shard_map/mix/pallas_call | solution.py:380
  20.2 2.2 %collective-permute-start.9 = (bf16[8,4480]{1,0:T(8,128)(2,1)S(1)}, bf16[8,4480]{1,0:T(8,128)(2,1)S(1)}, u32[]{:S(2)}, u32[]{:S(2)}) collective-permute-start(bf16[8,4480]{1,0:T(8,128)(2,1)S(1)} %get-tuple-element.23), channel_id=1, source_target_pairs={{0,10},{2,8},{4,14},{6,12},{8,2},{10,0},{12,6},{14,4},{1,11},{3,9}... | collective-permute-start | bytes 215048 | tf_op jit(solution)/shard_map/ppermute | solution.py:468
  22.4 1.7 %collective-permute-start.7 = (bf16[8,4480]{1,0:T(8,128)(2,1)S(1)}, bf16[8,4480]{1,0:T(8,128)(2,1)S(1)}, u32[]{:S(2)}, u32[]{:S(2)}) collective-permute-start(bf16[8,4480]{1,0:T(8,128)(2,1)S(1)} %get-tuple-element.23), channel_id=1, source_target_pairs={{0,8},{4,12},{8,0},{12,4},{1,9},{5,13},{9,1},{13,5},{2,10},{6,14},... | collective-permute-start | bytes 215048 | tf_op jit(solution)/shard_map/ppermute | solution.py:439
  24.1 0.6 %collective-permute-start.8 = (bf16[8,4480]{1,0:T(8,128)(2,1)S(1)}, bf16[8,4480]{1,0:T(8,128)(2,1)S(1)}, u32[]{:S(2)}, u32[]{:S(2)}) collective-permute-start(bf16[8,4480]{1,0:T(8,128)(2,1)S(1)} %get-tuple-element.24.refs_3_), channel_id=1, source_target_pairs={{0,2},{2,0},{1,3},{3,1},{4,6},{6,4},{5,7},{7,5},{8,10},{10,8},{9,1... | collective-permute-start | bytes 215048 | tf_op jit(solution)/shard_map/ppermute | solution.py:439
  24.7 5.6 %collective-permute-done.9.refs_2_ = bf16[8,4480]{1,0:T(8,128)(2,1)S(1)} collective-permute-done((bf16[8,4480]{1,0:T(8,128)(2,1)S(1)}, bf16[8,4480]{1,0:T(8,128)(2,1)S(1)}, u32[]{:S(2)}, u32[]{:S(2)}) %collective-permute-start.9) | collective-permute-done | bytes 71712 | tf_op jit(solution)/shard_map/ppermute | solution.py:468
  30.3 1.5 %collective-permute-done.7.refs_0_ = bf16[8,4480]{1,0:T(8,128)(2,1)S(1)} collective-permute-done((bf16[8,4480]{1,0:T(8,128)(2,1)S(1)}, bf16[8,4480]{1,0:T(8,128)(2,1)S(1)}, u32[]{:S(2)}, u32[]{:S(2)}) %collective-permute-start.7) | collective-permute-done | bytes 71712 | tf_op jit(solution)/shard_map/ppermute | solution.py:439
  31.8 1.0 %finish.1 = bf16[8,4096]{1,0:T(8,128)(2,1)} custom-call(bf16[8,4480]{1,0:T(8,128)(2,1)S(1)} %collective-permute-done.7.refs_0_, bf16[8,4480]{1,0:T(8,128)(2,1)S(1)} %collective-permute-done.8.refs_1_, bf16[8,4480]{1,0:T(8,128)(2,1)S(1)} %collective-permute-done.9.refs_2_, bf16[8,4480]{1,0:T(8,128)(2,1)S(1)} %get-tuple-element.24.refs_3_), custom_call_target="tpu_custom_call" | custom-call | tf_op jit(solution)/shard_map/finish/pallas_call | solution.py:429
  (18 shorter events, 0.1 us)
Async XLA Ops:
  0.0 6.8 %slice-start = ((s8[8388608]{0:T(1024)(128)(4,1)}), s8[4194304]{0:T(1024)(128)(4,1)S(1)}, s32[]{:S(2)}) async-start(s8[8388608]{0:T(1024)(128)(4,1)} %bitcast.4), calls=%async_computation | async-start | bytes 8388608
  0.1 6.8 %slice-start.1 = ((s8[8388608]{0:T(1024)(128)(4,1)}), s8[4194304]{0:T(1024)(128)(4,1)S(1)}, s32[]{:S(2)}) async-start(s8[8388608]{0:T(1024)(128)(4,1)} %bitcast.4), calls=%async_computation.1 | async-start | bytes 8388608
  0.1 6.8 %copy-start.1 = (bf16[256,4096]{1,0:T(8,128)(2,1)S(1)}, bf16[256,4096]{1,0:T(8,128)(2,1)}, u32[]{:S(2)}) copy-start(bf16[256,4096]{1,0:T(8,128)(2,1)} %tokens_ref.1) | copy-start | bytes 6291460
  1.1 9.6 %collective-permute-start.2 = (bf16[8,4224]{1,0:T(8,128)(2,1)S(1)}, bf16[8,4224]{1,0:T(8,128)(2,1)S(1)}, u32[]{:S(2)}, u32[]{:S(2)}) collective-permute-start(bf16[8,4224]{1,0:T(8,128)(2,1)S(1)} %make_message.1.refs_0_), channel_id=1, source_target_pairs={{0,12},{4,8},{8,4},{12,0},{1,13},{5,9},{9,5},{13,1},{2,14},{6,10},... | collective-permute-start | bytes 202760 | tf_op jit(solution)/shard_map/ppermute | solution.py:439
  6.2 6.9 %collective-permute-start.1 = (bf16[8,4224]{1,0:T(8,128)(2,1)S(1)}, bf16[8,4224]{1,0:T(8,128)(2,1)S(1)}, u32[]{:S(2)}, u32[]{:S(2)}) collective-permute-start(bf16[8,4224]{1,0:T(8,128)(2,1)S(1)} %make_message.1.refs_0_), channel_id=1, source_target_pairs={{0,8},{4,12},{8,0},{12,4},{1,9},{5,13},{9,1},{13,5},{2,10},{6,14},... | collective-permute-start | bytes 202760 | tf_op jit(solution)/shard_map/ppermute | solution.py:439
  6.2 6.9 %collective-permute-start = (bf16[8,4224]{1,0:T(8,128)(2,1)S(1)}, bf16[8,4224]{1,0:T(8,128)(2,1)S(1)}, u32[]{:S(2)}, u32[]{:S(2)}) collective-permute-start(bf16[8,4224]{1,0:T(8,128)(2,1)S(1)} %make_message.1.refs_0_), channel_id=1, source_target_pairs={{0,4},{4,0},{8,12},{12,8},{1,5},{5,1},{9,13},{13,9},{2,6},{6,2},{1... | collective-permute-start | bytes 202760 | tf_op jit(solution)/shard_map/ppermute | solution.py:439
  9.2 10.6 %collective-permute-start.3 = (bf16[256,512]{1,0:T(8,128)(2,1)S(1)}, bf16[256,512]{1,0:T(8,128)(2,1)S(1)}, u32[]{:S(2)}, u32[]{:S(2)}) collective-permute-start(bf16[256,512]{1,0:T(8,128)(2,1)S(1)} %get-tuple-element.18.values_ref), channel_id=1, source_target_pairs={{0,4},{4,0},{8,12},{12,8},{1,5},{5,1},{9,13},{13,9},{2,6},{6,2},{1... | collective-permute-start | bytes 786440 | tf_op jit(solution)/shard_map/ppermute | solution.py:439
  13.1 4.2 %copy-start = (bf16[1,1,8,128,1024]{4,3,2,1,0:T(8,128)(2,1)S(1)}, bf16[1,1,8,128,1024]{4,3,2,1,0:T(8,128)(2,1)}, u32[]{:S(2)}) copy-start(bf16[1,1,8,128,1024]{4,3,2,1,0:T(8,128)(2,1)} %param.14) | copy-start | bytes 6291460
  13.1 4.2 %copy-start.2 = (bf16[1,1,8,4096]{3,2,1,0:T(8,128)(2,1)S(1)}, bf16[1,1,8,4096]{3,2,1,0:T(8,128)(2,1)}, u32[]{:S(2)}) copy-start(bf16[1,1,8,4096]{3,2,1,0:T(8,128)(2,1)} %param.13) | copy-start | bytes 196612
  13.1 4.2 %copy-start.3 = (s32[8,128]{1,0:T(8,128)S(1)}, s32[8,128]{1,0:T(8,128)}, u32[]{:S(2)}) copy-start(s32[8,128]{1,0:T(8,128)} %signs_ref.3) | copy-start | bytes 12292
  13.1 4.2 %copy-start.4 = (s32[1,1,8]{2,1,0:T(1,128)S(1)}, s32[1,1,8]{2,1,0:T(1,128)}, u32[]{:S(2)}) copy-start(s32[1,1,8]{2,1,0:T(1,128)} %lengths_ref.3) | copy-start | bytes 100
  13.4 6.1 %collective-permute-start.6 = (bf16[32,256]{1,0:T(8,128)(2,1)S(1)}, bf16[32,256]{1,0:T(8,128)(2,1)S(1)}, u32[]{:S(2)}, u32[]{:S(2)}) collective-permute-start(bf16[32,256]{1,0:T(8,128)(2,1)S(1)} %get-tuple-element.22.refs_0_), channel_id=1, source_target_pairs={{0,4},{4,8},{8,12},{12,0},{1,5},{5,9},{9,13},{13,1},{2,6},{6,10},{... | collective-permute-start | bytes 49160 | tf_op jit(solution)/shard_map/ppermute | solution.py:444
  13.5 6.1 %collective-permute-start.5 = (bf16[32,256]{1,0:T(8,128)(2,1)S(1)}, bf16[32,256]{1,0:T(8,128)(2,1)S(1)}, u32[]{:S(2)}, u32[]{:S(2)}) collective-permute-start(bf16[32,256]{1,0:T(8,128)(2,1)S(1)} %get-tuple-element.22.refs_0_), channel_id=1, source_target_pairs={{0,8},{4,12},{8,0},{12,4},{1,9},{5,13},{9,1},{13,5},{2,10},{6,14},... | collective-permute-start | bytes 49160 | tf_op jit(solution)/shard_map/ppermute | solution.py:444
  14.3 5.5 %collective-permute-start.4 = (bf16[32,256]{1,0:T(8,128)(2,1)S(1)}, bf16[32,256]{1,0:T(8,128)(2,1)S(1)}, u32[]{:S(2)}, u32[]{:S(2)}) collective-permute-start(bf16[32,256]{1,0:T(8,128)(2,1)S(1)} %get-tuple-element.22.refs_0_), channel_id=1, source_target_pairs={{0,12},{4,0},{8,4},{12,8},{1,13},{5,1},{9,5},{13,9},{2,14},{6,2},{... | collective-permute-start | bytes 49160 | tf_op jit(solution)/shard_map/ppermute | solution.py:444
  20.2 10.0 %collective-permute-start.9 = (bf16[8,4480]{1,0:T(8,128)(2,1)S(1)}, bf16[8,4480]{1,0:T(8,128)(2,1)S(1)}, u32[]{:S(2)}, u32[]{:S(2)}) collective-permute-start(bf16[8,4480]{1,0:T(8,128)(2,1)S(1)} %get-tuple-element.23), channel_id=1, source_target_pairs={{0,10},{2,8},{4,14},{6,12},{8,2},{10,0},{12,6},{14,4},{1,11},{3,9}... | collective-permute-start | bytes 215048 | tf_op jit(solution)/shard_map/ppermute | solution.py:468
  22.4 9.3 %collective-permute-start.7 = (bf16[8,4480]{1,0:T(8,128)(2,1)S(1)}, bf16[8,4480]{1,0:T(8,128)(2,1)S(1)}, u32[]{:S(2)}, u32[]{:S(2)}) collective-permute-start(bf16[8,4480]{1,0:T(8,128)(2,1)S(1)} %get-tuple-element.23), channel_id=1, source_target_pairs={{0,8},{4,12},{8,0},{12,4},{1,9},{5,13},{9,1},{13,5},{2,10},{6,14},... | collective-permute-start | bytes 215048 | tf_op jit(solution)/shard_map/ppermute | solution.py:439
  24.1 7.7 %collective-permute-start.8 = (bf16[8,4480]{1,0:T(8,128)(2,1)S(1)}, bf16[8,4480]{1,0:T(8,128)(2,1)S(1)}, u32[]{:S(2)}, u32[]{:S(2)}) collective-permute-start(bf16[8,4480]{1,0:T(8,128)(2,1)S(1)} %get-tuple-element.24.refs_3_), channel_id=1, source_target_pairs={{0,2},{2,0},{1,3},{3,1},{4,6},{6,4},{5,7},{7,5},{8,10},{10,8},{9,1... | collective-permute-start | bytes 215048 | tf_op jit(solution)/shard_map/ppermute | solution.py:439

commit v24 on v20

--- a/solution.py
+++ b/solution.py
@@ -37,7 +37,7 @@
 
 QUERY_ORDER = (3, 2, 1)
 SCORE_ORDER = (1, 2, 3)
-FINISH_PLACES = (2, 0, 1)
+FINISH_PLACES = (2, 1, 0)
 
 
 def arranged(blocks, order):
@@ -255,24 +255,16 @@
 
 
 def packed(values, count):
-    rows, lanes = values[0].shape
-    lane = lax.broadcasted_iota(jnp.int32, (rows, lanes), 1)
-    tiles = [jnp.zeros((rows, lanes), jnp.float32)] * (8 * count // lanes)
-    slot = 0
-    for value, parts in zip(values, (3, 3, 2)):
-        for _ in range(parts):
-            piece = value.astype(jnp.bfloat16).astype(jnp.float32)
-            value = value - piece
-            tile, at = divmod(slot * count, lanes)
-            here = (lane >= at) & (lane < at + count)
-            tiles[tile] = jnp.where(here, pltpu.roll(piece, at, 1) if at else piece, tiles[tile])
-            slot += 1
-    return jnp.concatenate(tiles, axis=1)
+    lane = lax.broadcasted_iota(jnp.int32, values[0].shape, 1)
+    out = values[0]
+    for i, value in enumerate(values[1:], 1):
+        out = jnp.where(lane < i * count, out, pltpu.roll(value, i * count, 1))
+    return out
 
 
 def unpacked(message, count):
-    parts = [message[:, at * count : (at + 1) * count] for at in range(8)]
-    return parts[0] + parts[1] + parts[2], parts[3] + parts[4] + parts[5], parts[6] + parts[7]
+    parts = [message[:, i * count : (i + 1) * count] for i in range(4)]
+    return parts[0] + parts[1], parts[2], parts[3]
 
 
 def mix_kernel(heads, requests, code_ref, values_ref, near_ref, cache_ref, cache_stats_ref, *refs):
@@ -311,24 +303,26 @@
             far_ref[:, at] = mixed[g * span + requests : (g + 1) * span].astype(far_ref.dtype)
     cache_tops = cache_stats_ref[:requests, :]
     both = jnp.maximum(cache_tops, tops)
-    cache_factor = jnp.exp(cache_tops - both)
-    new_factor = jnp.exp(tops - both)
+    high = both.astype(jnp.bfloat16).astype(jnp.float32)
+    low = (both - high).astype(jnp.bfloat16).astype(jnp.float32)
+    cache_factor = jnp.exp(jnp.minimum(cache_tops - (high + low), 60.0))
+    new_factor = jnp.exp(jnp.minimum(tops - (high + low), 60.0))
     total = cache_stats_ref[requests:, :] * cache_factor + totals * new_factor
     for h, part in enumerate(parts):
         at = slice(h * size, (h + 1) * size)
         share = cache_ref[:, at] * cache_factor[:, h : h + 1] + part * new_factor[:, h : h + 1]
         share_ref[:, at] = share.astype(share_ref.dtype)
-    far_ref[:, columns:] = jnp.zeros((requests, 8 * count), far_ref.dtype)
-    share_ref[:, columns:] = packed((both, total, new_factor), count).astype(share_ref.dtype)
+    far_ref[:, columns:] = jnp.zeros((requests, 4 * count), far_ref.dtype)
+    share_ref[:, columns:] = packed((high, low, total, new_factor), count).astype(share_ref.dtype)
 
 
 def mix(heads, code, values, near_values, cache_mixed, cache_stats, scores):
-    requests, columns = cache_mixed.shape
-    count = columns // (values.shape[1] // heads)
+    requests, lanes = cache_stats.shape[0] // 2, cache_stats.shape[1]
+    columns = cache_mixed.shape[1]
     return pl.pallas_call(
         functools.partial(mix_kernel, heads, requests),
         out_shape=[
-            jax.ShapeDtypeStruct((requests, columns + 8 * count), jnp.bfloat16),
+            jax.ShapeDtypeStruct((requests, columns + lanes), jnp.bfloat16),
         ]
         * 2,
         compiler_params=params(),

time: 29.7 us -> 29.3 us (0.987)
  waiting for transfers between devices: 6.49 us -> 6.01 us
    ppermute x6, waiting for transfers between devices: 4.43 us -> 2.59 us  [from_partner(): return lax.ppermute(x, axis, [(i, i ^ distance) for i in range(count)])]
    ppermute x1, waiting for transfers between devices: 1.21 us -> 2.57 us  [on_device(): lax.ppermute(far, ('seq', 'tp'), far_pairs)]
    ppermute x1, starting transfers between devices: 2.72 us -> 2.12 us  [on_device(): lax.ppermute(far, ('seq', 'tp'), far_pairs)]
    ppermute x6, starting transfers between devices: 8.95 us -> 9.55 us  [from_partner(): return lax.ppermute(x, axis, [(i, i ^ distance) for i in range(count)])]
  transfers between devices with their start and end apart: 10 -> 10, of which waited for: 6 -> 6; matrix products, arithmetic and copies ran while one was open for 0% -> 0% of each run, Pallas kernels for 14% -> 15%
where the time goes in v24:
time: 29.3 us; the launch traced here: 29.1 us
  starting transfers between devices  16.2 us (55%)
  Pallas kernels  6.8 us (23%)
  waiting for transfers between devices  6.01 us (21%)
    ppermute x6, starting transfers between devices, from_partner(): return lax.ppermute(x, axis, [(i, i ^ distance) for i in range(count)])  9.55 us
    ppermute x3, starting transfers between devices, from_behind(): lax.ppermute(x, axis, [(i, (i + distance) % count) for i in range(count)])  4.52 us
    ppermute x6, waiting for transfers between devices, from_partner(): return lax.ppermute(x, axis, [(i, i ^ distance) for i in range(count)])  2.59 us
    ppermute x1, waiting for transfers between devices, on_device(): lax.ppermute(far, ('seq', 'tp'), far_pairs)  2.57 us
    pallas_call x1, Pallas kernels, project(): pl.pallas_call(project_kernel, in_specs=[vmem] * 2, out_specs=[vmem] * 2,...  2.32 us
    ppermute x1, starting transfers between devices, on_device(): lax.ppermute(far, ('seq', 'tp'), far_pairs)  2.12 us
    pallas_call x1, Pallas kernels, cache_part(): pl.pallas_call(cache_kernel, in_specs=[pl.BlockSpec(memory_space=pltpu.SM...  1.6 us
    pallas_call x1, Pallas kernels, finish(): pl.pallas_call(functools.partial(finish_kernel, count), out_shape=jax.Sha...  1.13 us
  transfers between devices with their start and end apart: 10, of which 6 were waited for; matrix products, arithmetic and copies ran while one was open for 0% of the time, Pallas kernels for 15%

profile of v24, /device:TPU:0, one launch (start us, length us, event | category | flops | bytes accessed | tf_op | source)
XLA Modules:
  0.0 29.1 jit_solution(2918476424498662348)
XLA Ops:
  0.0 1.0 %make_message.1.refs_0_ = bf16[8,4224]{1,0:T(8,128)(2,1)S(1)} custom-call(bf16[8,4096]{1,0:T(8,128)(2,1)} %bitcast.7, s32[1,64]{1,0:T(1,128)} %bitcast.9, s32[1,64]{1,0:T(1,128)} %requests_ref.1), custom_call_target="tpu_custom_call" | custom-call | flops 99999997952 | bytes 10000 | tf_op jit(solution)/shard_map/make_message/pallas_call | solution.py:100
  1.0 5.1 %collective-permute-start = (bf16[8,4224]{1,0:T(8,128)(2,1)S(1)}, bf16[8,4224]{1,0:T(8,128)(2,1)S(1)}, u32[]{:S(2)}, u32[]{:S(2)}) collective-permute-start(bf16[8,4224]{1,0:T(8,128)(2,1)S(1)} %make_message.1.refs_0_), channel_id=1, source_target_pairs={{0,12},{4,8},{8,4},{12,0},{1,13},{5,9},{9,5},{13,1},{2,14},{6,10},... | collective-permute-start | bytes 202760 | tf_op jit(solution)/shard_map/ppermute | solution.py:375
  6.2 0.6 %collective-permute-start.2 = (bf16[8,4224]{1,0:T(8,128)(2,1)S(1)}, bf16[8,4224]{1,0:T(8,128)(2,1)S(1)}, u32[]{:S(2)}, u32[]{:S(2)}) collective-permute-start(bf16[8,4224]{1,0:T(8,128)(2,1)S(1)} %make_message.1.refs_0_), channel_id=1, source_target_pairs={{0,4},{4,0},{8,12},{12,8},{1,5},{5,1},{9,13},{13,9},{2,6},{6,2},{1... | collective-permute-start | bytes 202760 | tf_op jit(solution)/shard_map/ppermute | solution.py:375
  6.8 2.3 %project.1 = (bf16[256,512]{1,0:T(8,128)(2,1)S(1)}, bf16[256,512]{1,0:T(8,128)(2,1)S(1)}) custom-call(bf16[256,4096]{1,0:T(8,128)(2,1)S(1)} %copy-done, bf16[4096,1024]{1,0:T(8,128)(2,1)S(1)} %bitcast.5), custom_call_target="tpu_custom_call" | custom-call | flops 2147483648 | bytes 10485760 | tf_op jit(solution)/shard_map/project/pallas_call | solution.py:63
  9.1 1.5 %collective-permute-start.3 = (bf16[256,512]{1,0:T(8,128)(2,1)S(1)}, bf16[256,512]{1,0:T(8,128)(2,1)S(1)}, u32[]{:S(2)}, u32[]{:S(2)}) collective-permute-start(bf16[256,512]{1,0:T(8,128)(2,1)S(1)} %get-tuple-element.15.values_ref), channel_id=1, source_target_pairs={{0,4},{4,0},{8,12},{12,8},{1,5},{5,1},{9,13},{13,9},{2,6},{6,2},{1... | collective-permute-start | bytes 786440 | tf_op jit(solution)/shard_map/ppermute | solution.py:375
  10.6 0.0 collective-permute-done.refs_1_
  10.6 1.4 %collective-permute-done.1.refs_2_ = bf16[8,4224]{1,0:T(8,128)(2,1)S(1)} collective-permute-done((bf16[8,4224]{1,0:T(8,128)(2,1)S(1)}, bf16[8,4224]{1,0:T(8,128)(2,1)S(1)}, u32[]{:S(2)}, u32[]{:S(2)}) %collective-permute-start.1) | collective-permute-done | bytes 67616 | tf_op jit(solution)/shard_map/ppermute | solution.py:375
  12.0 0.0 copy-start.4
  12.0 0.3 %partial_scores.1 = (bf16[32,256]{1,0:T(8,128)(2,1)S(1)}, s32[8,256]{1,0:T(8,128)S(1)}) custom-call(bf16[256,512]{1,0:T(8,128)(2,1)S(1)} %get-tuple-element.13.keys_ref, bf16[8,4224]{1,0:T(8,128)(2,1)S(1)} %make_message.1.refs_0_, bf16[8,4224]{1,0:T(8,128)(2,1)S(1)} %collective-permute-done.refs_1_, bf16[8,4224]{1,0:T(8,128)(2,1)S(1)} %collective-permute-done.1.refs_2_, ...), custom_call_target="tpu_custom_call" | custom-call | flops 99999997952 | bytes 10000 | tf_op jit(solution)/shard_map/partial_scores/pallas_call | solution.py:245
  12.3 1.5 %collective-permute-start.4 = (bf16[32,256]{1,0:T(8,128)(2,1)S(1)}, bf16[32,256]{1,0:T(8,128)(2,1)S(1)}, u32[]{:S(2)}, u32[]{:S(2)}) collective-permute-start(bf16[32,256]{1,0:T(8,128)(2,1)S(1)} %get-tuple-element.18.refs_0_), channel_id=1, source_target_pairs={{0,4},{4,8},{8,12},{12,0},{1,5},{5,9},{9,13},{13,1},{2,6},{6,10},{... | collective-permute-start | bytes 49160 | tf_op jit(solution)/shard_map/ppermute | solution.py:380
  13.8 1.8 %collective-permute-start.5 = (bf16[32,256]{1,0:T(8,128)(2,1)S(1)}, bf16[32,256]{1,0:T(8,128)(2,1)S(1)}, u32[]{:S(2)}, u32[]{:S(2)}) collective-permute-start(bf16[32,256]{1,0:T(8,128)(2,1)S(1)} %get-tuple-element.18.refs_0_), channel_id=1, source_target_pairs={{0,8},{4,12},{8,0},{12,4},{1,9},{5,13},{9,1},{13,5},{2,10},{6,14},... | collective-permute-start | bytes 49160 | tf_op jit(solution)/shard_map/ppermute | solution.py:380
  15.6 1.3 %collective-permute-start.6 = (bf16[32,256]{1,0:T(8,128)(2,1)S(1)}, bf16[32,256]{1,0:T(8,128)(2,1)S(1)}, u32[]{:S(2)}, u32[]{:S(2)}) collective-permute-start(bf16[32,256]{1,0:T(8,128)(2,1)S(1)} %get-tuple-element.18.refs_0_), channel_id=1, source_target_pairs={{0,12},{4,0},{8,4},{12,8},{1,13},{5,1},{9,5},{13,9},{2,14},{6,2},{... | collective-permute-start | bytes 49160 | tf_op jit(solution)/shard_map/ppermute | solution.py:380
  16.9 1.6 %cache_part.1 = (f32[8,4096]{1,0:T(8,128)S(1)}, f32[16,128]{1,0:T(8,128)S(1)}) custom-call(s32[1,1,8]{2,1,0:T(1,128)S(1)} %copy-done.4, bf16[8,4096]{1,0:T(8,128)(2,1)S(1)} %bitcast.8, bf16[8,128,1024]{2,1,0:T(8,128)(2,1)S(1)} %bitcast.6, s32[8,128]{1,0:T(8,128)S(1)} %copy-done.3), custom_call_target="tpu_custom_call" | custom-call | flops 16777216 | bytes 2097152 | tf_op jit(solution)/shard_map/cache_part/pallas_call | solution.py:189
  18.5 0.6 %collective-permute-done.4.refs_1_ = bf16[32,256]{1,0:T(8,128)(2,1)S(1)} collective-permute-done((bf16[32,256]{1,0:T(8,128)(2,1)S(1)}, bf16[32,256]{1,0:T(8,128)(2,1)S(1)}, u32[]{:S(2)}, u32[]{:S(2)}) %collective-permute-start.4) | collective-permute-done | bytes 16416 | tf_op jit(solution)/shard_map/ppermute | solution.py:380
  19.1 0.0 collective-permute-done.5.refs_2_
  19.1 0.2 collective-permute-done.6.refs_3_
  19.3 0.4 %mix.1 = (bf16[8,4224]{1,0:T(8,128)(2,1)S(1)}, bf16[8,4224]{1,0:T(8,128)(2,1)S(1)}) custom-call(s32[8,256]{1,0:T(8,128)S(1)} %get-tuple-element.14.code_ref, bf16[256,512]{1,0:T(8,128)(2,1)S(1)} %get-tuple-element.15.values_ref, bf16[256,512]{1,0:T(8,128)(2,1)S(1)} %collective-permute-done.3.near_ref, f32[8,4096]{1,0:T(8,128)S(1)} %get-tuple-element.16.cache_ref, ...), custom_call_target="tpu_custom_call" | custom-call | tf_op jit(solution)/shard_map/mix/pallas_call | solution.py:322
  19.8 2.1 %collective-permute-start.7 = (bf16[8,4224]{1,0:T(8,128)(2,1)S(1)}, bf16[8,4224]{1,0:T(8,128)(2,1)S(1)}, u32[]{:S(2)}, u32[]{:S(2)}) collective-permute-start(bf16[8,4224]{1,0:T(8,128)(2,1)S(1)} %get-tuple-element.20), channel_id=1, source_target_pairs={{0,10},{2,8},{4,14},{6,12},{8,2},{10,0},{12,6},{14,4},{1,11},{3,9}... | collective-permute-start | bytes 202760 | tf_op jit(solution)/shard_map/ppermute | solution.py:403
  21.9 1.8 %collective-permute-start.8 = (bf16[8,4224]{1,0:T(8,128)(2,1)S(1)}, bf16[8,4224]{1,0:T(8,128)(2,1)S(1)}, u32[]{:S(2)}, u32[]{:S(2)}) collective-permute-start(bf16[8,4224]{1,0:T(8,128)(2,1)S(1)} %get-tuple-element.20), channel_id=1, source_target_pairs={{0,8},{4,12},{8,0},{12,4},{1,9},{5,13},{9,1},{13,5},{2,10},{6,14},... | collective-permute-start | bytes 202760 | tf_op jit(solution)/shard_map/ppermute | solution.py:375
  23.7 0.5 %collective-permute-start.9 = (bf16[8,4224]{1,0:T(8,128)(2,1)S(1)}, bf16[8,4224]{1,0:T(8,128)(2,1)S(1)}, u32[]{:S(2)}, u32[]{:S(2)}) collective-permute-start(bf16[8,4224]{1,0:T(8,128)(2,1)S(1)} %get-tuple-element.19.own_ref), channel_id=1, source_target_pairs={{0,2},{2,0},{1,3},{3,1},{4,6},{6,4},{5,7},{7,5},{8,10},{10,8},{9,1... | collective-permute-start | bytes 202760 | tf_op jit(solution)/shard_map/ppermute | solution.py:375
  24.2 2.6 %collective-permute-done.7.refs_0_ = bf16[8,4224]{1,0:T(8,128)(2,1)S(1)} collective-permute-done((bf16[8,4224]{1,0:T(8,128)(2,1)S(1)}, bf16[8,4224]{1,0:T(8,128)(2,1)S(1)}, u32[]{:S(2)}, u32[]{:S(2)}) %collective-permute-start.7) | collective-permute-done | bytes 67616 | tf_op jit(solution)/shard_map/ppermute | solution.py:403
  26.8 1.1 %collective-permute-done.8.refs_1_ = bf16[8,4224]{1,0:T(8,128)(2,1)S(1)} collective-permute-done((bf16[8,4224]{1,0:T(8,128)(2,1)S(1)}, bf16[8,4224]{1,0:T(8,128)(2,1)S(1)}, u32[]{:S(2)}, u32[]{:S(2)}) %collective-permute-start.8) | collective-permute-done | bytes 67616 | tf_op jit(solution)/shard_map/ppermute | solution.py:375
  27.9 0.1 collective-permute-done.9.refs_2_
  28.0 1.1 %finish.1 = bf16[8,4096]{1,0:T(8,128)(2,1)} custom-call(bf16[8,4224]{1,0:T(8,128)(2,1)S(1)} %get-tuple-element.19.own_ref, bf16[8,4224]{1,0:T(8,128)(2,1)S(1)} %collective-permute-done.7.refs_0_, bf16[8,4224]{1,0:T(8,128)(2,1)S(1)} %collective-permute-done.8.refs_1_, bf16[8,4224]{1,0:T(8,128)(2,1)S(1)} %collective-permute-done.9.refs_2_), custom_call_target="tpu_custom_call" | custom-call | tf_op jit(solution)/shard_map/finish/pallas_call | solution.py:365
  (17 shorter events, 0.0 us)
Async XLA Ops:
  0.0 6.8 %slice-start = ((s8[8388608]{0:T(1024)(128)(4,1)}), s8[4194304]{0:T(1024)(128)(4,1)S(1)}, s32[]{:S(2)}) async-start(s8[8388608]{0:T(1024)(128)(4,1)} %bitcast.4), calls=%async_computation | async-start | bytes 8388608
  0.0 6.8 %slice-start.1 = ((s8[8388608]{0:T(1024)(128)(4,1)}), s8[4194304]{0:T(1024)(128)(4,1)S(1)}, s32[]{:S(2)}) async-start(s8[8388608]{0:T(1024)(128)(4,1)} %bitcast.4), calls=%async_computation.1 | async-start | bytes 8388608
  0.0 6.8 %copy-start = (bf16[256,4096]{1,0:T(8,128)(2,1)S(1)}, bf16[256,4096]{1,0:T(8,128)(2,1)}, u32[]{:S(2)}) copy-start(bf16[256,4096]{1,0:T(8,128)(2,1)} %tokens_ref.1) | copy-start | bytes 6291460
  1.0 9.6 %collective-permute-start = (bf16[8,4224]{1,0:T(8,128)(2,1)S(1)}, bf16[8,4224]{1,0:T(8,128)(2,1)S(1)}, u32[]{:S(2)}, u32[]{:S(2)}) collective-permute-start(bf16[8,4224]{1,0:T(8,128)(2,1)S(1)} %make_message.1.refs_0_), channel_id=1, source_target_pairs={{0,12},{4,8},{8,4},{12,0},{1,13},{5,9},{9,5},{13,1},{2,14},{6,10},... | collective-permute-start | bytes 202760 | tf_op jit(solution)/shard_map/ppermute | solution.py:375
  6.2 5.8 %collective-permute-start.1 = (bf16[8,4224]{1,0:T(8,128)(2,1)S(1)}, bf16[8,4224]{1,0:T(8,128)(2,1)S(1)}, u32[]{:S(2)}, u32[]{:S(2)}) collective-permute-start(bf16[8,4224]{1,0:T(8,128)(2,1)S(1)} %make_message.1.refs_0_), channel_id=1, source_target_pairs={{0,8},{4,12},{8,0},{12,4},{1,9},{5,13},{9,1},{13,5},{2,10},{6,14},... | collective-permute-start | bytes 202760 | tf_op jit(solution)/shard_map/ppermute | solution.py:375
  6.2 5.8 %collective-permute-start.2 = (bf16[8,4224]{1,0:T(8,128)(2,1)S(1)}, bf16[8,4224]{1,0:T(8,128)(2,1)S(1)}, u32[]{:S(2)}, u32[]{:S(2)}) collective-permute-start(bf16[8,4224]{1,0:T(8,128)(2,1)S(1)} %make_message.1.refs_0_), channel_id=1, source_target_pairs={{0,4},{4,0},{8,12},{12,8},{1,5},{5,1},{9,13},{13,9},{2,6},{6,2},{1... | collective-permute-start | bytes 202760 | tf_op jit(solution)/shard_map/ppermute | solution.py:375
  9.1 10.2 %collective-permute-start.3 = (bf16[256,512]{1,0:T(8,128)(2,1)S(1)}, bf16[256,512]{1,0:T(8,128)(2,1)S(1)}, u32[]{:S(2)}, u32[]{:S(2)}) collective-permute-start(bf16[256,512]{1,0:T(8,128)(2,1)S(1)} %get-tuple-element.15.values_ref), channel_id=1, source_target_pairs={{0,4},{4,0},{8,12},{12,8},{1,5},{5,1},{9,13},{13,9},{2,6},{6,2},{1... | collective-permute-start | bytes 786440 | tf_op jit(solution)/shard_map/ppermute | solution.py:375
  12.0 4.9 %copy-start.1 = (bf16[1,1,8,128,1024]{4,3,2,1,0:T(8,128)(2,1)S(1)}, bf16[1,1,8,128,1024]{4,3,2,1,0:T(8,128)(2,1)}, u32[]{:S(2)}) copy-start(bf16[1,1,8,128,1024]{4,3,2,1,0:T(8,128)(2,1)} %param.14) | copy-start | bytes 6291460
  12.0 4.9 %copy-start.2 = (bf16[1,1,8,4096]{3,2,1,0:T(8,128)(2,1)S(1)}, bf16[1,1,8,4096]{3,2,1,0:T(8,128)(2,1)}, u32[]{:S(2)}) copy-start(bf16[1,1,8,4096]{3,2,1,0:T(8,128)(2,1)} %param.13) | copy-start | bytes 196612
  12.0 4.9 %copy-start.3 = (s32[8,128]{1,0:T(8,128)S(1)}, s32[8,128]{1,0:T(8,128)}, u32[]{:S(2)}) copy-start(s32[8,128]{1,0:T(8,128)} %signs_ref.1) | copy-start | bytes 12292
  12.0 4.9 %copy-start.4 = (s32[1,1,8]{2,1,0:T(1,128)S(1)}, s32[1,1,8]{2,1,0:T(1,128)}, u32[]{:S(2)}) copy-start(s32[1,1,8]{2,1,0:T(1,128)} %lengths_ref.1) | copy-start | bytes 100
  12.3 6.8 %collective-permute-start.4 = (bf16[32,256]{1,0:T(8,128)(2,1)S(1)}, bf16[32,256]{1,0:T(8,128)(2,1)S(1)}, u32[]{:S(2)}, u32[]{:S(2)}) collective-permute-start(bf16[32,256]{1,0:T(8,128)(2,1)S(1)} %get-tuple-element.18.refs_0_), channel_id=1, source_target_pairs={{0,4},{4,8},{8,12},{12,0},{1,5},{5,9},{9,13},{13,1},{2,6},{6,10},{... | collective-permute-start | bytes 49160 | tf_op jit(solution)/shard_map/ppermute | solution.py:380
  13.8 5.3 %collective-permute-start.5 = (bf16[32,256]{1,0:T(8,128)(2,1)S(1)}, bf16[32,256]{1,0:T(8,128)(2,1)S(1)}, u32[]{:S(2)}, u32[]{:S(2)}) collective-permute-start(bf16[32,256]{1,0:T(8,128)(2,1)S(1)} %get-tuple-element.18.refs_0_), channel_id=1, source_target_pairs={{0,8},{4,12},{8,0},{12,4},{1,9},{5,13},{9,1},{13,5},{2,10},{6,14},... | collective-permute-start | bytes 49160 | tf_op jit(solution)/shard_map/ppermute | solution.py:380
  15.6 3.7 %collective-permute-start.6 = (bf16[32,256]{1,0:T(8,128)(2,1)S(1)}, bf16[32,256]{1,0:T(8,128)(2,1)S(1)}, u32[]{:S(2)}, u32[]{:S(2)}) collective-permute-start(bf16[32,256]{1,0:T(8,128)(2,1)S(1)} %get-tuple-element.18.refs_0_), channel_id=1, source_target_pairs={{0,12},{4,0},{8,4},{12,8},{1,13},{5,1},{9,5},{13,9},{2,14},{6,2},{... | collective-permute-start | bytes 49160 | tf_op jit(solution)/shard_map/ppermute | solution.py:380
  19.8 7.0 %collective-permute-start.7 = (bf16[8,4224]{1,0:T(8,128)(2,1)S(1)}, bf16[8,4224]{1,0:T(8,128)(2,1)S(1)}, u32[]{:S(2)}, u32[]{:S(2)}) collective-permute-start(bf16[8,4224]{1,0:T(8,128)(2,1)S(1)} %get-tuple-element.20), channel_id=1, source_target_pairs={{0,10},{2,8},{4,14},{6,12},{8,2},{10,0},{12,6},{14,4},{1,11},{3,9}... | collective-permute-start | bytes 202760 | tf_op jit(solution)/shard_map/ppermute | solution.py:403
  21.9 6.0 %collective-permute-start.8 = (bf16[8,4224]{1,0:T(8,128)(2,1)S(1)}, bf16[8,4224]{1,0:T(8,128)(2,1)S(1)}, u32[]{:S(2)}, u32[]{:S(2)}) collective-permute-start(bf16[8,4224]{1,0:T(8,128)(2,1)S(1)} %get-tuple-element.20), channel_id=1, source_target_pairs={{0,8},{4,12},{8,0},{12,4},{1,9},{5,13},{9,1},{13,5},{2,10},{6,14},... | collective-permute-start | bytes 202760 | tf_op jit(solution)/shard_map/ppermute | solution.py:375
  23.7 4.3 %collective-permute-start.9 = (bf16[8,4224]{1,0:T(8,128)(2,1)S(1)}, bf16[8,4224]{1,0:T(8,128)(2,1)S(1)}, u32[]{:S(2)}, u32[]{:S(2)}) collective-permute-start(bf16[8,4224]{1,0:T(8,128)(2,1)S(1)} %get-tuple-element.19.own_ref), channel_id=1, source_target_pairs={{0,2},{2,0},{1,3},{3,1},{4,6},{6,4},{5,7},{7,5},{8,10},{10,8},{9,1... | collective-permute-start | bytes 202760 | tf_op jit(solution)/shard_map/ppermute | solution.py:375

commit v25 on v19

--- a/solution.py
+++ b/solution.py
@@ -37,7 +37,7 @@
 
 QUERY_ORDER = (3, 2, 1)
 SCORE_ORDER = (1, 2, 3)
-FINISH_PLACES = (2, 1, 0)
+FINISH_PLACES = (1, 0)
 
 
 def arranged(blocks, order):
@@ -312,7 +312,6 @@
         share = cache_ref[:, at] * cache_factor[:, h : h + 1] + part * new_factor[:, h : h + 1]
         share_ref[:, at] = share.astype(share_ref.dtype)
     lanes = cache_stats_ref.shape[1]
-    far_ref[:, columns:] = jnp.zeros((requests, 3 * lanes), far_ref.dtype)
     for i, value in enumerate((both, total, new_factor)):
         share_ref[:, columns + i * lanes : columns + (i + 1) * lanes] = packed(value, count).astype(share_ref.dtype)
 
@@ -324,17 +323,15 @@
         functools.partial(mix_kernel, heads, requests),
         out_shape=[
             jax.ShapeDtypeStruct((requests, columns + 3 * lanes), jnp.bfloat16),
-        ]
-        * 2,
+            jax.ShapeDtypeStruct((requests, columns), jnp.bfloat16),
+        ],
         compiler_params=params(),
         name="mix",
     )(code, values, near_values, cache_mixed, cache_stats, *arranged(scores, SCORE_ORDER))
 
 
-def finish_kernel(count, own_ref, *refs):
-    out_ref = refs[-1]
-    other_ref, own_far_ref, other_far_ref = [refs[i] for i in FINISH_PLACES]
-    columns = out_ref.shape[1]
+def weigh_kernel(count, own_ref, other_ref, *out_refs):
+    columns = out_refs[0].shape[1]
     size = columns // count
     lanes = (own_ref.shape[1] - columns) // 3
     first = lax.axis_index("tp") == 0
@@ -350,31 +347,44 @@
     own_total, other_total = own_total * own_factor, other_total * other_factor
     total = jnp.where(first, own_total, other_total) + jnp.where(first, other_total, own_total)
     inverse = 1.0 / total
-    sides = []
-    for ref, far_ref, factor, new in (
-        (own_ref, own_far_ref, own_factor, own_new),
-        (other_ref, other_far_ref, other_factor, other_new),
-    ):
+    for i, (ref, factor, new) in enumerate(((own_ref, own_factor, own_new), (other_ref, other_factor, other_new))):
         factor = factor * inverse
-        sides.append((ref, far_ref, factor, factor * new))
-    for h in range(count):
-        at = slice(h * size, (h + 1) * size)
-        terms = [
-            ref[:, at].astype(jnp.float32) * factor[:, h : h + 1]
-            + far_ref[:, at].astype(jnp.float32) * far_factor[:, h : h + 1]
-            for ref, far_ref, factor, far_factor in sides
-        ]
-        out_ref[:, at] = (terms[0] + terms[1]).astype(out_ref.dtype)
-
-
-def finish(count, columns, own, other, own_far, other_far):
-    arrived = (other, own_far, other_far)
-    return pl.pallas_call(
-        functools.partial(finish_kernel, count),
-        out_shape=jax.ShapeDtypeStruct((own.shape[0], columns), jnp.bfloat16),
+        far_factor = factor * new
+        base_ref, weight_ref = out_refs[2 * i], out_refs[2 * i + 1]
+        for h in range(count):
+            at = slice(h * size, (h + 1) * size)
+            base_ref[:, at] = ref[:, at].astype(jnp.float32) * factor[:, h : h + 1]
+            weight_ref[:, at] = jnp.broadcast_to(far_factor[:, h : h + 1], (ref.shape[0], size))
+
+
+def weigh(count, columns, own, other):
+    return pl.pallas_call(
+        functools.partial(weigh_kernel, count),
+        out_shape=[jax.ShapeDtypeStruct((own.shape[0], columns), jnp.float32)] * 4,
+        compiler_params=params(),
+        name="weigh",
+    )(own, other)
+
+
+def finish_kernel(own_base, own_weight, other_base, other_weight, *refs):
+    out_ref = refs[-1]
+    own_far, other_far = [refs[i] for i in FINISH_PLACES]
+    columns = out_ref.shape[1]
+    terms = [
+        base[...] + far[:, :columns].astype(jnp.float32) * weight[...]
+        for base, far, weight in ((own_base, own_far, own_weight), (other_base, other_far, other_weight))
+    ]
+    out_ref[...] = (terms[0] + terms[1]).astype(out_ref.dtype)
+
+
+def finish(weighed, own_far, other_far):
+    arrived = (own_far, other_far)
+    return pl.pallas_call(
+        finish_kernel,
+        out_shape=jax.ShapeDtypeStruct(weighed[0].shape, own_far.dtype),
         compiler_params=params(),
         name="finish",
-    )(own, *[arrived[FINISH_PLACES.index(i)] for i in range(3)])
+    )(*weighed, *[arrived[FINISH_PLACES.index(i)] for i in range(2)])
 
 
 def from_partner(x, axis, distance):
@@ -401,14 +411,9 @@
     cache_mixed, cache_stats = cache_part(lengths, query, kv_cache[0, 0], signs)
     share, far = mix(heads, code, values, near_values, cache_mixed, cache_stats, scores)
     far_pairs = [(i, i ^ 5) for i in range(2 * seq_count)]
-    output = finish(
-        columns // signs.shape[1],
-        columns,
-        share,
-        from_partner(share, "tp", 1),
-        from_partner(far, "seq", 2),
-        lax.ppermute(far, ("seq", "tp"), far_pairs),
-    )
+    weighed = weigh(columns // signs.shape[1], columns, share, from_partner(share, "tp", 1))
+    diagonal = lax.ppermute(far, ("seq", "tp"), far_pairs)
+    output = finish(weighed, from_partner(far, "seq", 2), diagonal)
     return output.reshape(1, 1, request_count, columns)
 
 

time: 29.2 us -> 29.1 us (level)
    ppermute x1, starting transfers between devices: 2.12 us -> 1.1 us  [on_device(): diagonal = lax.ppermute(far, ('seq', 'tp'), far_pairs)]
    ppermute x6, starting transfers between devices: 9.55 us -> 10.6 us  [from_partner(): return lax.ppermute(x, axis, [(i, i ^ distance) for i in range(count)])]
    ppermute x6, waiting for transfers between devices: 2.53 us -> 2.06 us  [from_partner(): return lax.ppermute(x, axis, [(i, i ^ distance) for i in range(count)])]
    ppermute x1, waiting for transfers between devices: 2.7 us -> 3.02 us  [on_device(): diagonal = lax.ppermute(far, ('seq', 'tp'), far_pairs)]
    pallas_call x1 -> x2, Pallas kernels: 0.99 us -> 1.05 us  [the longest x1 0.68 us: finish(): pl.pallas_call(finish_kernel, out_shape=jax.ShapeDtypeStruct(weighed[0].s...]
  transfers between devices with their start and end apart: 10 -> 10, of which waited for: 5 -> 5; matrix products, arithmetic and copies ran while one was open for 0% -> 0% of each run, Pallas kernels for 15% -> 16%
where the time goes in v25:
time: 29.1 us; the launch traced here: 28.9 us
  starting transfers between devices  16.2 us (56%)
  Pallas kernels  6.72 us (23%)
  waiting for transfers between devices  5.93 us (20%)
    ppermute x6, starting transfers between devices, from_partner(): return lax.ppermute(x, axis, [(i, i ^ distance) for i in range(count)])  10.6 us
    ppermute x3, starting transfers between devices, from_behind(): lax.ppermute(x, axis, [(i, (i + distance) % count) for i in range(count)])  4.52 us
    ppermute x1, waiting for transfers between devices, on_device(): diagonal = lax.ppermute(far, ('seq', 'tp'), far_pairs)  3.02 us
    pallas_call x1, Pallas kernels, project(): pl.pallas_call(project_kernel, in_specs=[vmem] * 2, out_specs=[vmem] * 2,...  2.32 us
    ppermute x6, waiting for transfers between devices, from_partner(): return lax.ppermute(x, axis, [(i, i ^ distance) for i in range(count)])  2.06 us
    pallas_call x1, Pallas kernels, cache_part(): pl.pallas_call(cache_kernel, in_specs=[pl.BlockSpec(memory_space=pltpu.SM...  1.6 us
    ppermute x1, starting transfers between devices, on_device(): diagonal = lax.ppermute(far, ('seq', 'tp'), far_pairs)  1.1 us
    pallas_call x1, Pallas kernels, make_message(): pl.pallas_call(message_kernel, in_specs=[pl.BlockSpec(memory_space=pl.ANY...  1.01 us
  transfers between devices with their start and end apart: 10, of which 5 were waited for; matrix products, arithmetic and copies ran while one was open for 0% of the time, Pallas kernels for 16%

profile of v25, /device:TPU:0, one launch (start us, length us, event | category | flops | bytes accessed | tf_op | source)
XLA Modules:
  0.0 28.9 jit_solution(1524087850815982629)
XLA Ops:
  0.0 1.0 %make_message.1.refs_0_ = bf16[8,4224]{1,0:T(8,128)(2,1)S(1)} custom-call(bf16[8,4096]{1,0:T(8,128)(2,1)} %bitcast.7, s32[1,64]{1,0:T(1,128)} %bitcast.9, s32[1,64]{1,0:T(1,128)} %requests_ref.1), custom_call_target="tpu_custom_call" | custom-call | flops 99999997952 | bytes 10000 | tf_op jit(solution)/shard_map/make_message/pallas_call | solution.py:100
  1.0 5.1 %collective-permute-start = (bf16[8,4224]{1,0:T(8,128)(2,1)S(1)}, bf16[8,4224]{1,0:T(8,128)(2,1)S(1)}, u32[]{:S(2)}, u32[]{:S(2)}) collective-permute-start(bf16[8,4224]{1,0:T(8,128)(2,1)S(1)} %make_message.1.refs_0_), channel_id=1, source_target_pairs={{0,12},{4,8},{8,4},{12,0},{1,13},{5,9},{9,5},{13,1},{2,14},{6,10},... | collective-permute-start | bytes 202760 | tf_op jit(solution)/shard_map/ppermute | solution.py:392
  6.2 0.0 collective-permute-start.1
  6.2 0.6 %collective-permute-start.2 = (bf16[8,4224]{1,0:T(8,128)(2,1)S(1)}, bf16[8,4224]{1,0:T(8,128)(2,1)S(1)}, u32[]{:S(2)}, u32[]{:S(2)}) collective-permute-start(bf16[8,4224]{1,0:T(8,128)(2,1)S(1)} %make_message.1.refs_0_), channel_id=1, source_target_pairs={{0,4},{4,0},{8,12},{12,8},{1,5},{5,1},{9,13},{13,9},{2,6},{6,2},{1... | collective-permute-start | bytes 202760 | tf_op jit(solution)/shard_map/ppermute | solution.py:392
  6.8 2.3 %project.1 = (bf16[256,512]{1,0:T(8,128)(2,1)S(1)}, bf16[256,512]{1,0:T(8,128)(2,1)S(1)}) custom-call(bf16[256,4096]{1,0:T(8,128)(2,1)S(1)} %copy-done, bf16[4096,1024]{1,0:T(8,128)(2,1)S(1)} %bitcast.5), custom_call_target="tpu_custom_call" | custom-call | flops 2147483648 | bytes 10485760 | tf_op jit(solution)/shard_map/project/pallas_call | solution.py:63
  9.1 1.5 %collective-permute-start.3 = (bf16[256,512]{1,0:T(8,128)(2,1)S(1)}, bf16[256,512]{1,0:T(8,128)(2,1)S(1)}, u32[]{:S(2)}, u32[]{:S(2)}) collective-permute-start(bf16[256,512]{1,0:T(8,128)(2,1)S(1)} %get-tuple-element.19.values_ref), channel_id=1, source_target_pairs={{0,4},{4,0},{8,12},{12,8},{1,5},{5,1},{9,13},{13,9},{2,6},{6,2},{1... | collective-permute-start | bytes 786440 | tf_op jit(solution)/shard_map/ppermute | solution.py:392
  10.6 1.4 %collective-permute-done.1.refs_2_ = bf16[8,4224]{1,0:T(8,128)(2,1)S(1)} collective-permute-done((bf16[8,4224]{1,0:T(8,128)(2,1)S(1)}, bf16[8,4224]{1,0:T(8,128)(2,1)S(1)}, u32[]{:S(2)}, u32[]{:S(2)}) %collective-permute-start.1) | collective-permute-done | bytes 67616 | tf_op jit(solution)/shard_map/ppermute | solution.py:392
  12.0 0.0 collective-permute-done.2.refs_3_
  12.0 0.0 copy-start.4
  12.0 0.3 %partial_scores.1 = (bf16[32,256]{1,0:T(8,128)(2,1)S(1)}, s32[8,256]{1,0:T(8,128)S(1)}) custom-call(bf16[256,512]{1,0:T(8,128)(2,1)S(1)} %get-tuple-element.17.keys_ref, bf16[8,4224]{1,0:T(8,128)(2,1)S(1)} %make_message.1.refs_0_, bf16[8,4224]{1,0:T(8,128)(2,1)S(1)} %collective-permute-done.refs_1_, bf16[8,4224]{1,0:T(8,128)(2,1)S(1)} %collective-permute-done.1.refs_2_, ...), custom_call_target="tpu_custom_call" | custom-call | flops 99999997952 | bytes 10000 | tf_op jit(solution)/shard_map/partial_scores/pallas_call | solution.py:245
  12.3 1.5 %collective-permute-start.4 = (bf16[32,256]{1,0:T(8,128)(2,1)S(1)}, bf16[32,256]{1,0:T(8,128)(2,1)S(1)}, u32[]{:S(2)}, u32[]{:S(2)}) collective-permute-start(bf16[32,256]{1,0:T(8,128)(2,1)S(1)} %get-tuple-element.22.refs_0_), channel_id=1, source_target_pairs={{0,4},{4,8},{8,12},{12,0},{1,5},{5,9},{9,13},{13,1},{2,6},{6,10},{... | collective-permute-start | bytes 49160 | tf_op jit(solution)/shard_map/ppermute | solution.py:397
  13.8 1.8 %collective-permute-start.5 = (bf16[32,256]{1,0:T(8,128)(2,1)S(1)}, bf16[32,256]{1,0:T(8,128)(2,1)S(1)}, u32[]{:S(2)}, u32[]{:S(2)}) collective-permute-start(bf16[32,256]{1,0:T(8,128)(2,1)S(1)} %get-tuple-element.22.refs_0_), channel_id=1, source_target_pairs={{0,8},{4,12},{8,0},{12,4},{1,9},{5,13},{9,1},{13,5},{2,10},{6,14},... | collective-permute-start | bytes 49160 | tf_op jit(solution)/shard_map/ppermute | solution.py:397
  15.6 1.3 %collective-permute-start.6 = (bf16[32,256]{1,0:T(8,128)(2,1)S(1)}, bf16[32,256]{1,0:T(8,128)(2,1)S(1)}, u32[]{:S(2)}, u32[]{:S(2)}) collective-permute-start(bf16[32,256]{1,0:T(8,128)(2,1)S(1)} %get-tuple-element.22.refs_0_), channel_id=1, source_target_pairs={{0,12},{4,0},{8,4},{12,8},{1,13},{5,1},{9,5},{13,9},{2,14},{6,2},{... | collective-permute-start | bytes 49160 | tf_op jit(solution)/shard_map/ppermute | solution.py:397
  16.9 1.6 %cache_part.1 = (f32[8,4096]{1,0:T(8,128)S(1)}, f32[16,128]{1,0:T(8,128)S(1)}) custom-call(s32[1,1,8]{2,1,0:T(1,128)S(1)} %copy-done.4, bf16[8,4096]{1,0:T(8,128)(2,1)S(1)} %bitcast.8, bf16[8,128,1024]{2,1,0:T(8,128)(2,1)S(1)} %bitcast.6, s32[8,128]{1,0:T(8,128)S(1)} %copy-done.3), custom_call_target="tpu_custom_call" | custom-call | flops 16777216 | bytes 2097152 | tf_op jit(solution)/shard_map/cache_part/pallas_call | solution.py:189
  18.5 0.6 %collective-permute-done.4.refs_1_ = bf16[32,256]{1,0:T(8,128)(2,1)S(1)} collective-permute-done((bf16[32,256]{1,0:T(8,128)(2,1)S(1)}, bf16[32,256]{1,0:T(8,128)(2,1)S(1)}, u32[]{:S(2)}, u32[]{:S(2)}) %collective-permute-start.4) | collective-permute-done | bytes 16416 | tf_op jit(solution)/shard_map/ppermute | solution.py:397
  19.1 0.2 collective-permute-done.6.refs_3_
  19.3 0.4 %mix.1 = (bf16[8,4480]{1,0:T(8,128)(2,1)S(1)}, bf16[8,4096]{1,0:T(8,128)(2,1)S(1)}) custom-call(s32[8,256]{1,0:T(8,128)S(1)} %get-tuple-element.18.code_ref, bf16[256,512]{1,0:T(8,128)(2,1)S(1)} %get-tuple-element.19.values_ref, bf16[256,512]{1,0:T(8,128)(2,1)S(1)} %collective-permute-done.3.near_ref, f32[8,4096]{1,0:T(8,128)S(1)} %get-tuple-element.20.cache_ref, ...), custom_call_target="tpu_custom_call" | custom-call | tf_op jit(solution)/shard_map/mix/pallas_call | solution.py:322
  19.8 1.6 %collective-permute-start.7 = (bf16[8,4480]{1,0:T(8,128)(2,1)S(1)}, bf16[8,4480]{1,0:T(8,128)(2,1)S(1)}, u32[]{:S(2)}, u32[]{:S(2)}) collective-permute-start(bf16[8,4480]{1,0:T(8,128)(2,1)S(1)} %get-tuple-element.23.own_ref), channel_id=1, source_target_pairs={{0,2},{2,0},{1,3},{3,1},{4,6},{6,4},{5,7},{7,5},{8,10},{10,8},{9,1... | collective-permute-start | bytes 215048 | tf_op jit(solution)/shard_map/ppermute | solution.py:392
  21.3 1.1 %collective-permute-start.8 = (bf16[8,4096]{1,0:T(8,128)(2,1)S(1)}, bf16[8,4096]{1,0:T(8,128)(2,1)S(1)}, u32[]{:S(2)}, u32[]{:S(2)}) collective-permute-start(bf16[8,4096]{1,0:T(8,128)(2,1)S(1)} %get-tuple-element.28), channel_id=1, source_target_pairs={{0,10},{2,8},{4,14},{6,12},{8,2},{10,0},{12,6},{14,4},{1,11},{3,9}... | collective-permute-start | bytes 196616 | tf_op jit(solution)/shard_map/ppermute | solution.py:415
  22.4 1.8 %collective-permute-start.9 = (bf16[8,4096]{1,0:T(8,128)(2,1)S(1)}, bf16[8,4096]{1,0:T(8,128)(2,1)S(1)}, u32[]{:S(2)}, u32[]{:S(2)}) collective-permute-start(bf16[8,4096]{1,0:T(8,128)(2,1)S(1)} %get-tuple-element.28), channel_id=1, source_target_pairs={{0,8},{4,12},{8,0},{12,4},{1,9},{5,13},{9,1},{13,5},{2,10},{6,14},... | collective-permute-start | bytes 196616 | tf_op jit(solution)/shard_map/ppermute | solution.py:392
  24.2 0.6 %collective-permute-done.7.other_ref = bf16[8,4480]{1,0:T(8,128)(2,1)S(1)} collective-permute-done((bf16[8,4480]{1,0:T(8,128)(2,1)S(1)}, bf16[8,4480]{1,0:T(8,128)(2,1)S(1)}, u32[]{:S(2)}, u32[]{:S(2)}) %collective-permute-start.7) | collective-permute-done | bytes 71712 | tf_op jit(solution)/shard_map/ppermute | solution.py:392
  24.9 0.4 %weigh.1 = (f32[8,4096]{1,0:T(8,128)S(1)}, f32[8,4096]{1,0:T(8,128)S(1)}, f32[8,4096]{1,0:T(8,128)S(1)}, f32[8,4096]{1,0:T(8,128)S(1)}) custom-call(bf16[8,4480]{1,0:T(8,128)(2,1)S(1)} %get-tuple-element.23.own_ref, bf16[8,4480]{1,0:T(8,128)(2,1)S(1)} %collective-permute-done.7.other_ref), custom_call_target="tpu_custom_call" | custom-call | tf_op jit(solution)/shard_map/weigh/pallas_call | solution.py:361
  25.2 3.0 %collective-permute-done.8.refs_0_ = bf16[8,4096]{1,0:T(8,128)(2,1)S(1)} collective-permute-done((bf16[8,4096]{1,0:T(8,128)(2,1)S(1)}, bf16[8,4096]{1,0:T(8,128)(2,1)S(1)}, u32[]{:S(2)}, u32[]{:S(2)}) %collective-permute-start.8) | collective-permute-done | bytes 65568 | tf_op jit(solution)/shard_map/ppermute | solution.py:415
  28.3 0.7 %finish.1 = bf16[8,4096]{1,0:T(8,128)(2,1)} custom-call(f32[8,4096]{1,0:T(8,128)S(1)} %get-tuple-element.24.own_base, f32[8,4096]{1,0:T(8,128)S(1)} %get-tuple-element.25.own_weight, f32[8,4096]{1,0:T(8,128)S(1)} %get-tuple-element.26.other_base, f32[8,4096]{1,0:T(8,128)S(1)} %get-tuple-element.27.other_weight, ...), custom_call_target="tpu_custom_call" | custom-call | tf_op jit(solution)/shard_map/finish/pallas_call | solution.py:382
  (18 shorter events, 0.0 us)
Async XLA Ops:
  0.0 6.8 %slice-start = ((s8[8388608]{0:T(1024)(128)(4,1)}), s8[4194304]{0:T(1024)(128)(4,1)S(1)}, s32[]{:S(2)}) async-start(s8[8388608]{0:T(1024)(128)(4,1)} %bitcast.4), calls=%async_computation | async-start | bytes 8388608
  0.0 6.8 %slice-start.1 = ((s8[8388608]{0:T(1024)(128)(4,1)}), s8[4194304]{0:T(1024)(128)(4,1)S(1)}, s32[]{:S(2)}) async-start(s8[8388608]{0:T(1024)(128)(4,1)} %bitcast.4), calls=%async_computation.1 | async-start | bytes 8388608
  0.0 6.8 %copy-start = (bf16[256,4096]{1,0:T(8,128)(2,1)S(1)}, bf16[256,4096]{1,0:T(8,128)(2,1)}, u32[]{:S(2)}) copy-start(bf16[256,4096]{1,0:T(8,128)(2,1)} %tokens_ref.1) | copy-start | bytes 6291460
  1.0 9.6 %collective-permute-start = (bf16[8,4224]{1,0:T(8,128)(2,1)S(1)}, bf16[8,4224]{1,0:T(8,128)(2,1)S(1)}, u32[]{:S(2)}, u32[]{:S(2)}) collective-permute-start(bf16[8,4224]{1,0:T(8,128)(2,1)S(1)} %make_message.1.refs_0_), channel_id=1, source_target_pairs={{0,12},{4,8},{8,4},{12,0},{1,13},{5,9},{9,5},{13,1},{2,14},{6,10},... | collective-permute-start | bytes 202760 | tf_op jit(solution)/shard_map/ppermute | solution.py:392
  6.2 5.8 %collective-permute-start.1 = (bf16[8,4224]{1,0:T(8,128)(2,1)S(1)}, bf16[8,4224]{1,0:T(8,128)(2,1)S(1)}, u32[]{:S(2)}, u32[]{:S(2)}) collective-permute-start(bf16[8,4224]{1,0:T(8,128)(2,1)S(1)} %make_message.1.refs_0_), channel_id=1, source_target_pairs={{0,8},{4,12},{8,0},{12,4},{1,9},{5,13},{9,1},{13,5},{2,10},{6,14},... | collective-permute-start | bytes 202760 | tf_op jit(solution)/shard_map/ppermute | solution.py:392
  6.2 5.8 %collective-permute-start.2 = (bf16[8,4224]{1,0:T(8,128)(2,1)S(1)}, bf16[8,4224]{1,0:T(8,128)(2,1)S(1)}, u32[]{:S(2)}, u32[]{:S(2)}) collective-permute-start(bf16[8,4224]{1,0:T(8,128)(2,1)S(1)} %make_message.1.refs_0_), channel_id=1, source_target_pairs={{0,4},{4,0},{8,12},{12,8},{1,5},{5,1},{9,13},{13,9},{2,6},{6,2},{1... | collective-permute-start | bytes 202760 | tf_op jit(solution)/shard_map/ppermute | solution.py:392
  9.1 10.2 %collective-permute-start.3 = (bf16[256,512]{1,0:T(8,128)(2,1)S(1)}, bf16[256,512]{1,0:T(8,128)(2,1)S(1)}, u32[]{:S(2)}, u32[]{:S(2)}) collective-permute-start(bf16[256,512]{1,0:T(8,128)(2,1)S(1)} %get-tuple-element.19.values_ref), channel_id=1, source_target_pairs={{0,4},{4,0},{8,12},{12,8},{1,5},{5,1},{9,13},{13,9},{2,6},{6,2},{1... | collective-permute-start | bytes 786440 | tf_op jit(solution)/shard_map/ppermute | solution.py:392
  12.0 4.9 %copy-start.1 = (bf16[1,1,8,128,1024]{4,3,2,1,0:T(8,128)(2,1)S(1)}, bf16[1,1,8,128,1024]{4,3,2,1,0:T(8,128)(2,1)}, u32[]{:S(2)}) copy-start(bf16[1,1,8,128,1024]{4,3,2,1,0:T(8,128)(2,1)} %param.14) | copy-start | bytes 6291460
  12.0 4.9 %copy-start.2 = (bf16[1,1,8,4096]{3,2,1,0:T(8,128)(2,1)S(1)}, bf16[1,1,8,4096]{3,2,1,0:T(8,128)(2,1)}, u32[]{:S(2)}) copy-start(bf16[1,1,8,4096]{3,2,1,0:T(8,128)(2,1)} %param.13) | copy-start | bytes 196612
  12.0 4.9 %copy-start.3 = (s32[8,128]{1,0:T(8,128)S(1)}, s32[8,128]{1,0:T(8,128)}, u32[]{:S(2)}) copy-start(s32[8,128]{1,0:T(8,128)} %signs_ref.1) | copy-start | bytes 12292
  12.0 4.9 %copy-start.4 = (s32[1,1,8]{2,1,0:T(1,128)S(1)}, s32[1,1,8]{2,1,0:T(1,128)}, u32[]{:S(2)}) copy-start(s32[1,1,8]{2,1,0:T(1,128)} %lengths_ref.1) | copy-start | bytes 100
  12.3 6.8 %collective-permute-start.4 = (bf16[32,256]{1,0:T(8,128)(2,1)S(1)}, bf16[32,256]{1,0:T(8,128)(2,1)S(1)}, u32[]{:S(2)}, u32[]{:S(2)}) collective-permute-start(bf16[32,256]{1,0:T(8,128)(2,1)S(1)} %get-tuple-element.22.refs_0_), channel_id=1, source_target_pairs={{0,4},{4,8},{8,12},{12,0},{1,5},{5,9},{9,13},{13,1},{2,6},{6,10},{... | collective-permute-start | bytes 49160 | tf_op jit(solution)/shard_map/ppermute | solution.py:397
  13.8 5.3 %collective-permute-start.5 = (bf16[32,256]{1,0:T(8,128)(2,1)S(1)}, bf16[32,256]{1,0:T(8,128)(2,1)S(1)}, u32[]{:S(2)}, u32[]{:S(2)}) collective-permute-start(bf16[32,256]{1,0:T(8,128)(2,1)S(1)} %get-tuple-element.22.refs_0_), channel_id=1, source_target_pairs={{0,8},{4,12},{8,0},{12,4},{1,9},{5,13},{9,1},{13,5},{2,10},{6,14},... | collective-permute-start | bytes 49160 | tf_op jit(solution)/shard_map/ppermute | solution.py:397
  15.6 3.7 %collective-permute-start.6 = (bf16[32,256]{1,0:T(8,128)(2,1)S(1)}, bf16[32,256]{1,0:T(8,128)(2,1)S(1)}, u32[]{:S(2)}, u32[]{:S(2)}) collective-permute-start(bf16[32,256]{1,0:T(8,128)(2,1)S(1)} %get-tuple-element.22.refs_0_), channel_id=1, source_target_pairs={{0,12},{4,0},{8,4},{12,8},{1,13},{5,1},{9,5},{13,9},{2,14},{6,2},{... | collective-permute-start | bytes 49160 | tf_op jit(solution)/shard_map/ppermute | solution.py:397
  19.8 5.1 %collective-permute-start.7 = (bf16[8,4480]{1,0:T(8,128)(2,1)S(1)}, bf16[8,4480]{1,0:T(8,128)(2,1)S(1)}, u32[]{:S(2)}, u32[]{:S(2)}) collective-permute-start(bf16[8,4480]{1,0:T(8,128)(2,1)S(1)} %get-tuple-element.23.own_ref), channel_id=1, source_target_pairs={{0,2},{2,0},{1,3},{3,1},{4,6},{6,4},{5,7},{7,5},{8,10},{10,8},{9,1... | collective-permute-start | bytes 215048 | tf_op jit(solution)/shard_map/ppermute | solution.py:392
  21.3 6.9 %collective-permute-start.8 = (bf16[8,4096]{1,0:T(8,128)(2,1)S(1)}, bf16[8,4096]{1,0:T(8,128)(2,1)S(1)}, u32[]{:S(2)}, u32[]{:S(2)}) collective-permute-start(bf16[8,4096]{1,0:T(8,128)(2,1)S(1)} %get-tuple-element.28), channel_id=1, source_target_pairs={{0,10},{2,8},{4,14},{6,12},{8,2},{10,0},{12,6},{14,4},{1,11},{3,9}... | collective-permute-start | bytes 196616 | tf_op jit(solution)/shard_map/ppermute | solution.py:415
  22.4 5.8 %collective-permute-start.9 = (bf16[8,4096]{1,0:T(8,128)(2,1)S(1)}, bf16[8,4096]{1,0:T(8,128)(2,1)S(1)}, u32[]{:S(2)}, u32[]{:S(2)}) collective-permute-start(bf16[8,4096]{1,0:T(8,128)(2,1)S(1)} %get-tuple-element.28), channel_id=1, source_target_pairs={{0,8},{4,12},{8,0},{12,4},{1,9},{5,13},{9,1},{13,5},{2,10},{6,14},... | collective-permute-start | bytes 196616 | tf_op jit(solution)/shard_map/ppermute | solution.py:392

commit v26 on v19

--- a/solution.py
+++ b/solution.py
@@ -397,7 +397,7 @@
     keys, values = project(tokens, kv_weight)
     near_values = from_partner(values, "seq", 1)
     scores, code = partial_scores(heads, columns, keys, messages)
-    scores = [scores] + [from_behind(scores, "seq", d) for d in range(1, seq_count)]
+    scores = [scores] + [from_partner(scores, "seq", seq_count - d) for d in range(1, seq_count)]
     cache_mixed, cache_stats = cache_part(lengths, query, kv_cache[0, 0], signs)
     share, far = mix(heads, code, values, near_values, cache_mixed, cache_stats, scores)
     far_pairs = [(i, i ^ 5) for i in range(2 * seq_count)]

time: 29.2 us -> 30 us (1.027)
  waiting for transfers between devices: 6.08 us -> 6.96 us
    ppermute x3 -> x0, starting transfers between devices: 4.52 us -> none  [from_behind(): lax.ppermute(x, axis, [(i, (i + distance) % count) for i in range(count)])]
    ppermute x6 -> x9, starting transfers between devices: 9.55 us -> 13.1 us  [from_partner(): return lax.ppermute(x, axis, [(i, i ^ distance) for i in range(count)])]
    ppermute x6 -> x9, waiting for transfers between devices: 2.53 us -> 4.45 us  [from_partner(): return lax.ppermute(x, axis, [(i, i ^ distance) for i in range(count)])]
    ppermute x1, starting transfers between devices: 2.12 us -> 3.01 us  [on_device(): lax.ppermute(far, ('seq', 'tp'), far_pairs)]
    ppermute x3 -> x0, waiting for transfers between devices: 0.85 us -> none  [from_behind(): lax.ppermute(x, axis, [(i, (i + distance) % count) for i in range(count)])]
  transfers between devices with their start and end apart: 10 -> 10, of which waited for: 5 -> 5; matrix products, arithmetic and copies ran while one was open for 0% -> 0% of each run, Pallas kernels for 15% -> 14%
where the time goes in v26:
time: 30 us; the launch traced here: 29.8 us
  starting transfers between devices  16.1 us (54%)
  waiting for transfers between devices  6.96 us (23%)
  Pallas kernels  6.66 us (22%)
    ppermute x9, starting transfers between devices, from_partner(): return lax.ppermute(x, axis, [(i, i ^ distance) for i in range(count)])  13.1 us
    ppermute x9, waiting for transfers between devices, from_partner(): return lax.ppermute(x, axis, [(i, i ^ distance) for i in range(count)])  4.45 us
    ppermute x1, starting transfers between devices, on_device(): lax.ppermute(far, ('seq', 'tp'), far_pairs)  3.01 us
    ppermute x1, waiting for transfers between devices, on_device(): lax.ppermute(far, ('seq', 'tp'), far_pairs)  2.51 us
    pallas_call x1, Pallas kernels, project(): pl.pallas_call(project_kernel, in_specs=[vmem] * 2, out_specs=[vmem] * 2,...  2.32 us
    pallas_call x1, Pallas kernels, cache_part(): pl.pallas_call(cache_kernel, in_specs=[pl.BlockSpec(memory_space=pltpu.SM...  1.6 us
    pallas_call x1, Pallas kernels, make_message(): pl.pallas_call(message_kernel, in_specs=[pl.BlockSpec(memory_space=pl.ANY...  1.01 us
    pallas_call x1, Pallas kernels, finish(): pl.pallas_call(functools.partial(finish_kernel, count), out_shape=jax.Sha...  0.99 us
  transfers between devices with their start and end apart: 10, of which 5 were waited for; matrix products, arithmetic and copies ran while one was open for 0% of the time, Pallas kernels for 14%

profile of v26, /device:TPU:0, one launch (start us, length us, event | category | flops | bytes accessed | tf_op | source)
XLA Modules:
  0.0 29.8 jit_solution(5223487401117641215)
XLA Ops:
  0.0 1.0 %make_message.1.refs_0_ = bf16[8,4224]{1,0:T(8,128)(2,1)S(1)} custom-call(bf16[8,4096]{1,0:T(8,128)(2,1)} %bitcast.7, s32[1,64]{1,0:T(1,128)} %bitcast.9, s32[1,64]{1,0:T(1,128)} %requests_ref.1), custom_call_target="tpu_custom_call" | custom-call | flops 99999997952 | bytes 10000 | tf_op jit(solution)/shard_map/make_message/pallas_call | solution.py:100
  1.0 5.1 %collective-permute-start = (bf16[8,4224]{1,0:T(8,128)(2,1)S(1)}, bf16[8,4224]{1,0:T(8,128)(2,1)S(1)}, u32[]{:S(2)}, u32[]{:S(2)}) collective-permute-start(bf16[8,4224]{1,0:T(8,128)(2,1)S(1)} %make_message.1.refs_0_), channel_id=1, source_target_pairs={{0,12},{4,8},{8,4},{12,0},{1,13},{5,9},{9,5},{13,1},{2,14},{6,10},... | collective-permute-start | bytes 202760 | tf_op jit(solution)/shard_map/ppermute | solution.py:382
  6.2 0.0 collective-permute-start.1
  6.2 0.6 %collective-permute-start.2 = (bf16[8,4224]{1,0:T(8,128)(2,1)S(1)}, bf16[8,4224]{1,0:T(8,128)(2,1)S(1)}, u32[]{:S(2)}, u32[]{:S(2)}) collective-permute-start(bf16[8,4224]{1,0:T(8,128)(2,1)S(1)} %make_message.1.refs_0_), channel_id=1, source_target_pairs={{0,4},{4,0},{8,12},{12,8},{1,5},{5,1},{9,13},{13,9},{2,6},{6,2},{1... | collective-permute-start | bytes 202760 | tf_op jit(solution)/shard_map/ppermute | solution.py:382
  6.8 2.3 %project.1 = (bf16[256,512]{1,0:T(8,128)(2,1)S(1)}, bf16[256,512]{1,0:T(8,128)(2,1)S(1)}) custom-call(bf16[256,4096]{1,0:T(8,128)(2,1)S(1)} %copy-done, bf16[4096,1024]{1,0:T(8,128)(2,1)S(1)} %bitcast.5), custom_call_target="tpu_custom_call" | custom-call | flops 2147483648 | bytes 10485760 | tf_op jit(solution)/shard_map/project/pallas_call | solution.py:63
  9.1 1.5 %collective-permute-start.3 = (bf16[256,512]{1,0:T(8,128)(2,1)S(1)}, bf16[256,512]{1,0:T(8,128)(2,1)S(1)}, u32[]{:S(2)}, u32[]{:S(2)}) collective-permute-start(bf16[256,512]{1,0:T(8,128)(2,1)S(1)} %get-tuple-element.15.values_ref), channel_id=1, source_target_pairs={{0,4},{4,0},{8,12},{12,8},{1,5},{5,1},{9,13},{13,9},{2,6},{6,2},{1... | collective-permute-start | bytes 786440 | tf_op jit(solution)/shard_map/ppermute | solution.py:382
  10.6 1.4 %collective-permute-done.1.refs_2_ = bf16[8,4224]{1,0:T(8,128)(2,1)S(1)} collective-permute-done((bf16[8,4224]{1,0:T(8,128)(2,1)S(1)}, bf16[8,4224]{1,0:T(8,128)(2,1)S(1)}, u32[]{:S(2)}, u32[]{:S(2)}) %collective-permute-start.1) | collective-permute-done | bytes 67616 | tf_op jit(solution)/shard_map/ppermute | solution.py:382
  12.0 0.0 collective-permute-done.2.refs_3_
  12.0 0.0 copy-start.4
  12.0 0.3 %partial_scores.1 = (bf16[32,256]{1,0:T(8,128)(2,1)S(1)}, s32[8,256]{1,0:T(8,128)S(1)}) custom-call(bf16[256,512]{1,0:T(8,128)(2,1)S(1)} %get-tuple-element.13.keys_ref, bf16[8,4224]{1,0:T(8,128)(2,1)S(1)} %make_message.1.refs_0_, bf16[8,4224]{1,0:T(8,128)(2,1)S(1)} %collective-permute-done.refs_1_, bf16[8,4224]{1,0:T(8,128)(2,1)S(1)} %collective-permute-done.1.refs_2_, ...), custom_call_target="tpu_custom_call" | custom-call | flops 99999997952 | bytes 10000 | tf_op jit(solution)/shard_map/partial_scores/pallas_call | solution.py:245
  12.3 2.7 %collective-permute-start.4 = (bf16[32,256]{1,0:T(8,128)(2,1)S(1)}, bf16[32,256]{1,0:T(8,128)(2,1)S(1)}, u32[]{:S(2)}, u32[]{:S(2)}) collective-permute-start(bf16[32,256]{1,0:T(8,128)(2,1)S(1)} %get-tuple-element.18.refs_0_), channel_id=1, source_target_pairs={{0,12},{4,8},{8,4},{12,0},{1,13},{5,9},{9,5},{13,1},{2,14},{6,10},... | collective-permute-start | bytes 49160 | tf_op jit(solution)/shard_map/ppermute | solution.py:382
  15.0 0.2 collective-permute-start.5
  15.3 1.5 %collective-permute-start.6 = (bf16[32,256]{1,0:T(8,128)(2,1)S(1)}, bf16[32,256]{1,0:T(8,128)(2,1)S(1)}, u32[]{:S(2)}, u32[]{:S(2)}) collective-permute-start(bf16[32,256]{1,0:T(8,128)(2,1)S(1)} %get-tuple-element.18.refs_0_), channel_id=1, source_target_pairs={{0,4},{4,0},{8,12},{12,8},{1,5},{5,1},{9,13},{13,9},{2,6},{6,2},{1... | collective-permute-start | bytes 49160 | tf_op jit(solution)/shard_map/ppermute | solution.py:382
  16.8 1.6 %cache_part.1 = (f32[8,4096]{1,0:T(8,128)S(1)}, f32[16,128]{1,0:T(8,128)S(1)}) custom-call(s32[1,1,8]{2,1,0:T(1,128)S(1)} %copy-done.4, bf16[8,4096]{1,0:T(8,128)(2,1)S(1)} %bitcast.8, bf16[8,128,1024]{2,1,0:T(8,128)(2,1)S(1)} %bitcast.6, s32[8,128]{1,0:T(8,128)S(1)} %copy-done.3), custom_call_target="tpu_custom_call" | custom-call | flops 16777216 | bytes 2097152 | tf_op jit(solution)/shard_map/cache_part/pallas_call | solution.py:189
  18.4 0.8 %collective-permute-done.4.refs_1_ = bf16[32,256]{1,0:T(8,128)(2,1)S(1)} collective-permute-done((bf16[32,256]{1,0:T(8,128)(2,1)S(1)}, bf16[32,256]{1,0:T(8,128)(2,1)S(1)}, u32[]{:S(2)}, u32[]{:S(2)}) %collective-permute-start.4) | collective-permute-done | bytes 16416 | tf_op jit(solution)/shard_map/ppermute | solution.py:382
  19.2 0.5 %collective-permute-done.5.refs_2_ = bf16[32,256]{1,0:T(8,128)(2,1)S(1)} collective-permute-done((bf16[32,256]{1,0:T(8,128)(2,1)S(1)}, bf16[32,256]{1,0:T(8,128)(2,1)S(1)}, u32[]{:S(2)}, u32[]{:S(2)}) %collective-permute-start.5) | collective-permute-done | bytes 16416 | tf_op jit(solution)/shard_map/ppermute | solution.py:382
  19.7 0.0 collective-permute-done.6.refs_3_
  19.7 0.4 %mix.1 = (bf16[8,4480]{1,0:T(8,128)(2,1)S(1)}, bf16[8,4480]{1,0:T(8,128)(2,1)S(1)}) custom-call(s32[8,256]{1,0:T(8,128)S(1)} %get-tuple-element.14.code_ref, bf16[256,512]{1,0:T(8,128)(2,1)S(1)} %get-tuple-element.15.values_ref, bf16[256,512]{1,0:T(8,128)(2,1)S(1)} %collective-permute-done.3.near_ref, f32[8,4096]{1,0:T(8,128)S(1)} %get-tuple-element.16.cache_ref, ...), custom_call_target="tpu_custom_call" | custom-call | tf_op jit(solution)/shard_map/mix/pallas_call | solution.py:323
  20.1 3.0 %collective-permute-start.7 = (bf16[8,4480]{1,0:T(8,128)(2,1)S(1)}, bf16[8,4480]{1,0:T(8,128)(2,1)S(1)}, u32[]{:S(2)}, u32[]{:S(2)}) collective-permute-start(bf16[8,4480]{1,0:T(8,128)(2,1)S(1)} %get-tuple-element.20), channel_id=1, source_target_pairs={{0,10},{2,8},{4,14},{6,12},{8,2},{10,0},{12,6},{14,4},{1,11},{3,9}... | collective-permute-start | bytes 215048 | tf_op jit(solution)/shard_map/ppermute | solution.py:410
  23.1 0.9 %collective-permute-start.8 = (bf16[8,4480]{1,0:T(8,128)(2,1)S(1)}, bf16[8,4480]{1,0:T(8,128)(2,1)S(1)}, u32[]{:S(2)}, u32[]{:S(2)}) collective-permute-start(bf16[8,4480]{1,0:T(8,128)(2,1)S(1)} %get-tuple-element.20), channel_id=1, source_target_pairs={{0,8},{4,12},{8,0},{12,4},{1,9},{5,13},{9,1},{13,5},{2,10},{6,14},... | collective-permute-start | bytes 215048 | tf_op jit(solution)/shard_map/ppermute | solution.py:382
  24.0 0.5 %collective-permute-start.9 = (bf16[8,4480]{1,0:T(8,128)(2,1)S(1)}, bf16[8,4480]{1,0:T(8,128)(2,1)S(1)}, u32[]{:S(2)}, u32[]{:S(2)}) collective-permute-start(bf16[8,4480]{1,0:T(8,128)(2,1)S(1)} %get-tuple-element.19.own_ref), channel_id=1, source_target_pairs={{0,2},{2,0},{1,3},{3,1},{4,6},{6,4},{5,7},{7,5},{8,10},{10,8},{9,1... | collective-permute-start | bytes 215048 | tf_op jit(solution)/shard_map/ppermute | solution.py:382
  24.6 2.5 %collective-permute-done.7.refs_0_ = bf16[8,4480]{1,0:T(8,128)(2,1)S(1)} collective-permute-done((bf16[8,4480]{1,0:T(8,128)(2,1)S(1)}, bf16[8,4480]{1,0:T(8,128)(2,1)S(1)}, u32[]{:S(2)}, u32[]{:S(2)}) %collective-permute-start.7) | collective-permute-done | bytes 71712 | tf_op jit(solution)/shard_map/ppermute | solution.py:410
  27.1 1.8 %collective-permute-done.8.refs_1_ = bf16[8,4480]{1,0:T(8,128)(2,1)S(1)} collective-permute-done((bf16[8,4480]{1,0:T(8,128)(2,1)S(1)}, bf16[8,4480]{1,0:T(8,128)(2,1)S(1)}, u32[]{:S(2)}, u32[]{:S(2)}) %collective-permute-start.8) | collective-permute-done | bytes 71712 | tf_op jit(solution)/shard_map/ppermute | solution.py:382
  28.9 1.0 %finish.1 = bf16[8,4096]{1,0:T(8,128)(2,1)} custom-call(bf16[8,4480]{1,0:T(8,128)(2,1)S(1)} %get-tuple-element.19.own_ref, bf16[8,4480]{1,0:T(8,128)(2,1)S(1)} %collective-permute-done.7.refs_0_, bf16[8,4480]{1,0:T(8,128)(2,1)S(1)} %collective-permute-done.8.refs_1_, bf16[8,4480]{1,0:T(8,128)(2,1)S(1)} %collective-permute-done.9.refs_2_), custom_call_target="tpu_custom_call" | custom-call | tf_op jit(solution)/shard_map/finish/pallas_call | solution.py:372
  (17 shorter events, 0.0 us)
Async XLA Ops:
  0.0 6.8 %slice-start = ((s8[8388608]{0:T(1024)(128)(4,1)}), s8[4194304]{0:T(1024)(128)(4,1)S(1)}, s32[]{:S(2)}) async-start(s8[8388608]{0:T(1024)(128)(4,1)} %bitcast.4), calls=%async_computation | async-start | bytes 8388608
  0.0 6.8 %slice-start.1 = ((s8[8388608]{0:T(1024)(128)(4,1)}), s8[4194304]{0:T(1024)(128)(4,1)S(1)}, s32[]{:S(2)}) async-start(s8[8388608]{0:T(1024)(128)(4,1)} %bitcast.4), calls=%async_computation.1 | async-start | bytes 8388608
  0.0 6.8 %copy-start = (bf16[256,4096]{1,0:T(8,128)(2,1)S(1)}, bf16[256,4096]{1,0:T(8,128)(2,1)}, u32[]{:S(2)}) copy-start(bf16[256,4096]{1,0:T(8,128)(2,1)} %tokens_ref.1) | copy-start | bytes 6291460
  1.0 9.6 %collective-permute-start = (bf16[8,4224]{1,0:T(8,128)(2,1)S(1)}, bf16[8,4224]{1,0:T(8,128)(2,1)S(1)}, u32[]{:S(2)}, u32[]{:S(2)}) collective-permute-start(bf16[8,4224]{1,0:T(8,128)(2,1)S(1)} %make_message.1.refs_0_), channel_id=1, source_target_pairs={{0,12},{4,8},{8,4},{12,0},{1,13},{5,9},{9,5},{13,1},{2,14},{6,10},... | collective-permute-start | bytes 202760 | tf_op jit(solution)/shard_map/ppermute | solution.py:382
  6.2 5.8 %collective-permute-start.1 = (bf16[8,4224]{1,0:T(8,128)(2,1)S(1)}, bf16[8,4224]{1,0:T(8,128)(2,1)S(1)}, u32[]{:S(2)}, u32[]{:S(2)}) collective-permute-start(bf16[8,4224]{1,0:T(8,128)(2,1)S(1)} %make_message.1.refs_0_), channel_id=1, source_target_pairs={{0,8},{4,12},{8,0},{12,4},{1,9},{5,13},{9,1},{13,5},{2,10},{6,14},... | collective-permute-start | bytes 202760 | tf_op jit(solution)/shard_map/ppermute | solution.py:382
  6.2 5.8 %collective-permute-start.2 = (bf16[8,4224]{1,0:T(8,128)(2,1)S(1)}, bf16[8,4224]{1,0:T(8,128)(2,1)S(1)}, u32[]{:S(2)}, u32[]{:S(2)}) collective-permute-start(bf16[8,4224]{1,0:T(8,128)(2,1)S(1)} %make_message.1.refs_0_), channel_id=1, source_target_pairs={{0,4},{4,0},{8,12},{12,8},{1,5},{5,1},{9,13},{13,9},{2,6},{6,2},{1... | collective-permute-start | bytes 202760 | tf_op jit(solution)/shard_map/ppermute | solution.py:382
  9.1 10.6 %collective-permute-start.3 = (bf16[256,512]{1,0:T(8,128)(2,1)S(1)}, bf16[256,512]{1,0:T(8,128)(2,1)S(1)}, u32[]{:S(2)}, u32[]{:S(2)}) collective-permute-start(bf16[256,512]{1,0:T(8,128)(2,1)S(1)} %get-tuple-element.15.values_ref), channel_id=1, source_target_pairs={{0,4},{4,0},{8,12},{12,8},{1,5},{5,1},{9,13},{13,9},{2,6},{6,2},{1... | collective-permute-start | bytes 786440 | tf_op jit(solution)/shard_map/ppermute | solution.py:382
  12.0 4.8 %copy-start.1 = (bf16[1,1,8,128,1024]{4,3,2,1,0:T(8,128)(2,1)S(1)}, bf16[1,1,8,128,1024]{4,3,2,1,0:T(8,128)(2,1)}, u32[]{:S(2)}) copy-start(bf16[1,1,8,128,1024]{4,3,2,1,0:T(8,128)(2,1)} %param.14) | copy-start | bytes 6291460
  12.0 4.8 %copy-start.2 = (bf16[1,1,8,4096]{3,2,1,0:T(8,128)(2,1)S(1)}, bf16[1,1,8,4096]{3,2,1,0:T(8,128)(2,1)}, u32[]{:S(2)}) copy-start(bf16[1,1,8,4096]{3,2,1,0:T(8,128)(2,1)} %param.13) | copy-start | bytes 196612
  12.0 4.8 %copy-start.3 = (s32[8,128]{1,0:T(8,128)S(1)}, s32[8,128]{1,0:T(8,128)}, u32[]{:S(2)}) copy-start(s32[8,128]{1,0:T(8,128)} %signs_ref.1) | copy-start | bytes 12292
  12.0 4.8 %copy-start.4 = (s32[1,1,8]{2,1,0:T(1,128)S(1)}, s32[1,1,8]{2,1,0:T(1,128)}, u32[]{:S(2)}) copy-start(s32[1,1,8]{2,1,0:T(1,128)} %lengths_ref.1) | copy-start | bytes 100
  12.3 6.8 %collective-permute-start.4 = (bf16[32,256]{1,0:T(8,128)(2,1)S(1)}, bf16[32,256]{1,0:T(8,128)(2,1)S(1)}, u32[]{:S(2)}, u32[]{:S(2)}) collective-permute-start(bf16[32,256]{1,0:T(8,128)(2,1)S(1)} %get-tuple-element.18.refs_0_), channel_id=1, source_target_pairs={{0,12},{4,8},{8,4},{12,0},{1,13},{5,9},{9,5},{13,1},{2,14},{6,10},... | collective-permute-start | bytes 49160 | tf_op jit(solution)/shard_map/ppermute | solution.py:382
  15.0 4.6 %collective-permute-start.5 = (bf16[32,256]{1,0:T(8,128)(2,1)S(1)}, bf16[32,256]{1,0:T(8,128)(2,1)S(1)}, u32[]{:S(2)}, u32[]{:S(2)}) collective-permute-start(bf16[32,256]{1,0:T(8,128)(2,1)S(1)} %get-tuple-element.18.refs_0_), channel_id=1, source_target_pairs={{0,8},{4,12},{8,0},{12,4},{1,9},{5,13},{9,1},{13,5},{2,10},{6,14},... | collective-permute-start | bytes 49160 | tf_op jit(solution)/shard_map/ppermute | solution.py:382
  15.3 4.4 %collective-permute-start.6 = (bf16[32,256]{1,0:T(8,128)(2,1)S(1)}, bf16[32,256]{1,0:T(8,128)(2,1)S(1)}, u32[]{:S(2)}, u32[]{:S(2)}) collective-permute-start(bf16[32,256]{1,0:T(8,128)(2,1)S(1)} %get-tuple-element.18.refs_0_), channel_id=1, source_target_pairs={{0,4},{4,0},{8,12},{12,8},{1,5},{5,1},{9,13},{13,9},{2,6},{6,2},{1... | collective-permute-start | bytes 49160 | tf_op jit(solution)/shard_map/ppermute | solution.py:382
  20.1 7.0 %collective-permute-start.7 = (bf16[8,4480]{1,0:T(8,128)(2,1)S(1)}, bf16[8,4480]{1,0:T(8,128)(2,1)S(1)}, u32[]{:S(2)}, u32[]{:S(2)}) collective-permute-start(bf16[8,4480]{1,0:T(8,128)(2,1)S(1)} %get-tuple-element.20), channel_id=1, source_target_pairs={{0,10},{2,8},{4,14},{6,12},{8,2},{10,0},{12,6},{14,4},{1,11},{3,9}... | collective-permute-start | bytes 215048 | tf_op jit(solution)/shard_map/ppermute | solution.py:410
  23.1 5.7 %collective-permute-start.8 = (bf16[8,4480]{1,0:T(8,128)(2,1)S(1)}, bf16[8,4480]{1,0:T(8,128)(2,1)S(1)}, u32[]{:S(2)}, u32[]{:S(2)}) collective-permute-start(bf16[8,4480]{1,0:T(8,128)(2,1)S(1)} %get-tuple-element.20), channel_id=1, source_target_pairs={{0,8},{4,12},{8,0},{12,4},{1,9},{5,13},{9,1},{13,5},{2,10},{6,14},... | collective-permute-start | bytes 215048 | tf_op jit(solution)/shard_map/ppermute | solution.py:382
  24.0 4.8 %collective-permute-start.9 = (bf16[8,4480]{1,0:T(8,128)(2,1)S(1)}, bf16[8,4480]{1,0:T(8,128)(2,1)S(1)}, u32[]{:S(2)}, u32[]{:S(2)}) collective-permute-start(bf16[8,4480]{1,0:T(8,128)(2,1)S(1)} %get-tuple-element.19.own_ref), channel_id=1, source_target_pairs={{0,2},{2,0},{1,3},{3,1},{4,6},{6,4},{5,7},{7,5},{8,10},{10,8},{9,1... | collective-permute-start | bytes 215048 | tf_op jit(solution)/shard_map/ppermute | solution.py:382
